TPU v7x, 32 devices: a whole 2x2x4 slice. The times are simulated.
32 devices in a mesh: dp: 2 (over x), centers: 16 (over z, y, core).
Axes of the slice: x: 2, y: 2, z: 4, core: 2. Of those that a mesh axis runs over, the one named last changes fastest.
Arguments:
- features: bfloat16 [64, 8192], P(None, 'dp'), may hold values from -8 to 8
- prices: float32 [8192], P('dp'), may hold values from -6 to 6
- slots: int32 [8192], P('dp'), may hold values from 0 to 7
- center_idx: int32 [8192], P('centers'), may hold values from 0 to 8191
- center_scale: float32 [8192], P('centers'), may hold values from 0.5 to 18
Outputs:
- coefficients: float32 [8, 8192], P(None, 'centers')
- residual: float32 [8, 8192], P(None, 'centers')
All inputs are finite; a program needn't handle non-finite values.
Results may differ from a plain program's by a relative error of at most 0.00195.
Values may be sent and summed in bfloat16 or wider, within the bound.
No kernel may reach another device: no remote copies, remote signals or barrier semaphores. Data moves between devices by JAX's collectives and lax.ppermute only.
A program may use at most 64 MiB of HBM per device.

v0:
```python
import jax
import jax.numpy as jnp
from jax import lax
from jax.sharding import PartitionSpec as P

F = 64
SLOTS = 8
ITERS = 2


highest_prec = lax.Precision.HIGHEST
ridge_shift = 0.5
tile_rows = 512


def kernel_rows(features, center_f, center_norm, first_row, row_total):
    columns = lax.dynamic_slice_in_dim(features, first_row, row_total, 1)
    inner_prod = lax.dot_general(
        columns, center_f, (((0,), (0,)), ((), ())), preferred_element_type=jnp.float32
    )
    col32 = columns.astype(jnp.float32)
    row_norm = jnp.sum(col32 * col32, axis=0)
    return jnp.exp(-(row_norm[:, None] + center_norm[None, :] - 2.0 * inner_prod) / (2.0 * F))


def apply_rows(features, center_f, center_norm, scaled, first_row, row_total):

    def one_block(begin):
        kernel_tile = kernel_rows(features, center_f, center_norm, begin, tile_rows)
        return lax.dot_general(
            kernel_tile,
            scaled,
            (((1,), (1,)), ((), ())),
            precision=highest_prec,
            preferred_element_type=jnp.float32,
        )

    def apply_visit(turn, filled):
        return lax.dynamic_update_slice_in_dim(
            filled, one_block(first_row + turn * tile_rows), turn * tile_rows, 0
        )

    start_fill = jnp.zeros((row_total, scaled.shape[0]), jnp.float32)
    return lax.fori_loop(0, row_total // tile_rows, apply_visit, start_fill)


def fold_rows(features, center_f, center_norm, weights, first_row, summed):
    row_total = weights.shape[0]

    def fold_visit(turn, running):
        kernel_tile = kernel_rows(
            features, center_f, center_norm, first_row + turn * tile_rows, tile_rows
        )
        weight_blk = lax.dynamic_slice_in_dim(weights, turn * tile_rows, tile_rows, 0)
        return running + lax.dot_general(
            weight_blk,
            kernel_tile,
            (((0,), (0,)), ((), ())),
            precision=highest_prec,
            preferred_element_type=jnp.float32,
        )

    return lax.fori_loop(0, row_total // tile_rows, fold_visit, summed)


def group_total(partial_value):
    return lax.psum(partial_value, "dp")


def residual_norm(current):
    return lax.psum(jnp.sum(current * current, axis=1), "centers")


def per_device(features, prices, slots, center_idx, center_scale):
    row_count = features.shape[1]
    center_count = center_idx.shape[0]
    group_index = lax.axis_index("dp")
    local_idx = center_idx - group_index * row_count
    inside = (local_idx >= 0) & (local_idx < row_count)
    picked = jnp.take(features, jnp.clip(local_idx, 0, row_count - 1), axis=1)
    contrib = jnp.where(inside[None, :], picked.astype(jnp.float32), 0.0)
    center_f = lax.psum(contrib.astype(jnp.bfloat16), "dp")
    center32 = center_f.astype(jnp.float32)
    center_norm = jnp.sum(center32 * center32, axis=0)
    slot_mask = (slots[:, None] == jnp.arange(SLOTS, dtype=jnp.int32)[None, :]).astype(jnp.float32)
    all_rows = jnp.float32(row_count * lax.axis_size("dp"))
    zero_sum = jnp.zeros((SLOTS, center_count), jnp.float32)
    first_part = fold_rows(
        features, center_f, center_norm, slot_mask * prices[:, None], 0, zero_sum
    )
    target_side = center_scale[None, :] * group_total(first_part) / jnp.sqrt(all_rows)
    coefficients = jnp.zeros((SLOTS, center_count), jnp.float32)
    residual = target_side
    direction = target_side
    norm_now = residual_norm(residual)
    for iteration in range(ITERS):
        scaled = center_scale[None, :] * direction
        row_local = apply_rows(features, center_f, center_norm, scaled, 0, row_count)
        row_whole = lax.psum(row_local, "centers")
        partial_value = fold_rows(
            features, center_f, center_norm, row_whole * slot_mask, 0, zero_sum
        )
        summed = group_total(partial_value)
        applied = center_scale[None, :] * summed / all_rows + ridge_shift * direction
        curve_sum = lax.psum(jnp.sum(direction * applied, axis=1), "centers")
        step_size = norm_now / curve_sum
        coefficients = coefficients + step_size[:, None] * direction
        residual = residual - step_size[:, None] * applied
        norm_next = residual_norm(residual)
        direction = residual + (norm_next / norm_now)[:, None] * direction
        norm_now = norm_next
    return (coefficients, residual)


def solution(mesh):
    return jax.shard_map(
        per_device,
        mesh=mesh,
        in_specs=(P(None, "dp"), P("dp"), P("dp"), P("centers"), P("centers")),
        out_specs=(P(None, "centers"), P(None, "centers")),
        check_vma=False,
    )
```

profile of v0, /device:TPU:0, one launch (start us, length us, event | category | flops | bytes accessed | tf_op | source)
XLA Modules:
  0.0 381.3 jit_solution(9275397764055594447)
XLA Ops:
  7.2 0.7 copy-done.7
  7.9 1.5 copy.7
  9.5 1.3 gather_fusion
  10.8 0.9 fusion.36
  12.4 23.6 %all-reduce.5.cloned.1.call-done = bf16[64,512]{0,1:T(8,128)(2,1)} async-done(((bf16[64,512]{0,1:T(8,128)(2,1)}), bf16[64,512]{0,1:T(8,128)(2,1)}) %all-reduce.5.cloned.1.call-update) | async-done | bytes 65552 | tf_op jit(solution)/shard_map/psum | solution.py:82
  36.0 1.1 copy.8
  37.2 8.5 %while.70 = (s32[]{:T(128)}, f32[8,512]{1,0:T(8,128)S(1)}, f32[4096,8]{0,1:T(8,128)S(1)}, bf16[64,4096]{1,0:T(8,128)(2,1)S(1)}, f32[512]{0:T(512)S(1)}, /*index=...) while((s32[]{:T(128)}, f32[8,512]{1,0:T(8,128)S(1)}, ...), condition=%wide.region_4.5_spmd.clone, body=%wide.region_2.4_spmd.clone.sunk | while | flops 60136964 | bytes 2349225 | solution.py:63
  37.7 0.6 convolution_add_fusion.6
  38.8 0.6 convolution_add_fusion.6
  39.8 0.6 convolution_add_fusion.6
  40.9 0.6 convolution_add_fusion.6
  42.0 0.6 convolution_add_fusion.6
  43.0 0.6 convolution_add_fusion.6
  44.1 0.6 convolution_add_fusion.6
  45.2 0.6 convolution_add_fusion.6
  45.8 6.8 %psum.71 = f32[8,512]{1,0:T(8,128)S(1)} all-reduce(f32[8,512]{1,0:T(8,128)S(1)} %get-tuple-element.547), channel_id=1, replica_groups=mesh['dp'=2,'centers'=16] {'dp'}, use_global_device_ids=true, to_apply=%region_5.6 | all-reduce | flops 4096 | bytes 32768 | tf_op jit(solution)/shard_map/psum | solution.py:67
  52.6 11.6 %while.68 = (s32[]{:T(128)}, f32[4096,8]{0,1:T(8,128)S(1)}, bf16[64,4096]{1,0:T(8,128)(2,1)S(1)}, f32[512]{0:T(512)S(1)}, bf16[64,512]{1,0:T(8,128)(2,1)S(1)}, /...) while((s32[]{:T(128)}, f32[4096,8]{0,1:T(8,128)S(1)}, ...), condition=%wide.region_10.11_spmd, body=%wide.region_8.10_spmd.sunk | while | flops 60128772 | bytes 2332831 | solution.py:44
  53.1 1.0 convolution_dynamic-update-slice_fusion.4
  54.6 1.0 convolution_dynamic-update-slice_fusion.4
  56.0 1.0 convolution_dynamic-update-slice_fusion.4
  57.4 1.0 convolution_dynamic-update-slice_fusion.4
  58.9 1.0 convolution_dynamic-update-slice_fusion.4
  60.3 1.0 convolution_dynamic-update-slice_fusion.4
  61.8 1.0 convolution_dynamic-update-slice_fusion.4
  63.2 1.0 convolution_dynamic-update-slice_fusion.4
  64.2 0.7 copy-done.3
  65.0 88.3 %all-reduce.7.cloned.1.call-done = f32[4096,8]{0,1:T(8,128)} async-done(((f32[4096,8]{0,1:T(8,128)}), f32[4096,8]{0,1:T(8,128)}) %all-reduce.7.cloned.1.call-update) | async-done | bytes 131088 | tf_op jit(solution)/shard_map/psum | solution.py:99
  153.3 0.9 fusion.38
  154.2 8.5 %while.71 = (s32[]{:T(128)}, f32[8,512]{1,0:T(8,128)S(1)}, f32[4096,8]{0,1:T(8,128)S(1)}, bf16[64,4096]{1,0:T(8,128)(2,1)S(1)}, f32[512]{0:T(512)S(1)}, /*index=...) while((s32[]{:T(128)}, f32[8,512]{1,0:T(8,128)S(1)}, ...), condition=%wide.region_14.15_spmd.clone, body=%wide.region_12.14_spmd.clone.sunk | while | flops 60136964 | bytes 2349225 | solution.py:63
  154.7 0.6 convolution_add_fusion.7
  155.8 0.6 convolution_add_fusion.7
  156.8 0.6 convolution_add_fusion.7
  157.9 0.6 convolution_add_fusion.7
  159.0 0.6 convolution_add_fusion.7
  160.0 0.6 convolution_add_fusion.7
  161.1 0.6 convolution_add_fusion.7
  162.2 0.6 convolution_add_fusion.7
  162.8 8.1 %psum.74 = f32[8,512]{1,0:T(8,128)S(1)} all-reduce(f32[8,512]{1,0:T(8,128)S(1)} %get-tuple-element.549), channel_id=1, replica_groups=mesh['dp'=2,'centers'=16] {'dp'}, use_global_device_ids=true, to_apply=%region_15.16 | all-reduce | flops 4096 | bytes 32768 | tf_op jit(solution)/shard_map/psum | solution.py:67
  171.1 29.7 %all-reduce = (f32[8]{0:T(128)S(1)}, f32[8]{0:T(128)S(1)}) all-reduce(f32[8]{0:T(128)S(1)} %get-tuple-element.646, f32[8]{0:T(128)S(1)} %get-tuple-element.645), channel_id=1, replica_groups=mesh['dp'=2,'centers'=16] {'centers'}, use_global_device_ids=true, to_apply=%region_7.8 | all-reduce | flops 16 | bytes 128 | tf_op jit(solution)/shard_map/psum | solution.py:71
  201.0 29.8 %psum.76 = f32[8]{0:T(128)S(1)} all-reduce(f32[8]{0:T(128)S(1)} %multiply_reduce_fusion.7), channel_id=1, replica_groups=mesh['dp'=2,'centers'=16] {'centers'}, use_global_device_ids=true, to_apply=%region_19.20 | all-reduce | flops 8 | bytes 64 | tf_op jit(solution)/shard_map/psum | solution.py:71
  230.8 11.6 %while.69 = (s32[]{:T(128)}, f32[4096,8]{0,1:T(8,128)S(1)}, bf16[64,4096]{1,0:T(8,128)(2,1)S(1)}, f32[512]{0:T(512)S(1)}, bf16[64,512]{1,0:T(8,128)(2,1)S(1)}, /...) while((s32[]{:T(128)}, f32[4096,8]{0,1:T(8,128)S(1)}, ...), condition=%wide.region_22.23_spmd, body=%wide.region_20.22_spmd.sunk | while | flops 60128772 | bytes 2332831 | solution.py:44
  231.3 1.0 convolution_dynamic-update-slice_fusion.5
  232.8 1.0 convolution_dynamic-update-slice_fusion.5
  234.2 1.0 convolution_dynamic-update-slice_fusion.5
  235.6 1.0 convolution_dynamic-update-slice_fusion.5
  237.1 1.0 convolution_dynamic-update-slice_fusion.5
  238.5 1.0 convolution_dynamic-update-slice_fusion.5
  240.0 1.0 convolution_dynamic-update-slice_fusion.5
  241.4 1.0 convolution_dynamic-update-slice_fusion.5
  242.4 0.7 copy-done.2
  243.1 83.5 %all-reduce.9.cloned.1.call-done = f32[4096,8]{0,1:T(8,128)} async-done(((f32[4096,8]{0,1:T(8,128)}), f32[4096,8]{0,1:T(8,128)}) %all-reduce.9.cloned.1.call-update) | async-done | bytes 131088 | tf_op jit(solution)/shard_map/psum | solution.py:99
  326.6 0.9 fusion.37
  327.5 8.5 %while.72 = (s32[]{:T(128)}, f32[8,512]{1,0:T(8,128)S(1)}, f32[4096,8]{0,1:T(8,128)S(1)}, bf16[64,4096]{1,0:T(8,128)(2,1)S(1)}, f32[512]{0:T(512)S(1)}, /*index=...) while((s32[]{:T(128)}, f32[8,512]{1,0:T(8,128)S(1)}, ...), condition=%wide.region_26.27_spmd.clone, body=%wide.region_24.26_spmd.clone.sunk | while | flops 60136964 | bytes 2349225 | solution.py:63
  328.0 0.6 convolution_add_fusion.8
  329.1 0.6 convolution_add_fusion.8
  330.1 0.6 convolution_add_fusion.8
  331.2 0.6 convolution_add_fusion.8
  332.3 0.6 convolution_add_fusion.8
  333.3 0.6 convolution_add_fusion.8
  334.4 0.6 convolution_add_fusion.8
  335.5 0.6 convolution_add_fusion.8
  336.1 8.1 %psum.78 = f32[8,512]{1,0:T(8,128)S(1)} all-reduce(f32[8,512]{1,0:T(8,128)S(1)} %get-tuple-element.551), channel_id=1, replica_groups=mesh['dp'=2,'centers'=16] {'dp'}, use_global_device_ids=true, to_apply=%region_27.28 | all-reduce | flops 4096 | bytes 32768 | tf_op jit(solution)/shard_map/psum | solution.py:67
  344.4 29.7 %psum.79 = f32[8]{0:T(128)S(1)} all-reduce(f32[8]{0:T(128)S(1)} %multiply_reduce_fusion.6), channel_id=1, replica_groups=mesh['dp'=2,'centers'=16] {'centers'}, use_global_device_ids=true, to_apply=%region_29.30 | all-reduce | flops 8 | bytes 64 | tf_op jit(solution)/shard_map/psum | solution.py:105
  374.1 0.7 multiply_subtract_fusion
  (117 shorter events, 19.3 us)
Async XLA Ops:
  7.2 28.8 %all-reduce.5.cloned.1.call-start = ((), (), s32[]{:S(2)}) async-start(), calls=%async_computation | async-start | bytes 262144 | tf_op jit(solution)/shard_map/psum | solution.py:82
  7.2 0.7 copy-start.7
  9.4 2.3 copy-start.4
  9.5 2.3 copy-start.6
  10.8 26.4 %copy-start = (bf16[64,4096]{1,0:T(8,128)(2,1)S(1)}, bf16[64,4096]{1,0:T(8,128)(2,1)}, u32[]{:S(2)}) copy-start(bf16[64,4096]{1,0:T(8,128)(2,1)} %param.15) | copy-start | bytes 1572868
  11.7 0.7 copy-start.5
  11.7 141.6 %all-reduce.7.cloned.1.call-start = ((), (), s32[]{:S(2)}) async-start(), calls=%async_computation.1 | async-start | bytes 262144 | tf_op jit(solution)/shard_map/psum | solution.py:99
  36.0 1.1 copy-start.1
  64.2 0.7 copy-start.3
  64.9 261.7 %all-reduce.9.cloned.1.call-start = ((), (), s32[]{:S(2)}) async-start(), calls=%async_computation.2 | async-start | bytes 262144 | tf_op jit(solution)/shard_map/psum | solution.py:99
  242.4 0.7 copy-start.2
Sparse Core Ops, SparseCore 0:
  11.8 24.1 all-reduce.4
  65.0 88.2 all-reduce.6
  243.2 83.3 all-reduce.8
where the time goes:
time: 382 us; the launch traced here: 381 us
  waiting for transfers between devices  195 us (51%)
  blocking collectives  112 us (29%)
  matrix products  46.5 us (12%)
  between operations  13.9 us (4%)
  local copies, waits for them, and re-layouts  6.55 us (2%)
  other arithmetic  5.81 us (2%)
    psum x2, waiting for transfers between devices, per_device(): row_whole = lax.psum(row_local, 'centers')  172 us
    psum x2, blocking collectives, residual_norm(): return lax.psum(jnp.sum(current * current, axis=1), 'centers')  59.5 us
    psum x1, blocking collectives, per_device(): curve_sum = lax.psum(jnp.sum(direction * applied, axis=1), 'centers')  29.7 us
    psum x1, waiting for transfers between devices, per_device(): center_f = lax.psum(contrib.astype(jnp.bfloat16), 'dp')  23.6 us
    psum x3, blocking collectives, group_total(): return lax.psum(partial_value, 'dp')  23.1 us
    dot_general x40, matrix products, kernel_rows(): lax.dot_general(columns, center_f, (((0,), (0,)), ((), ())), preferred_el...  16.1 us
    dot_general x16, matrix products, one_block(): lax.dot_general(kernel_tile, scaled, (((1,), (1,)), ((), ())), precision=...  15.8 us
    dot_general x24, matrix products, fold_visit(): lax.dot_general(weight_blk, kernel_tile, (((0,), (0,)), ((), ())), precis...  14.6 us
  transfers between devices with their start and end apart: 3, of which 3 were waited for; matrix products, arithmetic and copies ran while one was open for 0% of the time, Pallas kernels for 0%

commit v1 on v0

v1 whole, which is shorter than its diff:
```python
import functools
import math

import jax
import jax.numpy as jnp
from jax import lax
from jax.experimental import pallas as pl
from jax.experimental.pallas import tpu as pltpu
from jax.sharding import PartitionSpec as P

SLOTS = 8
RIDGE = 0.5
CHUNK = 512
EXTRA = 128
f32 = jnp.float32
bf16 = jnp.bfloat16


def split3(value):
    high = value.astype(bf16).astype(f32)
    rest = value - high
    mid = rest.astype(bf16).astype(f32)
    return high, mid, rest - mid


def stack3(value):
    return jnp.concatenate(split3(value), axis=0).astype(bf16)


def unstack3(value):
    return value[0:8] + (value[8:16] + value[16:24])


def pair_total(parts):
    while len(parts) > 1:
        parts = [parts[i] + parts[i + 1] for i in range(0, len(parts), 2)]
    return parts[0]


def total_of(refs):
    return pair_total([ref[...] for ref in refs])


def slot_mask(slots_ref, begin):
    row = lax.broadcasted_iota(jnp.int32, (SLOTS, CHUNK), 0)
    return slots_ref[:, begin : begin + CHUNK] == row


def with_norms(feat, feat_first):
    feat32 = feat.astype(f32)
    half = -0.5 * jnp.sum(feat32 * feat32, axis=0, keepdims=True)
    high, mid, low = split3(half)
    row = lax.broadcasted_iota(jnp.int32, (16, feat.shape[1]), 0)
    base = 0 if feat_first else 3
    extra = jnp.where(row < 6, 1.0, 0.0)
    for place, part in enumerate((high, mid, low)):
        extra = jnp.where(row == base + place, part, extra)
    return jnp.concatenate([feat, extra.astype(bf16)], axis=0)


def pick_body(feat_ref, idx_ref, out_ref):
    total = jnp.zeros(out_ref.shape, f32)
    count = out_ref.shape[1]
    for begin in range(0, feat_ref.shape[1], CHUNK):
        row = lax.broadcasted_iota(jnp.int32, (CHUNK, count), 0)
        hit = row == (idx_ref[...] - begin)
        one_hot = jnp.where(hit, 1.0, 0.0).astype(bf16)
        total += jnp.dot(
            feat_ref[:, begin : begin + CHUNK], one_hot, preferred_element_type=f32
        )
    out_ref[...] = total.astype(bf16)


def kernel_body(parts, feat_ref, prices_ref, slots_ref, *refs):
    center_refs, (high_ref, low_ref, out_ref) = refs[:parts], refs[parts:]
    center = with_norms(total_of(center_refs), True)
    count = center.shape[1]
    total = jnp.zeros((24, count), f32)
    for begin in range(0, feat_ref.shape[1], CHUNK):
        here = slice(begin, begin + CHUNK)
        columns = with_norms(feat_ref[:, here], False)
        inner = lax.dot_general(
            center, columns, (((0,), (0,)), ((), ())), preferred_element_type=f32
        )
        value = jnp.exp2(inner * (math.log2(math.e) / 64.0))
        high = value.astype(bf16)
        low = (value - high.astype(f32)).astype(bf16)
        high_ref[:, here] = high
        low_ref[:, here] = low
        weight = stack3(jnp.where(slot_mask(slots_ref, begin), prices_ref[:, here], 0.0))
        for piece in (high, low):
            total += lax.dot_general(
                weight, piece, (((1,), (1,)), ((), ())), preferred_element_type=f32
            )
    out_ref[...] = unstack3(total)


def apply_rows(scaled, high_ref, low_ref, slots_ref, out_ref):
    stacked = stack3(scaled)
    for turn, begin in enumerate(range(0, high_ref.shape[1], CHUNK)):
        here = slice(begin, begin + CHUNK)
        value = jnp.dot(stacked, high_ref[:, here], preferred_element_type=f32)
        value += jnp.dot(stacked, low_ref[:, here], preferred_element_type=f32)
        own = jnp.where(slot_mask(slots_ref, begin), unstack3(value), 0.0)
        out_ref[turn : turn + 1, 0:CHUNK] = jnp.sum(own, axis=0, keepdims=True)


def fold_rows(row_weights, high_ref, low_ref, out_ref):
    count = high_ref.shape[0]
    total = jnp.zeros((24, count), f32)
    square = jnp.zeros((SLOTS, 1), f32)
    for turn, begin in enumerate(range(0, high_ref.shape[1], CHUNK)):
        here = slice(begin, begin + CHUNK)
        weight = row_weights(turn, begin)
        square += jnp.sum(weight * weight, axis=1, keepdims=True)
        weight = stack3(weight)
        for ref in (high_ref, low_ref):
            total += lax.dot_general(
                weight, ref[:, here], (((1,), (1,)), ((), ())), preferred_element_type=f32
            )
    out_ref[:, 0:count] = unstack3(total)
    out_ref[:, count : count + EXTRA] = jnp.broadcast_to(square, (SLOTS, EXTRA))


def row_sum(value):
    return jnp.sum(value, axis=1, keepdims=True)


def first_apply_body(parts, scale_over_root, *refs):
    first_refs = refs[:parts]
    scale_ref, slots_ref, high_ref, low_ref, target_ref, out_ref = refs[parts:]
    scale = scale_ref[...]
    target = scale * total_of(first_refs) * scale_over_root
    target_ref[...] = target
    out_ref[:, CHUNK:] = jnp.broadcast_to(row_sum(target * target), (SLOTS, EXTRA))
    apply_rows(scale * target, high_ref, low_ref, slots_ref, out_ref)


def first_fold_body(parts, *refs):
    row_refs = refs[:parts]
    slots_ref, high_ref, low_ref, rows_ref, out_ref = refs[parts:]
    rows_ref[...] = total_of(row_refs)

    def row_weights(turn, begin):
        value = rows_ref[turn : turn + 1, 0:CHUNK]
        return jnp.where(slot_mask(slots_ref, begin), value, 0.0)

    fold_rows(row_weights, high_ref, low_ref, out_ref)


def second_apply_body(parts, inv_rows, *refs):
    fold_refs = refs[:parts]
    (scale_ref, slots_ref, high_ref, low_ref, target_ref, rows_ref,
     residual_ref, step_ref, out_ref) = refs[parts:]
    count = scale_ref.shape[1]
    folded = total_of(fold_refs)
    scale = scale_ref[...]
    target = target_ref[...]
    norm = rows_ref[:, CHUNK : CHUNK + 1]
    applied = scale * folded[:, 0:count] * inv_rows + RIDGE * target
    step = norm / (folded[:, count : count + 1] * inv_rows + RIDGE * norm)
    residual = target - step * applied
    residual_ref[...] = residual
    step_ref[...] = jnp.broadcast_to(step, step_ref.shape)
    lane = lax.broadcasted_iota(jnp.int32, (SLOTS, EXTRA), 1)
    out_ref[:, CHUNK:] = jnp.where(
        lane == 0, row_sum(residual * residual), row_sum(residual * target)
    )
    apply_rows(scale * residual, high_ref, low_ref, slots_ref, out_ref)


def second_fold_body(parts, *refs):
    row_refs = refs[:parts]
    slots_ref, high_ref, low_ref, rows_ref, sums_ref, out_ref = refs[parts:]
    latest = total_of(row_refs)
    sums_ref[...] = latest[:, CHUNK:]
    ratio = latest[:, CHUNK : CHUNK + 1] / rows_ref[:, CHUNK : CHUNK + 1]

    def row_weights(turn, begin):
        value = latest[turn : turn + 1, 0:CHUNK] + ratio * rows_ref[turn : turn + 1, 0:CHUNK]
        return jnp.where(slot_mask(slots_ref, begin), value, 0.0)

    fold_rows(row_weights, high_ref, low_ref, out_ref)


def finish_body(parts, inv_rows, *refs):
    fold_refs = refs[:parts]
    (scale_ref, target_ref, residual_ref, step_ref, rows_ref, sums_ref,
     coefficients_ref, out_ref) = refs[parts:]
    count = scale_ref.shape[1]
    folded = total_of(fold_refs)
    target = target_ref[...]
    residual = residual_ref[...]
    first_norm = rows_ref[:, CHUNK : CHUNK + 1]
    norm = sums_ref[:, 0:1]
    cross = sums_ref[:, 1:2]
    ratio = norm / first_norm
    direction = residual + ratio * target
    square = norm + 2.0 * ratio * cross + ratio * ratio * first_norm
    applied = scale_ref[...] * folded[:, 0:count] * inv_rows + RIDGE * direction
    step = norm / (folded[:, count : count + 1] * inv_rows + RIDGE * square)
    coefficients_ref[...] = step_ref[:, 0:1] * target + step * direction
    out_ref[...] = residual - step * applied


def call(body, out_shape, *args):
    return pl.pallas_call(
        body,
        out_shape=out_shape,
        in_specs=[pl.BlockSpec(memory_space=pltpu.VMEM)] * len(args),
        out_specs=jax.tree.map(lambda _: pl.BlockSpec(memory_space=pltpu.VMEM), out_shape),
        compiler_params=pltpu.CompilerParams(vmem_limit_bytes=40 * 1024 * 1024),
    )(*args)


def exchange(value, axis):
    size = lax.axis_size(axis)
    parts = [value]
    stride = 1
    while stride < size:
        value = pair_total(parts)
        parts = [value]
        span = min(4, size // stride)
        for offset in range(1, span):
            pairs = [(i, i ^ (offset * stride)) for i in range(size)]
            parts.append(lax.ppermute(value, axis, pairs))
        stride *= span
    return parts


def shaped(shape, dtype=f32):
    return jax.ShapeDtypeStruct(shape, dtype)


def per_device(features, prices, slots, center_idx, center_scale):
    row_count = features.shape[1]
    count = center_idx.shape[0]
    all_rows = row_count * lax.axis_size("dp")
    local_idx = (center_idx - lax.axis_index("dp") * row_count).reshape(1, count)
    prices = prices.reshape(1, row_count)
    slots = slots.reshape(1, row_count)
    scale = center_scale.reshape(1, count)
    turns = row_count // CHUNK
    part = functools.partial

    picked = call(pick_body, shaped((features.shape[0], count), bf16), features, local_idx)
    centers = exchange(picked, "dp")
    block = shaped((count, row_count), bf16)
    high, low, first = call(
        part(kernel_body, len(centers)),
        (block, block, shaped((SLOTS, count))),
        features, prices, slots, *centers,
    )
    firsts = exchange(first, "dp")
    row_shape = shaped((turns, CHUNK + EXTRA))
    fold_shape = shaped((SLOTS, count + EXTRA))
    vector = shaped((SLOTS, count))
    narrow = shaped((SLOTS, EXTRA))
    target, rows = call(
        part(first_apply_body, len(firsts), 1.0 / math.sqrt(all_rows)),
        (vector, row_shape),
        *firsts, scale, slots, high, low,
    )
    rows = exchange(rows, "centers")
    rows, folded = call(
        part(first_fold_body, len(rows)), (row_shape, fold_shape), *rows, slots, high, low
    )
    folds = exchange(folded, "dp")
    residual, step, latest = call(
        part(second_apply_body, len(folds), 1.0 / all_rows),
        (vector, narrow, row_shape),
        *folds, scale, slots, high, low, target, rows,
    )
    latest = exchange(latest, "centers")
    sums, folded = call(
        part(second_fold_body, len(latest)),
        (narrow, fold_shape),
        *latest, slots, high, low, rows,
    )
    folds = exchange(folded, "dp")
    return call(
        part(finish_body, len(folds), 1.0 / all_rows),
        (vector, vector),
        *folds, scale, target, residual, step, rows, sums,
    )


def solution(mesh):
    return jax.shard_map(
        per_device,
        mesh=mesh,
        in_specs=(P(None, "dp"), P("dp"), P("dp"), P("centers"), P("centers")),
        out_specs=(P(None, "centers"), P(None, "centers")),
        check_vma=False,
    )
```

time: 382 us -> 58.5 us (0.15)
  waiting for transfers between devices: 195 us -> 18.4 us
  blocking collectives: 112 us -> 0 us
  matrix products: 46.5 us -> 0 us
  starting transfers between devices: 0.12 us -> 21.4 us
  Pallas kernels: 0 us -> 13.7 us
  between operations: 13.9 us -> 0.71 us
  other arithmetic: 5.81 us -> 0.7 us
    psum x3 -> x0, waiting for transfers between devices: 195 us -> none  [the longest x2 172 us: per_device(): row_whole = lax.psum(row_local, 'centers')]
    psum x6 -> x0, blocking collectives: 112 us -> none  [the longest x2 59.5 us: residual_norm(): return lax.psum(jnp.sum(current * current, axis=1), 'centers')]
    dot_general x80 -> x0, matrix products: 46.5 us -> none  [the longest x40 16.1 us: kernel_rows(): lax.dot_general(columns, center_f, (((0,), (0,)), ((), ())), preferred_el...]
    ppermute x0 -> x16, starting transfers between devices: none -> 21.4 us  [exchange(): parts.append(lax.ppermute(value, axis, pairs))]
    ppermute x0 -> x16, waiting for transfers between devices: none -> 18.4 us  [exchange(): parts.append(lax.ppermute(value, axis, pairs))]
    pallas_call x0 -> x7, Pallas kernels: none -> 13.7 us  [call(): pl.pallas_call(body, out_shape=out_shape, in_specs=[pl.BlockSpec(memory_s...]
  transfers between devices with their start and end apart: 3 -> 16, of which waited for: 3 -> 13; matrix products, arithmetic and copies ran while one was open for 0% -> 0% of each run, Pallas kernels for 0% -> 0%
where the time goes in v1:
time: 58.5 us; the launch traced here: 58.1 us
  starting transfers between devices  21.4 us (37%)
  waiting for transfers between devices  18.4 us (31%)
  Pallas kernels  13.7 us (23%)
  local copies, waits for them, and re-layouts  3.16 us (5%)
  between operations  0.71 us (1%)
  other arithmetic  0.7 us (1%)
    ppermute x16, starting transfers between devices, exchange(): parts.append(lax.ppermute(value, axis, pairs))  21.4 us
    ppermute x16, waiting for transfers between devices, exchange(): parts.append(lax.ppermute(value, axis, pairs))  18.4 us
    pallas_call x7, Pallas kernels, call(): pl.pallas_call(body, out_shape=out_shape, in_specs=[pl.BlockSpec(memory_s...  13.7 us
    unnamed x10, local copies, waits for them, and re-layouts  3.16 us
  transfers between devices with their start and end apart: 16, of which 13 were waited for; matrix products, arithmetic and copies ran while one was open for 0% of the time, Pallas kernels for 0%

profile of v1, /device:TPU:0, one launch (start us, length us, event | category | flops | bytes accessed | tf_op | source)
XLA Modules:
  0.0 58.1 jit_solution(10615153383762684619)
XLA Ops:
  0.6 0.7 %broadcast_subtract_fusion = s32[512]{0:T(512)S(1)} fusion(s32[512]{0:T(512)} %param.8, s32[]{:T(128)S(6)} %mul.3), kind=kLoop, calls=%fused_computation.2 | loop fusion | flops 512 | bytes 4100 | tf_op jit(solution)/shard_map/sub | solution.py:239
  1.3 0.0 copy-start
  1.3 1.0 %copy-done = bf16[64,4096]{1,0:T(8,128)(2,1)S(1)} copy-done((bf16[64,4096]{1,0:T(8,128)(2,1)S(1)}, bf16[64,4096]{1,0:T(8,128)(2,1)}, u32[]{:S(2)}) %copy-start) | copy-done | bytes 524312
  2.4 0.8 %shard_map.68.refs_0_ = bf16[64,512]{1,0:T(8,128)(2,1)S(1)} custom-call(bf16[64,4096]{1,0:T(8,128)(2,1)S(1)} %copy-done, s32[1,512]{1,0:T(1,128)S(1)} %bitcast.13), custom_call_target="tpu_custom_call" | custom-call | tf_op jit(solution)/shard_map/pallas_call | solution.py:207
  3.2 3.0 %collective-permute-start = (bf16[64,512]{1,0:T(8,128)(2,1)S(1)}, bf16[64,512]{1,0:T(8,128)(2,1)S(1)}, u32[]{:S(2)}, u32[]{:S(2)}) collective-permute-start(bf16[64,512]{1,0:T(8,128)(2,1)S(1)} %shard_map.68.refs_0_), channel_id=1, source_target_pairs={{0,16},{16,0},{1,17},{17,1},{2,18},{18,2},{3,19},{19,3},{4,20},{20... | collective-permute-start | bytes 196616 | tf_op jit(solution)/shard_map/ppermute | solution.py:226
  6.2 2.2 %collective-permute-done.refs_1_ = bf16[64,512]{1,0:T(8,128)(2,1)S(1)} collective-permute-done((bf16[64,512]{1,0:T(8,128)(2,1)S(1)}, bf16[64,512]{1,0:T(8,128)(2,1)S(1)}, u32[]{:S(2)}, u32[]{:S(2)}) %collective-permute-start) | collective-permute-done | bytes 65568 | tf_op jit(solution)/shard_map/ppermute | solution.py:226
  8.5 0.0 copy-start.1
  8.5 0.7 %copy-done.1 = s32[4096]{0:T(1024)S(1)} copy-done((s32[4096]{0:T(1024)S(1)}, s32[4096]{0:T(1024)}, u32[]{:S(2)}) %copy-start.1) | copy-done | bytes 16408
  9.2 0.0 copy-start.4
  9.2 0.7 %copy-done.4 = f32[4096]{0:T(1024)S(1)} copy-done((f32[4096]{0:T(1024)S(1)}, f32[4096]{0:T(1024)}, u32[]{:S(2)}) %copy-start.4) | copy-done | bytes 16408
  9.9 3.9 %shard_map.69 = (bf16[512,4096]{1,0:T(8,128)(2,1)S(1)}, bf16[512,4096]{1,0:T(8,128)(2,1)S(1)}, f32[8,512]{1,0:T(8,128)S(1)}) custom-call(bf16[64,4096]{1,0:T(8,128)(2,1)S(1)} %copy-done, f32[1,4096]{1,0:T(1,128)S(1)} %bitcast.12, s32[1,4096]{1,0:T(1,128)S(1)} %bitcast.4, bf16[64,512]{1,0:T(8,128)(2,1)S(1)} %shard_map.68.refs_0_, ...), custom_call_target="tpu_custom_call" | custom-call | tf_op jit(solution)/shard_map/pallas_call | solution.py:207
  13.8 2.1 %collective-permute-start.1 = (f32[8,512]{1,0:T(8,128)S(1)}, f32[8,512]{1,0:T(8,128)S(1)}, u32[]{:S(2)}, u32[]{:S(2)}) collective-permute-start(f32[8,512]{1,0:T(8,128)S(1)} %get-tuple-element.14.refs_0_), channel_id=1, source_target_pairs={{0,16},{16,0},{1,17},{17,1},{2,18},{18,2},{3,19},{19,3},{4,20},{20... | collective-permute-start | bytes 49160 | tf_op jit(solution)/shard_map/ppermute | solution.py:226
  15.8 1.7 %collective-permute-done.1.refs_1_ = f32[8,512]{1,0:T(8,128)S(1)} collective-permute-done((f32[8,512]{1,0:T(8,128)S(1)}, f32[8,512]{1,0:T(8,128)S(1)}, u32[]{:S(2)}, u32[]{:S(2)}) %collective-permute-start.1) | collective-permute-done | bytes 16416 | tf_op jit(solution)/shard_map/ppermute | solution.py:226
  17.5 0.0 copy-start.2
  17.5 0.7 %copy-done.2 = f32[512]{0:T(512)S(1)} copy-done((f32[512]{0:T(512)S(1)}, f32[512]{0:T(512)}, u32[]{:S(2)}) %copy-start.2) | copy-done | bytes 2072
  18.2 1.6 %shard_map.70 = (f32[8,512]{1,0:T(8,128)S(1)}, f32[8,640]{1,0:T(8,128)S(1)}) custom-call(f32[8,512]{1,0:T(8,128)S(1)} %get-tuple-element.14.refs_0_, f32[8,512]{1,0:T(8,128)S(1)} %collective-permute-done.1.refs_1_, f32[1,512]{1,0:T(1,128)S(1)} %bitcast.9, s32[1,4096]{1,0:T(1,128)S(1)} %bitcast.5, bf16[512,4096]{1,0:T(8,128)(2,1)S(1)} %get-tuple-element.15.refs_4_.refs_5_, ...), custom_call_target="tpu_custom_call" | custom-call | tf_op jit(solution)/shard_map/pallas_call | solution.py:207
  19.8 0.1 collective-permute-start.4
  19.9 2.1 %collective-permute-start.3 = (f32[8,640]{1,0:T(8,128)S(1)}, f32[8,640]{1,0:T(8,128)S(1)}, u32[]{:S(2)}, u32[]{:S(2)}) collective-permute-start(f32[8,640]{1,0:T(8,128)S(1)} %get-tuple-element.17), channel_id=1, source_target_pairs={{0,2},{1,3},{2,0},{3,1},{4,6},{5,7},{6,4},{7,5},{8,10},{9,11},{10,... | collective-permute-start | bytes 61448 | tf_op jit(solution)/shard_map/ppermute | solution.py:226
  22.0 0.0 collective-permute-start.2
  22.0 1.0 %collective-permute-done.4 = f32[8,640]{1,0:T(8,128)S(1)} collective-permute-done((f32[8,640]{1,0:T(8,128)S(1)}, f32[8,640]{1,0:T(8,128)S(1)}, u32[]{:S(2)}, u32[]{:S(2)}) %collective-permute-start.4) | collective-permute-done | bytes 20512 | tf_op jit(solution)/shard_map/ppermute | solution.py:226
  23.1 0.8 %collective-permute-done.3 = f32[8,640]{1,0:T(8,128)S(1)} collective-permute-done((f32[8,640]{1,0:T(8,128)S(1)}, f32[8,640]{1,0:T(8,128)S(1)}, u32[]{:S(2)}, u32[]{:S(2)}) %collective-permute-start.3) | collective-permute-done | bytes 20512 | tf_op jit(solution)/shard_map/ppermute | solution.py:226
  23.9 0.0 collective-permute-done.2
  23.9 0.0 copy-start.3
  23.9 4.0 %collective-permute-start.7 = (f32[8,640]{1,0:T(8,128)S(1)}, f32[8,640]{1,0:T(8,128)S(1)}, u32[]{:S(2)}, u32[]{:S(2)}) collective-permute-start(f32[8,640]{1,0:T(8,128)S(1)} %add_add_fusion.1.refs_0_), channel_id=1, source_target_pairs={{0,12},{1,13},{2,14},{3,15},{4,8},{5,9},{6,10},{7,11},{8,4},{9,5},... | collective-permute-start | bytes 61448 | tf_op jit(solution)/shard_map/ppermute | solution.py:226
  27.9 0.0 collective-permute-start.6
  27.9 0.6 %collective-permute-start.5 = (f32[8,640]{1,0:T(8,128)S(1)}, f32[8,640]{1,0:T(8,128)S(1)}, u32[]{:S(2)}, u32[]{:S(2)}) collective-permute-start(f32[8,640]{1,0:T(8,128)S(1)} %add_add_fusion.1.refs_0_), channel_id=1, source_target_pairs={{0,4},{1,5},{2,6},{3,7},{4,0},{5,1},{6,2},{7,3},{8,12},{9,13},{10,... | collective-permute-start | bytes 61448 | tf_op jit(solution)/shard_map/ppermute | solution.py:226
  28.6 1.1 %collective-permute-done.7.refs_3_ = f32[8,640]{1,0:T(8,128)S(1)} collective-permute-done((f32[8,640]{1,0:T(8,128)S(1)}, f32[8,640]{1,0:T(8,128)S(1)}, u32[]{:S(2)}, u32[]{:S(2)}) %collective-permute-start.7) | collective-permute-done | bytes 20512 | tf_op jit(solution)/shard_map/ppermute | solution.py:226
  29.7 2.9 %collective-permute-done.6.refs_2_ = f32[8,640]{1,0:T(8,128)S(1)} collective-permute-done((f32[8,640]{1,0:T(8,128)S(1)}, f32[8,640]{1,0:T(8,128)S(1)}, u32[]{:S(2)}, u32[]{:S(2)}) %collective-permute-start.6) | collective-permute-done | bytes 20512 | tf_op jit(solution)/shard_map/ppermute | solution.py:226
  32.6 0.0 collective-permute-done.5.refs_1_
  32.6 2.5 %shard_map.71 = (f32[8,640]{1,0:T(8,128)S(1)}, f32[8,640]{1,0:T(8,128)S(1)}) custom-call(f32[8,640]{1,0:T(8,128)S(1)} %add_add_fusion.1.refs_0_, f32[8,640]{1,0:T(8,128)S(1)} %collective-permute-done.5.refs_1_, f32[8,640]{1,0:T(8,128)S(1)} %collective-permute-done.6.refs_2_, f32[8,640]{1,0:T(8,128)S(1)} %collective-permute-done.7.refs_3_, ...), custom_call_target="tpu_custom_call" | custom-call | tf_op jit(solution)/shard_map/pallas_call | solution.py:207
  35.2 1.5 %collective-permute-start.8 = (f32[8,640]{1,0:T(8,128)S(1)}, f32[8,640]{1,0:T(8,128)S(1)}, u32[]{:S(2)}, u32[]{:S(2)}) collective-permute-start(f32[8,640]{1,0:T(8,128)S(1)} %get-tuple-element.18.refs_0_), channel_id=1, source_target_pairs={{0,16},{16,0},{1,17},{17,1},{2,18},{18,2},{3,19},{19,3},{4,20},{20... | collective-permute-start | bytes 61448 | tf_op jit(solution)/shard_map/ppermute | solution.py:226
  36.7 2.3 %collective-permute-done.8.refs_1_ = f32[8,640]{1,0:T(8,128)S(1)} collective-permute-done((f32[8,640]{1,0:T(8,128)S(1)}, f32[8,640]{1,0:T(8,128)S(1)}, u32[]{:S(2)}, u32[]{:S(2)}) %collective-permute-start.8) | collective-permute-done | bytes 20512 | tf_op jit(solution)/shard_map/ppermute | solution.py:226
  39.0 0.0 copy-done.3
  39.0 1.6 %shard_map.72 = (f32[8,512]{1,0:T(8,128)S(1)}, f32[8,128]{1,0:T(8,128)S(1)}, f32[8,640]{1,0:T(8,128)S(1)}) custom-call(f32[8,640]{1,0:T(8,128)S(1)} %get-tuple-element.18.refs_0_, f32[8,640]{1,0:T(8,128)S(1)} %collective-permute-done.8.refs_1_, f32[1,512]{1,0:T(1,128)S(1)} %bitcast.10, s32[1,4096]{1,0:T(1,128)S(1)} %bitcast.7, ...), custom_call_target="tpu_custom_call" | custom-call | tf_op jit(solution)/shard_map/pallas_call | solution.py:207
  40.6 0.1 collective-permute-start.11
  40.7 1.6 %collective-permute-start.10 = (f32[8,640]{1,0:T(8,128)S(1)}, f32[8,640]{1,0:T(8,128)S(1)}, u32[]{:S(2)}, u32[]{:S(2)}) collective-permute-start(f32[8,640]{1,0:T(8,128)S(1)} %get-tuple-element.21), channel_id=1, source_target_pairs={{0,2},{1,3},{2,0},{3,1},{4,6},{5,7},{6,4},{7,5},{8,10},{9,11},{10,... | collective-permute-start | bytes 61448 | tf_op jit(solution)/shard_map/ppermute | solution.py:226
  42.3 0.3 collective-permute-start.9
  42.5 1.5 %collective-permute-done.11 = f32[8,640]{1,0:T(8,128)S(1)} collective-permute-done((f32[8,640]{1,0:T(8,128)S(1)}, f32[8,640]{1,0:T(8,128)S(1)}, u32[]{:S(2)}, u32[]{:S(2)}) %collective-permute-start.11) | collective-permute-done | bytes 20512 | tf_op jit(solution)/shard_map/ppermute | solution.py:226
  44.0 0.5 collective-permute-done.10
  44.5 0.0 collective-permute-done.9
  44.6 1.5 %collective-permute-start.14 = (f32[8,640]{1,0:T(8,128)S(1)}, f32[8,640]{1,0:T(8,128)S(1)}, u32[]{:S(2)}, u32[]{:S(2)}) collective-permute-start(f32[8,640]{1,0:T(8,128)S(1)} %add_add_fusion.refs_0_), channel_id=1, source_target_pairs={{0,12},{1,13},{2,14},{3,15},{4,8},{5,9},{6,10},{7,11},{8,4},{9,5},... | collective-permute-start | bytes 61448 | tf_op jit(solution)/shard_map/ppermute | solution.py:226
  46.1 0.6 %collective-permute-start.13 = (f32[8,640]{1,0:T(8,128)S(1)}, f32[8,640]{1,0:T(8,128)S(1)}, u32[]{:S(2)}, u32[]{:S(2)}) collective-permute-start(f32[8,640]{1,0:T(8,128)S(1)} %add_add_fusion.refs_0_), channel_id=1, source_target_pairs={{0,8},{1,9},{2,10},{3,11},{4,12},{5,13},{6,14},{7,15},{8,0},{9,1},... | collective-permute-start | bytes 61448 | tf_op jit(solution)/shard_map/ppermute | solution.py:226
  46.7 2.3 %collective-permute-start.12 = (f32[8,640]{1,0:T(8,128)S(1)}, f32[8,640]{1,0:T(8,128)S(1)}, u32[]{:S(2)}, u32[]{:S(2)}) collective-permute-start(f32[8,640]{1,0:T(8,128)S(1)} %add_add_fusion.refs_0_), channel_id=1, source_target_pairs={{0,4},{1,5},{2,6},{3,7},{4,0},{5,1},{6,2},{7,3},{8,12},{9,13},{10,... | collective-permute-start | bytes 61448 | tf_op jit(solution)/shard_map/ppermute | solution.py:226
  49.0 1.2 %collective-permute-done.14.refs_3_ = f32[8,640]{1,0:T(8,128)S(1)} collective-permute-done((f32[8,640]{1,0:T(8,128)S(1)}, f32[8,640]{1,0:T(8,128)S(1)}, u32[]{:S(2)}, u32[]{:S(2)}) %collective-permute-start.14) | collective-permute-done | bytes 20512 | tf_op jit(solution)/shard_map/ppermute | solution.py:226
  50.2 0.6 collective-permute-done.13.refs_2_
  50.8 0.2 collective-permute-done.12.refs_1_
  51.0 2.6 %shard_map.73 = (f32[8,128]{1,0:T(8,128)S(1)}, f32[8,640]{1,0:T(8,128)S(1)}) custom-call(f32[8,640]{1,0:T(8,128)S(1)} %add_add_fusion.refs_0_, f32[8,640]{1,0:T(8,128)S(1)} %collective-permute-done.12.refs_1_, f32[8,640]{1,0:T(8,128)S(1)} %collective-permute-done.13.refs_2_, f32[8,640]{1,0:T(8,128)S(1)} %collective-permute-done.14.refs_3_, ...), custom_call_target="tpu_custom_call" | custom-call | tf_op jit(solution)/shard_map/pallas_call | solution.py:207
  53.5 1.6 %collective-permute-start.15 = (f32[8,640]{1,0:T(8,128)S(1)}, f32[8,640]{1,0:T(8,128)S(1)}, u32[]{:S(2)}, u32[]{:S(2)}) collective-permute-start(f32[8,640]{1,0:T(8,128)S(1)} %get-tuple-element.22.refs_0_), channel_id=1, source_target_pairs={{0,16},{16,0},{1,17},{17,1},{2,18},{18,2},{3,19},{19,3},{4,20},{20... | collective-permute-start | bytes 61448 | tf_op jit(solution)/shard_map/ppermute | solution.py:226
  55.1 2.3 %collective-permute-done.15.refs_1_ = f32[8,640]{1,0:T(8,128)S(1)} collective-permute-done((f32[8,640]{1,0:T(8,128)S(1)}, f32[8,640]{1,0:T(8,128)S(1)}, u32[]{:S(2)}, u32[]{:S(2)}) %collective-permute-start.15) | collective-permute-done | bytes 20512 | tf_op jit(solution)/shard_map/ppermute | solution.py:226
  57.4 0.8 %shard_map.74 = (f32[8,512]{1,0:T(8,128)}, f32[8,512]{1,0:T(8,128)}) custom-call(f32[8,640]{1,0:T(8,128)S(1)} %get-tuple-element.22.refs_0_, f32[8,640]{1,0:T(8,128)S(1)} %collective-permute-done.15.refs_1_, f32[1,512]{1,0:T(1,128)S(1)} %bitcast.11, f32[8,512]{1,0:T(8,128)S(1)} %get-tuple-element.19.refs_6_.refs_3_, f32[8,512]{1,0:T(8,128)S(1)} %get-tuple-element.23.refs_4_, ...), custom_call_target="tpu_custom_call" | custom-call | tf_op jit(solution)/shard_map/pallas_call | solution.py:207
  (2 shorter events, 0.0 us)
Async XLA Ops:
  1.3 1.0 %copy-start = (bf16[64,4096]{1,0:T(8,128)(2,1)S(1)}, bf16[64,4096]{1,0:T(8,128)(2,1)}, u32[]{:S(2)}) copy-start(bf16[64,4096]{1,0:T(8,128)(2,1)} %feat_ref.3) | copy-start | bytes 1572868
  3.2 5.2 %collective-permute-start = (bf16[64,512]{1,0:T(8,128)(2,1)S(1)}, bf16[64,512]{1,0:T(8,128)(2,1)S(1)}, u32[]{:S(2)}, u32[]{:S(2)}) collective-permute-start(bf16[64,512]{1,0:T(8,128)(2,1)S(1)} %shard_map.68.refs_0_), channel_id=1, source_target_pairs={{0,16},{16,0},{1,17},{17,1},{2,18},{18,2},{3,19},{19,3},{4,20},{20... | collective-permute-start | bytes 196616 | tf_op jit(solution)/shard_map/ppermute | solution.py:226
  8.5 0.7 %copy-start.1 = (s32[4096]{0:T(1024)S(1)}, s32[4096]{0:T(1024)}, u32[]{:S(2)}) copy-start(s32[4096]{0:T(1024)} %param.7) | copy-start | bytes 49156
  9.2 0.7 %copy-start.4 = (f32[4096]{0:T(1024)S(1)}, f32[4096]{0:T(1024)}, u32[]{:S(2)}) copy-start(f32[4096]{0:T(1024)} %param.6) | copy-start | bytes 49156
  13.8 3.8 %collective-permute-start.1 = (f32[8,512]{1,0:T(8,128)S(1)}, f32[8,512]{1,0:T(8,128)S(1)}, u32[]{:S(2)}, u32[]{:S(2)}) collective-permute-start(f32[8,512]{1,0:T(8,128)S(1)} %get-tuple-element.14.refs_0_), channel_id=1, source_target_pairs={{0,16},{16,0},{1,17},{17,1},{2,18},{18,2},{3,19},{19,3},{4,20},{20... | collective-permute-start | bytes 49160 | tf_op jit(solution)/shard_map/ppermute | solution.py:226
  17.5 0.7 %copy-start.2 = (f32[512]{0:T(512)S(1)}, f32[512]{0:T(512)}, u32[]{:S(2)}) copy-start(f32[512]{0:T(512)} %param.9) | copy-start | bytes 6148
  19.8 3.3 %collective-permute-start.4 = (f32[8,640]{1,0:T(8,128)S(1)}, f32[8,640]{1,0:T(8,128)S(1)}, u32[]{:S(2)}, u32[]{:S(2)}) collective-permute-start(f32[8,640]{1,0:T(8,128)S(1)} %get-tuple-element.17), channel_id=1, source_target_pairs={{0,3},{1,2},{2,1},{3,0},{4,7},{5,6},{6,5},{7,4},{8,11},{9,10},{10,... | collective-permute-start | bytes 61448 | tf_op jit(solution)/shard_map/ppermute | solution.py:226
  19.9 4.0 %collective-permute-start.3 = (f32[8,640]{1,0:T(8,128)S(1)}, f32[8,640]{1,0:T(8,128)S(1)}, u32[]{:S(2)}, u32[]{:S(2)}) collective-permute-start(f32[8,640]{1,0:T(8,128)S(1)} %get-tuple-element.17), channel_id=1, source_target_pairs={{0,2},{1,3},{2,0},{3,1},{4,6},{5,7},{6,4},{7,5},{8,10},{9,11},{10,... | collective-permute-start | bytes 61448 | tf_op jit(solution)/shard_map/ppermute | solution.py:226
  22.0 1.9 %collective-permute-start.2 = (f32[8,640]{1,0:T(8,128)S(1)}, f32[8,640]{1,0:T(8,128)S(1)}, u32[]{:S(2)}, u32[]{:S(2)}) collective-permute-start(f32[8,640]{1,0:T(8,128)S(1)} %get-tuple-element.17), channel_id=1, source_target_pairs={{0,1},{1,0},{2,3},{3,2},{4,5},{5,4},{6,7},{7,6},{8,9},{9,8},{10,11... | collective-permute-start | bytes 61448 | tf_op jit(solution)/shard_map/ppermute | solution.py:226
  23.9 15.1 %copy-start.3 = (f32[512]{0:T(512)S(1)}, f32[512]{0:T(512)}, u32[]{:S(2)}) copy-start(f32[512]{0:T(512)} %param.9) | copy-start | bytes 6148
  23.9 5.8 %collective-permute-start.7 = (f32[8,640]{1,0:T(8,128)S(1)}, f32[8,640]{1,0:T(8,128)S(1)}, u32[]{:S(2)}, u32[]{:S(2)}) collective-permute-start(f32[8,640]{1,0:T(8,128)S(1)} %add_add_fusion.1.refs_0_), channel_id=1, source_target_pairs={{0,12},{1,13},{2,14},{3,15},{4,8},{5,9},{6,10},{7,11},{8,4},{9,5},... | collective-permute-start | bytes 61448 | tf_op jit(solution)/shard_map/ppermute | solution.py:226
  27.9 4.7 %collective-permute-start.6 = (f32[8,640]{1,0:T(8,128)S(1)}, f32[8,640]{1,0:T(8,128)S(1)}, u32[]{:S(2)}, u32[]{:S(2)}) collective-permute-start(f32[8,640]{1,0:T(8,128)S(1)} %add_add_fusion.1.refs_0_), channel_id=1, source_target_pairs={{0,8},{1,9},{2,10},{3,11},{4,12},{5,13},{6,14},{7,15},{8,0},{9,1},... | collective-permute-start | bytes 61448 | tf_op jit(solution)/shard_map/ppermute | solution.py:226
  27.9 4.7 %collective-permute-start.5 = (f32[8,640]{1,0:T(8,128)S(1)}, f32[8,640]{1,0:T(8,128)S(1)}, u32[]{:S(2)}, u32[]{:S(2)}) collective-permute-start(f32[8,640]{1,0:T(8,128)S(1)} %add_add_fusion.1.refs_0_), channel_id=1, source_target_pairs={{0,4},{1,5},{2,6},{3,7},{4,0},{5,1},{6,2},{7,3},{8,12},{9,13},{10,... | collective-permute-start | bytes 61448 | tf_op jit(solution)/shard_map/ppermute | solution.py:226
  35.2 3.8 %collective-permute-start.8 = (f32[8,640]{1,0:T(8,128)S(1)}, f32[8,640]{1,0:T(8,128)S(1)}, u32[]{:S(2)}, u32[]{:S(2)}) collective-permute-start(f32[8,640]{1,0:T(8,128)S(1)} %get-tuple-element.18.refs_0_), channel_id=1, source_target_pairs={{0,16},{16,0},{1,17},{17,1},{2,18},{18,2},{3,19},{19,3},{4,20},{20... | collective-permute-start | bytes 61448 | tf_op jit(solution)/shard_map/ppermute | solution.py:226
  40.6 3.4 %collective-permute-start.11 = (f32[8,640]{1,0:T(8,128)S(1)}, f32[8,640]{1,0:T(8,128)S(1)}, u32[]{:S(2)}, u32[]{:S(2)}) collective-permute-start(f32[8,640]{1,0:T(8,128)S(1)} %get-tuple-element.21), channel_id=1, source_target_pairs={{0,3},{1,2},{2,1},{3,0},{4,7},{5,6},{6,5},{7,4},{8,11},{9,10},{10,... | collective-permute-start | bytes 61448 | tf_op jit(solution)/shard_map/ppermute | solution.py:226
  40.7 3.8 %collective-permute-start.10 = (f32[8,640]{1,0:T(8,128)S(1)}, f32[8,640]{1,0:T(8,128)S(1)}, u32[]{:S(2)}, u32[]{:S(2)}) collective-permute-start(f32[8,640]{1,0:T(8,128)S(1)} %get-tuple-element.21), channel_id=1, source_target_pairs={{0,2},{1,3},{2,0},{3,1},{4,6},{5,7},{6,4},{7,5},{8,10},{9,11},{10,... | collective-permute-start | bytes 61448 | tf_op jit(solution)/shard_map/ppermute | solution.py:226
  42.3 2.3 %collective-permute-start.9 = (f32[8,640]{1,0:T(8,128)S(1)}, f32[8,640]{1,0:T(8,128)S(1)}, u32[]{:S(2)}, u32[]{:S(2)}) collective-permute-start(f32[8,640]{1,0:T(8,128)S(1)} %get-tuple-element.21), channel_id=1, source_target_pairs={{0,1},{1,0},{2,3},{3,2},{4,5},{5,4},{6,7},{7,6},{8,9},{9,8},{10,11... | collective-permute-start | bytes 61448 | tf_op jit(solution)/shard_map/ppermute | solution.py:226
  44.6 5.7 %collective-permute-start.14 = (f32[8,640]{1,0:T(8,128)S(1)}, f32[8,640]{1,0:T(8,128)S(1)}, u32[]{:S(2)}, u32[]{:S(2)}) collective-permute-start(f32[8,640]{1,0:T(8,128)S(1)} %add_add_fusion.refs_0_), channel_id=1, source_target_pairs={{0,12},{1,13},{2,14},{3,15},{4,8},{5,9},{6,10},{7,11},{8,4},{9,5},... | collective-permute-start | bytes 61448 | tf_op jit(solution)/shard_map/ppermute | solution.py:226
  46.1 4.7 %collective-permute-start.13 = (f32[8,640]{1,0:T(8,128)S(1)}, f32[8,640]{1,0:T(8,128)S(1)}, u32[]{:S(2)}, u32[]{:S(2)}) collective-permute-start(f32[8,640]{1,0:T(8,128)S(1)} %add_add_fusion.refs_0_), channel_id=1, source_target_pairs={{0,8},{1,9},{2,10},{3,11},{4,12},{5,13},{6,14},{7,15},{8,0},{9,1},... | collective-permute-start | bytes 61448 | tf_op jit(solution)/shard_map/ppermute | solution.py:226
  46.7 4.3 %collective-permute-start.12 = (f32[8,640]{1,0:T(8,128)S(1)}, f32[8,640]{1,0:T(8,128)S(1)}, u32[]{:S(2)}, u32[]{:S(2)}) collective-permute-start(f32[8,640]{1,0:T(8,128)S(1)} %add_add_fusion.refs_0_), channel_id=1, source_target_pairs={{0,4},{1,5},{2,6},{3,7},{4,0},{5,1},{6,2},{7,3},{8,12},{9,13},{10,... | collective-permute-start | bytes 61448 | tf_op jit(solution)/shard_map/ppermute | solution.py:226
  53.5 3.8 %collective-permute-start.15 = (f32[8,640]{1,0:T(8,128)S(1)}, f32[8,640]{1,0:T(8,128)S(1)}, u32[]{:S(2)}, u32[]{:S(2)}) collective-permute-start(f32[8,640]{1,0:T(8,128)S(1)} %get-tuple-element.22.refs_0_), channel_id=1, source_target_pairs={{0,16},{16,0},{1,17},{17,1},{2,18},{18,2},{3,19},{19,3},{4,20},{20... | collective-permute-start | bytes 61448 | tf_op jit(solution)/shard_map/ppermute | solution.py:226

commit v2 on v1

--- a/solution.py
+++ b/solution.py
@@ -38,12 +38,16 @@
 
 
 def total_of(refs):
-    return pair_total([ref[...] for ref in refs])
-
-
-def slot_mask(slots_ref, begin):
-    row = lax.broadcasted_iota(jnp.int32, (SLOTS, CHUNK), 0)
-    return slots_ref[:, begin : begin + CHUNK] == row
+    return pair_total([ref[i] for ref in refs for i in range(ref.shape[0])])
+
+
+def slot_mask(small_ref, begin):
+    row = lax.broadcasted_iota(jnp.int32, (SLOTS, CHUNK), 0).astype(f32)
+    return small_ref[:, begin : begin + CHUNK] == row
+
+
+def scale_of(small_ref, count):
+    return small_ref[:, -2 * count : -count]
 
 
 def with_norms(feat, feat_first):
@@ -58,20 +62,20 @@
     return jnp.concatenate([feat, extra.astype(bf16)], axis=0)
 
 
-def pick_body(feat_ref, idx_ref, out_ref):
+def pick_body(feat_ref, small_ref, out_ref):
     total = jnp.zeros(out_ref.shape, f32)
     count = out_ref.shape[1]
+    local_idx = small_ref[:, -count:]
     for begin in range(0, feat_ref.shape[1], CHUNK):
-        row = lax.broadcasted_iota(jnp.int32, (CHUNK, count), 0)
-        hit = row == (idx_ref[...] - begin)
-        one_hot = jnp.where(hit, 1.0, 0.0).astype(bf16)
+        row = lax.broadcasted_iota(jnp.int32, (CHUNK, count), 0).astype(f32)
+        one_hot = jnp.where(row == local_idx - float(begin), 1.0, 0.0).astype(bf16)
         total += jnp.dot(
             feat_ref[:, begin : begin + CHUNK], one_hot, preferred_element_type=f32
         )
     out_ref[...] = total.astype(bf16)
 
 
-def kernel_body(parts, feat_ref, prices_ref, slots_ref, *refs):
+def kernel_body(parts, feat_ref, small_ref, *refs):
     center_refs, (high_ref, low_ref, out_ref) = refs[:parts], refs[parts:]
     center = with_norms(total_of(center_refs), True)
     count = center.shape[1]
@@ -87,7 +91,9 @@
         low = (value - high.astype(f32)).astype(bf16)
         high_ref[:, here] = high
         low_ref[:, here] = low
-        weight = stack3(jnp.where(slot_mask(slots_ref, begin), prices_ref[:, here], 0.0))
+        rows = feat_ref.shape[1]
+        price = small_ref[:, rows + begin : rows + begin + CHUNK]
+        weight = stack3(jnp.where(slot_mask(small_ref, begin), price, 0.0))
         for piece in (high, low):
             total += lax.dot_general(
                 weight, piece, (((1,), (1,)), ((), ())), preferred_element_type=f32
@@ -95,13 +101,13 @@
     out_ref[...] = unstack3(total)
 
 
-def apply_rows(scaled, high_ref, low_ref, slots_ref, out_ref):
+def apply_rows(scaled, high_ref, low_ref, small_ref, out_ref):
     stacked = stack3(scaled)
     for turn, begin in enumerate(range(0, high_ref.shape[1], CHUNK)):
         here = slice(begin, begin + CHUNK)
         value = jnp.dot(stacked, high_ref[:, here], preferred_element_type=f32)
         value += jnp.dot(stacked, low_ref[:, here], preferred_element_type=f32)
-        own = jnp.where(slot_mask(slots_ref, begin), unstack3(value), 0.0)
+        own = jnp.where(slot_mask(small_ref, begin), unstack3(value), 0.0)
         out_ref[turn : turn + 1, 0:CHUNK] = jnp.sum(own, axis=0, keepdims=True)
 
 
@@ -128,33 +134,33 @@
 
 def first_apply_body(parts, scale_over_root, *refs):
     first_refs = refs[:parts]
-    scale_ref, slots_ref, high_ref, low_ref, target_ref, out_ref = refs[parts:]
-    scale = scale_ref[...]
+    small_ref, high_ref, low_ref, target_ref, out_ref = refs[parts:]
+    scale = scale_of(small_ref, target_ref.shape[1])
     target = scale * total_of(first_refs) * scale_over_root
     target_ref[...] = target
     out_ref[:, CHUNK:] = jnp.broadcast_to(row_sum(target * target), (SLOTS, EXTRA))
-    apply_rows(scale * target, high_ref, low_ref, slots_ref, out_ref)
+    apply_rows(scale * target, high_ref, low_ref, small_ref, out_ref)
 
 
 def first_fold_body(parts, *refs):
     row_refs = refs[:parts]
-    slots_ref, high_ref, low_ref, rows_ref, out_ref = refs[parts:]
+    small_ref, high_ref, low_ref, rows_ref, out_ref = refs[parts:]
     rows_ref[...] = total_of(row_refs)
 
     def row_weights(turn, begin):
         value = rows_ref[turn : turn + 1, 0:CHUNK]
-        return jnp.where(slot_mask(slots_ref, begin), value, 0.0)
+        return jnp.where(slot_mask(small_ref, begin), value, 0.0)
 
     fold_rows(row_weights, high_ref, low_ref, out_ref)
 
 
 def second_apply_body(parts, inv_rows, *refs):
     fold_refs = refs[:parts]
-    (scale_ref, slots_ref, high_ref, low_ref, target_ref, rows_ref,
+    (small_ref, high_ref, low_ref, target_ref, rows_ref,
      residual_ref, step_ref, out_ref) = refs[parts:]
-    count = scale_ref.shape[1]
+    count = target_ref.shape[1]
     folded = total_of(fold_refs)
-    scale = scale_ref[...]
+    scale = scale_of(small_ref, count)
     target = target_ref[...]
     norm = rows_ref[:, CHUNK : CHUNK + 1]
     applied = scale * folded[:, 0:count] * inv_rows + RIDGE * target
@@ -166,28 +172,28 @@
     out_ref[:, CHUNK:] = jnp.where(
         lane == 0, row_sum(residual * residual), row_sum(residual * target)
     )
-    apply_rows(scale * residual, high_ref, low_ref, slots_ref, out_ref)
+    apply_rows(scale * residual, high_ref, low_ref, small_ref, out_ref)
 
 
 def second_fold_body(parts, *refs):
     row_refs = refs[:parts]
-    slots_ref, high_ref, low_ref, rows_ref, sums_ref, out_ref = refs[parts:]
+    small_ref, high_ref, low_ref, rows_ref, sums_ref, out_ref = refs[parts:]
     latest = total_of(row_refs)
     sums_ref[...] = latest[:, CHUNK:]
     ratio = latest[:, CHUNK : CHUNK + 1] / rows_ref[:, CHUNK : CHUNK + 1]
 
     def row_weights(turn, begin):
         value = latest[turn : turn + 1, 0:CHUNK] + ratio * rows_ref[turn : turn + 1, 0:CHUNK]
-        return jnp.where(slot_mask(slots_ref, begin), value, 0.0)
+        return jnp.where(slot_mask(small_ref, begin), value, 0.0)
 
     fold_rows(row_weights, high_ref, low_ref, out_ref)
 
 
 def finish_body(parts, inv_rows, *refs):
     fold_refs = refs[:parts]
-    (scale_ref, target_ref, residual_ref, step_ref, rows_ref, sums_ref,
+    (small_ref, target_ref, residual_ref, step_ref, rows_ref, sums_ref,
      coefficients_ref, out_ref) = refs[parts:]
-    count = scale_ref.shape[1]
+    count = target_ref.shape[1]
     folded = total_of(fold_refs)
     target = target_ref[...]
     residual = residual_ref[...]
@@ -197,7 +203,7 @@
     ratio = norm / first_norm
     direction = residual + ratio * target
     square = norm + 2.0 * ratio * cross + ratio * ratio * first_norm
-    applied = scale_ref[...] * folded[:, 0:count] * inv_rows + RIDGE * direction
+    applied = scale_of(small_ref, count) * folded[:, 0:count] * inv_rows + RIDGE * direction
     step = norm / (folded[:, count : count + 1] * inv_rows + RIDGE * square)
     coefficients_ref[...] = step_ref[:, 0:1] * target + step * direction
     out_ref[...] = residual - step * applied
@@ -219,13 +225,24 @@
     stride = 1
     while stride < size:
         value = pair_total(parts)
+        span = min(4, size // stride)
         parts = [value]
-        span = min(4, size // stride)
-        for offset in range(1, span):
-            pairs = [(i, i ^ (offset * stride)) for i in range(size)]
+        if span == 2:
+            pairs = [(i, i ^ stride) for i in range(size)]
             parts.append(lax.ppermute(value, axis, pairs))
+        else:
+            groups = [
+                [first + offset * stride for offset in range(span)]
+                for first in range(size)
+                if (first // stride) % span == 0
+            ]
+            copies = jnp.broadcast_to(value[None], (span, *value.shape))
+            got = lax.all_to_all(copies, axis, 0, 0, axis_index_groups=groups, tiled=True)
+            parts = [got[i] for i in range(span)]
         stride *= span
-    return parts
+    if len(parts) == 4:
+        return [got]
+    return [part[None] for part in parts]
 
 
 def shaped(shape, dtype=f32):
@@ -236,20 +253,20 @@
     row_count = features.shape[1]
     count = center_idx.shape[0]
     all_rows = row_count * lax.axis_size("dp")
-    local_idx = (center_idx - lax.axis_index("dp") * row_count).reshape(1, count)
-    prices = prices.reshape(1, row_count)
-    slots = slots.reshape(1, row_count)
-    scale = center_scale.reshape(1, count)
+    local_idx = center_idx - lax.axis_index("dp") * row_count
+    small = jnp.concatenate(
+        [slots.astype(f32), prices, center_scale, local_idx.astype(f32)]
+    ).reshape(1, -1)
     turns = row_count // CHUNK
     part = functools.partial
 
-    picked = call(pick_body, shaped((features.shape[0], count), bf16), features, local_idx)
+    picked = call(pick_body, shaped((features.shape[0], count), bf16), features, small)
     centers = exchange(picked, "dp")
     block = shaped((count, row_count), bf16)
     high, low, first = call(
         part(kernel_body, len(centers)),
         (block, block, shaped((SLOTS, count))),
-        features, prices, slots, *centers,
+        features, small, *centers,
     )
     firsts = exchange(first, "dp")
     row_shape = shaped((turns, CHUNK + EXTRA))
@@ -259,29 +276,29 @@
     target, rows = call(
         part(first_apply_body, len(firsts), 1.0 / math.sqrt(all_rows)),
         (vector, row_shape),
-        *firsts, scale, slots, high, low,
+        *firsts, small, high, low,
     )
     rows = exchange(rows, "centers")
     rows, folded = call(
-        part(first_fold_body, len(rows)), (row_shape, fold_shape), *rows, slots, high, low
+        part(first_fold_body, len(rows)), (row_shape, fold_shape), *rows, small, high, low
     )
     folds = exchange(folded, "dp")
     residual, step, latest = call(
         part(second_apply_body, len(folds), 1.0 / all_rows),
         (vector, narrow, row_shape),
-        *folds, scale, slots, high, low, target, rows,
+        *folds, small, high, low, target, rows,
     )
     latest = exchange(latest, "centers")
     sums, folded = call(
         part(second_fold_body, len(latest)),
         (narrow, fold_shape),
-        *latest, slots, high, low, rows,
+        *latest, small, high, low, rows,
     )
     folds = exchange(folded, "dp")
     return call(
         part(finish_body, len(folds), 1.0 / all_rows),
         (vector, vector),
-        *folds, scale, target, residual, step, rows, sums,
+        *folds, small, target, residual, step, rows, sums,
     )
 
 

time: 58.5 us -> 67.4 us (1.15)
  blocking collectives: 0 us -> 32.5 us
  starting transfers between devices: 21.4 us -> 8.14 us
  waiting for transfers between devices: 18.4 us -> 8.55 us
  local copies, waits for them, and re-layouts: 3.16 us -> 1.07 us
  other arithmetic: 0.7 us -> 2.16 us
    all_to_all x0 -> x4, blocking collectives: none -> 32.5 us  [exchange(): lax.all_to_all(copies, axis, 0, 0, axis_index_groups=groups, tiled=True)]
    ppermute x16 -> x4, starting transfers between devices: 21.4 us -> 8.14 us  [exchange(): parts.append(lax.ppermute(value, axis, pairs))]
    ppermute x16 -> x4, waiting for transfers between devices: 18.4 us -> 8.55 us  [exchange(): parts.append(lax.ppermute(value, axis, pairs))]
    unnamed x10 -> x2, local copies, waits for them, and re-layouts: 3.16 us -> 1.04 us
    convert_element_type x0 -> x2, other arithmetic: none -> 1.41 us  [the longest x1 0.72 us: per_device(): slots.astype(f32)]
    concatenate x0 -> x1, other arithmetic: none -> 0.74 us  [per_device(): jnp.concatenate([slots.astype(f32), prices, center_scale, local_idx.astyp...]
    sub x1 -> x0, other arithmetic: 0.69 us -> none  [per_device(): center_idx - lax.axis_index('dp') * row_count]
  transfers between devices with their start and end apart: 16 -> 4, of which waited for: 13 -> 4; matrix products, arithmetic and copies ran while one was open for 0% -> 0% of each run, Pallas kernels for 0% -> 0%
where the time goes in v2:
time: 67.4 us; the launch traced here: 66.9 us
  blocking collectives  32.5 us (48%)
  Pallas kernels  13.7 us (20%)
  waiting for transfers between devices  8.55 us (13%)
  starting transfers between devices  8.14 us (12%)
  other arithmetic  2.16 us (3%)
  local copies, waits for them, and re-layouts  1.07 us (2%)
  between operations  0.69 us (1%)
    all_to_all x4, blocking collectives, exchange(): lax.all_to_all(copies, axis, 0, 0, axis_index_groups=groups, tiled=True)  32.5 us
    pallas_call x7, Pallas kernels, call(): pl.pallas_call(body, out_shape=out_shape, in_specs=[pl.BlockSpec(memory_s...  13.7 us
    ppermute x4, waiting for transfers between devices, exchange(): parts.append(lax.ppermute(value, axis, pairs))  8.55 us
    ppermute x4, starting transfers between devices, exchange(): parts.append(lax.ppermute(value, axis, pairs))  8.14 us
  transfers between devices with their start and end apart: 4, of which 4 were waited for; matrix products, arithmetic and copies ran while one was open for 0% of the time, Pallas kernels for 0%

profile of v2, /device:TPU:0, one launch (start us, length us, event | category | flops | bytes accessed | tf_op | source)
XLA Modules:
  0.0 66.9 jit_solution(668209513984047690)
XLA Ops:
  0.6 0.7 %convert_element_type.6 = f32[4096]{0:T(1024)S(1)} convert(s32[4096]{0:T(1024)} %param.7) | non-fusion elementwise | flops 4096 | bytes 32768 | tf_op jit(solution)/shard_map/convert_element_type | solution.py:258
  1.4 0.7 %subtract_convert_fusion = f32[512]{0:T(512)S(1)} fusion(s32[512]{0:T(512)} %param.8, s32[]{:T(128)S(6)} %mul.3), kind=kLoop, calls=%fused_computation.9 | loop fusion | flops 1024 | bytes 4100 | tf_op jit(solution)/shard_map/convert_element_type | solution.py:258
  2.0 0.7 %pad_maximum_fusion = f32[9216]{0:T(1024)S(1)} fusion(f32[512]{0:T(512)S(1)} %subtract_convert_fusion, f32[512]{0:T(512)} %param.9, f32[4096]{0:T(1024)} %param.6, f32[4096]{0:T(1024)S(1)} %convert_element_type.6), kind=kLoop, calls=%fused_computation | loop fusion | flops 27648 | bytes 73728 | tf_op jit(solution)/shard_map/concatenate | solution.py:257
  2.8 0.0 copy-start
  2.8 1.0 %copy-done = bf16[64,4096]{1,0:T(8,128)(2,1)S(1)} copy-done((bf16[64,4096]{1,0:T(8,128)(2,1)S(1)}, bf16[64,4096]{1,0:T(8,128)(2,1)}, u32[]{:S(2)}) %copy-start) | copy-done | bytes 524312
  3.8 0.8 %shard_map.68 = bf16[64,512]{1,0:T(8,128)(2,1)S(1)} custom-call(bf16[64,4096]{1,0:T(8,128)(2,1)S(1)} %copy-done, f32[1,9216]{1,0:T(1,128)S(1)} %bitcast.13), custom_call_target="tpu_custom_call" | custom-call | tf_op jit(solution)/shard_map/pallas_call | solution.py:213
  4.7 3.0 %collective-permute-start = (bf16[64,512]{1,0:T(8,128)(2,1)S(1)}, bf16[64,512]{1,0:T(8,128)(2,1)S(1)}, u32[]{:S(2)}, u32[]{:S(2)}) collective-permute-start(bf16[64,512]{1,0:T(8,128)(2,1)S(1)} %shard_map.68), channel_id=1, source_target_pairs={{0,16},{16,0},{1,17},{17,1},{2,18},{18,2},{3,19},{19,3},{4,20},{20... | collective-permute-start | bytes 196616 | tf_op jit(solution)/shard_map/ppermute | solution.py:232
  7.7 2.2 %collective-permute-done = bf16[64,512]{1,0:T(8,128)(2,1)S(1)} collective-permute-done((bf16[64,512]{1,0:T(8,128)(2,1)S(1)}, bf16[64,512]{1,0:T(8,128)(2,1)S(1)}, u32[]{:S(2)}, u32[]{:S(2)}) %collective-permute-start) | collective-permute-done | bytes 65568 | tf_op jit(solution)/shard_map/ppermute | solution.py:232
  9.9 3.9 %shard_map.69 = (bf16[512,4096]{1,0:T(8,128)(2,1)S(1)}, bf16[512,4096]{1,0:T(8,128)(2,1)S(1)}, f32[8,512]{1,0:T(8,128)S(1)}) custom-call(bf16[64,4096]{1,0:T(8,128)(2,1)S(1)} %copy-done, f32[1,9216]{1,0:T(1,128)S(1)} %bitcast.14, bf16[1,64,512]{2,1,0:T(8,128)(2,1)S(1)} %bitcast.20, bf16[1,64,512]{2,1,0:T(8,128)(2,1)S(1)} %bitcast.21), custom_call_target="tpu_custom_call" | custom-call | tf_op jit(solution)/shard_map/pallas_call | solution.py:213
  13.8 2.1 %collective-permute-start.1 = (f32[8,512]{1,0:T(8,128)S(1)}, f32[8,512]{1,0:T(8,128)S(1)}, u32[]{:S(2)}, u32[]{:S(2)}) collective-permute-start(f32[8,512]{1,0:T(8,128)S(1)} %get-tuple-element.14), channel_id=1, source_target_pairs={{0,16},{16,0},{1,17},{17,1},{2,18},{18,2},{3,19},{19,3},{4,20},{20... | collective-permute-start | bytes 49160 | tf_op jit(solution)/shard_map/ppermute | solution.py:232
  15.9 1.7 %collective-permute-done.1 = f32[8,512]{1,0:T(8,128)S(1)} collective-permute-done((f32[8,512]{1,0:T(8,128)S(1)}, f32[8,512]{1,0:T(8,128)S(1)}, u32[]{:S(2)}, u32[]{:S(2)}) %collective-permute-start.1) | collective-permute-done | bytes 16416 | tf_op jit(solution)/shard_map/ppermute | solution.py:232
  17.6 1.6 %shard_map.70 = (f32[8,512]{1,0:T(8,128)S(1)}, f32[8,640]{1,0:T(8,128)S(1)}) custom-call(f32[1,8,512]{2,1,0:T(8,128)S(1)} %bitcast.26, f32[1,8,512]{2,1,0:T(8,128)S(1)} %bitcast.27, f32[1,9216]{1,0:T(1,128)S(1)} %bitcast.15, bf16[512,4096]{1,0:T(8,128)(2,1)S(1)} %get-tuple-element.15.refs_3_.refs_2_, bf16[512,4096]{1,0:T(8,128)(2,1)S(1)} %get-tuple-element.16.refs_4_.refs_3_), custom_call_target="tpu_custom_call" | custom-call | tf_op jit(solution)/shard_map/pallas_call | solution.py:213
  19.1 7.3 %all_to_all.20 = f32[4,8,640]{2,1,0:T(8,128)S(1)} all-to-all(f32[4,8,640]{2,1,0:T(8,128)S(1)} %broadcast_in_dim.56), channel_id=1, replica_groups={{0,1,2,3},{4,5,6,7},{8,9,10,11},{12,13,14,15},{16,17,18,19},{20,21,22,2..., dimensions={0} | all-to-all | bytes 163840 | tf_op jit(solution)/shard_map/all_to_all | solution.py:240
  26.5 10.5 %all_to_all.21.refs_0_ = f32[4,8,640]{2,1,0:T(8,128)S(1)} all-to-all(f32[4,8,640]{2,1,0:T(8,128)S(1)} %broadcast_in_dim.58), channel_id=1, replica_groups={{0,4,8,12},{1,5,9,13},{2,6,10,14},{3,7,11,15},{16,20,24,28},{17,21,25,2..., dimensions={0} | all-to-all | bytes 163840 | tf_op jit(solution)/shard_map/all_to_all | solution.py:240
  37.0 2.5 %shard_map.71 = (f32[8,640]{1,0:T(8,128)S(1)}, f32[8,640]{1,0:T(8,128)S(1)}) custom-call(f32[4,8,640]{2,1,0:T(8,128)S(1)} %all_to_all.21.refs_0_, f32[1,9216]{1,0:T(1,128)S(1)} %bitcast.16, bf16[512,4096]{1,0:T(8,128)(2,1)S(1)} %get-tuple-element.15.refs_3_.refs_2_, bf16[512,4096]{1,0:T(8,128)(2,1)S(1)} %get-tuple-element.16.refs_4_.refs_3_), custom_call_target="tpu_custom_call" | custom-call | tf_op jit(solution)/shard_map/pallas_call | solution.py:213
  39.5 1.5 %collective-permute-start.2 = (f32[8,640]{1,0:T(8,128)S(1)}, f32[8,640]{1,0:T(8,128)S(1)}, u32[]{:S(2)}, u32[]{:S(2)}) collective-permute-start(f32[8,640]{1,0:T(8,128)S(1)} %get-tuple-element.18), channel_id=1, source_target_pairs={{0,16},{16,0},{1,17},{17,1},{2,18},{18,2},{3,19},{19,3},{4,20},{20... | collective-permute-start | bytes 61448 | tf_op jit(solution)/shard_map/ppermute | solution.py:232
  41.0 2.3 %collective-permute-done.2 = f32[8,640]{1,0:T(8,128)S(1)} collective-permute-done((f32[8,640]{1,0:T(8,128)S(1)}, f32[8,640]{1,0:T(8,128)S(1)}, u32[]{:S(2)}, u32[]{:S(2)}) %collective-permute-start.2) | collective-permute-done | bytes 20512 | tf_op jit(solution)/shard_map/ppermute | solution.py:232
  43.3 1.6 %shard_map.72 = (f32[8,512]{1,0:T(8,128)S(1)}, f32[8,128]{1,0:T(8,128)S(1)}, f32[8,640]{1,0:T(8,128)S(1)}) custom-call(f32[1,8,640]{2,1,0:T(8,128)S(1)} %bitcast.22, f32[1,8,640]{2,1,0:T(8,128)S(1)} %bitcast.23, f32[1,9216]{1,0:T(1,128)S(1)} %bitcast.17, bf16[512,4096]{1,0:T(8,128)(2,1)S(1)} %get-tuple-element.15.refs_3_.refs_2_, ...), custom_call_target="tpu_custom_call" | custom-call | tf_op jit(solution)/shard_map/pallas_call | solution.py:213
  45.0 6.6 %all_to_all.22 = f32[4,8,640]{2,1,0:T(8,128)S(1)} all-to-all(f32[4,8,640]{2,1,0:T(8,128)S(1)} %broadcast_in_dim.61), channel_id=1, replica_groups={{0,1,2,3},{4,5,6,7},{8,9,10,11},{12,13,14,15},{16,17,18,19},{20,21,22,2..., dimensions={0} | all-to-all | bytes 163840 | tf_op jit(solution)/shard_map/all_to_all | solution.py:240
  51.6 8.2 %all_to_all.23.refs_0_ = f32[4,8,640]{2,1,0:T(8,128)S(1)} all-to-all(f32[4,8,640]{2,1,0:T(8,128)S(1)} %broadcast_in_dim.63), channel_id=1, replica_groups={{0,4,8,12},{1,5,9,13},{2,6,10,14},{3,7,11,15},{16,20,24,28},{17,21,25,2..., dimensions={0} | all-to-all | bytes 163840 | tf_op jit(solution)/shard_map/all_to_all | solution.py:240
  59.7 2.6 %shard_map.73 = (f32[8,128]{1,0:T(8,128)S(1)}, f32[8,640]{1,0:T(8,128)S(1)}) custom-call(f32[4,8,640]{2,1,0:T(8,128)S(1)} %all_to_all.23.refs_0_, f32[1,9216]{1,0:T(1,128)S(1)} %bitcast.18, bf16[512,4096]{1,0:T(8,128)(2,1)S(1)} %get-tuple-element.15.refs_3_.refs_2_, bf16[512,4096]{1,0:T(8,128)(2,1)S(1)} %get-tuple-element.16.refs_4_.refs_3_, ...), custom_call_target="tpu_custom_call" | custom-call | tf_op jit(solution)/shard_map/pallas_call | solution.py:213
  62.3 1.5 %collective-permute-start.3 = (f32[8,640]{1,0:T(8,128)S(1)}, f32[8,640]{1,0:T(8,128)S(1)}, u32[]{:S(2)}, u32[]{:S(2)}) collective-permute-start(f32[8,640]{1,0:T(8,128)S(1)} %get-tuple-element.22), channel_id=1, source_target_pairs={{0,16},{16,0},{1,17},{17,1},{2,18},{18,2},{3,19},{19,3},{4,20},{20... | collective-permute-start | bytes 61448 | tf_op jit(solution)/shard_map/ppermute | solution.py:232
  63.8 2.3 %collective-permute-done.3 = f32[8,640]{1,0:T(8,128)S(1)} collective-permute-done((f32[8,640]{1,0:T(8,128)S(1)}, f32[8,640]{1,0:T(8,128)S(1)}, u32[]{:S(2)}, u32[]{:S(2)}) %collective-permute-start.3) | collective-permute-done | bytes 20512 | tf_op jit(solution)/shard_map/ppermute | solution.py:232
  66.1 0.8 %shard_map.74 = (f32[8,512]{1,0:T(8,128)}, f32[8,512]{1,0:T(8,128)}) custom-call(f32[1,8,640]{2,1,0:T(8,128)S(1)} %bitcast.24, f32[1,8,640]{2,1,0:T(8,128)S(1)} %bitcast.25, f32[1,9216]{1,0:T(1,128)S(1)} %bitcast.19, f32[8,512]{1,0:T(8,128)S(1)} %get-tuple-element.19.refs_5_.refs_3_, f32[8,512]{1,0:T(8,128)S(1)} %get-tuple-element.23.refs_4_, ...), custom_call_target="tpu_custom_call" | custom-call | tf_op jit(solution)/shard_map/pallas_call | solution.py:213
  (6 shorter events, 0.0 us)
Async XLA Ops:
  2.8 1.0 %copy-start = (bf16[64,4096]{1,0:T(8,128)(2,1)S(1)}, bf16[64,4096]{1,0:T(8,128)(2,1)}, u32[]{:S(2)}) copy-start(bf16[64,4096]{1,0:T(8,128)(2,1)} %feat_ref.3) | copy-start | bytes 1572868
  4.7 5.2 %collective-permute-start = (bf16[64,512]{1,0:T(8,128)(2,1)S(1)}, bf16[64,512]{1,0:T(8,128)(2,1)S(1)}, u32[]{:S(2)}, u32[]{:S(2)}) collective-permute-start(bf16[64,512]{1,0:T(8,128)(2,1)S(1)} %shard_map.68), channel_id=1, source_target_pairs={{0,16},{16,0},{1,17},{17,1},{2,18},{18,2},{3,19},{19,3},{4,20},{20... | collective-permute-start | bytes 196616 | tf_op jit(solution)/shard_map/ppermute | solution.py:232
  13.8 3.8 %collective-permute-start.1 = (f32[8,512]{1,0:T(8,128)S(1)}, f32[8,512]{1,0:T(8,128)S(1)}, u32[]{:S(2)}, u32[]{:S(2)}) collective-permute-start(f32[8,512]{1,0:T(8,128)S(1)} %get-tuple-element.14), channel_id=1, source_target_pairs={{0,16},{16,0},{1,17},{17,1},{2,18},{18,2},{3,19},{19,3},{4,20},{20... | collective-permute-start | bytes 49160 | tf_op jit(solution)/shard_map/ppermute | solution.py:232
  39.5 3.8 %collective-permute-start.2 = (f32[8,640]{1,0:T(8,128)S(1)}, f32[8,640]{1,0:T(8,128)S(1)}, u32[]{:S(2)}, u32[]{:S(2)}) collective-permute-start(f32[8,640]{1,0:T(8,128)S(1)} %get-tuple-element.18), channel_id=1, source_target_pairs={{0,16},{16,0},{1,17},{17,1},{2,18},{18,2},{3,19},{19,3},{4,20},{20... | collective-permute-start | bytes 61448 | tf_op jit(solution)/shard_map/ppermute | solution.py:232
  62.3 3.8 %collective-permute-start.3 = (f32[8,640]{1,0:T(8,128)S(1)}, f32[8,640]{1,0:T(8,128)S(1)}, u32[]{:S(2)}, u32[]{:S(2)}) collective-permute-start(f32[8,640]{1,0:T(8,128)S(1)} %get-tuple-element.22), channel_id=1, source_target_pairs={{0,16},{16,0},{1,17},{17,1},{2,18},{18,2},{3,19},{19,3},{4,20},{20... | collective-permute-start | bytes 61448 | tf_op jit(solution)/shard_map/ppermute | solution.py:232

commit v3 on v1

v3 whole, which is shorter than its diff:
```python
import math
from functools import partial

import jax
import jax.numpy as jnp
from jax import lax
from jax.experimental import pallas as pl
from jax.experimental.pallas import tpu as pltpu
from jax.sharding import PartitionSpec as P

SLOTS = 8
RIDGE = 0.5
CHUNK = 512
EXTRA = 128
DEPTH = 128
f32 = jnp.float32
bf16 = jnp.bfloat16
VMEM = pl.BlockSpec(memory_space=pltpu.VMEM)
HBM = pl.BlockSpec(memory_space=pltpu.HBM)


def split3(value):
    high = value.astype(bf16).astype(f32)
    rest = value - high
    mid = rest.astype(bf16).astype(f32)
    return high, mid, rest - mid


def stack3(value):
    return jnp.concatenate(split3(value), axis=0).astype(bf16)


def unstack3(value):
    return value[0:8] + (value[8:16] + value[16:24])


def pair_total(parts):
    while len(parts) > 1:
        parts = [parts[i] + parts[i + 1] for i in range(0, len(parts), 2)]
    return parts[0]


def total_of(refs):
    return pair_total([ref[...] for ref in refs])


def row_sum(value):
    return jnp.sum(value, axis=1, keepdims=True)


def slot_mask(slots):
    row = lax.broadcasted_iota(jnp.int32, (SLOTS, slots.shape[1]), 0)
    return slots == row


def with_norms(feat, feat_first):
    feat32 = feat.astype(f32)
    half = -0.5 * jnp.sum(feat32 * feat32, axis=0, keepdims=True)
    rows = DEPTH - feat.shape[0]
    row = lax.broadcasted_iota(jnp.int32, (rows, feat.shape[1]), 0)
    base = 0 if feat_first else 3
    extra = jnp.where(row < 6, 1.0, 0.0)
    for place, part in enumerate(split3(half)):
        extra = jnp.where(row == base + place, part, extra)
    return jnp.concatenate([feat32, extra], axis=0)


def kernel_parts(left, right):
    inner = jnp.dot(left, right, preferred_element_type=f32)
    value = jnp.exp2(inner * (math.log2(math.e) / 64.0))
    high = value.astype(bf16)
    return high, (value - high.astype(f32)).astype(bf16)


def pick_body(feat_hbm, *refs):
    small_hbm, refs = refs[:4], refs[4:]
    feat_ref, idx_ref, slots_ref, prices_ref, scale_ref, out_ref, sems = refs
    row_count = feat_ref.shape[1]
    copies = []
    for source, target in zip(small_hbm, (idx_ref, slots_ref, prices_ref, scale_ref)):
        copies.append(pltpu.make_async_copy(source, target, sems.at[len(copies)]))
    for begin in range(0, row_count, CHUNK):
        here = pl.ds(begin, CHUNK)
        copies.append(
            pltpu.make_async_copy(feat_hbm.at[:, here], feat_ref.at[:, here], sems.at[len(copies)])
        )
    for copy in copies:
        copy.start()
    total = jnp.zeros(out_ref.shape, f32)
    count = out_ref.shape[1]
    copies[0].wait()
    local_idx = idx_ref[...] - lax.axis_index("dp") * row_count
    for turn, begin in enumerate(range(0, row_count, CHUNK)):
        row = lax.broadcasted_iota(jnp.int32, (CHUNK, count), 0)
        one_hot = jnp.where(row == local_idx - begin, 1.0, 0.0).astype(bf16)
        copies[4 + turn].wait()
        total += jnp.dot(
            feat_ref[:, begin : begin + CHUNK], one_hot, preferred_element_type=f32
        )
    out_ref[...] = total.astype(bf16)
    for copy in copies[1:4]:
        copy.wait()


def columns_body(feat_ref, slots_ref, prices_ref, columns_ref, turned_ref, weight_ref):
    for begin in range(0, feat_ref.shape[1], CHUNK):
        here = slice(begin, begin + CHUNK)
        columns = with_norms(feat_ref[:, here], False)
        columns_ref[:, here] = columns.astype(bf16)
        turned_ref[here, :] = columns.T.astype(bf16)
        weight = jnp.where(slot_mask(slots_ref[:, here]), prices_ref[:, here], 0.0)
        weight_ref[:, here] = stack3(weight)


def rows_body(parts, turned_ref, weight_ref, *refs):
    center_refs, (block_ref, center_ref, out_ref) = refs[:parts], refs[parts:]
    center = with_norms(total_of(center_refs), True).astype(bf16)
    center_ref[...] = center
    total = jnp.zeros((24, center.shape[1]), f32)
    for begin in range(0, turned_ref.shape[0], CHUNK):
        here = slice(begin, begin + CHUNK)
        high, low = kernel_parts(turned_ref[here, :], center)
        block_ref[2 * begin : 2 * begin + CHUNK, :] = high
        block_ref[2 * begin + CHUNK : 2 * begin + 2 * CHUNK, :] = low
        weight = weight_ref[:, here]
        total += jnp.dot(weight, high, preferred_element_type=f32)
        total += jnp.dot(weight, low, preferred_element_type=f32)
    out_ref[...] = unstack3(total)


def turned_body(columns_ref, center_ref, block_ref):
    center = center_ref[...].astype(f32).T.astype(bf16)
    count = center.shape[0]
    for begin in range(0, columns_ref.shape[1], CHUNK):
        here = slice(begin, begin + CHUNK)
        high, low = kernel_parts(center, columns_ref[:, here])
        block_ref[0:count, here] = high
        block_ref[count:, here] = low


def apply_rows(scaled, turned_ref, slots_ref, out_ref):
    stacked = stack3(scaled)
    stacked = jnp.concatenate([stacked, stacked], axis=1)
    for turn, begin in enumerate(range(0, turned_ref.shape[1], CHUNK)):
        here = slice(begin, begin + CHUNK)
        value = jnp.dot(stacked, turned_ref[:, here], preferred_element_type=f32)
        own = jnp.where(slot_mask(slots_ref[:, here]), unstack3(value), 0.0)
        out_ref[turn : turn + 1, 0:CHUNK] = jnp.sum(own, axis=0, keepdims=True)


def fold_rows(row_weights, block_ref, slots_ref, out_ref):
    count = block_ref.shape[1]
    total = jnp.zeros((24, count), f32)
    square = jnp.zeros((SLOTS, 1), f32)
    for turn, begin in enumerate(range(0, slots_ref.shape[1], CHUNK)):
        mask = slot_mask(slots_ref[:, begin : begin + CHUNK])
        weight = jnp.where(mask, row_weights(turn), 0.0)
        square += row_sum(weight * weight)
        weight = stack3(weight)
        weight = jnp.concatenate([weight, weight], axis=1)
        block = block_ref[2 * begin : 2 * begin + 2 * CHUNK, :]
        total += jnp.dot(weight, block, preferred_element_type=f32)
    out_ref[:, 0:count] = unstack3(total)
    out_ref[:, count : count + EXTRA] = jnp.broadcast_to(square, (SLOTS, EXTRA))


def first_apply_body(parts, scale_over_root, *refs):
    first_refs = refs[:parts]
    scale_ref, slots_ref, turned_ref, target_ref, out_ref = refs[parts:]
    scale = scale_ref[...]
    target = scale * total_of(first_refs) * scale_over_root
    target_ref[...] = target
    out_ref[:, CHUNK:] = jnp.broadcast_to(row_sum(target * target), (SLOTS, EXTRA))
    apply_rows(scale * target, turned_ref, slots_ref, out_ref)


def first_fold_body(parts, *refs):
    row_refs = refs[:parts]
    slots_ref, block_ref, rows_ref, out_ref = refs[parts:]
    rows = total_of(row_refs)
    rows_ref[...] = rows
    fold_rows(lambda turn: rows[turn : turn + 1, 0:CHUNK], block_ref, slots_ref, out_ref)


def second_apply_body(parts, inv_rows, *refs):
    fold_refs = refs[:parts]
    (scale_ref, slots_ref, turned_ref, target_ref, rows_ref,
     residual_ref, step_ref, out_ref) = refs[parts:]
    count = scale_ref.shape[1]
    folded = total_of(fold_refs)
    scale = scale_ref[...]
    target = target_ref[...]
    norm = rows_ref[:, CHUNK : CHUNK + 1]
    applied = scale * folded[:, 0:count] * inv_rows + RIDGE * target
    step = norm / (folded[:, count : count + 1] * inv_rows + RIDGE * norm)
    residual = target - step * applied
    residual_ref[...] = residual
    step_ref[...] = jnp.broadcast_to(step, step_ref.shape)
    lane = lax.broadcasted_iota(jnp.int32, (SLOTS, EXTRA), 1)
    out_ref[:, CHUNK:] = jnp.where(
        lane == 0, row_sum(residual * residual), row_sum(residual * target)
    )
    apply_rows(scale * residual, turned_ref, slots_ref, out_ref)


def second_fold_body(parts, *refs):
    row_refs = refs[:parts]
    slots_ref, block_ref, rows_ref, sums_ref, out_ref = refs[parts:]
    latest = total_of(row_refs)
    sums_ref[...] = latest[:, CHUNK:]
    rows = rows_ref[...]
    ratio = latest[:, CHUNK : CHUNK + 1] / rows[:, CHUNK : CHUNK + 1]

    def row_weights(turn):
        return latest[turn : turn + 1, 0:CHUNK] + ratio * rows[turn : turn + 1, 0:CHUNK]

    fold_rows(row_weights, block_ref, slots_ref, out_ref)


def finish_body(parts, inv_rows, *refs):
    fold_refs = refs[:parts]
    (scale_ref, target_ref, residual_ref, step_ref, rows_ref, sums_ref,
     coefficients_ref, out_ref) = refs[parts:]
    count = scale_ref.shape[1]
    folded = total_of(fold_refs)
    target = target_ref[...]
    residual = residual_ref[...]
    first_norm = rows_ref[:, CHUNK : CHUNK + 1]
    norm = sums_ref[:, 0:1]
    cross = sums_ref[:, 1:2]
    ratio = norm / first_norm
    direction = residual + ratio * target
    square = norm + 2.0 * ratio * cross + ratio * ratio * first_norm
    applied = scale_ref[...] * folded[:, 0:count] * inv_rows + RIDGE * direction
    step = norm / (folded[:, count : count + 1] * inv_rows + RIDGE * square)
    coefficients_ref[...] = step_ref[:, 0:1] * target + step * direction
    out_ref[...] = residual - step * applied


def call(body, out_shape, *args, source=VMEM, flops=0, bytes_accessed=0, **more):
    return pl.pallas_call(
        body,
        out_shape=out_shape,
        in_specs=[source] * len(args),
        out_specs=jax.tree.map(lambda _: VMEM, out_shape),
        compiler_params=pltpu.CompilerParams(vmem_limit_bytes=36 * 1024 * 1024),
        cost_estimate=pl.CostEstimate(
            flops=flops, bytes_accessed=bytes_accessed, transcendentals=0
        ),
        **more,
    )(*args)


def exchange(value, axis):
    size = lax.axis_size(axis)
    parts = [value]
    stride = 1
    while stride < size:
        value = pair_total(parts)
        parts = [value]
        span = min(4, size // stride)
        for offset in range(1, span):
            pairs = [(i, i ^ (offset * stride)) for i in range(size)]
            parts.append(lax.ppermute(value, axis, pairs))
        stride *= span
    return parts


def shaped(shape, dtype=f32):
    return jax.ShapeDtypeStruct(shape, dtype)


def per_device(features, prices, slots, center_idx, center_scale):
    depth, row_count = features.shape
    count = center_idx.shape[0]
    all_rows = row_count * lax.axis_size("dp")
    turns = row_count // CHUNK
    row_shape = shaped((turns, CHUNK + EXTRA))
    fold_shape = shaped((SLOTS, count + EXTRA))
    vector = shaped((SLOTS, count))
    narrow = shaped((SLOTS, EXTRA))
    pass_cost = dict(flops=64 * row_count * count, bytes_accessed=4 * row_count * count)

    inputs = [
        pltpu.with_memory_space_constraint(array, pltpu.HBM)
        for array in (
            features,
            center_idx.reshape(1, count),
            slots.reshape(1, row_count),
            prices.reshape(1, row_count),
            center_scale.reshape(1, count),
        )
    ]
    features, _, slots, prices, scale, picked = call(
        pick_body,
        (
            shaped(features.shape, bf16),
            shaped((1, count), jnp.int32),
            shaped((1, row_count), jnp.int32),
            shaped((1, row_count)),
            shaped((1, count)),
            shaped((depth, count), bf16),
        ),
        *inputs,
        source=HBM,
        scratch_shapes=[pltpu.SemaphoreType.DMA((4 + turns,))],
    )
    centers = exchange(picked, "dp")
    columns, turned_columns, weight = call(
        columns_body,
        (
            shaped((DEPTH, row_count), bf16),
            shaped((row_count, DEPTH), bf16),
            shaped((24, row_count), bf16),
        ),
        features, slots, prices,
        flops=1000 * row_count,
        bytes_accessed=1024 * row_count,
    )
    block, center, first = call(
        partial(rows_body, len(centers)),
        (shaped((2 * row_count, count), bf16), shaped((DEPTH, count), bf16), vector),
        turned_columns, weight, *centers,
        **pass_cost,
    )
    firsts = exchange(first, "dp")
    turned = call(
        turned_body, shaped((2 * count, row_count), bf16), columns, center, **pass_cost
    )
    target, rows = call(
        partial(first_apply_body, len(firsts), 1.0 / math.sqrt(all_rows)),
        (vector, row_shape),
        *firsts, scale, slots, turned,
    )
    rows = exchange(rows, "centers")
    rows, folded = call(
        partial(first_fold_body, len(rows)), (row_shape, fold_shape), *rows, slots, block
    )
    folds = exchange(folded, "dp")
    residual, step, latest = call(
        partial(second_apply_body, len(folds), 1.0 / all_rows),
        (vector, narrow, row_shape),
        *folds, scale, slots, turned, target, rows,
    )
    latest = exchange(latest, "centers")
    sums, folded = call(
        partial(second_fold_body, len(latest)),
        (narrow, fold_shape),
        *latest, slots, block, rows,
    )
    folds = exchange(folded, "dp")
    return call(
        partial(finish_body, len(folds), 1.0 / all_rows),
        (vector, vector),
        *folds, scale, target, residual, step, rows, sums,
    )


def solution(mesh):
    return jax.shard_map(
        per_device,
        mesh=mesh,
        in_specs=(P(None, "dp"), P("dp"), P("dp"), P("centers"), P("centers")),
        out_specs=(P(None, "centers"), P(None, "centers")),
        check_vma=False,
    )
```

time: 58.5 us -> 57 us (0.974)
  local copies, waits for them, and re-layouts: 3.16 us -> 0 us
  Pallas kernels: 13.7 us -> 16.2 us
  other arithmetic: 0.7 us -> 0.01 us
    unnamed x10 -> x0, local copies, waits for them, and re-layouts: 3.16 us -> none
    pallas_call x7 -> x9, Pallas kernels: 13.7 us -> 16.2 us  [call(): pl.pallas_call(body, out_shape=out_shape, in_specs=[source] * len(args),...]
    sub x1 -> x0, other arithmetic: 0.69 us -> none  [per_device(): center_idx - lax.axis_index('dp') * row_count]
  transfers between devices with their start and end apart: 16 -> 16, of which waited for: 13 -> 11; matrix products, arithmetic and copies ran while one was open for 0% -> 0% of each run, Pallas kernels for 0% -> 4%
where the time goes in v3:
time: 57 us; the launch traced here: 56.8 us
  starting transfers between devices  21.1 us (37%)
  waiting for transfers between devices  18.8 us (33%)
  Pallas kernels  16.2 us (28%)
  between operations  0.71 us (1%)
    ppermute x16, starting transfers between devices, exchange(): parts.append(lax.ppermute(value, axis, pairs))  21.1 us
    ppermute x16, waiting for transfers between devices, exchange(): parts.append(lax.ppermute(value, axis, pairs))  18.8 us
    pallas_call x9, Pallas kernels, call(): pl.pallas_call(body, out_shape=out_shape, in_specs=[source] * len(args),...  16.2 us
  transfers between devices with their start and end apart: 16, of which 11 were waited for; matrix products, arithmetic and copies ran while one was open for 0% of the time, Pallas kernels for 4%

profile of v3, /device:TPU:0, one launch (start us, length us, event | category | flops | bytes accessed | tf_op | source)
XLA Modules:
  0.0 56.8 jit_solution(12605925382810049981)
XLA Ops:
  0.6 3.3 %shard_map.68 = (bf16[64,4096]{1,0:T(8,128)(2,1)S(1)}, s32[1,512]{1,0:T(1,128)}, s32[1,4096]{1,0:T(1,128)S(1)}, f32[1,4096]{1,0:T(1,128)S(1)}, f32[1,512]{1,0:T(1,128)S(1)}, /*index=5*/bf16[64,512]{1,0:T(8,128)(2,1)S(1)}) custom-call(bf16[64,4096]{1,0:T(8,128)(2,1)} %feat_hbm.1, s32[1,512]{1,0:T(1,128)} %bitcast.6, s32[1,4096]{1,0:T(1,128)} %bitcast.4, ...), custom_call_target="tpu_custom_call" | custom-call | tf_op jit(solution)/shard_map/pallas_call | solution.py:241
  3.9 3.0 %collective-permute-start = (bf16[64,512]{1,0:T(8,128)(2,1)S(1)}, bf16[64,512]{1,0:T(8,128)(2,1)S(1)}, u32[]{:S(2)}, u32[]{:S(2)}) collective-permute-start(bf16[64,512]{1,0:T(8,128)(2,1)S(1)} %get-tuple-element.27.refs_0_), channel_id=1, source_target_pairs={{0,16},{16,0},{1,17},{17,1},{2,18},{18,2},{3,19},{19,3},{4,20},{20... | collective-permute-start | bytes 196616 | tf_op jit(solution)/shard_map/ppermute | solution.py:264
  6.9 0.4 shard_map.69
  7.4 1.8 %collective-permute-done.refs_1_ = bf16[64,512]{1,0:T(8,128)(2,1)S(1)} collective-permute-done((bf16[64,512]{1,0:T(8,128)(2,1)S(1)}, bf16[64,512]{1,0:T(8,128)(2,1)S(1)}, u32[]{:S(2)}, u32[]{:S(2)}) %collective-permute-start) | collective-permute-done | bytes 65568 | tf_op jit(solution)/shard_map/ppermute | solution.py:264
  9.2 3.3 %shard_map.70 = (bf16[8192,512]{1,0:T(8,128)(2,1)S(1)}, bf16[128,512]{1,0:T(8,128)(2,1)S(1)}, f32[8,512]{1,0:T(8,128)S(1)}) custom-call(bf16[4096,128]{1,0:T(8,128)(2,1)S(1)} %get-tuple-element.25.turned_ref, bf16[24,4096]{1,0:T(8,128)(2,1)S(1)} %get-tuple-element.26.weight_ref, bf16[64,512]{1,0:T(8,128)(2,1)S(1)} %get-tuple-element.27.refs_0_, ...), custom_call_target="tpu_custom_call" | custom-call | flops 134217728 | bytes 8388608 | tf_op jit(solution)/shard_map/pallas_call | solution.py:241
  12.5 2.0 %collective-permute-start.1 = (f32[8,512]{1,0:T(8,128)S(1)}, f32[8,512]{1,0:T(8,128)S(1)}, u32[]{:S(2)}, u32[]{:S(2)}) collective-permute-start(f32[8,512]{1,0:T(8,128)S(1)} %get-tuple-element.28.refs_0_), channel_id=1, source_target_pairs={{0,16},{16,0},{1,17},{17,1},{2,18},{18,2},{3,19},{19,3},{4,20},{20... | collective-permute-start | bytes 49160 | tf_op jit(solution)/shard_map/ppermute | solution.py:264
  14.6 2.1 %shard_map.71.refs_4_ = bf16[1024,4096]{1,0:T(8,128)(2,1)S(1)} custom-call(bf16[128,4096]{1,0:T(8,128)(2,1)S(1)} %get-tuple-element.30.columns_ref, bf16[128,512]{1,0:T(8,128)(2,1)S(1)} %get-tuple-element.31.center_ref), custom_call_target="tpu_custom_call" | custom-call | flops 134217728 | bytes 8388608 | tf_op jit(solution)/shard_map/pallas_call | solution.py:241
  16.6 0.0 collective-permute-done.1.refs_1_
  16.7 1.6 %shard_map.72 = (f32[8,512]{1,0:T(8,128)S(1)}, f32[8,640]{1,0:T(8,128)S(1)}) custom-call(f32[8,512]{1,0:T(8,128)S(1)} %get-tuple-element.28.refs_0_, f32[8,512]{1,0:T(8,128)S(1)} %collective-permute-done.1.refs_1_, f32[1,512]{1,0:T(1,128)S(1)} %get-tuple-element.29.refs_2_, s32[1,4096]{1,0:T(1,128)S(1)} %get-tuple-element.23.slots_ref.refs_3_.refs_4_, ...), custom_call_target="tpu_custom_call" | custom-call | tf_op jit(solution)/shard_map/pallas_call | solution.py:241
  18.2 0.1 collective-permute-start.2
  18.3 1.7 %collective-permute-start.3 = (f32[8,640]{1,0:T(8,128)S(1)}, f32[8,640]{1,0:T(8,128)S(1)}, u32[]{:S(2)}, u32[]{:S(2)}) collective-permute-start(f32[8,640]{1,0:T(8,128)S(1)} %get-tuple-element.32), channel_id=1, source_target_pairs={{0,2},{1,3},{2,0},{3,1},{4,6},{5,7},{6,4},{7,5},{8,10},{9,11},{10,... | collective-permute-start | bytes 61448 | tf_op jit(solution)/shard_map/ppermute | solution.py:264
  20.0 0.1 collective-permute-start.4
  20.2 0.0 collective-permute-done.2
  20.2 2.0 %collective-permute-done.3 = f32[8,640]{1,0:T(8,128)S(1)} collective-permute-done((f32[8,640]{1,0:T(8,128)S(1)}, f32[8,640]{1,0:T(8,128)S(1)}, u32[]{:S(2)}, u32[]{:S(2)}) %collective-permute-start.3) | collective-permute-done | bytes 20512 | tf_op jit(solution)/shard_map/ppermute | solution.py:264
  22.1 1.1 %collective-permute-done.4 = f32[8,640]{1,0:T(8,128)S(1)} collective-permute-done((f32[8,640]{1,0:T(8,128)S(1)}, f32[8,640]{1,0:T(8,128)S(1)}, u32[]{:S(2)}, u32[]{:S(2)}) %collective-permute-start.4) | collective-permute-done | bytes 20512 | tf_op jit(solution)/shard_map/ppermute | solution.py:264
  23.3 1.6 %collective-permute-start.5 = (f32[8,640]{1,0:T(8,128)S(1)}, f32[8,640]{1,0:T(8,128)S(1)}, u32[]{:S(2)}, u32[]{:S(2)}) collective-permute-start(f32[8,640]{1,0:T(8,128)S(1)} %add_add_fusion.1.refs_0_), channel_id=1, source_target_pairs={{0,4},{1,5},{2,6},{3,7},{4,0},{5,1},{6,2},{7,3},{8,12},{9,13},{10,... | collective-permute-start | bytes 61448 | tf_op jit(solution)/shard_map/ppermute | solution.py:264
  24.9 2.6 %collective-permute-start.6 = (f32[8,640]{1,0:T(8,128)S(1)}, f32[8,640]{1,0:T(8,128)S(1)}, u32[]{:S(2)}, u32[]{:S(2)}) collective-permute-start(f32[8,640]{1,0:T(8,128)S(1)} %add_add_fusion.1.refs_0_), channel_id=1, source_target_pairs={{0,8},{1,9},{2,10},{3,11},{4,12},{5,13},{6,14},{7,15},{8,0},{9,1},... | collective-permute-start | bytes 61448 | tf_op jit(solution)/shard_map/ppermute | solution.py:264
  27.5 0.2 collective-permute-start.7
  27.7 0.0 collective-permute-done.5.refs_1_
  27.7 2.1 %collective-permute-done.6.refs_2_ = f32[8,640]{1,0:T(8,128)S(1)} collective-permute-done((f32[8,640]{1,0:T(8,128)S(1)}, f32[8,640]{1,0:T(8,128)S(1)}, u32[]{:S(2)}, u32[]{:S(2)}) %collective-permute-start.6) | collective-permute-done | bytes 20512 | tf_op jit(solution)/shard_map/ppermute | solution.py:264
  29.8 3.3 %collective-permute-done.7.refs_3_ = f32[8,640]{1,0:T(8,128)S(1)} collective-permute-done((f32[8,640]{1,0:T(8,128)S(1)}, f32[8,640]{1,0:T(8,128)S(1)}, u32[]{:S(2)}, u32[]{:S(2)}) %collective-permute-start.7) | collective-permute-done | bytes 20512 | tf_op jit(solution)/shard_map/ppermute | solution.py:264
  33.1 1.5 %shard_map.73 = (f32[8,640]{1,0:T(8,128)S(1)}, f32[8,640]{1,0:T(8,128)S(1)}) custom-call(f32[8,640]{1,0:T(8,128)S(1)} %add_add_fusion.1.refs_0_, f32[8,640]{1,0:T(8,128)S(1)} %collective-permute-done.5.refs_1_, f32[8,640]{1,0:T(8,128)S(1)} %collective-permute-done.6.refs_2_, f32[8,640]{1,0:T(8,128)S(1)} %collective-permute-done.7.refs_3_, ...), custom_call_target="tpu_custom_call" | custom-call | tf_op jit(solution)/shard_map/pallas_call | solution.py:241
  34.6 1.5 %collective-permute-start.8 = (f32[8,640]{1,0:T(8,128)S(1)}, f32[8,640]{1,0:T(8,128)S(1)}, u32[]{:S(2)}, u32[]{:S(2)}) collective-permute-start(f32[8,640]{1,0:T(8,128)S(1)} %get-tuple-element.34.refs_0_), channel_id=1, source_target_pairs={{0,16},{16,0},{1,17},{17,1},{2,18},{18,2},{3,19},{19,3},{4,20},{20... | collective-permute-start | bytes 61448 | tf_op jit(solution)/shard_map/ppermute | solution.py:264
  36.1 2.3 %collective-permute-done.8.refs_1_ = f32[8,640]{1,0:T(8,128)S(1)} collective-permute-done((f32[8,640]{1,0:T(8,128)S(1)}, f32[8,640]{1,0:T(8,128)S(1)}, u32[]{:S(2)}, u32[]{:S(2)}) %collective-permute-start.8) | collective-permute-done | bytes 20512 | tf_op jit(solution)/shard_map/ppermute | solution.py:264
  38.4 1.6 %shard_map.74 = (f32[8,512]{1,0:T(8,128)S(1)}, f32[8,128]{1,0:T(8,128)S(1)}, f32[8,640]{1,0:T(8,128)S(1)}) custom-call(f32[8,640]{1,0:T(8,128)S(1)} %get-tuple-element.34.refs_0_, f32[8,640]{1,0:T(8,128)S(1)} %collective-permute-done.8.refs_1_, f32[1,512]{1,0:T(1,128)S(1)} %get-tuple-element.29.refs_2_, ...), custom_call_target="tpu_custom_call" | custom-call | tf_op jit(solution)/shard_map/pallas_call | solution.py:241
  40.0 0.8 %collective-permute-start.10 = (f32[8,640]{1,0:T(8,128)S(1)}, f32[8,640]{1,0:T(8,128)S(1)}, u32[]{:S(2)}, u32[]{:S(2)}) collective-permute-start(f32[8,640]{1,0:T(8,128)S(1)} %get-tuple-element.37), channel_id=1, source_target_pairs={{0,2},{1,3},{2,0},{3,1},{4,6},{5,7},{6,4},{7,5},{8,10},{9,11},{10,... | collective-permute-start | bytes 61448 | tf_op jit(solution)/shard_map/ppermute | solution.py:264
  40.8 0.0 collective-permute-start.11
  40.8 1.4 %collective-permute-start.9 = (f32[8,640]{1,0:T(8,128)S(1)}, f32[8,640]{1,0:T(8,128)S(1)}, u32[]{:S(2)}, u32[]{:S(2)}) collective-permute-start(f32[8,640]{1,0:T(8,128)S(1)} %get-tuple-element.37), channel_id=1, source_target_pairs={{0,1},{1,0},{2,3},{3,2},{4,5},{5,4},{6,7},{7,6},{8,9},{9,8},{10,11... | collective-permute-start | bytes 61448 | tf_op jit(solution)/shard_map/ppermute | solution.py:264
  42.2 1.7 %collective-permute-done.10 = f32[8,640]{1,0:T(8,128)S(1)} collective-permute-done((f32[8,640]{1,0:T(8,128)S(1)}, f32[8,640]{1,0:T(8,128)S(1)}, u32[]{:S(2)}, u32[]{:S(2)}) %collective-permute-start.10) | collective-permute-done | bytes 20512 | tf_op jit(solution)/shard_map/ppermute | solution.py:264
  43.9 0.3 collective-permute-done.11
  44.2 0.0 collective-permute-done.9
  44.3 0.1 collective-permute-start.12
  44.3 0.8 %collective-permute-start.13 = (f32[8,640]{1,0:T(8,128)S(1)}, f32[8,640]{1,0:T(8,128)S(1)}, u32[]{:S(2)}, u32[]{:S(2)}) collective-permute-start(f32[8,640]{1,0:T(8,128)S(1)} %add_add_fusion.refs_0_), channel_id=1, source_target_pairs={{0,8},{1,9},{2,10},{3,11},{4,12},{5,13},{6,14},{7,15},{8,0},{9,1},... | collective-permute-start | bytes 61448 | tf_op jit(solution)/shard_map/ppermute | solution.py:264
  45.1 3.6 %collective-permute-start.14 = (f32[8,640]{1,0:T(8,128)S(1)}, f32[8,640]{1,0:T(8,128)S(1)}, u32[]{:S(2)}, u32[]{:S(2)}) collective-permute-start(f32[8,640]{1,0:T(8,128)S(1)} %add_add_fusion.refs_0_), channel_id=1, source_target_pairs={{0,12},{1,13},{2,14},{3,15},{4,8},{5,9},{6,10},{7,11},{8,4},{9,5},... | collective-permute-start | bytes 61448 | tf_op jit(solution)/shard_map/ppermute | solution.py:264
  48.7 0.0 collective-permute-done.12.refs_1_
  48.7 0.4 collective-permute-done.13.refs_2_
  49.1 1.6 %collective-permute-done.14.refs_3_ = f32[8,640]{1,0:T(8,128)S(1)} collective-permute-done((f32[8,640]{1,0:T(8,128)S(1)}, f32[8,640]{1,0:T(8,128)S(1)}, u32[]{:S(2)}, u32[]{:S(2)}) %collective-permute-start.14) | collective-permute-done | bytes 20512 | tf_op jit(solution)/shard_map/ppermute | solution.py:264
  50.7 1.6 %shard_map.75 = (f32[8,128]{1,0:T(8,128)S(1)}, f32[8,640]{1,0:T(8,128)S(1)}) custom-call(f32[8,640]{1,0:T(8,128)S(1)} %add_add_fusion.refs_0_, f32[8,640]{1,0:T(8,128)S(1)} %collective-permute-done.12.refs_1_, f32[8,640]{1,0:T(8,128)S(1)} %collective-permute-done.13.refs_2_, f32[8,640]{1,0:T(8,128)S(1)} %collective-permute-done.14.refs_3_, ...), custom_call_target="tpu_custom_call" | custom-call | tf_op jit(solution)/shard_map/pallas_call | solution.py:241
  52.3 1.5 %collective-permute-start.15 = (f32[8,640]{1,0:T(8,128)S(1)}, f32[8,640]{1,0:T(8,128)S(1)}, u32[]{:S(2)}, u32[]{:S(2)}) collective-permute-start(f32[8,640]{1,0:T(8,128)S(1)} %get-tuple-element.38.refs_0_), channel_id=1, source_target_pairs={{0,16},{16,0},{1,17},{17,1},{2,18},{18,2},{3,19},{19,3},{4,20},{20... | collective-permute-start | bytes 61448 | tf_op jit(solution)/shard_map/ppermute | solution.py:264
  53.8 2.3 %collective-permute-done.15.refs_1_ = f32[8,640]{1,0:T(8,128)S(1)} collective-permute-done((f32[8,640]{1,0:T(8,128)S(1)}, f32[8,640]{1,0:T(8,128)S(1)}, u32[]{:S(2)}, u32[]{:S(2)}) %collective-permute-start.15) | collective-permute-done | bytes 20512 | tf_op jit(solution)/shard_map/ppermute | solution.py:264
  56.1 0.8 %shard_map.76 = (f32[8,512]{1,0:T(8,128)}, f32[8,512]{1,0:T(8,128)}) custom-call(f32[8,640]{1,0:T(8,128)S(1)} %get-tuple-element.38.refs_0_, f32[8,640]{1,0:T(8,128)S(1)} %collective-permute-done.15.refs_1_, f32[1,512]{1,0:T(1,128)S(1)} %get-tuple-element.29.refs_2_, f32[8,512]{1,0:T(8,128)S(1)} %get-tuple-element.35.refs_5_.refs_3_, ...), custom_call_target="tpu_custom_call" | custom-call | tf_op jit(solution)/shard_map/pallas_call | solution.py:241
  (2 shorter events, 0.0 us)
Async XLA Ops:
  3.9 5.2 %collective-permute-start = (bf16[64,512]{1,0:T(8,128)(2,1)S(1)}, bf16[64,512]{1,0:T(8,128)(2,1)S(1)}, u32[]{:S(2)}, u32[]{:S(2)}) collective-permute-start(bf16[64,512]{1,0:T(8,128)(2,1)S(1)} %get-tuple-element.27.refs_0_), channel_id=1, source_target_pairs={{0,16},{16,0},{1,17},{17,1},{2,18},{18,2},{3,19},{19,3},{4,20},{20... | collective-permute-start | bytes 196616 | tf_op jit(solution)/shard_map/ppermute | solution.py:264
  12.5 4.1 %collective-permute-start.1 = (f32[8,512]{1,0:T(8,128)S(1)}, f32[8,512]{1,0:T(8,128)S(1)}, u32[]{:S(2)}, u32[]{:S(2)}) collective-permute-start(f32[8,512]{1,0:T(8,128)S(1)} %get-tuple-element.28.refs_0_), channel_id=1, source_target_pairs={{0,16},{16,0},{1,17},{17,1},{2,18},{18,2},{3,19},{19,3},{4,20},{20... | collective-permute-start | bytes 49160 | tf_op jit(solution)/shard_map/ppermute | solution.py:264
  18.2 1.9 %collective-permute-start.2 = (f32[8,640]{1,0:T(8,128)S(1)}, f32[8,640]{1,0:T(8,128)S(1)}, u32[]{:S(2)}, u32[]{:S(2)}) collective-permute-start(f32[8,640]{1,0:T(8,128)S(1)} %get-tuple-element.32), channel_id=1, source_target_pairs={{0,1},{1,0},{2,3},{3,2},{4,5},{5,4},{6,7},{7,6},{8,9},{9,8},{10,11... | collective-permute-start | bytes 61448 | tf_op jit(solution)/shard_map/ppermute | solution.py:264
  18.3 3.8 %collective-permute-start.3 = (f32[8,640]{1,0:T(8,128)S(1)}, f32[8,640]{1,0:T(8,128)S(1)}, u32[]{:S(2)}, u32[]{:S(2)}) collective-permute-start(f32[8,640]{1,0:T(8,128)S(1)} %get-tuple-element.32), channel_id=1, source_target_pairs={{0,2},{1,3},{2,0},{3,1},{4,6},{5,7},{6,4},{7,5},{8,10},{9,11},{10,... | collective-permute-start | bytes 61448 | tf_op jit(solution)/shard_map/ppermute | solution.py:264
  20.0 3.2 %collective-permute-start.4 = (f32[8,640]{1,0:T(8,128)S(1)}, f32[8,640]{1,0:T(8,128)S(1)}, u32[]{:S(2)}, u32[]{:S(2)}) collective-permute-start(f32[8,640]{1,0:T(8,128)S(1)} %get-tuple-element.32), channel_id=1, source_target_pairs={{0,3},{1,2},{2,1},{3,0},{4,7},{5,6},{6,5},{7,4},{8,11},{9,10},{10,... | collective-permute-start | bytes 61448 | tf_op jit(solution)/shard_map/ppermute | solution.py:264
  23.3 4.5 %collective-permute-start.5 = (f32[8,640]{1,0:T(8,128)S(1)}, f32[8,640]{1,0:T(8,128)S(1)}, u32[]{:S(2)}, u32[]{:S(2)}) collective-permute-start(f32[8,640]{1,0:T(8,128)S(1)} %add_add_fusion.1.refs_0_), channel_id=1, source_target_pairs={{0,4},{1,5},{2,6},{3,7},{4,0},{5,1},{6,2},{7,3},{8,12},{9,13},{10,... | collective-permute-start | bytes 61448 | tf_op jit(solution)/shard_map/ppermute | solution.py:264
  24.9 4.9 %collective-permute-start.6 = (f32[8,640]{1,0:T(8,128)S(1)}, f32[8,640]{1,0:T(8,128)S(1)}, u32[]{:S(2)}, u32[]{:S(2)}) collective-permute-start(f32[8,640]{1,0:T(8,128)S(1)} %add_add_fusion.1.refs_0_), channel_id=1, source_target_pairs={{0,8},{1,9},{2,10},{3,11},{4,12},{5,13},{6,14},{7,15},{8,0},{9,1},... | collective-permute-start | bytes 61448 | tf_op jit(solution)/shard_map/ppermute | solution.py:264
  27.5 5.6 %collective-permute-start.7 = (f32[8,640]{1,0:T(8,128)S(1)}, f32[8,640]{1,0:T(8,128)S(1)}, u32[]{:S(2)}, u32[]{:S(2)}) collective-permute-start(f32[8,640]{1,0:T(8,128)S(1)} %add_add_fusion.1.refs_0_), channel_id=1, source_target_pairs={{0,12},{1,13},{2,14},{3,15},{4,8},{5,9},{6,10},{7,11},{8,4},{9,5},... | collective-permute-start | bytes 61448 | tf_op jit(solution)/shard_map/ppermute | solution.py:264
  34.6 3.8 %collective-permute-start.8 = (f32[8,640]{1,0:T(8,128)S(1)}, f32[8,640]{1,0:T(8,128)S(1)}, u32[]{:S(2)}, u32[]{:S(2)}) collective-permute-start(f32[8,640]{1,0:T(8,128)S(1)} %get-tuple-element.34.refs_0_), channel_id=1, source_target_pairs={{0,16},{16,0},{1,17},{17,1},{2,18},{18,2},{3,19},{19,3},{4,20},{20... | collective-permute-start | bytes 61448 | tf_op jit(solution)/shard_map/ppermute | solution.py:264
  40.0 3.9 %collective-permute-start.10 = (f32[8,640]{1,0:T(8,128)S(1)}, f32[8,640]{1,0:T(8,128)S(1)}, u32[]{:S(2)}, u32[]{:S(2)}) collective-permute-start(f32[8,640]{1,0:T(8,128)S(1)} %get-tuple-element.37), channel_id=1, source_target_pairs={{0,2},{1,3},{2,0},{3,1},{4,6},{5,7},{6,4},{7,5},{8,10},{9,11},{10,... | collective-permute-start | bytes 61448 | tf_op jit(solution)/shard_map/ppermute | solution.py:264
  40.8 3.4 %collective-permute-start.11 = (f32[8,640]{1,0:T(8,128)S(1)}, f32[8,640]{1,0:T(8,128)S(1)}, u32[]{:S(2)}, u32[]{:S(2)}) collective-permute-start(f32[8,640]{1,0:T(8,128)S(1)} %get-tuple-element.37), channel_id=1, source_target_pairs={{0,3},{1,2},{2,1},{3,0},{4,7},{5,6},{6,5},{7,4},{8,11},{9,10},{10,... | collective-permute-start | bytes 61448 | tf_op jit(solution)/shard_map/ppermute | solution.py:264
  40.8 3.4 %collective-permute-start.9 = (f32[8,640]{1,0:T(8,128)S(1)}, f32[8,640]{1,0:T(8,128)S(1)}, u32[]{:S(2)}, u32[]{:S(2)}) collective-permute-start(f32[8,640]{1,0:T(8,128)S(1)} %get-tuple-element.37), channel_id=1, source_target_pairs={{0,1},{1,0},{2,3},{3,2},{4,5},{5,4},{6,7},{7,6},{8,9},{9,8},{10,11... | collective-permute-start | bytes 61448 | tf_op jit(solution)/shard_map/ppermute | solution.py:264
  44.3 4.5 %collective-permute-start.12 = (f32[8,640]{1,0:T(8,128)S(1)}, f32[8,640]{1,0:T(8,128)S(1)}, u32[]{:S(2)}, u32[]{:S(2)}) collective-permute-start(f32[8,640]{1,0:T(8,128)S(1)} %add_add_fusion.refs_0_), channel_id=1, source_target_pairs={{0,4},{1,5},{2,6},{3,7},{4,0},{5,1},{6,2},{7,3},{8,12},{9,13},{10,... | collective-permute-start | bytes 61448 | tf_op jit(solution)/shard_map/ppermute | solution.py:264
  44.3 4.7 %collective-permute-start.13 = (f32[8,640]{1,0:T(8,128)S(1)}, f32[8,640]{1,0:T(8,128)S(1)}, u32[]{:S(2)}, u32[]{:S(2)}) collective-permute-start(f32[8,640]{1,0:T(8,128)S(1)} %add_add_fusion.refs_0_), channel_id=1, source_target_pairs={{0,8},{1,9},{2,10},{3,11},{4,12},{5,13},{6,14},{7,15},{8,0},{9,1},... | collective-permute-start | bytes 61448 | tf_op jit(solution)/shard_map/ppermute | solution.py:264
  45.1 5.6 %collective-permute-start.14 = (f32[8,640]{1,0:T(8,128)S(1)}, f32[8,640]{1,0:T(8,128)S(1)}, u32[]{:S(2)}, u32[]{:S(2)}) collective-permute-start(f32[8,640]{1,0:T(8,128)S(1)} %add_add_fusion.refs_0_), channel_id=1, source_target_pairs={{0,12},{1,13},{2,14},{3,15},{4,8},{5,9},{6,10},{7,11},{8,4},{9,5},... | collective-permute-start | bytes 61448 | tf_op jit(solution)/shard_map/ppermute | solution.py:264
  52.3 3.8 %collective-permute-start.15 = (f32[8,640]{1,0:T(8,128)S(1)}, f32[8,640]{1,0:T(8,128)S(1)}, u32[]{:S(2)}, u32[]{:S(2)}) collective-permute-start(f32[8,640]{1,0:T(8,128)S(1)} %get-tuple-element.38.refs_0_), channel_id=1, source_target_pairs={{0,16},{16,0},{1,17},{17,1},{2,18},{18,2},{3,19},{19,3},{4,20},{20... | collective-permute-start | bytes 61448 | tf_op jit(solution)/shard_map/ppermute | solution.py:264

commit v4 on v3

--- a/solution.py
+++ b/solution.py
@@ -12,7 +12,9 @@
 RIDGE = 0.5
 CHUNK = 512
 EXTRA = 128
-DEPTH = 128
+DEPTH = 256
+STEP = 256
+FACTOR = math.log2(math.e) / 64.0
 f32 = jnp.float32
 bf16 = jnp.bfloat16
 VMEM = pl.BlockSpec(memory_space=pltpu.VMEM)
@@ -53,79 +55,84 @@
     return slots == row
 
 
-def with_norms(feat, feat_first):
-    feat32 = feat.astype(f32)
-    half = -0.5 * jnp.sum(feat32 * feat32, axis=0, keepdims=True)
-    rows = DEPTH - feat.shape[0]
-    row = lax.broadcasted_iota(jnp.int32, (rows, feat.shape[1]), 0)
-    base = 0 if feat_first else 3
+def norm_rows(feat32, base):
+    half = (-0.5 * FACTOR) * jnp.sum(feat32 * feat32, axis=0, keepdims=True)
+    row = lax.broadcasted_iota(jnp.int32, (feat32.shape[0], feat32.shape[1]), 0)
     extra = jnp.where(row < 6, 1.0, 0.0)
     for place, part in enumerate(split3(half)):
         extra = jnp.where(row == base + place, part, extra)
-    return jnp.concatenate([feat32, extra], axis=0)
+    return extra
 
 
 def kernel_parts(left, right):
-    inner = jnp.dot(left, right, preferred_element_type=f32)
-    value = jnp.exp2(inner * (math.log2(math.e) / 64.0))
+    value = jnp.exp2(jnp.dot(left, right, preferred_element_type=f32))
     high = value.astype(bf16)
     return high, (value - high.astype(f32)).astype(bf16)
 
 
-def pick_body(feat_hbm, *refs):
-    small_hbm, refs = refs[:4], refs[4:]
-    feat_ref, idx_ref, slots_ref, prices_ref, scale_ref, out_ref, sems = refs
+def pick_body(feat_hbm, idx_hbm, slots_hbm, prices_hbm, scale_hbm, *refs):
+    feat_ref, slots_ref, prices_ref, scale_ref, out_ref, idx_ref, hit_ref, sems = refs
     row_count = feat_ref.shape[1]
-    copies = []
-    for source, target in zip(small_hbm, (idx_ref, slots_ref, prices_ref, scale_ref)):
-        copies.append(pltpu.make_async_copy(source, target, sems.at[len(copies)]))
-    for begin in range(0, row_count, CHUNK):
-        here = pl.ds(begin, CHUNK)
-        copies.append(
-            pltpu.make_async_copy(feat_hbm.at[:, here], feat_ref.at[:, here], sems.at[len(copies)])
-        )
+    count = out_ref.shape[1]
+    sources = (idx_hbm, feat_hbm, slots_hbm, prices_hbm, scale_hbm)
+    targets = (idx_ref, feat_ref, slots_ref, prices_ref, scale_ref)
+    copies = [
+        pltpu.make_async_copy(source, target, sems.at[place])
+        for place, (source, target) in enumerate(zip(sources, targets))
+    ]
     for copy in copies:
         copy.start()
-    total = jnp.zeros(out_ref.shape, f32)
-    count = out_ref.shape[1]
     copies[0].wait()
     local_idx = idx_ref[...] - lax.axis_index("dp") * row_count
-    for turn, begin in enumerate(range(0, row_count, CHUNK)):
+    for begin in range(0, row_count, CHUNK):
         row = lax.broadcasted_iota(jnp.int32, (CHUNK, count), 0)
-        one_hot = jnp.where(row == local_idx - begin, 1.0, 0.0).astype(bf16)
-        copies[4 + turn].wait()
-        total += jnp.dot(
-            feat_ref[:, begin : begin + CHUNK], one_hot, preferred_element_type=f32
-        )
-    out_ref[...] = total.astype(bf16)
-    for copy in copies[1:4]:
+        hit = jnp.where(row == local_idx - begin, 1.0, 0.0)
+        hit_ref[begin : begin + CHUNK, :] = hit.astype(bf16)
+    copies[1].wait()
+    out_ref[...] = jnp.dot(
+        feat_ref[...], hit_ref[...], preferred_element_type=f32
+    ).astype(bf16)
+    for copy in copies[2:]:
         copy.wait()
 
 
 def columns_body(feat_ref, slots_ref, prices_ref, columns_ref, turned_ref, weight_ref):
     for begin in range(0, feat_ref.shape[1], CHUNK):
         here = slice(begin, begin + CHUNK)
-        columns = with_norms(feat_ref[:, here], False)
-        columns_ref[:, here] = columns.astype(bf16)
-        turned_ref[here, :] = columns.T.astype(bf16)
+        feat32 = feat_ref[:, here].astype(f32)
+        pair = jnp.concatenate([feat32, feat32], axis=0)
+        last = jnp.concatenate([feat32, norm_rows(feat32, 3)], axis=0)
+        columns_ref[0:128, here] = pair.astype(bf16)
+        columns_ref[128:256, here] = last.astype(bf16)
+        turned_ref[here, 0:128] = pair.T.astype(bf16)
+        turned_ref[here, 128:256] = last.T.astype(bf16)
         weight = jnp.where(slot_mask(slots_ref[:, here]), prices_ref[:, here], 0.0)
         weight_ref[:, here] = stack3(weight)
 
 
 def rows_body(parts, turned_ref, weight_ref, *refs):
     center_refs, (block_ref, center_ref, out_ref) = refs[:parts], refs[parts:]
-    center = with_norms(total_of(center_refs), True).astype(bf16)
+    center = total_of(center_refs).astype(f32)
+    center = jnp.concatenate(
+        [*split3(center * FACTOR), norm_rows(center, 0)], axis=0
+    ).astype(bf16)
     center_ref[...] = center
     total = jnp.zeros((24, center.shape[1]), f32)
-    for begin in range(0, turned_ref.shape[0], CHUNK):
-        here = slice(begin, begin + CHUNK)
-        high, low = kernel_parts(turned_ref[here, :], center)
-        block_ref[2 * begin : 2 * begin + CHUNK, :] = high
-        block_ref[2 * begin + CHUNK : 2 * begin + 2 * CHUNK, :] = low
-        weight = weight_ref[:, here]
-        total += jnp.dot(weight, high, preferred_element_type=f32)
-        total += jnp.dot(weight, low, preferred_element_type=f32)
-    out_ref[...] = unstack3(total)
+
+    def fold(begin):
+        weight = weight_ref[:, begin : begin + STEP]
+        weight = jnp.concatenate([weight, weight], axis=1)
+        block = block_ref[2 * begin : 2 * begin + 2 * STEP, :]
+        return jnp.dot(weight, block, preferred_element_type=f32)
+
+    row_count = turned_ref.shape[0]
+    for begin in range(0, row_count, STEP):
+        high, low = kernel_parts(turned_ref[begin : begin + STEP, :], center)
+        block_ref[2 * begin : 2 * begin + STEP, :] = high
+        block_ref[2 * begin + STEP : 2 * begin + 2 * STEP, :] = low
+        if begin > 0:
+            total += fold(begin - STEP)
+    out_ref[...] = unstack3(total + fold(row_count - STEP))
 
 
 def turned_body(columns_ref, center_ref, block_ref):
@@ -141,25 +148,27 @@
 def apply_rows(scaled, turned_ref, slots_ref, out_ref):
     stacked = stack3(scaled)
     stacked = jnp.concatenate([stacked, stacked], axis=1)
+    value = jnp.dot(stacked, turned_ref[...], preferred_element_type=f32)
+    own = jnp.where(slot_mask(slots_ref[...]), unstack3(value), 0.0)
+    own = jnp.sum(own, axis=0, keepdims=True)
     for turn, begin in enumerate(range(0, turned_ref.shape[1], CHUNK)):
-        here = slice(begin, begin + CHUNK)
-        value = jnp.dot(stacked, turned_ref[:, here], preferred_element_type=f32)
-        own = jnp.where(slot_mask(slots_ref[:, here]), unstack3(value), 0.0)
-        out_ref[turn : turn + 1, 0:CHUNK] = jnp.sum(own, axis=0, keepdims=True)
+        out_ref[turn : turn + 1, 0:CHUNK] = own[:, begin : begin + CHUNK]
 
 
 def fold_rows(row_weights, block_ref, slots_ref, out_ref):
     count = block_ref.shape[1]
-    total = jnp.zeros((24, count), f32)
     square = jnp.zeros((SLOTS, 1), f32)
+    weights = []
     for turn, begin in enumerate(range(0, slots_ref.shape[1], CHUNK)):
         mask = slot_mask(slots_ref[:, begin : begin + CHUNK])
         weight = jnp.where(mask, row_weights(turn), 0.0)
         square += row_sum(weight * weight)
         weight = stack3(weight)
-        weight = jnp.concatenate([weight, weight], axis=1)
-        block = block_ref[2 * begin : 2 * begin + 2 * CHUNK, :]
-        total += jnp.dot(weight, block, preferred_element_type=f32)
+        for inner in range(0, CHUNK, STEP):
+            weights += [weight[:, inner : inner + STEP]] * 2
+    total = jnp.dot(
+        jnp.concatenate(weights, axis=1), block_ref[...], preferred_element_type=f32
+    )
     out_ref[:, 0:count] = unstack3(total)
     out_ref[:, count : count + EXTRA] = jnp.broadcast_to(square, (SLOTS, EXTRA))
 
@@ -291,11 +300,10 @@
             center_scale.reshape(1, count),
         )
     ]
-    features, _, slots, prices, scale, picked = call(
+    features, slots, prices, scale, picked = call(
         pick_body,
         (
             shaped(features.shape, bf16),
-            shaped((1, count), jnp.int32),
             shaped((1, row_count), jnp.int32),
             shaped((1, row_count)),
             shaped((1, count)),
@@ -303,7 +311,11 @@
         ),
         *inputs,
         source=HBM,
-        scratch_shapes=[pltpu.SemaphoreType.DMA((4 + turns,))],
+        scratch_shapes=[
+            pltpu.VMEM((1, count), jnp.int32),
+            pltpu.VMEM((row_count, count), bf16),
+            pltpu.SemaphoreType.DMA((5,)),
+        ],
     )
     centers = exchange(picked, "dp")
     columns, turned_columns, weight = call(

time: 57 us -> 56.1 us (0.984)
  Pallas kernels: 16.2 us -> 15.4 us
    pallas_call x9, Pallas kernels: 16.2 us -> 15.4 us  [call(): pl.pallas_call(body, out_shape=out_shape, in_specs=[source] * len(args),...]
  transfers between devices with their start and end apart: 16 -> 16, of which waited for: 11 -> 11; matrix products, arithmetic and copies ran while one was open for 0% -> 0% of each run, Pallas kernels for 4% -> 5%
where the time goes in v4:
time: 56.1 us; the launch traced here: 56 us
  starting transfers between devices  21.2 us (38%)
  waiting for transfers between devices  18.6 us (33%)
  Pallas kernels  15.4 us (27%)
  between operations  0.71 us (1%)
    ppermute x16, starting transfers between devices, exchange(): parts.append(lax.ppermute(value, axis, pairs))  21.2 us
    ppermute x16, waiting for transfers between devices, exchange(): parts.append(lax.ppermute(value, axis, pairs))  18.6 us
    pallas_call x9, Pallas kernels, call(): pl.pallas_call(body, out_shape=out_shape, in_specs=[source] * len(args),...  15.4 us
  transfers between devices with their start and end apart: 16, of which 11 were waited for; matrix products, arithmetic and copies ran while one was open for 0% of the time, Pallas kernels for 5%

profile of v4, /device:TPU:0, one launch (start us, length us, event | category | flops | bytes accessed | tf_op | source)
XLA Modules:
  0.0 56.0 jit_solution(13095754467425503716)
XLA Ops:
  0.6 2.7 %shard_map.68 = (bf16[64,4096]{1,0:T(8,128)(2,1)S(1)}, s32[1,4096]{1,0:T(1,128)S(1)}, f32[1,4096]{1,0:T(1,128)S(1)}, f32[1,512]{1,0:T(1,128)S(1)}, bf16[64,512]{1,0:T(8,128)(2,1)S(1)}) custom-call(bf16[64,4096]{1,0:T(8,128)(2,1)} %feat_hbm.1, s32[1,512]{1,0:T(1,128)} %bitcast.6, s32[1,4096]{1,0:T(1,128)} %bitcast.4, f32[1,4096]{1,0:T(1,128)} %bitcast.5, ...), custom_call_target="tpu_custom_call" | custom-call | tf_op jit(solution)/shard_map/pallas_call | solution.py:250
  3.3 3.0 %collective-permute-start = (bf16[64,512]{1,0:T(8,128)(2,1)S(1)}, bf16[64,512]{1,0:T(8,128)(2,1)S(1)}, u32[]{:S(2)}, u32[]{:S(2)}) collective-permute-start(bf16[64,512]{1,0:T(8,128)(2,1)S(1)} %get-tuple-element.27.refs_0_), channel_id=1, source_target_pairs={{0,16},{16,0},{1,17},{17,1},{2,18},{18,2},{3,19},{19,3},{4,20},{20... | collective-permute-start | bytes 196616 | tf_op jit(solution)/shard_map/ppermute | solution.py:273
  6.3 0.7 %shard_map.69 = (bf16[256,4096]{1,0:T(8,128)(2,1)S(1)}, bf16[4096,256]{1,0:T(8,128)(2,1)S(1)}, bf16[24,4096]{1,0:T(8,128)(2,1)S(1)}) custom-call(bf16[64,4096]{1,0:T(8,128)(2,1)S(1)} %get-tuple-element.22.feat_ref, s32[1,4096]{1,0:T(1,128)S(1)} %get-tuple-element.23.slots_ref.refs_3_.refs_4_, f32[1,4096]{1,0:T(1,128)S(1)} %get-tuple-element.24.prices_ref), custom_call_target="tpu_custom_call" | custom-call | flops 4096000 | bytes 4194304 | tf_op jit(solution)/shard_map/pallas_call | solution.py:250
  7.0 1.6 %collective-permute-done.refs_1_ = bf16[64,512]{1,0:T(8,128)(2,1)S(1)} collective-permute-done((bf16[64,512]{1,0:T(8,128)(2,1)S(1)}, bf16[64,512]{1,0:T(8,128)(2,1)S(1)}, u32[]{:S(2)}, u32[]{:S(2)}) %collective-permute-start) | collective-permute-done | bytes 65568 | tf_op jit(solution)/shard_map/ppermute | solution.py:273
  8.6 3.1 %shard_map.70 = (bf16[8192,512]{1,0:T(8,128)(2,1)S(1)}, bf16[256,512]{1,0:T(8,128)(2,1)S(1)}, f32[8,512]{1,0:T(8,128)S(1)}) custom-call(bf16[4096,256]{1,0:T(8,128)(2,1)S(1)} %get-tuple-element.25.turned_ref, bf16[24,4096]{1,0:T(8,128)(2,1)S(1)} %get-tuple-element.26.weight_ref, bf16[64,512]{1,0:T(8,128)(2,1)S(1)} %get-tuple-element.27.refs_0_, ...), custom_call_target="tpu_custom_call" | custom-call | flops 134217728 | bytes 8388608 | tf_op jit(solution)/shard_map/pallas_call | solution.py:250
  11.7 2.0 %collective-permute-start.1 = (f32[8,512]{1,0:T(8,128)S(1)}, f32[8,512]{1,0:T(8,128)S(1)}, u32[]{:S(2)}, u32[]{:S(2)}) collective-permute-start(f32[8,512]{1,0:T(8,128)S(1)} %get-tuple-element.28.refs_0_), channel_id=1, source_target_pairs={{0,16},{16,0},{1,17},{17,1},{2,18},{18,2},{3,19},{19,3},{4,20},{20... | collective-permute-start | bytes 49160 | tf_op jit(solution)/shard_map/ppermute | solution.py:273
  13.7 1.9 %shard_map.71.refs_4_ = bf16[1024,4096]{1,0:T(8,128)(2,1)S(1)} custom-call(bf16[256,4096]{1,0:T(8,128)(2,1)S(1)} %get-tuple-element.30.columns_ref, bf16[256,512]{1,0:T(8,128)(2,1)S(1)} %get-tuple-element.31.center_ref), custom_call_target="tpu_custom_call" | custom-call | flops 134217728 | bytes 8388608 | tf_op jit(solution)/shard_map/pallas_call | solution.py:250
  15.6 0.0 collective-permute-done.1.refs_1_
  15.6 1.6 %shard_map.72 = (f32[8,512]{1,0:T(8,128)S(1)}, f32[8,640]{1,0:T(8,128)S(1)}) custom-call(f32[8,512]{1,0:T(8,128)S(1)} %get-tuple-element.28.refs_0_, f32[8,512]{1,0:T(8,128)S(1)} %collective-permute-done.1.refs_1_, f32[1,512]{1,0:T(1,128)S(1)} %get-tuple-element.29.refs_2_, s32[1,4096]{1,0:T(1,128)S(1)} %get-tuple-element.23.slots_ref.refs_3_.refs_4_, ...), custom_call_target="tpu_custom_call" | custom-call | tf_op jit(solution)/shard_map/pallas_call | solution.py:250
  17.2 0.1 collective-permute-start.2
  17.3 1.9 %collective-permute-start.3 = (f32[8,640]{1,0:T(8,128)S(1)}, f32[8,640]{1,0:T(8,128)S(1)}, u32[]{:S(2)}, u32[]{:S(2)}) collective-permute-start(f32[8,640]{1,0:T(8,128)S(1)} %get-tuple-element.32), channel_id=1, source_target_pairs={{0,2},{1,3},{2,0},{3,1},{4,6},{5,7},{6,4},{7,5},{8,10},{9,11},{10,... | collective-permute-start | bytes 61448 | tf_op jit(solution)/shard_map/ppermute | solution.py:273
  19.2 0.1 collective-permute-start.4
  19.2 0.0 collective-permute-done.2
  19.2 1.9 %collective-permute-done.3 = f32[8,640]{1,0:T(8,128)S(1)} collective-permute-done((f32[8,640]{1,0:T(8,128)S(1)}, f32[8,640]{1,0:T(8,128)S(1)}, u32[]{:S(2)}, u32[]{:S(2)}) %collective-permute-start.3) | collective-permute-done | bytes 20512 | tf_op jit(solution)/shard_map/ppermute | solution.py:273
  21.1 1.2 %collective-permute-done.4 = f32[8,640]{1,0:T(8,128)S(1)} collective-permute-done((f32[8,640]{1,0:T(8,128)S(1)}, f32[8,640]{1,0:T(8,128)S(1)}, u32[]{:S(2)}, u32[]{:S(2)}) %collective-permute-start.4) | collective-permute-done | bytes 20512 | tf_op jit(solution)/shard_map/ppermute | solution.py:273
  22.4 1.6 %collective-permute-start.5 = (f32[8,640]{1,0:T(8,128)S(1)}, f32[8,640]{1,0:T(8,128)S(1)}, u32[]{:S(2)}, u32[]{:S(2)}) collective-permute-start(f32[8,640]{1,0:T(8,128)S(1)} %add_add_fusion.1.refs_0_), channel_id=1, source_target_pairs={{0,4},{1,5},{2,6},{3,7},{4,0},{5,1},{6,2},{7,3},{8,12},{9,13},{10,... | collective-permute-start | bytes 61448 | tf_op jit(solution)/shard_map/ppermute | solution.py:273
  24.0 2.6 %collective-permute-start.6 = (f32[8,640]{1,0:T(8,128)S(1)}, f32[8,640]{1,0:T(8,128)S(1)}, u32[]{:S(2)}, u32[]{:S(2)}) collective-permute-start(f32[8,640]{1,0:T(8,128)S(1)} %add_add_fusion.1.refs_0_), channel_id=1, source_target_pairs={{0,8},{1,9},{2,10},{3,11},{4,12},{5,13},{6,14},{7,15},{8,0},{9,1},... | collective-permute-start | bytes 61448 | tf_op jit(solution)/shard_map/ppermute | solution.py:273
  26.6 0.2 collective-permute-start.7
  26.8 0.0 collective-permute-done.5.refs_1_
  26.8 2.1 %collective-permute-done.6.refs_2_ = f32[8,640]{1,0:T(8,128)S(1)} collective-permute-done((f32[8,640]{1,0:T(8,128)S(1)}, f32[8,640]{1,0:T(8,128)S(1)}, u32[]{:S(2)}, u32[]{:S(2)}) %collective-permute-start.6) | collective-permute-done | bytes 20512 | tf_op jit(solution)/shard_map/ppermute | solution.py:273
  28.9 3.3 %collective-permute-done.7.refs_3_ = f32[8,640]{1,0:T(8,128)S(1)} collective-permute-done((f32[8,640]{1,0:T(8,128)S(1)}, f32[8,640]{1,0:T(8,128)S(1)}, u32[]{:S(2)}, u32[]{:S(2)}) %collective-permute-start.7) | collective-permute-done | bytes 20512 | tf_op jit(solution)/shard_map/ppermute | solution.py:273
  32.2 1.5 %shard_map.73 = (f32[8,640]{1,0:T(8,128)S(1)}, f32[8,640]{1,0:T(8,128)S(1)}) custom-call(f32[8,640]{1,0:T(8,128)S(1)} %add_add_fusion.1.refs_0_, f32[8,640]{1,0:T(8,128)S(1)} %collective-permute-done.5.refs_1_, f32[8,640]{1,0:T(8,128)S(1)} %collective-permute-done.6.refs_2_, f32[8,640]{1,0:T(8,128)S(1)} %collective-permute-done.7.refs_3_, ...), custom_call_target="tpu_custom_call" | custom-call | tf_op jit(solution)/shard_map/pallas_call | solution.py:250
  33.7 1.5 %collective-permute-start.8 = (f32[8,640]{1,0:T(8,128)S(1)}, f32[8,640]{1,0:T(8,128)S(1)}, u32[]{:S(2)}, u32[]{:S(2)}) collective-permute-start(f32[8,640]{1,0:T(8,128)S(1)} %get-tuple-element.34.refs_0_), channel_id=1, source_target_pairs={{0,16},{16,0},{1,17},{17,1},{2,18},{18,2},{3,19},{19,3},{4,20},{20... | collective-permute-start | bytes 61448 | tf_op jit(solution)/shard_map/ppermute | solution.py:273
  35.2 2.3 %collective-permute-done.8.refs_1_ = f32[8,640]{1,0:T(8,128)S(1)} collective-permute-done((f32[8,640]{1,0:T(8,128)S(1)}, f32[8,640]{1,0:T(8,128)S(1)}, u32[]{:S(2)}, u32[]{:S(2)}) %collective-permute-start.8) | collective-permute-done | bytes 20512 | tf_op jit(solution)/shard_map/ppermute | solution.py:273
  37.5 1.6 %shard_map.74 = (f32[8,512]{1,0:T(8,128)S(1)}, f32[8,128]{1,0:T(8,128)S(1)}, f32[8,640]{1,0:T(8,128)S(1)}) custom-call(f32[8,640]{1,0:T(8,128)S(1)} %get-tuple-element.34.refs_0_, f32[8,640]{1,0:T(8,128)S(1)} %collective-permute-done.8.refs_1_, f32[1,512]{1,0:T(1,128)S(1)} %get-tuple-element.29.refs_2_, ...), custom_call_target="tpu_custom_call" | custom-call | tf_op jit(solution)/shard_map/pallas_call | solution.py:250
  39.1 0.8 %collective-permute-start.10 = (f32[8,640]{1,0:T(8,128)S(1)}, f32[8,640]{1,0:T(8,128)S(1)}, u32[]{:S(2)}, u32[]{:S(2)}) collective-permute-start(f32[8,640]{1,0:T(8,128)S(1)} %get-tuple-element.37), channel_id=1, source_target_pairs={{0,2},{1,3},{2,0},{3,1},{4,6},{5,7},{6,4},{7,5},{8,10},{9,11},{10,... | collective-permute-start | bytes 61448 | tf_op jit(solution)/shard_map/ppermute | solution.py:273
  40.0 0.0 collective-permute-start.11
  40.0 1.4 %collective-permute-start.9 = (f32[8,640]{1,0:T(8,128)S(1)}, f32[8,640]{1,0:T(8,128)S(1)}, u32[]{:S(2)}, u32[]{:S(2)}) collective-permute-start(f32[8,640]{1,0:T(8,128)S(1)} %get-tuple-element.37), channel_id=1, source_target_pairs={{0,1},{1,0},{2,3},{3,2},{4,5},{5,4},{6,7},{7,6},{8,9},{9,8},{10,11... | collective-permute-start | bytes 61448 | tf_op jit(solution)/shard_map/ppermute | solution.py:273
  41.4 1.7 %collective-permute-done.10 = f32[8,640]{1,0:T(8,128)S(1)} collective-permute-done((f32[8,640]{1,0:T(8,128)S(1)}, f32[8,640]{1,0:T(8,128)S(1)}, u32[]{:S(2)}, u32[]{:S(2)}) %collective-permute-start.10) | collective-permute-done | bytes 20512 | tf_op jit(solution)/shard_map/ppermute | solution.py:273
  43.1 0.3 collective-permute-done.11
  43.4 0.0 collective-permute-done.9
  43.4 0.1 collective-permute-start.12
  43.5 0.8 %collective-permute-start.13 = (f32[8,640]{1,0:T(8,128)S(1)}, f32[8,640]{1,0:T(8,128)S(1)}, u32[]{:S(2)}, u32[]{:S(2)}) collective-permute-start(f32[8,640]{1,0:T(8,128)S(1)} %add_add_fusion.refs_0_), channel_id=1, source_target_pairs={{0,8},{1,9},{2,10},{3,11},{4,12},{5,13},{6,14},{7,15},{8,0},{9,1},... | collective-permute-start | bytes 61448 | tf_op jit(solution)/shard_map/ppermute | solution.py:273
  44.2 3.6 %collective-permute-start.14 = (f32[8,640]{1,0:T(8,128)S(1)}, f32[8,640]{1,0:T(8,128)S(1)}, u32[]{:S(2)}, u32[]{:S(2)}) collective-permute-start(f32[8,640]{1,0:T(8,128)S(1)} %add_add_fusion.refs_0_), channel_id=1, source_target_pairs={{0,12},{1,13},{2,14},{3,15},{4,8},{5,9},{6,10},{7,11},{8,4},{9,5},... | collective-permute-start | bytes 61448 | tf_op jit(solution)/shard_map/ppermute | solution.py:273
  47.8 0.0 collective-permute-done.12.refs_1_
  47.8 0.4 collective-permute-done.13.refs_2_
  48.2 1.6 %collective-permute-done.14.refs_3_ = f32[8,640]{1,0:T(8,128)S(1)} collective-permute-done((f32[8,640]{1,0:T(8,128)S(1)}, f32[8,640]{1,0:T(8,128)S(1)}, u32[]{:S(2)}, u32[]{:S(2)}) %collective-permute-start.14) | collective-permute-done | bytes 20512 | tf_op jit(solution)/shard_map/ppermute | solution.py:273
  49.8 1.6 %shard_map.75 = (f32[8,128]{1,0:T(8,128)S(1)}, f32[8,640]{1,0:T(8,128)S(1)}) custom-call(f32[8,640]{1,0:T(8,128)S(1)} %add_add_fusion.refs_0_, f32[8,640]{1,0:T(8,128)S(1)} %collective-permute-done.12.refs_1_, f32[8,640]{1,0:T(8,128)S(1)} %collective-permute-done.13.refs_2_, f32[8,640]{1,0:T(8,128)S(1)} %collective-permute-done.14.refs_3_, ...), custom_call_target="tpu_custom_call" | custom-call | tf_op jit(solution)/shard_map/pallas_call | solution.py:250
  51.4 1.5 %collective-permute-start.15 = (f32[8,640]{1,0:T(8,128)S(1)}, f32[8,640]{1,0:T(8,128)S(1)}, u32[]{:S(2)}, u32[]{:S(2)}) collective-permute-start(f32[8,640]{1,0:T(8,128)S(1)} %get-tuple-element.38.refs_0_), channel_id=1, source_target_pairs={{0,16},{16,0},{1,17},{17,1},{2,18},{18,2},{3,19},{19,3},{4,20},{20... | collective-permute-start | bytes 61448 | tf_op jit(solution)/shard_map/ppermute | solution.py:273
  52.9 2.3 %collective-permute-done.15.refs_1_ = f32[8,640]{1,0:T(8,128)S(1)} collective-permute-done((f32[8,640]{1,0:T(8,128)S(1)}, f32[8,640]{1,0:T(8,128)S(1)}, u32[]{:S(2)}, u32[]{:S(2)}) %collective-permute-start.15) | collective-permute-done | bytes 20512 | tf_op jit(solution)/shard_map/ppermute | solution.py:273
  55.2 0.8 %shard_map.76 = (f32[8,512]{1,0:T(8,128)}, f32[8,512]{1,0:T(8,128)}) custom-call(f32[8,640]{1,0:T(8,128)S(1)} %get-tuple-element.38.refs_0_, f32[8,640]{1,0:T(8,128)S(1)} %collective-permute-done.15.refs_1_, f32[1,512]{1,0:T(1,128)S(1)} %get-tuple-element.29.refs_2_, f32[8,512]{1,0:T(8,128)S(1)} %get-tuple-element.35.refs_5_.refs_3_, ...), custom_call_target="tpu_custom_call" | custom-call | tf_op jit(solution)/shard_map/pallas_call | solution.py:250
  (2 shorter events, 0.0 us)
Async XLA Ops:
  3.3 5.3 %collective-permute-start = (bf16[64,512]{1,0:T(8,128)(2,1)S(1)}, bf16[64,512]{1,0:T(8,128)(2,1)S(1)}, u32[]{:S(2)}, u32[]{:S(2)}) collective-permute-start(bf16[64,512]{1,0:T(8,128)(2,1)S(1)} %get-tuple-element.27.refs_0_), channel_id=1, source_target_pairs={{0,16},{16,0},{1,17},{17,1},{2,18},{18,2},{3,19},{19,3},{4,20},{20... | collective-permute-start | bytes 196616 | tf_op jit(solution)/shard_map/ppermute | solution.py:273
  11.7 4.0 %collective-permute-start.1 = (f32[8,512]{1,0:T(8,128)S(1)}, f32[8,512]{1,0:T(8,128)S(1)}, u32[]{:S(2)}, u32[]{:S(2)}) collective-permute-start(f32[8,512]{1,0:T(8,128)S(1)} %get-tuple-element.28.refs_0_), channel_id=1, source_target_pairs={{0,16},{16,0},{1,17},{17,1},{2,18},{18,2},{3,19},{19,3},{4,20},{20... | collective-permute-start | bytes 49160 | tf_op jit(solution)/shard_map/ppermute | solution.py:273
  17.2 2.0 %collective-permute-start.2 = (f32[8,640]{1,0:T(8,128)S(1)}, f32[8,640]{1,0:T(8,128)S(1)}, u32[]{:S(2)}, u32[]{:S(2)}) collective-permute-start(f32[8,640]{1,0:T(8,128)S(1)} %get-tuple-element.32), channel_id=1, source_target_pairs={{0,1},{1,0},{2,3},{3,2},{4,5},{5,4},{6,7},{7,6},{8,9},{9,8},{10,11... | collective-permute-start | bytes 61448 | tf_op jit(solution)/shard_map/ppermute | solution.py:273
  17.3 3.8 %collective-permute-start.3 = (f32[8,640]{1,0:T(8,128)S(1)}, f32[8,640]{1,0:T(8,128)S(1)}, u32[]{:S(2)}, u32[]{:S(2)}) collective-permute-start(f32[8,640]{1,0:T(8,128)S(1)} %get-tuple-element.32), channel_id=1, source_target_pairs={{0,2},{1,3},{2,0},{3,1},{4,6},{5,7},{6,4},{7,5},{8,10},{9,11},{10,... | collective-permute-start | bytes 61448 | tf_op jit(solution)/shard_map/ppermute | solution.py:273
  19.2 3.2 %collective-permute-start.4 = (f32[8,640]{1,0:T(8,128)S(1)}, f32[8,640]{1,0:T(8,128)S(1)}, u32[]{:S(2)}, u32[]{:S(2)}) collective-permute-start(f32[8,640]{1,0:T(8,128)S(1)} %get-tuple-element.32), channel_id=1, source_target_pairs={{0,3},{1,2},{2,1},{3,0},{4,7},{5,6},{6,5},{7,4},{8,11},{9,10},{10,... | collective-permute-start | bytes 61448 | tf_op jit(solution)/shard_map/ppermute | solution.py:273
  22.4 4.5 %collective-permute-start.5 = (f32[8,640]{1,0:T(8,128)S(1)}, f32[8,640]{1,0:T(8,128)S(1)}, u32[]{:S(2)}, u32[]{:S(2)}) collective-permute-start(f32[8,640]{1,0:T(8,128)S(1)} %add_add_fusion.1.refs_0_), channel_id=1, source_target_pairs={{0,4},{1,5},{2,6},{3,7},{4,0},{5,1},{6,2},{7,3},{8,12},{9,13},{10,... | collective-permute-start | bytes 61448 | tf_op jit(solution)/shard_map/ppermute | solution.py:273
  24.0 4.9 %collective-permute-start.6 = (f32[8,640]{1,0:T(8,128)S(1)}, f32[8,640]{1,0:T(8,128)S(1)}, u32[]{:S(2)}, u32[]{:S(2)}) collective-permute-start(f32[8,640]{1,0:T(8,128)S(1)} %add_add_fusion.1.refs_0_), channel_id=1, source_target_pairs={{0,8},{1,9},{2,10},{3,11},{4,12},{5,13},{6,14},{7,15},{8,0},{9,1},... | collective-permute-start | bytes 61448 | tf_op jit(solution)/shard_map/ppermute | solution.py:273
  26.6 5.6 %collective-permute-start.7 = (f32[8,640]{1,0:T(8,128)S(1)}, f32[8,640]{1,0:T(8,128)S(1)}, u32[]{:S(2)}, u32[]{:S(2)}) collective-permute-start(f32[8,640]{1,0:T(8,128)S(1)} %add_add_fusion.1.refs_0_), channel_id=1, source_target_pairs={{0,12},{1,13},{2,14},{3,15},{4,8},{5,9},{6,10},{7,11},{8,4},{9,5},... | collective-permute-start | bytes 61448 | tf_op jit(solution)/shard_map/ppermute | solution.py:273
  33.7 3.8 %collective-permute-start.8 = (f32[8,640]{1,0:T(8,128)S(1)}, f32[8,640]{1,0:T(8,128)S(1)}, u32[]{:S(2)}, u32[]{:S(2)}) collective-permute-start(f32[8,640]{1,0:T(8,128)S(1)} %get-tuple-element.34.refs_0_), channel_id=1, source_target_pairs={{0,16},{16,0},{1,17},{17,1},{2,18},{18,2},{3,19},{19,3},{4,20},{20... | collective-permute-start | bytes 61448 | tf_op jit(solution)/shard_map/ppermute | solution.py:273
  39.1 3.9 %collective-permute-start.10 = (f32[8,640]{1,0:T(8,128)S(1)}, f32[8,640]{1,0:T(8,128)S(1)}, u32[]{:S(2)}, u32[]{:S(2)}) collective-permute-start(f32[8,640]{1,0:T(8,128)S(1)} %get-tuple-element.37), channel_id=1, source_target_pairs={{0,2},{1,3},{2,0},{3,1},{4,6},{5,7},{6,4},{7,5},{8,10},{9,11},{10,... | collective-permute-start | bytes 61448 | tf_op jit(solution)/shard_map/ppermute | solution.py:273
  40.0 3.4 %collective-permute-start.11 = (f32[8,640]{1,0:T(8,128)S(1)}, f32[8,640]{1,0:T(8,128)S(1)}, u32[]{:S(2)}, u32[]{:S(2)}) collective-permute-start(f32[8,640]{1,0:T(8,128)S(1)} %get-tuple-element.37), channel_id=1, source_target_pairs={{0,3},{1,2},{2,1},{3,0},{4,7},{5,6},{6,5},{7,4},{8,11},{9,10},{10,... | collective-permute-start | bytes 61448 | tf_op jit(solution)/shard_map/ppermute | solution.py:273
  40.0 3.4 %collective-permute-start.9 = (f32[8,640]{1,0:T(8,128)S(1)}, f32[8,640]{1,0:T(8,128)S(1)}, u32[]{:S(2)}, u32[]{:S(2)}) collective-permute-start(f32[8,640]{1,0:T(8,128)S(1)} %get-tuple-element.37), channel_id=1, source_target_pairs={{0,1},{1,0},{2,3},{3,2},{4,5},{5,4},{6,7},{7,6},{8,9},{9,8},{10,11... | collective-permute-start | bytes 61448 | tf_op jit(solution)/shard_map/ppermute | solution.py:273
  43.4 4.5 %collective-permute-start.12 = (f32[8,640]{1,0:T(8,128)S(1)}, f32[8,640]{1,0:T(8,128)S(1)}, u32[]{:S(2)}, u32[]{:S(2)}) collective-permute-start(f32[8,640]{1,0:T(8,128)S(1)} %add_add_fusion.refs_0_), channel_id=1, source_target_pairs={{0,4},{1,5},{2,6},{3,7},{4,0},{5,1},{6,2},{7,3},{8,12},{9,13},{10,... | collective-permute-start | bytes 61448 | tf_op jit(solution)/shard_map/ppermute | solution.py:273
  43.5 4.7 %collective-permute-start.13 = (f32[8,640]{1,0:T(8,128)S(1)}, f32[8,640]{1,0:T(8,128)S(1)}, u32[]{:S(2)}, u32[]{:S(2)}) collective-permute-start(f32[8,640]{1,0:T(8,128)S(1)} %add_add_fusion.refs_0_), channel_id=1, source_target_pairs={{0,8},{1,9},{2,10},{3,11},{4,12},{5,13},{6,14},{7,15},{8,0},{9,1},... | collective-permute-start | bytes 61448 | tf_op jit(solution)/shard_map/ppermute | solution.py:273
  44.2 5.6 %collective-permute-start.14 = (f32[8,640]{1,0:T(8,128)S(1)}, f32[8,640]{1,0:T(8,128)S(1)}, u32[]{:S(2)}, u32[]{:S(2)}) collective-permute-start(f32[8,640]{1,0:T(8,128)S(1)} %add_add_fusion.refs_0_), channel_id=1, source_target_pairs={{0,12},{1,13},{2,14},{3,15},{4,8},{5,9},{6,10},{7,11},{8,4},{9,5},... | collective-permute-start | bytes 61448 | tf_op jit(solution)/shard_map/ppermute | solution.py:273
  51.4 3.8 %collective-permute-start.15 = (f32[8,640]{1,0:T(8,128)S(1)}, f32[8,640]{1,0:T(8,128)S(1)}, u32[]{:S(2)}, u32[]{:S(2)}) collective-permute-start(f32[8,640]{1,0:T(8,128)S(1)} %get-tuple-element.38.refs_0_), channel_id=1, source_target_pairs={{0,16},{16,0},{1,17},{17,1},{2,18},{18,2},{3,19},{19,3},{4,20},{20... | collective-permute-start | bytes 61448 | tf_op jit(solution)/shard_map/ppermute | solution.py:273

commit v5 on v4

--- a/solution.py
+++ b/solution.py
@@ -84,14 +84,24 @@
         copy.start()
     copies[0].wait()
     local_idx = idx_ref[...] - lax.axis_index("dp") * row_count
-    for begin in range(0, row_count, CHUNK):
-        row = lax.broadcasted_iota(jnp.int32, (CHUNK, count), 0)
-        hit = jnp.where(row == local_idx - begin, 1.0, 0.0)
-        hit_ref[begin : begin + CHUNK, :] = hit.astype(bf16)
+    row = lax.broadcasted_iota(jnp.int32, (STEP, count), 0).astype(f32).astype(bf16)
+    block = lax.div(local_idx, STEP)
+    place = (local_idx - block * STEP).astype(f32)
+
+    def hits(begin):
+        own = jnp.where(block == begin // STEP, place, -1.0).astype(bf16)
+        return jnp.where(row == own, jnp.ones_like(row), jnp.zeros_like(row))
+
+    half = row_count // 2
+    for begin in range(0, half, STEP):
+        hit_ref[begin : begin + STEP, :] = hits(begin)
     copies[1].wait()
-    out_ref[...] = jnp.dot(
-        feat_ref[...], hit_ref[...], preferred_element_type=f32
-    ).astype(bf16)
+    total = jnp.dot(feat_ref[:, :half], hit_ref[...], preferred_element_type=f32)
+    for begin in range(half, row_count, STEP):
+        total += jnp.dot(
+            feat_ref[:, begin : begin + STEP], hits(begin), preferred_element_type=f32
+        )
+    out_ref[...] = total.astype(bf16)
     for copy in copies[2:]:
         copy.wait()
 
@@ -268,9 +278,12 @@
         value = pair_total(parts)
         parts = [value]
         span = min(4, size // stride)
-        for offset in range(1, span):
-            pairs = [(i, i ^ (offset * stride)) for i in range(size)]
-            parts.append(lax.ppermute(value, axis, pairs))
+        side = 0 if stride == 1 else 1
+        got = []
+        for offset in reversed(range(1, span)):
+            pairs = [(i, i ^ (offset * stride) ^ side) for i in range(size)]
+            got.append(lax.ppermute(value, axis, pairs))
+        parts = got + parts
         stride *= span
     return parts
 
@@ -313,7 +326,7 @@
         source=HBM,
         scratch_shapes=[
             pltpu.VMEM((1, count), jnp.int32),
-            pltpu.VMEM((row_count, count), bf16),
+            pltpu.VMEM((row_count // 2, count), bf16),
             pltpu.SemaphoreType.DMA((5,)),
         ],
     )

time: 56.1 us -> 52.1 us (0.929)
  waiting for transfers between devices: 18.6 us -> 15.3 us
  Pallas kernels: 15.4 us -> 14.7 us
    ppermute x16, waiting for transfers between devices: 18.6 us -> 15.3 us  [exchange(): got.append(lax.ppermute(value, axis, pairs))]
    pallas_call x9, Pallas kernels: 15.4 us -> 14.7 us  [call(): pl.pallas_call(body, out_shape=out_shape, in_specs=[source] * len(args),...]
where the time goes in v5:
time: 52.1 us; the launch traced here: 51.9 us
  starting transfers between devices  21.2 us (41%)
  waiting for transfers between devices  15.3 us (29%)
  Pallas kernels  14.7 us (28%)
  between operations  0.7 us (1%)
    ppermute x16, starting transfers between devices, exchange(): got.append(lax.ppermute(value, axis, pairs))  21.2 us
    ppermute x16, waiting for transfers between devices, exchange(): got.append(lax.ppermute(value, axis, pairs))  15.3 us
    pallas_call x9, Pallas kernels, call(): pl.pallas_call(body, out_shape=out_shape, in_specs=[source] * len(args),...  14.7 us
  transfers between devices with their start and end apart: 16, of which 11 were waited for; matrix products, arithmetic and copies ran while one was open for 0% of the time, Pallas kernels for 5%

profile of v5, /device:TPU:0, one launch (start us, length us, event | category | flops | bytes accessed | tf_op | source)
XLA Modules:
  0.0 51.9 jit_solution(1336569121271179579)
XLA Ops:
  0.6 2.0 %shard_map.68 = (bf16[64,4096]{1,0:T(8,128)(2,1)S(1)}, s32[1,4096]{1,0:T(1,128)S(1)}, f32[1,4096]{1,0:T(1,128)S(1)}, f32[1,512]{1,0:T(1,128)S(1)}, bf16[64,512]{1,0:T(8,128)(2,1)S(1)}) custom-call(bf16[64,4096]{1,0:T(8,128)(2,1)} %feat_hbm.1, s32[1,512]{1,0:T(1,128)} %bitcast.6, s32[1,4096]{1,0:T(1,128)} %bitcast.4, f32[1,4096]{1,0:T(1,128)} %bitcast.5, ...), custom_call_target="tpu_custom_call" | custom-call | tf_op jit(solution)/shard_map/pallas_call | solution.py:260
  2.6 3.0 %collective-permute-start = (bf16[64,512]{1,0:T(8,128)(2,1)S(1)}, bf16[64,512]{1,0:T(8,128)(2,1)S(1)}, u32[]{:S(2)}, u32[]{:S(2)}) collective-permute-start(bf16[64,512]{1,0:T(8,128)(2,1)S(1)} %get-tuple-element.27.refs_1_), channel_id=1, source_target_pairs={{0,16},{16,0},{1,17},{17,1},{2,18},{18,2},{3,19},{19,3},{4,20},{20... | collective-permute-start | bytes 196616 | tf_op jit(solution)/shard_map/ppermute | solution.py:285
  5.6 0.7 %shard_map.69 = (bf16[256,4096]{1,0:T(8,128)(2,1)S(1)}, bf16[4096,256]{1,0:T(8,128)(2,1)S(1)}, bf16[24,4096]{1,0:T(8,128)(2,1)S(1)}) custom-call(bf16[64,4096]{1,0:T(8,128)(2,1)S(1)} %get-tuple-element.22.feat_ref, s32[1,4096]{1,0:T(1,128)S(1)} %get-tuple-element.23.slots_ref.refs_3_.refs_4_, f32[1,4096]{1,0:T(1,128)S(1)} %get-tuple-element.24.prices_ref), custom_call_target="tpu_custom_call" | custom-call | flops 4096000 | bytes 4194304 | tf_op jit(solution)/shard_map/pallas_call | solution.py:260
  6.3 1.6 %collective-permute-done.refs_0_ = bf16[64,512]{1,0:T(8,128)(2,1)S(1)} collective-permute-done((bf16[64,512]{1,0:T(8,128)(2,1)S(1)}, bf16[64,512]{1,0:T(8,128)(2,1)S(1)}, u32[]{:S(2)}, u32[]{:S(2)}) %collective-permute-start) | collective-permute-done | bytes 65568 | tf_op jit(solution)/shard_map/ppermute | solution.py:285
  7.8 3.1 %shard_map.70 = (bf16[8192,512]{1,0:T(8,128)(2,1)S(1)}, bf16[256,512]{1,0:T(8,128)(2,1)S(1)}, f32[8,512]{1,0:T(8,128)S(1)}) custom-call(bf16[4096,256]{1,0:T(8,128)(2,1)S(1)} %get-tuple-element.25.turned_ref, bf16[24,4096]{1,0:T(8,128)(2,1)S(1)} %get-tuple-element.26.weight_ref, bf16[64,512]{1,0:T(8,128)(2,1)S(1)} %collective-permute-done.refs_0_, ...), custom_call_target="tpu_custom_call" | custom-call | flops 134217728 | bytes 8388608 | tf_op jit(solution)/shard_map/pallas_call | solution.py:260
  10.9 2.0 %collective-permute-start.1 = (f32[8,512]{1,0:T(8,128)S(1)}, f32[8,512]{1,0:T(8,128)S(1)}, u32[]{:S(2)}, u32[]{:S(2)}) collective-permute-start(f32[8,512]{1,0:T(8,128)S(1)} %get-tuple-element.28.refs_1_), channel_id=1, source_target_pairs={{0,16},{16,0},{1,17},{17,1},{2,18},{18,2},{3,19},{19,3},{4,20},{20... | collective-permute-start | bytes 49160 | tf_op jit(solution)/shard_map/ppermute | solution.py:285
  13.0 1.9 %shard_map.71.refs_4_ = bf16[1024,4096]{1,0:T(8,128)(2,1)S(1)} custom-call(bf16[256,4096]{1,0:T(8,128)(2,1)S(1)} %get-tuple-element.30.columns_ref, bf16[256,512]{1,0:T(8,128)(2,1)S(1)} %get-tuple-element.31.center_ref), custom_call_target="tpu_custom_call" | custom-call | flops 134217728 | bytes 8388608 | tf_op jit(solution)/shard_map/pallas_call | solution.py:260
  14.9 0.0 collective-permute-done.1.refs_0_
  14.9 1.6 %shard_map.72 = (f32[8,512]{1,0:T(8,128)S(1)}, f32[8,640]{1,0:T(8,128)S(1)}) custom-call(f32[8,512]{1,0:T(8,128)S(1)} %collective-permute-done.1.refs_0_, f32[8,512]{1,0:T(8,128)S(1)} %get-tuple-element.28.refs_1_, f32[1,512]{1,0:T(1,128)S(1)} %get-tuple-element.29.refs_2_, s32[1,4096]{1,0:T(1,128)S(1)} %get-tuple-element.23.slots_ref.refs_3_.refs_4_, ...), custom_call_target="tpu_custom_call" | custom-call | tf_op jit(solution)/shard_map/pallas_call | solution.py:260
  16.5 0.1 collective-permute-start.2
  16.6 1.9 %collective-permute-start.3 = (f32[8,640]{1,0:T(8,128)S(1)}, f32[8,640]{1,0:T(8,128)S(1)}, u32[]{:S(2)}, u32[]{:S(2)}) collective-permute-start(f32[8,640]{1,0:T(8,128)S(1)} %get-tuple-element.32), channel_id=1, source_target_pairs={{0,2},{1,3},{2,0},{3,1},{4,6},{5,7},{6,4},{7,5},{8,10},{9,11},{10,... | collective-permute-start | bytes 61448 | tf_op jit(solution)/shard_map/ppermute | solution.py:285
  18.5 0.0 collective-permute-start.4
  18.5 1.3 %collective-permute-done.2 = f32[8,640]{1,0:T(8,128)S(1)} collective-permute-done((f32[8,640]{1,0:T(8,128)S(1)}, f32[8,640]{1,0:T(8,128)S(1)}, u32[]{:S(2)}, u32[]{:S(2)}) %collective-permute-start.2) | collective-permute-done | bytes 20512 | tf_op jit(solution)/shard_map/ppermute | solution.py:285
  19.8 0.7 %collective-permute-done.3 = f32[8,640]{1,0:T(8,128)S(1)} collective-permute-done((f32[8,640]{1,0:T(8,128)S(1)}, f32[8,640]{1,0:T(8,128)S(1)}, u32[]{:S(2)}, u32[]{:S(2)}) %collective-permute-start.3) | collective-permute-done | bytes 20512 | tf_op jit(solution)/shard_map/ppermute | solution.py:285
  20.4 0.0 collective-permute-done.4
  20.4 4.0 %collective-permute-start.5 = (f32[8,640]{1,0:T(8,128)S(1)}, f32[8,640]{1,0:T(8,128)S(1)}, u32[]{:S(2)}, u32[]{:S(2)}) collective-permute-start(f32[8,640]{1,0:T(8,128)S(1)} %add_add_fusion.1.refs_3_), channel_id=1, source_target_pairs={{0,13},{1,12},{2,15},{3,14},{4,9},{5,8},{6,11},{7,10},{8,5},{9,4},... | collective-permute-start | bytes 61448 | tf_op jit(solution)/shard_map/ppermute | solution.py:285
  24.4 0.0 collective-permute-start.6
  24.4 0.5 collective-permute-start.7
  24.9 1.0 %collective-permute-done.5.refs_0_ = f32[8,640]{1,0:T(8,128)S(1)} collective-permute-done((f32[8,640]{1,0:T(8,128)S(1)}, f32[8,640]{1,0:T(8,128)S(1)}, u32[]{:S(2)}, u32[]{:S(2)}) %collective-permute-start.5) | collective-permute-done | bytes 20512 | tf_op jit(solution)/shard_map/ppermute | solution.py:285
  25.9 2.6 %collective-permute-done.6.refs_1_ = f32[8,640]{1,0:T(8,128)S(1)} collective-permute-done((f32[8,640]{1,0:T(8,128)S(1)}, f32[8,640]{1,0:T(8,128)S(1)}, u32[]{:S(2)}, u32[]{:S(2)}) %collective-permute-start.6) | collective-permute-done | bytes 20512 | tf_op jit(solution)/shard_map/ppermute | solution.py:285
  28.5 0.0 collective-permute-done.7.refs_2_
  28.5 1.5 %shard_map.73 = (f32[8,640]{1,0:T(8,128)S(1)}, f32[8,640]{1,0:T(8,128)S(1)}) custom-call(f32[8,640]{1,0:T(8,128)S(1)} %collective-permute-done.5.refs_0_, f32[8,640]{1,0:T(8,128)S(1)} %collective-permute-done.6.refs_1_, f32[8,640]{1,0:T(8,128)S(1)} %collective-permute-done.7.refs_2_, f32[8,640]{1,0:T(8,128)S(1)} %add_add_fusion.1.refs_3_, ...), custom_call_target="tpu_custom_call" | custom-call | tf_op jit(solution)/shard_map/pallas_call | solution.py:260
  30.1 1.5 %collective-permute-start.8 = (f32[8,640]{1,0:T(8,128)S(1)}, f32[8,640]{1,0:T(8,128)S(1)}, u32[]{:S(2)}, u32[]{:S(2)}) collective-permute-start(f32[8,640]{1,0:T(8,128)S(1)} %get-tuple-element.34.refs_1_), channel_id=1, source_target_pairs={{0,16},{16,0},{1,17},{17,1},{2,18},{18,2},{3,19},{19,3},{4,20},{20... | collective-permute-start | bytes 61448 | tf_op jit(solution)/shard_map/ppermute | solution.py:285
  31.6 2.3 %collective-permute-done.8.refs_0_ = f32[8,640]{1,0:T(8,128)S(1)} collective-permute-done((f32[8,640]{1,0:T(8,128)S(1)}, f32[8,640]{1,0:T(8,128)S(1)}, u32[]{:S(2)}, u32[]{:S(2)}) %collective-permute-start.8) | collective-permute-done | bytes 20512 | tf_op jit(solution)/shard_map/ppermute | solution.py:285
  33.9 1.6 %shard_map.74 = (f32[8,512]{1,0:T(8,128)S(1)}, f32[8,128]{1,0:T(8,128)S(1)}, f32[8,640]{1,0:T(8,128)S(1)}) custom-call(f32[8,640]{1,0:T(8,128)S(1)} %collective-permute-done.8.refs_0_, f32[8,640]{1,0:T(8,128)S(1)} %get-tuple-element.34.refs_1_, f32[1,512]{1,0:T(1,128)S(1)} %get-tuple-element.29.refs_2_, ...), custom_call_target="tpu_custom_call" | custom-call | tf_op jit(solution)/shard_map/pallas_call | solution.py:260
  35.5 0.8 %collective-permute-start.10 = (f32[8,640]{1,0:T(8,128)S(1)}, f32[8,640]{1,0:T(8,128)S(1)}, u32[]{:S(2)}, u32[]{:S(2)}) collective-permute-start(f32[8,640]{1,0:T(8,128)S(1)} %get-tuple-element.37), channel_id=1, source_target_pairs={{0,2},{1,3},{2,0},{3,1},{4,6},{5,7},{6,4},{7,5},{8,10},{9,11},{10,... | collective-permute-start | bytes 61448 | tf_op jit(solution)/shard_map/ppermute | solution.py:285
  36.3 0.0 collective-permute-start.11
  36.3 1.4 %collective-permute-start.9 = (f32[8,640]{1,0:T(8,128)S(1)}, f32[8,640]{1,0:T(8,128)S(1)}, u32[]{:S(2)}, u32[]{:S(2)}) collective-permute-start(f32[8,640]{1,0:T(8,128)S(1)} %get-tuple-element.37), channel_id=1, source_target_pairs={{0,3},{1,2},{2,1},{3,0},{4,7},{5,6},{6,5},{7,4},{8,11},{9,10},{10,... | collective-permute-start | bytes 61448 | tf_op jit(solution)/shard_map/ppermute | solution.py:285
  37.7 1.7 %collective-permute-done.10 = f32[8,640]{1,0:T(8,128)S(1)} collective-permute-done((f32[8,640]{1,0:T(8,128)S(1)}, f32[8,640]{1,0:T(8,128)S(1)}, u32[]{:S(2)}, u32[]{:S(2)}) %collective-permute-start.10) | collective-permute-done | bytes 20512 | tf_op jit(solution)/shard_map/ppermute | solution.py:285
  39.4 0.0 collective-permute-done.11
  39.4 0.1 collective-permute-done.9
  39.6 2.0 %collective-permute-start.12 = (f32[8,640]{1,0:T(8,128)S(1)}, f32[8,640]{1,0:T(8,128)S(1)}, u32[]{:S(2)}, u32[]{:S(2)}) collective-permute-start(f32[8,640]{1,0:T(8,128)S(1)} %add_add_fusion.refs_3_), channel_id=1, source_target_pairs={{0,13},{1,12},{2,15},{3,14},{4,9},{5,8},{6,11},{7,10},{8,5},{9,4},... | collective-permute-start | bytes 61448 | tf_op jit(solution)/shard_map/ppermute | solution.py:285
  41.5 0.7 %collective-permute-start.13 = (f32[8,640]{1,0:T(8,128)S(1)}, f32[8,640]{1,0:T(8,128)S(1)}, u32[]{:S(2)}, u32[]{:S(2)}) collective-permute-start(f32[8,640]{1,0:T(8,128)S(1)} %add_add_fusion.refs_3_), channel_id=1, source_target_pairs={{0,9},{1,8},{2,11},{3,10},{4,13},{5,12},{6,15},{7,14},{8,1},{9,0},... | collective-permute-start | bytes 61448 | tf_op jit(solution)/shard_map/ppermute | solution.py:285
  42.3 1.5 %collective-permute-start.14 = (f32[8,640]{1,0:T(8,128)S(1)}, f32[8,640]{1,0:T(8,128)S(1)}, u32[]{:S(2)}, u32[]{:S(2)}) collective-permute-start(f32[8,640]{1,0:T(8,128)S(1)} %add_add_fusion.refs_3_), channel_id=1, source_target_pairs={{0,5},{1,4},{2,7},{3,6},{4,1},{5,0},{6,3},{7,2},{8,13},{9,12},{10,... | collective-permute-start | bytes 61448 | tf_op jit(solution)/shard_map/ppermute | solution.py:285
  43.8 0.8 %collective-permute-done.12.refs_0_ = f32[8,640]{1,0:T(8,128)S(1)} collective-permute-done((f32[8,640]{1,0:T(8,128)S(1)}, f32[8,640]{1,0:T(8,128)S(1)}, u32[]{:S(2)}, u32[]{:S(2)}) %collective-permute-start.12) | collective-permute-done | bytes 20512 | tf_op jit(solution)/shard_map/ppermute | solution.py:285
  44.6 1.1 %collective-permute-done.13.refs_1_ = f32[8,640]{1,0:T(8,128)S(1)} collective-permute-done((f32[8,640]{1,0:T(8,128)S(1)}, f32[8,640]{1,0:T(8,128)S(1)}, u32[]{:S(2)}, u32[]{:S(2)}) %collective-permute-start.13) | collective-permute-done | bytes 20512 | tf_op jit(solution)/shard_map/ppermute | solution.py:285
  45.8 0.0 collective-permute-done.14.refs_2_
  45.8 1.6 %shard_map.75 = (f32[8,128]{1,0:T(8,128)S(1)}, f32[8,640]{1,0:T(8,128)S(1)}) custom-call(f32[8,640]{1,0:T(8,128)S(1)} %collective-permute-done.12.refs_0_, f32[8,640]{1,0:T(8,128)S(1)} %collective-permute-done.13.refs_1_, f32[8,640]{1,0:T(8,128)S(1)} %collective-permute-done.14.refs_2_, f32[8,640]{1,0:T(8,128)S(1)} %add_add_fusion.refs_3_, ...), custom_call_target="tpu_custom_call" | custom-call | tf_op jit(solution)/shard_map/pallas_call | solution.py:260
  47.4 1.7 %collective-permute-start.15 = (f32[8,640]{1,0:T(8,128)S(1)}, f32[8,640]{1,0:T(8,128)S(1)}, u32[]{:S(2)}, u32[]{:S(2)}) collective-permute-start(f32[8,640]{1,0:T(8,128)S(1)} %get-tuple-element.38.refs_1_), channel_id=1, source_target_pairs={{0,16},{16,0},{1,17},{17,1},{2,18},{18,2},{3,19},{19,3},{4,20},{20... | collective-permute-start | bytes 61448 | tf_op jit(solution)/shard_map/ppermute | solution.py:285
  49.1 2.1 %collective-permute-done.15.refs_0_ = f32[8,640]{1,0:T(8,128)S(1)} collective-permute-done((f32[8,640]{1,0:T(8,128)S(1)}, f32[8,640]{1,0:T(8,128)S(1)}, u32[]{:S(2)}, u32[]{:S(2)}) %collective-permute-start.15) | collective-permute-done | bytes 20512 | tf_op jit(solution)/shard_map/ppermute | solution.py:285
  51.2 0.8 %shard_map.76 = (f32[8,512]{1,0:T(8,128)}, f32[8,512]{1,0:T(8,128)}) custom-call(f32[8,640]{1,0:T(8,128)S(1)} %collective-permute-done.15.refs_0_, f32[8,640]{1,0:T(8,128)S(1)} %get-tuple-element.38.refs_1_, f32[1,512]{1,0:T(1,128)S(1)} %get-tuple-element.29.refs_2_, f32[8,512]{1,0:T(8,128)S(1)} %get-tuple-element.35.refs_5_.refs_3_, ...), custom_call_target="tpu_custom_call" | custom-call | tf_op jit(solution)/shard_map/pallas_call | solution.py:260
  (2 shorter events, 0.0 us)
Async XLA Ops:
  2.6 5.2 %collective-permute-start = (bf16[64,512]{1,0:T(8,128)(2,1)S(1)}, bf16[64,512]{1,0:T(8,128)(2,1)S(1)}, u32[]{:S(2)}, u32[]{:S(2)}) collective-permute-start(bf16[64,512]{1,0:T(8,128)(2,1)S(1)} %get-tuple-element.27.refs_1_), channel_id=1, source_target_pairs={{0,16},{16,0},{1,17},{17,1},{2,18},{18,2},{3,19},{19,3},{4,20},{20... | collective-permute-start | bytes 196616 | tf_op jit(solution)/shard_map/ppermute | solution.py:285
  10.9 4.0 %collective-permute-start.1 = (f32[8,512]{1,0:T(8,128)S(1)}, f32[8,512]{1,0:T(8,128)S(1)}, u32[]{:S(2)}, u32[]{:S(2)}) collective-permute-start(f32[8,512]{1,0:T(8,128)S(1)} %get-tuple-element.28.refs_1_), channel_id=1, source_target_pairs={{0,16},{16,0},{1,17},{17,1},{2,18},{18,2},{3,19},{19,3},{4,20},{20... | collective-permute-start | bytes 49160 | tf_op jit(solution)/shard_map/ppermute | solution.py:285
  16.5 3.3 %collective-permute-start.2 = (f32[8,640]{1,0:T(8,128)S(1)}, f32[8,640]{1,0:T(8,128)S(1)}, u32[]{:S(2)}, u32[]{:S(2)}) collective-permute-start(f32[8,640]{1,0:T(8,128)S(1)} %get-tuple-element.32), channel_id=1, source_target_pairs={{0,3},{1,2},{2,1},{3,0},{4,7},{5,6},{6,5},{7,4},{8,11},{9,10},{10,... | collective-permute-start | bytes 61448 | tf_op jit(solution)/shard_map/ppermute | solution.py:285
  16.6 3.8 %collective-permute-start.3 = (f32[8,640]{1,0:T(8,128)S(1)}, f32[8,640]{1,0:T(8,128)S(1)}, u32[]{:S(2)}, u32[]{:S(2)}) collective-permute-start(f32[8,640]{1,0:T(8,128)S(1)} %get-tuple-element.32), channel_id=1, source_target_pairs={{0,2},{1,3},{2,0},{3,1},{4,6},{5,7},{6,4},{7,5},{8,10},{9,11},{10,... | collective-permute-start | bytes 61448 | tf_op jit(solution)/shard_map/ppermute | solution.py:285
  18.5 2.0 %collective-permute-start.4 = (f32[8,640]{1,0:T(8,128)S(1)}, f32[8,640]{1,0:T(8,128)S(1)}, u32[]{:S(2)}, u32[]{:S(2)}) collective-permute-start(f32[8,640]{1,0:T(8,128)S(1)} %get-tuple-element.32), channel_id=1, source_target_pairs={{0,1},{1,0},{2,3},{3,2},{4,5},{5,4},{6,7},{7,6},{8,9},{9,8},{10,11... | collective-permute-start | bytes 61448 | tf_op jit(solution)/shard_map/ppermute | solution.py:285
  20.4 5.5 %collective-permute-start.5 = (f32[8,640]{1,0:T(8,128)S(1)}, f32[8,640]{1,0:T(8,128)S(1)}, u32[]{:S(2)}, u32[]{:S(2)}) collective-permute-start(f32[8,640]{1,0:T(8,128)S(1)} %add_add_fusion.1.refs_3_), channel_id=1, source_target_pairs={{0,13},{1,12},{2,15},{3,14},{4,9},{5,8},{6,11},{7,10},{8,5},{9,4},... | collective-permute-start | bytes 61448 | tf_op jit(solution)/shard_map/ppermute | solution.py:285
  24.4 4.1 %collective-permute-start.6 = (f32[8,640]{1,0:T(8,128)S(1)}, f32[8,640]{1,0:T(8,128)S(1)}, u32[]{:S(2)}, u32[]{:S(2)}) collective-permute-start(f32[8,640]{1,0:T(8,128)S(1)} %add_add_fusion.1.refs_3_), channel_id=1, source_target_pairs={{0,9},{1,8},{2,11},{3,10},{4,13},{5,12},{6,15},{7,14},{8,1},{9,0},... | collective-permute-start | bytes 61448 | tf_op jit(solution)/shard_map/ppermute | solution.py:285
  24.4 4.1 %collective-permute-start.7 = (f32[8,640]{1,0:T(8,128)S(1)}, f32[8,640]{1,0:T(8,128)S(1)}, u32[]{:S(2)}, u32[]{:S(2)}) collective-permute-start(f32[8,640]{1,0:T(8,128)S(1)} %add_add_fusion.1.refs_3_), channel_id=1, source_target_pairs={{0,5},{1,4},{2,7},{3,6},{4,1},{5,0},{6,3},{7,2},{8,13},{9,12},{10,... | collective-permute-start | bytes 61448 | tf_op jit(solution)/shard_map/ppermute | solution.py:285
  30.1 3.8 %collective-permute-start.8 = (f32[8,640]{1,0:T(8,128)S(1)}, f32[8,640]{1,0:T(8,128)S(1)}, u32[]{:S(2)}, u32[]{:S(2)}) collective-permute-start(f32[8,640]{1,0:T(8,128)S(1)} %get-tuple-element.34.refs_1_), channel_id=1, source_target_pairs={{0,16},{16,0},{1,17},{17,1},{2,18},{18,2},{3,19},{19,3},{4,20},{20... | collective-permute-start | bytes 61448 | tf_op jit(solution)/shard_map/ppermute | solution.py:285
  35.5 3.9 %collective-permute-start.10 = (f32[8,640]{1,0:T(8,128)S(1)}, f32[8,640]{1,0:T(8,128)S(1)}, u32[]{:S(2)}, u32[]{:S(2)}) collective-permute-start(f32[8,640]{1,0:T(8,128)S(1)} %get-tuple-element.37), channel_id=1, source_target_pairs={{0,2},{1,3},{2,0},{3,1},{4,6},{5,7},{6,4},{7,5},{8,10},{9,11},{10,... | collective-permute-start | bytes 61448 | tf_op jit(solution)/shard_map/ppermute | solution.py:285
  36.3 3.2 %collective-permute-start.11 = (f32[8,640]{1,0:T(8,128)S(1)}, f32[8,640]{1,0:T(8,128)S(1)}, u32[]{:S(2)}, u32[]{:S(2)}) collective-permute-start(f32[8,640]{1,0:T(8,128)S(1)} %get-tuple-element.37), channel_id=1, source_target_pairs={{0,1},{1,0},{2,3},{3,2},{4,5},{5,4},{6,7},{7,6},{8,9},{9,8},{10,11... | collective-permute-start | bytes 61448 | tf_op jit(solution)/shard_map/ppermute | solution.py:285
  36.3 3.3 %collective-permute-start.9 = (f32[8,640]{1,0:T(8,128)S(1)}, f32[8,640]{1,0:T(8,128)S(1)}, u32[]{:S(2)}, u32[]{:S(2)}) collective-permute-start(f32[8,640]{1,0:T(8,128)S(1)} %get-tuple-element.37), channel_id=1, source_target_pairs={{0,3},{1,2},{2,1},{3,0},{4,7},{5,6},{6,5},{7,4},{8,11},{9,10},{10,... | collective-permute-start | bytes 61448 | tf_op jit(solution)/shard_map/ppermute | solution.py:285
  39.6 5.1 %collective-permute-start.12 = (f32[8,640]{1,0:T(8,128)S(1)}, f32[8,640]{1,0:T(8,128)S(1)}, u32[]{:S(2)}, u32[]{:S(2)}) collective-permute-start(f32[8,640]{1,0:T(8,128)S(1)} %add_add_fusion.refs_3_), channel_id=1, source_target_pairs={{0,13},{1,12},{2,15},{3,14},{4,9},{5,8},{6,11},{7,10},{8,5},{9,4},... | collective-permute-start | bytes 61448 | tf_op jit(solution)/shard_map/ppermute | solution.py:285
  41.5 4.2 %collective-permute-start.13 = (f32[8,640]{1,0:T(8,128)S(1)}, f32[8,640]{1,0:T(8,128)S(1)}, u32[]{:S(2)}, u32[]{:S(2)}) collective-permute-start(f32[8,640]{1,0:T(8,128)S(1)} %add_add_fusion.refs_3_), channel_id=1, source_target_pairs={{0,9},{1,8},{2,11},{3,10},{4,13},{5,12},{6,15},{7,14},{8,1},{9,0},... | collective-permute-start | bytes 61448 | tf_op jit(solution)/shard_map/ppermute | solution.py:285
  42.3 3.5 %collective-permute-start.14 = (f32[8,640]{1,0:T(8,128)S(1)}, f32[8,640]{1,0:T(8,128)S(1)}, u32[]{:S(2)}, u32[]{:S(2)}) collective-permute-start(f32[8,640]{1,0:T(8,128)S(1)} %add_add_fusion.refs_3_), channel_id=1, source_target_pairs={{0,5},{1,4},{2,7},{3,6},{4,1},{5,0},{6,3},{7,2},{8,13},{9,12},{10,... | collective-permute-start | bytes 61448 | tf_op jit(solution)/shard_map/ppermute | solution.py:285
  47.4 3.8 %collective-permute-start.15 = (f32[8,640]{1,0:T(8,128)S(1)}, f32[8,640]{1,0:T(8,128)S(1)}, u32[]{:S(2)}, u32[]{:S(2)}) collective-permute-start(f32[8,640]{1,0:T(8,128)S(1)} %get-tuple-element.38.refs_1_), channel_id=1, source_target_pairs={{0,16},{16,0},{1,17},{17,1},{2,18},{18,2},{3,19},{19,3},{4,20},{20... | collective-permute-start | bytes 61448 | tf_op jit(solution)/shard_map/ppermute | solution.py:285

commit v6 on v5

--- a/solution.py
+++ b/solution.py
@@ -28,12 +28,13 @@
     return high, mid, rest - mid
 
 
-def stack3(value):
-    return jnp.concatenate(split3(value), axis=0).astype(bf16)
-
-
-def unstack3(value):
-    return value[0:8] + (value[8:16] + value[16:24])
+def stack2(value):
+    high = value.astype(bf16).astype(f32)
+    return jnp.concatenate([high, value - high], axis=0).astype(bf16)
+
+
+def unstack2(value):
+    return value[0:8] + value[8:16]
 
 
 def pair_total(parts):
@@ -117,7 +118,7 @@
         turned_ref[here, 0:128] = pair.T.astype(bf16)
         turned_ref[here, 128:256] = last.T.astype(bf16)
         weight = jnp.where(slot_mask(slots_ref[:, here]), prices_ref[:, here], 0.0)
-        weight_ref[:, here] = stack3(weight)
+        weight_ref[:, here] = stack2(weight)
 
 
 def rows_body(parts, turned_ref, weight_ref, *refs):
@@ -127,22 +128,28 @@
         [*split3(center * FACTOR), norm_rows(center, 0)], axis=0
     ).astype(bf16)
     center_ref[...] = center
-    total = jnp.zeros((24, center.shape[1]), f32)
+    total = jnp.zeros((16, center.shape[1]), f32)
+
+    def build(begin):
+        high, low = kernel_parts(turned_ref[pl.ds(begin, STEP), :], center)
+        block_ref[pl.ds(2 * begin, STEP), :] = high
+        block_ref[pl.ds(2 * begin + STEP, STEP), :] = low
 
     def fold(begin):
-        weight = weight_ref[:, begin : begin + STEP]
+        weight = weight_ref[:, pl.ds(begin, STEP)]
         weight = jnp.concatenate([weight, weight], axis=1)
-        block = block_ref[2 * begin : 2 * begin + 2 * STEP, :]
+        block = block_ref[pl.ds(2 * begin, 2 * STEP), :]
         return jnp.dot(weight, block, preferred_element_type=f32)
 
+    def visit(turn, total):
+        begin = pl.multiple_of(turn * STEP, STEP)
+        build(begin)
+        return total + fold(pl.multiple_of(begin - STEP, STEP))
+
     row_count = turned_ref.shape[0]
-    for begin in range(0, row_count, STEP):
-        high, low = kernel_parts(turned_ref[begin : begin + STEP, :], center)
-        block_ref[2 * begin : 2 * begin + STEP, :] = high
-        block_ref[2 * begin + STEP : 2 * begin + 2 * STEP, :] = low
-        if begin > 0:
-            total += fold(begin - STEP)
-    out_ref[...] = unstack3(total + fold(row_count - STEP))
+    build(0)
+    total = lax.fori_loop(1, row_count // STEP, visit, total)
+    out_ref[...] = unstack2(total + fold(row_count - STEP))
 
 
 def turned_body(columns_ref, center_ref, block_ref):
@@ -156,10 +163,10 @@
 
 
 def apply_rows(scaled, turned_ref, slots_ref, out_ref):
-    stacked = stack3(scaled)
+    stacked = stack2(scaled)
     stacked = jnp.concatenate([stacked, stacked], axis=1)
     value = jnp.dot(stacked, turned_ref[...], preferred_element_type=f32)
-    own = jnp.where(slot_mask(slots_ref[...]), unstack3(value), 0.0)
+    own = jnp.where(slot_mask(slots_ref[...]), unstack2(value), 0.0)
     own = jnp.sum(own, axis=0, keepdims=True)
     for turn, begin in enumerate(range(0, turned_ref.shape[1], CHUNK)):
         out_ref[turn : turn + 1, 0:CHUNK] = own[:, begin : begin + CHUNK]
@@ -173,13 +180,13 @@
         mask = slot_mask(slots_ref[:, begin : begin + CHUNK])
         weight = jnp.where(mask, row_weights(turn), 0.0)
         square += row_sum(weight * weight)
-        weight = stack3(weight)
+        weight = stack2(weight)
         for inner in range(0, CHUNK, STEP):
             weights += [weight[:, inner : inner + STEP]] * 2
     total = jnp.dot(
         jnp.concatenate(weights, axis=1), block_ref[...], preferred_element_type=f32
     )
-    out_ref[:, 0:count] = unstack3(total)
+    out_ref[:, 0:count] = unstack2(total)
     out_ref[:, count : count + EXTRA] = jnp.broadcast_to(square, (SLOTS, EXTRA))
 
 
@@ -270,7 +277,7 @@
     )(*args)
 
 
-def exchange(value, axis):
+def exchange(value, axis, near_first=False):
     size = lax.axis_size(axis)
     parts = [value]
     stride = 1
@@ -284,6 +291,8 @@
             pairs = [(i, i ^ (offset * stride) ^ side) for i in range(size)]
             got.append(lax.ppermute(value, axis, pairs))
         parts = got + parts
+        if near_first and stride == 1:
+            parts = parts[-2:] + parts[:-2]
         stride *= span
     return parts
 
@@ -336,7 +345,7 @@
         (
             shaped((DEPTH, row_count), bf16),
             shaped((row_count, DEPTH), bf16),
-            shaped((24, row_count), bf16),
+            shaped((16, row_count), bf16),
         ),
         features, slots, prices,
         flops=1000 * row_count,
@@ -367,7 +376,7 @@
         (vector, narrow, row_shape),
         *folds, scale, slots, turned, target, rows,
     )
-    latest = exchange(latest, "centers")
+    latest = exchange(latest, "centers", True)
     sums, folded = call(
         partial(second_fold_body, len(latest)),
         (narrow, fold_shape),

time: 52.1 us -> 54.2 us (1.040)
  Pallas kernels: 14.7 us -> 17.6 us
  starting transfers between devices: 21.2 us -> 20 us
    pallas_call x9, Pallas kernels: 14.7 us -> 17.6 us  [call(): pl.pallas_call(body, out_shape=out_shape, in_specs=[source] * len(args),...]
    ppermute x16, starting transfers between devices: 21.2 us -> 20 us  [exchange(): got.append(lax.ppermute(value, axis, pairs))]
where the time goes in v6:
time: 54.2 us; the launch traced here: 54 us
  starting transfers between devices  20 us (37%)
  Pallas kernels  17.6 us (32%)
  waiting for transfers between devices  15.7 us (29%)
  between operations  0.71 us (1%)
    ppermute x16, starting transfers between devices, exchange(): got.append(lax.ppermute(value, axis, pairs))  20 us
    pallas_call x9, Pallas kernels, call(): pl.pallas_call(body, out_shape=out_shape, in_specs=[source] * len(args),...  17.6 us
    ppermute x16, waiting for transfers between devices, exchange(): got.append(lax.ppermute(value, axis, pairs))  15.7 us
  transfers between devices with their start and end apart: 16, of which 11 were waited for; matrix products, arithmetic and copies ran while one was open for 0% of the time, Pallas kernels for 5%

profile of v6, /device:TPU:0, one launch (start us, length us, event | category | flops | bytes accessed | tf_op | source)
XLA Modules:
  0.0 54.0 jit_solution(18104025242378727051)
XLA Ops:
  0.6 2.0 %shard_map.68 = (bf16[64,4096]{1,0:T(8,128)(2,1)S(1)}, s32[1,4096]{1,0:T(1,128)S(1)}, f32[1,4096]{1,0:T(1,128)S(1)}, f32[1,512]{1,0:T(1,128)S(1)}, bf16[64,512]{1,0:T(8,128)(2,1)S(1)}) custom-call(bf16[64,4096]{1,0:T(8,128)(2,1)} %feat_hbm.1, s32[1,512]{1,0:T(1,128)} %bitcast.6, s32[1,4096]{1,0:T(1,128)} %bitcast.4, f32[1,4096]{1,0:T(1,128)} %bitcast.5, ...), custom_call_target="tpu_custom_call" | custom-call | tf_op jit(solution)/shard_map/pallas_call | solution.py:267
  2.6 3.0 %collective-permute-start = (bf16[64,512]{1,0:T(8,128)(2,1)S(1)}, bf16[64,512]{1,0:T(8,128)(2,1)S(1)}, u32[]{:S(2)}, u32[]{:S(2)}) collective-permute-start(bf16[64,512]{1,0:T(8,128)(2,1)S(1)} %get-tuple-element.27.refs_1_), channel_id=1, source_target_pairs={{0,16},{16,0},{1,17},{17,1},{2,18},{18,2},{3,19},{19,3},{4,20},{20... | collective-permute-start | bytes 196616 | tf_op jit(solution)/shard_map/ppermute | solution.py:292
  5.6 0.7 %shard_map.69 = (bf16[256,4096]{1,0:T(8,128)(2,1)S(1)}, bf16[4096,256]{1,0:T(8,128)(2,1)S(1)}, bf16[16,4096]{1,0:T(8,128)(2,1)S(1)}) custom-call(bf16[64,4096]{1,0:T(8,128)(2,1)S(1)} %get-tuple-element.22.feat_ref, s32[1,4096]{1,0:T(1,128)S(1)} %get-tuple-element.23.slots_ref.refs_3_.refs_4_, f32[1,4096]{1,0:T(1,128)S(1)} %get-tuple-element.24.prices_ref), custom_call_target="tpu_custom_call" | custom-call | flops 4096000 | bytes 4194304 | tf_op jit(solution)/shard_map/pallas_call | solution.py:267
  6.3 1.6 %collective-permute-done.refs_0_ = bf16[64,512]{1,0:T(8,128)(2,1)S(1)} collective-permute-done((bf16[64,512]{1,0:T(8,128)(2,1)S(1)}, bf16[64,512]{1,0:T(8,128)(2,1)S(1)}, u32[]{:S(2)}, u32[]{:S(2)}) %collective-permute-start) | collective-permute-done | bytes 65568 | tf_op jit(solution)/shard_map/ppermute | solution.py:292
  7.8 7.4 %shard_map.70 = (bf16[8192,512]{1,0:T(8,128)(2,1)S(1)}, bf16[256,512]{1,0:T(8,128)(2,1)S(1)}, f32[8,512]{1,0:T(8,128)S(1)}) custom-call(bf16[4096,256]{1,0:T(8,128)(2,1)S(1)} %get-tuple-element.25.turned_ref, bf16[16,4096]{1,0:T(8,128)(2,1)S(1)} %get-tuple-element.26.weight_ref, bf16[64,512]{1,0:T(8,128)(2,1)S(1)} %collective-permute-done.refs_0_, ...), custom_call_target="tpu_custom_call" | custom-call | flops 134217728 | bytes 8388608 | tf_op jit(solution)/shard_map/pallas_call | solution.py:267
  15.2 1.9 %collective-permute-start.1 = (f32[8,512]{1,0:T(8,128)S(1)}, f32[8,512]{1,0:T(8,128)S(1)}, u32[]{:S(2)}, u32[]{:S(2)}) collective-permute-start(f32[8,512]{1,0:T(8,128)S(1)} %get-tuple-element.28.refs_1_), channel_id=1, source_target_pairs={{0,16},{16,0},{1,17},{17,1},{2,18},{18,2},{3,19},{19,3},{4,20},{20... | collective-permute-start | bytes 49160 | tf_op jit(solution)/shard_map/ppermute | solution.py:292
  17.2 1.9 %shard_map.71.refs_4_ = bf16[1024,4096]{1,0:T(8,128)(2,1)S(1)} custom-call(bf16[256,4096]{1,0:T(8,128)(2,1)S(1)} %get-tuple-element.30.columns_ref, bf16[256,512]{1,0:T(8,128)(2,1)S(1)} %get-tuple-element.31.center_ref), custom_call_target="tpu_custom_call" | custom-call | flops 134217728 | bytes 8388608 | tf_op jit(solution)/shard_map/pallas_call | solution.py:267
  19.1 0.0 collective-permute-done.1.refs_0_
  19.1 1.2 %shard_map.72 = (f32[8,512]{1,0:T(8,128)S(1)}, f32[8,640]{1,0:T(8,128)S(1)}) custom-call(f32[8,512]{1,0:T(8,128)S(1)} %collective-permute-done.1.refs_0_, f32[8,512]{1,0:T(8,128)S(1)} %get-tuple-element.28.refs_1_, f32[1,512]{1,0:T(1,128)S(1)} %get-tuple-element.29.refs_2_, s32[1,4096]{1,0:T(1,128)S(1)} %get-tuple-element.23.slots_ref.refs_3_.refs_4_, ...), custom_call_target="tpu_custom_call" | custom-call | tf_op jit(solution)/shard_map/pallas_call | solution.py:267
  20.3 0.1 collective-permute-start.2
  20.4 1.9 %collective-permute-start.3 = (f32[8,640]{1,0:T(8,128)S(1)}, f32[8,640]{1,0:T(8,128)S(1)}, u32[]{:S(2)}, u32[]{:S(2)}) collective-permute-start(f32[8,640]{1,0:T(8,128)S(1)} %get-tuple-element.32), channel_id=1, source_target_pairs={{0,2},{1,3},{2,0},{3,1},{4,6},{5,7},{6,4},{7,5},{8,10},{9,11},{10,... | collective-permute-start | bytes 61448 | tf_op jit(solution)/shard_map/ppermute | solution.py:292
  22.3 0.0 collective-permute-start.4
  22.3 1.3 %collective-permute-done.2 = f32[8,640]{1,0:T(8,128)S(1)} collective-permute-done((f32[8,640]{1,0:T(8,128)S(1)}, f32[8,640]{1,0:T(8,128)S(1)}, u32[]{:S(2)}, u32[]{:S(2)}) %collective-permute-start.2) | collective-permute-done | bytes 20512 | tf_op jit(solution)/shard_map/ppermute | solution.py:292
  23.6 0.7 %collective-permute-done.3 = f32[8,640]{1,0:T(8,128)S(1)} collective-permute-done((f32[8,640]{1,0:T(8,128)S(1)}, f32[8,640]{1,0:T(8,128)S(1)}, u32[]{:S(2)}, u32[]{:S(2)}) %collective-permute-start.3) | collective-permute-done | bytes 20512 | tf_op jit(solution)/shard_map/ppermute | solution.py:292
  24.3 0.0 collective-permute-done.4
  24.3 4.0 %collective-permute-start.5 = (f32[8,640]{1,0:T(8,128)S(1)}, f32[8,640]{1,0:T(8,128)S(1)}, u32[]{:S(2)}, u32[]{:S(2)}) collective-permute-start(f32[8,640]{1,0:T(8,128)S(1)} %add_add_fusion.1.refs_3_), channel_id=1, source_target_pairs={{0,13},{1,12},{2,15},{3,14},{4,9},{5,8},{6,11},{7,10},{8,5},{9,4},... | collective-permute-start | bytes 61448 | tf_op jit(solution)/shard_map/ppermute | solution.py:292
  28.3 0.0 collective-permute-start.6
  28.3 0.5 collective-permute-start.7
  28.8 1.0 %collective-permute-done.5.refs_0_ = f32[8,640]{1,0:T(8,128)S(1)} collective-permute-done((f32[8,640]{1,0:T(8,128)S(1)}, f32[8,640]{1,0:T(8,128)S(1)}, u32[]{:S(2)}, u32[]{:S(2)}) %collective-permute-start.5) | collective-permute-done | bytes 20512 | tf_op jit(solution)/shard_map/ppermute | solution.py:292
  29.8 2.6 %collective-permute-done.6.refs_1_ = f32[8,640]{1,0:T(8,128)S(1)} collective-permute-done((f32[8,640]{1,0:T(8,128)S(1)}, f32[8,640]{1,0:T(8,128)S(1)}, u32[]{:S(2)}, u32[]{:S(2)}) %collective-permute-start.6) | collective-permute-done | bytes 20512 | tf_op jit(solution)/shard_map/ppermute | solution.py:292
  32.4 0.0 collective-permute-done.7.refs_2_
  32.4 1.2 %shard_map.73 = (f32[8,640]{1,0:T(8,128)S(1)}, f32[8,640]{1,0:T(8,128)S(1)}) custom-call(f32[8,640]{1,0:T(8,128)S(1)} %collective-permute-done.5.refs_0_, f32[8,640]{1,0:T(8,128)S(1)} %collective-permute-done.6.refs_1_, f32[8,640]{1,0:T(8,128)S(1)} %collective-permute-done.7.refs_2_, f32[8,640]{1,0:T(8,128)S(1)} %add_add_fusion.1.refs_3_, ...), custom_call_target="tpu_custom_call" | custom-call | tf_op jit(solution)/shard_map/pallas_call | solution.py:267
  33.6 1.7 %collective-permute-start.8 = (f32[8,640]{1,0:T(8,128)S(1)}, f32[8,640]{1,0:T(8,128)S(1)}, u32[]{:S(2)}, u32[]{:S(2)}) collective-permute-start(f32[8,640]{1,0:T(8,128)S(1)} %get-tuple-element.34.refs_1_), channel_id=1, source_target_pairs={{0,16},{16,0},{1,17},{17,1},{2,18},{18,2},{3,19},{19,3},{4,20},{20... | collective-permute-start | bytes 61448 | tf_op jit(solution)/shard_map/ppermute | solution.py:292
  35.2 2.1 %collective-permute-done.8.refs_0_ = f32[8,640]{1,0:T(8,128)S(1)} collective-permute-done((f32[8,640]{1,0:T(8,128)S(1)}, f32[8,640]{1,0:T(8,128)S(1)}, u32[]{:S(2)}, u32[]{:S(2)}) %collective-permute-start.8) | collective-permute-done | bytes 20512 | tf_op jit(solution)/shard_map/ppermute | solution.py:292
  37.4 1.3 %shard_map.74 = (f32[8,512]{1,0:T(8,128)S(1)}, f32[8,128]{1,0:T(8,128)S(1)}, f32[8,640]{1,0:T(8,128)S(1)}) custom-call(f32[8,640]{1,0:T(8,128)S(1)} %collective-permute-done.8.refs_0_, f32[8,640]{1,0:T(8,128)S(1)} %get-tuple-element.34.refs_1_, f32[1,512]{1,0:T(1,128)S(1)} %get-tuple-element.29.refs_2_, ...), custom_call_target="tpu_custom_call" | custom-call | tf_op jit(solution)/shard_map/pallas_call | solution.py:267
  38.6 0.5 collective-permute-start.10
  39.1 0.4 collective-permute-start.11
  39.5 1.1 %collective-permute-start.9 = (f32[8,640]{1,0:T(8,128)S(1)}, f32[8,640]{1,0:T(8,128)S(1)}, u32[]{:S(2)}, u32[]{:S(2)}) collective-permute-start(f32[8,640]{1,0:T(8,128)S(1)} %get-tuple-element.37), channel_id=1, source_target_pairs={{0,1},{1,0},{2,3},{3,2},{4,5},{5,4},{6,7},{7,6},{8,9},{9,8},{10,11... | collective-permute-start | bytes 61448 | tf_op jit(solution)/shard_map/ppermute | solution.py:292
  40.6 1.3 %collective-permute-done.10 = f32[8,640]{1,0:T(8,128)S(1)} collective-permute-done((f32[8,640]{1,0:T(8,128)S(1)}, f32[8,640]{1,0:T(8,128)S(1)}, u32[]{:S(2)}, u32[]{:S(2)}) %collective-permute-start.10) | collective-permute-done | bytes 20512 | tf_op jit(solution)/shard_map/ppermute | solution.py:292
  41.9 1.0 %collective-permute-done.11 = f32[8,640]{1,0:T(8,128)S(1)} collective-permute-done((f32[8,640]{1,0:T(8,128)S(1)}, f32[8,640]{1,0:T(8,128)S(1)}, u32[]{:S(2)}, u32[]{:S(2)}) %collective-permute-start.11) | collective-permute-done | bytes 20512 | tf_op jit(solution)/shard_map/ppermute | solution.py:292
  42.9 0.0 collective-permute-done.9
  42.9 1.2 %collective-permute-start.12 = (f32[8,640]{1,0:T(8,128)S(1)}, f32[8,640]{1,0:T(8,128)S(1)}, u32[]{:S(2)}, u32[]{:S(2)}) collective-permute-start(f32[8,640]{1,0:T(8,128)S(1)} %add_add_fusion.refs_3_), channel_id=1, source_target_pairs={{0,13},{1,12},{2,15},{3,14},{4,9},{5,8},{6,11},{7,10},{8,5},{9,4},... | collective-permute-start | bytes 61448 | tf_op jit(solution)/shard_map/ppermute | solution.py:292
  44.1 0.4 collective-permute-start.13
  44.5 1.5 %collective-permute-start.14 = (f32[8,640]{1,0:T(8,128)S(1)}, f32[8,640]{1,0:T(8,128)S(1)}, u32[]{:S(2)}, u32[]{:S(2)}) collective-permute-start(f32[8,640]{1,0:T(8,128)S(1)} %add_add_fusion.refs_3_), channel_id=1, source_target_pairs={{0,5},{1,4},{2,7},{3,6},{4,1},{5,0},{6,3},{7,2},{8,13},{9,12},{10,... | collective-permute-start | bytes 61448 | tf_op jit(solution)/shard_map/ppermute | solution.py:292
  46.0 2.0 %collective-permute-done.12.refs_0_ = f32[8,640]{1,0:T(8,128)S(1)} collective-permute-done((f32[8,640]{1,0:T(8,128)S(1)}, f32[8,640]{1,0:T(8,128)S(1)}, u32[]{:S(2)}, u32[]{:S(2)}) %collective-permute-start.12) | collective-permute-done | bytes 20512 | tf_op jit(solution)/shard_map/ppermute | solution.py:292
  48.0 0.2 collective-permute-done.13.refs_1_
  48.2 0.0 collective-permute-done.14.refs_2_
  48.2 1.2 %shard_map.75 = (f32[8,128]{1,0:T(8,128)S(1)}, f32[8,640]{1,0:T(8,128)S(1)}) custom-call(f32[8,640]{1,0:T(8,128)S(1)} %collective-permute-done.12.refs_0_, f32[8,640]{1,0:T(8,128)S(1)} %collective-permute-done.13.refs_1_, f32[8,640]{1,0:T(8,128)S(1)} %collective-permute-done.14.refs_2_, f32[8,640]{1,0:T(8,128)S(1)} %add_add_fusion.refs_3_, ...), custom_call_target="tpu_custom_call" | custom-call | tf_op jit(solution)/shard_map/pallas_call | solution.py:267
  49.5 1.9 %collective-permute-start.15 = (f32[8,640]{1,0:T(8,128)S(1)}, f32[8,640]{1,0:T(8,128)S(1)}, u32[]{:S(2)}, u32[]{:S(2)}) collective-permute-start(f32[8,640]{1,0:T(8,128)S(1)} %get-tuple-element.38.refs_1_), channel_id=1, source_target_pairs={{0,16},{16,0},{1,17},{17,1},{2,18},{18,2},{3,19},{19,3},{4,20},{20... | collective-permute-start | bytes 61448 | tf_op jit(solution)/shard_map/ppermute | solution.py:292
  51.4 1.9 %collective-permute-done.15.refs_0_ = f32[8,640]{1,0:T(8,128)S(1)} collective-permute-done((f32[8,640]{1,0:T(8,128)S(1)}, f32[8,640]{1,0:T(8,128)S(1)}, u32[]{:S(2)}, u32[]{:S(2)}) %collective-permute-start.15) | collective-permute-done | bytes 20512 | tf_op jit(solution)/shard_map/ppermute | solution.py:292
  53.2 0.8 %shard_map.76 = (f32[8,512]{1,0:T(8,128)}, f32[8,512]{1,0:T(8,128)}) custom-call(f32[8,640]{1,0:T(8,128)S(1)} %collective-permute-done.15.refs_0_, f32[8,640]{1,0:T(8,128)S(1)} %get-tuple-element.38.refs_1_, f32[1,512]{1,0:T(1,128)S(1)} %get-tuple-element.29.refs_2_, f32[8,512]{1,0:T(8,128)S(1)} %get-tuple-element.35.refs_5_.refs_3_, ...), custom_call_target="tpu_custom_call" | custom-call | tf_op jit(solution)/shard_map/pallas_call | solution.py:267
  (2 shorter events, 0.0 us)
Async XLA Ops:
  2.6 5.2 %collective-permute-start = (bf16[64,512]{1,0:T(8,128)(2,1)S(1)}, bf16[64,512]{1,0:T(8,128)(2,1)S(1)}, u32[]{:S(2)}, u32[]{:S(2)}) collective-permute-start(bf16[64,512]{1,0:T(8,128)(2,1)S(1)} %get-tuple-element.27.refs_1_), channel_id=1, source_target_pairs={{0,16},{16,0},{1,17},{17,1},{2,18},{18,2},{3,19},{19,3},{4,20},{20... | collective-permute-start | bytes 196616 | tf_op jit(solution)/shard_map/ppermute | solution.py:292
  15.2 3.8 %collective-permute-start.1 = (f32[8,512]{1,0:T(8,128)S(1)}, f32[8,512]{1,0:T(8,128)S(1)}, u32[]{:S(2)}, u32[]{:S(2)}) collective-permute-start(f32[8,512]{1,0:T(8,128)S(1)} %get-tuple-element.28.refs_1_), channel_id=1, source_target_pairs={{0,16},{16,0},{1,17},{17,1},{2,18},{18,2},{3,19},{19,3},{4,20},{20... | collective-permute-start | bytes 49160 | tf_op jit(solution)/shard_map/ppermute | solution.py:292
  20.3 3.3 %collective-permute-start.2 = (f32[8,640]{1,0:T(8,128)S(1)}, f32[8,640]{1,0:T(8,128)S(1)}, u32[]{:S(2)}, u32[]{:S(2)}) collective-permute-start(f32[8,640]{1,0:T(8,128)S(1)} %get-tuple-element.32), channel_id=1, source_target_pairs={{0,3},{1,2},{2,1},{3,0},{4,7},{5,6},{6,5},{7,4},{8,11},{9,10},{10,... | collective-permute-start | bytes 61448 | tf_op jit(solution)/shard_map/ppermute | solution.py:292
  20.4 3.8 %collective-permute-start.3 = (f32[8,640]{1,0:T(8,128)S(1)}, f32[8,640]{1,0:T(8,128)S(1)}, u32[]{:S(2)}, u32[]{:S(2)}) collective-permute-start(f32[8,640]{1,0:T(8,128)S(1)} %get-tuple-element.32), channel_id=1, source_target_pairs={{0,2},{1,3},{2,0},{3,1},{4,6},{5,7},{6,4},{7,5},{8,10},{9,11},{10,... | collective-permute-start | bytes 61448 | tf_op jit(solution)/shard_map/ppermute | solution.py:292
  22.3 2.0 %collective-permute-start.4 = (f32[8,640]{1,0:T(8,128)S(1)}, f32[8,640]{1,0:T(8,128)S(1)}, u32[]{:S(2)}, u32[]{:S(2)}) collective-permute-start(f32[8,640]{1,0:T(8,128)S(1)} %get-tuple-element.32), channel_id=1, source_target_pairs={{0,1},{1,0},{2,3},{3,2},{4,5},{5,4},{6,7},{7,6},{8,9},{9,8},{10,11... | collective-permute-start | bytes 61448 | tf_op jit(solution)/shard_map/ppermute | solution.py:292
  24.3 5.5 %collective-permute-start.5 = (f32[8,640]{1,0:T(8,128)S(1)}, f32[8,640]{1,0:T(8,128)S(1)}, u32[]{:S(2)}, u32[]{:S(2)}) collective-permute-start(f32[8,640]{1,0:T(8,128)S(1)} %add_add_fusion.1.refs_3_), channel_id=1, source_target_pairs={{0,13},{1,12},{2,15},{3,14},{4,9},{5,8},{6,11},{7,10},{8,5},{9,4},... | collective-permute-start | bytes 61448 | tf_op jit(solution)/shard_map/ppermute | solution.py:292
  28.3 4.1 %collective-permute-start.6 = (f32[8,640]{1,0:T(8,128)S(1)}, f32[8,640]{1,0:T(8,128)S(1)}, u32[]{:S(2)}, u32[]{:S(2)}) collective-permute-start(f32[8,640]{1,0:T(8,128)S(1)} %add_add_fusion.1.refs_3_), channel_id=1, source_target_pairs={{0,9},{1,8},{2,11},{3,10},{4,13},{5,12},{6,15},{7,14},{8,1},{9,0},... | collective-permute-start | bytes 61448 | tf_op jit(solution)/shard_map/ppermute | solution.py:292
  28.3 4.1 %collective-permute-start.7 = (f32[8,640]{1,0:T(8,128)S(1)}, f32[8,640]{1,0:T(8,128)S(1)}, u32[]{:S(2)}, u32[]{:S(2)}) collective-permute-start(f32[8,640]{1,0:T(8,128)S(1)} %add_add_fusion.1.refs_3_), channel_id=1, source_target_pairs={{0,5},{1,4},{2,7},{3,6},{4,1},{5,0},{6,3},{7,2},{8,13},{9,12},{10,... | collective-permute-start | bytes 61448 | tf_op jit(solution)/shard_map/ppermute | solution.py:292
  33.6 3.8 %collective-permute-start.8 = (f32[8,640]{1,0:T(8,128)S(1)}, f32[8,640]{1,0:T(8,128)S(1)}, u32[]{:S(2)}, u32[]{:S(2)}) collective-permute-start(f32[8,640]{1,0:T(8,128)S(1)} %get-tuple-element.34.refs_1_), channel_id=1, source_target_pairs={{0,16},{16,0},{1,17},{17,1},{2,18},{18,2},{3,19},{19,3},{4,20},{20... | collective-permute-start | bytes 61448 | tf_op jit(solution)/shard_map/ppermute | solution.py:292
  38.6 3.3 %collective-permute-start.10 = (f32[8,640]{1,0:T(8,128)S(1)}, f32[8,640]{1,0:T(8,128)S(1)}, u32[]{:S(2)}, u32[]{:S(2)}) collective-permute-start(f32[8,640]{1,0:T(8,128)S(1)} %get-tuple-element.37), channel_id=1, source_target_pairs={{0,3},{1,2},{2,1},{3,0},{4,7},{5,6},{6,5},{7,4},{8,11},{9,10},{10,... | collective-permute-start | bytes 61448 | tf_op jit(solution)/shard_map/ppermute | solution.py:292
  39.1 3.8 %collective-permute-start.11 = (f32[8,640]{1,0:T(8,128)S(1)}, f32[8,640]{1,0:T(8,128)S(1)}, u32[]{:S(2)}, u32[]{:S(2)}) collective-permute-start(f32[8,640]{1,0:T(8,128)S(1)} %get-tuple-element.37), channel_id=1, source_target_pairs={{0,2},{1,3},{2,0},{3,1},{4,6},{5,7},{6,4},{7,5},{8,10},{9,11},{10,... | collective-permute-start | bytes 61448 | tf_op jit(solution)/shard_map/ppermute | solution.py:292
  39.5 3.4 %collective-permute-start.9 = (f32[8,640]{1,0:T(8,128)S(1)}, f32[8,640]{1,0:T(8,128)S(1)}, u32[]{:S(2)}, u32[]{:S(2)}) collective-permute-start(f32[8,640]{1,0:T(8,128)S(1)} %get-tuple-element.37), channel_id=1, source_target_pairs={{0,1},{1,0},{2,3},{3,2},{4,5},{5,4},{6,7},{7,6},{8,9},{9,8},{10,11... | collective-permute-start | bytes 61448 | tf_op jit(solution)/shard_map/ppermute | solution.py:292
  42.9 5.1 %collective-permute-start.12 = (f32[8,640]{1,0:T(8,128)S(1)}, f32[8,640]{1,0:T(8,128)S(1)}, u32[]{:S(2)}, u32[]{:S(2)}) collective-permute-start(f32[8,640]{1,0:T(8,128)S(1)} %add_add_fusion.refs_3_), channel_id=1, source_target_pairs={{0,13},{1,12},{2,15},{3,14},{4,9},{5,8},{6,11},{7,10},{8,5},{9,4},... | collective-permute-start | bytes 61448 | tf_op jit(solution)/shard_map/ppermute | solution.py:292
  44.1 4.1 %collective-permute-start.13 = (f32[8,640]{1,0:T(8,128)S(1)}, f32[8,640]{1,0:T(8,128)S(1)}, u32[]{:S(2)}, u32[]{:S(2)}) collective-permute-start(f32[8,640]{1,0:T(8,128)S(1)} %add_add_fusion.refs_3_), channel_id=1, source_target_pairs={{0,9},{1,8},{2,11},{3,10},{4,13},{5,12},{6,15},{7,14},{8,1},{9,0},... | collective-permute-start | bytes 61448 | tf_op jit(solution)/shard_map/ppermute | solution.py:292
  44.5 3.7 %collective-permute-start.14 = (f32[8,640]{1,0:T(8,128)S(1)}, f32[8,640]{1,0:T(8,128)S(1)}, u32[]{:S(2)}, u32[]{:S(2)}) collective-permute-start(f32[8,640]{1,0:T(8,128)S(1)} %add_add_fusion.refs_3_), channel_id=1, source_target_pairs={{0,5},{1,4},{2,7},{3,6},{4,1},{5,0},{6,3},{7,2},{8,13},{9,12},{10,... | collective-permute-start | bytes 61448 | tf_op jit(solution)/shard_map/ppermute | solution.py:292
  49.5 3.8 %collective-permute-start.15 = (f32[8,640]{1,0:T(8,128)S(1)}, f32[8,640]{1,0:T(8,128)S(1)}, u32[]{:S(2)}, u32[]{:S(2)}) collective-permute-start(f32[8,640]{1,0:T(8,128)S(1)} %get-tuple-element.38.refs_1_), channel_id=1, source_target_pairs={{0,16},{16,0},{1,17},{17,1},{2,18},{18,2},{3,19},{19,3},{4,20},{20... | collective-permute-start | bytes 61448 | tf_op jit(solution)/shard_map/ppermute | solution.py:292

commit v7 on v6

--- a/solution.py
+++ b/solution.py
@@ -130,26 +130,20 @@
     center_ref[...] = center
     total = jnp.zeros((16, center.shape[1]), f32)
 
-    def build(begin):
-        high, low = kernel_parts(turned_ref[pl.ds(begin, STEP), :], center)
-        block_ref[pl.ds(2 * begin, STEP), :] = high
-        block_ref[pl.ds(2 * begin + STEP, STEP), :] = low
-
     def fold(begin):
-        weight = weight_ref[:, pl.ds(begin, STEP)]
+        weight = weight_ref[:, begin : begin + CHUNK]
         weight = jnp.concatenate([weight, weight], axis=1)
-        block = block_ref[pl.ds(2 * begin, 2 * STEP), :]
+        block = block_ref[2 * begin : 2 * begin + 2 * CHUNK, :]
         return jnp.dot(weight, block, preferred_element_type=f32)
 
-    def visit(turn, total):
-        begin = pl.multiple_of(turn * STEP, STEP)
-        build(begin)
-        return total + fold(pl.multiple_of(begin - STEP, STEP))
-
     row_count = turned_ref.shape[0]
-    build(0)
-    total = lax.fori_loop(1, row_count // STEP, visit, total)
-    out_ref[...] = unstack2(total + fold(row_count - STEP))
+    for begin in range(0, row_count, CHUNK):
+        high, low = kernel_parts(turned_ref[begin : begin + CHUNK, :], center)
+        block_ref[2 * begin : 2 * begin + CHUNK, :] = high
+        block_ref[2 * begin + CHUNK : 2 * begin + 2 * CHUNK, :] = low
+        if begin > 0:
+            total += fold(begin - CHUNK)
+    out_ref[...] = unstack2(total + fold(row_count - CHUNK))
 
 
 def turned_body(columns_ref, center_ref, block_ref):
@@ -181,8 +175,7 @@
         weight = jnp.where(mask, row_weights(turn), 0.0)
         square += row_sum(weight * weight)
         weight = stack2(weight)
-        for inner in range(0, CHUNK, STEP):
-            weights += [weight[:, inner : inner + STEP]] * 2
+        weights += [weight, weight]
     total = jnp.dot(
         jnp.concatenate(weights, axis=1), block_ref[...], preferred_element_type=f32
     )

time: 54.2 us -> 49.5 us (0.913)
  Pallas kernels: 17.6 us -> 12.8 us
  waiting for transfers between devices: 15.7 us -> 16.4 us
    pallas_call x9, Pallas kernels: 17.6 us -> 12.8 us  [call(): pl.pallas_call(body, out_shape=out_shape, in_specs=[source] * len(args),...]
    ppermute x16, waiting for transfers between devices: 15.7 us -> 16.4 us  [exchange(): got.append(lax.ppermute(value, axis, pairs))]
where the time goes in v7:
time: 49.5 us; the launch traced here: 49.3 us
  starting transfers between devices  19.5 us (39%)
  waiting for transfers between devices  16.4 us (33%)
  Pallas kernels  12.8 us (26%)
  between operations  0.71 us (1%)
    ppermute x16, starting transfers between devices, exchange(): got.append(lax.ppermute(value, axis, pairs))  19.5 us
    ppermute x16, waiting for transfers between devices, exchange(): got.append(lax.ppermute(value, axis, pairs))  16.4 us
    pallas_call x9, Pallas kernels, call(): pl.pallas_call(body, out_shape=out_shape, in_specs=[source] * len(args),...  12.8 us
  transfers between devices with their start and end apart: 16, of which 11 were waited for; matrix products, arithmetic and copies ran while one was open for 0% of the time, Pallas kernels for 5%

profile of v7, /device:TPU:0, one launch (start us, length us, event | category | flops | bytes accessed | tf_op | source)
XLA Modules:
  0.0 49.3 jit_solution(15736755770286281684)
XLA Ops:
  0.6 2.0 %shard_map.68 = (bf16[64,4096]{1,0:T(8,128)(2,1)S(1)}, s32[1,4096]{1,0:T(1,128)S(1)}, f32[1,4096]{1,0:T(1,128)S(1)}, f32[1,512]{1,0:T(1,128)S(1)}, bf16[64,512]{1,0:T(8,128)(2,1)S(1)}) custom-call(bf16[64,4096]{1,0:T(8,128)(2,1)} %feat_hbm.1, s32[1,512]{1,0:T(1,128)} %bitcast.6, s32[1,4096]{1,0:T(1,128)} %bitcast.4, f32[1,4096]{1,0:T(1,128)} %bitcast.5, ...), custom_call_target="tpu_custom_call" | custom-call | tf_op jit(solution)/shard_map/pallas_call | solution.py:260
  2.6 3.0 %collective-permute-start = (bf16[64,512]{1,0:T(8,128)(2,1)S(1)}, bf16[64,512]{1,0:T(8,128)(2,1)S(1)}, u32[]{:S(2)}, u32[]{:S(2)}) collective-permute-start(bf16[64,512]{1,0:T(8,128)(2,1)S(1)} %get-tuple-element.27.refs_1_), channel_id=1, source_target_pairs={{0,16},{16,0},{1,17},{17,1},{2,18},{18,2},{3,19},{19,3},{4,20},{20... | collective-permute-start | bytes 196616 | tf_op jit(solution)/shard_map/ppermute | solution.py:285
  5.6 0.7 %shard_map.69 = (bf16[256,4096]{1,0:T(8,128)(2,1)S(1)}, bf16[4096,256]{1,0:T(8,128)(2,1)S(1)}, bf16[16,4096]{1,0:T(8,128)(2,1)S(1)}) custom-call(bf16[64,4096]{1,0:T(8,128)(2,1)S(1)} %get-tuple-element.22.feat_ref, s32[1,4096]{1,0:T(1,128)S(1)} %get-tuple-element.23.slots_ref.refs_3_.refs_4_, f32[1,4096]{1,0:T(1,128)S(1)} %get-tuple-element.24.prices_ref), custom_call_target="tpu_custom_call" | custom-call | flops 4096000 | bytes 4194304 | tf_op jit(solution)/shard_map/pallas_call | solution.py:260
  6.3 1.6 %collective-permute-done.refs_0_ = bf16[64,512]{1,0:T(8,128)(2,1)S(1)} collective-permute-done((bf16[64,512]{1,0:T(8,128)(2,1)S(1)}, bf16[64,512]{1,0:T(8,128)(2,1)S(1)}, u32[]{:S(2)}, u32[]{:S(2)}) %collective-permute-start) | collective-permute-done | bytes 65568 | tf_op jit(solution)/shard_map/ppermute | solution.py:285
  7.8 2.5 %shard_map.70 = (bf16[8192,512]{1,0:T(8,128)(2,1)S(1)}, bf16[256,512]{1,0:T(8,128)(2,1)S(1)}, f32[8,512]{1,0:T(8,128)S(1)}) custom-call(bf16[4096,256]{1,0:T(8,128)(2,1)S(1)} %get-tuple-element.25.turned_ref, bf16[16,4096]{1,0:T(8,128)(2,1)S(1)} %get-tuple-element.26.weight_ref, bf16[64,512]{1,0:T(8,128)(2,1)S(1)} %collective-permute-done.refs_0_, ...), custom_call_target="tpu_custom_call" | custom-call | flops 134217728 | bytes 8388608 | tf_op jit(solution)/shard_map/pallas_call | solution.py:260
  10.4 2.1 %collective-permute-start.1 = (f32[8,512]{1,0:T(8,128)S(1)}, f32[8,512]{1,0:T(8,128)S(1)}, u32[]{:S(2)}, u32[]{:S(2)}) collective-permute-start(f32[8,512]{1,0:T(8,128)S(1)} %get-tuple-element.28.refs_1_), channel_id=1, source_target_pairs={{0,16},{16,0},{1,17},{17,1},{2,18},{18,2},{3,19},{19,3},{4,20},{20... | collective-permute-start | bytes 49160 | tf_op jit(solution)/shard_map/ppermute | solution.py:285
  12.4 1.9 %shard_map.71.refs_4_ = bf16[1024,4096]{1,0:T(8,128)(2,1)S(1)} custom-call(bf16[256,4096]{1,0:T(8,128)(2,1)S(1)} %get-tuple-element.30.columns_ref, bf16[256,512]{1,0:T(8,128)(2,1)S(1)} %get-tuple-element.31.center_ref), custom_call_target="tpu_custom_call" | custom-call | flops 134217728 | bytes 8388608 | tf_op jit(solution)/shard_map/pallas_call | solution.py:260
  14.4 0.0 collective-permute-done.1.refs_0_
  14.4 1.2 %shard_map.72 = (f32[8,512]{1,0:T(8,128)S(1)}, f32[8,640]{1,0:T(8,128)S(1)}) custom-call(f32[8,512]{1,0:T(8,128)S(1)} %collective-permute-done.1.refs_0_, f32[8,512]{1,0:T(8,128)S(1)} %get-tuple-element.28.refs_1_, f32[1,512]{1,0:T(1,128)S(1)} %get-tuple-element.29.refs_2_, s32[1,4096]{1,0:T(1,128)S(1)} %get-tuple-element.23.slots_ref.refs_3_.refs_4_, ...), custom_call_target="tpu_custom_call" | custom-call | tf_op jit(solution)/shard_map/pallas_call | solution.py:260
  15.6 0.1 collective-permute-start.2
  15.7 1.9 %collective-permute-start.3 = (f32[8,640]{1,0:T(8,128)S(1)}, f32[8,640]{1,0:T(8,128)S(1)}, u32[]{:S(2)}, u32[]{:S(2)}) collective-permute-start(f32[8,640]{1,0:T(8,128)S(1)} %get-tuple-element.32), channel_id=1, source_target_pairs={{0,2},{1,3},{2,0},{3,1},{4,6},{5,7},{6,4},{7,5},{8,10},{9,11},{10,... | collective-permute-start | bytes 61448 | tf_op jit(solution)/shard_map/ppermute | solution.py:285
  17.6 0.0 collective-permute-start.4
  17.6 1.3 %collective-permute-done.2 = f32[8,640]{1,0:T(8,128)S(1)} collective-permute-done((f32[8,640]{1,0:T(8,128)S(1)}, f32[8,640]{1,0:T(8,128)S(1)}, u32[]{:S(2)}, u32[]{:S(2)}) %collective-permute-start.2) | collective-permute-done | bytes 20512 | tf_op jit(solution)/shard_map/ppermute | solution.py:285
  18.9 0.7 %collective-permute-done.3 = f32[8,640]{1,0:T(8,128)S(1)} collective-permute-done((f32[8,640]{1,0:T(8,128)S(1)}, f32[8,640]{1,0:T(8,128)S(1)}, u32[]{:S(2)}, u32[]{:S(2)}) %collective-permute-start.3) | collective-permute-done | bytes 20512 | tf_op jit(solution)/shard_map/ppermute | solution.py:285
  19.5 0.0 collective-permute-done.4
  19.5 4.0 %collective-permute-start.5 = (f32[8,640]{1,0:T(8,128)S(1)}, f32[8,640]{1,0:T(8,128)S(1)}, u32[]{:S(2)}, u32[]{:S(2)}) collective-permute-start(f32[8,640]{1,0:T(8,128)S(1)} %add_add_fusion.1.refs_3_), channel_id=1, source_target_pairs={{0,13},{1,12},{2,15},{3,14},{4,9},{5,8},{6,11},{7,10},{8,5},{9,4},... | collective-permute-start | bytes 61448 | tf_op jit(solution)/shard_map/ppermute | solution.py:285
  23.5 0.0 collective-permute-start.6
  23.5 0.5 collective-permute-start.7
  24.0 1.0 %collective-permute-done.5.refs_0_ = f32[8,640]{1,0:T(8,128)S(1)} collective-permute-done((f32[8,640]{1,0:T(8,128)S(1)}, f32[8,640]{1,0:T(8,128)S(1)}, u32[]{:S(2)}, u32[]{:S(2)}) %collective-permute-start.5) | collective-permute-done | bytes 20512 | tf_op jit(solution)/shard_map/ppermute | solution.py:285
  25.0 2.6 %collective-permute-done.6.refs_1_ = f32[8,640]{1,0:T(8,128)S(1)} collective-permute-done((f32[8,640]{1,0:T(8,128)S(1)}, f32[8,640]{1,0:T(8,128)S(1)}, u32[]{:S(2)}, u32[]{:S(2)}) %collective-permute-start.6) | collective-permute-done | bytes 20512 | tf_op jit(solution)/shard_map/ppermute | solution.py:285
  27.6 0.0 collective-permute-done.7.refs_2_
  27.7 1.2 %shard_map.73 = (f32[8,640]{1,0:T(8,128)S(1)}, f32[8,640]{1,0:T(8,128)S(1)}) custom-call(f32[8,640]{1,0:T(8,128)S(1)} %collective-permute-done.5.refs_0_, f32[8,640]{1,0:T(8,128)S(1)} %collective-permute-done.6.refs_1_, f32[8,640]{1,0:T(8,128)S(1)} %collective-permute-done.7.refs_2_, f32[8,640]{1,0:T(8,128)S(1)} %add_add_fusion.1.refs_3_, ...), custom_call_target="tpu_custom_call" | custom-call | tf_op jit(solution)/shard_map/pallas_call | solution.py:260
  28.8 1.5 %collective-permute-start.8 = (f32[8,640]{1,0:T(8,128)S(1)}, f32[8,640]{1,0:T(8,128)S(1)}, u32[]{:S(2)}, u32[]{:S(2)}) collective-permute-start(f32[8,640]{1,0:T(8,128)S(1)} %get-tuple-element.34.refs_1_), channel_id=1, source_target_pairs={{0,16},{16,0},{1,17},{17,1},{2,18},{18,2},{3,19},{19,3},{4,20},{20... | collective-permute-start | bytes 61448 | tf_op jit(solution)/shard_map/ppermute | solution.py:285
  30.3 2.3 %collective-permute-done.8.refs_0_ = f32[8,640]{1,0:T(8,128)S(1)} collective-permute-done((f32[8,640]{1,0:T(8,128)S(1)}, f32[8,640]{1,0:T(8,128)S(1)}, u32[]{:S(2)}, u32[]{:S(2)}) %collective-permute-start.8) | collective-permute-done | bytes 20512 | tf_op jit(solution)/shard_map/ppermute | solution.py:285
  32.6 1.3 %shard_map.74 = (f32[8,512]{1,0:T(8,128)S(1)}, f32[8,128]{1,0:T(8,128)S(1)}, f32[8,640]{1,0:T(8,128)S(1)}) custom-call(f32[8,640]{1,0:T(8,128)S(1)} %collective-permute-done.8.refs_0_, f32[8,640]{1,0:T(8,128)S(1)} %get-tuple-element.34.refs_1_, f32[1,512]{1,0:T(1,128)S(1)} %get-tuple-element.29.refs_2_, ...), custom_call_target="tpu_custom_call" | custom-call | tf_op jit(solution)/shard_map/pallas_call | solution.py:260
  33.9 0.5 %collective-permute-start.10 = (f32[8,640]{1,0:T(8,128)S(1)}, f32[8,640]{1,0:T(8,128)S(1)}, u32[]{:S(2)}, u32[]{:S(2)}) collective-permute-start(f32[8,640]{1,0:T(8,128)S(1)} %get-tuple-element.37), channel_id=1, source_target_pairs={{0,3},{1,2},{2,1},{3,0},{4,7},{5,6},{6,5},{7,4},{8,11},{9,10},{10,... | collective-permute-start | bytes 61448 | tf_op jit(solution)/shard_map/ppermute | solution.py:285
  34.4 0.4 collective-permute-start.11
  34.8 1.1 %collective-permute-start.9 = (f32[8,640]{1,0:T(8,128)S(1)}, f32[8,640]{1,0:T(8,128)S(1)}, u32[]{:S(2)}, u32[]{:S(2)}) collective-permute-start(f32[8,640]{1,0:T(8,128)S(1)} %get-tuple-element.37), channel_id=1, source_target_pairs={{0,1},{1,0},{2,3},{3,2},{4,5},{5,4},{6,7},{7,6},{8,9},{9,8},{10,11... | collective-permute-start | bytes 61448 | tf_op jit(solution)/shard_map/ppermute | solution.py:285
  35.8 1.3 %collective-permute-done.10 = f32[8,640]{1,0:T(8,128)S(1)} collective-permute-done((f32[8,640]{1,0:T(8,128)S(1)}, f32[8,640]{1,0:T(8,128)S(1)}, u32[]{:S(2)}, u32[]{:S(2)}) %collective-permute-start.10) | collective-permute-done | bytes 20512 | tf_op jit(solution)/shard_map/ppermute | solution.py:285
  37.2 1.0 %collective-permute-done.11 = f32[8,640]{1,0:T(8,128)S(1)} collective-permute-done((f32[8,640]{1,0:T(8,128)S(1)}, f32[8,640]{1,0:T(8,128)S(1)}, u32[]{:S(2)}, u32[]{:S(2)}) %collective-permute-start.11) | collective-permute-done | bytes 20512 | tf_op jit(solution)/shard_map/ppermute | solution.py:285
  38.2 0.0 collective-permute-done.9
  38.2 1.1 %collective-permute-start.12 = (f32[8,640]{1,0:T(8,128)S(1)}, f32[8,640]{1,0:T(8,128)S(1)}, u32[]{:S(2)}, u32[]{:S(2)}) collective-permute-start(f32[8,640]{1,0:T(8,128)S(1)} %add_add_fusion.refs_3_), channel_id=1, source_target_pairs={{0,13},{1,12},{2,15},{3,14},{4,9},{5,8},{6,11},{7,10},{8,5},{9,4},... | collective-permute-start | bytes 61448 | tf_op jit(solution)/shard_map/ppermute | solution.py:285
  39.3 0.4 collective-permute-start.13
  39.7 1.5 %collective-permute-start.14 = (f32[8,640]{1,0:T(8,128)S(1)}, f32[8,640]{1,0:T(8,128)S(1)}, u32[]{:S(2)}, u32[]{:S(2)}) collective-permute-start(f32[8,640]{1,0:T(8,128)S(1)} %add_add_fusion.refs_3_), channel_id=1, source_target_pairs={{0,5},{1,4},{2,7},{3,6},{4,1},{5,0},{6,3},{7,2},{8,13},{9,12},{10,... | collective-permute-start | bytes 61448 | tf_op jit(solution)/shard_map/ppermute | solution.py:285
  41.3 2.0 %collective-permute-done.12.refs_0_ = f32[8,640]{1,0:T(8,128)S(1)} collective-permute-done((f32[8,640]{1,0:T(8,128)S(1)}, f32[8,640]{1,0:T(8,128)S(1)}, u32[]{:S(2)}, u32[]{:S(2)}) %collective-permute-start.12) | collective-permute-done | bytes 20512 | tf_op jit(solution)/shard_map/ppermute | solution.py:285
  43.3 0.2 collective-permute-done.13.refs_1_
  43.5 0.0 collective-permute-done.14.refs_2_
  43.5 1.2 %shard_map.75 = (f32[8,128]{1,0:T(8,128)S(1)}, f32[8,640]{1,0:T(8,128)S(1)}) custom-call(f32[8,640]{1,0:T(8,128)S(1)} %collective-permute-done.12.refs_0_, f32[8,640]{1,0:T(8,128)S(1)} %collective-permute-done.13.refs_1_, f32[8,640]{1,0:T(8,128)S(1)} %collective-permute-done.14.refs_2_, f32[8,640]{1,0:T(8,128)S(1)} %add_add_fusion.refs_3_, ...), custom_call_target="tpu_custom_call" | custom-call | tf_op jit(solution)/shard_map/pallas_call | solution.py:260
  44.7 1.5 %collective-permute-start.15 = (f32[8,640]{1,0:T(8,128)S(1)}, f32[8,640]{1,0:T(8,128)S(1)}, u32[]{:S(2)}, u32[]{:S(2)}) collective-permute-start(f32[8,640]{1,0:T(8,128)S(1)} %get-tuple-element.38.refs_1_), channel_id=1, source_target_pairs={{0,16},{16,0},{1,17},{17,1},{2,18},{18,2},{3,19},{19,3},{4,20},{20... | collective-permute-start | bytes 61448 | tf_op jit(solution)/shard_map/ppermute | solution.py:285
  46.2 2.3 %collective-permute-done.15.refs_0_ = f32[8,640]{1,0:T(8,128)S(1)} collective-permute-done((f32[8,640]{1,0:T(8,128)S(1)}, f32[8,640]{1,0:T(8,128)S(1)}, u32[]{:S(2)}, u32[]{:S(2)}) %collective-permute-start.15) | collective-permute-done | bytes 20512 | tf_op jit(solution)/shard_map/ppermute | solution.py:285
  48.5 0.8 %shard_map.76 = (f32[8,512]{1,0:T(8,128)}, f32[8,512]{1,0:T(8,128)}) custom-call(f32[8,640]{1,0:T(8,128)S(1)} %collective-permute-done.15.refs_0_, f32[8,640]{1,0:T(8,128)S(1)} %get-tuple-element.38.refs_1_, f32[1,512]{1,0:T(1,128)S(1)} %get-tuple-element.29.refs_2_, f32[8,512]{1,0:T(8,128)S(1)} %get-tuple-element.35.refs_5_.refs_3_, ...), custom_call_target="tpu_custom_call" | custom-call | tf_op jit(solution)/shard_map/pallas_call | solution.py:260
  (2 shorter events, 0.0 us)
Async XLA Ops:
  2.6 5.2 %collective-permute-start = (bf16[64,512]{1,0:T(8,128)(2,1)S(1)}, bf16[64,512]{1,0:T(8,128)(2,1)S(1)}, u32[]{:S(2)}, u32[]{:S(2)}) collective-permute-start(bf16[64,512]{1,0:T(8,128)(2,1)S(1)} %get-tuple-element.27.refs_1_), channel_id=1, source_target_pairs={{0,16},{16,0},{1,17},{17,1},{2,18},{18,2},{3,19},{19,3},{4,20},{20... | collective-permute-start | bytes 196616 | tf_op jit(solution)/shard_map/ppermute | solution.py:285
  10.4 4.0 %collective-permute-start.1 = (f32[8,512]{1,0:T(8,128)S(1)}, f32[8,512]{1,0:T(8,128)S(1)}, u32[]{:S(2)}, u32[]{:S(2)}) collective-permute-start(f32[8,512]{1,0:T(8,128)S(1)} %get-tuple-element.28.refs_1_), channel_id=1, source_target_pairs={{0,16},{16,0},{1,17},{17,1},{2,18},{18,2},{3,19},{19,3},{4,20},{20... | collective-permute-start | bytes 49160 | tf_op jit(solution)/shard_map/ppermute | solution.py:285
  15.6 3.3 %collective-permute-start.2 = (f32[8,640]{1,0:T(8,128)S(1)}, f32[8,640]{1,0:T(8,128)S(1)}, u32[]{:S(2)}, u32[]{:S(2)}) collective-permute-start(f32[8,640]{1,0:T(8,128)S(1)} %get-tuple-element.32), channel_id=1, source_target_pairs={{0,3},{1,2},{2,1},{3,0},{4,7},{5,6},{6,5},{7,4},{8,11},{9,10},{10,... | collective-permute-start | bytes 61448 | tf_op jit(solution)/shard_map/ppermute | solution.py:285
  15.7 3.8 %collective-permute-start.3 = (f32[8,640]{1,0:T(8,128)S(1)}, f32[8,640]{1,0:T(8,128)S(1)}, u32[]{:S(2)}, u32[]{:S(2)}) collective-permute-start(f32[8,640]{1,0:T(8,128)S(1)} %get-tuple-element.32), channel_id=1, source_target_pairs={{0,2},{1,3},{2,0},{3,1},{4,6},{5,7},{6,4},{7,5},{8,10},{9,11},{10,... | collective-permute-start | bytes 61448 | tf_op jit(solution)/shard_map/ppermute | solution.py:285
  17.6 2.0 %collective-permute-start.4 = (f32[8,640]{1,0:T(8,128)S(1)}, f32[8,640]{1,0:T(8,128)S(1)}, u32[]{:S(2)}, u32[]{:S(2)}) collective-permute-start(f32[8,640]{1,0:T(8,128)S(1)} %get-tuple-element.32), channel_id=1, source_target_pairs={{0,1},{1,0},{2,3},{3,2},{4,5},{5,4},{6,7},{7,6},{8,9},{9,8},{10,11... | collective-permute-start | bytes 61448 | tf_op jit(solution)/shard_map/ppermute | solution.py:285
  19.5 5.5 %collective-permute-start.5 = (f32[8,640]{1,0:T(8,128)S(1)}, f32[8,640]{1,0:T(8,128)S(1)}, u32[]{:S(2)}, u32[]{:S(2)}) collective-permute-start(f32[8,640]{1,0:T(8,128)S(1)} %add_add_fusion.1.refs_3_), channel_id=1, source_target_pairs={{0,13},{1,12},{2,15},{3,14},{4,9},{5,8},{6,11},{7,10},{8,5},{9,4},... | collective-permute-start | bytes 61448 | tf_op jit(solution)/shard_map/ppermute | solution.py:285
  23.5 4.1 %collective-permute-start.6 = (f32[8,640]{1,0:T(8,128)S(1)}, f32[8,640]{1,0:T(8,128)S(1)}, u32[]{:S(2)}, u32[]{:S(2)}) collective-permute-start(f32[8,640]{1,0:T(8,128)S(1)} %add_add_fusion.1.refs_3_), channel_id=1, source_target_pairs={{0,9},{1,8},{2,11},{3,10},{4,13},{5,12},{6,15},{7,14},{8,1},{9,0},... | collective-permute-start | bytes 61448 | tf_op jit(solution)/shard_map/ppermute | solution.py:285
  23.5 4.1 %collective-permute-start.7 = (f32[8,640]{1,0:T(8,128)S(1)}, f32[8,640]{1,0:T(8,128)S(1)}, u32[]{:S(2)}, u32[]{:S(2)}) collective-permute-start(f32[8,640]{1,0:T(8,128)S(1)} %add_add_fusion.1.refs_3_), channel_id=1, source_target_pairs={{0,5},{1,4},{2,7},{3,6},{4,1},{5,0},{6,3},{7,2},{8,13},{9,12},{10,... | collective-permute-start | bytes 61448 | tf_op jit(solution)/shard_map/ppermute | solution.py:285
  28.8 3.8 %collective-permute-start.8 = (f32[8,640]{1,0:T(8,128)S(1)}, f32[8,640]{1,0:T(8,128)S(1)}, u32[]{:S(2)}, u32[]{:S(2)}) collective-permute-start(f32[8,640]{1,0:T(8,128)S(1)} %get-tuple-element.34.refs_1_), channel_id=1, source_target_pairs={{0,16},{16,0},{1,17},{17,1},{2,18},{18,2},{3,19},{19,3},{4,20},{20... | collective-permute-start | bytes 61448 | tf_op jit(solution)/shard_map/ppermute | solution.py:285
  33.9 3.3 %collective-permute-start.10 = (f32[8,640]{1,0:T(8,128)S(1)}, f32[8,640]{1,0:T(8,128)S(1)}, u32[]{:S(2)}, u32[]{:S(2)}) collective-permute-start(f32[8,640]{1,0:T(8,128)S(1)} %get-tuple-element.37), channel_id=1, source_target_pairs={{0,3},{1,2},{2,1},{3,0},{4,7},{5,6},{6,5},{7,4},{8,11},{9,10},{10,... | collective-permute-start | bytes 61448 | tf_op jit(solution)/shard_map/ppermute | solution.py:285
  34.4 3.8 %collective-permute-start.11 = (f32[8,640]{1,0:T(8,128)S(1)}, f32[8,640]{1,0:T(8,128)S(1)}, u32[]{:S(2)}, u32[]{:S(2)}) collective-permute-start(f32[8,640]{1,0:T(8,128)S(1)} %get-tuple-element.37), channel_id=1, source_target_pairs={{0,2},{1,3},{2,0},{3,1},{4,6},{5,7},{6,4},{7,5},{8,10},{9,11},{10,... | collective-permute-start | bytes 61448 | tf_op jit(solution)/shard_map/ppermute | solution.py:285
  34.8 3.4 %collective-permute-start.9 = (f32[8,640]{1,0:T(8,128)S(1)}, f32[8,640]{1,0:T(8,128)S(1)}, u32[]{:S(2)}, u32[]{:S(2)}) collective-permute-start(f32[8,640]{1,0:T(8,128)S(1)} %get-tuple-element.37), channel_id=1, source_target_pairs={{0,1},{1,0},{2,3},{3,2},{4,5},{5,4},{6,7},{7,6},{8,9},{9,8},{10,11... | collective-permute-start | bytes 61448 | tf_op jit(solution)/shard_map/ppermute | solution.py:285
  38.2 5.1 %collective-permute-start.12 = (f32[8,640]{1,0:T(8,128)S(1)}, f32[8,640]{1,0:T(8,128)S(1)}, u32[]{:S(2)}, u32[]{:S(2)}) collective-permute-start(f32[8,640]{1,0:T(8,128)S(1)} %add_add_fusion.refs_3_), channel_id=1, source_target_pairs={{0,13},{1,12},{2,15},{3,14},{4,9},{5,8},{6,11},{7,10},{8,5},{9,4},... | collective-permute-start | bytes 61448 | tf_op jit(solution)/shard_map/ppermute | solution.py:285
  39.3 4.2 %collective-permute-start.13 = (f32[8,640]{1,0:T(8,128)S(1)}, f32[8,640]{1,0:T(8,128)S(1)}, u32[]{:S(2)}, u32[]{:S(2)}) collective-permute-start(f32[8,640]{1,0:T(8,128)S(1)} %add_add_fusion.refs_3_), channel_id=1, source_target_pairs={{0,9},{1,8},{2,11},{3,10},{4,13},{5,12},{6,15},{7,14},{8,1},{9,0},... | collective-permute-start | bytes 61448 | tf_op jit(solution)/shard_map/ppermute | solution.py:285
  39.7 3.8 %collective-permute-start.14 = (f32[8,640]{1,0:T(8,128)S(1)}, f32[8,640]{1,0:T(8,128)S(1)}, u32[]{:S(2)}, u32[]{:S(2)}) collective-permute-start(f32[8,640]{1,0:T(8,128)S(1)} %add_add_fusion.refs_3_), channel_id=1, source_target_pairs={{0,5},{1,4},{2,7},{3,6},{4,1},{5,0},{6,3},{7,2},{8,13},{9,12},{10,... | collective-permute-start | bytes 61448 | tf_op jit(solution)/shard_map/ppermute | solution.py:285
  44.7 3.8 %collective-permute-start.15 = (f32[8,640]{1,0:T(8,128)S(1)}, f32[8,640]{1,0:T(8,128)S(1)}, u32[]{:S(2)}, u32[]{:S(2)}) collective-permute-start(f32[8,640]{1,0:T(8,128)S(1)} %get-tuple-element.38.refs_1_), channel_id=1, source_target_pairs={{0,16},{16,0},{1,17},{17,1},{2,18},{18,2},{3,19},{19,3},{4,20},{20... | collective-permute-start | bytes 61448 | tf_op jit(solution)/shard_map/ppermute | solution.py:285

commit v8 on v7

--- a/solution.py
+++ b/solution.py
@@ -33,8 +33,23 @@
     return jnp.concatenate([high, value - high], axis=0).astype(bf16)
 
 
-def unstack2(value):
-    return value[0:8] + value[8:16]
+def product(stacked, high_block, low_block):
+    main = jnp.dot(stacked, high_block, preferred_element_type=f32)
+    rest = jnp.dot(stacked[0:SLOTS], low_block, preferred_element_type=f32)
+    return main[0:SLOTS] + (main[SLOTS:] + rest)
+
+
+def slot_lanes(first):
+    lane = lax.broadcasted_iota(jnp.int32, (SLOTS, EXTRA), 1)
+    return lane == lax.broadcasted_iota(jnp.int32, (SLOTS, EXTRA), 0) + first
+
+
+def to_lanes(column, first):
+    return jnp.sum(jnp.where(slot_lanes(first), column, 0.0), axis=0, keepdims=True)
+
+
+def from_lanes(row, first):
+    return jnp.sum(jnp.where(slot_lanes(first), row, 0.0), axis=1, keepdims=True)
 
 
 def pair_total(parts):
@@ -75,8 +90,14 @@
     feat_ref, slots_ref, prices_ref, scale_ref, out_ref, idx_ref, hit_ref, sems = refs
     row_count = feat_ref.shape[1]
     count = out_ref.shape[1]
-    sources = (idx_hbm, feat_hbm, slots_hbm, prices_hbm, scale_hbm)
-    targets = (idx_ref, feat_ref, slots_ref, prices_ref, scale_ref)
+    half = row_count // 2
+    left, right = pl.ds(0, half), pl.ds(half, half)
+    sources = (
+        idx_hbm, feat_hbm.at[:, left], feat_hbm.at[:, right], slots_hbm, prices_hbm, scale_hbm
+    )
+    targets = (
+        idx_ref, feat_ref.at[:, left], feat_ref.at[:, right], slots_ref, prices_ref, scale_ref
+    )
     copies = [
         pltpu.make_async_copy(source, target, sems.at[place])
         for place, (source, target) in enumerate(zip(sources, targets))
@@ -93,17 +114,17 @@
         own = jnp.where(block == begin // STEP, place, -1.0).astype(bf16)
         return jnp.where(row == own, jnp.ones_like(row), jnp.zeros_like(row))
 
-    half = row_count // 2
     for begin in range(0, half, STEP):
         hit_ref[begin : begin + STEP, :] = hits(begin)
     copies[1].wait()
     total = jnp.dot(feat_ref[:, :half], hit_ref[...], preferred_element_type=f32)
+    copies[2].wait()
     for begin in range(half, row_count, STEP):
         total += jnp.dot(
             feat_ref[:, begin : begin + STEP], hits(begin), preferred_element_type=f32
         )
     out_ref[...] = total.astype(bf16)
-    for copy in copies[2:]:
+    for copy in copies[3:]:
         copy.wait()
 
 
@@ -128,22 +149,24 @@
         [*split3(center * FACTOR), norm_rows(center, 0)], axis=0
     ).astype(bf16)
     center_ref[...] = center
-    total = jnp.zeros((16, center.shape[1]), f32)
+    row_count = turned_ref.shape[0]
+    total = jnp.zeros(out_ref.shape, f32)
 
     def fold(begin):
-        weight = weight_ref[:, begin : begin + CHUNK]
-        weight = jnp.concatenate([weight, weight], axis=1)
-        block = block_ref[2 * begin : 2 * begin + 2 * CHUNK, :]
-        return jnp.dot(weight, block, preferred_element_type=f32)
-
-    row_count = turned_ref.shape[0]
+        end = begin + CHUNK
+        return product(
+            weight_ref[:, begin:end],
+            block_ref[begin:end, :],
+            block_ref[row_count + begin : row_count + end, :],
+        )
+
     for begin in range(0, row_count, CHUNK):
         high, low = kernel_parts(turned_ref[begin : begin + CHUNK, :], center)
-        block_ref[2 * begin : 2 * begin + CHUNK, :] = high
-        block_ref[2 * begin + CHUNK : 2 * begin + 2 * CHUNK, :] = low
+        block_ref[begin : begin + CHUNK, :] = high
+        block_ref[row_count + begin : row_count + begin + CHUNK, :] = low
         if begin > 0:
             total += fold(begin - CHUNK)
-    out_ref[...] = unstack2(total + fold(row_count - CHUNK))
+    out_ref[...] = total + fold(row_count - CHUNK)
 
 
 def turned_body(columns_ref, center_ref, block_ref):
@@ -157,29 +180,19 @@
 
 
 def apply_rows(scaled, turned_ref, slots_ref, out_ref):
-    stacked = stack2(scaled)
-    stacked = jnp.concatenate([stacked, stacked], axis=1)
-    value = jnp.dot(stacked, turned_ref[...], preferred_element_type=f32)
-    own = jnp.where(slot_mask(slots_ref[...]), unstack2(value), 0.0)
-    own = jnp.sum(own, axis=0, keepdims=True)
-    for turn, begin in enumerate(range(0, turned_ref.shape[1], CHUNK)):
-        out_ref[turn : turn + 1, 0:CHUNK] = own[:, begin : begin + CHUNK]
-
-
-def fold_rows(row_weights, block_ref, slots_ref, out_ref):
-    count = block_ref.shape[1]
-    square = jnp.zeros((SLOTS, 1), f32)
-    weights = []
-    for turn, begin in enumerate(range(0, slots_ref.shape[1], CHUNK)):
-        mask = slot_mask(slots_ref[:, begin : begin + CHUNK])
-        weight = jnp.where(mask, row_weights(turn), 0.0)
-        square += row_sum(weight * weight)
-        weight = stack2(weight)
-        weights += [weight, weight]
-    total = jnp.dot(
-        jnp.concatenate(weights, axis=1), block_ref[...], preferred_element_type=f32
-    )
-    out_ref[:, 0:count] = unstack2(total)
+    count, row_count = scaled.shape[1], turned_ref.shape[1]
+    value = product(stack2(scaled), turned_ref[0:count, :], turned_ref[count:, :])
+    own = jnp.where(slot_mask(slots_ref[...]), value, 0.0)
+    out_ref[:, 0:row_count] = jnp.sum(own, axis=0, keepdims=True)
+
+
+def fold_rows(rows, block_ref, slots_ref, out_ref):
+    row_count, count = slots_ref.shape[1], block_ref.shape[1]
+    weight = jnp.where(slot_mask(slots_ref[...]), rows, 0.0)
+    out_ref[:, 0:count] = product(
+        stack2(weight), block_ref[0:row_count, :], block_ref[row_count:, :]
+    )
+    square = row_sum(weight * weight)
     out_ref[:, count : count + EXTRA] = jnp.broadcast_to(square, (SLOTS, EXTRA))
 
 
@@ -189,7 +202,7 @@
     scale = scale_ref[...]
     target = scale * total_of(first_refs) * scale_over_root
     target_ref[...] = target
-    out_ref[:, CHUNK:] = jnp.broadcast_to(row_sum(target * target), (SLOTS, EXTRA))
+    out_ref[:, turned_ref.shape[1] :] = to_lanes(row_sum(target * target), 0)
     apply_rows(scale * target, turned_ref, slots_ref, out_ref)
 
 
@@ -198,26 +211,25 @@
     slots_ref, block_ref, rows_ref, out_ref = refs[parts:]
     rows = total_of(row_refs)
     rows_ref[...] = rows
-    fold_rows(lambda turn: rows[turn : turn + 1, 0:CHUNK], block_ref, slots_ref, out_ref)
+    fold_rows(rows[:, 0 : slots_ref.shape[1]], block_ref, slots_ref, out_ref)
 
 
 def second_apply_body(parts, inv_rows, *refs):
     fold_refs = refs[:parts]
     (scale_ref, slots_ref, turned_ref, target_ref, rows_ref,
      residual_ref, step_ref, out_ref) = refs[parts:]
-    count = scale_ref.shape[1]
+    row_count, count = turned_ref.shape[1], scale_ref.shape[1]
     folded = total_of(fold_refs)
     scale = scale_ref[...]
     target = target_ref[...]
-    norm = rows_ref[:, CHUNK : CHUNK + 1]
+    norm = from_lanes(rows_ref[:, row_count:], 0)
     applied = scale * folded[:, 0:count] * inv_rows + RIDGE * target
     step = norm / (folded[:, count : count + 1] * inv_rows + RIDGE * norm)
     residual = target - step * applied
     residual_ref[...] = residual
     step_ref[...] = jnp.broadcast_to(step, step_ref.shape)
-    lane = lax.broadcasted_iota(jnp.int32, (SLOTS, EXTRA), 1)
-    out_ref[:, CHUNK:] = jnp.where(
-        lane == 0, row_sum(residual * residual), row_sum(residual * target)
+    out_ref[:, row_count:] = to_lanes(row_sum(residual * residual), 0) + to_lanes(
+        row_sum(residual * target), SLOTS
     )
     apply_rows(scale * residual, turned_ref, slots_ref, out_ref)
 
@@ -225,28 +237,26 @@
 def second_fold_body(parts, *refs):
     row_refs = refs[:parts]
     slots_ref, block_ref, rows_ref, sums_ref, out_ref = refs[parts:]
+    row_count = slots_ref.shape[1]
     latest = total_of(row_refs)
-    sums_ref[...] = latest[:, CHUNK:]
-    rows = rows_ref[...]
-    ratio = latest[:, CHUNK : CHUNK + 1] / rows[:, CHUNK : CHUNK + 1]
-
-    def row_weights(turn):
-        return latest[turn : turn + 1, 0:CHUNK] + ratio * rows[turn : turn + 1, 0:CHUNK]
-
-    fold_rows(row_weights, block_ref, slots_ref, out_ref)
+    first_norm = from_lanes(rows_ref[:, row_count:], 0)
+    norm = from_lanes(latest[:, row_count:], 0)
+    cross = from_lanes(latest[:, row_count:], SLOTS)
+    lane = lax.broadcasted_iota(jnp.int32, (SLOTS, EXTRA), 1)
+    sums_ref[...] = jnp.where(lane == 0, first_norm, jnp.where(lane == 1, norm, cross))
+    rows = latest[:, 0:row_count] + (norm / first_norm) * rows_ref[:, 0:row_count]
+    fold_rows(rows, block_ref, slots_ref, out_ref)
 
 
 def finish_body(parts, inv_rows, *refs):
     fold_refs = refs[:parts]
-    (scale_ref, target_ref, residual_ref, step_ref, rows_ref, sums_ref,
+    (scale_ref, target_ref, residual_ref, step_ref, sums_ref,
      coefficients_ref, out_ref) = refs[parts:]
     count = scale_ref.shape[1]
     folded = total_of(fold_refs)
     target = target_ref[...]
     residual = residual_ref[...]
-    first_norm = rows_ref[:, CHUNK : CHUNK + 1]
-    norm = sums_ref[:, 0:1]
-    cross = sums_ref[:, 1:2]
+    first_norm, norm, cross = (sums_ref[:, i : i + 1] for i in range(3))
     ratio = norm / first_norm
     direction = residual + ratio * target
     square = norm + 2.0 * ratio * cross + ratio * ratio * first_norm
@@ -298,8 +308,7 @@
     depth, row_count = features.shape
     count = center_idx.shape[0]
     all_rows = row_count * lax.axis_size("dp")
-    turns = row_count // CHUNK
-    row_shape = shaped((turns, CHUNK + EXTRA))
+    row_shape = shaped((1, row_count + EXTRA))
     fold_shape = shaped((SLOTS, count + EXTRA))
     vector = shaped((SLOTS, count))
     narrow = shaped((SLOTS, EXTRA))
@@ -329,7 +338,7 @@
         scratch_shapes=[
             pltpu.VMEM((1, count), jnp.int32),
             pltpu.VMEM((row_count // 2, count), bf16),
-            pltpu.SemaphoreType.DMA((5,)),
+            pltpu.SemaphoreType.DMA((6,)),
         ],
     )
     centers = exchange(picked, "dp")
@@ -379,7 +388,7 @@
     return call(
         partial(finish_body, len(folds), 1.0 / all_rows),
         (vector, vector),
-        *folds, scale, target, residual, step, rows, sums,
+        *folds, scale, target, residual, step, sums,
     )
 
 

time: 49.5 us -> 49.6 us (level)
  no operation moved by 1% of the time
where the time goes in v8:
time: 49.6 us; the launch traced here: 49.4 us
  starting transfers between devices  19.6 us (40%)
  waiting for transfers between devices  16.1 us (32%)
  Pallas kernels  12.9 us (26%)
  between operations  0.71 us (1%)
    ppermute x16, starting transfers between devices, exchange(): got.append(lax.ppermute(value, axis, pairs))  19.6 us
    ppermute x16, waiting for transfers between devices, exchange(): got.append(lax.ppermute(value, axis, pairs))  16.1 us
    pallas_call x9, Pallas kernels, call(): pl.pallas_call(body, out_shape=out_shape, in_specs=[source] * len(args),...  12.9 us
  transfers between devices with their start and end apart: 16, of which 11 were waited for; matrix products, arithmetic and copies ran while one was open for 0% of the time, Pallas kernels for 5%

profile of v8, /device:TPU:0, one launch (start us, length us, event | category | flops | bytes accessed | tf_op | source)
XLA Modules:
  0.0 49.4 jit_solution(1281446333387924802)
XLA Ops:
  0.6 1.9 %shard_map.68 = (bf16[64,4096]{1,0:T(8,128)(2,1)S(1)}, s32[1,4096]{1,0:T(1,128)S(1)}, f32[1,4096]{1,0:T(1,128)S(1)}, f32[1,512]{1,0:T(1,128)S(1)}, bf16[64,512]{1,0:T(8,128)(2,1)S(1)}) custom-call(bf16[64,4096]{1,0:T(8,128)(2,1)} %feat_hbm.1, s32[1,512]{1,0:T(1,128)} %bitcast.6, s32[1,4096]{1,0:T(1,128)} %bitcast.4, f32[1,4096]{1,0:T(1,128)} %bitcast.5, ...), custom_call_target="tpu_custom_call" | custom-call | tf_op jit(solution)/shard_map/pallas_call | solution.py:270
  2.6 3.0 %collective-permute-start = (bf16[64,512]{1,0:T(8,128)(2,1)S(1)}, bf16[64,512]{1,0:T(8,128)(2,1)S(1)}, u32[]{:S(2)}, u32[]{:S(2)}) collective-permute-start(bf16[64,512]{1,0:T(8,128)(2,1)S(1)} %get-tuple-element.27.refs_1_), channel_id=1, source_target_pairs={{0,16},{16,0},{1,17},{17,1},{2,18},{18,2},{3,19},{19,3},{4,20},{20... | collective-permute-start | bytes 196616 | tf_op jit(solution)/shard_map/ppermute | solution.py:295
  5.6 0.7 %shard_map.69 = (bf16[256,4096]{1,0:T(8,128)(2,1)S(1)}, bf16[4096,256]{1,0:T(8,128)(2,1)S(1)}, bf16[16,4096]{1,0:T(8,128)(2,1)S(1)}) custom-call(bf16[64,4096]{1,0:T(8,128)(2,1)S(1)} %get-tuple-element.22.feat_ref, s32[1,4096]{1,0:T(1,128)S(1)} %get-tuple-element.23.slots_ref.refs_3_.refs_4_, f32[1,4096]{1,0:T(1,128)S(1)} %get-tuple-element.24.prices_ref), custom_call_target="tpu_custom_call" | custom-call | flops 4096000 | bytes 4194304 | tf_op jit(solution)/shard_map/pallas_call | solution.py:270
  6.3 1.6 %collective-permute-done.refs_0_ = bf16[64,512]{1,0:T(8,128)(2,1)S(1)} collective-permute-done((bf16[64,512]{1,0:T(8,128)(2,1)S(1)}, bf16[64,512]{1,0:T(8,128)(2,1)S(1)}, u32[]{:S(2)}, u32[]{:S(2)}) %collective-permute-start) | collective-permute-done | bytes 65568 | tf_op jit(solution)/shard_map/ppermute | solution.py:295
  7.8 2.5 %shard_map.70 = (bf16[8192,512]{1,0:T(8,128)(2,1)S(1)}, bf16[256,512]{1,0:T(8,128)(2,1)S(1)}, f32[8,512]{1,0:T(8,128)S(1)}) custom-call(bf16[4096,256]{1,0:T(8,128)(2,1)S(1)} %get-tuple-element.25.turned_ref, bf16[16,4096]{1,0:T(8,128)(2,1)S(1)} %get-tuple-element.26.weight_ref, bf16[64,512]{1,0:T(8,128)(2,1)S(1)} %collective-permute-done.refs_0_, ...), custom_call_target="tpu_custom_call" | custom-call | flops 134217728 | bytes 8388608 | tf_op jit(solution)/shard_map/pallas_call | solution.py:270
  10.3 2.1 %collective-permute-start.1 = (f32[8,512]{1,0:T(8,128)S(1)}, f32[8,512]{1,0:T(8,128)S(1)}, u32[]{:S(2)}, u32[]{:S(2)}) collective-permute-start(f32[8,512]{1,0:T(8,128)S(1)} %get-tuple-element.28.refs_1_), channel_id=1, source_target_pairs={{0,16},{16,0},{1,17},{17,1},{2,18},{18,2},{3,19},{19,3},{4,20},{20... | collective-permute-start | bytes 49160 | tf_op jit(solution)/shard_map/ppermute | solution.py:295
  12.4 1.9 %shard_map.71.refs_4_ = bf16[1024,4096]{1,0:T(8,128)(2,1)S(1)} custom-call(bf16[256,4096]{1,0:T(8,128)(2,1)S(1)} %get-tuple-element.30.columns_ref, bf16[256,512]{1,0:T(8,128)(2,1)S(1)} %get-tuple-element.31.center_ref), custom_call_target="tpu_custom_call" | custom-call | flops 134217728 | bytes 8388608 | tf_op jit(solution)/shard_map/pallas_call | solution.py:270
  14.4 0.0 collective-permute-done.1.refs_0_
  14.4 1.2 %shard_map.72 = (f32[8,512]{1,0:T(8,128)S(1)}, f32[1,4224]{1,0:T(1,128)S(1)}) custom-call(f32[8,512]{1,0:T(8,128)S(1)} %collective-permute-done.1.refs_0_, f32[8,512]{1,0:T(8,128)S(1)} %get-tuple-element.28.refs_1_, f32[1,512]{1,0:T(1,128)S(1)} %get-tuple-element.29.refs_2_, s32[1,4096]{1,0:T(1,128)S(1)} %get-tuple-element.23.slots_ref.refs_3_.refs_4_, ...), custom_call_target="tpu_custom_call" | custom-call | tf_op jit(solution)/shard_map/pallas_call | solution.py:270
  15.6 0.1 collective-permute-start.2
  15.7 1.9 %collective-permute-start.3 = (f32[1,4224]{1,0:T(1,128)S(1)}, f32[1,4224]{1,0:T(1,128)S(1)}, u32[]{:S(2)}, u32[]{:S(2)}) collective-permute-start(f32[1,4224]{1,0:T(1,128)S(1)} %get-tuple-element.32), channel_id=1, source_target_pairs={{0,2},{1,3},{2,0},{3,1},{4,6},{5,7},{6,4},{7,5},{8,10},{9,11},{10,... | collective-permute-start | bytes 50696 | tf_op jit(solution)/shard_map/ppermute | solution.py:295
  17.6 0.0 collective-permute-start.4
  17.6 1.2 %collective-permute-done.2 = f32[1,4224]{1,0:T(1,128)S(1)} collective-permute-done((f32[1,4224]{1,0:T(1,128)S(1)}, f32[1,4224]{1,0:T(1,128)S(1)}, u32[]{:S(2)}, u32[]{:S(2)}) %collective-permute-start.2) | collective-permute-done | bytes 16928 | tf_op jit(solution)/shard_map/ppermute | solution.py:295
  18.8 0.7 %collective-permute-done.3 = f32[1,4224]{1,0:T(1,128)S(1)} collective-permute-done((f32[1,4224]{1,0:T(1,128)S(1)}, f32[1,4224]{1,0:T(1,128)S(1)}, u32[]{:S(2)}, u32[]{:S(2)}) %collective-permute-start.3) | collective-permute-done | bytes 16928 | tf_op jit(solution)/shard_map/ppermute | solution.py:295
  19.5 0.0 collective-permute-done.4
  19.5 4.0 %collective-permute-start.5 = (f32[1,4224]{1,0:T(1,128)S(1)}, f32[1,4224]{1,0:T(1,128)S(1)}, u32[]{:S(2)}, u32[]{:S(2)}) collective-permute-start(f32[1,4224]{1,0:T(1,128)S(1)} %add_add_fusion.1.refs_3_), channel_id=1, source_target_pairs={{0,13},{1,12},{2,15},{3,14},{4,9},{5,8},{6,11},{7,10},{8,5},{9,4},... | collective-permute-start | bytes 50696 | tf_op jit(solution)/shard_map/ppermute | solution.py:295
  23.5 0.0 collective-permute-start.6
  23.5 0.5 collective-permute-start.7
  24.0 1.0 %collective-permute-done.5.refs_0_ = f32[1,4224]{1,0:T(1,128)S(1)} collective-permute-done((f32[1,4224]{1,0:T(1,128)S(1)}, f32[1,4224]{1,0:T(1,128)S(1)}, u32[]{:S(2)}, u32[]{:S(2)}) %collective-permute-start.5) | collective-permute-done | bytes 16928 | tf_op jit(solution)/shard_map/ppermute | solution.py:295
  25.0 2.6 %collective-permute-done.6.refs_1_ = f32[1,4224]{1,0:T(1,128)S(1)} collective-permute-done((f32[1,4224]{1,0:T(1,128)S(1)}, f32[1,4224]{1,0:T(1,128)S(1)}, u32[]{:S(2)}, u32[]{:S(2)}) %collective-permute-start.6) | collective-permute-done | bytes 16928 | tf_op jit(solution)/shard_map/ppermute | solution.py:295
  27.6 0.0 collective-permute-done.7.refs_2_
  27.6 1.2 %shard_map.73 = (f32[1,4224]{1,0:T(1,128)S(1)}, f32[8,640]{1,0:T(8,128)S(1)}) custom-call(f32[1,4224]{1,0:T(1,128)S(1)} %collective-permute-done.5.refs_0_, f32[1,4224]{1,0:T(1,128)S(1)} %collective-permute-done.6.refs_1_, f32[1,4224]{1,0:T(1,128)S(1)} %collective-permute-done.7.refs_2_, f32[1,4224]{1,0:T(1,128)S(1)} %add_add_fusion.1.refs_3_, ...), custom_call_target="tpu_custom_call" | custom-call | tf_op jit(solution)/shard_map/pallas_call | solution.py:270
  28.8 1.5 %collective-permute-start.8 = (f32[8,640]{1,0:T(8,128)S(1)}, f32[8,640]{1,0:T(8,128)S(1)}, u32[]{:S(2)}, u32[]{:S(2)}) collective-permute-start(f32[8,640]{1,0:T(8,128)S(1)} %get-tuple-element.34.refs_1_), channel_id=1, source_target_pairs={{0,16},{16,0},{1,17},{17,1},{2,18},{18,2},{3,19},{19,3},{4,20},{20... | collective-permute-start | bytes 61448 | tf_op jit(solution)/shard_map/ppermute | solution.py:295
  30.3 2.3 %collective-permute-done.8.refs_0_ = f32[8,640]{1,0:T(8,128)S(1)} collective-permute-done((f32[8,640]{1,0:T(8,128)S(1)}, f32[8,640]{1,0:T(8,128)S(1)}, u32[]{:S(2)}, u32[]{:S(2)}) %collective-permute-start.8) | collective-permute-done | bytes 20512 | tf_op jit(solution)/shard_map/ppermute | solution.py:295
  32.6 1.4 %shard_map.74 = (f32[8,512]{1,0:T(8,128)S(1)}, f32[8,128]{1,0:T(8,128)S(1)}, f32[1,4224]{1,0:T(1,128)S(1)}) custom-call(f32[8,640]{1,0:T(8,128)S(1)} %collective-permute-done.8.refs_0_, f32[8,640]{1,0:T(8,128)S(1)} %get-tuple-element.34.refs_1_, f32[1,512]{1,0:T(1,128)S(1)} %get-tuple-element.29.refs_2_, ...), custom_call_target="tpu_custom_call" | custom-call | tf_op jit(solution)/shard_map/pallas_call | solution.py:270
  34.0 0.5 collective-permute-start.10
  34.4 0.4 collective-permute-start.11
  34.8 1.1 %collective-permute-start.9 = (f32[1,4224]{1,0:T(1,128)S(1)}, f32[1,4224]{1,0:T(1,128)S(1)}, u32[]{:S(2)}, u32[]{:S(2)}) collective-permute-start(f32[1,4224]{1,0:T(1,128)S(1)} %get-tuple-element.37), channel_id=1, source_target_pairs={{0,1},{1,0},{2,3},{3,2},{4,5},{5,4},{6,7},{7,6},{8,9},{9,8},{10,11... | collective-permute-start | bytes 50696 | tf_op jit(solution)/shard_map/ppermute | solution.py:295
  35.9 1.3 %collective-permute-done.10 = f32[1,4224]{1,0:T(1,128)S(1)} collective-permute-done((f32[1,4224]{1,0:T(1,128)S(1)}, f32[1,4224]{1,0:T(1,128)S(1)}, u32[]{:S(2)}, u32[]{:S(2)}) %collective-permute-start.10) | collective-permute-done | bytes 16928 | tf_op jit(solution)/shard_map/ppermute | solution.py:295
  37.2 1.0 %collective-permute-done.11 = f32[1,4224]{1,0:T(1,128)S(1)} collective-permute-done((f32[1,4224]{1,0:T(1,128)S(1)}, f32[1,4224]{1,0:T(1,128)S(1)}, u32[]{:S(2)}, u32[]{:S(2)}) %collective-permute-start.11) | collective-permute-done | bytes 16928 | tf_op jit(solution)/shard_map/ppermute | solution.py:295
  38.2 0.0 collective-permute-done.9
  38.2 1.0 %collective-permute-start.12 = (f32[1,4224]{1,0:T(1,128)S(1)}, f32[1,4224]{1,0:T(1,128)S(1)}, u32[]{:S(2)}, u32[]{:S(2)}) collective-permute-start(f32[1,4224]{1,0:T(1,128)S(1)} %add_add_fusion.refs_3_), channel_id=1, source_target_pairs={{0,13},{1,12},{2,15},{3,14},{4,9},{5,8},{6,11},{7,10},{8,5},{9,4},... | collective-permute-start | bytes 50696 | tf_op jit(solution)/shard_map/ppermute | solution.py:295
  39.3 0.5 %collective-permute-start.13 = (f32[1,4224]{1,0:T(1,128)S(1)}, f32[1,4224]{1,0:T(1,128)S(1)}, u32[]{:S(2)}, u32[]{:S(2)}) collective-permute-start(f32[1,4224]{1,0:T(1,128)S(1)} %add_add_fusion.refs_3_), channel_id=1, source_target_pairs={{0,9},{1,8},{2,11},{3,10},{4,13},{5,12},{6,15},{7,14},{8,1},{9,0},... | collective-permute-start | bytes 50696 | tf_op jit(solution)/shard_map/ppermute | solution.py:295
  39.8 1.5 %collective-permute-start.14 = (f32[1,4224]{1,0:T(1,128)S(1)}, f32[1,4224]{1,0:T(1,128)S(1)}, u32[]{:S(2)}, u32[]{:S(2)}) collective-permute-start(f32[1,4224]{1,0:T(1,128)S(1)} %add_add_fusion.refs_3_), channel_id=1, source_target_pairs={{0,5},{1,4},{2,7},{3,6},{4,1},{5,0},{6,3},{7,2},{8,13},{9,12},{10,... | collective-permute-start | bytes 50696 | tf_op jit(solution)/shard_map/ppermute | solution.py:295
  41.3 2.0 %collective-permute-done.12.refs_0_ = f32[1,4224]{1,0:T(1,128)S(1)} collective-permute-done((f32[1,4224]{1,0:T(1,128)S(1)}, f32[1,4224]{1,0:T(1,128)S(1)}, u32[]{:S(2)}, u32[]{:S(2)}) %collective-permute-start.12) | collective-permute-done | bytes 16928 | tf_op jit(solution)/shard_map/ppermute | solution.py:295
  43.3 0.2 collective-permute-done.13.refs_1_
  43.4 0.0 collective-permute-done.14.refs_2_
  43.4 1.3 %shard_map.75 = (f32[8,128]{1,0:T(8,128)S(1)}, f32[8,640]{1,0:T(8,128)S(1)}) custom-call(f32[1,4224]{1,0:T(1,128)S(1)} %collective-permute-done.12.refs_0_, f32[1,4224]{1,0:T(1,128)S(1)} %collective-permute-done.13.refs_1_, f32[1,4224]{1,0:T(1,128)S(1)} %collective-permute-done.14.refs_2_, f32[1,4224]{1,0:T(1,128)S(1)} %add_add_fusion.refs_3_, ...), custom_call_target="tpu_custom_call" | custom-call | tf_op jit(solution)/shard_map/pallas_call | solution.py:270
  44.7 1.5 %collective-permute-start.15 = (f32[8,640]{1,0:T(8,128)S(1)}, f32[8,640]{1,0:T(8,128)S(1)}, u32[]{:S(2)}, u32[]{:S(2)}) collective-permute-start(f32[8,640]{1,0:T(8,128)S(1)} %get-tuple-element.38.refs_1_), channel_id=1, source_target_pairs={{0,16},{16,0},{1,17},{17,1},{2,18},{18,2},{3,19},{19,3},{4,20},{20... | collective-permute-start | bytes 61448 | tf_op jit(solution)/shard_map/ppermute | solution.py:295
  46.2 2.3 %collective-permute-done.15.refs_0_ = f32[8,640]{1,0:T(8,128)S(1)} collective-permute-done((f32[8,640]{1,0:T(8,128)S(1)}, f32[8,640]{1,0:T(8,128)S(1)}, u32[]{:S(2)}, u32[]{:S(2)}) %collective-permute-start.15) | collective-permute-done | bytes 20512 | tf_op jit(solution)/shard_map/ppermute | solution.py:295
  48.5 0.9 %shard_map.76 = (f32[8,512]{1,0:T(8,128)}, f32[8,512]{1,0:T(8,128)}) custom-call(f32[8,640]{1,0:T(8,128)S(1)} %collective-permute-done.15.refs_0_, f32[8,640]{1,0:T(8,128)S(1)} %get-tuple-element.38.refs_1_, f32[1,512]{1,0:T(1,128)S(1)} %get-tuple-element.29.refs_2_, f32[8,512]{1,0:T(8,128)S(1)} %get-tuple-element.35.refs_5_.refs_3_, ...), custom_call_target="tpu_custom_call" | custom-call | tf_op jit(solution)/shard_map/pallas_call | solution.py:270
  (2 shorter events, 0.1 us)
Async XLA Ops:
  2.6 5.3 %collective-permute-start = (bf16[64,512]{1,0:T(8,128)(2,1)S(1)}, bf16[64,512]{1,0:T(8,128)(2,1)S(1)}, u32[]{:S(2)}, u32[]{:S(2)}) collective-permute-start(bf16[64,512]{1,0:T(8,128)(2,1)S(1)} %get-tuple-element.27.refs_1_), channel_id=1, source_target_pairs={{0,16},{16,0},{1,17},{17,1},{2,18},{18,2},{3,19},{19,3},{4,20},{20... | collective-permute-start | bytes 196616 | tf_op jit(solution)/shard_map/ppermute | solution.py:295
  10.3 4.1 %collective-permute-start.1 = (f32[8,512]{1,0:T(8,128)S(1)}, f32[8,512]{1,0:T(8,128)S(1)}, u32[]{:S(2)}, u32[]{:S(2)}) collective-permute-start(f32[8,512]{1,0:T(8,128)S(1)} %get-tuple-element.28.refs_1_), channel_id=1, source_target_pairs={{0,16},{16,0},{1,17},{17,1},{2,18},{18,2},{3,19},{19,3},{4,20},{20... | collective-permute-start | bytes 49160 | tf_op jit(solution)/shard_map/ppermute | solution.py:295
  15.6 3.2 %collective-permute-start.2 = (f32[1,4224]{1,0:T(1,128)S(1)}, f32[1,4224]{1,0:T(1,128)S(1)}, u32[]{:S(2)}, u32[]{:S(2)}) collective-permute-start(f32[1,4224]{1,0:T(1,128)S(1)} %get-tuple-element.32), channel_id=1, source_target_pairs={{0,3},{1,2},{2,1},{3,0},{4,7},{5,6},{6,5},{7,4},{8,11},{9,10},{10,... | collective-permute-start | bytes 50696 | tf_op jit(solution)/shard_map/ppermute | solution.py:295
  15.7 3.8 %collective-permute-start.3 = (f32[1,4224]{1,0:T(1,128)S(1)}, f32[1,4224]{1,0:T(1,128)S(1)}, u32[]{:S(2)}, u32[]{:S(2)}) collective-permute-start(f32[1,4224]{1,0:T(1,128)S(1)} %get-tuple-element.32), channel_id=1, source_target_pairs={{0,2},{1,3},{2,0},{3,1},{4,6},{5,7},{6,4},{7,5},{8,10},{9,11},{10,... | collective-permute-start | bytes 50696 | tf_op jit(solution)/shard_map/ppermute | solution.py:295
  17.6 1.9 %collective-permute-start.4 = (f32[1,4224]{1,0:T(1,128)S(1)}, f32[1,4224]{1,0:T(1,128)S(1)}, u32[]{:S(2)}, u32[]{:S(2)}) collective-permute-start(f32[1,4224]{1,0:T(1,128)S(1)} %get-tuple-element.32), channel_id=1, source_target_pairs={{0,1},{1,0},{2,3},{3,2},{4,5},{5,4},{6,7},{7,6},{8,9},{9,8},{10,11... | collective-permute-start | bytes 50696 | tf_op jit(solution)/shard_map/ppermute | solution.py:295
  19.5 5.5 %collective-permute-start.5 = (f32[1,4224]{1,0:T(1,128)S(1)}, f32[1,4224]{1,0:T(1,128)S(1)}, u32[]{:S(2)}, u32[]{:S(2)}) collective-permute-start(f32[1,4224]{1,0:T(1,128)S(1)} %add_add_fusion.1.refs_3_), channel_id=1, source_target_pairs={{0,13},{1,12},{2,15},{3,14},{4,9},{5,8},{6,11},{7,10},{8,5},{9,4},... | collective-permute-start | bytes 50696 | tf_op jit(solution)/shard_map/ppermute | solution.py:295
  23.5 4.1 %collective-permute-start.6 = (f32[1,4224]{1,0:T(1,128)S(1)}, f32[1,4224]{1,0:T(1,128)S(1)}, u32[]{:S(2)}, u32[]{:S(2)}) collective-permute-start(f32[1,4224]{1,0:T(1,128)S(1)} %add_add_fusion.1.refs_3_), channel_id=1, source_target_pairs={{0,9},{1,8},{2,11},{3,10},{4,13},{5,12},{6,15},{7,14},{8,1},{9,0},... | collective-permute-start | bytes 50696 | tf_op jit(solution)/shard_map/ppermute | solution.py:295
  23.5 4.1 %collective-permute-start.7 = (f32[1,4224]{1,0:T(1,128)S(1)}, f32[1,4224]{1,0:T(1,128)S(1)}, u32[]{:S(2)}, u32[]{:S(2)}) collective-permute-start(f32[1,4224]{1,0:T(1,128)S(1)} %add_add_fusion.1.refs_3_), channel_id=1, source_target_pairs={{0,5},{1,4},{2,7},{3,6},{4,1},{5,0},{6,3},{7,2},{8,13},{9,12},{10,... | collective-permute-start | bytes 50696 | tf_op jit(solution)/shard_map/ppermute | solution.py:295
  28.8 3.8 %collective-permute-start.8 = (f32[8,640]{1,0:T(8,128)S(1)}, f32[8,640]{1,0:T(8,128)S(1)}, u32[]{:S(2)}, u32[]{:S(2)}) collective-permute-start(f32[8,640]{1,0:T(8,128)S(1)} %get-tuple-element.34.refs_1_), channel_id=1, source_target_pairs={{0,16},{16,0},{1,17},{17,1},{2,18},{18,2},{3,19},{19,3},{4,20},{20... | collective-permute-start | bytes 61448 | tf_op jit(solution)/shard_map/ppermute | solution.py:295
  34.0 3.2 %collective-permute-start.10 = (f32[1,4224]{1,0:T(1,128)S(1)}, f32[1,4224]{1,0:T(1,128)S(1)}, u32[]{:S(2)}, u32[]{:S(2)}) collective-permute-start(f32[1,4224]{1,0:T(1,128)S(1)} %get-tuple-element.37), channel_id=1, source_target_pairs={{0,3},{1,2},{2,1},{3,0},{4,7},{5,6},{6,5},{7,4},{8,11},{9,10},{10,... | collective-permute-start | bytes 50696 | tf_op jit(solution)/shard_map/ppermute | solution.py:295
  34.4 3.7 %collective-permute-start.11 = (f32[1,4224]{1,0:T(1,128)S(1)}, f32[1,4224]{1,0:T(1,128)S(1)}, u32[]{:S(2)}, u32[]{:S(2)}) collective-permute-start(f32[1,4224]{1,0:T(1,128)S(1)} %get-tuple-element.37), channel_id=1, source_target_pairs={{0,2},{1,3},{2,0},{3,1},{4,6},{5,7},{6,4},{7,5},{8,10},{9,11},{10,... | collective-permute-start | bytes 50696 | tf_op jit(solution)/shard_map/ppermute | solution.py:295
  34.8 3.4 %collective-permute-start.9 = (f32[1,4224]{1,0:T(1,128)S(1)}, f32[1,4224]{1,0:T(1,128)S(1)}, u32[]{:S(2)}, u32[]{:S(2)}) collective-permute-start(f32[1,4224]{1,0:T(1,128)S(1)} %get-tuple-element.37), channel_id=1, source_target_pairs={{0,1},{1,0},{2,3},{3,2},{4,5},{5,4},{6,7},{7,6},{8,9},{9,8},{10,11... | collective-permute-start | bytes 50696 | tf_op jit(solution)/shard_map/ppermute | solution.py:295
  38.2 5.0 %collective-permute-start.12 = (f32[1,4224]{1,0:T(1,128)S(1)}, f32[1,4224]{1,0:T(1,128)S(1)}, u32[]{:S(2)}, u32[]{:S(2)}) collective-permute-start(f32[1,4224]{1,0:T(1,128)S(1)} %add_add_fusion.refs_3_), channel_id=1, source_target_pairs={{0,13},{1,12},{2,15},{3,14},{4,9},{5,8},{6,11},{7,10},{8,5},{9,4},... | collective-permute-start | bytes 50696 | tf_op jit(solution)/shard_map/ppermute | solution.py:295
  39.3 4.2 %collective-permute-start.13 = (f32[1,4224]{1,0:T(1,128)S(1)}, f32[1,4224]{1,0:T(1,128)S(1)}, u32[]{:S(2)}, u32[]{:S(2)}) collective-permute-start(f32[1,4224]{1,0:T(1,128)S(1)} %add_add_fusion.refs_3_), channel_id=1, source_target_pairs={{0,9},{1,8},{2,11},{3,10},{4,13},{5,12},{6,15},{7,14},{8,1},{9,0},... | collective-permute-start | bytes 50696 | tf_op jit(solution)/shard_map/ppermute | solution.py:295
  39.8 3.7 %collective-permute-start.14 = (f32[1,4224]{1,0:T(1,128)S(1)}, f32[1,4224]{1,0:T(1,128)S(1)}, u32[]{:S(2)}, u32[]{:S(2)}) collective-permute-start(f32[1,4224]{1,0:T(1,128)S(1)} %add_add_fusion.refs_3_), channel_id=1, source_target_pairs={{0,5},{1,4},{2,7},{3,6},{4,1},{5,0},{6,3},{7,2},{8,13},{9,12},{10,... | collective-permute-start | bytes 50696 | tf_op jit(solution)/shard_map/ppermute | solution.py:295
  44.7 3.8 %collective-permute-start.15 = (f32[8,640]{1,0:T(8,128)S(1)}, f32[8,640]{1,0:T(8,128)S(1)}, u32[]{:S(2)}, u32[]{:S(2)}) collective-permute-start(f32[8,640]{1,0:T(8,128)S(1)} %get-tuple-element.38.refs_1_), channel_id=1, source_target_pairs={{0,16},{16,0},{1,17},{17,1},{2,18},{18,2},{3,19},{19,3},{4,20},{20... | collective-permute-start | bytes 61448 | tf_op jit(solution)/shard_map/ppermute | solution.py:295

commit v9 on v8

--- a/solution.py
+++ b/solution.py
@@ -50,6 +50,14 @@
 
 def from_lanes(row, first):
     return jnp.sum(jnp.where(slot_lanes(first), row, 0.0), axis=1, keepdims=True)
+
+
+def spread(column):
+    return jnp.broadcast_to(column, (SLOTS, EXTRA))
+
+
+def wide(narrow, count):
+    return jnp.concatenate([narrow] * (count // EXTRA), axis=1)
 
 
 def pair_total(parts):
@@ -193,7 +201,7 @@
         stack2(weight), block_ref[0:row_count, :], block_ref[row_count:, :]
     )
     square = row_sum(weight * weight)
-    out_ref[:, count : count + EXTRA] = jnp.broadcast_to(square, (SLOTS, EXTRA))
+    out_ref[:, count : count + EXTRA] = spread(square)
 
 
 def first_apply_body(parts, scale_over_root, *refs):
@@ -208,26 +216,28 @@
 
 def first_fold_body(parts, *refs):
     row_refs = refs[:parts]
-    slots_ref, block_ref, rows_ref, out_ref = refs[parts:]
+    slots_ref, block_ref, rows_ref, norm_ref, out_ref = refs[parts:]
+    row_count = slots_ref.shape[1]
     rows = total_of(row_refs)
     rows_ref[...] = rows
-    fold_rows(rows[:, 0 : slots_ref.shape[1]], block_ref, slots_ref, out_ref)
+    norm_ref[...] = spread(from_lanes(rows[:, row_count:], 0))
+    fold_rows(rows[:, 0:row_count], block_ref, slots_ref, out_ref)
 
 
 def second_apply_body(parts, inv_rows, *refs):
     fold_refs = refs[:parts]
-    (scale_ref, slots_ref, turned_ref, target_ref, rows_ref,
+    (scale_ref, slots_ref, turned_ref, target_ref, norm_ref,
      residual_ref, step_ref, out_ref) = refs[parts:]
     row_count, count = turned_ref.shape[1], scale_ref.shape[1]
     folded = total_of(fold_refs)
     scale = scale_ref[...]
     target = target_ref[...]
-    norm = from_lanes(rows_ref[:, row_count:], 0)
+    norm = norm_ref[...]
     applied = scale * folded[:, 0:count] * inv_rows + RIDGE * target
-    step = norm / (folded[:, count : count + 1] * inv_rows + RIDGE * norm)
-    residual = target - step * applied
+    step = norm / (folded[:, count:] * inv_rows + RIDGE * norm)
+    residual = target - wide(step, count) * applied
     residual_ref[...] = residual
-    step_ref[...] = jnp.broadcast_to(step, step_ref.shape)
+    step_ref[...] = step
     out_ref[:, row_count:] = to_lanes(row_sum(residual * residual), 0) + to_lanes(
         row_sum(residual * target), SLOTS
     )
@@ -236,33 +246,33 @@
 
 def second_fold_body(parts, *refs):
     row_refs = refs[:parts]
-    slots_ref, block_ref, rows_ref, sums_ref, out_ref = refs[parts:]
+    slots_ref, block_ref, rows_ref, norm_ref, sums_ref, out_ref = refs[parts:]
     row_count = slots_ref.shape[1]
     latest = total_of(row_refs)
-    first_norm = from_lanes(rows_ref[:, row_count:], 0)
-    norm = from_lanes(latest[:, row_count:], 0)
-    cross = from_lanes(latest[:, row_count:], SLOTS)
-    lane = lax.broadcasted_iota(jnp.int32, (SLOTS, EXTRA), 1)
-    sums_ref[...] = jnp.where(lane == 0, first_norm, jnp.where(lane == 1, norm, cross))
-    rows = latest[:, 0:row_count] + (norm / first_norm) * rows_ref[:, 0:row_count]
+    norm = spread(from_lanes(latest[:, row_count:], 0))
+    ratio = norm / norm_ref[...]
+    sums_ref[:, 0:EXTRA] = norm
+    sums_ref[:, EXTRA:] = spread(from_lanes(latest[:, row_count:], SLOTS))
+    rows = latest[:, 0:row_count] + wide(ratio, row_count) * rows_ref[:, 0:row_count]
     fold_rows(rows, block_ref, slots_ref, out_ref)
 
 
 def finish_body(parts, inv_rows, *refs):
     fold_refs = refs[:parts]
-    (scale_ref, target_ref, residual_ref, step_ref, sums_ref,
+    (scale_ref, target_ref, residual_ref, step_ref, norm_ref, sums_ref,
      coefficients_ref, out_ref) = refs[parts:]
     count = scale_ref.shape[1]
     folded = total_of(fold_refs)
     target = target_ref[...]
     residual = residual_ref[...]
-    first_norm, norm, cross = (sums_ref[:, i : i + 1] for i in range(3))
+    first_norm = norm_ref[...]
+    norm, cross = sums_ref[:, 0:EXTRA], sums_ref[:, EXTRA:]
     ratio = norm / first_norm
-    direction = residual + ratio * target
+    direction = residual + wide(ratio, count) * target
     square = norm + 2.0 * ratio * cross + ratio * ratio * first_norm
     applied = scale_ref[...] * folded[:, 0:count] * inv_rows + RIDGE * direction
-    step = norm / (folded[:, count : count + 1] * inv_rows + RIDGE * square)
-    coefficients_ref[...] = step_ref[:, 0:1] * target + step * direction
+    step = wide(norm / (folded[:, count:] * inv_rows + RIDGE * square), count)
+    coefficients_ref[...] = wide(step_ref[...], count) * target + step * direction
     out_ref[...] = residual - step * applied
 
 
@@ -282,21 +292,18 @@
 
 def exchange(value, axis, near_first=False):
     size = lax.axis_size(axis)
+    bits = size.bit_length() - 1
     parts = [value]
-    stride = 1
-    while stride < size:
+    for low in range((bits + 1) // 2):
         value = pair_total(parts)
+        near, far = 1 << low, 1 << (bits - 1 - low)
+        side = 0 if low == 0 else 1
         parts = [value]
-        span = min(4, size // stride)
-        side = 0 if stride == 1 else 1
-        got = []
-        for offset in reversed(range(1, span)):
-            pairs = [(i, i ^ (offset * stride) ^ side) for i in range(size)]
-            got.append(lax.ppermute(value, axis, pairs))
-        parts = got + parts
-        if near_first and stride == 1:
+        for step in (near, far, near | far) if near != far else (near,):
+            pairs = [(i, i ^ step ^ side) for i in range(size)]
+            parts.insert(0, lax.ppermute(value, axis, pairs))
+        if near_first and low == 0:
             parts = parts[-2:] + parts[:-2]
-        stride *= span
     return parts
 
 
@@ -369,26 +376,26 @@
         *firsts, scale, slots, turned,
     )
     rows = exchange(rows, "centers")
-    rows, folded = call(
-        partial(first_fold_body, len(rows)), (row_shape, fold_shape), *rows, slots, block
+    rows, norm, folded = call(
+        partial(first_fold_body, len(rows)), (row_shape, narrow, fold_shape), *rows, slots, block
     )
     folds = exchange(folded, "dp")
     residual, step, latest = call(
         partial(second_apply_body, len(folds), 1.0 / all_rows),
         (vector, narrow, row_shape),
-        *folds, scale, slots, turned, target, rows,
+        *folds, scale, slots, turned, target, norm,
     )
     latest = exchange(latest, "centers", True)
     sums, folded = call(
         partial(second_fold_body, len(latest)),
-        (narrow, fold_shape),
-        *latest, slots, block, rows,
+        (shaped((SLOTS, 2 * EXTRA)), fold_shape),
+        *latest, slots, block, rows, norm,
     )
     folds = exchange(folded, "dp")
     return call(
         partial(finish_body, len(folds), 1.0 / all_rows),
         (vector, vector),
-        *folds, scale, target, residual, step, sums,
+        *folds, scale, target, residual, step, norm, sums,
     )
 
 

time: 49.6 us -> 49.7 us (level)
  starting transfers between devices: 19.6 us -> 21.5 us
  waiting for transfers between devices: 16.1 us -> 14.7 us
    ppermute x16, starting transfers between devices: 19.6 us -> 21.5 us  [exchange(): parts.insert(0, lax.ppermute(value, axis, pairs))]
    ppermute x16, waiting for transfers between devices: 16.1 us -> 14.7 us  [exchange(): parts.insert(0, lax.ppermute(value, axis, pairs))]
  transfers between devices with their start and end apart: 16 -> 16, of which waited for: 11 -> 12; matrix products, arithmetic and copies ran while one was open for 0% -> 0% of each run, Pallas kernels for 5% -> 5%
where the time goes in v9:
time: 49.7 us; the launch traced here: 49.5 us
  starting transfers between devices  21.5 us (43%)
  waiting for transfers between devices  14.7 us (30%)
  Pallas kernels  12.6 us (25%)
  between operations  0.7 us (1%)
    ppermute x16, starting transfers between devices, exchange(): parts.insert(0, lax.ppermute(value, axis, pairs))  21.5 us
    ppermute x16, waiting for transfers between devices, exchange(): parts.insert(0, lax.ppermute(value, axis, pairs))  14.7 us
    pallas_call x9, Pallas kernels, call(): pl.pallas_call(body, out_shape=out_shape, in_specs=[source] * len(args),...  12.6 us
  transfers between devices with their start and end apart: 16, of which 12 were waited for; matrix products, arithmetic and copies ran while one was open for 0% of the time, Pallas kernels for 5%

profile of v9, /device:TPU:0, one launch (start us, length us, event | category | flops | bytes accessed | tf_op | source)
XLA Modules:
  0.0 49.5 jit_solution(11971135233224503719)
XLA Ops:
  0.6 1.9 %shard_map.68 = (bf16[64,4096]{1,0:T(8,128)(2,1)S(1)}, s32[1,4096]{1,0:T(1,128)S(1)}, f32[1,4096]{1,0:T(1,128)S(1)}, f32[1,512]{1,0:T(1,128)S(1)}, bf16[64,512]{1,0:T(8,128)(2,1)S(1)}) custom-call(bf16[64,4096]{1,0:T(8,128)(2,1)} %feat_hbm.1, s32[1,512]{1,0:T(1,128)} %bitcast.6, s32[1,4096]{1,0:T(1,128)} %bitcast.4, f32[1,4096]{1,0:T(1,128)} %bitcast.5, ...), custom_call_target="tpu_custom_call" | custom-call | tf_op jit(solution)/shard_map/pallas_call | solution.py:280
  2.6 3.0 %collective-permute-start = (bf16[64,512]{1,0:T(8,128)(2,1)S(1)}, bf16[64,512]{1,0:T(8,128)(2,1)S(1)}, u32[]{:S(2)}, u32[]{:S(2)}) collective-permute-start(bf16[64,512]{1,0:T(8,128)(2,1)S(1)} %get-tuple-element.28.refs_1_), channel_id=1, source_target_pairs={{0,16},{16,0},{1,17},{17,1},{2,18},{18,2},{3,19},{19,3},{4,20},{20... | collective-permute-start | bytes 196616 | tf_op jit(solution)/shard_map/ppermute | solution.py:304
  5.6 0.7 %shard_map.69 = (bf16[256,4096]{1,0:T(8,128)(2,1)S(1)}, bf16[4096,256]{1,0:T(8,128)(2,1)S(1)}, bf16[16,4096]{1,0:T(8,128)(2,1)S(1)}) custom-call(bf16[64,4096]{1,0:T(8,128)(2,1)S(1)} %get-tuple-element.23.feat_ref, s32[1,4096]{1,0:T(1,128)S(1)} %get-tuple-element.24.slots_ref.refs_3_.refs_4_, f32[1,4096]{1,0:T(1,128)S(1)} %get-tuple-element.25.prices_ref), custom_call_target="tpu_custom_call" | custom-call | flops 4096000 | bytes 4194304 | tf_op jit(solution)/shard_map/pallas_call | solution.py:280
  6.3 1.6 %collective-permute-done.refs_0_ = bf16[64,512]{1,0:T(8,128)(2,1)S(1)} collective-permute-done((bf16[64,512]{1,0:T(8,128)(2,1)S(1)}, bf16[64,512]{1,0:T(8,128)(2,1)S(1)}, u32[]{:S(2)}, u32[]{:S(2)}) %collective-permute-start) | collective-permute-done | bytes 65568 | tf_op jit(solution)/shard_map/ppermute | solution.py:304
  7.8 2.5 %shard_map.70 = (bf16[8192,512]{1,0:T(8,128)(2,1)S(1)}, bf16[256,512]{1,0:T(8,128)(2,1)S(1)}, f32[8,512]{1,0:T(8,128)S(1)}) custom-call(bf16[4096,256]{1,0:T(8,128)(2,1)S(1)} %get-tuple-element.26.turned_ref, bf16[16,4096]{1,0:T(8,128)(2,1)S(1)} %get-tuple-element.27.weight_ref, bf16[64,512]{1,0:T(8,128)(2,1)S(1)} %collective-permute-done.refs_0_, ...), custom_call_target="tpu_custom_call" | custom-call | flops 134217728 | bytes 8388608 | tf_op jit(solution)/shard_map/pallas_call | solution.py:280
  10.4 2.1 %collective-permute-start.1 = (f32[8,512]{1,0:T(8,128)S(1)}, f32[8,512]{1,0:T(8,128)S(1)}, u32[]{:S(2)}, u32[]{:S(2)}) collective-permute-start(f32[8,512]{1,0:T(8,128)S(1)} %get-tuple-element.29.refs_1_), channel_id=1, source_target_pairs={{0,16},{16,0},{1,17},{17,1},{2,18},{18,2},{3,19},{19,3},{4,20},{20... | collective-permute-start | bytes 49160 | tf_op jit(solution)/shard_map/ppermute | solution.py:304
  12.5 1.9 %shard_map.71.refs_4_ = bf16[1024,4096]{1,0:T(8,128)(2,1)S(1)} custom-call(bf16[256,4096]{1,0:T(8,128)(2,1)S(1)} %get-tuple-element.31.columns_ref, bf16[256,512]{1,0:T(8,128)(2,1)S(1)} %get-tuple-element.32.center_ref), custom_call_target="tpu_custom_call" | custom-call | flops 134217728 | bytes 8388608 | tf_op jit(solution)/shard_map/pallas_call | solution.py:280
  14.4 0.0 collective-permute-done.1.refs_0_
  14.4 1.2 %shard_map.72 = (f32[8,512]{1,0:T(8,128)S(1)}, f32[1,4224]{1,0:T(1,128)S(1)}) custom-call(f32[8,512]{1,0:T(8,128)S(1)} %collective-permute-done.1.refs_0_, f32[8,512]{1,0:T(8,128)S(1)} %get-tuple-element.29.refs_1_, f32[1,512]{1,0:T(1,128)S(1)} %get-tuple-element.30.refs_2_, s32[1,4096]{1,0:T(1,128)S(1)} %get-tuple-element.24.slots_ref.refs_3_.refs_4_, ...), custom_call_target="tpu_custom_call" | custom-call | tf_op jit(solution)/shard_map/pallas_call | solution.py:280
  15.6 0.7 %collective-permute-start.2 = (f32[1,4224]{1,0:T(1,128)S(1)}, f32[1,4224]{1,0:T(1,128)S(1)}, u32[]{:S(2)}, u32[]{:S(2)}) collective-permute-start(f32[1,4224]{1,0:T(1,128)S(1)} %get-tuple-element.33), channel_id=1, source_target_pairs={{0,9},{1,8},{2,11},{3,10},{4,13},{5,12},{6,15},{7,14},{8,1},{9,0},... | collective-permute-start | bytes 50696 | tf_op jit(solution)/shard_map/ppermute | solution.py:304
  16.3 2.4 %collective-permute-start.3 = (f32[1,4224]{1,0:T(1,128)S(1)}, f32[1,4224]{1,0:T(1,128)S(1)}, u32[]{:S(2)}, u32[]{:S(2)}) collective-permute-start(f32[1,4224]{1,0:T(1,128)S(1)} %get-tuple-element.33), channel_id=1, source_target_pairs={{0,8},{1,9},{2,10},{3,11},{4,12},{5,13},{6,14},{7,15},{8,0},{9,1},... | collective-permute-start | bytes 50696 | tf_op jit(solution)/shard_map/ppermute | solution.py:304
  18.7 0.0 collective-permute-start.4
  18.7 1.1 %collective-permute-done.2 = f32[1,4224]{1,0:T(1,128)S(1)} collective-permute-done((f32[1,4224]{1,0:T(1,128)S(1)}, f32[1,4224]{1,0:T(1,128)S(1)}, u32[]{:S(2)}, u32[]{:S(2)}) %collective-permute-start.2) | collective-permute-done | bytes 16928 | tf_op jit(solution)/shard_map/ppermute | solution.py:304
  19.8 1.2 %collective-permute-done.3 = f32[1,4224]{1,0:T(1,128)S(1)} collective-permute-done((f32[1,4224]{1,0:T(1,128)S(1)}, f32[1,4224]{1,0:T(1,128)S(1)}, u32[]{:S(2)}, u32[]{:S(2)}) %collective-permute-start.3) | collective-permute-done | bytes 16928 | tf_op jit(solution)/shard_map/ppermute | solution.py:304
  21.0 0.0 collective-permute-done.4
  21.0 3.4 %collective-permute-start.5 = (f32[1,4224]{1,0:T(1,128)S(1)}, f32[1,4224]{1,0:T(1,128)S(1)}, u32[]{:S(2)}, u32[]{:S(2)}) collective-permute-start(f32[1,4224]{1,0:T(1,128)S(1)} %add_add_fusion.1.refs_3_), channel_id=1, source_target_pairs={{0,7},{1,6},{2,5},{3,4},{4,3},{5,2},{6,1},{7,0},{8,15},{9,14},{10,... | collective-permute-start | bytes 50696 | tf_op jit(solution)/shard_map/ppermute | solution.py:304
  24.4 0.0 collective-permute-start.6
  24.4 0.7 %collective-permute-start.7 = (f32[1,4224]{1,0:T(1,128)S(1)}, f32[1,4224]{1,0:T(1,128)S(1)}, u32[]{:S(2)}, u32[]{:S(2)}) collective-permute-start(f32[1,4224]{1,0:T(1,128)S(1)} %add_add_fusion.1.refs_3_), channel_id=1, source_target_pairs={{0,3},{1,2},{2,1},{3,0},{4,7},{5,6},{6,5},{7,4},{8,11},{9,10},{10,... | collective-permute-start | bytes 50696 | tf_op jit(solution)/shard_map/ppermute | solution.py:304
  25.1 0.8 %collective-permute-done.5.refs_0_ = f32[1,4224]{1,0:T(1,128)S(1)} collective-permute-done((f32[1,4224]{1,0:T(1,128)S(1)}, f32[1,4224]{1,0:T(1,128)S(1)}, u32[]{:S(2)}, u32[]{:S(2)}) %collective-permute-start.5) | collective-permute-done | bytes 16928 | tf_op jit(solution)/shard_map/ppermute | solution.py:304
  25.9 1.7 %collective-permute-done.6.refs_1_ = f32[1,4224]{1,0:T(1,128)S(1)} collective-permute-done((f32[1,4224]{1,0:T(1,128)S(1)}, f32[1,4224]{1,0:T(1,128)S(1)}, u32[]{:S(2)}, u32[]{:S(2)}) %collective-permute-start.6) | collective-permute-done | bytes 16928 | tf_op jit(solution)/shard_map/ppermute | solution.py:304
  27.6 0.0 collective-permute-done.7.refs_2_
  27.6 1.2 %shard_map.73 = (f32[1,4224]{1,0:T(1,128)S(1)}, f32[8,128]{1,0:T(8,128)S(1)}, f32[8,640]{1,0:T(8,128)S(1)}) custom-call(f32[1,4224]{1,0:T(1,128)S(1)} %collective-permute-done.5.refs_0_, f32[1,4224]{1,0:T(1,128)S(1)} %collective-permute-done.6.refs_1_, f32[1,4224]{1,0:T(1,128)S(1)} %collective-permute-done.7.refs_2_, f32[1,4224]{1,0:T(1,128)S(1)} %add_add_fusion.1.refs_3_, ...), custom_call_target="tpu_custom_call" | custom-call | tf_op jit(solution)/shard_map/pallas_call | solution.py:280
  28.8 1.5 %collective-permute-start.8 = (f32[8,640]{1,0:T(8,128)S(1)}, f32[8,640]{1,0:T(8,128)S(1)}, u32[]{:S(2)}, u32[]{:S(2)}) collective-permute-start(f32[8,640]{1,0:T(8,128)S(1)} %get-tuple-element.35.refs_1_), channel_id=1, source_target_pairs={{0,16},{16,0},{1,17},{17,1},{2,18},{18,2},{3,19},{19,3},{4,20},{20... | collective-permute-start | bytes 61448 | tf_op jit(solution)/shard_map/ppermute | solution.py:304
  30.3 2.3 %collective-permute-done.8.refs_0_ = f32[8,640]{1,0:T(8,128)S(1)} collective-permute-done((f32[8,640]{1,0:T(8,128)S(1)}, f32[8,640]{1,0:T(8,128)S(1)}, u32[]{:S(2)}, u32[]{:S(2)}) %collective-permute-start.8) | collective-permute-done | bytes 20512 | tf_op jit(solution)/shard_map/ppermute | solution.py:304
  32.6 1.2 %shard_map.74 = (f32[8,512]{1,0:T(8,128)S(1)}, f32[8,128]{1,0:T(8,128)S(1)}, f32[1,4224]{1,0:T(1,128)S(1)}) custom-call(f32[8,640]{1,0:T(8,128)S(1)} %collective-permute-done.8.refs_0_, f32[8,640]{1,0:T(8,128)S(1)} %get-tuple-element.35.refs_1_, f32[1,512]{1,0:T(1,128)S(1)} %get-tuple-element.30.refs_2_, ...), custom_call_target="tpu_custom_call" | custom-call | tf_op jit(solution)/shard_map/pallas_call | solution.py:280
  33.8 0.3 collective-permute-start.10
  34.2 1.7 %collective-permute-start.11 = (f32[1,4224]{1,0:T(1,128)S(1)}, f32[1,4224]{1,0:T(1,128)S(1)}, u32[]{:S(2)}, u32[]{:S(2)}) collective-permute-start(f32[1,4224]{1,0:T(1,128)S(1)} %get-tuple-element.38), channel_id=1, source_target_pairs={{0,8},{1,9},{2,10},{3,11},{4,12},{5,13},{6,14},{7,15},{8,0},{9,1},... | collective-permute-start | bytes 50696 | tf_op jit(solution)/shard_map/ppermute | solution.py:304
  35.8 0.8 %collective-permute-start.9 = (f32[1,4224]{1,0:T(1,128)S(1)}, f32[1,4224]{1,0:T(1,128)S(1)}, u32[]{:S(2)}, u32[]{:S(2)}) collective-permute-start(f32[1,4224]{1,0:T(1,128)S(1)} %get-tuple-element.38), channel_id=1, source_target_pairs={{0,1},{1,0},{2,3},{3,2},{4,5},{5,4},{6,7},{7,6},{8,9},{9,8},{10,11... | collective-permute-start | bytes 50696 | tf_op jit(solution)/shard_map/ppermute | solution.py:304
  36.6 1.3 %collective-permute-done.10 = f32[1,4224]{1,0:T(1,128)S(1)} collective-permute-done((f32[1,4224]{1,0:T(1,128)S(1)}, f32[1,4224]{1,0:T(1,128)S(1)}, u32[]{:S(2)}, u32[]{:S(2)}) %collective-permute-start.10) | collective-permute-done | bytes 16928 | tf_op jit(solution)/shard_map/ppermute | solution.py:304
  38.0 0.8 %collective-permute-done.11 = f32[1,4224]{1,0:T(1,128)S(1)} collective-permute-done((f32[1,4224]{1,0:T(1,128)S(1)}, f32[1,4224]{1,0:T(1,128)S(1)}, u32[]{:S(2)}, u32[]{:S(2)}) %collective-permute-start.11) | collective-permute-done | bytes 16928 | tf_op jit(solution)/shard_map/ppermute | solution.py:304
  38.8 0.0 collective-permute-done.9
  38.8 1.7 %collective-permute-start.12 = (f32[1,4224]{1,0:T(1,128)S(1)}, f32[1,4224]{1,0:T(1,128)S(1)}, u32[]{:S(2)}, u32[]{:S(2)}) collective-permute-start(f32[1,4224]{1,0:T(1,128)S(1)} %add_add_fusion.refs_3_), channel_id=1, source_target_pairs={{0,7},{1,6},{2,5},{3,4},{4,3},{5,2},{6,1},{7,0},{8,15},{9,14},{10,... | collective-permute-start | bytes 50696 | tf_op jit(solution)/shard_map/ppermute | solution.py:304
  40.6 0.1 collective-permute-start.13
  40.7 1.4 %collective-permute-start.14 = (f32[1,4224]{1,0:T(1,128)S(1)}, f32[1,4224]{1,0:T(1,128)S(1)}, u32[]{:S(2)}, u32[]{:S(2)}) collective-permute-start(f32[1,4224]{1,0:T(1,128)S(1)} %add_add_fusion.refs_3_), channel_id=1, source_target_pairs={{0,3},{1,2},{2,1},{3,0},{4,7},{5,6},{6,5},{7,4},{8,11},{9,10},{10,... | collective-permute-start | bytes 50696 | tf_op jit(solution)/shard_map/ppermute | solution.py:304
  42.1 0.9 %collective-permute-done.12.refs_0_ = f32[1,4224]{1,0:T(1,128)S(1)} collective-permute-done((f32[1,4224]{1,0:T(1,128)S(1)}, f32[1,4224]{1,0:T(1,128)S(1)}, u32[]{:S(2)}, u32[]{:S(2)}) %collective-permute-start.12) | collective-permute-done | bytes 16928 | tf_op jit(solution)/shard_map/ppermute | solution.py:304
  43.0 0.7 %collective-permute-done.13.refs_1_ = f32[1,4224]{1,0:T(1,128)S(1)} collective-permute-done((f32[1,4224]{1,0:T(1,128)S(1)}, f32[1,4224]{1,0:T(1,128)S(1)}, u32[]{:S(2)}, u32[]{:S(2)}) %collective-permute-start.13) | collective-permute-done | bytes 16928 | tf_op jit(solution)/shard_map/ppermute | solution.py:304
  43.7 0.1 collective-permute-done.14.refs_2_
  43.9 1.3 %shard_map.75 = (f32[8,256]{1,0:T(8,128)S(1)}, f32[8,640]{1,0:T(8,128)S(1)}) custom-call(f32[1,4224]{1,0:T(1,128)S(1)} %collective-permute-done.12.refs_0_, f32[1,4224]{1,0:T(1,128)S(1)} %collective-permute-done.13.refs_1_, f32[1,4224]{1,0:T(1,128)S(1)} %collective-permute-done.14.refs_2_, f32[1,4224]{1,0:T(1,128)S(1)} %add_add_fusion.refs_3_, ...), custom_call_target="tpu_custom_call" | custom-call | tf_op jit(solution)/shard_map/pallas_call | solution.py:280
  45.1 1.5 %collective-permute-start.15 = (f32[8,640]{1,0:T(8,128)S(1)}, f32[8,640]{1,0:T(8,128)S(1)}, u32[]{:S(2)}, u32[]{:S(2)}) collective-permute-start(f32[8,640]{1,0:T(8,128)S(1)} %get-tuple-element.40.refs_1_), channel_id=1, source_target_pairs={{0,16},{16,0},{1,17},{17,1},{2,18},{18,2},{3,19},{19,3},{4,20},{20... | collective-permute-start | bytes 61448 | tf_op jit(solution)/shard_map/ppermute | solution.py:304
  46.7 2.3 %collective-permute-done.15.refs_0_ = f32[8,640]{1,0:T(8,128)S(1)} collective-permute-done((f32[8,640]{1,0:T(8,128)S(1)}, f32[8,640]{1,0:T(8,128)S(1)}, u32[]{:S(2)}, u32[]{:S(2)}) %collective-permute-start.15) | collective-permute-done | bytes 20512 | tf_op jit(solution)/shard_map/ppermute | solution.py:304
  48.9 0.6 %shard_map.76 = (f32[8,512]{1,0:T(8,128)}, f32[8,512]{1,0:T(8,128)}) custom-call(f32[8,640]{1,0:T(8,128)S(1)} %collective-permute-done.15.refs_0_, f32[8,640]{1,0:T(8,128)S(1)} %get-tuple-element.40.refs_1_, f32[1,512]{1,0:T(1,128)S(1)} %get-tuple-element.30.refs_2_, f32[8,512]{1,0:T(8,128)S(1)} %get-tuple-element.36.refs_5_.refs_3_, ...), custom_call_target="tpu_custom_call" | custom-call | tf_op jit(solution)/shard_map/pallas_call | solution.py:280
  (2 shorter events, 0.1 us)
Async XLA Ops:
  2.6 5.3 %collective-permute-start = (bf16[64,512]{1,0:T(8,128)(2,1)S(1)}, bf16[64,512]{1,0:T(8,128)(2,1)S(1)}, u32[]{:S(2)}, u32[]{:S(2)}) collective-permute-start(bf16[64,512]{1,0:T(8,128)(2,1)S(1)} %get-tuple-element.28.refs_1_), channel_id=1, source_target_pairs={{0,16},{16,0},{1,17},{17,1},{2,18},{18,2},{3,19},{19,3},{4,20},{20... | collective-permute-start | bytes 196616 | tf_op jit(solution)/shard_map/ppermute | solution.py:304
  10.4 4.0 %collective-permute-start.1 = (f32[8,512]{1,0:T(8,128)S(1)}, f32[8,512]{1,0:T(8,128)S(1)}, u32[]{:S(2)}, u32[]{:S(2)}) collective-permute-start(f32[8,512]{1,0:T(8,128)S(1)} %get-tuple-element.29.refs_1_), channel_id=1, source_target_pairs={{0,16},{16,0},{1,17},{17,1},{2,18},{18,2},{3,19},{19,3},{4,20},{20... | collective-permute-start | bytes 49160 | tf_op jit(solution)/shard_map/ppermute | solution.py:304
  15.6 4.1 %collective-permute-start.2 = (f32[1,4224]{1,0:T(1,128)S(1)}, f32[1,4224]{1,0:T(1,128)S(1)}, u32[]{:S(2)}, u32[]{:S(2)}) collective-permute-start(f32[1,4224]{1,0:T(1,128)S(1)} %get-tuple-element.33), channel_id=1, source_target_pairs={{0,9},{1,8},{2,11},{3,10},{4,13},{5,12},{6,15},{7,14},{8,1},{9,0},... | collective-permute-start | bytes 50696 | tf_op jit(solution)/shard_map/ppermute | solution.py:304
  16.3 4.7 %collective-permute-start.3 = (f32[1,4224]{1,0:T(1,128)S(1)}, f32[1,4224]{1,0:T(1,128)S(1)}, u32[]{:S(2)}, u32[]{:S(2)}) collective-permute-start(f32[1,4224]{1,0:T(1,128)S(1)} %get-tuple-element.33), channel_id=1, source_target_pairs={{0,8},{1,9},{2,10},{3,11},{4,12},{5,13},{6,14},{7,15},{8,0},{9,1},... | collective-permute-start | bytes 50696 | tf_op jit(solution)/shard_map/ppermute | solution.py:304
  18.7 2.3 %collective-permute-start.4 = (f32[1,4224]{1,0:T(1,128)S(1)}, f32[1,4224]{1,0:T(1,128)S(1)}, u32[]{:S(2)}, u32[]{:S(2)}) collective-permute-start(f32[1,4224]{1,0:T(1,128)S(1)} %get-tuple-element.33), channel_id=1, source_target_pairs={{0,1},{1,0},{2,3},{3,2},{4,5},{5,4},{6,7},{7,6},{8,9},{9,8},{10,11... | collective-permute-start | bytes 50696 | tf_op jit(solution)/shard_map/ppermute | solution.py:304
  21.0 4.9 %collective-permute-start.5 = (f32[1,4224]{1,0:T(1,128)S(1)}, f32[1,4224]{1,0:T(1,128)S(1)}, u32[]{:S(2)}, u32[]{:S(2)}) collective-permute-start(f32[1,4224]{1,0:T(1,128)S(1)} %add_add_fusion.1.refs_3_), channel_id=1, source_target_pairs={{0,7},{1,6},{2,5},{3,4},{4,3},{5,2},{6,1},{7,0},{8,15},{9,14},{10,... | collective-permute-start | bytes 50696 | tf_op jit(solution)/shard_map/ppermute | solution.py:304
  24.4 3.2 %collective-permute-start.6 = (f32[1,4224]{1,0:T(1,128)S(1)}, f32[1,4224]{1,0:T(1,128)S(1)}, u32[]{:S(2)}, u32[]{:S(2)}) collective-permute-start(f32[1,4224]{1,0:T(1,128)S(1)} %add_add_fusion.1.refs_3_), channel_id=1, source_target_pairs={{0,5},{1,4},{2,7},{3,6},{4,1},{5,0},{6,3},{7,2},{8,13},{9,12},{10,... | collective-permute-start | bytes 50696 | tf_op jit(solution)/shard_map/ppermute | solution.py:304
  24.4 3.2 %collective-permute-start.7 = (f32[1,4224]{1,0:T(1,128)S(1)}, f32[1,4224]{1,0:T(1,128)S(1)}, u32[]{:S(2)}, u32[]{:S(2)}) collective-permute-start(f32[1,4224]{1,0:T(1,128)S(1)} %add_add_fusion.1.refs_3_), channel_id=1, source_target_pairs={{0,3},{1,2},{2,1},{3,0},{4,7},{5,6},{6,5},{7,4},{8,11},{9,10},{10,... | collective-permute-start | bytes 50696 | tf_op jit(solution)/shard_map/ppermute | solution.py:304
  28.8 3.8 %collective-permute-start.8 = (f32[8,640]{1,0:T(8,128)S(1)}, f32[8,640]{1,0:T(8,128)S(1)}, u32[]{:S(2)}, u32[]{:S(2)}) collective-permute-start(f32[8,640]{1,0:T(8,128)S(1)} %get-tuple-element.35.refs_1_), channel_id=1, source_target_pairs={{0,16},{16,0},{1,17},{17,1},{2,18},{18,2},{3,19},{19,3},{4,20},{20... | collective-permute-start | bytes 61448 | tf_op jit(solution)/shard_map/ppermute | solution.py:304
  33.8 4.1 %collective-permute-start.10 = (f32[1,4224]{1,0:T(1,128)S(1)}, f32[1,4224]{1,0:T(1,128)S(1)}, u32[]{:S(2)}, u32[]{:S(2)}) collective-permute-start(f32[1,4224]{1,0:T(1,128)S(1)} %get-tuple-element.38), channel_id=1, source_target_pairs={{0,9},{1,8},{2,11},{3,10},{4,13},{5,12},{6,15},{7,14},{8,1},{9,0},... | collective-permute-start | bytes 50696 | tf_op jit(solution)/shard_map/ppermute | solution.py:304
  34.2 4.6 %collective-permute-start.11 = (f32[1,4224]{1,0:T(1,128)S(1)}, f32[1,4224]{1,0:T(1,128)S(1)}, u32[]{:S(2)}, u32[]{:S(2)}) collective-permute-start(f32[1,4224]{1,0:T(1,128)S(1)} %get-tuple-element.38), channel_id=1, source_target_pairs={{0,8},{1,9},{2,10},{3,11},{4,12},{5,13},{6,14},{7,15},{8,0},{9,1},... | collective-permute-start | bytes 50696 | tf_op jit(solution)/shard_map/ppermute | solution.py:304
  35.8 3.0 %collective-permute-start.9 = (f32[1,4224]{1,0:T(1,128)S(1)}, f32[1,4224]{1,0:T(1,128)S(1)}, u32[]{:S(2)}, u32[]{:S(2)}) collective-permute-start(f32[1,4224]{1,0:T(1,128)S(1)} %get-tuple-element.38), channel_id=1, source_target_pairs={{0,1},{1,0},{2,3},{3,2},{4,5},{5,4},{6,7},{7,6},{8,9},{9,8},{10,11... | collective-permute-start | bytes 50696 | tf_op jit(solution)/shard_map/ppermute | solution.py:304
  38.8 4.2 %collective-permute-start.12 = (f32[1,4224]{1,0:T(1,128)S(1)}, f32[1,4224]{1,0:T(1,128)S(1)}, u32[]{:S(2)}, u32[]{:S(2)}) collective-permute-start(f32[1,4224]{1,0:T(1,128)S(1)} %add_add_fusion.refs_3_), channel_id=1, source_target_pairs={{0,7},{1,6},{2,5},{3,4},{4,3},{5,2},{6,1},{7,0},{8,15},{9,14},{10,... | collective-permute-start | bytes 50696 | tf_op jit(solution)/shard_map/ppermute | solution.py:304
  40.6 3.2 %collective-permute-start.13 = (f32[1,4224]{1,0:T(1,128)S(1)}, f32[1,4224]{1,0:T(1,128)S(1)}, u32[]{:S(2)}, u32[]{:S(2)}) collective-permute-start(f32[1,4224]{1,0:T(1,128)S(1)} %add_add_fusion.refs_3_), channel_id=1, source_target_pairs={{0,5},{1,4},{2,7},{3,6},{4,1},{5,0},{6,3},{7,2},{8,13},{9,12},{10,... | collective-permute-start | bytes 50696 | tf_op jit(solution)/shard_map/ppermute | solution.py:304
  40.7 3.2 %collective-permute-start.14 = (f32[1,4224]{1,0:T(1,128)S(1)}, f32[1,4224]{1,0:T(1,128)S(1)}, u32[]{:S(2)}, u32[]{:S(2)}) collective-permute-start(f32[1,4224]{1,0:T(1,128)S(1)} %add_add_fusion.refs_3_), channel_id=1, source_target_pairs={{0,3},{1,2},{2,1},{3,0},{4,7},{5,6},{6,5},{7,4},{8,11},{9,10},{10,... | collective-permute-start | bytes 50696 | tf_op jit(solution)/shard_map/ppermute | solution.py:304
  45.1 3.8 %collective-permute-start.15 = (f32[8,640]{1,0:T(8,128)S(1)}, f32[8,640]{1,0:T(8,128)S(1)}, u32[]{:S(2)}, u32[]{:S(2)}) collective-permute-start(f32[8,640]{1,0:T(8,128)S(1)} %get-tuple-element.40.refs_1_), channel_id=1, source_target_pairs={{0,16},{16,0},{1,17},{17,1},{2,18},{18,2},{3,19},{19,3},{4,20},{20... | collective-permute-start | bytes 61448 | tf_op jit(solution)/shard_map/ppermute | solution.py:304

commit v10 on v9

--- a/solution.py
+++ b/solution.py
@@ -290,20 +290,19 @@
     )(*args)
 
 
-def exchange(value, axis, near_first=False):
+def exchange(value, axis):
     size = lax.axis_size(axis)
-    bits = size.bit_length() - 1
     parts = [value]
-    for low in range((bits + 1) // 2):
+    stride = 1
+    while stride < size:
         value = pair_total(parts)
-        near, far = 1 << low, 1 << (bits - 1 - low)
-        side = 0 if low == 0 else 1
+        span = 2 if stride < 4 else min(4, size // stride)
+        side = 0 if stride == 1 else 1
         parts = [value]
-        for step in (near, far, near | far) if near != far else (near,):
-            pairs = [(i, i ^ step ^ side) for i in range(size)]
+        for offset in range(1, span):
+            pairs = [(i, i ^ (offset * stride) ^ side) for i in range(size)]
             parts.insert(0, lax.ppermute(value, axis, pairs))
-        if near_first and low == 0:
-            parts = parts[-2:] + parts[:-2]
+        stride *= span
     return parts
 
 
@@ -385,7 +384,7 @@
         (vector, narrow, row_shape),
         *folds, scale, slots, turned, target, norm,
     )
-    latest = exchange(latest, "centers", True)
+    latest = exchange(latest, "centers")
     sums, folded = call(
         partial(second_fold_body, len(latest)),
         (shaped((SLOTS, 2 * EXTRA)), fold_shape),

time: 49.7 us -> 50.3 us (1.012)
  waiting for transfers between devices: 14.7 us -> 17.2 us
  starting transfers between devices: 21.5 us -> 19.6 us
    ppermute x16 -> x14, waiting for transfers between devices: 14.7 us -> 17.2 us  [exchange(): parts.insert(0, lax.ppermute(value, axis, pairs))]
    ppermute x16 -> x14, starting transfers between devices: 21.5 us -> 19.6 us  [exchange(): parts.insert(0, lax.ppermute(value, axis, pairs))]
  transfers between devices with their start and end apart: 16 -> 14, of which waited for: 12 -> 12; matrix products, arithmetic and copies ran while one was open for 0% -> 0% of each run, Pallas kernels for 5% -> 5%
where the time goes in v10:
time: 50.3 us; the launch traced here: 50.1 us
  starting transfers between devices  19.6 us (39%)
  waiting for transfers between devices  17.2 us (34%)
  Pallas kernels  12.6 us (25%)
  between operations  0.72 us (1%)
    ppermute x14, starting transfers between devices, exchange(): parts.insert(0, lax.ppermute(value, axis, pairs))  19.6 us
    ppermute x14, waiting for transfers between devices, exchange(): parts.insert(0, lax.ppermute(value, axis, pairs))  17.2 us
    pallas_call x9, Pallas kernels, call(): pl.pallas_call(body, out_shape=out_shape, in_specs=[source] * len(args),...  12.6 us
  transfers between devices with their start and end apart: 14, of which 12 were waited for; matrix products, arithmetic and copies ran while one was open for 0% of the time, Pallas kernels for 5%

profile of v10, /device:TPU:0, one launch (start us, length us, event | category | flops | bytes accessed | tf_op | source)
XLA Modules:
  0.0 50.1 jit_solution(5674241785324716062)
XLA Ops:
  0.6 1.9 %shard_map.68 = (bf16[64,4096]{1,0:T(8,128)(2,1)S(1)}, s32[1,4096]{1,0:T(1,128)S(1)}, f32[1,4096]{1,0:T(1,128)S(1)}, f32[1,512]{1,0:T(1,128)S(1)}, bf16[64,512]{1,0:T(8,128)(2,1)S(1)}) custom-call(bf16[64,4096]{1,0:T(8,128)(2,1)} %feat_hbm.1, s32[1,512]{1,0:T(1,128)} %bitcast.6, s32[1,4096]{1,0:T(1,128)} %bitcast.4, f32[1,4096]{1,0:T(1,128)} %bitcast.5, ...), custom_call_target="tpu_custom_call" | custom-call | tf_op jit(solution)/shard_map/pallas_call | solution.py:280
  2.6 3.0 %collective-permute-start = (bf16[64,512]{1,0:T(8,128)(2,1)S(1)}, bf16[64,512]{1,0:T(8,128)(2,1)S(1)}, u32[]{:S(2)}, u32[]{:S(2)}) collective-permute-start(bf16[64,512]{1,0:T(8,128)(2,1)S(1)} %get-tuple-element.28.refs_1_), channel_id=1, source_target_pairs={{0,16},{16,0},{1,17},{17,1},{2,18},{18,2},{3,19},{19,3},{4,20},{20... | collective-permute-start | bytes 196616 | tf_op jit(solution)/shard_map/ppermute | solution.py:304
  5.6 0.7 %shard_map.69 = (bf16[256,4096]{1,0:T(8,128)(2,1)S(1)}, bf16[4096,256]{1,0:T(8,128)(2,1)S(1)}, bf16[16,4096]{1,0:T(8,128)(2,1)S(1)}) custom-call(bf16[64,4096]{1,0:T(8,128)(2,1)S(1)} %get-tuple-element.23.feat_ref, s32[1,4096]{1,0:T(1,128)S(1)} %get-tuple-element.24.slots_ref.refs_3_.refs_4_, f32[1,4096]{1,0:T(1,128)S(1)} %get-tuple-element.25.prices_ref), custom_call_target="tpu_custom_call" | custom-call | flops 4096000 | bytes 4194304 | tf_op jit(solution)/shard_map/pallas_call | solution.py:280
  6.3 1.6 %collective-permute-done.refs_0_ = bf16[64,512]{1,0:T(8,128)(2,1)S(1)} collective-permute-done((bf16[64,512]{1,0:T(8,128)(2,1)S(1)}, bf16[64,512]{1,0:T(8,128)(2,1)S(1)}, u32[]{:S(2)}, u32[]{:S(2)}) %collective-permute-start) | collective-permute-done | bytes 65568 | tf_op jit(solution)/shard_map/ppermute | solution.py:304
  7.8 2.5 %shard_map.70 = (bf16[8192,512]{1,0:T(8,128)(2,1)S(1)}, bf16[256,512]{1,0:T(8,128)(2,1)S(1)}, f32[8,512]{1,0:T(8,128)S(1)}) custom-call(bf16[4096,256]{1,0:T(8,128)(2,1)S(1)} %get-tuple-element.26.turned_ref, bf16[16,4096]{1,0:T(8,128)(2,1)S(1)} %get-tuple-element.27.weight_ref, bf16[64,512]{1,0:T(8,128)(2,1)S(1)} %collective-permute-done.refs_0_, ...), custom_call_target="tpu_custom_call" | custom-call | flops 134217728 | bytes 8388608 | tf_op jit(solution)/shard_map/pallas_call | solution.py:280
  10.4 2.1 %collective-permute-start.1 = (f32[8,512]{1,0:T(8,128)S(1)}, f32[8,512]{1,0:T(8,128)S(1)}, u32[]{:S(2)}, u32[]{:S(2)}) collective-permute-start(f32[8,512]{1,0:T(8,128)S(1)} %get-tuple-element.29.refs_1_), channel_id=1, source_target_pairs={{0,16},{16,0},{1,17},{17,1},{2,18},{18,2},{3,19},{19,3},{4,20},{20... | collective-permute-start | bytes 49160 | tf_op jit(solution)/shard_map/ppermute | solution.py:304
  12.5 1.9 %shard_map.71.refs_4_ = bf16[1024,4096]{1,0:T(8,128)(2,1)S(1)} custom-call(bf16[256,4096]{1,0:T(8,128)(2,1)S(1)} %get-tuple-element.31.columns_ref, bf16[256,512]{1,0:T(8,128)(2,1)S(1)} %get-tuple-element.32.center_ref), custom_call_target="tpu_custom_call" | custom-call | flops 134217728 | bytes 8388608 | tf_op jit(solution)/shard_map/pallas_call | solution.py:280
  14.4 0.0 collective-permute-done.1.refs_0_
  14.4 1.2 %shard_map.72 = (f32[8,512]{1,0:T(8,128)S(1)}, f32[1,4224]{1,0:T(1,128)S(1)}) custom-call(f32[8,512]{1,0:T(8,128)S(1)} %collective-permute-done.1.refs_0_, f32[8,512]{1,0:T(8,128)S(1)} %get-tuple-element.29.refs_1_, f32[1,512]{1,0:T(1,128)S(1)} %get-tuple-element.30.refs_2_, s32[1,4096]{1,0:T(1,128)S(1)} %get-tuple-element.24.slots_ref.refs_3_.refs_4_, ...), custom_call_target="tpu_custom_call" | custom-call | tf_op jit(solution)/shard_map/pallas_call | solution.py:280
  15.6 0.1 collective-permute-start.2
  15.7 1.2 %collective-permute-done.2 = f32[1,4224]{1,0:T(1,128)S(1)} collective-permute-done((f32[1,4224]{1,0:T(1,128)S(1)}, f32[1,4224]{1,0:T(1,128)S(1)}, u32[]{:S(2)}, u32[]{:S(2)}) %collective-permute-start.2) | collective-permute-done | bytes 16928 | tf_op jit(solution)/shard_map/ppermute | solution.py:304
  16.9 1.7 %collective-permute-start.3 = (f32[1,4224]{1,0:T(1,128)S(1)}, f32[1,4224]{1,0:T(1,128)S(1)}, u32[]{:S(2)}, u32[]{:S(2)}) collective-permute-start(f32[1,4224]{1,0:T(1,128)S(1)} %add.12), channel_id=1, source_target_pairs={{0,3},{1,2},{2,1},{3,0},{4,7},{5,6},{6,5},{7,4},{8,11},{9,10},{10,... | collective-permute-start | bytes 50696 | tf_op jit(solution)/shard_map/ppermute | solution.py:304
  18.6 1.6 %collective-permute-done.3 = f32[1,4224]{1,0:T(1,128)S(1)} collective-permute-done((f32[1,4224]{1,0:T(1,128)S(1)}, f32[1,4224]{1,0:T(1,128)S(1)}, u32[]{:S(2)}, u32[]{:S(2)}) %collective-permute-start.3) | collective-permute-done | bytes 16928 | tf_op jit(solution)/shard_map/ppermute | solution.py:304
  20.2 3.7 %collective-permute-start.4 = (f32[1,4224]{1,0:T(1,128)S(1)}, f32[1,4224]{1,0:T(1,128)S(1)}, u32[]{:S(2)}, u32[]{:S(2)}) collective-permute-start(f32[1,4224]{1,0:T(1,128)S(1)} %add.13.refs_3_), channel_id=1, source_target_pairs={{0,13},{1,12},{2,15},{3,14},{4,9},{5,8},{6,11},{7,10},{8,5},{9,4},... | collective-permute-start | bytes 50696 | tf_op jit(solution)/shard_map/ppermute | solution.py:304
  23.9 0.0 collective-permute-start.5
  23.9 0.6 %collective-permute-start.6 = (f32[1,4224]{1,0:T(1,128)S(1)}, f32[1,4224]{1,0:T(1,128)S(1)}, u32[]{:S(2)}, u32[]{:S(2)}) collective-permute-start(f32[1,4224]{1,0:T(1,128)S(1)} %add.13.refs_3_), channel_id=1, source_target_pairs={{0,5},{1,4},{2,7},{3,6},{4,1},{5,0},{6,3},{7,2},{8,13},{9,12},{10,... | collective-permute-start | bytes 50696 | tf_op jit(solution)/shard_map/ppermute | solution.py:304
  24.5 0.9 %collective-permute-done.4.refs_0_ = f32[1,4224]{1,0:T(1,128)S(1)} collective-permute-done((f32[1,4224]{1,0:T(1,128)S(1)}, f32[1,4224]{1,0:T(1,128)S(1)}, u32[]{:S(2)}, u32[]{:S(2)}) %collective-permute-start.4) | collective-permute-done | bytes 16928 | tf_op jit(solution)/shard_map/ppermute | solution.py:304
  25.4 2.6 %collective-permute-done.5.refs_1_ = f32[1,4224]{1,0:T(1,128)S(1)} collective-permute-done((f32[1,4224]{1,0:T(1,128)S(1)}, f32[1,4224]{1,0:T(1,128)S(1)}, u32[]{:S(2)}, u32[]{:S(2)}) %collective-permute-start.5) | collective-permute-done | bytes 16928 | tf_op jit(solution)/shard_map/ppermute | solution.py:304
  28.0 0.0 collective-permute-done.6.refs_2_
  28.0 1.2 %shard_map.73 = (f32[1,4224]{1,0:T(1,128)S(1)}, f32[8,128]{1,0:T(8,128)S(1)}, f32[8,640]{1,0:T(8,128)S(1)}) custom-call(f32[1,4224]{1,0:T(1,128)S(1)} %collective-permute-done.4.refs_0_, f32[1,4224]{1,0:T(1,128)S(1)} %collective-permute-done.5.refs_1_, f32[1,4224]{1,0:T(1,128)S(1)} %collective-permute-done.6.refs_2_, f32[1,4224]{1,0:T(1,128)S(1)} %add.13.refs_3_, ...), custom_call_target="tpu_custom_call" | custom-call | tf_op jit(solution)/shard_map/pallas_call | solution.py:280
  29.2 1.5 %collective-permute-start.7 = (f32[8,640]{1,0:T(8,128)S(1)}, f32[8,640]{1,0:T(8,128)S(1)}, u32[]{:S(2)}, u32[]{:S(2)}) collective-permute-start(f32[8,640]{1,0:T(8,128)S(1)} %get-tuple-element.35.refs_1_), channel_id=1, source_target_pairs={{0,16},{16,0},{1,17},{17,1},{2,18},{18,2},{3,19},{19,3},{4,20},{20... | collective-permute-start | bytes 61448 | tf_op jit(solution)/shard_map/ppermute | solution.py:304
  30.7 2.3 %collective-permute-done.7.refs_0_ = f32[8,640]{1,0:T(8,128)S(1)} collective-permute-done((f32[8,640]{1,0:T(8,128)S(1)}, f32[8,640]{1,0:T(8,128)S(1)}, u32[]{:S(2)}, u32[]{:S(2)}) %collective-permute-start.7) | collective-permute-done | bytes 20512 | tf_op jit(solution)/shard_map/ppermute | solution.py:304
  33.0 1.2 %shard_map.74 = (f32[8,512]{1,0:T(8,128)S(1)}, f32[8,128]{1,0:T(8,128)S(1)}, f32[1,4224]{1,0:T(1,128)S(1)}) custom-call(f32[8,640]{1,0:T(8,128)S(1)} %collective-permute-done.7.refs_0_, f32[8,640]{1,0:T(8,128)S(1)} %get-tuple-element.35.refs_1_, f32[1,512]{1,0:T(1,128)S(1)} %get-tuple-element.30.refs_2_, ...), custom_call_target="tpu_custom_call" | custom-call | tf_op jit(solution)/shard_map/pallas_call | solution.py:280
  34.2 0.1 collective-permute-start.8
  34.3 1.2 %collective-permute-done.8 = f32[1,4224]{1,0:T(1,128)S(1)} collective-permute-done((f32[1,4224]{1,0:T(1,128)S(1)}, f32[1,4224]{1,0:T(1,128)S(1)}, u32[]{:S(2)}, u32[]{:S(2)}) %collective-permute-start.8) | collective-permute-done | bytes 16928 | tf_op jit(solution)/shard_map/ppermute | solution.py:304
  35.5 1.4 %collective-permute-start.9 = (f32[1,4224]{1,0:T(1,128)S(1)}, f32[1,4224]{1,0:T(1,128)S(1)}, u32[]{:S(2)}, u32[]{:S(2)}) collective-permute-start(f32[1,4224]{1,0:T(1,128)S(1)} %add.14), channel_id=1, source_target_pairs={{0,3},{1,2},{2,1},{3,0},{4,7},{5,6},{6,5},{7,4},{8,11},{9,10},{10,... | collective-permute-start | bytes 50696 | tf_op jit(solution)/shard_map/ppermute | solution.py:304
  36.8 1.9 %collective-permute-done.9 = f32[1,4224]{1,0:T(1,128)S(1)} collective-permute-done((f32[1,4224]{1,0:T(1,128)S(1)}, f32[1,4224]{1,0:T(1,128)S(1)}, u32[]{:S(2)}, u32[]{:S(2)}) %collective-permute-start.9) | collective-permute-done | bytes 16928 | tf_op jit(solution)/shard_map/ppermute | solution.py:304
  38.7 1.5 %collective-permute-start.10 = (f32[1,4224]{1,0:T(1,128)S(1)}, f32[1,4224]{1,0:T(1,128)S(1)}, u32[]{:S(2)}, u32[]{:S(2)}) collective-permute-start(f32[1,4224]{1,0:T(1,128)S(1)} %add.15.refs_3_), channel_id=1, source_target_pairs={{0,13},{1,12},{2,15},{3,14},{4,9},{5,8},{6,11},{7,10},{8,5},{9,4},... | collective-permute-start | bytes 50696 | tf_op jit(solution)/shard_map/ppermute | solution.py:304
  40.2 0.4 collective-permute-start.11
  40.6 2.1 %collective-permute-start.12 = (f32[1,4224]{1,0:T(1,128)S(1)}, f32[1,4224]{1,0:T(1,128)S(1)}, u32[]{:S(2)}, u32[]{:S(2)}) collective-permute-start(f32[1,4224]{1,0:T(1,128)S(1)} %add.15.refs_3_), channel_id=1, source_target_pairs={{0,5},{1,4},{2,7},{3,6},{4,1},{5,0},{6,3},{7,2},{8,13},{9,12},{10,... | collective-permute-start | bytes 50696 | tf_op jit(solution)/shard_map/ppermute | solution.py:304
  42.7 1.1 %collective-permute-done.10.refs_0_ = f32[1,4224]{1,0:T(1,128)S(1)} collective-permute-done((f32[1,4224]{1,0:T(1,128)S(1)}, f32[1,4224]{1,0:T(1,128)S(1)}, u32[]{:S(2)}, u32[]{:S(2)}) %collective-permute-start.10) | collective-permute-done | bytes 16928 | tf_op jit(solution)/shard_map/ppermute | solution.py:304
  43.7 0.6 %collective-permute-done.11.refs_1_ = f32[1,4224]{1,0:T(1,128)S(1)} collective-permute-done((f32[1,4224]{1,0:T(1,128)S(1)}, f32[1,4224]{1,0:T(1,128)S(1)}, u32[]{:S(2)}, u32[]{:S(2)}) %collective-permute-start.11) | collective-permute-done | bytes 16928 | tf_op jit(solution)/shard_map/ppermute | solution.py:304
  44.4 0.1 collective-permute-done.12.refs_2_
  44.5 1.3 %shard_map.75 = (f32[8,256]{1,0:T(8,128)S(1)}, f32[8,640]{1,0:T(8,128)S(1)}) custom-call(f32[1,4224]{1,0:T(1,128)S(1)} %collective-permute-done.10.refs_0_, f32[1,4224]{1,0:T(1,128)S(1)} %collective-permute-done.11.refs_1_, f32[1,4224]{1,0:T(1,128)S(1)} %collective-permute-done.12.refs_2_, f32[1,4224]{1,0:T(1,128)S(1)} %add.15.refs_3_, ...), custom_call_target="tpu_custom_call" | custom-call | tf_op jit(solution)/shard_map/pallas_call | solution.py:280
  45.7 1.5 %collective-permute-start.13 = (f32[8,640]{1,0:T(8,128)S(1)}, f32[8,640]{1,0:T(8,128)S(1)}, u32[]{:S(2)}, u32[]{:S(2)}) collective-permute-start(f32[8,640]{1,0:T(8,128)S(1)} %get-tuple-element.40.refs_1_), channel_id=1, source_target_pairs={{0,16},{16,0},{1,17},{17,1},{2,18},{18,2},{3,19},{19,3},{4,20},{20... | collective-permute-start | bytes 61448 | tf_op jit(solution)/shard_map/ppermute | solution.py:304
  47.2 2.3 %collective-permute-done.13.refs_0_ = f32[8,640]{1,0:T(8,128)S(1)} collective-permute-done((f32[8,640]{1,0:T(8,128)S(1)}, f32[8,640]{1,0:T(8,128)S(1)}, u32[]{:S(2)}, u32[]{:S(2)}) %collective-permute-start.13) | collective-permute-done | bytes 20512 | tf_op jit(solution)/shard_map/ppermute | solution.py:304
  49.5 0.6 %shard_map.76 = (f32[8,512]{1,0:T(8,128)}, f32[8,512]{1,0:T(8,128)}) custom-call(f32[8,640]{1,0:T(8,128)S(1)} %collective-permute-done.13.refs_0_, f32[8,640]{1,0:T(8,128)S(1)} %get-tuple-element.40.refs_1_, f32[1,512]{1,0:T(1,128)S(1)} %get-tuple-element.30.refs_2_, f32[8,512]{1,0:T(8,128)S(1)} %get-tuple-element.36.refs_5_.refs_3_, ...), custom_call_target="tpu_custom_call" | custom-call | tf_op jit(solution)/shard_map/pallas_call | solution.py:280
  (4 shorter events, 0.1 us)
Async XLA Ops:
  2.6 5.3 %collective-permute-start = (bf16[64,512]{1,0:T(8,128)(2,1)S(1)}, bf16[64,512]{1,0:T(8,128)(2,1)S(1)}, u32[]{:S(2)}, u32[]{:S(2)}) collective-permute-start(bf16[64,512]{1,0:T(8,128)(2,1)S(1)} %get-tuple-element.28.refs_1_), channel_id=1, source_target_pairs={{0,16},{16,0},{1,17},{17,1},{2,18},{18,2},{3,19},{19,3},{4,20},{20... | collective-permute-start | bytes 196616 | tf_op jit(solution)/shard_map/ppermute | solution.py:304
  10.4 4.0 %collective-permute-start.1 = (f32[8,512]{1,0:T(8,128)S(1)}, f32[8,512]{1,0:T(8,128)S(1)}, u32[]{:S(2)}, u32[]{:S(2)}) collective-permute-start(f32[8,512]{1,0:T(8,128)S(1)} %get-tuple-element.29.refs_1_), channel_id=1, source_target_pairs={{0,16},{16,0},{1,17},{17,1},{2,18},{18,2},{3,19},{19,3},{4,20},{20... | collective-permute-start | bytes 49160 | tf_op jit(solution)/shard_map/ppermute | solution.py:304
  15.6 1.2 %collective-permute-start.2 = (f32[1,4224]{1,0:T(1,128)S(1)}, f32[1,4224]{1,0:T(1,128)S(1)}, u32[]{:S(2)}, u32[]{:S(2)}) collective-permute-start(f32[1,4224]{1,0:T(1,128)S(1)} %get-tuple-element.33), channel_id=1, source_target_pairs={{0,1},{1,0},{2,3},{3,2},{4,5},{5,4},{6,7},{7,6},{8,9},{9,8},{10,11... | collective-permute-start | bytes 50696 | tf_op jit(solution)/shard_map/ppermute | solution.py:304
  16.9 3.2 %collective-permute-start.3 = (f32[1,4224]{1,0:T(1,128)S(1)}, f32[1,4224]{1,0:T(1,128)S(1)}, u32[]{:S(2)}, u32[]{:S(2)}) collective-permute-start(f32[1,4224]{1,0:T(1,128)S(1)} %add.12), channel_id=1, source_target_pairs={{0,3},{1,2},{2,1},{3,0},{4,7},{5,6},{6,5},{7,4},{8,11},{9,10},{10,... | collective-permute-start | bytes 50696 | tf_op jit(solution)/shard_map/ppermute | solution.py:304
  20.2 5.2 %collective-permute-start.4 = (f32[1,4224]{1,0:T(1,128)S(1)}, f32[1,4224]{1,0:T(1,128)S(1)}, u32[]{:S(2)}, u32[]{:S(2)}) collective-permute-start(f32[1,4224]{1,0:T(1,128)S(1)} %add.13.refs_3_), channel_id=1, source_target_pairs={{0,13},{1,12},{2,15},{3,14},{4,9},{5,8},{6,11},{7,10},{8,5},{9,4},... | collective-permute-start | bytes 50696 | tf_op jit(solution)/shard_map/ppermute | solution.py:304
  23.9 4.1 %collective-permute-start.5 = (f32[1,4224]{1,0:T(1,128)S(1)}, f32[1,4224]{1,0:T(1,128)S(1)}, u32[]{:S(2)}, u32[]{:S(2)}) collective-permute-start(f32[1,4224]{1,0:T(1,128)S(1)} %add.13.refs_3_), channel_id=1, source_target_pairs={{0,9},{1,8},{2,11},{3,10},{4,13},{5,12},{6,15},{7,14},{8,1},{9,0},... | collective-permute-start | bytes 50696 | tf_op jit(solution)/shard_map/ppermute | solution.py:304
  23.9 4.1 %collective-permute-start.6 = (f32[1,4224]{1,0:T(1,128)S(1)}, f32[1,4224]{1,0:T(1,128)S(1)}, u32[]{:S(2)}, u32[]{:S(2)}) collective-permute-start(f32[1,4224]{1,0:T(1,128)S(1)} %add.13.refs_3_), channel_id=1, source_target_pairs={{0,5},{1,4},{2,7},{3,6},{4,1},{5,0},{6,3},{7,2},{8,13},{9,12},{10,... | collective-permute-start | bytes 50696 | tf_op jit(solution)/shard_map/ppermute | solution.py:304
  29.2 3.8 %collective-permute-start.7 = (f32[8,640]{1,0:T(8,128)S(1)}, f32[8,640]{1,0:T(8,128)S(1)}, u32[]{:S(2)}, u32[]{:S(2)}) collective-permute-start(f32[8,640]{1,0:T(8,128)S(1)} %get-tuple-element.35.refs_1_), channel_id=1, source_target_pairs={{0,16},{16,0},{1,17},{17,1},{2,18},{18,2},{3,19},{19,3},{4,20},{20... | collective-permute-start | bytes 61448 | tf_op jit(solution)/shard_map/ppermute | solution.py:304
  34.2 1.2 %collective-permute-start.8 = (f32[1,4224]{1,0:T(1,128)S(1)}, f32[1,4224]{1,0:T(1,128)S(1)}, u32[]{:S(2)}, u32[]{:S(2)}) collective-permute-start(f32[1,4224]{1,0:T(1,128)S(1)} %get-tuple-element.38), channel_id=1, source_target_pairs={{0,1},{1,0},{2,3},{3,2},{4,5},{5,4},{6,7},{7,6},{8,9},{9,8},{10,11... | collective-permute-start | bytes 50696 | tf_op jit(solution)/shard_map/ppermute | solution.py:304
  35.5 3.2 %collective-permute-start.9 = (f32[1,4224]{1,0:T(1,128)S(1)}, f32[1,4224]{1,0:T(1,128)S(1)}, u32[]{:S(2)}, u32[]{:S(2)}) collective-permute-start(f32[1,4224]{1,0:T(1,128)S(1)} %add.14), channel_id=1, source_target_pairs={{0,3},{1,2},{2,1},{3,0},{4,7},{5,6},{6,5},{7,4},{8,11},{9,10},{10,... | collective-permute-start | bytes 50696 | tf_op jit(solution)/shard_map/ppermute | solution.py:304
  38.7 5.0 %collective-permute-start.10 = (f32[1,4224]{1,0:T(1,128)S(1)}, f32[1,4224]{1,0:T(1,128)S(1)}, u32[]{:S(2)}, u32[]{:S(2)}) collective-permute-start(f32[1,4224]{1,0:T(1,128)S(1)} %add.15.refs_3_), channel_id=1, source_target_pairs={{0,13},{1,12},{2,15},{3,14},{4,9},{5,8},{6,11},{7,10},{8,5},{9,4},... | collective-permute-start | bytes 50696 | tf_op jit(solution)/shard_map/ppermute | solution.py:304
  40.2 4.2 %collective-permute-start.11 = (f32[1,4224]{1,0:T(1,128)S(1)}, f32[1,4224]{1,0:T(1,128)S(1)}, u32[]{:S(2)}, u32[]{:S(2)}) collective-permute-start(f32[1,4224]{1,0:T(1,128)S(1)} %add.15.refs_3_), channel_id=1, source_target_pairs={{0,9},{1,8},{2,11},{3,10},{4,13},{5,12},{6,15},{7,14},{8,1},{9,0},... | collective-permute-start | bytes 50696 | tf_op jit(solution)/shard_map/ppermute | solution.py:304
  40.6 3.9 %collective-permute-start.12 = (f32[1,4224]{1,0:T(1,128)S(1)}, f32[1,4224]{1,0:T(1,128)S(1)}, u32[]{:S(2)}, u32[]{:S(2)}) collective-permute-start(f32[1,4224]{1,0:T(1,128)S(1)} %add.15.refs_3_), channel_id=1, source_target_pairs={{0,5},{1,4},{2,7},{3,6},{4,1},{5,0},{6,3},{7,2},{8,13},{9,12},{10,... | collective-permute-start | bytes 50696 | tf_op jit(solution)/shard_map/ppermute | solution.py:304
  45.7 3.8 %collective-permute-start.13 = (f32[8,640]{1,0:T(8,128)S(1)}, f32[8,640]{1,0:T(8,128)S(1)}, u32[]{:S(2)}, u32[]{:S(2)}) collective-permute-start(f32[8,640]{1,0:T(8,128)S(1)} %get-tuple-element.40.refs_1_), channel_id=1, source_target_pairs={{0,16},{16,0},{1,17},{17,1},{2,18},{18,2},{3,19},{19,3},{4,20},{20... | collective-permute-start | bytes 61448 | tf_op jit(solution)/shard_map/ppermute | solution.py:304

commit v11 on v10

--- a/solution.py
+++ b/solution.py
@@ -98,14 +98,8 @@
     feat_ref, slots_ref, prices_ref, scale_ref, out_ref, idx_ref, hit_ref, sems = refs
     row_count = feat_ref.shape[1]
     count = out_ref.shape[1]
-    half = row_count // 2
-    left, right = pl.ds(0, half), pl.ds(half, half)
-    sources = (
-        idx_hbm, feat_hbm.at[:, left], feat_hbm.at[:, right], slots_hbm, prices_hbm, scale_hbm
-    )
-    targets = (
-        idx_ref, feat_ref.at[:, left], feat_ref.at[:, right], slots_ref, prices_ref, scale_ref
-    )
+    sources = (idx_hbm, feat_hbm, slots_hbm, prices_hbm, scale_hbm)
+    targets = (idx_ref, feat_ref, slots_ref, prices_ref, scale_ref)
     copies = [
         pltpu.make_async_copy(source, target, sems.at[place])
         for place, (source, target) in enumerate(zip(sources, targets))
@@ -122,17 +116,13 @@
         own = jnp.where(block == begin // STEP, place, -1.0).astype(bf16)
         return jnp.where(row == own, jnp.ones_like(row), jnp.zeros_like(row))
 
-    for begin in range(0, half, STEP):
+    for begin in range(0, row_count, STEP):
         hit_ref[begin : begin + STEP, :] = hits(begin)
     copies[1].wait()
-    total = jnp.dot(feat_ref[:, :half], hit_ref[...], preferred_element_type=f32)
-    copies[2].wait()
-    for begin in range(half, row_count, STEP):
-        total += jnp.dot(
-            feat_ref[:, begin : begin + STEP], hits(begin), preferred_element_type=f32
-        )
-    out_ref[...] = total.astype(bf16)
-    for copy in copies[3:]:
+    out_ref[...] = jnp.dot(
+        feat_ref[...], hit_ref[...], preferred_element_type=f32
+    ).astype(bf16)
+    for copy in copies[2:]:
         copy.wait()
 
 
@@ -290,18 +280,20 @@
     )(*args)
 
 
-def exchange(value, axis):
+def exchange(value, axis, near_first=False):
     size = lax.axis_size(axis)
     parts = [value]
     stride = 1
     while stride < size:
         value = pair_total(parts)
-        span = 2 if stride < 4 else min(4, size // stride)
+        span = min(4, size // stride)
         side = 0 if stride == 1 else 1
         parts = [value]
         for offset in range(1, span):
             pairs = [(i, i ^ (offset * stride) ^ side) for i in range(size)]
             parts.insert(0, lax.ppermute(value, axis, pairs))
+        if near_first and stride == 1:
+            parts = parts[-2:] + parts[:-2]
         stride *= span
     return parts
 
@@ -343,8 +335,8 @@
         source=HBM,
         scratch_shapes=[
             pltpu.VMEM((1, count), jnp.int32),
-            pltpu.VMEM((row_count // 2, count), bf16),
-            pltpu.SemaphoreType.DMA((6,)),
+            pltpu.VMEM((row_count, count), bf16),
+            pltpu.SemaphoreType.DMA((5,)),
         ],
     )
     centers = exchange(picked, "dp")
@@ -384,7 +376,7 @@
         (vector, narrow, row_shape),
         *folds, scale, slots, turned, target, norm,
     )
-    latest = exchange(latest, "centers")
+    latest = exchange(latest, "centers", True)
     sums, folded = call(
         partial(second_fold_body, len(latest)),
         (shaped((SLOTS, 2 * EXTRA)), fold_shape),

time: 50.3 us -> 49.2 us (0.978)
  waiting for transfers between devices: 17.2 us -> 16 us
    ppermute x14 -> x16, waiting for transfers between devices: 17.2 us -> 16 us  [exchange(): parts.insert(0, lax.ppermute(value, axis, pairs))]
    ppermute x14 -> x16, starting transfers between devices: 19.6 us -> 19.6 us  [exchange(): parts.insert(0, lax.ppermute(value, axis, pairs))]
  transfers between devices with their start and end apart: 14 -> 16, of which waited for: 12 -> 11; matrix products, arithmetic and copies ran while one was open for 0% -> 0% of each run, Pallas kernels for 5% -> 5%
where the time goes in v11:
time: 49.2 us; the launch traced here: 49 us
  starting transfers between devices  19.6 us (40%)
  waiting for transfers between devices  16 us (33%)
  Pallas kernels  12.5 us (25%)
  between operations  0.71 us (1%)
    ppermute x16, starting transfers between devices, exchange(): parts.insert(0, lax.ppermute(value, axis, pairs))  19.6 us
    ppermute x16, waiting for transfers between devices, exchange(): parts.insert(0, lax.ppermute(value, axis, pairs))  16 us
    pallas_call x9, Pallas kernels, call(): pl.pallas_call(body, out_shape=out_shape, in_specs=[source] * len(args),...  12.5 us
  transfers between devices with their start and end apart: 16, of which 11 were waited for; matrix products, arithmetic and copies ran while one was open for 0% of the time, Pallas kernels for 5%

profile of v11, /device:TPU:0, one launch (start us, length us, event | category | flops | bytes accessed | tf_op | source)
XLA Modules:
  0.0 49.0 jit_solution(8297220608381524704)
XLA Ops:
  0.6 1.9 %shard_map.68 = (bf16[64,4096]{1,0:T(8,128)(2,1)S(1)}, s32[1,4096]{1,0:T(1,128)S(1)}, f32[1,4096]{1,0:T(1,128)S(1)}, f32[1,512]{1,0:T(1,128)S(1)}, bf16[64,512]{1,0:T(8,128)(2,1)S(1)}) custom-call(bf16[64,4096]{1,0:T(8,128)(2,1)} %feat_hbm.1, s32[1,512]{1,0:T(1,128)} %bitcast.6, s32[1,4096]{1,0:T(1,128)} %bitcast.4, f32[1,4096]{1,0:T(1,128)} %bitcast.5, ...), custom_call_target="tpu_custom_call" | custom-call | tf_op jit(solution)/shard_map/pallas_call | solution.py:270
  2.6 3.0 %collective-permute-start = (bf16[64,512]{1,0:T(8,128)(2,1)S(1)}, bf16[64,512]{1,0:T(8,128)(2,1)S(1)}, u32[]{:S(2)}, u32[]{:S(2)}) collective-permute-start(bf16[64,512]{1,0:T(8,128)(2,1)S(1)} %get-tuple-element.28.refs_1_), channel_id=1, source_target_pairs={{0,16},{16,0},{1,17},{17,1},{2,18},{18,2},{3,19},{19,3},{4,20},{20... | collective-permute-start | bytes 196616 | tf_op jit(solution)/shard_map/ppermute | solution.py:294
  5.6 0.7 %shard_map.69 = (bf16[256,4096]{1,0:T(8,128)(2,1)S(1)}, bf16[4096,256]{1,0:T(8,128)(2,1)S(1)}, bf16[16,4096]{1,0:T(8,128)(2,1)S(1)}) custom-call(bf16[64,4096]{1,0:T(8,128)(2,1)S(1)} %get-tuple-element.23.feat_ref, s32[1,4096]{1,0:T(1,128)S(1)} %get-tuple-element.24.slots_ref.refs_3_.refs_4_, f32[1,4096]{1,0:T(1,128)S(1)} %get-tuple-element.25.prices_ref), custom_call_target="tpu_custom_call" | custom-call | flops 4096000 | bytes 4194304 | tf_op jit(solution)/shard_map/pallas_call | solution.py:270
  6.3 1.6 %collective-permute-done.refs_0_ = bf16[64,512]{1,0:T(8,128)(2,1)S(1)} collective-permute-done((bf16[64,512]{1,0:T(8,128)(2,1)S(1)}, bf16[64,512]{1,0:T(8,128)(2,1)S(1)}, u32[]{:S(2)}, u32[]{:S(2)}) %collective-permute-start) | collective-permute-done | bytes 65568 | tf_op jit(solution)/shard_map/ppermute | solution.py:294
  7.8 2.5 %shard_map.70 = (bf16[8192,512]{1,0:T(8,128)(2,1)S(1)}, bf16[256,512]{1,0:T(8,128)(2,1)S(1)}, f32[8,512]{1,0:T(8,128)S(1)}) custom-call(bf16[4096,256]{1,0:T(8,128)(2,1)S(1)} %get-tuple-element.26.turned_ref, bf16[16,4096]{1,0:T(8,128)(2,1)S(1)} %get-tuple-element.27.weight_ref, bf16[64,512]{1,0:T(8,128)(2,1)S(1)} %collective-permute-done.refs_0_, ...), custom_call_target="tpu_custom_call" | custom-call | flops 134217728 | bytes 8388608 | tf_op jit(solution)/shard_map/pallas_call | solution.py:270
  10.3 2.1 %collective-permute-start.1 = (f32[8,512]{1,0:T(8,128)S(1)}, f32[8,512]{1,0:T(8,128)S(1)}, u32[]{:S(2)}, u32[]{:S(2)}) collective-permute-start(f32[8,512]{1,0:T(8,128)S(1)} %get-tuple-element.29.refs_1_), channel_id=1, source_target_pairs={{0,16},{16,0},{1,17},{17,1},{2,18},{18,2},{3,19},{19,3},{4,20},{20... | collective-permute-start | bytes 49160 | tf_op jit(solution)/shard_map/ppermute | solution.py:294
  12.5 1.9 %shard_map.71.refs_4_ = bf16[1024,4096]{1,0:T(8,128)(2,1)S(1)} custom-call(bf16[256,4096]{1,0:T(8,128)(2,1)S(1)} %get-tuple-element.31.columns_ref, bf16[256,512]{1,0:T(8,128)(2,1)S(1)} %get-tuple-element.32.center_ref), custom_call_target="tpu_custom_call" | custom-call | flops 134217728 | bytes 8388608 | tf_op jit(solution)/shard_map/pallas_call | solution.py:270
  14.4 0.0 collective-permute-done.1.refs_0_
  14.4 1.2 %shard_map.72 = (f32[8,512]{1,0:T(8,128)S(1)}, f32[1,4224]{1,0:T(1,128)S(1)}) custom-call(f32[8,512]{1,0:T(8,128)S(1)} %collective-permute-done.1.refs_0_, f32[8,512]{1,0:T(8,128)S(1)} %get-tuple-element.29.refs_1_, f32[1,512]{1,0:T(1,128)S(1)} %get-tuple-element.30.refs_2_, s32[1,4096]{1,0:T(1,128)S(1)} %get-tuple-element.24.slots_ref.refs_3_.refs_4_, ...), custom_call_target="tpu_custom_call" | custom-call | tf_op jit(solution)/shard_map/pallas_call | solution.py:270
  15.6 0.1 collective-permute-start.2
  15.7 1.9 %collective-permute-start.3 = (f32[1,4224]{1,0:T(1,128)S(1)}, f32[1,4224]{1,0:T(1,128)S(1)}, u32[]{:S(2)}, u32[]{:S(2)}) collective-permute-start(f32[1,4224]{1,0:T(1,128)S(1)} %get-tuple-element.33), channel_id=1, source_target_pairs={{0,2},{1,3},{2,0},{3,1},{4,6},{5,7},{6,4},{7,5},{8,10},{9,11},{10,... | collective-permute-start | bytes 50696 | tf_op jit(solution)/shard_map/ppermute | solution.py:294
  17.6 0.0 collective-permute-start.4
  17.6 1.2 %collective-permute-done.2 = f32[1,4224]{1,0:T(1,128)S(1)} collective-permute-done((f32[1,4224]{1,0:T(1,128)S(1)}, f32[1,4224]{1,0:T(1,128)S(1)}, u32[]{:S(2)}, u32[]{:S(2)}) %collective-permute-start.2) | collective-permute-done | bytes 16928 | tf_op jit(solution)/shard_map/ppermute | solution.py:294
  18.8 0.7 %collective-permute-done.3 = f32[1,4224]{1,0:T(1,128)S(1)} collective-permute-done((f32[1,4224]{1,0:T(1,128)S(1)}, f32[1,4224]{1,0:T(1,128)S(1)}, u32[]{:S(2)}, u32[]{:S(2)}) %collective-permute-start.3) | collective-permute-done | bytes 16928 | tf_op jit(solution)/shard_map/ppermute | solution.py:294
  19.5 0.0 collective-permute-done.4
  19.5 4.0 %collective-permute-start.5 = (f32[1,4224]{1,0:T(1,128)S(1)}, f32[1,4224]{1,0:T(1,128)S(1)}, u32[]{:S(2)}, u32[]{:S(2)}) collective-permute-start(f32[1,4224]{1,0:T(1,128)S(1)} %add_add_fusion.1.refs_3_), channel_id=1, source_target_pairs={{0,13},{1,12},{2,15},{3,14},{4,9},{5,8},{6,11},{7,10},{8,5},{9,4},... | collective-permute-start | bytes 50696 | tf_op jit(solution)/shard_map/ppermute | solution.py:294
  23.6 0.0 collective-permute-start.6
  23.6 0.5 collective-permute-start.7
  24.0 1.0 %collective-permute-done.5.refs_0_ = f32[1,4224]{1,0:T(1,128)S(1)} collective-permute-done((f32[1,4224]{1,0:T(1,128)S(1)}, f32[1,4224]{1,0:T(1,128)S(1)}, u32[]{:S(2)}, u32[]{:S(2)}) %collective-permute-start.5) | collective-permute-done | bytes 16928 | tf_op jit(solution)/shard_map/ppermute | solution.py:294
  25.0 2.6 %collective-permute-done.6.refs_1_ = f32[1,4224]{1,0:T(1,128)S(1)} collective-permute-done((f32[1,4224]{1,0:T(1,128)S(1)}, f32[1,4224]{1,0:T(1,128)S(1)}, u32[]{:S(2)}, u32[]{:S(2)}) %collective-permute-start.6) | collective-permute-done | bytes 16928 | tf_op jit(solution)/shard_map/ppermute | solution.py:294
  27.6 0.0 collective-permute-done.7.refs_2_
  27.6 1.2 %shard_map.73 = (f32[1,4224]{1,0:T(1,128)S(1)}, f32[8,128]{1,0:T(8,128)S(1)}, f32[8,640]{1,0:T(8,128)S(1)}) custom-call(f32[1,4224]{1,0:T(1,128)S(1)} %collective-permute-done.5.refs_0_, f32[1,4224]{1,0:T(1,128)S(1)} %collective-permute-done.6.refs_1_, f32[1,4224]{1,0:T(1,128)S(1)} %collective-permute-done.7.refs_2_, f32[1,4224]{1,0:T(1,128)S(1)} %add_add_fusion.1.refs_3_, ...), custom_call_target="tpu_custom_call" | custom-call | tf_op jit(solution)/shard_map/pallas_call | solution.py:270
  28.8 1.5 %collective-permute-start.8 = (f32[8,640]{1,0:T(8,128)S(1)}, f32[8,640]{1,0:T(8,128)S(1)}, u32[]{:S(2)}, u32[]{:S(2)}) collective-permute-start(f32[8,640]{1,0:T(8,128)S(1)} %get-tuple-element.35.refs_1_), channel_id=1, source_target_pairs={{0,16},{16,0},{1,17},{17,1},{2,18},{18,2},{3,19},{19,3},{4,20},{20... | collective-permute-start | bytes 61448 | tf_op jit(solution)/shard_map/ppermute | solution.py:294
  30.3 2.3 %collective-permute-done.8.refs_0_ = f32[8,640]{1,0:T(8,128)S(1)} collective-permute-done((f32[8,640]{1,0:T(8,128)S(1)}, f32[8,640]{1,0:T(8,128)S(1)}, u32[]{:S(2)}, u32[]{:S(2)}) %collective-permute-start.8) | collective-permute-done | bytes 20512 | tf_op jit(solution)/shard_map/ppermute | solution.py:294
  32.6 1.2 %shard_map.74 = (f32[8,512]{1,0:T(8,128)S(1)}, f32[8,128]{1,0:T(8,128)S(1)}, f32[1,4224]{1,0:T(1,128)S(1)}) custom-call(f32[8,640]{1,0:T(8,128)S(1)} %collective-permute-done.8.refs_0_, f32[8,640]{1,0:T(8,128)S(1)} %get-tuple-element.35.refs_1_, f32[1,512]{1,0:T(1,128)S(1)} %get-tuple-element.30.refs_2_, ...), custom_call_target="tpu_custom_call" | custom-call | tf_op jit(solution)/shard_map/pallas_call | solution.py:270
  33.8 0.5 collective-permute-start.10
  34.3 0.4 collective-permute-start.11
  34.7 1.1 %collective-permute-start.9 = (f32[1,4224]{1,0:T(1,128)S(1)}, f32[1,4224]{1,0:T(1,128)S(1)}, u32[]{:S(2)}, u32[]{:S(2)}) collective-permute-start(f32[1,4224]{1,0:T(1,128)S(1)} %get-tuple-element.38), channel_id=1, source_target_pairs={{0,1},{1,0},{2,3},{3,2},{4,5},{5,4},{6,7},{7,6},{8,9},{9,8},{10,11... | collective-permute-start | bytes 50696 | tf_op jit(solution)/shard_map/ppermute | solution.py:294
  35.8 1.3 %collective-permute-done.10 = f32[1,4224]{1,0:T(1,128)S(1)} collective-permute-done((f32[1,4224]{1,0:T(1,128)S(1)}, f32[1,4224]{1,0:T(1,128)S(1)}, u32[]{:S(2)}, u32[]{:S(2)}) %collective-permute-start.10) | collective-permute-done | bytes 16928 | tf_op jit(solution)/shard_map/ppermute | solution.py:294
  37.1 1.0 %collective-permute-done.11 = f32[1,4224]{1,0:T(1,128)S(1)} collective-permute-done((f32[1,4224]{1,0:T(1,128)S(1)}, f32[1,4224]{1,0:T(1,128)S(1)}, u32[]{:S(2)}, u32[]{:S(2)}) %collective-permute-start.11) | collective-permute-done | bytes 16928 | tf_op jit(solution)/shard_map/ppermute | solution.py:294
  38.1 0.0 collective-permute-done.9
  38.1 1.1 %collective-permute-start.12 = (f32[1,4224]{1,0:T(1,128)S(1)}, f32[1,4224]{1,0:T(1,128)S(1)}, u32[]{:S(2)}, u32[]{:S(2)}) collective-permute-start(f32[1,4224]{1,0:T(1,128)S(1)} %add_add_fusion.refs_3_), channel_id=1, source_target_pairs={{0,13},{1,12},{2,15},{3,14},{4,9},{5,8},{6,11},{7,10},{8,5},{9,4},... | collective-permute-start | bytes 50696 | tf_op jit(solution)/shard_map/ppermute | solution.py:294
  39.2 0.5 %collective-permute-start.13 = (f32[1,4224]{1,0:T(1,128)S(1)}, f32[1,4224]{1,0:T(1,128)S(1)}, u32[]{:S(2)}, u32[]{:S(2)}) collective-permute-start(f32[1,4224]{1,0:T(1,128)S(1)} %add_add_fusion.refs_3_), channel_id=1, source_target_pairs={{0,9},{1,8},{2,11},{3,10},{4,13},{5,12},{6,15},{7,14},{8,1},{9,0},... | collective-permute-start | bytes 50696 | tf_op jit(solution)/shard_map/ppermute | solution.py:294
  39.7 1.5 %collective-permute-start.14 = (f32[1,4224]{1,0:T(1,128)S(1)}, f32[1,4224]{1,0:T(1,128)S(1)}, u32[]{:S(2)}, u32[]{:S(2)}) collective-permute-start(f32[1,4224]{1,0:T(1,128)S(1)} %add_add_fusion.refs_3_), channel_id=1, source_target_pairs={{0,5},{1,4},{2,7},{3,6},{4,1},{5,0},{6,3},{7,2},{8,13},{9,12},{10,... | collective-permute-start | bytes 50696 | tf_op jit(solution)/shard_map/ppermute | solution.py:294
  41.2 2.0 %collective-permute-done.12.refs_0_ = f32[1,4224]{1,0:T(1,128)S(1)} collective-permute-done((f32[1,4224]{1,0:T(1,128)S(1)}, f32[1,4224]{1,0:T(1,128)S(1)}, u32[]{:S(2)}, u32[]{:S(2)}) %collective-permute-start.12) | collective-permute-done | bytes 16928 | tf_op jit(solution)/shard_map/ppermute | solution.py:294
  43.1 0.2 collective-permute-done.13.refs_1_
  43.3 0.0 collective-permute-done.14.refs_2_
  43.3 1.3 %shard_map.75 = (f32[8,256]{1,0:T(8,128)S(1)}, f32[8,640]{1,0:T(8,128)S(1)}) custom-call(f32[1,4224]{1,0:T(1,128)S(1)} %collective-permute-done.12.refs_0_, f32[1,4224]{1,0:T(1,128)S(1)} %collective-permute-done.13.refs_1_, f32[1,4224]{1,0:T(1,128)S(1)} %collective-permute-done.14.refs_2_, f32[1,4224]{1,0:T(1,128)S(1)} %add_add_fusion.refs_3_, ...), custom_call_target="tpu_custom_call" | custom-call | tf_op jit(solution)/shard_map/pallas_call | solution.py:270
  44.6 1.5 %collective-permute-start.15 = (f32[8,640]{1,0:T(8,128)S(1)}, f32[8,640]{1,0:T(8,128)S(1)}, u32[]{:S(2)}, u32[]{:S(2)}) collective-permute-start(f32[8,640]{1,0:T(8,128)S(1)} %get-tuple-element.40.refs_1_), channel_id=1, source_target_pairs={{0,16},{16,0},{1,17},{17,1},{2,18},{18,2},{3,19},{19,3},{4,20},{20... | collective-permute-start | bytes 61448 | tf_op jit(solution)/shard_map/ppermute | solution.py:294
  46.1 2.3 %collective-permute-done.15.refs_0_ = f32[8,640]{1,0:T(8,128)S(1)} collective-permute-done((f32[8,640]{1,0:T(8,128)S(1)}, f32[8,640]{1,0:T(8,128)S(1)}, u32[]{:S(2)}, u32[]{:S(2)}) %collective-permute-start.15) | collective-permute-done | bytes 20512 | tf_op jit(solution)/shard_map/ppermute | solution.py:294
  48.4 0.6 %shard_map.76 = (f32[8,512]{1,0:T(8,128)}, f32[8,512]{1,0:T(8,128)}) custom-call(f32[8,640]{1,0:T(8,128)S(1)} %collective-permute-done.15.refs_0_, f32[8,640]{1,0:T(8,128)S(1)} %get-tuple-element.40.refs_1_, f32[1,512]{1,0:T(1,128)S(1)} %get-tuple-element.30.refs_2_, f32[8,512]{1,0:T(8,128)S(1)} %get-tuple-element.36.refs_5_.refs_3_, ...), custom_call_target="tpu_custom_call" | custom-call | tf_op jit(solution)/shard_map/pallas_call | solution.py:270
  (2 shorter events, 0.1 us)
Async XLA Ops:
  2.6 5.2 %collective-permute-start = (bf16[64,512]{1,0:T(8,128)(2,1)S(1)}, bf16[64,512]{1,0:T(8,128)(2,1)S(1)}, u32[]{:S(2)}, u32[]{:S(2)}) collective-permute-start(bf16[64,512]{1,0:T(8,128)(2,1)S(1)} %get-tuple-element.28.refs_1_), channel_id=1, source_target_pairs={{0,16},{16,0},{1,17},{17,1},{2,18},{18,2},{3,19},{19,3},{4,20},{20... | collective-permute-start | bytes 196616 | tf_op jit(solution)/shard_map/ppermute | solution.py:294
  10.3 4.0 %collective-permute-start.1 = (f32[8,512]{1,0:T(8,128)S(1)}, f32[8,512]{1,0:T(8,128)S(1)}, u32[]{:S(2)}, u32[]{:S(2)}) collective-permute-start(f32[8,512]{1,0:T(8,128)S(1)} %get-tuple-element.29.refs_1_), channel_id=1, source_target_pairs={{0,16},{16,0},{1,17},{17,1},{2,18},{18,2},{3,19},{19,3},{4,20},{20... | collective-permute-start | bytes 49160 | tf_op jit(solution)/shard_map/ppermute | solution.py:294
  15.6 3.2 %collective-permute-start.2 = (f32[1,4224]{1,0:T(1,128)S(1)}, f32[1,4224]{1,0:T(1,128)S(1)}, u32[]{:S(2)}, u32[]{:S(2)}) collective-permute-start(f32[1,4224]{1,0:T(1,128)S(1)} %get-tuple-element.33), channel_id=1, source_target_pairs={{0,3},{1,2},{2,1},{3,0},{4,7},{5,6},{6,5},{7,4},{8,11},{9,10},{10,... | collective-permute-start | bytes 50696 | tf_op jit(solution)/shard_map/ppermute | solution.py:294
  15.7 3.8 %collective-permute-start.3 = (f32[1,4224]{1,0:T(1,128)S(1)}, f32[1,4224]{1,0:T(1,128)S(1)}, u32[]{:S(2)}, u32[]{:S(2)}) collective-permute-start(f32[1,4224]{1,0:T(1,128)S(1)} %get-tuple-element.33), channel_id=1, source_target_pairs={{0,2},{1,3},{2,0},{3,1},{4,6},{5,7},{6,4},{7,5},{8,10},{9,11},{10,... | collective-permute-start | bytes 50696 | tf_op jit(solution)/shard_map/ppermute | solution.py:294
  17.6 1.9 %collective-permute-start.4 = (f32[1,4224]{1,0:T(1,128)S(1)}, f32[1,4224]{1,0:T(1,128)S(1)}, u32[]{:S(2)}, u32[]{:S(2)}) collective-permute-start(f32[1,4224]{1,0:T(1,128)S(1)} %get-tuple-element.33), channel_id=1, source_target_pairs={{0,1},{1,0},{2,3},{3,2},{4,5},{5,4},{6,7},{7,6},{8,9},{9,8},{10,11... | collective-permute-start | bytes 50696 | tf_op jit(solution)/shard_map/ppermute | solution.py:294
  19.5 5.5 %collective-permute-start.5 = (f32[1,4224]{1,0:T(1,128)S(1)}, f32[1,4224]{1,0:T(1,128)S(1)}, u32[]{:S(2)}, u32[]{:S(2)}) collective-permute-start(f32[1,4224]{1,0:T(1,128)S(1)} %add_add_fusion.1.refs_3_), channel_id=1, source_target_pairs={{0,13},{1,12},{2,15},{3,14},{4,9},{5,8},{6,11},{7,10},{8,5},{9,4},... | collective-permute-start | bytes 50696 | tf_op jit(solution)/shard_map/ppermute | solution.py:294
  23.6 4.1 %collective-permute-start.6 = (f32[1,4224]{1,0:T(1,128)S(1)}, f32[1,4224]{1,0:T(1,128)S(1)}, u32[]{:S(2)}, u32[]{:S(2)}) collective-permute-start(f32[1,4224]{1,0:T(1,128)S(1)} %add_add_fusion.1.refs_3_), channel_id=1, source_target_pairs={{0,9},{1,8},{2,11},{3,10},{4,13},{5,12},{6,15},{7,14},{8,1},{9,0},... | collective-permute-start | bytes 50696 | tf_op jit(solution)/shard_map/ppermute | solution.py:294
  23.6 4.1 %collective-permute-start.7 = (f32[1,4224]{1,0:T(1,128)S(1)}, f32[1,4224]{1,0:T(1,128)S(1)}, u32[]{:S(2)}, u32[]{:S(2)}) collective-permute-start(f32[1,4224]{1,0:T(1,128)S(1)} %add_add_fusion.1.refs_3_), channel_id=1, source_target_pairs={{0,5},{1,4},{2,7},{3,6},{4,1},{5,0},{6,3},{7,2},{8,13},{9,12},{10,... | collective-permute-start | bytes 50696 | tf_op jit(solution)/shard_map/ppermute | solution.py:294
  28.8 3.8 %collective-permute-start.8 = (f32[8,640]{1,0:T(8,128)S(1)}, f32[8,640]{1,0:T(8,128)S(1)}, u32[]{:S(2)}, u32[]{:S(2)}) collective-permute-start(f32[8,640]{1,0:T(8,128)S(1)} %get-tuple-element.35.refs_1_), channel_id=1, source_target_pairs={{0,16},{16,0},{1,17},{17,1},{2,18},{18,2},{3,19},{19,3},{4,20},{20... | collective-permute-start | bytes 61448 | tf_op jit(solution)/shard_map/ppermute | solution.py:294
  33.8 3.2 %collective-permute-start.10 = (f32[1,4224]{1,0:T(1,128)S(1)}, f32[1,4224]{1,0:T(1,128)S(1)}, u32[]{:S(2)}, u32[]{:S(2)}) collective-permute-start(f32[1,4224]{1,0:T(1,128)S(1)} %get-tuple-element.38), channel_id=1, source_target_pairs={{0,3},{1,2},{2,1},{3,0},{4,7},{5,6},{6,5},{7,4},{8,11},{9,10},{10,... | collective-permute-start | bytes 50696 | tf_op jit(solution)/shard_map/ppermute | solution.py:294
  34.3 3.7 %collective-permute-start.11 = (f32[1,4224]{1,0:T(1,128)S(1)}, f32[1,4224]{1,0:T(1,128)S(1)}, u32[]{:S(2)}, u32[]{:S(2)}) collective-permute-start(f32[1,4224]{1,0:T(1,128)S(1)} %get-tuple-element.38), channel_id=1, source_target_pairs={{0,2},{1,3},{2,0},{3,1},{4,6},{5,7},{6,4},{7,5},{8,10},{9,11},{10,... | collective-permute-start | bytes 50696 | tf_op jit(solution)/shard_map/ppermute | solution.py:294
  34.7 3.4 %collective-permute-start.9 = (f32[1,4224]{1,0:T(1,128)S(1)}, f32[1,4224]{1,0:T(1,128)S(1)}, u32[]{:S(2)}, u32[]{:S(2)}) collective-permute-start(f32[1,4224]{1,0:T(1,128)S(1)} %get-tuple-element.38), channel_id=1, source_target_pairs={{0,1},{1,0},{2,3},{3,2},{4,5},{5,4},{6,7},{7,6},{8,9},{9,8},{10,11... | collective-permute-start | bytes 50696 | tf_op jit(solution)/shard_map/ppermute | solution.py:294
  38.1 5.0 %collective-permute-start.12 = (f32[1,4224]{1,0:T(1,128)S(1)}, f32[1,4224]{1,0:T(1,128)S(1)}, u32[]{:S(2)}, u32[]{:S(2)}) collective-permute-start(f32[1,4224]{1,0:T(1,128)S(1)} %add_add_fusion.refs_3_), channel_id=1, source_target_pairs={{0,13},{1,12},{2,15},{3,14},{4,9},{5,8},{6,11},{7,10},{8,5},{9,4},... | collective-permute-start | bytes 50696 | tf_op jit(solution)/shard_map/ppermute | solution.py:294
  39.2 4.2 %collective-permute-start.13 = (f32[1,4224]{1,0:T(1,128)S(1)}, f32[1,4224]{1,0:T(1,128)S(1)}, u32[]{:S(2)}, u32[]{:S(2)}) collective-permute-start(f32[1,4224]{1,0:T(1,128)S(1)} %add_add_fusion.refs_3_), channel_id=1, source_target_pairs={{0,9},{1,8},{2,11},{3,10},{4,13},{5,12},{6,15},{7,14},{8,1},{9,0},... | collective-permute-start | bytes 50696 | tf_op jit(solution)/shard_map/ppermute | solution.py:294
  39.7 3.7 %collective-permute-start.14 = (f32[1,4224]{1,0:T(1,128)S(1)}, f32[1,4224]{1,0:T(1,128)S(1)}, u32[]{:S(2)}, u32[]{:S(2)}) collective-permute-start(f32[1,4224]{1,0:T(1,128)S(1)} %add_add_fusion.refs_3_), channel_id=1, source_target_pairs={{0,5},{1,4},{2,7},{3,6},{4,1},{5,0},{6,3},{7,2},{8,13},{9,12},{10,... | collective-permute-start | bytes 50696 | tf_op jit(solution)/shard_map/ppermute | solution.py:294
  44.6 3.8 %collective-permute-start.15 = (f32[8,640]{1,0:T(8,128)S(1)}, f32[8,640]{1,0:T(8,128)S(1)}, u32[]{:S(2)}, u32[]{:S(2)}) collective-permute-start(f32[8,640]{1,0:T(8,128)S(1)} %get-tuple-element.40.refs_1_), channel_id=1, source_target_pairs={{0,16},{16,0},{1,17},{17,1},{2,18},{18,2},{3,19},{19,3},{4,20},{20... | collective-permute-start | bytes 61448 | tf_op jit(solution)/shard_map/ppermute | solution.py:294

commit v12 on v11

--- a/solution.py
+++ b/solution.py
@@ -151,37 +151,56 @@
     total = jnp.zeros(out_ref.shape, f32)
 
     def fold(begin):
-        end = begin + CHUNK
         return product(
-            weight_ref[:, begin:end],
-            block_ref[begin:end, :],
-            block_ref[row_count + begin : row_count + end, :],
+            weight_ref[:, pl.ds(begin, CHUNK)],
+            block_ref[pl.ds(begin, CHUNK), :],
+            block_ref[pl.ds(row_count + begin, CHUNK), :],
         )
 
-    for begin in range(0, row_count, CHUNK):
-        high, low = kernel_parts(turned_ref[begin : begin + CHUNK, :], center)
-        block_ref[begin : begin + CHUNK, :] = high
-        block_ref[row_count + begin : row_count + begin + CHUNK, :] = low
-        if begin > 0:
-            total += fold(begin - CHUNK)
-    out_ref[...] = total + fold(row_count - CHUNK)
+    half = row_count // 2
+
+    def visit(turn, total):
+        first = pl.multiple_of(turn * half, half)
+        for begin in range(0, half, CHUNK):
+            high, low = kernel_parts(turned_ref[pl.ds(first + begin, CHUNK), :], center)
+            block_ref[pl.ds(first + begin, CHUNK), :] = high
+            block_ref[pl.ds(first + row_count + begin, CHUNK), :] = low
+            if begin > 0:
+                total += fold(first + begin - CHUNK)
+        return total + fold(first + half - CHUNK)
+
+    out_ref[...] = lax.fori_loop(0, 2, visit, total)
 
 
 def turned_body(columns_ref, center_ref, block_ref):
     center = center_ref[...].astype(f32).T.astype(bf16)
     count = center.shape[0]
-    for begin in range(0, columns_ref.shape[1], CHUNK):
-        here = slice(begin, begin + CHUNK)
-        high, low = kernel_parts(center, columns_ref[:, here])
-        block_ref[0:count, here] = high
-        block_ref[count:, here] = low
+    half = columns_ref.shape[1] // 2
+
+    def visit(turn, carry):
+        first = pl.multiple_of(turn * half, half)
+        for begin in range(0, half, CHUNK):
+            here = pl.ds(first + begin, CHUNK)
+            high, low = kernel_parts(center, columns_ref[:, here])
+            block_ref[0:count, here] = high
+            block_ref[count:, here] = low
+        return carry
+
+    lax.fori_loop(0, 2, visit, 0)
 
 
 def apply_rows(scaled, turned_ref, slots_ref, out_ref):
-    count, row_count = scaled.shape[1], turned_ref.shape[1]
-    value = product(stack2(scaled), turned_ref[0:count, :], turned_ref[count:, :])
-    own = jnp.where(slot_mask(slots_ref[...]), value, 0.0)
-    out_ref[:, 0:row_count] = jnp.sum(own, axis=0, keepdims=True)
+    count, half = scaled.shape[1], turned_ref.shape[1] // 2
+    stacked = stack2(scaled)
+
+    def visit(turn, carry):
+        here = pl.ds(pl.multiple_of(turn * half, half), half)
+        value = product(stacked, turned_ref[0:count, here], turned_ref[count:, here])
+        own = jnp.where(slot_mask(slots_ref[:, here]), value, 0.0)
+        out_ref[:, here] = jnp.sum(own, axis=0, keepdims=True)
+        return carry
+
+    lax.fori_loop(0, 2, visit, 0)
 
 
 def fold_rows(rows, block_ref, slots_ref, out_ref):

time: 49.2 us -> 51.2 us (1.041)
  Pallas kernels: 12.5 us -> 14.9 us
    pallas_call x9, Pallas kernels: 12.5 us -> 14.9 us  [call(): pl.pallas_call(body, out_shape=out_shape, in_specs=[source] * len(args),...]
where the time goes in v12:
time: 51.2 us; the launch traced here: 51.1 us
  starting transfers between devices  19.3 us (38%)
  waiting for transfers between devices  16.1 us (31%)
  Pallas kernels  14.9 us (29%)
  between operations  0.71 us (1%)
    ppermute x16, starting transfers between devices, exchange(): parts.insert(0, lax.ppermute(value, axis, pairs))  19.3 us
    ppermute x16, waiting for transfers between devices, exchange(): parts.insert(0, lax.ppermute(value, axis, pairs))  16.1 us
    pallas_call x9, Pallas kernels, call(): pl.pallas_call(body, out_shape=out_shape, in_specs=[source] * len(args),...  14.9 us
  transfers between devices with their start and end apart: 16, of which 11 were waited for; matrix products, arithmetic and copies ran while one was open for 0% of the time, Pallas kernels for 5%

profile of v12, /device:TPU:0, one launch (start us, length us, event | category | flops | bytes accessed | tf_op | source)
XLA Modules:
  0.0 51.1 jit_solution(2576248664137856848)
XLA Ops:
  0.6 1.9 %shard_map.68 = (bf16[64,4096]{1,0:T(8,128)(2,1)S(1)}, s32[1,4096]{1,0:T(1,128)S(1)}, f32[1,4096]{1,0:T(1,128)S(1)}, f32[1,512]{1,0:T(1,128)S(1)}, bf16[64,512]{1,0:T(8,128)(2,1)S(1)}) custom-call(bf16[64,4096]{1,0:T(8,128)(2,1)} %feat_hbm.1, s32[1,512]{1,0:T(1,128)} %bitcast.6, s32[1,4096]{1,0:T(1,128)} %bitcast.4, f32[1,4096]{1,0:T(1,128)} %bitcast.5, ...), custom_call_target="tpu_custom_call" | custom-call | tf_op jit(solution)/shard_map/pallas_call | solution.py:289
  2.6 3.0 %collective-permute-start = (bf16[64,512]{1,0:T(8,128)(2,1)S(1)}, bf16[64,512]{1,0:T(8,128)(2,1)S(1)}, u32[]{:S(2)}, u32[]{:S(2)}) collective-permute-start(bf16[64,512]{1,0:T(8,128)(2,1)S(1)} %get-tuple-element.28.refs_1_), channel_id=1, source_target_pairs={{0,16},{16,0},{1,17},{17,1},{2,18},{18,2},{3,19},{19,3},{4,20},{20... | collective-permute-start | bytes 196616 | tf_op jit(solution)/shard_map/ppermute | solution.py:313
  5.6 0.7 %shard_map.69 = (bf16[256,4096]{1,0:T(8,128)(2,1)S(1)}, bf16[4096,256]{1,0:T(8,128)(2,1)S(1)}, bf16[16,4096]{1,0:T(8,128)(2,1)S(1)}) custom-call(bf16[64,4096]{1,0:T(8,128)(2,1)S(1)} %get-tuple-element.23.feat_ref, s32[1,4096]{1,0:T(1,128)S(1)} %get-tuple-element.24.slots_ref.refs_3_.refs_4_, f32[1,4096]{1,0:T(1,128)S(1)} %get-tuple-element.25.prices_ref), custom_call_target="tpu_custom_call" | custom-call | flops 4096000 | bytes 4194304 | tf_op jit(solution)/shard_map/pallas_call | solution.py:289
  6.3 1.6 %collective-permute-done.refs_0_ = bf16[64,512]{1,0:T(8,128)(2,1)S(1)} collective-permute-done((bf16[64,512]{1,0:T(8,128)(2,1)S(1)}, bf16[64,512]{1,0:T(8,128)(2,1)S(1)}, u32[]{:S(2)}, u32[]{:S(2)}) %collective-permute-start) | collective-permute-done | bytes 65568 | tf_op jit(solution)/shard_map/ppermute | solution.py:313
  7.8 4.2 %shard_map.70 = (bf16[8192,512]{1,0:T(8,128)(2,1)S(1)}, bf16[256,512]{1,0:T(8,128)(2,1)S(1)}, f32[8,512]{1,0:T(8,128)S(1)}) custom-call(bf16[4096,256]{1,0:T(8,128)(2,1)S(1)} %get-tuple-element.26.turned_ref, bf16[16,4096]{1,0:T(8,128)(2,1)S(1)} %get-tuple-element.27.weight_ref, bf16[64,512]{1,0:T(8,128)(2,1)S(1)} %collective-permute-done.refs_0_, ...), custom_call_target="tpu_custom_call" | custom-call | flops 134217728 | bytes 8388608 | tf_op jit(solution)/shard_map/pallas_call | solution.py:289
  12.0 2.1 %collective-permute-start.1 = (f32[8,512]{1,0:T(8,128)S(1)}, f32[8,512]{1,0:T(8,128)S(1)}, u32[]{:S(2)}, u32[]{:S(2)}) collective-permute-start(f32[8,512]{1,0:T(8,128)S(1)} %get-tuple-element.29.refs_1_), channel_id=1, source_target_pairs={{0,16},{16,0},{1,17},{17,1},{2,18},{18,2},{3,19},{19,3},{4,20},{20... | collective-permute-start | bytes 49160 | tf_op jit(solution)/shard_map/ppermute | solution.py:313
  14.1 2.1 %shard_map.71.refs_4_ = bf16[1024,4096]{1,0:T(8,128)(2,1)S(1)} custom-call(bf16[256,4096]{1,0:T(8,128)(2,1)S(1)} %get-tuple-element.31.columns_ref, bf16[256,512]{1,0:T(8,128)(2,1)S(1)} %get-tuple-element.32.center_ref), custom_call_target="tpu_custom_call" | custom-call | flops 134217728 | bytes 8388608 | tf_op jit(solution)/shard_map/pallas_call | solution.py:289
  16.2 0.0 collective-permute-done.1.refs_0_
  16.2 1.4 %shard_map.72 = (f32[8,512]{1,0:T(8,128)S(1)}, f32[1,4224]{1,0:T(1,128)S(1)}) custom-call(f32[8,512]{1,0:T(8,128)S(1)} %collective-permute-done.1.refs_0_, f32[8,512]{1,0:T(8,128)S(1)} %get-tuple-element.29.refs_1_, f32[1,512]{1,0:T(1,128)S(1)} %get-tuple-element.30.refs_2_, s32[1,4096]{1,0:T(1,128)S(1)} %get-tuple-element.24.slots_ref.refs_3_.refs_4_, ...), custom_call_target="tpu_custom_call" | custom-call | tf_op jit(solution)/shard_map/pallas_call | solution.py:289
  17.7 0.1 collective-permute-start.2
  17.8 1.7 %collective-permute-start.3 = (f32[1,4224]{1,0:T(1,128)S(1)}, f32[1,4224]{1,0:T(1,128)S(1)}, u32[]{:S(2)}, u32[]{:S(2)}) collective-permute-start(f32[1,4224]{1,0:T(1,128)S(1)} %get-tuple-element.33), channel_id=1, source_target_pairs={{0,2},{1,3},{2,0},{3,1},{4,6},{5,7},{6,4},{7,5},{8,10},{9,11},{10,... | collective-permute-start | bytes 50696 | tf_op jit(solution)/shard_map/ppermute | solution.py:313
  19.5 0.2 collective-permute-start.4
  19.6 1.3 %collective-permute-done.2 = f32[1,4224]{1,0:T(1,128)S(1)} collective-permute-done((f32[1,4224]{1,0:T(1,128)S(1)}, f32[1,4224]{1,0:T(1,128)S(1)}, u32[]{:S(2)}, u32[]{:S(2)}) %collective-permute-start.2) | collective-permute-done | bytes 16928 | tf_op jit(solution)/shard_map/ppermute | solution.py:313
  20.9 0.7 %collective-permute-done.3 = f32[1,4224]{1,0:T(1,128)S(1)} collective-permute-done((f32[1,4224]{1,0:T(1,128)S(1)}, f32[1,4224]{1,0:T(1,128)S(1)}, u32[]{:S(2)}, u32[]{:S(2)}) %collective-permute-start.3) | collective-permute-done | bytes 16928 | tf_op jit(solution)/shard_map/ppermute | solution.py:313
  21.6 0.0 collective-permute-done.4
  21.6 3.8 %collective-permute-start.5 = (f32[1,4224]{1,0:T(1,128)S(1)}, f32[1,4224]{1,0:T(1,128)S(1)}, u32[]{:S(2)}, u32[]{:S(2)}) collective-permute-start(f32[1,4224]{1,0:T(1,128)S(1)} %add_add_fusion.1.refs_3_), channel_id=1, source_target_pairs={{0,13},{1,12},{2,15},{3,14},{4,9},{5,8},{6,11},{7,10},{8,5},{9,4},... | collective-permute-start | bytes 50696 | tf_op jit(solution)/shard_map/ppermute | solution.py:313
  25.4 0.0 collective-permute-start.6
  25.4 0.5 collective-permute-start.7
  25.9 1.0 %collective-permute-done.5.refs_0_ = f32[1,4224]{1,0:T(1,128)S(1)} collective-permute-done((f32[1,4224]{1,0:T(1,128)S(1)}, f32[1,4224]{1,0:T(1,128)S(1)}, u32[]{:S(2)}, u32[]{:S(2)}) %collective-permute-start.5) | collective-permute-done | bytes 16928 | tf_op jit(solution)/shard_map/ppermute | solution.py:313
  26.9 2.6 %collective-permute-done.6.refs_1_ = f32[1,4224]{1,0:T(1,128)S(1)} collective-permute-done((f32[1,4224]{1,0:T(1,128)S(1)}, f32[1,4224]{1,0:T(1,128)S(1)}, u32[]{:S(2)}, u32[]{:S(2)}) %collective-permute-start.6) | collective-permute-done | bytes 16928 | tf_op jit(solution)/shard_map/ppermute | solution.py:313
  29.5 0.0 collective-permute-done.7.refs_2_
  29.5 1.2 %shard_map.73 = (f32[1,4224]{1,0:T(1,128)S(1)}, f32[8,128]{1,0:T(8,128)S(1)}, f32[8,640]{1,0:T(8,128)S(1)}) custom-call(f32[1,4224]{1,0:T(1,128)S(1)} %collective-permute-done.5.refs_0_, f32[1,4224]{1,0:T(1,128)S(1)} %collective-permute-done.6.refs_1_, f32[1,4224]{1,0:T(1,128)S(1)} %collective-permute-done.7.refs_2_, f32[1,4224]{1,0:T(1,128)S(1)} %add_add_fusion.1.refs_3_, ...), custom_call_target="tpu_custom_call" | custom-call | tf_op jit(solution)/shard_map/pallas_call | solution.py:289
  30.7 1.5 %collective-permute-start.8 = (f32[8,640]{1,0:T(8,128)S(1)}, f32[8,640]{1,0:T(8,128)S(1)}, u32[]{:S(2)}, u32[]{:S(2)}) collective-permute-start(f32[8,640]{1,0:T(8,128)S(1)} %get-tuple-element.35.refs_1_), channel_id=1, source_target_pairs={{0,16},{16,0},{1,17},{17,1},{2,18},{18,2},{3,19},{19,3},{4,20},{20... | collective-permute-start | bytes 61448 | tf_op jit(solution)/shard_map/ppermute | solution.py:313
  32.2 2.3 %collective-permute-done.8.refs_0_ = f32[8,640]{1,0:T(8,128)S(1)} collective-permute-done((f32[8,640]{1,0:T(8,128)S(1)}, f32[8,640]{1,0:T(8,128)S(1)}, u32[]{:S(2)}, u32[]{:S(2)}) %collective-permute-start.8) | collective-permute-done | bytes 20512 | tf_op jit(solution)/shard_map/ppermute | solution.py:313
  34.5 1.4 %shard_map.74 = (f32[8,512]{1,0:T(8,128)S(1)}, f32[8,128]{1,0:T(8,128)S(1)}, f32[1,4224]{1,0:T(1,128)S(1)}) custom-call(f32[8,640]{1,0:T(8,128)S(1)} %collective-permute-done.8.refs_0_, f32[8,640]{1,0:T(8,128)S(1)} %get-tuple-element.35.refs_1_, f32[1,512]{1,0:T(1,128)S(1)} %get-tuple-element.30.refs_2_, ...), custom_call_target="tpu_custom_call" | custom-call | tf_op jit(solution)/shard_map/pallas_call | solution.py:289
  35.9 0.5 collective-permute-start.10
  36.4 0.4 collective-permute-start.11
  36.8 1.1 %collective-permute-start.9 = (f32[1,4224]{1,0:T(1,128)S(1)}, f32[1,4224]{1,0:T(1,128)S(1)}, u32[]{:S(2)}, u32[]{:S(2)}) collective-permute-start(f32[1,4224]{1,0:T(1,128)S(1)} %get-tuple-element.38), channel_id=1, source_target_pairs={{0,1},{1,0},{2,3},{3,2},{4,5},{5,4},{6,7},{7,6},{8,9},{9,8},{10,11... | collective-permute-start | bytes 50696 | tf_op jit(solution)/shard_map/ppermute | solution.py:313
  37.9 1.3 %collective-permute-done.10 = f32[1,4224]{1,0:T(1,128)S(1)} collective-permute-done((f32[1,4224]{1,0:T(1,128)S(1)}, f32[1,4224]{1,0:T(1,128)S(1)}, u32[]{:S(2)}, u32[]{:S(2)}) %collective-permute-start.10) | collective-permute-done | bytes 16928 | tf_op jit(solution)/shard_map/ppermute | solution.py:313
  39.2 1.0 %collective-permute-done.11 = f32[1,4224]{1,0:T(1,128)S(1)} collective-permute-done((f32[1,4224]{1,0:T(1,128)S(1)}, f32[1,4224]{1,0:T(1,128)S(1)}, u32[]{:S(2)}, u32[]{:S(2)}) %collective-permute-start.11) | collective-permute-done | bytes 16928 | tf_op jit(solution)/shard_map/ppermute | solution.py:313
  40.1 0.0 collective-permute-done.9
  40.2 1.1 %collective-permute-start.12 = (f32[1,4224]{1,0:T(1,128)S(1)}, f32[1,4224]{1,0:T(1,128)S(1)}, u32[]{:S(2)}, u32[]{:S(2)}) collective-permute-start(f32[1,4224]{1,0:T(1,128)S(1)} %add_add_fusion.refs_3_), channel_id=1, source_target_pairs={{0,13},{1,12},{2,15},{3,14},{4,9},{5,8},{6,11},{7,10},{8,5},{9,4},... | collective-permute-start | bytes 50696 | tf_op jit(solution)/shard_map/ppermute | solution.py:313
  41.2 0.5 collective-permute-start.13
  41.7 1.5 %collective-permute-start.14 = (f32[1,4224]{1,0:T(1,128)S(1)}, f32[1,4224]{1,0:T(1,128)S(1)}, u32[]{:S(2)}, u32[]{:S(2)}) collective-permute-start(f32[1,4224]{1,0:T(1,128)S(1)} %add_add_fusion.refs_3_), channel_id=1, source_target_pairs={{0,5},{1,4},{2,7},{3,6},{4,1},{5,0},{6,3},{7,2},{8,13},{9,12},{10,... | collective-permute-start | bytes 50696 | tf_op jit(solution)/shard_map/ppermute | solution.py:313
  43.2 2.0 %collective-permute-done.12.refs_0_ = f32[1,4224]{1,0:T(1,128)S(1)} collective-permute-done((f32[1,4224]{1,0:T(1,128)S(1)}, f32[1,4224]{1,0:T(1,128)S(1)}, u32[]{:S(2)}, u32[]{:S(2)}) %collective-permute-start.12) | collective-permute-done | bytes 16928 | tf_op jit(solution)/shard_map/ppermute | solution.py:313
  45.2 0.2 collective-permute-done.13.refs_1_
  45.4 0.0 collective-permute-done.14.refs_2_
  45.4 1.3 %shard_map.75 = (f32[8,256]{1,0:T(8,128)S(1)}, f32[8,640]{1,0:T(8,128)S(1)}) custom-call(f32[1,4224]{1,0:T(1,128)S(1)} %collective-permute-done.12.refs_0_, f32[1,4224]{1,0:T(1,128)S(1)} %collective-permute-done.13.refs_1_, f32[1,4224]{1,0:T(1,128)S(1)} %collective-permute-done.14.refs_2_, f32[1,4224]{1,0:T(1,128)S(1)} %add_add_fusion.refs_3_, ...), custom_call_target="tpu_custom_call" | custom-call | tf_op jit(solution)/shard_map/pallas_call | solution.py:289
  46.7 1.5 %collective-permute-start.15 = (f32[8,640]{1,0:T(8,128)S(1)}, f32[8,640]{1,0:T(8,128)S(1)}, u32[]{:S(2)}, u32[]{:S(2)}) collective-permute-start(f32[8,640]{1,0:T(8,128)S(1)} %get-tuple-element.40.refs_1_), channel_id=1, source_target_pairs={{0,16},{16,0},{1,17},{17,1},{2,18},{18,2},{3,19},{19,3},{4,20},{20... | collective-permute-start | bytes 61448 | tf_op jit(solution)/shard_map/ppermute | solution.py:313
  48.2 2.3 %collective-permute-done.15.refs_0_ = f32[8,640]{1,0:T(8,128)S(1)} collective-permute-done((f32[8,640]{1,0:T(8,128)S(1)}, f32[8,640]{1,0:T(8,128)S(1)}, u32[]{:S(2)}, u32[]{:S(2)}) %collective-permute-start.15) | collective-permute-done | bytes 20512 | tf_op jit(solution)/shard_map/ppermute | solution.py:313
  50.4 0.6 %shard_map.76 = (f32[8,512]{1,0:T(8,128)}, f32[8,512]{1,0:T(8,128)}) custom-call(f32[8,640]{1,0:T(8,128)S(1)} %collective-permute-done.15.refs_0_, f32[8,640]{1,0:T(8,128)S(1)} %get-tuple-element.40.refs_1_, f32[1,512]{1,0:T(1,128)S(1)} %get-tuple-element.30.refs_2_, f32[8,512]{1,0:T(8,128)S(1)} %get-tuple-element.36.refs_5_.refs_3_, ...), custom_call_target="tpu_custom_call" | custom-call | tf_op jit(solution)/shard_map/pallas_call | solution.py:289
  (2 shorter events, 0.1 us)
Async XLA Ops:
  2.6 5.2 %collective-permute-start = (bf16[64,512]{1,0:T(8,128)(2,1)S(1)}, bf16[64,512]{1,0:T(8,128)(2,1)S(1)}, u32[]{:S(2)}, u32[]{:S(2)}) collective-permute-start(bf16[64,512]{1,0:T(8,128)(2,1)S(1)} %get-tuple-element.28.refs_1_), channel_id=1, source_target_pairs={{0,16},{16,0},{1,17},{17,1},{2,18},{18,2},{3,19},{19,3},{4,20},{20... | collective-permute-start | bytes 196616 | tf_op jit(solution)/shard_map/ppermute | solution.py:313
  12.0 4.2 %collective-permute-start.1 = (f32[8,512]{1,0:T(8,128)S(1)}, f32[8,512]{1,0:T(8,128)S(1)}, u32[]{:S(2)}, u32[]{:S(2)}) collective-permute-start(f32[8,512]{1,0:T(8,128)S(1)} %get-tuple-element.29.refs_1_), channel_id=1, source_target_pairs={{0,16},{16,0},{1,17},{17,1},{2,18},{18,2},{3,19},{19,3},{4,20},{20... | collective-permute-start | bytes 49160 | tf_op jit(solution)/shard_map/ppermute | solution.py:313
  17.7 3.2 %collective-permute-start.2 = (f32[1,4224]{1,0:T(1,128)S(1)}, f32[1,4224]{1,0:T(1,128)S(1)}, u32[]{:S(2)}, u32[]{:S(2)}) collective-permute-start(f32[1,4224]{1,0:T(1,128)S(1)} %get-tuple-element.33), channel_id=1, source_target_pairs={{0,3},{1,2},{2,1},{3,0},{4,7},{5,6},{6,5},{7,4},{8,11},{9,10},{10,... | collective-permute-start | bytes 50696 | tf_op jit(solution)/shard_map/ppermute | solution.py:313
  17.8 3.8 %collective-permute-start.3 = (f32[1,4224]{1,0:T(1,128)S(1)}, f32[1,4224]{1,0:T(1,128)S(1)}, u32[]{:S(2)}, u32[]{:S(2)}) collective-permute-start(f32[1,4224]{1,0:T(1,128)S(1)} %get-tuple-element.33), channel_id=1, source_target_pairs={{0,2},{1,3},{2,0},{3,1},{4,6},{5,7},{6,4},{7,5},{8,10},{9,11},{10,... | collective-permute-start | bytes 50696 | tf_op jit(solution)/shard_map/ppermute | solution.py:313
  19.5 2.1 %collective-permute-start.4 = (f32[1,4224]{1,0:T(1,128)S(1)}, f32[1,4224]{1,0:T(1,128)S(1)}, u32[]{:S(2)}, u32[]{:S(2)}) collective-permute-start(f32[1,4224]{1,0:T(1,128)S(1)} %get-tuple-element.33), channel_id=1, source_target_pairs={{0,1},{1,0},{2,3},{3,2},{4,5},{5,4},{6,7},{7,6},{8,9},{9,8},{10,11... | collective-permute-start | bytes 50696 | tf_op jit(solution)/shard_map/ppermute | solution.py:313
  21.6 5.3 %collective-permute-start.5 = (f32[1,4224]{1,0:T(1,128)S(1)}, f32[1,4224]{1,0:T(1,128)S(1)}, u32[]{:S(2)}, u32[]{:S(2)}) collective-permute-start(f32[1,4224]{1,0:T(1,128)S(1)} %add_add_fusion.1.refs_3_), channel_id=1, source_target_pairs={{0,13},{1,12},{2,15},{3,14},{4,9},{5,8},{6,11},{7,10},{8,5},{9,4},... | collective-permute-start | bytes 50696 | tf_op jit(solution)/shard_map/ppermute | solution.py:313
  25.4 4.1 %collective-permute-start.6 = (f32[1,4224]{1,0:T(1,128)S(1)}, f32[1,4224]{1,0:T(1,128)S(1)}, u32[]{:S(2)}, u32[]{:S(2)}) collective-permute-start(f32[1,4224]{1,0:T(1,128)S(1)} %add_add_fusion.1.refs_3_), channel_id=1, source_target_pairs={{0,9},{1,8},{2,11},{3,10},{4,13},{5,12},{6,15},{7,14},{8,1},{9,0},... | collective-permute-start | bytes 50696 | tf_op jit(solution)/shard_map/ppermute | solution.py:313
  25.4 4.1 %collective-permute-start.7 = (f32[1,4224]{1,0:T(1,128)S(1)}, f32[1,4224]{1,0:T(1,128)S(1)}, u32[]{:S(2)}, u32[]{:S(2)}) collective-permute-start(f32[1,4224]{1,0:T(1,128)S(1)} %add_add_fusion.1.refs_3_), channel_id=1, source_target_pairs={{0,5},{1,4},{2,7},{3,6},{4,1},{5,0},{6,3},{7,2},{8,13},{9,12},{10,... | collective-permute-start | bytes 50696 | tf_op jit(solution)/shard_map/ppermute | solution.py:313
  30.7 3.8 %collective-permute-start.8 = (f32[8,640]{1,0:T(8,128)S(1)}, f32[8,640]{1,0:T(8,128)S(1)}, u32[]{:S(2)}, u32[]{:S(2)}) collective-permute-start(f32[8,640]{1,0:T(8,128)S(1)} %get-tuple-element.35.refs_1_), channel_id=1, source_target_pairs={{0,16},{16,0},{1,17},{17,1},{2,18},{18,2},{3,19},{19,3},{4,20},{20... | collective-permute-start | bytes 61448 | tf_op jit(solution)/shard_map/ppermute | solution.py:313
  35.9 3.2 %collective-permute-start.10 = (f32[1,4224]{1,0:T(1,128)S(1)}, f32[1,4224]{1,0:T(1,128)S(1)}, u32[]{:S(2)}, u32[]{:S(2)}) collective-permute-start(f32[1,4224]{1,0:T(1,128)S(1)} %get-tuple-element.38), channel_id=1, source_target_pairs={{0,3},{1,2},{2,1},{3,0},{4,7},{5,6},{6,5},{7,4},{8,11},{9,10},{10,... | collective-permute-start | bytes 50696 | tf_op jit(solution)/shard_map/ppermute | solution.py:313
  36.4 3.7 %collective-permute-start.11 = (f32[1,4224]{1,0:T(1,128)S(1)}, f32[1,4224]{1,0:T(1,128)S(1)}, u32[]{:S(2)}, u32[]{:S(2)}) collective-permute-start(f32[1,4224]{1,0:T(1,128)S(1)} %get-tuple-element.38), channel_id=1, source_target_pairs={{0,2},{1,3},{2,0},{3,1},{4,6},{5,7},{6,4},{7,5},{8,10},{9,11},{10,... | collective-permute-start | bytes 50696 | tf_op jit(solution)/shard_map/ppermute | solution.py:313
  36.8 3.4 %collective-permute-start.9 = (f32[1,4224]{1,0:T(1,128)S(1)}, f32[1,4224]{1,0:T(1,128)S(1)}, u32[]{:S(2)}, u32[]{:S(2)}) collective-permute-start(f32[1,4224]{1,0:T(1,128)S(1)} %get-tuple-element.38), channel_id=1, source_target_pairs={{0,1},{1,0},{2,3},{3,2},{4,5},{5,4},{6,7},{7,6},{8,9},{9,8},{10,11... | collective-permute-start | bytes 50696 | tf_op jit(solution)/shard_map/ppermute | solution.py:313
  40.2 5.0 %collective-permute-start.12 = (f32[1,4224]{1,0:T(1,128)S(1)}, f32[1,4224]{1,0:T(1,128)S(1)}, u32[]{:S(2)}, u32[]{:S(2)}) collective-permute-start(f32[1,4224]{1,0:T(1,128)S(1)} %add_add_fusion.refs_3_), channel_id=1, source_target_pairs={{0,13},{1,12},{2,15},{3,14},{4,9},{5,8},{6,11},{7,10},{8,5},{9,4},... | collective-permute-start | bytes 50696 | tf_op jit(solution)/shard_map/ppermute | solution.py:313
  41.2 4.2 %collective-permute-start.13 = (f32[1,4224]{1,0:T(1,128)S(1)}, f32[1,4224]{1,0:T(1,128)S(1)}, u32[]{:S(2)}, u32[]{:S(2)}) collective-permute-start(f32[1,4224]{1,0:T(1,128)S(1)} %add_add_fusion.refs_3_), channel_id=1, source_target_pairs={{0,9},{1,8},{2,11},{3,10},{4,13},{5,12},{6,15},{7,14},{8,1},{9,0},... | collective-permute-start | bytes 50696 | tf_op jit(solution)/shard_map/ppermute | solution.py:313
  41.7 3.7 %collective-permute-start.14 = (f32[1,4224]{1,0:T(1,128)S(1)}, f32[1,4224]{1,0:T(1,128)S(1)}, u32[]{:S(2)}, u32[]{:S(2)}) collective-permute-start(f32[1,4224]{1,0:T(1,128)S(1)} %add_add_fusion.refs_3_), channel_id=1, source_target_pairs={{0,5},{1,4},{2,7},{3,6},{4,1},{5,0},{6,3},{7,2},{8,13},{9,12},{10,... | collective-permute-start | bytes 50696 | tf_op jit(solution)/shard_map/ppermute | solution.py:313
  46.7 3.8 %collective-permute-start.15 = (f32[8,640]{1,0:T(8,128)S(1)}, f32[8,640]{1,0:T(8,128)S(1)}, u32[]{:S(2)}, u32[]{:S(2)}) collective-permute-start(f32[8,640]{1,0:T(8,128)S(1)} %get-tuple-element.40.refs_1_), channel_id=1, source_target_pairs={{0,16},{16,0},{1,17},{17,1},{2,18},{18,2},{3,19},{19,3},{4,20},{20... | collective-permute-start | bytes 61448 | tf_op jit(solution)/shard_map/ppermute | solution.py:313

commit v13 on v11

--- a/solution.py
+++ b/solution.py
@@ -88,8 +88,8 @@
     return extra
 
 
-def kernel_parts(left, right):
-    value = jnp.exp2(jnp.dot(left, right, preferred_element_type=f32))
+def kernel_parts(exponent):
+    value = jnp.exp2(exponent)
     high = value.astype(bf16)
     return high, (value - high.astype(f32)).astype(bf16)
 
@@ -158,8 +158,17 @@
             block_ref[row_count + begin : row_count + end, :],
         )
 
+    def inner(begin):
+        return jnp.dot(
+            turned_ref[begin : begin + CHUNK, :], center, preferred_element_type=f32
+        )
+
+    ahead = inner(0)
     for begin in range(0, row_count, CHUNK):
-        high, low = kernel_parts(turned_ref[begin : begin + CHUNK, :], center)
+        exponent = ahead
+        if begin + CHUNK < row_count:
+            ahead = inner(begin + CHUNK)
+        high, low = kernel_parts(exponent)
         block_ref[begin : begin + CHUNK, :] = high
         block_ref[row_count + begin : row_count + begin + CHUNK, :] = low
         if begin > 0:
@@ -169,12 +178,21 @@
 
 def turned_body(columns_ref, center_ref, block_ref):
     center = center_ref[...].astype(f32).T.astype(bf16)
-    count = center.shape[0]
-    for begin in range(0, columns_ref.shape[1], CHUNK):
-        here = slice(begin, begin + CHUNK)
-        high, low = kernel_parts(center, columns_ref[:, here])
-        block_ref[0:count, here] = high
-        block_ref[count:, here] = low
+    count, row_count = center.shape[0], columns_ref.shape[1]
+
+    def inner(begin):
+        return jnp.dot(
+            center, columns_ref[:, begin : begin + CHUNK], preferred_element_type=f32
+        )
+
+    ahead = inner(0)
+    for begin in range(0, row_count, CHUNK):
+        exponent = ahead
+        if begin + CHUNK < row_count:
+            ahead = inner(begin + CHUNK)
+        high, low = kernel_parts(exponent)
+        block_ref[0:count, begin : begin + CHUNK] = high
+        block_ref[count:, begin : begin + CHUNK] = low
 
 
 def apply_rows(scaled, turned_ref, slots_ref, out_ref):

time: 49.2 us -> 49.1 us (level)
  no operation moved by 1% of the time
where the time goes in v13:
time: 49.1 us; the launch traced here: 49 us
  starting transfers between devices  19.6 us (40%)
  waiting for transfers between devices  16.1 us (33%)
  Pallas kernels  12.6 us (26%)
  between operations  0.71 us (1%)
    ppermute x16, starting transfers between devices, exchange(): parts.insert(0, lax.ppermute(value, axis, pairs))  19.6 us
    ppermute x16, waiting for transfers between devices, exchange(): parts.insert(0, lax.ppermute(value, axis, pairs))  16.1 us
    pallas_call x9, Pallas kernels, call(): pl.pallas_call(body, out_shape=out_shape, in_specs=[source] * len(args),...  12.6 us
  transfers between devices with their start and end apart: 16, of which 11 were waited for; matrix products, arithmetic and copies ran while one was open for 0% of the time, Pallas kernels for 5%

profile of v13, /device:TPU:0, one launch (start us, length us, event | category | flops | bytes accessed | tf_op | source)
XLA Modules:
  0.0 49.0 jit_solution(7239920271017509399)
XLA Ops:
  0.6 1.9 %shard_map.68 = (bf16[64,4096]{1,0:T(8,128)(2,1)S(1)}, s32[1,4096]{1,0:T(1,128)S(1)}, f32[1,4096]{1,0:T(1,128)S(1)}, f32[1,512]{1,0:T(1,128)S(1)}, bf16[64,512]{1,0:T(8,128)(2,1)S(1)}) custom-call(bf16[64,4096]{1,0:T(8,128)(2,1)} %feat_hbm.1, s32[1,512]{1,0:T(1,128)} %bitcast.6, s32[1,4096]{1,0:T(1,128)} %bitcast.4, f32[1,4096]{1,0:T(1,128)} %bitcast.5, ...), custom_call_target="tpu_custom_call" | custom-call | tf_op jit(solution)/shard_map/pallas_call | solution.py:288
  2.6 3.0 %collective-permute-start = (bf16[64,512]{1,0:T(8,128)(2,1)S(1)}, bf16[64,512]{1,0:T(8,128)(2,1)S(1)}, u32[]{:S(2)}, u32[]{:S(2)}) collective-permute-start(bf16[64,512]{1,0:T(8,128)(2,1)S(1)} %get-tuple-element.28.refs_1_), channel_id=1, source_target_pairs={{0,16},{16,0},{1,17},{17,1},{2,18},{18,2},{3,19},{19,3},{4,20},{20... | collective-permute-start | bytes 196616 | tf_op jit(solution)/shard_map/ppermute | solution.py:312
  5.6 0.7 %shard_map.69 = (bf16[256,4096]{1,0:T(8,128)(2,1)S(1)}, bf16[4096,256]{1,0:T(8,128)(2,1)S(1)}, bf16[16,4096]{1,0:T(8,128)(2,1)S(1)}) custom-call(bf16[64,4096]{1,0:T(8,128)(2,1)S(1)} %get-tuple-element.23.feat_ref, s32[1,4096]{1,0:T(1,128)S(1)} %get-tuple-element.24.slots_ref.refs_3_.refs_4_, f32[1,4096]{1,0:T(1,128)S(1)} %get-tuple-element.25.prices_ref), custom_call_target="tpu_custom_call" | custom-call | flops 4096000 | bytes 4194304 | tf_op jit(solution)/shard_map/pallas_call | solution.py:288
  6.3 1.6 %collective-permute-done.refs_0_ = bf16[64,512]{1,0:T(8,128)(2,1)S(1)} collective-permute-done((bf16[64,512]{1,0:T(8,128)(2,1)S(1)}, bf16[64,512]{1,0:T(8,128)(2,1)S(1)}, u32[]{:S(2)}, u32[]{:S(2)}) %collective-permute-start) | collective-permute-done | bytes 65568 | tf_op jit(solution)/shard_map/ppermute | solution.py:312
  7.8 2.5 %shard_map.70 = (bf16[8192,512]{1,0:T(8,128)(2,1)S(1)}, bf16[256,512]{1,0:T(8,128)(2,1)S(1)}, f32[8,512]{1,0:T(8,128)S(1)}) custom-call(bf16[4096,256]{1,0:T(8,128)(2,1)S(1)} %get-tuple-element.26.turned_ref, bf16[16,4096]{1,0:T(8,128)(2,1)S(1)} %get-tuple-element.27.weight_ref, bf16[64,512]{1,0:T(8,128)(2,1)S(1)} %collective-permute-done.refs_0_, ...), custom_call_target="tpu_custom_call" | custom-call | flops 134217728 | bytes 8388608 | tf_op jit(solution)/shard_map/pallas_call | solution.py:288
  10.4 2.1 %collective-permute-start.1 = (f32[8,512]{1,0:T(8,128)S(1)}, f32[8,512]{1,0:T(8,128)S(1)}, u32[]{:S(2)}, u32[]{:S(2)}) collective-permute-start(f32[8,512]{1,0:T(8,128)S(1)} %get-tuple-element.29.refs_1_), channel_id=1, source_target_pairs={{0,16},{16,0},{1,17},{17,1},{2,18},{18,2},{3,19},{19,3},{4,20},{20... | collective-permute-start | bytes 49160 | tf_op jit(solution)/shard_map/ppermute | solution.py:312
  12.4 1.9 %shard_map.71.refs_4_ = bf16[1024,4096]{1,0:T(8,128)(2,1)S(1)} custom-call(bf16[256,4096]{1,0:T(8,128)(2,1)S(1)} %get-tuple-element.31.columns_ref, bf16[256,512]{1,0:T(8,128)(2,1)S(1)} %get-tuple-element.32.center_ref), custom_call_target="tpu_custom_call" | custom-call | flops 134217728 | bytes 8388608 | tf_op jit(solution)/shard_map/pallas_call | solution.py:288
  14.4 0.0 collective-permute-done.1.refs_0_
  14.4 1.2 %shard_map.72 = (f32[8,512]{1,0:T(8,128)S(1)}, f32[1,4224]{1,0:T(1,128)S(1)}) custom-call(f32[8,512]{1,0:T(8,128)S(1)} %collective-permute-done.1.refs_0_, f32[8,512]{1,0:T(8,128)S(1)} %get-tuple-element.29.refs_1_, f32[1,512]{1,0:T(1,128)S(1)} %get-tuple-element.30.refs_2_, s32[1,4096]{1,0:T(1,128)S(1)} %get-tuple-element.24.slots_ref.refs_3_.refs_4_, ...), custom_call_target="tpu_custom_call" | custom-call | tf_op jit(solution)/shard_map/pallas_call | solution.py:288
  15.6 0.1 collective-permute-start.2
  15.7 1.9 %collective-permute-start.3 = (f32[1,4224]{1,0:T(1,128)S(1)}, f32[1,4224]{1,0:T(1,128)S(1)}, u32[]{:S(2)}, u32[]{:S(2)}) collective-permute-start(f32[1,4224]{1,0:T(1,128)S(1)} %get-tuple-element.33), channel_id=1, source_target_pairs={{0,2},{1,3},{2,0},{3,1},{4,6},{5,7},{6,4},{7,5},{8,10},{9,11},{10,... | collective-permute-start | bytes 50696 | tf_op jit(solution)/shard_map/ppermute | solution.py:312
  17.6 0.0 collective-permute-start.4
  17.6 1.2 %collective-permute-done.2 = f32[1,4224]{1,0:T(1,128)S(1)} collective-permute-done((f32[1,4224]{1,0:T(1,128)S(1)}, f32[1,4224]{1,0:T(1,128)S(1)}, u32[]{:S(2)}, u32[]{:S(2)}) %collective-permute-start.2) | collective-permute-done | bytes 16928 | tf_op jit(solution)/shard_map/ppermute | solution.py:312
  18.8 0.7 %collective-permute-done.3 = f32[1,4224]{1,0:T(1,128)S(1)} collective-permute-done((f32[1,4224]{1,0:T(1,128)S(1)}, f32[1,4224]{1,0:T(1,128)S(1)}, u32[]{:S(2)}, u32[]{:S(2)}) %collective-permute-start.3) | collective-permute-done | bytes 16928 | tf_op jit(solution)/shard_map/ppermute | solution.py:312
  19.5 0.0 collective-permute-done.4
  19.5 4.0 %collective-permute-start.5 = (f32[1,4224]{1,0:T(1,128)S(1)}, f32[1,4224]{1,0:T(1,128)S(1)}, u32[]{:S(2)}, u32[]{:S(2)}) collective-permute-start(f32[1,4224]{1,0:T(1,128)S(1)} %add_add_fusion.1.refs_3_), channel_id=1, source_target_pairs={{0,13},{1,12},{2,15},{3,14},{4,9},{5,8},{6,11},{7,10},{8,5},{9,4},... | collective-permute-start | bytes 50696 | tf_op jit(solution)/shard_map/ppermute | solution.py:312
  23.5 0.0 collective-permute-start.6
  23.5 0.5 %collective-permute-start.7 = (f32[1,4224]{1,0:T(1,128)S(1)}, f32[1,4224]{1,0:T(1,128)S(1)}, u32[]{:S(2)}, u32[]{:S(2)}) collective-permute-start(f32[1,4224]{1,0:T(1,128)S(1)} %add_add_fusion.1.refs_3_), channel_id=1, source_target_pairs={{0,5},{1,4},{2,7},{3,6},{4,1},{5,0},{6,3},{7,2},{8,13},{9,12},{10,... | collective-permute-start | bytes 50696 | tf_op jit(solution)/shard_map/ppermute | solution.py:312
  24.0 1.0 %collective-permute-done.5.refs_0_ = f32[1,4224]{1,0:T(1,128)S(1)} collective-permute-done((f32[1,4224]{1,0:T(1,128)S(1)}, f32[1,4224]{1,0:T(1,128)S(1)}, u32[]{:S(2)}, u32[]{:S(2)}) %collective-permute-start.5) | collective-permute-done | bytes 16928 | tf_op jit(solution)/shard_map/ppermute | solution.py:312
  25.0 2.6 %collective-permute-done.6.refs_1_ = f32[1,4224]{1,0:T(1,128)S(1)} collective-permute-done((f32[1,4224]{1,0:T(1,128)S(1)}, f32[1,4224]{1,0:T(1,128)S(1)}, u32[]{:S(2)}, u32[]{:S(2)}) %collective-permute-start.6) | collective-permute-done | bytes 16928 | tf_op jit(solution)/shard_map/ppermute | solution.py:312
  27.6 0.0 collective-permute-done.7.refs_2_
  27.6 1.2 %shard_map.73 = (f32[1,4224]{1,0:T(1,128)S(1)}, f32[8,128]{1,0:T(8,128)S(1)}, f32[8,640]{1,0:T(8,128)S(1)}) custom-call(f32[1,4224]{1,0:T(1,128)S(1)} %collective-permute-done.5.refs_0_, f32[1,4224]{1,0:T(1,128)S(1)} %collective-permute-done.6.refs_1_, f32[1,4224]{1,0:T(1,128)S(1)} %collective-permute-done.7.refs_2_, f32[1,4224]{1,0:T(1,128)S(1)} %add_add_fusion.1.refs_3_, ...), custom_call_target="tpu_custom_call" | custom-call | tf_op jit(solution)/shard_map/pallas_call | solution.py:288
  28.8 1.5 %collective-permute-start.8 = (f32[8,640]{1,0:T(8,128)S(1)}, f32[8,640]{1,0:T(8,128)S(1)}, u32[]{:S(2)}, u32[]{:S(2)}) collective-permute-start(f32[8,640]{1,0:T(8,128)S(1)} %get-tuple-element.35.refs_1_), channel_id=1, source_target_pairs={{0,16},{16,0},{1,17},{17,1},{2,18},{18,2},{3,19},{19,3},{4,20},{20... | collective-permute-start | bytes 61448 | tf_op jit(solution)/shard_map/ppermute | solution.py:312
  30.3 2.3 %collective-permute-done.8.refs_0_ = f32[8,640]{1,0:T(8,128)S(1)} collective-permute-done((f32[8,640]{1,0:T(8,128)S(1)}, f32[8,640]{1,0:T(8,128)S(1)}, u32[]{:S(2)}, u32[]{:S(2)}) %collective-permute-start.8) | collective-permute-done | bytes 20512 | tf_op jit(solution)/shard_map/ppermute | solution.py:312
  32.6 1.2 %shard_map.74 = (f32[8,512]{1,0:T(8,128)S(1)}, f32[8,128]{1,0:T(8,128)S(1)}, f32[1,4224]{1,0:T(1,128)S(1)}) custom-call(f32[8,640]{1,0:T(8,128)S(1)} %collective-permute-done.8.refs_0_, f32[8,640]{1,0:T(8,128)S(1)} %get-tuple-element.35.refs_1_, f32[1,512]{1,0:T(1,128)S(1)} %get-tuple-element.30.refs_2_, ...), custom_call_target="tpu_custom_call" | custom-call | tf_op jit(solution)/shard_map/pallas_call | solution.py:288
  33.8 0.5 collective-permute-start.10
  34.3 0.4 collective-permute-start.11
  34.6 1.1 %collective-permute-start.9 = (f32[1,4224]{1,0:T(1,128)S(1)}, f32[1,4224]{1,0:T(1,128)S(1)}, u32[]{:S(2)}, u32[]{:S(2)}) collective-permute-start(f32[1,4224]{1,0:T(1,128)S(1)} %get-tuple-element.38), channel_id=1, source_target_pairs={{0,1},{1,0},{2,3},{3,2},{4,5},{5,4},{6,7},{7,6},{8,9},{9,8},{10,11... | collective-permute-start | bytes 50696 | tf_op jit(solution)/shard_map/ppermute | solution.py:312
  35.7 1.3 %collective-permute-done.10 = f32[1,4224]{1,0:T(1,128)S(1)} collective-permute-done((f32[1,4224]{1,0:T(1,128)S(1)}, f32[1,4224]{1,0:T(1,128)S(1)}, u32[]{:S(2)}, u32[]{:S(2)}) %collective-permute-start.10) | collective-permute-done | bytes 16928 | tf_op jit(solution)/shard_map/ppermute | solution.py:312
  37.0 1.0 %collective-permute-done.11 = f32[1,4224]{1,0:T(1,128)S(1)} collective-permute-done((f32[1,4224]{1,0:T(1,128)S(1)}, f32[1,4224]{1,0:T(1,128)S(1)}, u32[]{:S(2)}, u32[]{:S(2)}) %collective-permute-start.11) | collective-permute-done | bytes 16928 | tf_op jit(solution)/shard_map/ppermute | solution.py:312
  38.0 0.0 collective-permute-done.9
  38.1 1.1 %collective-permute-start.12 = (f32[1,4224]{1,0:T(1,128)S(1)}, f32[1,4224]{1,0:T(1,128)S(1)}, u32[]{:S(2)}, u32[]{:S(2)}) collective-permute-start(f32[1,4224]{1,0:T(1,128)S(1)} %add_add_fusion.refs_3_), channel_id=1, source_target_pairs={{0,13},{1,12},{2,15},{3,14},{4,9},{5,8},{6,11},{7,10},{8,5},{9,4},... | collective-permute-start | bytes 50696 | tf_op jit(solution)/shard_map/ppermute | solution.py:312
  39.1 0.5 %collective-permute-start.13 = (f32[1,4224]{1,0:T(1,128)S(1)}, f32[1,4224]{1,0:T(1,128)S(1)}, u32[]{:S(2)}, u32[]{:S(2)}) collective-permute-start(f32[1,4224]{1,0:T(1,128)S(1)} %add_add_fusion.refs_3_), channel_id=1, source_target_pairs={{0,9},{1,8},{2,11},{3,10},{4,13},{5,12},{6,15},{7,14},{8,1},{9,0},... | collective-permute-start | bytes 50696 | tf_op jit(solution)/shard_map/ppermute | solution.py:312
  39.6 1.5 %collective-permute-start.14 = (f32[1,4224]{1,0:T(1,128)S(1)}, f32[1,4224]{1,0:T(1,128)S(1)}, u32[]{:S(2)}, u32[]{:S(2)}) collective-permute-start(f32[1,4224]{1,0:T(1,128)S(1)} %add_add_fusion.refs_3_), channel_id=1, source_target_pairs={{0,5},{1,4},{2,7},{3,6},{4,1},{5,0},{6,3},{7,2},{8,13},{9,12},{10,... | collective-permute-start | bytes 50696 | tf_op jit(solution)/shard_map/ppermute | solution.py:312
  41.1 2.0 %collective-permute-done.12.refs_0_ = f32[1,4224]{1,0:T(1,128)S(1)} collective-permute-done((f32[1,4224]{1,0:T(1,128)S(1)}, f32[1,4224]{1,0:T(1,128)S(1)}, u32[]{:S(2)}, u32[]{:S(2)}) %collective-permute-start.12) | collective-permute-done | bytes 16928 | tf_op jit(solution)/shard_map/ppermute | solution.py:312
  43.1 0.2 collective-permute-done.13.refs_1_
  43.3 0.0 collective-permute-done.14.refs_2_
  43.3 1.3 %shard_map.75 = (f32[8,256]{1,0:T(8,128)S(1)}, f32[8,640]{1,0:T(8,128)S(1)}) custom-call(f32[1,4224]{1,0:T(1,128)S(1)} %collective-permute-done.12.refs_0_, f32[1,4224]{1,0:T(1,128)S(1)} %collective-permute-done.13.refs_1_, f32[1,4224]{1,0:T(1,128)S(1)} %collective-permute-done.14.refs_2_, f32[1,4224]{1,0:T(1,128)S(1)} %add_add_fusion.refs_3_, ...), custom_call_target="tpu_custom_call" | custom-call | tf_op jit(solution)/shard_map/pallas_call | solution.py:288
  44.5 1.5 %collective-permute-start.15 = (f32[8,640]{1,0:T(8,128)S(1)}, f32[8,640]{1,0:T(8,128)S(1)}, u32[]{:S(2)}, u32[]{:S(2)}) collective-permute-start(f32[8,640]{1,0:T(8,128)S(1)} %get-tuple-element.40.refs_1_), channel_id=1, source_target_pairs={{0,16},{16,0},{1,17},{17,1},{2,18},{18,2},{3,19},{19,3},{4,20},{20... | collective-permute-start | bytes 61448 | tf_op jit(solution)/shard_map/ppermute | solution.py:312
  46.1 2.3 %collective-permute-done.15.refs_0_ = f32[8,640]{1,0:T(8,128)S(1)} collective-permute-done((f32[8,640]{1,0:T(8,128)S(1)}, f32[8,640]{1,0:T(8,128)S(1)}, u32[]{:S(2)}, u32[]{:S(2)}) %collective-permute-start.15) | collective-permute-done | bytes 20512 | tf_op jit(solution)/shard_map/ppermute | solution.py:312
  48.3 0.6 %shard_map.76 = (f32[8,512]{1,0:T(8,128)}, f32[8,512]{1,0:T(8,128)}) custom-call(f32[8,640]{1,0:T(8,128)S(1)} %collective-permute-done.15.refs_0_, f32[8,640]{1,0:T(8,128)S(1)} %get-tuple-element.40.refs_1_, f32[1,512]{1,0:T(1,128)S(1)} %get-tuple-element.30.refs_2_, f32[8,512]{1,0:T(8,128)S(1)} %get-tuple-element.36.refs_5_.refs_3_, ...), custom_call_target="tpu_custom_call" | custom-call | tf_op jit(solution)/shard_map/pallas_call | solution.py:288
  (2 shorter events, 0.1 us)
Async XLA Ops:
  2.6 5.2 %collective-permute-start = (bf16[64,512]{1,0:T(8,128)(2,1)S(1)}, bf16[64,512]{1,0:T(8,128)(2,1)S(1)}, u32[]{:S(2)}, u32[]{:S(2)}) collective-permute-start(bf16[64,512]{1,0:T(8,128)(2,1)S(1)} %get-tuple-element.28.refs_1_), channel_id=1, source_target_pairs={{0,16},{16,0},{1,17},{17,1},{2,18},{18,2},{3,19},{19,3},{4,20},{20... | collective-permute-start | bytes 196616 | tf_op jit(solution)/shard_map/ppermute | solution.py:312
  10.4 4.0 %collective-permute-start.1 = (f32[8,512]{1,0:T(8,128)S(1)}, f32[8,512]{1,0:T(8,128)S(1)}, u32[]{:S(2)}, u32[]{:S(2)}) collective-permute-start(f32[8,512]{1,0:T(8,128)S(1)} %get-tuple-element.29.refs_1_), channel_id=1, source_target_pairs={{0,16},{16,0},{1,17},{17,1},{2,18},{18,2},{3,19},{19,3},{4,20},{20... | collective-permute-start | bytes 49160 | tf_op jit(solution)/shard_map/ppermute | solution.py:312
  15.6 3.2 %collective-permute-start.2 = (f32[1,4224]{1,0:T(1,128)S(1)}, f32[1,4224]{1,0:T(1,128)S(1)}, u32[]{:S(2)}, u32[]{:S(2)}) collective-permute-start(f32[1,4224]{1,0:T(1,128)S(1)} %get-tuple-element.33), channel_id=1, source_target_pairs={{0,3},{1,2},{2,1},{3,0},{4,7},{5,6},{6,5},{7,4},{8,11},{9,10},{10,... | collective-permute-start | bytes 50696 | tf_op jit(solution)/shard_map/ppermute | solution.py:312
  15.7 3.8 %collective-permute-start.3 = (f32[1,4224]{1,0:T(1,128)S(1)}, f32[1,4224]{1,0:T(1,128)S(1)}, u32[]{:S(2)}, u32[]{:S(2)}) collective-permute-start(f32[1,4224]{1,0:T(1,128)S(1)} %get-tuple-element.33), channel_id=1, source_target_pairs={{0,2},{1,3},{2,0},{3,1},{4,6},{5,7},{6,4},{7,5},{8,10},{9,11},{10,... | collective-permute-start | bytes 50696 | tf_op jit(solution)/shard_map/ppermute | solution.py:312
  17.6 1.9 %collective-permute-start.4 = (f32[1,4224]{1,0:T(1,128)S(1)}, f32[1,4224]{1,0:T(1,128)S(1)}, u32[]{:S(2)}, u32[]{:S(2)}) collective-permute-start(f32[1,4224]{1,0:T(1,128)S(1)} %get-tuple-element.33), channel_id=1, source_target_pairs={{0,1},{1,0},{2,3},{3,2},{4,5},{5,4},{6,7},{7,6},{8,9},{9,8},{10,11... | collective-permute-start | bytes 50696 | tf_op jit(solution)/shard_map/ppermute | solution.py:312
  19.5 5.5 %collective-permute-start.5 = (f32[1,4224]{1,0:T(1,128)S(1)}, f32[1,4224]{1,0:T(1,128)S(1)}, u32[]{:S(2)}, u32[]{:S(2)}) collective-permute-start(f32[1,4224]{1,0:T(1,128)S(1)} %add_add_fusion.1.refs_3_), channel_id=1, source_target_pairs={{0,13},{1,12},{2,15},{3,14},{4,9},{5,8},{6,11},{7,10},{8,5},{9,4},... | collective-permute-start | bytes 50696 | tf_op jit(solution)/shard_map/ppermute | solution.py:312
  23.5 4.1 %collective-permute-start.6 = (f32[1,4224]{1,0:T(1,128)S(1)}, f32[1,4224]{1,0:T(1,128)S(1)}, u32[]{:S(2)}, u32[]{:S(2)}) collective-permute-start(f32[1,4224]{1,0:T(1,128)S(1)} %add_add_fusion.1.refs_3_), channel_id=1, source_target_pairs={{0,9},{1,8},{2,11},{3,10},{4,13},{5,12},{6,15},{7,14},{8,1},{9,0},... | collective-permute-start | bytes 50696 | tf_op jit(solution)/shard_map/ppermute | solution.py:312
  23.5 4.1 %collective-permute-start.7 = (f32[1,4224]{1,0:T(1,128)S(1)}, f32[1,4224]{1,0:T(1,128)S(1)}, u32[]{:S(2)}, u32[]{:S(2)}) collective-permute-start(f32[1,4224]{1,0:T(1,128)S(1)} %add_add_fusion.1.refs_3_), channel_id=1, source_target_pairs={{0,5},{1,4},{2,7},{3,6},{4,1},{5,0},{6,3},{7,2},{8,13},{9,12},{10,... | collective-permute-start | bytes 50696 | tf_op jit(solution)/shard_map/ppermute | solution.py:312
  28.8 3.8 %collective-permute-start.8 = (f32[8,640]{1,0:T(8,128)S(1)}, f32[8,640]{1,0:T(8,128)S(1)}, u32[]{:S(2)}, u32[]{:S(2)}) collective-permute-start(f32[8,640]{1,0:T(8,128)S(1)} %get-tuple-element.35.refs_1_), channel_id=1, source_target_pairs={{0,16},{16,0},{1,17},{17,1},{2,18},{18,2},{3,19},{19,3},{4,20},{20... | collective-permute-start | bytes 61448 | tf_op jit(solution)/shard_map/ppermute | solution.py:312
  33.8 3.2 %collective-permute-start.10 = (f32[1,4224]{1,0:T(1,128)S(1)}, f32[1,4224]{1,0:T(1,128)S(1)}, u32[]{:S(2)}, u32[]{:S(2)}) collective-permute-start(f32[1,4224]{1,0:T(1,128)S(1)} %get-tuple-element.38), channel_id=1, source_target_pairs={{0,3},{1,2},{2,1},{3,0},{4,7},{5,6},{6,5},{7,4},{8,11},{9,10},{10,... | collective-permute-start | bytes 50696 | tf_op jit(solution)/shard_map/ppermute | solution.py:312
  34.3 3.7 %collective-permute-start.11 = (f32[1,4224]{1,0:T(1,128)S(1)}, f32[1,4224]{1,0:T(1,128)S(1)}, u32[]{:S(2)}, u32[]{:S(2)}) collective-permute-start(f32[1,4224]{1,0:T(1,128)S(1)} %get-tuple-element.38), channel_id=1, source_target_pairs={{0,2},{1,3},{2,0},{3,1},{4,6},{5,7},{6,4},{7,5},{8,10},{9,11},{10,... | collective-permute-start | bytes 50696 | tf_op jit(solution)/shard_map/ppermute | solution.py:312
  34.6 3.4 %collective-permute-start.9 = (f32[1,4224]{1,0:T(1,128)S(1)}, f32[1,4224]{1,0:T(1,128)S(1)}, u32[]{:S(2)}, u32[]{:S(2)}) collective-permute-start(f32[1,4224]{1,0:T(1,128)S(1)} %get-tuple-element.38), channel_id=1, source_target_pairs={{0,1},{1,0},{2,3},{3,2},{4,5},{5,4},{6,7},{7,6},{8,9},{9,8},{10,11... | collective-permute-start | bytes 50696 | tf_op jit(solution)/shard_map/ppermute | solution.py:312
  38.1 5.0 %collective-permute-start.12 = (f32[1,4224]{1,0:T(1,128)S(1)}, f32[1,4224]{1,0:T(1,128)S(1)}, u32[]{:S(2)}, u32[]{:S(2)}) collective-permute-start(f32[1,4224]{1,0:T(1,128)S(1)} %add_add_fusion.refs_3_), channel_id=1, source_target_pairs={{0,13},{1,12},{2,15},{3,14},{4,9},{5,8},{6,11},{7,10},{8,5},{9,4},... | collective-permute-start | bytes 50696 | tf_op jit(solution)/shard_map/ppermute | solution.py:312
  39.1 4.2 %collective-permute-start.13 = (f32[1,4224]{1,0:T(1,128)S(1)}, f32[1,4224]{1,0:T(1,128)S(1)}, u32[]{:S(2)}, u32[]{:S(2)}) collective-permute-start(f32[1,4224]{1,0:T(1,128)S(1)} %add_add_fusion.refs_3_), channel_id=1, source_target_pairs={{0,9},{1,8},{2,11},{3,10},{4,13},{5,12},{6,15},{7,14},{8,1},{9,0},... | collective-permute-start | bytes 50696 | tf_op jit(solution)/shard_map/ppermute | solution.py:312
  39.6 3.7 %collective-permute-start.14 = (f32[1,4224]{1,0:T(1,128)S(1)}, f32[1,4224]{1,0:T(1,128)S(1)}, u32[]{:S(2)}, u32[]{:S(2)}) collective-permute-start(f32[1,4224]{1,0:T(1,128)S(1)} %add_add_fusion.refs_3_), channel_id=1, source_target_pairs={{0,5},{1,4},{2,7},{3,6},{4,1},{5,0},{6,3},{7,2},{8,13},{9,12},{10,... | collective-permute-start | bytes 50696 | tf_op jit(solution)/shard_map/ppermute | solution.py:312
  44.5 3.8 %collective-permute-start.15 = (f32[8,640]{1,0:T(8,128)S(1)}, f32[8,640]{1,0:T(8,128)S(1)}, u32[]{:S(2)}, u32[]{:S(2)}) collective-permute-start(f32[8,640]{1,0:T(8,128)S(1)} %get-tuple-element.40.refs_1_), channel_id=1, source_target_pairs={{0,16},{16,0},{1,17},{17,1},{2,18},{18,2},{3,19},{19,3},{4,20},{20... | collective-permute-start | bytes 61448 | tf_op jit(solution)/shard_map/ppermute | solution.py:312

commit v14 on v13

--- a/solution.py
+++ b/solution.py
@@ -235,7 +235,7 @@
 def second_apply_body(parts, inv_rows, *refs):
     fold_refs = refs[:parts]
     (scale_ref, slots_ref, turned_ref, target_ref, norm_ref,
-     residual_ref, step_ref, out_ref) = refs[parts:]
+     state_ref, step_ref, out_ref) = refs[parts:]
     row_count, count = turned_ref.shape[1], scale_ref.shape[1]
     folded = total_of(fold_refs)
     scale = scale_ref[...]
@@ -244,7 +244,8 @@
     applied = scale * folded[:, 0:count] * inv_rows + RIDGE * target
     step = norm / (folded[:, count:] * inv_rows + RIDGE * norm)
     residual = target - wide(step, count) * applied
-    residual_ref[...] = residual
+    state_ref[0:SLOTS, :] = target
+    state_ref[SLOTS:, :] = residual
     step_ref[...] = step
     out_ref[:, row_count:] = to_lanes(row_sum(residual * residual), 0) + to_lanes(
         row_sum(residual * target), SLOTS
@@ -267,12 +268,11 @@
 
 def finish_body(parts, inv_rows, *refs):
     fold_refs = refs[:parts]
-    (scale_ref, target_ref, residual_ref, step_ref, norm_ref, sums_ref,
+    (scale_ref, state_ref, step_ref, norm_ref, sums_ref,
      coefficients_ref, out_ref) = refs[parts:]
     count = scale_ref.shape[1]
     folded = total_of(fold_refs)
-    target = target_ref[...]
-    residual = residual_ref[...]
+    target, residual = state_ref[0:SLOTS, :], state_ref[SLOTS:, :]
     first_norm = norm_ref[...]
     norm, cross = sums_ref[:, 0:EXTRA], sums_ref[:, EXTRA:]
     ratio = norm / first_norm
@@ -284,11 +284,11 @@
     out_ref[...] = residual - step * applied
 
 
-def call(body, out_shape, *args, source=VMEM, flops=0, bytes_accessed=0, **more):
+def call(body, out_shape, *args, sources=None, flops=0, bytes_accessed=0, **more):
     return pl.pallas_call(
         body,
         out_shape=out_shape,
-        in_specs=[source] * len(args),
+        in_specs=sources or [VMEM] * len(args),
         out_specs=jax.tree.map(lambda _: VMEM, out_shape),
         compiler_params=pltpu.CompilerParams(vmem_limit_bytes=36 * 1024 * 1024),
         cost_estimate=pl.CostEstimate(
@@ -298,7 +298,7 @@
     )(*args)
 
 
-def exchange(value, axis, near_first=False):
+def exchange(value, axis):
     size = lax.axis_size(axis)
     parts = [value]
     stride = 1
@@ -310,10 +310,38 @@
         for offset in range(1, span):
             pairs = [(i, i ^ (offset * stride) ^ side) for i in range(size)]
             parts.insert(0, lax.ppermute(value, axis, pairs))
-        if near_first and stride == 1:
-            parts = parts[-2:] + parts[:-2]
         stride *= span
     return parts
+
+
+def pairs_over(target_of):
+    groups, count = lax.axis_size("dp"), lax.axis_size("centers")
+    pairs = []
+    for group in range(groups):
+        for place in range(count):
+            to_group, to_place = target_of(group, place)
+            pairs.append((group * count + place, to_group * count + to_place))
+    return pairs
+
+
+def moved(value, target_of):
+    return lax.ppermute(value, ("dp", "centers"), pairs_over(target_of))
+
+
+def across(group, place):
+    return 1 - group, place ^ 1
+
+
+def beside(group, place):
+    return group, place ^ group
+
+
+def outward(group, place):
+    return 1 - group, place ^ (1 - group)
+
+
+def homeward(group, place):
+    return 1 - group, place ^ group
 
 
 def shaped(shape, dtype=f32):
@@ -329,6 +357,14 @@
     vector = shaped((SLOTS, count))
     narrow = shaped((SLOTS, EXTRA))
     pass_cost = dict(flops=64 * row_count * count, bytes_accessed=4 * row_count * count)
+
+    crossed = lax.axis_size("dp") == 2
+
+    def in_place(value):
+        return moved(value, beside) if crossed else value
+
+    def share(value):
+        return [moved(value, across), value] if crossed else exchange(value, "dp")
 
     inputs = [
         pltpu.with_memory_space_constraint(array, pltpu.HBM)
@@ -340,7 +376,7 @@
             center_scale.reshape(1, count),
         )
     ]
-    features, slots, prices, scale, picked = call(
+    features, slots, prices, own_scale, picked = call(
         pick_body,
         (
             shaped(features.shape, bf16),
@@ -350,14 +386,18 @@
             shaped((depth, count), bf16),
         ),
         *inputs,
-        source=HBM,
+        sources=[HBM] * 5,
         scratch_shapes=[
             pltpu.VMEM((1, count), jnp.int32),
             pltpu.VMEM((row_count, count), bf16),
             pltpu.SemaphoreType.DMA((5,)),
         ],
     )
-    centers = exchange(picked, "dp")
+    if crossed:
+        centers = [moved(picked, outward), moved(picked, beside)]
+    else:
+        centers = exchange(picked, "dp")
+    scale = in_place(own_scale)
     columns, turned_columns, weight = call(
         columns_body,
         (
@@ -375,7 +415,7 @@
         turned_columns, weight, *centers,
         **pass_cost,
     )
-    firsts = exchange(first, "dp")
+    firsts = share(first)
     turned = call(
         turned_body, shaped((2 * count, row_count), bf16), columns, center, **pass_cost
     )
@@ -388,23 +428,26 @@
     rows, norm, folded = call(
         partial(first_fold_body, len(rows)), (row_shape, narrow, fold_shape), *rows, slots, block
     )
-    folds = exchange(folded, "dp")
-    residual, step, latest = call(
+    folds = share(folded)
+    state, step, latest = call(
         partial(second_apply_body, len(folds), 1.0 / all_rows),
-        (vector, narrow, row_shape),
+        (shaped((2 * SLOTS, count)), narrow, row_shape),
         *folds, scale, slots, turned, target, norm,
     )
-    latest = exchange(latest, "centers", True)
+    latest = exchange(latest, "centers")
     sums, folded = call(
         partial(second_fold_body, len(latest)),
         (shaped((SLOTS, 2 * EXTRA)), fold_shape),
         *latest, slots, block, rows, norm,
     )
-    folds = exchange(folded, "dp")
+    if crossed:
+        folds = [moved(folded, homeward), moved(folded, beside)]
+    else:
+        folds = exchange(folded, "dp")
     return call(
         partial(finish_body, len(folds), 1.0 / all_rows),
         (vector, vector),
-        *folds, scale, target, residual, step, norm, sums,
+        *folds, own_scale, in_place(state), step, norm, sums,
     )
 
 

time: 49.1 us -> 50.4 us (1.026)
  starting transfers between devices: 19.6 us -> 24.1 us
  waiting for transfers between devices: 16.1 us -> 12.8 us
    ppermute x0 -> x8, starting transfers between devices: none -> 12.6 us  [moved(): return lax.ppermute(value, ('dp', 'centers'), pairs_over(target_of))]
    ppermute x16 -> x12, starting transfers between devices: 19.6 us -> 11.5 us  [exchange(): parts.insert(0, lax.ppermute(value, axis, pairs))]
    ppermute x16 -> x12, waiting for transfers between devices: 16.1 us -> 8.98 us  [exchange(): parts.insert(0, lax.ppermute(value, axis, pairs))]
    ppermute x0 -> x8, waiting for transfers between devices: none -> 3.78 us  [moved(): return lax.ppermute(value, ('dp', 'centers'), pairs_over(target_of))]
  transfers between devices with their start and end apart: 16 -> 20, of which waited for: 11 -> 10; matrix products, arithmetic and copies ran while one was open for 0% -> 0% of each run, Pallas kernels for 5% -> 8%
where the time goes in v14:
time: 50.4 us; the launch traced here: 50.2 us
  starting transfers between devices  24.1 us (48%)
  waiting for transfers between devices  12.8 us (25%)
  Pallas kernels  12.6 us (25%)
  between operations  0.75 us (1%)
    ppermute x8, starting transfers between devices, moved(): return lax.ppermute(value, ('dp', 'centers'), pairs_over(target_of))  12.6 us
    pallas_call x9, Pallas kernels, call(): pl.pallas_call(body, out_shape=out_shape, in_specs=sources or [VMEM] * le...  12.6 us
    ppermute x12, starting transfers between devices, exchange(): parts.insert(0, lax.ppermute(value, axis, pairs))  11.5 us
    ppermute x12, waiting for transfers between devices, exchange(): parts.insert(0, lax.ppermute(value, axis, pairs))  8.98 us
    ppermute x8, waiting for transfers between devices, moved(): return lax.ppermute(value, ('dp', 'centers'), pairs_over(target_of))  3.78 us
  transfers between devices with their start and end apart: 20, of which 10 were waited for; matrix products, arithmetic and copies ran while one was open for 0% of the time, Pallas kernels for 8%

profile of v14, /device:TPU:0, one launch (start us, length us, event | category | flops | bytes accessed | tf_op | source)
XLA Modules:
  0.0 50.2 jit_solution(10632459929817435394)
XLA Ops:
  0.6 1.9 %shard_map.68 = (bf16[64,4096]{1,0:T(8,128)(2,1)S(1)}, s32[1,4096]{1,0:T(1,128)S(1)}, f32[1,4096]{1,0:T(1,128)S(1)}, f32[1,512]{1,0:T(1,128)S(1)}, bf16[64,512]{1,0:T(8,128)(2,1)S(1)}) custom-call(bf16[64,4096]{1,0:T(8,128)(2,1)} %feat_hbm.1, s32[1,512]{1,0:T(1,128)} %bitcast.6, s32[1,4096]{1,0:T(1,128)} %bitcast.4, f32[1,4096]{1,0:T(1,128)} %bitcast.5, ...), custom_call_target="tpu_custom_call" | custom-call | tf_op jit(solution)/shard_map/pallas_call | solution.py:288
  2.6 2.4 %collective-permute-start = (bf16[64,512]{1,0:T(8,128)(2,1)S(1)}, bf16[64,512]{1,0:T(8,128)(2,1)S(1)}, u32[]{:S(2)}, u32[]{:S(2)}) collective-permute-start(bf16[64,512]{1,0:T(8,128)(2,1)S(1)} %get-tuple-element.28), channel_id=1, source_target_pairs={{0,17},{1,16},{2,19},{3,18},{4,21},{5,20},{6,23},{7,22},{8,25},{9,... | collective-permute-start | bytes 196616 | tf_op jit(solution)/shard_map/ppermute | solution.py:328
  5.0 0.7 %collective-permute-start.1 = (bf16[64,512]{1,0:T(8,128)(2,1)S(1)}, bf16[64,512]{1,0:T(8,128)(2,1)S(1)}, u32[]{:S(2)}, u32[]{:S(2)}) collective-permute-start(bf16[64,512]{1,0:T(8,128)(2,1)S(1)} %get-tuple-element.28), channel_id=1, source_target_pairs={{0,0},{1,1},{2,2},{3,3},{4,4},{5,5},{6,6},{7,7},{8,8},{9,9},{10,10... | collective-permute-start | bytes 196616 | tf_op jit(solution)/shard_map/ppermute | solution.py:328
  5.7 0.7 %shard_map.69 = (bf16[256,4096]{1,0:T(8,128)(2,1)S(1)}, bf16[4096,256]{1,0:T(8,128)(2,1)S(1)}, bf16[16,4096]{1,0:T(8,128)(2,1)S(1)}) custom-call(bf16[64,4096]{1,0:T(8,128)(2,1)S(1)} %get-tuple-element.23.feat_ref, s32[1,4096]{1,0:T(1,128)S(1)} %get-tuple-element.24.slots_ref.refs_3_.refs_4_, f32[1,4096]{1,0:T(1,128)S(1)} %get-tuple-element.25.prices_ref), custom_call_target="tpu_custom_call" | custom-call | flops 4096000 | bytes 4194304 | tf_op jit(solution)/shard_map/pallas_call | solution.py:288
  6.3 1.5 %collective-permute-done.refs_0_ = bf16[64,512]{1,0:T(8,128)(2,1)S(1)} collective-permute-done((bf16[64,512]{1,0:T(8,128)(2,1)S(1)}, bf16[64,512]{1,0:T(8,128)(2,1)S(1)}, u32[]{:S(2)}, u32[]{:S(2)}) %collective-permute-start) | collective-permute-done | bytes 65568 | tf_op jit(solution)/shard_map/ppermute | solution.py:328
  7.8 0.0 collective-permute-done.1.refs_1_
  7.8 2.5 %shard_map.70 = (bf16[8192,512]{1,0:T(8,128)(2,1)S(1)}, bf16[256,512]{1,0:T(8,128)(2,1)S(1)}, f32[8,512]{1,0:T(8,128)S(1)}) custom-call(bf16[4096,256]{1,0:T(8,128)(2,1)S(1)} %get-tuple-element.26.turned_ref, bf16[16,4096]{1,0:T(8,128)(2,1)S(1)} %get-tuple-element.27.weight_ref, bf16[64,512]{1,0:T(8,128)(2,1)S(1)} %collective-permute-done.refs_0_, ...), custom_call_target="tpu_custom_call" | custom-call | flops 134217728 | bytes 8388608 | tf_op jit(solution)/shard_map/pallas_call | solution.py:288
  10.4 1.9 %collective-permute-start.2 = (f32[8,512]{1,0:T(8,128)S(1)}, f32[8,512]{1,0:T(8,128)S(1)}, u32[]{:S(2)}, u32[]{:S(2)}) collective-permute-start(f32[8,512]{1,0:T(8,128)S(1)} %get-tuple-element.29.refs_1_), channel_id=1, source_target_pairs={{0,17},{1,16},{2,19},{3,18},{4,21},{5,20},{6,23},{7,22},{8,25},{9,... | collective-permute-start | bytes 49160 | tf_op jit(solution)/shard_map/ppermute | solution.py:328
  12.3 0.6 %collective-permute-start.3 = (f32[1,512]{1,0:T(1,128)S(1)}, f32[1,512]{1,0:T(1,128)S(1)}, u32[]{:S(2)}, u32[]{:S(2)}) collective-permute-start(f32[1,512]{1,0:T(1,128)S(1)} %get-tuple-element.30.refs_2_), channel_id=1, source_target_pairs={{0,0},{1,1},{2,2},{3,3},{4,4},{5,5},{6,6},{7,7},{8,8},{9,9},{10,10... | collective-permute-start | bytes 6152 | tf_op jit(solution)/shard_map/ppermute | solution.py:328
  12.9 1.9 %shard_map.71.refs_4_ = bf16[1024,4096]{1,0:T(8,128)(2,1)S(1)} custom-call(bf16[256,4096]{1,0:T(8,128)(2,1)S(1)} %get-tuple-element.31.columns_ref, bf16[256,512]{1,0:T(8,128)(2,1)S(1)} %get-tuple-element.32.center_ref), custom_call_target="tpu_custom_call" | custom-call | flops 134217728 | bytes 8388608 | tf_op jit(solution)/shard_map/pallas_call | solution.py:288
  14.8 0.0 collective-permute-done.3.refs_2_
  14.9 0.0 collective-permute-done.2.refs_0_
  14.9 1.2 %shard_map.72 = (f32[8,512]{1,0:T(8,128)S(1)}, f32[1,4224]{1,0:T(1,128)S(1)}) custom-call(f32[8,512]{1,0:T(8,128)S(1)} %collective-permute-done.2.refs_0_, f32[8,512]{1,0:T(8,128)S(1)} %get-tuple-element.29.refs_1_, f32[1,512]{1,0:T(1,128)S(1)} %collective-permute-done.3.refs_2_, s32[1,4096]{1,0:T(1,128)S(1)} %get-tuple-element.24.slots_ref.refs_3_.refs_4_, ...), custom_call_target="tpu_custom_call" | custom-call | tf_op jit(solution)/shard_map/pallas_call | solution.py:288
  16.1 1.6 %collective-permute-start.4 = (f32[1,4224]{1,0:T(1,128)S(1)}, f32[1,4224]{1,0:T(1,128)S(1)}, u32[]{:S(2)}, u32[]{:S(2)}) collective-permute-start(f32[1,4224]{1,0:T(1,128)S(1)} %get-tuple-element.33), channel_id=1, source_target_pairs={{0,3},{1,2},{2,1},{3,0},{4,7},{5,6},{6,5},{7,4},{8,11},{9,10},{10,... | collective-permute-start | bytes 50696 | tf_op jit(solution)/shard_map/ppermute | solution.py:312
  17.7 0.5 %collective-permute-start.5 = (f32[1,4224]{1,0:T(1,128)S(1)}, f32[1,4224]{1,0:T(1,128)S(1)}, u32[]{:S(2)}, u32[]{:S(2)}) collective-permute-start(f32[1,4224]{1,0:T(1,128)S(1)} %get-tuple-element.33), channel_id=1, source_target_pairs={{0,2},{1,3},{2,0},{3,1},{4,6},{5,7},{6,4},{7,5},{8,10},{9,11},{10,... | collective-permute-start | bytes 50696 | tf_op jit(solution)/shard_map/ppermute | solution.py:312
  18.2 0.0 collective-permute-start.6
  18.2 1.1 %collective-permute-done.4 = f32[1,4224]{1,0:T(1,128)S(1)} collective-permute-done((f32[1,4224]{1,0:T(1,128)S(1)}, f32[1,4224]{1,0:T(1,128)S(1)}, u32[]{:S(2)}, u32[]{:S(2)}) %collective-permute-start.4) | collective-permute-done | bytes 16928 | tf_op jit(solution)/shard_map/ppermute | solution.py:312
  19.3 2.1 %collective-permute-done.5 = f32[1,4224]{1,0:T(1,128)S(1)} collective-permute-done((f32[1,4224]{1,0:T(1,128)S(1)}, f32[1,4224]{1,0:T(1,128)S(1)}, u32[]{:S(2)}, u32[]{:S(2)}) %collective-permute-start.5) | collective-permute-done | bytes 16928 | tf_op jit(solution)/shard_map/ppermute | solution.py:312
  21.5 0.0 collective-permute-done.6
  21.5 2.2 %collective-permute-start.7 = (f32[1,4224]{1,0:T(1,128)S(1)}, f32[1,4224]{1,0:T(1,128)S(1)}, u32[]{:S(2)}, u32[]{:S(2)}) collective-permute-start(f32[1,4224]{1,0:T(1,128)S(1)} %add_add_fusion.1.refs_3_), channel_id=1, source_target_pairs={{0,13},{1,12},{2,15},{3,14},{4,9},{5,8},{6,11},{7,10},{8,5},{9,4},... | collective-permute-start | bytes 50696 | tf_op jit(solution)/shard_map/ppermute | solution.py:312
  23.7 0.6 %collective-permute-start.8 = (f32[1,4224]{1,0:T(1,128)S(1)}, f32[1,4224]{1,0:T(1,128)S(1)}, u32[]{:S(2)}, u32[]{:S(2)}) collective-permute-start(f32[1,4224]{1,0:T(1,128)S(1)} %add_add_fusion.1.refs_3_), channel_id=1, source_target_pairs={{0,9},{1,8},{2,11},{3,10},{4,13},{5,12},{6,15},{7,14},{8,1},{9,0},... | collective-permute-start | bytes 50696 | tf_op jit(solution)/shard_map/ppermute | solution.py:312
  24.3 1.2 %collective-permute-start.9 = (f32[1,4224]{1,0:T(1,128)S(1)}, f32[1,4224]{1,0:T(1,128)S(1)}, u32[]{:S(2)}, u32[]{:S(2)}) collective-permute-start(f32[1,4224]{1,0:T(1,128)S(1)} %add_add_fusion.1.refs_3_), channel_id=1, source_target_pairs={{0,5},{1,4},{2,7},{3,6},{4,1},{5,0},{6,3},{7,2},{8,13},{9,12},{10,... | collective-permute-start | bytes 50696 | tf_op jit(solution)/shard_map/ppermute | solution.py:312
  25.5 1.0 %collective-permute-done.7.refs_0_ = f32[1,4224]{1,0:T(1,128)S(1)} collective-permute-done((f32[1,4224]{1,0:T(1,128)S(1)}, f32[1,4224]{1,0:T(1,128)S(1)}, u32[]{:S(2)}, u32[]{:S(2)}) %collective-permute-start.7) | collective-permute-done | bytes 16928 | tf_op jit(solution)/shard_map/ppermute | solution.py:312
  26.5 1.2 %collective-permute-done.8.refs_1_ = f32[1,4224]{1,0:T(1,128)S(1)} collective-permute-done((f32[1,4224]{1,0:T(1,128)S(1)}, f32[1,4224]{1,0:T(1,128)S(1)}, u32[]{:S(2)}, u32[]{:S(2)}) %collective-permute-start.8) | collective-permute-done | bytes 16928 | tf_op jit(solution)/shard_map/ppermute | solution.py:312
  27.8 0.0 collective-permute-done.9.refs_2_
  27.8 1.2 %shard_map.73 = (f32[1,4224]{1,0:T(1,128)S(1)}, f32[8,128]{1,0:T(8,128)S(1)}, f32[8,640]{1,0:T(8,128)S(1)}) custom-call(f32[1,4224]{1,0:T(1,128)S(1)} %collective-permute-done.7.refs_0_, f32[1,4224]{1,0:T(1,128)S(1)} %collective-permute-done.8.refs_1_, f32[1,4224]{1,0:T(1,128)S(1)} %collective-permute-done.9.refs_2_, f32[1,4224]{1,0:T(1,128)S(1)} %add_add_fusion.1.refs_3_, ...), custom_call_target="tpu_custom_call" | custom-call | tf_op jit(solution)/shard_map/pallas_call | solution.py:288
  29.0 2.9 %collective-permute-start.10 = (f32[8,640]{1,0:T(8,128)S(1)}, f32[8,640]{1,0:T(8,128)S(1)}, u32[]{:S(2)}, u32[]{:S(2)}) collective-permute-start(f32[8,640]{1,0:T(8,128)S(1)} %get-tuple-element.35.refs_1_), channel_id=1, source_target_pairs={{0,17},{1,16},{2,19},{3,18},{4,21},{5,20},{6,23},{7,22},{8,25},{9,... | collective-permute-start | bytes 61448 | tf_op jit(solution)/shard_map/ppermute | solution.py:328
  31.8 1.5 %collective-permute-done.10.refs_0_ = f32[8,640]{1,0:T(8,128)S(1)} collective-permute-done((f32[8,640]{1,0:T(8,128)S(1)}, f32[8,640]{1,0:T(8,128)S(1)}, u32[]{:S(2)}, u32[]{:S(2)}) %collective-permute-start.10) | collective-permute-done | bytes 20512 | tf_op jit(solution)/shard_map/ppermute | solution.py:328
  33.3 1.2 %shard_map.74 = (f32[16,512]{1,0:T(8,128)S(1)}, f32[8,128]{1,0:T(8,128)S(1)}, f32[1,4224]{1,0:T(1,128)S(1)}) custom-call(f32[8,640]{1,0:T(8,128)S(1)} %collective-permute-done.10.refs_0_, f32[8,640]{1,0:T(8,128)S(1)} %get-tuple-element.35.refs_1_, f32[1,512]{1,0:T(1,128)S(1)} %collective-permute-done.3.refs_2_, ...), custom_call_target="tpu_custom_call" | custom-call | tf_op jit(solution)/shard_map/pallas_call | solution.py:288
  34.5 0.6 %collective-permute-start.11 = (f32[1,4224]{1,0:T(1,128)S(1)}, f32[1,4224]{1,0:T(1,128)S(1)}, u32[]{:S(2)}, u32[]{:S(2)}) collective-permute-start(f32[1,4224]{1,0:T(1,128)S(1)} %get-tuple-element.38), channel_id=1, source_target_pairs={{0,3},{1,2},{2,1},{3,0},{4,7},{5,6},{6,5},{7,4},{8,11},{9,10},{10,... | collective-permute-start | bytes 50696 | tf_op jit(solution)/shard_map/ppermute | solution.py:312
  35.1 1.5 %collective-permute-start.12 = (f32[1,4224]{1,0:T(1,128)S(1)}, f32[1,4224]{1,0:T(1,128)S(1)}, u32[]{:S(2)}, u32[]{:S(2)}) collective-permute-start(f32[1,4224]{1,0:T(1,128)S(1)} %get-tuple-element.38), channel_id=1, source_target_pairs={{0,2},{1,3},{2,0},{3,1},{4,6},{5,7},{6,4},{7,5},{8,10},{9,11},{10,... | collective-permute-start | bytes 50696 | tf_op jit(solution)/shard_map/ppermute | solution.py:312
  36.7 0.0 collective-permute-start.13
  36.7 1.1 %collective-permute-done.11 = f32[1,4224]{1,0:T(1,128)S(1)} collective-permute-done((f32[1,4224]{1,0:T(1,128)S(1)}, f32[1,4224]{1,0:T(1,128)S(1)}, u32[]{:S(2)}, u32[]{:S(2)}) %collective-permute-start.11) | collective-permute-done | bytes 16928 | tf_op jit(solution)/shard_map/ppermute | solution.py:312
  37.8 1.1 %collective-permute-done.12 = f32[1,4224]{1,0:T(1,128)S(1)} collective-permute-done((f32[1,4224]{1,0:T(1,128)S(1)}, f32[1,4224]{1,0:T(1,128)S(1)}, u32[]{:S(2)}, u32[]{:S(2)}) %collective-permute-start.12) | collective-permute-done | bytes 16928 | tf_op jit(solution)/shard_map/ppermute | solution.py:312
  38.9 0.0 collective-permute-done.13
  38.9 0.5 collective-permute-start.14
  39.4 0.5 %collective-permute-start.15 = (f32[1,4224]{1,0:T(1,128)S(1)}, f32[1,4224]{1,0:T(1,128)S(1)}, u32[]{:S(2)}, u32[]{:S(2)}) collective-permute-start(f32[1,4224]{1,0:T(1,128)S(1)} %add_add_fusion.refs_3_), channel_id=1, source_target_pairs={{0,9},{1,8},{2,11},{3,10},{4,13},{5,12},{6,15},{7,14},{8,1},{9,0},... | collective-permute-start | bytes 50696 | tf_op jit(solution)/shard_map/ppermute | solution.py:312
  39.9 2.1 %collective-permute-start.16 = (f32[1,4224]{1,0:T(1,128)S(1)}, f32[1,4224]{1,0:T(1,128)S(1)}, u32[]{:S(2)}, u32[]{:S(2)}) collective-permute-start(f32[1,4224]{1,0:T(1,128)S(1)} %add_add_fusion.refs_3_), channel_id=1, source_target_pairs={{0,5},{1,4},{2,7},{3,6},{4,1},{5,0},{6,3},{7,2},{8,13},{9,12},{10,... | collective-permute-start | bytes 50696 | tf_op jit(solution)/shard_map/ppermute | solution.py:312
  42.0 0.7 %collective-permute-start.19 = (f32[16,512]{1,0:T(8,128)S(1)}, f32[16,512]{1,0:T(8,128)S(1)}, u32[]{:S(2)}, u32[]{:S(2)}) collective-permute-start(f32[16,512]{1,0:T(8,128)S(1)} %get-tuple-element.41), channel_id=1, source_target_pairs={{0,0},{1,1},{2,2},{3,3},{4,4},{5,5},{6,6},{7,7},{8,8},{9,9},{10,10... | collective-permute-start | bytes 98312 | tf_op jit(solution)/shard_map/ppermute | solution.py:328
  42.7 1.3 %collective-permute-done.14.refs_0_ = f32[1,4224]{1,0:T(1,128)S(1)} collective-permute-done((f32[1,4224]{1,0:T(1,128)S(1)}, f32[1,4224]{1,0:T(1,128)S(1)}, u32[]{:S(2)}, u32[]{:S(2)}) %collective-permute-start.14) | collective-permute-done | bytes 16928 | tf_op jit(solution)/shard_map/ppermute | solution.py:312
  44.0 0.0 collective-permute-done.15.refs_1_
  44.0 0.0 collective-permute-done.16.refs_2_
  44.0 1.3 %shard_map.75 = (f32[8,256]{1,0:T(8,128)S(1)}, f32[8,640]{1,0:T(8,128)S(1)}) custom-call(f32[1,4224]{1,0:T(1,128)S(1)} %collective-permute-done.14.refs_0_, f32[1,4224]{1,0:T(1,128)S(1)} %collective-permute-done.15.refs_1_, f32[1,4224]{1,0:T(1,128)S(1)} %collective-permute-done.16.refs_2_, f32[1,4224]{1,0:T(1,128)S(1)} %add_add_fusion.refs_3_, ...), custom_call_target="tpu_custom_call" | custom-call | tf_op jit(solution)/shard_map/pallas_call | solution.py:288
  45.3 2.8 %collective-permute-start.17 = (f32[8,640]{1,0:T(8,128)S(1)}, f32[8,640]{1,0:T(8,128)S(1)}, u32[]{:S(2)}, u32[]{:S(2)}) collective-permute-start(f32[8,640]{1,0:T(8,128)S(1)} %get-tuple-element.40), channel_id=1, source_target_pairs={{0,16},{1,17},{2,18},{3,19},{4,20},{5,21},{6,22},{7,23},{8,24},{9,... | collective-permute-start | bytes 61448 | tf_op jit(solution)/shard_map/ppermute | solution.py:328
  48.1 0.7 %collective-permute-start.18 = (f32[8,640]{1,0:T(8,128)S(1)}, f32[8,640]{1,0:T(8,128)S(1)}, u32[]{:S(2)}, u32[]{:S(2)}) collective-permute-start(f32[8,640]{1,0:T(8,128)S(1)} %get-tuple-element.40), channel_id=1, source_target_pairs={{0,0},{1,1},{2,2},{3,3},{4,4},{5,5},{6,6},{7,7},{8,8},{9,9},{10,10... | collective-permute-start | bytes 61448 | tf_op jit(solution)/shard_map/ppermute | solution.py:328
  48.7 0.0 collective-permute-done.19.refs_3_
  48.7 0.8 %collective-permute-done.17.refs_0_ = f32[8,640]{1,0:T(8,128)S(1)} collective-permute-done((f32[8,640]{1,0:T(8,128)S(1)}, f32[8,640]{1,0:T(8,128)S(1)}, u32[]{:S(2)}, u32[]{:S(2)}) %collective-permute-start.17) | collective-permute-done | bytes 20512 | tf_op jit(solution)/shard_map/ppermute | solution.py:328
  49.6 0.0 collective-permute-done.18.refs_1_
  49.6 0.6 %shard_map.76 = (f32[8,512]{1,0:T(8,128)}, f32[8,512]{1,0:T(8,128)}) custom-call(f32[8,640]{1,0:T(8,128)S(1)} %collective-permute-done.17.refs_0_, f32[8,640]{1,0:T(8,128)S(1)} %collective-permute-done.18.refs_1_, f32[1,512]{1,0:T(1,128)S(1)} %get-tuple-element.30.refs_2_, f32[16,512]{1,0:T(8,128)S(1)} %collective-permute-done.19.refs_3_, ...), custom_call_target="tpu_custom_call" | custom-call | tf_op jit(solution)/shard_map/pallas_call | solution.py:288
  (2 shorter events, 0.1 us)
Async XLA Ops:
  2.6 5.2 %collective-permute-start = (bf16[64,512]{1,0:T(8,128)(2,1)S(1)}, bf16[64,512]{1,0:T(8,128)(2,1)S(1)}, u32[]{:S(2)}, u32[]{:S(2)}) collective-permute-start(bf16[64,512]{1,0:T(8,128)(2,1)S(1)} %get-tuple-element.28), channel_id=1, source_target_pairs={{0,17},{1,16},{2,19},{3,18},{4,21},{5,20},{6,23},{7,22},{8,25},{9,... | collective-permute-start | bytes 196616 | tf_op jit(solution)/shard_map/ppermute | solution.py:328
  5.0 2.8 %collective-permute-start.1 = (bf16[64,512]{1,0:T(8,128)(2,1)S(1)}, bf16[64,512]{1,0:T(8,128)(2,1)S(1)}, u32[]{:S(2)}, u32[]{:S(2)}) collective-permute-start(bf16[64,512]{1,0:T(8,128)(2,1)S(1)} %get-tuple-element.28), channel_id=1, source_target_pairs={{0,0},{1,1},{2,2},{3,3},{4,4},{5,5},{6,6},{7,7},{8,8},{9,9},{10,10... | collective-permute-start | bytes 196616 | tf_op jit(solution)/shard_map/ppermute | solution.py:328
  10.4 4.5 %collective-permute-start.2 = (f32[8,512]{1,0:T(8,128)S(1)}, f32[8,512]{1,0:T(8,128)S(1)}, u32[]{:S(2)}, u32[]{:S(2)}) collective-permute-start(f32[8,512]{1,0:T(8,128)S(1)} %get-tuple-element.29.refs_1_), channel_id=1, source_target_pairs={{0,17},{1,16},{2,19},{3,18},{4,21},{5,20},{6,23},{7,22},{8,25},{9,... | collective-permute-start | bytes 49160 | tf_op jit(solution)/shard_map/ppermute | solution.py:328
  12.3 2.6 %collective-permute-start.3 = (f32[1,512]{1,0:T(1,128)S(1)}, f32[1,512]{1,0:T(1,128)S(1)}, u32[]{:S(2)}, u32[]{:S(2)}) collective-permute-start(f32[1,512]{1,0:T(1,128)S(1)} %get-tuple-element.30.refs_2_), channel_id=1, source_target_pairs={{0,0},{1,1},{2,2},{3,3},{4,4},{5,5},{6,6},{7,7},{8,8},{9,9},{10,10... | collective-permute-start | bytes 6152 | tf_op jit(solution)/shard_map/ppermute | solution.py:328
  16.1 3.2 %collective-permute-start.4 = (f32[1,4224]{1,0:T(1,128)S(1)}, f32[1,4224]{1,0:T(1,128)S(1)}, u32[]{:S(2)}, u32[]{:S(2)}) collective-permute-start(f32[1,4224]{1,0:T(1,128)S(1)} %get-tuple-element.33), channel_id=1, source_target_pairs={{0,3},{1,2},{2,1},{3,0},{4,7},{5,6},{6,5},{7,4},{8,11},{9,10},{10,... | collective-permute-start | bytes 50696 | tf_op jit(solution)/shard_map/ppermute | solution.py:312
  17.7 3.7 %collective-permute-start.5 = (f32[1,4224]{1,0:T(1,128)S(1)}, f32[1,4224]{1,0:T(1,128)S(1)}, u32[]{:S(2)}, u32[]{:S(2)}) collective-permute-start(f32[1,4224]{1,0:T(1,128)S(1)} %get-tuple-element.33), channel_id=1, source_target_pairs={{0,2},{1,3},{2,0},{3,1},{4,6},{5,7},{6,4},{7,5},{8,10},{9,11},{10,... | collective-permute-start | bytes 50696 | tf_op jit(solution)/shard_map/ppermute | solution.py:312
  18.2 3.2 %collective-permute-start.6 = (f32[1,4224]{1,0:T(1,128)S(1)}, f32[1,4224]{1,0:T(1,128)S(1)}, u32[]{:S(2)}, u32[]{:S(2)}) collective-permute-start(f32[1,4224]{1,0:T(1,128)S(1)} %get-tuple-element.33), channel_id=1, source_target_pairs={{0,1},{1,0},{2,3},{3,2},{4,5},{5,4},{6,7},{7,6},{8,9},{9,8},{10,11... | collective-permute-start | bytes 50696 | tf_op jit(solution)/shard_map/ppermute | solution.py:312
  21.5 5.0 %collective-permute-start.7 = (f32[1,4224]{1,0:T(1,128)S(1)}, f32[1,4224]{1,0:T(1,128)S(1)}, u32[]{:S(2)}, u32[]{:S(2)}) collective-permute-start(f32[1,4224]{1,0:T(1,128)S(1)} %add_add_fusion.1.refs_3_), channel_id=1, source_target_pairs={{0,13},{1,12},{2,15},{3,14},{4,9},{5,8},{6,11},{7,10},{8,5},{9,4},... | collective-permute-start | bytes 50696 | tf_op jit(solution)/shard_map/ppermute | solution.py:312
  23.7 4.1 %collective-permute-start.8 = (f32[1,4224]{1,0:T(1,128)S(1)}, f32[1,4224]{1,0:T(1,128)S(1)}, u32[]{:S(2)}, u32[]{:S(2)}) collective-permute-start(f32[1,4224]{1,0:T(1,128)S(1)} %add_add_fusion.1.refs_3_), channel_id=1, source_target_pairs={{0,9},{1,8},{2,11},{3,10},{4,13},{5,12},{6,15},{7,14},{8,1},{9,0},... | collective-permute-start | bytes 50696 | tf_op jit(solution)/shard_map/ppermute | solution.py:312
  24.3 3.5 %collective-permute-start.9 = (f32[1,4224]{1,0:T(1,128)S(1)}, f32[1,4224]{1,0:T(1,128)S(1)}, u32[]{:S(2)}, u32[]{:S(2)}) collective-permute-start(f32[1,4224]{1,0:T(1,128)S(1)} %add_add_fusion.1.refs_3_), channel_id=1, source_target_pairs={{0,5},{1,4},{2,7},{3,6},{4,1},{5,0},{6,3},{7,2},{8,13},{9,12},{10,... | collective-permute-start | bytes 50696 | tf_op jit(solution)/shard_map/ppermute | solution.py:312
  29.0 4.3 %collective-permute-start.10 = (f32[8,640]{1,0:T(8,128)S(1)}, f32[8,640]{1,0:T(8,128)S(1)}, u32[]{:S(2)}, u32[]{:S(2)}) collective-permute-start(f32[8,640]{1,0:T(8,128)S(1)} %get-tuple-element.35.refs_1_), channel_id=1, source_target_pairs={{0,17},{1,16},{2,19},{3,18},{4,21},{5,20},{6,23},{7,22},{8,25},{9,... | collective-permute-start | bytes 61448 | tf_op jit(solution)/shard_map/ppermute | solution.py:328
  34.5 3.2 %collective-permute-start.11 = (f32[1,4224]{1,0:T(1,128)S(1)}, f32[1,4224]{1,0:T(1,128)S(1)}, u32[]{:S(2)}, u32[]{:S(2)}) collective-permute-start(f32[1,4224]{1,0:T(1,128)S(1)} %get-tuple-element.38), channel_id=1, source_target_pairs={{0,3},{1,2},{2,1},{3,0},{4,7},{5,6},{6,5},{7,4},{8,11},{9,10},{10,... | collective-permute-start | bytes 50696 | tf_op jit(solution)/shard_map/ppermute | solution.py:312
  35.1 3.7 %collective-permute-start.12 = (f32[1,4224]{1,0:T(1,128)S(1)}, f32[1,4224]{1,0:T(1,128)S(1)}, u32[]{:S(2)}, u32[]{:S(2)}) collective-permute-start(f32[1,4224]{1,0:T(1,128)S(1)} %get-tuple-element.38), channel_id=1, source_target_pairs={{0,2},{1,3},{2,0},{3,1},{4,6},{5,7},{6,4},{7,5},{8,10},{9,11},{10,... | collective-permute-start | bytes 50696 | tf_op jit(solution)/shard_map/ppermute | solution.py:312
  36.7 2.2 %collective-permute-start.13 = (f32[1,4224]{1,0:T(1,128)S(1)}, f32[1,4224]{1,0:T(1,128)S(1)}, u32[]{:S(2)}, u32[]{:S(2)}) collective-permute-start(f32[1,4224]{1,0:T(1,128)S(1)} %get-tuple-element.38), channel_id=1, source_target_pairs={{0,1},{1,0},{2,3},{3,2},{4,5},{5,4},{6,7},{7,6},{8,9},{9,8},{10,11... | collective-permute-start | bytes 50696 | tf_op jit(solution)/shard_map/ppermute | solution.py:312
  38.9 5.1 %collective-permute-start.14 = (f32[1,4224]{1,0:T(1,128)S(1)}, f32[1,4224]{1,0:T(1,128)S(1)}, u32[]{:S(2)}, u32[]{:S(2)}) collective-permute-start(f32[1,4224]{1,0:T(1,128)S(1)} %add_add_fusion.refs_3_), channel_id=1, source_target_pairs={{0,13},{1,12},{2,15},{3,14},{4,9},{5,8},{6,11},{7,10},{8,5},{9,4},... | collective-permute-start | bytes 50696 | tf_op jit(solution)/shard_map/ppermute | solution.py:312
  39.4 4.6 %collective-permute-start.15 = (f32[1,4224]{1,0:T(1,128)S(1)}, f32[1,4224]{1,0:T(1,128)S(1)}, u32[]{:S(2)}, u32[]{:S(2)}) collective-permute-start(f32[1,4224]{1,0:T(1,128)S(1)} %add_add_fusion.refs_3_), channel_id=1, source_target_pairs={{0,9},{1,8},{2,11},{3,10},{4,13},{5,12},{6,15},{7,14},{8,1},{9,0},... | collective-permute-start | bytes 50696 | tf_op jit(solution)/shard_map/ppermute | solution.py:312
  39.9 4.1 %collective-permute-start.16 = (f32[1,4224]{1,0:T(1,128)S(1)}, f32[1,4224]{1,0:T(1,128)S(1)}, u32[]{:S(2)}, u32[]{:S(2)}) collective-permute-start(f32[1,4224]{1,0:T(1,128)S(1)} %add_add_fusion.refs_3_), channel_id=1, source_target_pairs={{0,5},{1,4},{2,7},{3,6},{4,1},{5,0},{6,3},{7,2},{8,13},{9,12},{10,... | collective-permute-start | bytes 50696 | tf_op jit(solution)/shard_map/ppermute | solution.py:312
  42.0 6.7 %collective-permute-start.19 = (f32[16,512]{1,0:T(8,128)S(1)}, f32[16,512]{1,0:T(8,128)S(1)}, u32[]{:S(2)}, u32[]{:S(2)}) collective-permute-start(f32[16,512]{1,0:T(8,128)S(1)} %get-tuple-element.41), channel_id=1, source_target_pairs={{0,0},{1,1},{2,2},{3,3},{4,4},{5,5},{6,6},{7,7},{8,8},{9,9},{10,10... | collective-permute-start | bytes 98312 | tf_op jit(solution)/shard_map/ppermute | solution.py:328
  45.3 4.3 %collective-permute-start.17 = (f32[8,640]{1,0:T(8,128)S(1)}, f32[8,640]{1,0:T(8,128)S(1)}, u32[]{:S(2)}, u32[]{:S(2)}) collective-permute-start(f32[8,640]{1,0:T(8,128)S(1)} %get-tuple-element.40), channel_id=1, source_target_pairs={{0,16},{1,17},{2,18},{3,19},{4,20},{5,21},{6,22},{7,23},{8,24},{9,... | collective-permute-start | bytes 61448 | tf_op jit(solution)/shard_map/ppermute | solution.py:328
  48.1 1.5 %collective-permute-start.18 = (f32[8,640]{1,0:T(8,128)S(1)}, f32[8,640]{1,0:T(8,128)S(1)}, u32[]{:S(2)}, u32[]{:S(2)}) collective-permute-start(f32[8,640]{1,0:T(8,128)S(1)} %get-tuple-element.40), channel_id=1, source_target_pairs={{0,0},{1,1},{2,2},{3,3},{4,4},{5,5},{6,6},{7,7},{8,8},{9,9},{10,10... | collective-permute-start | bytes 61448 | tf_op jit(solution)/shard_map/ppermute | solution.py:328

commit v15 on v14

--- a/solution.py
+++ b/solution.py
@@ -68,6 +68,15 @@
 
 def total_of(refs):
     return pair_total([ref[...] for ref in refs])
+
+
+def resident(moved, own):
+    return moved + own * (lax.axis_index("dp") == 0).astype(own.dtype)
+
+
+def home_total(refs):
+    far, moved, own = (ref[...].astype(f32) for ref in refs)
+    return far + resident(moved, own)
 
 
 def row_sum(value):
@@ -119,11 +128,14 @@
     for begin in range(0, row_count, STEP):
         hit_ref[begin : begin + STEP, :] = hits(begin)
     copies[1].wait()
-    out_ref[...] = jnp.dot(
-        feat_ref[...], hit_ref[...], preferred_element_type=f32
-    ).astype(bf16)
+    picked = jnp.dot(feat_ref[...], hit_ref[...], preferred_element_type=f32)
     for copy in copies[2:]:
         copy.wait()
+    row = lax.broadcasted_iota(jnp.int32, (16, count), 0)
+    extra = jnp.zeros((16, count), f32)
+    for place, part in enumerate(split3(scale_ref[...])):
+        extra = jnp.where(row == place, part, extra)
+    out_ref[...] = jnp.concatenate([picked, extra], axis=0).astype(bf16)
 
 
 def columns_body(feat_ref, slots_ref, prices_ref, columns_ref, turned_ref, weight_ref):
@@ -140,9 +152,12 @@
         weight_ref[:, here] = stack2(weight)
 
 
-def rows_body(parts, turned_ref, weight_ref, *refs):
-    center_refs, (block_ref, center_ref, out_ref) = refs[:parts], refs[parts:]
-    center = total_of(center_refs).astype(f32)
+def rows_body(crossed, parts, turned_ref, weight_ref, *refs):
+    center_refs, (block_ref, center_ref, scale_ref, out_ref) = refs[:parts], refs[parts:]
+    arrived = home_total(center_refs) if crossed else total_of(center_refs).astype(f32)
+    rows = arrived[-16:] * (1.0 / lax.axis_size("dp"))
+    scale_ref[...] = rows[0:1] + (rows[1:2] + rows[2:3])
+    center = arrived[:-16]
     center = jnp.concatenate(
         [*split3(center * FACTOR), norm_rows(center, 0)], axis=0
     ).astype(bf16)
@@ -266,13 +281,18 @@
     fold_rows(rows, block_ref, slots_ref, out_ref)
 
 
-def finish_body(parts, inv_rows, *refs):
+def finish_body(crossed, parts, inv_rows, *refs):
     fold_refs = refs[:parts]
-    (scale_ref, state_ref, step_ref, norm_ref, sums_ref,
+    (moved_ref, state_ref, scale_ref, step_ref, norm_ref, sums_ref,
      coefficients_ref, out_ref) = refs[parts:]
     count = scale_ref.shape[1]
-    folded = total_of(fold_refs)
-    target, residual = state_ref[0:SLOTS, :], state_ref[SLOTS:, :]
+    state = state_ref[...]
+    if crossed:
+        folded = home_total(fold_refs)
+        state = resident(moved_ref[...], state)
+    else:
+        folded = total_of(fold_refs)
+    target, residual = state[0:SLOTS], state[SLOTS:]
     first_norm = norm_ref[...]
     norm, cross = sums_ref[:, 0:EXTRA], sums_ref[:, EXTRA:]
     ratio = norm / first_norm
@@ -320,7 +340,8 @@
     for group in range(groups):
         for place in range(count):
             to_group, to_place = target_of(group, place)
-            pairs.append((group * count + place, to_group * count + to_place))
+            if (to_group, to_place) != (group, place):
+                pairs.append((group * count + place, to_group * count + to_place))
     return pairs
 
 
@@ -359,9 +380,6 @@
     pass_cost = dict(flops=64 * row_count * count, bytes_accessed=4 * row_count * count)
 
     crossed = lax.axis_size("dp") == 2
-
-    def in_place(value):
-        return moved(value, beside) if crossed else value
 
     def share(value):
         return [moved(value, across), value] if crossed else exchange(value, "dp")
@@ -383,7 +401,7 @@
             shaped((1, row_count), jnp.int32),
             shaped((1, row_count)),
             shaped((1, count)),
-            shaped((depth, count), bf16),
+            shaped((depth + 16, count), bf16),
         ),
         *inputs,
         sources=[HBM] * 5,
@@ -394,10 +412,9 @@
         ],
     )
     if crossed:
-        centers = [moved(picked, outward), moved(picked, beside)]
+        centers = [moved(picked, outward), moved(picked, beside), picked]
     else:
         centers = exchange(picked, "dp")
-    scale = in_place(own_scale)
     columns, turned_columns, weight = call(
         columns_body,
         (
@@ -409,9 +426,14 @@
         flops=1000 * row_count,
         bytes_accessed=1024 * row_count,
     )
-    block, center, first = call(
-        partial(rows_body, len(centers)),
-        (shaped((2 * row_count, count), bf16), shaped((DEPTH, count), bf16), vector),
+    block, center, scale, first = call(
+        partial(rows_body, crossed, len(centers)),
+        (
+            shaped((2 * row_count, count), bf16),
+            shaped((DEPTH, count), bf16),
+            shaped((1, count)),
+            vector,
+        ),
         turned_columns, weight, *centers,
         **pass_cost,
     )
@@ -441,13 +463,15 @@
         *latest, slots, block, rows, norm,
     )
     if crossed:
-        folds = [moved(folded, homeward), moved(folded, beside)]
+        folds = [moved(folded, homeward), moved(folded, beside), folded]
+        moved_state = moved(state, beside)
     else:
         folds = exchange(folded, "dp")
+        moved_state = state
     return call(
-        partial(finish_body, len(folds), 1.0 / all_rows),
+        partial(finish_body, crossed, len(folds), 1.0 / all_rows),
         (vector, vector),
-        *folds, own_scale, in_place(state), step, norm, sums,
+        *folds, moved_state, state, own_scale, step, norm, sums,
     )
 
 

time: 50.4 us -> 49.7 us (0.986)
  starting transfers between devices: 24.1 us -> 23 us
    ppermute x8 -> x7, starting transfers between devices: 12.6 us -> 11.2 us  [moved(): return lax.ppermute(value, ('dp', 'centers'), pairs_over(target_of))]
    ppermute x8 -> x7, waiting for transfers between devices: 3.78 us -> 3.98 us  [moved(): return lax.ppermute(value, ('dp', 'centers'), pairs_over(target_of))]
  transfers between devices with their start and end apart: 20 -> 19, of which waited for: 10 -> 10; matrix products, arithmetic and copies ran while one was open for 0% -> 0% of each run, Pallas kernels for 8% -> 8%
where the time goes in v15:
time: 49.7 us; the launch traced here: 49.5 us
  starting transfers between devices  23 us (46%)
  waiting for transfers between devices  13.1 us (26%)
  Pallas kernels  12.7 us (26%)
  between operations  0.73 us (1%)
    pallas_call x9, Pallas kernels, call(): pl.pallas_call(body, out_shape=out_shape, in_specs=sources or [VMEM] * le...  12.7 us
    ppermute x12, starting transfers between devices, exchange(): parts.insert(0, lax.ppermute(value, axis, pairs))  11.8 us
    ppermute x7, starting transfers between devices, moved(): return lax.ppermute(value, ('dp', 'centers'), pairs_over(target_of))  11.2 us
    ppermute x12, waiting for transfers between devices, exchange(): parts.insert(0, lax.ppermute(value, axis, pairs))  9.08 us
    ppermute x7, waiting for transfers between devices, moved(): return lax.ppermute(value, ('dp', 'centers'), pairs_over(target_of))  3.98 us
  transfers between devices with their start and end apart: 19, of which 10 were waited for; matrix products, arithmetic and copies ran while one was open for 0% of the time, Pallas kernels for 8%

profile of v15, /device:TPU:0, one launch (start us, length us, event | category | flops | bytes accessed | tf_op | source)
XLA Modules:
  0.0 49.5 jit_solution(11639839469462168455)
XLA Ops:
  0.6 2.0 %shard_map.68 = (bf16[64,4096]{1,0:T(8,128)(2,1)S(1)}, s32[1,4096]{1,0:T(1,128)S(1)}, f32[1,4096]{1,0:T(1,128)S(1)}, f32[1,512]{1,0:T(1,128)S(1)}, bf16[80,512]{1,0:T(8,128)(2,1)S(1)}) custom-call(bf16[64,4096]{1,0:T(8,128)(2,1)} %feat_hbm.1, s32[1,512]{1,0:T(1,128)} %bitcast.6, s32[1,4096]{1,0:T(1,128)} %bitcast.4, f32[1,4096]{1,0:T(1,128)} %bitcast.5, ...), custom_call_target="tpu_custom_call" | custom-call | tf_op jit(solution)/shard_map/pallas_call | solution.py:308
  2.6 2.4 %collective-permute-start = (bf16[80,512]{1,0:T(8,128)(2,1)S(1)}, bf16[80,512]{1,0:T(8,128)(2,1)S(1)}, u32[]{:S(2)}, u32[]{:S(2)}) collective-permute-start(bf16[80,512]{1,0:T(8,128)(2,1)S(1)} %get-tuple-element.29.refs_2_), channel_id=1, source_target_pairs={{0,17},{1,16},{2,19},{3,18},{4,21},{5,20},{6,23},{7,22},{8,25},{9,... | collective-permute-start | bytes 245768 | tf_op jit(solution)/shard_map/ppermute | solution.py:349
  5.0 0.7 %collective-permute-start.1 = (bf16[80,512]{1,0:T(8,128)(2,1)S(1)}, bf16[80,512]{1,0:T(8,128)(2,1)S(1)}, u32[]{:S(2)}, u32[]{:S(2)}) collective-permute-start(bf16[80,512]{1,0:T(8,128)(2,1)S(1)} %get-tuple-element.29.refs_2_), channel_id=1, source_target_pairs={{16,17},{17,16},{18,19},{19,18},{20,21},{21,20},{22,23},{23,22},{2... | collective-permute-start | bytes 245768 | tf_op jit(solution)/shard_map/ppermute | solution.py:349
  5.7 0.7 %shard_map.69 = (bf16[256,4096]{1,0:T(8,128)(2,1)S(1)}, bf16[4096,256]{1,0:T(8,128)(2,1)S(1)}, bf16[16,4096]{1,0:T(8,128)(2,1)S(1)}) custom-call(bf16[64,4096]{1,0:T(8,128)(2,1)S(1)} %get-tuple-element.24.feat_ref, s32[1,4096]{1,0:T(1,128)S(1)} %get-tuple-element.25.slots_ref.refs_3_.refs_4_, f32[1,4096]{1,0:T(1,128)S(1)} %get-tuple-element.26.prices_ref), custom_call_target="tpu_custom_call" | custom-call | flops 4096000 | bytes 4194304 | tf_op jit(solution)/shard_map/pallas_call | solution.py:308
  6.4 1.7 %collective-permute-done.refs_0_ = bf16[80,512]{1,0:T(8,128)(2,1)S(1)} collective-permute-done((bf16[80,512]{1,0:T(8,128)(2,1)S(1)}, bf16[80,512]{1,0:T(8,128)(2,1)S(1)}, u32[]{:S(2)}, u32[]{:S(2)}) %collective-permute-start) | collective-permute-done | bytes 81952 | tf_op jit(solution)/shard_map/ppermute | solution.py:349
  8.0 0.0 collective-permute-done.1.refs_1_
  8.0 2.6 %shard_map.70 = (bf16[8192,512]{1,0:T(8,128)(2,1)S(1)}, bf16[256,512]{1,0:T(8,128)(2,1)S(1)}, f32[1,512]{1,0:T(1,128)S(1)}, f32[8,512]{1,0:T(8,128)S(1)}) custom-call(bf16[4096,256]{1,0:T(8,128)(2,1)S(1)} %get-tuple-element.27.turned_ref, bf16[16,4096]{1,0:T(8,128)(2,1)S(1)} %get-tuple-element.28.weight_ref, ...), custom_call_target="tpu_custom_call" | custom-call | flops 134217728 | bytes 8388608 | tf_op jit(solution)/shard_map/pallas_call | solution.py:308
  10.6 2.1 %collective-permute-start.2 = (f32[8,512]{1,0:T(8,128)S(1)}, f32[8,512]{1,0:T(8,128)S(1)}, u32[]{:S(2)}, u32[]{:S(2)}) collective-permute-start(f32[8,512]{1,0:T(8,128)S(1)} %get-tuple-element.30.refs_1_), channel_id=1, source_target_pairs={{0,17},{1,16},{2,19},{3,18},{4,21},{5,20},{6,23},{7,22},{8,25},{9,... | collective-permute-start | bytes 49160 | tf_op jit(solution)/shard_map/ppermute | solution.py:349
  12.7 1.9 %shard_map.71.refs_4_ = bf16[1024,4096]{1,0:T(8,128)(2,1)S(1)} custom-call(bf16[256,4096]{1,0:T(8,128)(2,1)S(1)} %get-tuple-element.32.columns_ref, bf16[256,512]{1,0:T(8,128)(2,1)S(1)} %get-tuple-element.33.center_ref), custom_call_target="tpu_custom_call" | custom-call | flops 134217728 | bytes 8388608 | tf_op jit(solution)/shard_map/pallas_call | solution.py:308
  14.6 0.0 collective-permute-done.2.refs_0_
  14.6 1.2 %shard_map.72 = (f32[8,512]{1,0:T(8,128)S(1)}, f32[1,4224]{1,0:T(1,128)S(1)}) custom-call(f32[8,512]{1,0:T(8,128)S(1)} %collective-permute-done.2.refs_0_, f32[8,512]{1,0:T(8,128)S(1)} %get-tuple-element.30.refs_1_, f32[1,512]{1,0:T(1,128)S(1)} %get-tuple-element.31.refs_2_, s32[1,4096]{1,0:T(1,128)S(1)} %get-tuple-element.25.slots_ref.refs_3_.refs_4_, ...), custom_call_target="tpu_custom_call" | custom-call | tf_op jit(solution)/shard_map/pallas_call | solution.py:308
  15.9 1.6 %collective-permute-start.3 = (f32[1,4224]{1,0:T(1,128)S(1)}, f32[1,4224]{1,0:T(1,128)S(1)}, u32[]{:S(2)}, u32[]{:S(2)}) collective-permute-start(f32[1,4224]{1,0:T(1,128)S(1)} %get-tuple-element.34), channel_id=1, source_target_pairs={{0,3},{1,2},{2,1},{3,0},{4,7},{5,6},{6,5},{7,4},{8,11},{9,10},{10,... | collective-permute-start | bytes 50696 | tf_op jit(solution)/shard_map/ppermute | solution.py:332
  17.4 0.5 collective-permute-start.4
  17.9 0.0 collective-permute-start.5
  17.9 1.2 %collective-permute-done.3 = f32[1,4224]{1,0:T(1,128)S(1)} collective-permute-done((f32[1,4224]{1,0:T(1,128)S(1)}, f32[1,4224]{1,0:T(1,128)S(1)}, u32[]{:S(2)}, u32[]{:S(2)}) %collective-permute-start.3) | collective-permute-done | bytes 16928 | tf_op jit(solution)/shard_map/ppermute | solution.py:332
  19.1 2.1 %collective-permute-done.4 = f32[1,4224]{1,0:T(1,128)S(1)} collective-permute-done((f32[1,4224]{1,0:T(1,128)S(1)}, f32[1,4224]{1,0:T(1,128)S(1)}, u32[]{:S(2)}, u32[]{:S(2)}) %collective-permute-start.4) | collective-permute-done | bytes 16928 | tf_op jit(solution)/shard_map/ppermute | solution.py:332
  21.2 0.0 collective-permute-done.5
  21.2 2.3 %collective-permute-start.6 = (f32[1,4224]{1,0:T(1,128)S(1)}, f32[1,4224]{1,0:T(1,128)S(1)}, u32[]{:S(2)}, u32[]{:S(2)}) collective-permute-start(f32[1,4224]{1,0:T(1,128)S(1)} %add_add_fusion.1.refs_3_), channel_id=1, source_target_pairs={{0,13},{1,12},{2,15},{3,14},{4,9},{5,8},{6,11},{7,10},{8,5},{9,4},... | collective-permute-start | bytes 50696 | tf_op jit(solution)/shard_map/ppermute | solution.py:332
  23.5 0.5 %collective-permute-start.7 = (f32[1,4224]{1,0:T(1,128)S(1)}, f32[1,4224]{1,0:T(1,128)S(1)}, u32[]{:S(2)}, u32[]{:S(2)}) collective-permute-start(f32[1,4224]{1,0:T(1,128)S(1)} %add_add_fusion.1.refs_3_), channel_id=1, source_target_pairs={{0,9},{1,8},{2,11},{3,10},{4,13},{5,12},{6,15},{7,14},{8,1},{9,0},... | collective-permute-start | bytes 50696 | tf_op jit(solution)/shard_map/ppermute | solution.py:332
  24.0 1.2 %collective-permute-start.8 = (f32[1,4224]{1,0:T(1,128)S(1)}, f32[1,4224]{1,0:T(1,128)S(1)}, u32[]{:S(2)}, u32[]{:S(2)}) collective-permute-start(f32[1,4224]{1,0:T(1,128)S(1)} %add_add_fusion.1.refs_3_), channel_id=1, source_target_pairs={{0,5},{1,4},{2,7},{3,6},{4,1},{5,0},{6,3},{7,2},{8,13},{9,12},{10,... | collective-permute-start | bytes 50696 | tf_op jit(solution)/shard_map/ppermute | solution.py:332
  25.3 1.0 %collective-permute-done.6.refs_0_ = f32[1,4224]{1,0:T(1,128)S(1)} collective-permute-done((f32[1,4224]{1,0:T(1,128)S(1)}, f32[1,4224]{1,0:T(1,128)S(1)}, u32[]{:S(2)}, u32[]{:S(2)}) %collective-permute-start.6) | collective-permute-done | bytes 16928 | tf_op jit(solution)/shard_map/ppermute | solution.py:332
  26.3 1.3 %collective-permute-done.7.refs_1_ = f32[1,4224]{1,0:T(1,128)S(1)} collective-permute-done((f32[1,4224]{1,0:T(1,128)S(1)}, f32[1,4224]{1,0:T(1,128)S(1)}, u32[]{:S(2)}, u32[]{:S(2)}) %collective-permute-start.7) | collective-permute-done | bytes 16928 | tf_op jit(solution)/shard_map/ppermute | solution.py:332
  27.6 0.0 collective-permute-done.8.refs_2_
  27.6 1.2 %shard_map.73 = (f32[1,4224]{1,0:T(1,128)S(1)}, f32[8,128]{1,0:T(8,128)S(1)}, f32[8,640]{1,0:T(8,128)S(1)}) custom-call(f32[1,4224]{1,0:T(1,128)S(1)} %collective-permute-done.6.refs_0_, f32[1,4224]{1,0:T(1,128)S(1)} %collective-permute-done.7.refs_1_, f32[1,4224]{1,0:T(1,128)S(1)} %collective-permute-done.8.refs_2_, f32[1,4224]{1,0:T(1,128)S(1)} %add_add_fusion.1.refs_3_, ...), custom_call_target="tpu_custom_call" | custom-call | tf_op jit(solution)/shard_map/pallas_call | solution.py:308
  28.8 2.4 %collective-permute-start.9 = (f32[8,640]{1,0:T(8,128)S(1)}, f32[8,640]{1,0:T(8,128)S(1)}, u32[]{:S(2)}, u32[]{:S(2)}) collective-permute-start(f32[8,640]{1,0:T(8,128)S(1)} %get-tuple-element.36.refs_1_), channel_id=1, source_target_pairs={{0,17},{1,16},{2,19},{3,18},{4,21},{5,20},{6,23},{7,22},{8,25},{9,... | collective-permute-start | bytes 61448 | tf_op jit(solution)/shard_map/ppermute | solution.py:349
  31.1 1.5 %collective-permute-done.9.refs_0_ = f32[8,640]{1,0:T(8,128)S(1)} collective-permute-done((f32[8,640]{1,0:T(8,128)S(1)}, f32[8,640]{1,0:T(8,128)S(1)}, u32[]{:S(2)}, u32[]{:S(2)}) %collective-permute-start.9) | collective-permute-done | bytes 20512 | tf_op jit(solution)/shard_map/ppermute | solution.py:349
  32.6 1.2 %shard_map.74 = (f32[16,512]{1,0:T(8,128)S(1)}, f32[8,128]{1,0:T(8,128)S(1)}, f32[1,4224]{1,0:T(1,128)S(1)}) custom-call(f32[8,640]{1,0:T(8,128)S(1)} %collective-permute-done.9.refs_0_, f32[8,640]{1,0:T(8,128)S(1)} %get-tuple-element.36.refs_1_, f32[1,512]{1,0:T(1,128)S(1)} %get-tuple-element.31.refs_2_, ...), custom_call_target="tpu_custom_call" | custom-call | tf_op jit(solution)/shard_map/pallas_call | solution.py:308
  33.8 1.1 %collective-permute-start.10 = (f32[1,4224]{1,0:T(1,128)S(1)}, f32[1,4224]{1,0:T(1,128)S(1)}, u32[]{:S(2)}, u32[]{:S(2)}) collective-permute-start(f32[1,4224]{1,0:T(1,128)S(1)} %get-tuple-element.39), channel_id=1, source_target_pairs={{0,3},{1,2},{2,1},{3,0},{4,7},{5,6},{6,5},{7,4},{8,11},{9,10},{10,... | collective-permute-start | bytes 50696 | tf_op jit(solution)/shard_map/ppermute | solution.py:332
  34.9 1.5 %collective-permute-start.11 = (f32[1,4224]{1,0:T(1,128)S(1)}, f32[1,4224]{1,0:T(1,128)S(1)}, u32[]{:S(2)}, u32[]{:S(2)}) collective-permute-start(f32[1,4224]{1,0:T(1,128)S(1)} %get-tuple-element.39), channel_id=1, source_target_pairs={{0,2},{1,3},{2,0},{3,1},{4,6},{5,7},{6,4},{7,5},{8,10},{9,11},{10,... | collective-permute-start | bytes 50696 | tf_op jit(solution)/shard_map/ppermute | solution.py:332
  36.4 0.0 collective-permute-start.12
  36.4 0.6 %collective-permute-done.10 = f32[1,4224]{1,0:T(1,128)S(1)} collective-permute-done((f32[1,4224]{1,0:T(1,128)S(1)}, f32[1,4224]{1,0:T(1,128)S(1)}, u32[]{:S(2)}, u32[]{:S(2)}) %collective-permute-start.10) | collective-permute-done | bytes 16928 | tf_op jit(solution)/shard_map/ppermute | solution.py:332
  37.1 1.6 %collective-permute-done.11 = f32[1,4224]{1,0:T(1,128)S(1)} collective-permute-done((f32[1,4224]{1,0:T(1,128)S(1)}, f32[1,4224]{1,0:T(1,128)S(1)}, u32[]{:S(2)}, u32[]{:S(2)}) %collective-permute-start.11) | collective-permute-done | bytes 16928 | tf_op jit(solution)/shard_map/ppermute | solution.py:332
  38.6 0.0 collective-permute-done.12
  38.7 0.5 collective-permute-start.13
  39.1 0.5 %collective-permute-start.14 = (f32[1,4224]{1,0:T(1,128)S(1)}, f32[1,4224]{1,0:T(1,128)S(1)}, u32[]{:S(2)}, u32[]{:S(2)}) collective-permute-start(f32[1,4224]{1,0:T(1,128)S(1)} %add_add_fusion.refs_3_), channel_id=1, source_target_pairs={{0,9},{1,8},{2,11},{3,10},{4,13},{5,12},{6,15},{7,14},{8,1},{9,0},... | collective-permute-start | bytes 50696 | tf_op jit(solution)/shard_map/ppermute | solution.py:332
  39.7 2.1 %collective-permute-start.15 = (f32[1,4224]{1,0:T(1,128)S(1)}, f32[1,4224]{1,0:T(1,128)S(1)}, u32[]{:S(2)}, u32[]{:S(2)}) collective-permute-start(f32[1,4224]{1,0:T(1,128)S(1)} %add_add_fusion.refs_3_), channel_id=1, source_target_pairs={{0,5},{1,4},{2,7},{3,6},{4,1},{5,0},{6,3},{7,2},{8,13},{9,12},{10,... | collective-permute-start | bytes 50696 | tf_op jit(solution)/shard_map/ppermute | solution.py:332
  41.8 0.7 %collective-permute-start.18 = (f32[16,512]{1,0:T(8,128)S(1)}, f32[16,512]{1,0:T(8,128)S(1)}, u32[]{:S(2)}, u32[]{:S(2)}) collective-permute-start(f32[16,512]{1,0:T(8,128)S(1)} %get-tuple-element.42.refs_4_), channel_id=1, source_target_pairs={{16,17},{17,16},{18,19},{19,18},{20,21},{21,20},{22,23},{23,22},{2... | collective-permute-start | bytes 98312 | tf_op jit(solution)/shard_map/ppermute | solution.py:349
  42.4 1.3 %collective-permute-done.13.refs_0_ = f32[1,4224]{1,0:T(1,128)S(1)} collective-permute-done((f32[1,4224]{1,0:T(1,128)S(1)}, f32[1,4224]{1,0:T(1,128)S(1)}, u32[]{:S(2)}, u32[]{:S(2)}) %collective-permute-start.13) | collective-permute-done | bytes 16928 | tf_op jit(solution)/shard_map/ppermute | solution.py:332
  43.7 0.0 collective-permute-done.14.refs_1_
  43.7 0.0 collective-permute-done.15.refs_2_
  43.7 1.3 %shard_map.75 = (f32[8,256]{1,0:T(8,128)S(1)}, f32[8,640]{1,0:T(8,128)S(1)}) custom-call(f32[1,4224]{1,0:T(1,128)S(1)} %collective-permute-done.13.refs_0_, f32[1,4224]{1,0:T(1,128)S(1)} %collective-permute-done.14.refs_1_, f32[1,4224]{1,0:T(1,128)S(1)} %collective-permute-done.15.refs_2_, f32[1,4224]{1,0:T(1,128)S(1)} %add_add_fusion.refs_3_, ...), custom_call_target="tpu_custom_call" | custom-call | tf_op jit(solution)/shard_map/pallas_call | solution.py:308
  45.0 2.4 %collective-permute-start.16 = (f32[8,640]{1,0:T(8,128)S(1)}, f32[8,640]{1,0:T(8,128)S(1)}, u32[]{:S(2)}, u32[]{:S(2)}) collective-permute-start(f32[8,640]{1,0:T(8,128)S(1)} %get-tuple-element.41.refs_2_), channel_id=1, source_target_pairs={{0,16},{1,17},{2,18},{3,19},{4,20},{5,21},{6,22},{7,23},{8,24},{9,... | collective-permute-start | bytes 61448 | tf_op jit(solution)/shard_map/ppermute | solution.py:349
  47.4 0.7 %collective-permute-start.17 = (f32[8,640]{1,0:T(8,128)S(1)}, f32[8,640]{1,0:T(8,128)S(1)}, u32[]{:S(2)}, u32[]{:S(2)}) collective-permute-start(f32[8,640]{1,0:T(8,128)S(1)} %get-tuple-element.41.refs_2_), channel_id=1, source_target_pairs={{16,17},{17,16},{18,19},{19,18},{20,21},{21,20},{22,23},{23,22},{2... | collective-permute-start | bytes 61448 | tf_op jit(solution)/shard_map/ppermute | solution.py:349
  48.1 0.0 collective-permute-done.18.refs_3_
  48.1 0.8 %collective-permute-done.16.refs_0_ = f32[8,640]{1,0:T(8,128)S(1)} collective-permute-done((f32[8,640]{1,0:T(8,128)S(1)}, f32[8,640]{1,0:T(8,128)S(1)}, u32[]{:S(2)}, u32[]{:S(2)}) %collective-permute-start.16) | collective-permute-done | bytes 20512 | tf_op jit(solution)/shard_map/ppermute | solution.py:349
  48.9 0.0 collective-permute-done.17.refs_1_
  48.9 0.6 %shard_map.76 = (f32[8,512]{1,0:T(8,128)}, f32[8,512]{1,0:T(8,128)}) custom-call(f32[8,640]{1,0:T(8,128)S(1)} %collective-permute-done.16.refs_0_, f32[8,640]{1,0:T(8,128)S(1)} %collective-permute-done.17.refs_1_, f32[8,640]{1,0:T(8,128)S(1)} %get-tuple-element.41.refs_2_, f32[16,512]{1,0:T(8,128)S(1)} %collective-permute-done.18.refs_3_, ...), custom_call_target="tpu_custom_call" | custom-call | tf_op jit(solution)/shard_map/pallas_call | solution.py:308
  (2 shorter events, 0.1 us)
Async XLA Ops:
  2.6 5.4 %collective-permute-start = (bf16[80,512]{1,0:T(8,128)(2,1)S(1)}, bf16[80,512]{1,0:T(8,128)(2,1)S(1)}, u32[]{:S(2)}, u32[]{:S(2)}) collective-permute-start(bf16[80,512]{1,0:T(8,128)(2,1)S(1)} %get-tuple-element.29.refs_2_), channel_id=1, source_target_pairs={{0,17},{1,16},{2,19},{3,18},{4,21},{5,20},{6,23},{7,22},{8,25},{9,... | collective-permute-start | bytes 245768 | tf_op jit(solution)/shard_map/ppermute | solution.py:349
  5.0 3.0 %collective-permute-start.1 = (bf16[80,512]{1,0:T(8,128)(2,1)S(1)}, bf16[80,512]{1,0:T(8,128)(2,1)S(1)}, u32[]{:S(2)}, u32[]{:S(2)}) collective-permute-start(bf16[80,512]{1,0:T(8,128)(2,1)S(1)} %get-tuple-element.29.refs_2_), channel_id=1, source_target_pairs={{16,17},{17,16},{18,19},{19,18},{20,21},{21,20},{22,23},{23,22},{2... | collective-permute-start | bytes 245768 | tf_op jit(solution)/shard_map/ppermute | solution.py:349
  10.6 4.0 %collective-permute-start.2 = (f32[8,512]{1,0:T(8,128)S(1)}, f32[8,512]{1,0:T(8,128)S(1)}, u32[]{:S(2)}, u32[]{:S(2)}) collective-permute-start(f32[8,512]{1,0:T(8,128)S(1)} %get-tuple-element.30.refs_1_), channel_id=1, source_target_pairs={{0,17},{1,16},{2,19},{3,18},{4,21},{5,20},{6,23},{7,22},{8,25},{9,... | collective-permute-start | bytes 49160 | tf_op jit(solution)/shard_map/ppermute | solution.py:349
  15.9 3.2 %collective-permute-start.3 = (f32[1,4224]{1,0:T(1,128)S(1)}, f32[1,4224]{1,0:T(1,128)S(1)}, u32[]{:S(2)}, u32[]{:S(2)}) collective-permute-start(f32[1,4224]{1,0:T(1,128)S(1)} %get-tuple-element.34), channel_id=1, source_target_pairs={{0,3},{1,2},{2,1},{3,0},{4,7},{5,6},{6,5},{7,4},{8,11},{9,10},{10,... | collective-permute-start | bytes 50696 | tf_op jit(solution)/shard_map/ppermute | solution.py:332
  17.4 3.7 %collective-permute-start.4 = (f32[1,4224]{1,0:T(1,128)S(1)}, f32[1,4224]{1,0:T(1,128)S(1)}, u32[]{:S(2)}, u32[]{:S(2)}) collective-permute-start(f32[1,4224]{1,0:T(1,128)S(1)} %get-tuple-element.34), channel_id=1, source_target_pairs={{0,2},{1,3},{2,0},{3,1},{4,6},{5,7},{6,4},{7,5},{8,10},{9,11},{10,... | collective-permute-start | bytes 50696 | tf_op jit(solution)/shard_map/ppermute | solution.py:332
  17.9 3.3 %collective-permute-start.5 = (f32[1,4224]{1,0:T(1,128)S(1)}, f32[1,4224]{1,0:T(1,128)S(1)}, u32[]{:S(2)}, u32[]{:S(2)}) collective-permute-start(f32[1,4224]{1,0:T(1,128)S(1)} %get-tuple-element.34), channel_id=1, source_target_pairs={{0,1},{1,0},{2,3},{3,2},{4,5},{5,4},{6,7},{7,6},{8,9},{9,8},{10,11... | collective-permute-start | bytes 50696 | tf_op jit(solution)/shard_map/ppermute | solution.py:332
  21.2 5.0 %collective-permute-start.6 = (f32[1,4224]{1,0:T(1,128)S(1)}, f32[1,4224]{1,0:T(1,128)S(1)}, u32[]{:S(2)}, u32[]{:S(2)}) collective-permute-start(f32[1,4224]{1,0:T(1,128)S(1)} %add_add_fusion.1.refs_3_), channel_id=1, source_target_pairs={{0,13},{1,12},{2,15},{3,14},{4,9},{5,8},{6,11},{7,10},{8,5},{9,4},... | collective-permute-start | bytes 50696 | tf_op jit(solution)/shard_map/ppermute | solution.py:332
  23.5 4.1 %collective-permute-start.7 = (f32[1,4224]{1,0:T(1,128)S(1)}, f32[1,4224]{1,0:T(1,128)S(1)}, u32[]{:S(2)}, u32[]{:S(2)}) collective-permute-start(f32[1,4224]{1,0:T(1,128)S(1)} %add_add_fusion.1.refs_3_), channel_id=1, source_target_pairs={{0,9},{1,8},{2,11},{3,10},{4,13},{5,12},{6,15},{7,14},{8,1},{9,0},... | collective-permute-start | bytes 50696 | tf_op jit(solution)/shard_map/ppermute | solution.py:332
  24.0 3.5 %collective-permute-start.8 = (f32[1,4224]{1,0:T(1,128)S(1)}, f32[1,4224]{1,0:T(1,128)S(1)}, u32[]{:S(2)}, u32[]{:S(2)}) collective-permute-start(f32[1,4224]{1,0:T(1,128)S(1)} %add_add_fusion.1.refs_3_), channel_id=1, source_target_pairs={{0,5},{1,4},{2,7},{3,6},{4,1},{5,0},{6,3},{7,2},{8,13},{9,12},{10,... | collective-permute-start | bytes 50696 | tf_op jit(solution)/shard_map/ppermute | solution.py:332
  28.8 3.8 %collective-permute-start.9 = (f32[8,640]{1,0:T(8,128)S(1)}, f32[8,640]{1,0:T(8,128)S(1)}, u32[]{:S(2)}, u32[]{:S(2)}) collective-permute-start(f32[8,640]{1,0:T(8,128)S(1)} %get-tuple-element.36.refs_1_), channel_id=1, source_target_pairs={{0,17},{1,16},{2,19},{3,18},{4,21},{5,20},{6,23},{7,22},{8,25},{9,... | collective-permute-start | bytes 61448 | tf_op jit(solution)/shard_map/ppermute | solution.py:349
  33.8 3.2 %collective-permute-start.10 = (f32[1,4224]{1,0:T(1,128)S(1)}, f32[1,4224]{1,0:T(1,128)S(1)}, u32[]{:S(2)}, u32[]{:S(2)}) collective-permute-start(f32[1,4224]{1,0:T(1,128)S(1)} %get-tuple-element.39), channel_id=1, source_target_pairs={{0,3},{1,2},{2,1},{3,0},{4,7},{5,6},{6,5},{7,4},{8,11},{9,10},{10,... | collective-permute-start | bytes 50696 | tf_op jit(solution)/shard_map/ppermute | solution.py:332
  34.9 3.7 %collective-permute-start.11 = (f32[1,4224]{1,0:T(1,128)S(1)}, f32[1,4224]{1,0:T(1,128)S(1)}, u32[]{:S(2)}, u32[]{:S(2)}) collective-permute-start(f32[1,4224]{1,0:T(1,128)S(1)} %get-tuple-element.39), channel_id=1, source_target_pairs={{0,2},{1,3},{2,0},{3,1},{4,6},{5,7},{6,4},{7,5},{8,10},{9,11},{10,... | collective-permute-start | bytes 50696 | tf_op jit(solution)/shard_map/ppermute | solution.py:332
  36.4 2.2 %collective-permute-start.12 = (f32[1,4224]{1,0:T(1,128)S(1)}, f32[1,4224]{1,0:T(1,128)S(1)}, u32[]{:S(2)}, u32[]{:S(2)}) collective-permute-start(f32[1,4224]{1,0:T(1,128)S(1)} %get-tuple-element.39), channel_id=1, source_target_pairs={{0,1},{1,0},{2,3},{3,2},{4,5},{5,4},{6,7},{7,6},{8,9},{9,8},{10,11... | collective-permute-start | bytes 50696 | tf_op jit(solution)/shard_map/ppermute | solution.py:332
  38.7 5.1 %collective-permute-start.13 = (f32[1,4224]{1,0:T(1,128)S(1)}, f32[1,4224]{1,0:T(1,128)S(1)}, u32[]{:S(2)}, u32[]{:S(2)}) collective-permute-start(f32[1,4224]{1,0:T(1,128)S(1)} %add_add_fusion.refs_3_), channel_id=1, source_target_pairs={{0,13},{1,12},{2,15},{3,14},{4,9},{5,8},{6,11},{7,10},{8,5},{9,4},... | collective-permute-start | bytes 50696 | tf_op jit(solution)/shard_map/ppermute | solution.py:332
  39.1 4.6 %collective-permute-start.14 = (f32[1,4224]{1,0:T(1,128)S(1)}, f32[1,4224]{1,0:T(1,128)S(1)}, u32[]{:S(2)}, u32[]{:S(2)}) collective-permute-start(f32[1,4224]{1,0:T(1,128)S(1)} %add_add_fusion.refs_3_), channel_id=1, source_target_pairs={{0,9},{1,8},{2,11},{3,10},{4,13},{5,12},{6,15},{7,14},{8,1},{9,0},... | collective-permute-start | bytes 50696 | tf_op jit(solution)/shard_map/ppermute | solution.py:332
  39.7 4.1 %collective-permute-start.15 = (f32[1,4224]{1,0:T(1,128)S(1)}, f32[1,4224]{1,0:T(1,128)S(1)}, u32[]{:S(2)}, u32[]{:S(2)}) collective-permute-start(f32[1,4224]{1,0:T(1,128)S(1)} %add_add_fusion.refs_3_), channel_id=1, source_target_pairs={{0,5},{1,4},{2,7},{3,6},{4,1},{5,0},{6,3},{7,2},{8,13},{9,12},{10,... | collective-permute-start | bytes 50696 | tf_op jit(solution)/shard_map/ppermute | solution.py:332
  41.8 6.3 %collective-permute-start.18 = (f32[16,512]{1,0:T(8,128)S(1)}, f32[16,512]{1,0:T(8,128)S(1)}, u32[]{:S(2)}, u32[]{:S(2)}) collective-permute-start(f32[16,512]{1,0:T(8,128)S(1)} %get-tuple-element.42.refs_4_), channel_id=1, source_target_pairs={{16,17},{17,16},{18,19},{19,18},{20,21},{21,20},{22,23},{23,22},{2... | collective-permute-start | bytes 98312 | tf_op jit(solution)/shard_map/ppermute | solution.py:349
  45.0 3.9 %collective-permute-start.16 = (f32[8,640]{1,0:T(8,128)S(1)}, f32[8,640]{1,0:T(8,128)S(1)}, u32[]{:S(2)}, u32[]{:S(2)}) collective-permute-start(f32[8,640]{1,0:T(8,128)S(1)} %get-tuple-element.41.refs_2_), channel_id=1, source_target_pairs={{0,16},{1,17},{2,18},{3,19},{4,20},{5,21},{6,22},{7,23},{8,24},{9,... | collective-permute-start | bytes 61448 | tf_op jit(solution)/shard_map/ppermute | solution.py:349
  47.4 1.5 %collective-permute-start.17 = (f32[8,640]{1,0:T(8,128)S(1)}, f32[8,640]{1,0:T(8,128)S(1)}, u32[]{:S(2)}, u32[]{:S(2)}) collective-permute-start(f32[8,640]{1,0:T(8,128)S(1)} %get-tuple-element.41.refs_2_), channel_id=1, source_target_pairs={{16,17},{17,16},{18,19},{19,18},{20,21},{21,20},{22,23},{23,22},{2... | collective-permute-start | bytes 61448 | tf_op jit(solution)/shard_map/ppermute | solution.py:349

commit v16 on v15

--- a/solution.py
+++ b/solution.py
@@ -71,7 +71,7 @@
 
 
 def resident(moved, own):
-    return moved + own * (lax.axis_index("dp") == 0).astype(own.dtype)
+    return jnp.where(lax.axis_index("dp") == 0, own, moved)
 
 
 def home_total(refs):
@@ -340,8 +340,7 @@
     for group in range(groups):
         for place in range(count):
             to_group, to_place = target_of(group, place)
-            if (to_group, to_place) != (group, place):
-                pairs.append((group * count + place, to_group * count + to_place))
+            pairs.append((group * count + place, to_group * count + to_place))
     return pairs
 
 
@@ -354,7 +353,7 @@
 
 
 def beside(group, place):
-    return group, place ^ group
+    return group, place ^ 1
 
 
 def outward(group, place):

time: 49.7 us -> 49.4 us (level)
  starting transfers between devices: 23 us -> 22.3 us
    ppermute x7, starting transfers between devices: 11.2 us -> 10.5 us  [moved(): return lax.ppermute(value, ('dp', 'centers'), pairs_over(target_of))]
    ppermute x7, waiting for transfers between devices: 3.98 us -> 4.55 us  [moved(): return lax.ppermute(value, ('dp', 'centers'), pairs_over(target_of))]
    ppermute x12, waiting for transfers between devices: 9.08 us -> 8.54 us  [exchange(): parts.insert(0, lax.ppermute(value, axis, pairs))]
where the time goes in v16:
time: 49.4 us; the launch traced here: 48.9 us
  starting transfers between devices  22.3 us (45%)
  waiting for transfers between devices  13.1 us (27%)
  Pallas kernels  12.7 us (26%)
  between operations  0.7 us (1%)
    pallas_call x9, Pallas kernels, call(): pl.pallas_call(body, out_shape=out_shape, in_specs=sources or [VMEM] * le...  12.7 us
    ppermute x12, starting transfers between devices, exchange(): parts.insert(0, lax.ppermute(value, axis, pairs))  11.8 us
    ppermute x7, starting transfers between devices, moved(): return lax.ppermute(value, ('dp', 'centers'), pairs_over(target_of))  10.5 us
    ppermute x12, waiting for transfers between devices, exchange(): parts.insert(0, lax.ppermute(value, axis, pairs))  8.54 us
    ppermute x7, waiting for transfers between devices, moved(): return lax.ppermute(value, ('dp', 'centers'), pairs_over(target_of))  4.55 us
  transfers between devices with their start and end apart: 19, of which 10 were waited for; matrix products, arithmetic and copies ran while one was open for 0% of the time, Pallas kernels for 8%

profile of v16, /device:TPU:0, one launch (start us, length us, event | category | flops | bytes accessed | tf_op | source)
XLA Modules:
  0.0 48.9 jit_solution(1563689883722774075)
XLA Ops:
  0.6 2.0 %shard_map.68 = (bf16[64,4096]{1,0:T(8,128)(2,1)S(1)}, s32[1,4096]{1,0:T(1,128)S(1)}, f32[1,4096]{1,0:T(1,128)S(1)}, f32[1,512]{1,0:T(1,128)S(1)}, bf16[80,512]{1,0:T(8,128)(2,1)S(1)}) custom-call(bf16[64,4096]{1,0:T(8,128)(2,1)} %feat_hbm.1, s32[1,512]{1,0:T(1,128)} %bitcast.6, s32[1,4096]{1,0:T(1,128)} %bitcast.4, f32[1,4096]{1,0:T(1,128)} %bitcast.5, ...), custom_call_target="tpu_custom_call" | custom-call | tf_op jit(solution)/shard_map/pallas_call | solution.py:308
  2.6 2.4 %collective-permute-start = (bf16[80,512]{1,0:T(8,128)(2,1)S(1)}, bf16[80,512]{1,0:T(8,128)(2,1)S(1)}, u32[]{:S(2)}, u32[]{:S(2)}) collective-permute-start(bf16[80,512]{1,0:T(8,128)(2,1)S(1)} %get-tuple-element.29.refs_2_), channel_id=1, source_target_pairs={{0,17},{1,16},{2,19},{3,18},{4,21},{5,20},{6,23},{7,22},{8,25},{9,... | collective-permute-start | bytes 245768 | tf_op jit(solution)/shard_map/ppermute | solution.py:348
  5.0 0.7 %collective-permute-start.1 = (bf16[80,512]{1,0:T(8,128)(2,1)S(1)}, bf16[80,512]{1,0:T(8,128)(2,1)S(1)}, u32[]{:S(2)}, u32[]{:S(2)}) collective-permute-start(bf16[80,512]{1,0:T(8,128)(2,1)S(1)} %get-tuple-element.29.refs_2_), channel_id=1, source_target_pairs={{0,1},{1,0},{2,3},{3,2},{4,5},{5,4},{6,7},{7,6},{8,9},{9,8},{10,11... | collective-permute-start | bytes 245768 | tf_op jit(solution)/shard_map/ppermute | solution.py:348
  5.7 0.7 %shard_map.69 = (bf16[256,4096]{1,0:T(8,128)(2,1)S(1)}, bf16[4096,256]{1,0:T(8,128)(2,1)S(1)}, bf16[16,4096]{1,0:T(8,128)(2,1)S(1)}) custom-call(bf16[64,4096]{1,0:T(8,128)(2,1)S(1)} %get-tuple-element.24.feat_ref, s32[1,4096]{1,0:T(1,128)S(1)} %get-tuple-element.25.slots_ref.refs_3_.refs_4_, f32[1,4096]{1,0:T(1,128)S(1)} %get-tuple-element.26.prices_ref), custom_call_target="tpu_custom_call" | custom-call | flops 4096000 | bytes 4194304 | tf_op jit(solution)/shard_map/pallas_call | solution.py:308
  6.4 1.7 %collective-permute-done.refs_0_ = bf16[80,512]{1,0:T(8,128)(2,1)S(1)} collective-permute-done((bf16[80,512]{1,0:T(8,128)(2,1)S(1)}, bf16[80,512]{1,0:T(8,128)(2,1)S(1)}, u32[]{:S(2)}, u32[]{:S(2)}) %collective-permute-start) | collective-permute-done | bytes 81952 | tf_op jit(solution)/shard_map/ppermute | solution.py:348
  8.0 0.0 collective-permute-done.1.refs_1_
  8.0 2.6 %shard_map.70 = (bf16[8192,512]{1,0:T(8,128)(2,1)S(1)}, bf16[256,512]{1,0:T(8,128)(2,1)S(1)}, f32[1,512]{1,0:T(1,128)S(1)}, f32[8,512]{1,0:T(8,128)S(1)}) custom-call(bf16[4096,256]{1,0:T(8,128)(2,1)S(1)} %get-tuple-element.27.turned_ref, bf16[16,4096]{1,0:T(8,128)(2,1)S(1)} %get-tuple-element.28.weight_ref, ...), custom_call_target="tpu_custom_call" | custom-call | flops 134217728 | bytes 8388608 | tf_op jit(solution)/shard_map/pallas_call | solution.py:308
  10.7 2.1 %collective-permute-start.2 = (f32[8,512]{1,0:T(8,128)S(1)}, f32[8,512]{1,0:T(8,128)S(1)}, u32[]{:S(2)}, u32[]{:S(2)}) collective-permute-start(f32[8,512]{1,0:T(8,128)S(1)} %get-tuple-element.30.refs_1_), channel_id=1, source_target_pairs={{0,17},{1,16},{2,19},{3,18},{4,21},{5,20},{6,23},{7,22},{8,25},{9,... | collective-permute-start | bytes 49160 | tf_op jit(solution)/shard_map/ppermute | solution.py:348
  12.7 1.9 %shard_map.71.refs_4_ = bf16[1024,4096]{1,0:T(8,128)(2,1)S(1)} custom-call(bf16[256,4096]{1,0:T(8,128)(2,1)S(1)} %get-tuple-element.32.columns_ref, bf16[256,512]{1,0:T(8,128)(2,1)S(1)} %get-tuple-element.33.center_ref), custom_call_target="tpu_custom_call" | custom-call | flops 134217728 | bytes 8388608 | tf_op jit(solution)/shard_map/pallas_call | solution.py:308
  14.6 0.0 collective-permute-done.2.refs_0_
  14.7 1.2 %shard_map.72 = (f32[8,512]{1,0:T(8,128)S(1)}, f32[1,4224]{1,0:T(1,128)S(1)}) custom-call(f32[8,512]{1,0:T(8,128)S(1)} %collective-permute-done.2.refs_0_, f32[8,512]{1,0:T(8,128)S(1)} %get-tuple-element.30.refs_1_, f32[1,512]{1,0:T(1,128)S(1)} %get-tuple-element.31.refs_2_, s32[1,4096]{1,0:T(1,128)S(1)} %get-tuple-element.25.slots_ref.refs_3_.refs_4_, ...), custom_call_target="tpu_custom_call" | custom-call | tf_op jit(solution)/shard_map/pallas_call | solution.py:308
  15.9 1.6 %collective-permute-start.3 = (f32[1,4224]{1,0:T(1,128)S(1)}, f32[1,4224]{1,0:T(1,128)S(1)}, u32[]{:S(2)}, u32[]{:S(2)}) collective-permute-start(f32[1,4224]{1,0:T(1,128)S(1)} %get-tuple-element.34), channel_id=1, source_target_pairs={{0,3},{1,2},{2,1},{3,0},{4,7},{5,6},{6,5},{7,4},{8,11},{9,10},{10,... | collective-permute-start | bytes 50696 | tf_op jit(solution)/shard_map/ppermute | solution.py:332
  17.5 0.5 %collective-permute-start.4 = (f32[1,4224]{1,0:T(1,128)S(1)}, f32[1,4224]{1,0:T(1,128)S(1)}, u32[]{:S(2)}, u32[]{:S(2)}) collective-permute-start(f32[1,4224]{1,0:T(1,128)S(1)} %get-tuple-element.34), channel_id=1, source_target_pairs={{0,2},{1,3},{2,0},{3,1},{4,6},{5,7},{6,4},{7,5},{8,10},{9,11},{10,... | collective-permute-start | bytes 50696 | tf_op jit(solution)/shard_map/ppermute | solution.py:332
  18.0 0.0 collective-permute-start.5
  18.0 1.2 %collective-permute-done.3 = f32[1,4224]{1,0:T(1,128)S(1)} collective-permute-done((f32[1,4224]{1,0:T(1,128)S(1)}, f32[1,4224]{1,0:T(1,128)S(1)}, u32[]{:S(2)}, u32[]{:S(2)}) %collective-permute-start.3) | collective-permute-done | bytes 16928 | tf_op jit(solution)/shard_map/ppermute | solution.py:332
  19.1 2.1 %collective-permute-done.4 = f32[1,4224]{1,0:T(1,128)S(1)} collective-permute-done((f32[1,4224]{1,0:T(1,128)S(1)}, f32[1,4224]{1,0:T(1,128)S(1)}, u32[]{:S(2)}, u32[]{:S(2)}) %collective-permute-start.4) | collective-permute-done | bytes 16928 | tf_op jit(solution)/shard_map/ppermute | solution.py:332
  21.2 0.0 collective-permute-done.5
  21.2 2.3 %collective-permute-start.6 = (f32[1,4224]{1,0:T(1,128)S(1)}, f32[1,4224]{1,0:T(1,128)S(1)}, u32[]{:S(2)}, u32[]{:S(2)}) collective-permute-start(f32[1,4224]{1,0:T(1,128)S(1)} %add_add_fusion.1.refs_3_), channel_id=1, source_target_pairs={{0,13},{1,12},{2,15},{3,14},{4,9},{5,8},{6,11},{7,10},{8,5},{9,4},... | collective-permute-start | bytes 50696 | tf_op jit(solution)/shard_map/ppermute | solution.py:332
  23.5 0.6 %collective-permute-start.7 = (f32[1,4224]{1,0:T(1,128)S(1)}, f32[1,4224]{1,0:T(1,128)S(1)}, u32[]{:S(2)}, u32[]{:S(2)}) collective-permute-start(f32[1,4224]{1,0:T(1,128)S(1)} %add_add_fusion.1.refs_3_), channel_id=1, source_target_pairs={{0,9},{1,8},{2,11},{3,10},{4,13},{5,12},{6,15},{7,14},{8,1},{9,0},... | collective-permute-start | bytes 50696 | tf_op jit(solution)/shard_map/ppermute | solution.py:332
  24.1 1.2 %collective-permute-start.8 = (f32[1,4224]{1,0:T(1,128)S(1)}, f32[1,4224]{1,0:T(1,128)S(1)}, u32[]{:S(2)}, u32[]{:S(2)}) collective-permute-start(f32[1,4224]{1,0:T(1,128)S(1)} %add_add_fusion.1.refs_3_), channel_id=1, source_target_pairs={{0,5},{1,4},{2,7},{3,6},{4,1},{5,0},{6,3},{7,2},{8,13},{9,12},{10,... | collective-permute-start | bytes 50696 | tf_op jit(solution)/shard_map/ppermute | solution.py:332
  25.3 1.0 %collective-permute-done.6.refs_0_ = f32[1,4224]{1,0:T(1,128)S(1)} collective-permute-done((f32[1,4224]{1,0:T(1,128)S(1)}, f32[1,4224]{1,0:T(1,128)S(1)}, u32[]{:S(2)}, u32[]{:S(2)}) %collective-permute-start.6) | collective-permute-done | bytes 16928 | tf_op jit(solution)/shard_map/ppermute | solution.py:332
  26.3 1.3 %collective-permute-done.7.refs_1_ = f32[1,4224]{1,0:T(1,128)S(1)} collective-permute-done((f32[1,4224]{1,0:T(1,128)S(1)}, f32[1,4224]{1,0:T(1,128)S(1)}, u32[]{:S(2)}, u32[]{:S(2)}) %collective-permute-start.7) | collective-permute-done | bytes 16928 | tf_op jit(solution)/shard_map/ppermute | solution.py:332
  27.6 0.0 collective-permute-done.8.refs_2_
  27.6 1.2 %shard_map.73 = (f32[1,4224]{1,0:T(1,128)S(1)}, f32[8,128]{1,0:T(8,128)S(1)}, f32[8,640]{1,0:T(8,128)S(1)}) custom-call(f32[1,4224]{1,0:T(1,128)S(1)} %collective-permute-done.6.refs_0_, f32[1,4224]{1,0:T(1,128)S(1)} %collective-permute-done.7.refs_1_, f32[1,4224]{1,0:T(1,128)S(1)} %collective-permute-done.8.refs_2_, f32[1,4224]{1,0:T(1,128)S(1)} %add_add_fusion.1.refs_3_, ...), custom_call_target="tpu_custom_call" | custom-call | tf_op jit(solution)/shard_map/pallas_call | solution.py:308
  28.8 2.4 %collective-permute-start.9 = (f32[8,640]{1,0:T(8,128)S(1)}, f32[8,640]{1,0:T(8,128)S(1)}, u32[]{:S(2)}, u32[]{:S(2)}) collective-permute-start(f32[8,640]{1,0:T(8,128)S(1)} %get-tuple-element.36.refs_1_), channel_id=1, source_target_pairs={{0,17},{1,16},{2,19},{3,18},{4,21},{5,20},{6,23},{7,22},{8,25},{9,... | collective-permute-start | bytes 61448 | tf_op jit(solution)/shard_map/ppermute | solution.py:348
  31.1 1.5 %collective-permute-done.9.refs_0_ = f32[8,640]{1,0:T(8,128)S(1)} collective-permute-done((f32[8,640]{1,0:T(8,128)S(1)}, f32[8,640]{1,0:T(8,128)S(1)}, u32[]{:S(2)}, u32[]{:S(2)}) %collective-permute-start.9) | collective-permute-done | bytes 20512 | tf_op jit(solution)/shard_map/ppermute | solution.py:348
  32.6 1.2 %shard_map.74 = (f32[16,512]{1,0:T(8,128)S(1)}, f32[8,128]{1,0:T(8,128)S(1)}, f32[1,4224]{1,0:T(1,128)S(1)}) custom-call(f32[8,640]{1,0:T(8,128)S(1)} %collective-permute-done.9.refs_0_, f32[8,640]{1,0:T(8,128)S(1)} %get-tuple-element.36.refs_1_, f32[1,512]{1,0:T(1,128)S(1)} %get-tuple-element.31.refs_2_, ...), custom_call_target="tpu_custom_call" | custom-call | tf_op jit(solution)/shard_map/pallas_call | solution.py:308
  33.8 1.1 %collective-permute-start.10 = (f32[1,4224]{1,0:T(1,128)S(1)}, f32[1,4224]{1,0:T(1,128)S(1)}, u32[]{:S(2)}, u32[]{:S(2)}) collective-permute-start(f32[1,4224]{1,0:T(1,128)S(1)} %get-tuple-element.39), channel_id=1, source_target_pairs={{0,3},{1,2},{2,1},{3,0},{4,7},{5,6},{6,5},{7,4},{8,11},{9,10},{10,... | collective-permute-start | bytes 50696 | tf_op jit(solution)/shard_map/ppermute | solution.py:332
  34.9 1.5 %collective-permute-start.11 = (f32[1,4224]{1,0:T(1,128)S(1)}, f32[1,4224]{1,0:T(1,128)S(1)}, u32[]{:S(2)}, u32[]{:S(2)}) collective-permute-start(f32[1,4224]{1,0:T(1,128)S(1)} %get-tuple-element.39), channel_id=1, source_target_pairs={{0,2},{1,3},{2,0},{3,1},{4,6},{5,7},{6,4},{7,5},{8,10},{9,11},{10,... | collective-permute-start | bytes 50696 | tf_op jit(solution)/shard_map/ppermute | solution.py:332
  36.4 0.0 collective-permute-start.12
  36.4 0.6 %collective-permute-done.10 = f32[1,4224]{1,0:T(1,128)S(1)} collective-permute-done((f32[1,4224]{1,0:T(1,128)S(1)}, f32[1,4224]{1,0:T(1,128)S(1)}, u32[]{:S(2)}, u32[]{:S(2)}) %collective-permute-start.10) | collective-permute-done | bytes 16928 | tf_op jit(solution)/shard_map/ppermute | solution.py:332
  37.1 1.6 %collective-permute-done.11 = f32[1,4224]{1,0:T(1,128)S(1)} collective-permute-done((f32[1,4224]{1,0:T(1,128)S(1)}, f32[1,4224]{1,0:T(1,128)S(1)}, u32[]{:S(2)}, u32[]{:S(2)}) %collective-permute-start.11) | collective-permute-done | bytes 16928 | tf_op jit(solution)/shard_map/ppermute | solution.py:332
  38.6 0.0 collective-permute-done.12
  38.7 0.5 collective-permute-start.13
  39.1 0.5 %collective-permute-start.14 = (f32[1,4224]{1,0:T(1,128)S(1)}, f32[1,4224]{1,0:T(1,128)S(1)}, u32[]{:S(2)}, u32[]{:S(2)}) collective-permute-start(f32[1,4224]{1,0:T(1,128)S(1)} %add_add_fusion.refs_3_), channel_id=1, source_target_pairs={{0,9},{1,8},{2,11},{3,10},{4,13},{5,12},{6,15},{7,14},{8,1},{9,0},... | collective-permute-start | bytes 50696 | tf_op jit(solution)/shard_map/ppermute | solution.py:332
  39.7 2.1 %collective-permute-start.15 = (f32[1,4224]{1,0:T(1,128)S(1)}, f32[1,4224]{1,0:T(1,128)S(1)}, u32[]{:S(2)}, u32[]{:S(2)}) collective-permute-start(f32[1,4224]{1,0:T(1,128)S(1)} %add_add_fusion.refs_3_), channel_id=1, source_target_pairs={{0,5},{1,4},{2,7},{3,6},{4,1},{5,0},{6,3},{7,2},{8,13},{9,12},{10,... | collective-permute-start | bytes 50696 | tf_op jit(solution)/shard_map/ppermute | solution.py:332
  41.8 1.2 %collective-permute-start.18 = (f32[16,512]{1,0:T(8,128)S(1)}, f32[16,512]{1,0:T(8,128)S(1)}, u32[]{:S(2)}, u32[]{:S(2)}) collective-permute-start(f32[16,512]{1,0:T(8,128)S(1)} %get-tuple-element.42.refs_4_), channel_id=1, source_target_pairs={{0,1},{1,0},{2,3},{3,2},{4,5},{5,4},{6,7},{7,6},{8,9},{9,8},{10,11... | collective-permute-start | bytes 98312 | tf_op jit(solution)/shard_map/ppermute | solution.py:348
  43.0 0.8 %collective-permute-done.13.refs_0_ = f32[1,4224]{1,0:T(1,128)S(1)} collective-permute-done((f32[1,4224]{1,0:T(1,128)S(1)}, f32[1,4224]{1,0:T(1,128)S(1)}, u32[]{:S(2)}, u32[]{:S(2)}) %collective-permute-start.13) | collective-permute-done | bytes 16928 | tf_op jit(solution)/shard_map/ppermute | solution.py:332
  43.7 0.0 collective-permute-done.14.refs_1_
  43.7 0.0 collective-permute-done.15.refs_2_
  43.8 1.3 %shard_map.75 = (f32[8,256]{1,0:T(8,128)S(1)}, f32[8,640]{1,0:T(8,128)S(1)}) custom-call(f32[1,4224]{1,0:T(1,128)S(1)} %collective-permute-done.13.refs_0_, f32[1,4224]{1,0:T(1,128)S(1)} %collective-permute-done.14.refs_1_, f32[1,4224]{1,0:T(1,128)S(1)} %collective-permute-done.15.refs_2_, f32[1,4224]{1,0:T(1,128)S(1)} %add_add_fusion.refs_3_, ...), custom_call_target="tpu_custom_call" | custom-call | tf_op jit(solution)/shard_map/pallas_call | solution.py:308
  45.0 1.2 %collective-permute-start.16 = (f32[8,640]{1,0:T(8,128)S(1)}, f32[8,640]{1,0:T(8,128)S(1)}, u32[]{:S(2)}, u32[]{:S(2)}) collective-permute-start(f32[8,640]{1,0:T(8,128)S(1)} %get-tuple-element.41.refs_2_), channel_id=1, source_target_pairs={{0,16},{1,17},{2,18},{3,19},{4,20},{5,21},{6,22},{7,23},{8,24},{9,... | collective-permute-start | bytes 61448 | tf_op jit(solution)/shard_map/ppermute | solution.py:348
  46.3 0.6 %collective-permute-start.17 = (f32[8,640]{1,0:T(8,128)S(1)}, f32[8,640]{1,0:T(8,128)S(1)}, u32[]{:S(2)}, u32[]{:S(2)}) collective-permute-start(f32[8,640]{1,0:T(8,128)S(1)} %get-tuple-element.41.refs_2_), channel_id=1, source_target_pairs={{0,1},{1,0},{2,3},{3,2},{4,5},{5,4},{6,7},{7,6},{8,9},{9,8},{10,11... | collective-permute-start | bytes 61448 | tf_op jit(solution)/shard_map/ppermute | solution.py:348
  46.8 0.0 collective-permute-done.18.refs_3_
  46.8 1.4 %collective-permute-done.16.refs_0_ = f32[8,640]{1,0:T(8,128)S(1)} collective-permute-done((f32[8,640]{1,0:T(8,128)S(1)}, f32[8,640]{1,0:T(8,128)S(1)}, u32[]{:S(2)}, u32[]{:S(2)}) %collective-permute-start.16) | collective-permute-done | bytes 20512 | tf_op jit(solution)/shard_map/ppermute | solution.py:348
  48.2 0.0 collective-permute-done.17.refs_1_
  48.2 0.6 %shard_map.76 = (f32[8,512]{1,0:T(8,128)}, f32[8,512]{1,0:T(8,128)}) custom-call(f32[8,640]{1,0:T(8,128)S(1)} %collective-permute-done.16.refs_0_, f32[8,640]{1,0:T(8,128)S(1)} %collective-permute-done.17.refs_1_, f32[8,640]{1,0:T(8,128)S(1)} %get-tuple-element.41.refs_2_, f32[16,512]{1,0:T(8,128)S(1)} %collective-permute-done.18.refs_3_, ...), custom_call_target="tpu_custom_call" | custom-call | tf_op jit(solution)/shard_map/pallas_call | solution.py:308
  (2 shorter events, 0.1 us)
Async XLA Ops:
  2.6 5.4 %collective-permute-start = (bf16[80,512]{1,0:T(8,128)(2,1)S(1)}, bf16[80,512]{1,0:T(8,128)(2,1)S(1)}, u32[]{:S(2)}, u32[]{:S(2)}) collective-permute-start(bf16[80,512]{1,0:T(8,128)(2,1)S(1)} %get-tuple-element.29.refs_2_), channel_id=1, source_target_pairs={{0,17},{1,16},{2,19},{3,18},{4,21},{5,20},{6,23},{7,22},{8,25},{9,... | collective-permute-start | bytes 245768 | tf_op jit(solution)/shard_map/ppermute | solution.py:348
  5.0 3.0 %collective-permute-start.1 = (bf16[80,512]{1,0:T(8,128)(2,1)S(1)}, bf16[80,512]{1,0:T(8,128)(2,1)S(1)}, u32[]{:S(2)}, u32[]{:S(2)}) collective-permute-start(bf16[80,512]{1,0:T(8,128)(2,1)S(1)} %get-tuple-element.29.refs_2_), channel_id=1, source_target_pairs={{0,1},{1,0},{2,3},{3,2},{4,5},{5,4},{6,7},{7,6},{8,9},{9,8},{10,11... | collective-permute-start | bytes 245768 | tf_op jit(solution)/shard_map/ppermute | solution.py:348
  10.7 4.0 %collective-permute-start.2 = (f32[8,512]{1,0:T(8,128)S(1)}, f32[8,512]{1,0:T(8,128)S(1)}, u32[]{:S(2)}, u32[]{:S(2)}) collective-permute-start(f32[8,512]{1,0:T(8,128)S(1)} %get-tuple-element.30.refs_1_), channel_id=1, source_target_pairs={{0,17},{1,16},{2,19},{3,18},{4,21},{5,20},{6,23},{7,22},{8,25},{9,... | collective-permute-start | bytes 49160 | tf_op jit(solution)/shard_map/ppermute | solution.py:348
  15.9 3.3 %collective-permute-start.3 = (f32[1,4224]{1,0:T(1,128)S(1)}, f32[1,4224]{1,0:T(1,128)S(1)}, u32[]{:S(2)}, u32[]{:S(2)}) collective-permute-start(f32[1,4224]{1,0:T(1,128)S(1)} %get-tuple-element.34), channel_id=1, source_target_pairs={{0,3},{1,2},{2,1},{3,0},{4,7},{5,6},{6,5},{7,4},{8,11},{9,10},{10,... | collective-permute-start | bytes 50696 | tf_op jit(solution)/shard_map/ppermute | solution.py:332
  17.5 3.7 %collective-permute-start.4 = (f32[1,4224]{1,0:T(1,128)S(1)}, f32[1,4224]{1,0:T(1,128)S(1)}, u32[]{:S(2)}, u32[]{:S(2)}) collective-permute-start(f32[1,4224]{1,0:T(1,128)S(1)} %get-tuple-element.34), channel_id=1, source_target_pairs={{0,2},{1,3},{2,0},{3,1},{4,6},{5,7},{6,4},{7,5},{8,10},{9,11},{10,... | collective-permute-start | bytes 50696 | tf_op jit(solution)/shard_map/ppermute | solution.py:332
  18.0 3.2 %collective-permute-start.5 = (f32[1,4224]{1,0:T(1,128)S(1)}, f32[1,4224]{1,0:T(1,128)S(1)}, u32[]{:S(2)}, u32[]{:S(2)}) collective-permute-start(f32[1,4224]{1,0:T(1,128)S(1)} %get-tuple-element.34), channel_id=1, source_target_pairs={{0,1},{1,0},{2,3},{3,2},{4,5},{5,4},{6,7},{7,6},{8,9},{9,8},{10,11... | collective-permute-start | bytes 50696 | tf_op jit(solution)/shard_map/ppermute | solution.py:332
  21.2 5.0 %collective-permute-start.6 = (f32[1,4224]{1,0:T(1,128)S(1)}, f32[1,4224]{1,0:T(1,128)S(1)}, u32[]{:S(2)}, u32[]{:S(2)}) collective-permute-start(f32[1,4224]{1,0:T(1,128)S(1)} %add_add_fusion.1.refs_3_), channel_id=1, source_target_pairs={{0,13},{1,12},{2,15},{3,14},{4,9},{5,8},{6,11},{7,10},{8,5},{9,4},... | collective-permute-start | bytes 50696 | tf_op jit(solution)/shard_map/ppermute | solution.py:332
  23.5 4.1 %collective-permute-start.7 = (f32[1,4224]{1,0:T(1,128)S(1)}, f32[1,4224]{1,0:T(1,128)S(1)}, u32[]{:S(2)}, u32[]{:S(2)}) collective-permute-start(f32[1,4224]{1,0:T(1,128)S(1)} %add_add_fusion.1.refs_3_), channel_id=1, source_target_pairs={{0,9},{1,8},{2,11},{3,10},{4,13},{5,12},{6,15},{7,14},{8,1},{9,0},... | collective-permute-start | bytes 50696 | tf_op jit(solution)/shard_map/ppermute | solution.py:332
  24.1 3.5 %collective-permute-start.8 = (f32[1,4224]{1,0:T(1,128)S(1)}, f32[1,4224]{1,0:T(1,128)S(1)}, u32[]{:S(2)}, u32[]{:S(2)}) collective-permute-start(f32[1,4224]{1,0:T(1,128)S(1)} %add_add_fusion.1.refs_3_), channel_id=1, source_target_pairs={{0,5},{1,4},{2,7},{3,6},{4,1},{5,0},{6,3},{7,2},{8,13},{9,12},{10,... | collective-permute-start | bytes 50696 | tf_op jit(solution)/shard_map/ppermute | solution.py:332
  28.8 3.8 %collective-permute-start.9 = (f32[8,640]{1,0:T(8,128)S(1)}, f32[8,640]{1,0:T(8,128)S(1)}, u32[]{:S(2)}, u32[]{:S(2)}) collective-permute-start(f32[8,640]{1,0:T(8,128)S(1)} %get-tuple-element.36.refs_1_), channel_id=1, source_target_pairs={{0,17},{1,16},{2,19},{3,18},{4,21},{5,20},{6,23},{7,22},{8,25},{9,... | collective-permute-start | bytes 61448 | tf_op jit(solution)/shard_map/ppermute | solution.py:348
  33.8 3.2 %collective-permute-start.10 = (f32[1,4224]{1,0:T(1,128)S(1)}, f32[1,4224]{1,0:T(1,128)S(1)}, u32[]{:S(2)}, u32[]{:S(2)}) collective-permute-start(f32[1,4224]{1,0:T(1,128)S(1)} %get-tuple-element.39), channel_id=1, source_target_pairs={{0,3},{1,2},{2,1},{3,0},{4,7},{5,6},{6,5},{7,4},{8,11},{9,10},{10,... | collective-permute-start | bytes 50696 | tf_op jit(solution)/shard_map/ppermute | solution.py:332
  34.9 3.7 %collective-permute-start.11 = (f32[1,4224]{1,0:T(1,128)S(1)}, f32[1,4224]{1,0:T(1,128)S(1)}, u32[]{:S(2)}, u32[]{:S(2)}) collective-permute-start(f32[1,4224]{1,0:T(1,128)S(1)} %get-tuple-element.39), channel_id=1, source_target_pairs={{0,2},{1,3},{2,0},{3,1},{4,6},{5,7},{6,4},{7,5},{8,10},{9,11},{10,... | collective-permute-start | bytes 50696 | tf_op jit(solution)/shard_map/ppermute | solution.py:332
  36.4 2.2 %collective-permute-start.12 = (f32[1,4224]{1,0:T(1,128)S(1)}, f32[1,4224]{1,0:T(1,128)S(1)}, u32[]{:S(2)}, u32[]{:S(2)}) collective-permute-start(f32[1,4224]{1,0:T(1,128)S(1)} %get-tuple-element.39), channel_id=1, source_target_pairs={{0,1},{1,0},{2,3},{3,2},{4,5},{5,4},{6,7},{7,6},{8,9},{9,8},{10,11... | collective-permute-start | bytes 50696 | tf_op jit(solution)/shard_map/ppermute | solution.py:332
  38.7 5.1 %collective-permute-start.13 = (f32[1,4224]{1,0:T(1,128)S(1)}, f32[1,4224]{1,0:T(1,128)S(1)}, u32[]{:S(2)}, u32[]{:S(2)}) collective-permute-start(f32[1,4224]{1,0:T(1,128)S(1)} %add_add_fusion.refs_3_), channel_id=1, source_target_pairs={{0,13},{1,12},{2,15},{3,14},{4,9},{5,8},{6,11},{7,10},{8,5},{9,4},... | collective-permute-start | bytes 50696 | tf_op jit(solution)/shard_map/ppermute | solution.py:332
  39.1 4.6 %collective-permute-start.14 = (f32[1,4224]{1,0:T(1,128)S(1)}, f32[1,4224]{1,0:T(1,128)S(1)}, u32[]{:S(2)}, u32[]{:S(2)}) collective-permute-start(f32[1,4224]{1,0:T(1,128)S(1)} %add_add_fusion.refs_3_), channel_id=1, source_target_pairs={{0,9},{1,8},{2,11},{3,10},{4,13},{5,12},{6,15},{7,14},{8,1},{9,0},... | collective-permute-start | bytes 50696 | tf_op jit(solution)/shard_map/ppermute | solution.py:332
  39.7 4.1 %collective-permute-start.15 = (f32[1,4224]{1,0:T(1,128)S(1)}, f32[1,4224]{1,0:T(1,128)S(1)}, u32[]{:S(2)}, u32[]{:S(2)}) collective-permute-start(f32[1,4224]{1,0:T(1,128)S(1)} %add_add_fusion.refs_3_), channel_id=1, source_target_pairs={{0,5},{1,4},{2,7},{3,6},{4,1},{5,0},{6,3},{7,2},{8,13},{9,12},{10,... | collective-permute-start | bytes 50696 | tf_op jit(solution)/shard_map/ppermute | solution.py:332
  41.8 5.0 %collective-permute-start.18 = (f32[16,512]{1,0:T(8,128)S(1)}, f32[16,512]{1,0:T(8,128)S(1)}, u32[]{:S(2)}, u32[]{:S(2)}) collective-permute-start(f32[16,512]{1,0:T(8,128)S(1)} %get-tuple-element.42.refs_4_), channel_id=1, source_target_pairs={{0,1},{1,0},{2,3},{3,2},{4,5},{5,4},{6,7},{7,6},{8,9},{9,8},{10,11... | collective-permute-start | bytes 98312 | tf_op jit(solution)/shard_map/ppermute | solution.py:348
  45.0 3.2 %collective-permute-start.16 = (f32[8,640]{1,0:T(8,128)S(1)}, f32[8,640]{1,0:T(8,128)S(1)}, u32[]{:S(2)}, u32[]{:S(2)}) collective-permute-start(f32[8,640]{1,0:T(8,128)S(1)} %get-tuple-element.41.refs_2_), channel_id=1, source_target_pairs={{0,16},{1,17},{2,18},{3,19},{4,20},{5,21},{6,22},{7,23},{8,24},{9,... | collective-permute-start | bytes 61448 | tf_op jit(solution)/shard_map/ppermute | solution.py:348
  46.3 2.0 %collective-permute-start.17 = (f32[8,640]{1,0:T(8,128)S(1)}, f32[8,640]{1,0:T(8,128)S(1)}, u32[]{:S(2)}, u32[]{:S(2)}) collective-permute-start(f32[8,640]{1,0:T(8,128)S(1)} %get-tuple-element.41.refs_2_), channel_id=1, source_target_pairs={{0,1},{1,0},{2,3},{3,2},{4,5},{5,4},{6,7},{7,6},{8,9},{9,8},{10,11... | collective-permute-start | bytes 61448 | tf_op jit(solution)/shard_map/ppermute | solution.py:348

commit v17 on v16

--- a/solution.py
+++ b/solution.py
@@ -270,8 +270,10 @@
 
 def second_fold_body(parts, *refs):
     row_refs = refs[:parts]
-    slots_ref, block_ref, rows_ref, norm_ref, sums_ref, out_ref = refs[parts:]
+    slots_ref, block_ref, rows_ref, norm_ref, state_ref, sums_ref, out_ref, bundle_ref = refs[parts:]
     row_count = slots_ref.shape[1]
+    bundle_ref[SLOTS:, 0 : state_ref.shape[1]] = state_ref[...]
+    bundle_ref[SLOTS:, state_ref.shape[1] :] = jnp.zeros((2 * SLOTS, EXTRA), f32)
     latest = total_of(row_refs)
     norm = spread(from_lanes(latest[:, row_count:], 0))
     ratio = norm / norm_ref[...]
@@ -279,20 +281,22 @@
     sums_ref[:, EXTRA:] = spread(from_lanes(latest[:, row_count:], SLOTS))
     rows = latest[:, 0:row_count] + wide(ratio, row_count) * rows_ref[:, 0:row_count]
     fold_rows(rows, block_ref, slots_ref, out_ref)
+    bundle_ref[0:SLOTS, :] = out_ref[...]
 
 
 def finish_body(crossed, parts, inv_rows, *refs):
     fold_refs = refs[:parts]
-    (moved_ref, state_ref, scale_ref, step_ref, norm_ref, sums_ref,
+    (scale_ref, step_ref, norm_ref, sums_ref,
      coefficients_ref, out_ref) = refs[parts:]
     count = scale_ref.shape[1]
-    state = state_ref[...]
+    bundle = fold_refs[-1][...]
     if crossed:
-        folded = home_total(fold_refs)
-        state = resident(moved_ref[...], state)
+        far_ref, moved_ref = fold_refs[:-1]
+        bundle = resident(moved_ref[...], bundle)
+        folded = far_ref[...] + bundle[0:SLOTS]
     else:
-        folded = total_of(fold_refs)
-    target, residual = state[0:SLOTS], state[SLOTS:]
+        folded = total_of(fold_refs[:-1])
+    target, residual = bundle[SLOTS : 2 * SLOTS, 0:count], bundle[2 * SLOTS :, 0:count]
     first_norm = norm_ref[...]
     norm, cross = sums_ref[:, 0:EXTRA], sums_ref[:, EXTRA:]
     ratio = norm / first_norm
@@ -327,7 +331,8 @@
         span = min(4, size // stride)
         side = 0 if stride == 1 else 1
         parts = [value]
-        for offset in range(1, span):
+        offsets = (1, 3, 2) if stride == 1 else (1, 2, 3)
+        for offset in offsets[: span - 1]:
             pairs = [(i, i ^ (offset * stride) ^ side) for i in range(size)]
             parts.insert(0, lax.ppermute(value, axis, pairs))
         stride *= span
@@ -456,21 +461,23 @@
         *folds, scale, slots, turned, target, norm,
     )
     latest = exchange(latest, "centers")
-    sums, folded = call(
+    sums, folded, bundle = call(
         partial(second_fold_body, len(latest)),
-        (shaped((SLOTS, 2 * EXTRA)), fold_shape),
-        *latest, slots, block, rows, norm,
+        (
+            shaped((SLOTS, 2 * EXTRA)),
+            fold_shape,
+            shaped((3 * SLOTS, count + EXTRA)),
+        ),
+        *latest, slots, block, rows, norm, state,
     )
     if crossed:
-        folds = [moved(folded, homeward), moved(folded, beside), folded]
-        moved_state = moved(state, beside)
+        folds = [moved(folded, homeward), moved(bundle, beside), bundle]
     else:
-        folds = exchange(folded, "dp")
-        moved_state = state
+        folds = exchange(folded, "dp") + [bundle]
     return call(
         partial(finish_body, crossed, len(folds), 1.0 / all_rows),
         (vector, vector),
-        *folds, moved_state, state, own_scale, step, norm, sums,
+        *folds, own_scale, step, norm, sums,
     )
 
 

time: 49.4 us -> 49.1 us (level)
  waiting for transfers between devices: 13.1 us -> 14.4 us
  starting transfers between devices: 22.3 us -> 21.1 us
    ppermute x7 -> x6, starting transfers between devices: 10.5 us -> 8.71 us  [moved(): return lax.ppermute(value, ('dp', 'centers'), pairs_over(target_of))]
    ppermute x12, waiting for transfers between devices: 8.54 us -> 9.55 us  [exchange(): parts.insert(0, lax.ppermute(value, axis, pairs))]
    ppermute x12, starting transfers between devices: 11.8 us -> 12.4 us  [exchange(): parts.insert(0, lax.ppermute(value, axis, pairs))]
    ppermute x7 -> x6, waiting for transfers between devices: 4.55 us -> 4.9 us  [moved(): return lax.ppermute(value, ('dp', 'centers'), pairs_over(target_of))]
  transfers between devices with their start and end apart: 19 -> 18, of which waited for: 10 -> 12; matrix products, arithmetic and copies ran while one was open for 0% -> 0% of each run, Pallas kernels for 8% -> 5%
where the time goes in v17:
time: 49.1 us; the launch traced here: 49 us
  starting transfers between devices  21.1 us (43%)
  waiting for transfers between devices  14.4 us (29%)
  Pallas kernels  12.7 us (26%)
  between operations  0.7 us (1%)
    pallas_call x9, Pallas kernels, call(): pl.pallas_call(body, out_shape=out_shape, in_specs=sources or [VMEM] * le...  12.7 us
    ppermute x12, starting transfers between devices, exchange(): parts.insert(0, lax.ppermute(value, axis, pairs))  12.4 us
    ppermute x12, waiting for transfers between devices, exchange(): parts.insert(0, lax.ppermute(value, axis, pairs))  9.55 us
    ppermute x6, starting transfers between devices, moved(): return lax.ppermute(value, ('dp', 'centers'), pairs_over(target_of))  8.71 us
    ppermute x6, waiting for transfers between devices, moved(): return lax.ppermute(value, ('dp', 'centers'), pairs_over(target_of))  4.9 us
  transfers between devices with their start and end apart: 18, of which 12 were waited for; matrix products, arithmetic and copies ran while one was open for 0% of the time, Pallas kernels for 5%

profile of v17, /device:TPU:0, one launch (start us, length us, event | category | flops | bytes accessed | tf_op | source)
XLA Modules:
  0.0 49.0 jit_solution(2818877974535759909)
XLA Ops:
  0.6 2.0 %shard_map.68 = (bf16[64,4096]{1,0:T(8,128)(2,1)S(1)}, s32[1,4096]{1,0:T(1,128)S(1)}, f32[1,4096]{1,0:T(1,128)S(1)}, f32[1,512]{1,0:T(1,128)S(1)}, bf16[80,512]{1,0:T(8,128)(2,1)S(1)}) custom-call(bf16[64,4096]{1,0:T(8,128)(2,1)} %feat_hbm.1, s32[1,512]{1,0:T(1,128)} %bitcast.6, s32[1,4096]{1,0:T(1,128)} %bitcast.4, f32[1,4096]{1,0:T(1,128)} %bitcast.5, ...), custom_call_target="tpu_custom_call" | custom-call | tf_op jit(solution)/shard_map/pallas_call | solution.py:312
  2.6 2.4 %collective-permute-start = (bf16[80,512]{1,0:T(8,128)(2,1)S(1)}, bf16[80,512]{1,0:T(8,128)(2,1)S(1)}, u32[]{:S(2)}, u32[]{:S(2)}) collective-permute-start(bf16[80,512]{1,0:T(8,128)(2,1)S(1)} %get-tuple-element.30.refs_2_), channel_id=1, source_target_pairs={{0,17},{1,16},{2,19},{3,18},{4,21},{5,20},{6,23},{7,22},{8,25},{9,... | collective-permute-start | bytes 245768 | tf_op jit(solution)/shard_map/ppermute | solution.py:353
  5.0 0.7 %collective-permute-start.1 = (bf16[80,512]{1,0:T(8,128)(2,1)S(1)}, bf16[80,512]{1,0:T(8,128)(2,1)S(1)}, u32[]{:S(2)}, u32[]{:S(2)}) collective-permute-start(bf16[80,512]{1,0:T(8,128)(2,1)S(1)} %get-tuple-element.30.refs_2_), channel_id=1, source_target_pairs={{0,1},{1,0},{2,3},{3,2},{4,5},{5,4},{6,7},{7,6},{8,9},{9,8},{10,11... | collective-permute-start | bytes 245768 | tf_op jit(solution)/shard_map/ppermute | solution.py:353
  5.7 0.7 %shard_map.69 = (bf16[256,4096]{1,0:T(8,128)(2,1)S(1)}, bf16[4096,256]{1,0:T(8,128)(2,1)S(1)}, bf16[16,4096]{1,0:T(8,128)(2,1)S(1)}) custom-call(bf16[64,4096]{1,0:T(8,128)(2,1)S(1)} %get-tuple-element.25.feat_ref, s32[1,4096]{1,0:T(1,128)S(1)} %get-tuple-element.26.slots_ref.refs_3_.refs_4_, f32[1,4096]{1,0:T(1,128)S(1)} %get-tuple-element.27.prices_ref), custom_call_target="tpu_custom_call" | custom-call | flops 4096000 | bytes 4194304 | tf_op jit(solution)/shard_map/pallas_call | solution.py:312
  6.4 1.7 %collective-permute-done.refs_0_ = bf16[80,512]{1,0:T(8,128)(2,1)S(1)} collective-permute-done((bf16[80,512]{1,0:T(8,128)(2,1)S(1)}, bf16[80,512]{1,0:T(8,128)(2,1)S(1)}, u32[]{:S(2)}, u32[]{:S(2)}) %collective-permute-start) | collective-permute-done | bytes 81952 | tf_op jit(solution)/shard_map/ppermute | solution.py:353
  8.0 0.0 collective-permute-done.1.refs_1_
  8.0 2.6 %shard_map.70 = (bf16[8192,512]{1,0:T(8,128)(2,1)S(1)}, bf16[256,512]{1,0:T(8,128)(2,1)S(1)}, f32[1,512]{1,0:T(1,128)S(1)}, f32[8,512]{1,0:T(8,128)S(1)}) custom-call(bf16[4096,256]{1,0:T(8,128)(2,1)S(1)} %get-tuple-element.28.turned_ref, bf16[16,4096]{1,0:T(8,128)(2,1)S(1)} %get-tuple-element.29.weight_ref, ...), custom_call_target="tpu_custom_call" | custom-call | flops 134217728 | bytes 8388608 | tf_op jit(solution)/shard_map/pallas_call | solution.py:312
  10.7 2.1 %collective-permute-start.2 = (f32[8,512]{1,0:T(8,128)S(1)}, f32[8,512]{1,0:T(8,128)S(1)}, u32[]{:S(2)}, u32[]{:S(2)}) collective-permute-start(f32[8,512]{1,0:T(8,128)S(1)} %get-tuple-element.31.refs_1_), channel_id=1, source_target_pairs={{0,17},{1,16},{2,19},{3,18},{4,21},{5,20},{6,23},{7,22},{8,25},{9,... | collective-permute-start | bytes 49160 | tf_op jit(solution)/shard_map/ppermute | solution.py:353
  12.7 1.9 %shard_map.71.refs_4_ = bf16[1024,4096]{1,0:T(8,128)(2,1)S(1)} custom-call(bf16[256,4096]{1,0:T(8,128)(2,1)S(1)} %get-tuple-element.33.columns_ref, bf16[256,512]{1,0:T(8,128)(2,1)S(1)} %get-tuple-element.34.center_ref), custom_call_target="tpu_custom_call" | custom-call | flops 134217728 | bytes 8388608 | tf_op jit(solution)/shard_map/pallas_call | solution.py:312
  14.6 0.0 collective-permute-done.2.refs_0_
  14.7 1.2 %shard_map.72 = (f32[8,512]{1,0:T(8,128)S(1)}, f32[1,4224]{1,0:T(1,128)S(1)}) custom-call(f32[8,512]{1,0:T(8,128)S(1)} %collective-permute-done.2.refs_0_, f32[8,512]{1,0:T(8,128)S(1)} %get-tuple-element.31.refs_1_, f32[1,512]{1,0:T(1,128)S(1)} %get-tuple-element.32.refs_2_, s32[1,4096]{1,0:T(1,128)S(1)} %get-tuple-element.26.slots_ref.refs_3_.refs_4_, ...), custom_call_target="tpu_custom_call" | custom-call | tf_op jit(solution)/shard_map/pallas_call | solution.py:312
  15.9 1.6 %collective-permute-start.3 = (f32[1,4224]{1,0:T(1,128)S(1)}, f32[1,4224]{1,0:T(1,128)S(1)}, u32[]{:S(2)}, u32[]{:S(2)}) collective-permute-start(f32[1,4224]{1,0:T(1,128)S(1)} %get-tuple-element.35), channel_id=1, source_target_pairs={{0,2},{1,3},{2,0},{3,1},{4,6},{5,7},{6,4},{7,5},{8,10},{9,11},{10,... | collective-permute-start | bytes 50696 | tf_op jit(solution)/shard_map/ppermute | solution.py:337
  17.5 0.2 collective-permute-start.4
  17.7 0.4 collective-permute-start.5
  18.1 1.6 %collective-permute-done.3 = f32[1,4224]{1,0:T(1,128)S(1)} collective-permute-done((f32[1,4224]{1,0:T(1,128)S(1)}, f32[1,4224]{1,0:T(1,128)S(1)}, u32[]{:S(2)}, u32[]{:S(2)}) %collective-permute-start.3) | collective-permute-done | bytes 16928 | tf_op jit(solution)/shard_map/ppermute | solution.py:337
  19.7 0.9 %collective-permute-done.4 = f32[1,4224]{1,0:T(1,128)S(1)} collective-permute-done((f32[1,4224]{1,0:T(1,128)S(1)}, f32[1,4224]{1,0:T(1,128)S(1)}, u32[]{:S(2)}, u32[]{:S(2)}) %collective-permute-start.4) | collective-permute-done | bytes 16928 | tf_op jit(solution)/shard_map/ppermute | solution.py:337
  20.7 0.0 collective-permute-done.5
  20.7 3.4 %collective-permute-start.6 = (f32[1,4224]{1,0:T(1,128)S(1)}, f32[1,4224]{1,0:T(1,128)S(1)}, u32[]{:S(2)}, u32[]{:S(2)}) collective-permute-start(f32[1,4224]{1,0:T(1,128)S(1)} %add_add_fusion.1.refs_3_), channel_id=1, source_target_pairs={{0,13},{1,12},{2,15},{3,14},{4,9},{5,8},{6,11},{7,10},{8,5},{9,4},... | collective-permute-start | bytes 50696 | tf_op jit(solution)/shard_map/ppermute | solution.py:337
  24.1 0.0 collective-permute-start.7
  24.1 0.6 %collective-permute-start.8 = (f32[1,4224]{1,0:T(1,128)S(1)}, f32[1,4224]{1,0:T(1,128)S(1)}, u32[]{:S(2)}, u32[]{:S(2)}) collective-permute-start(f32[1,4224]{1,0:T(1,128)S(1)} %add_add_fusion.1.refs_3_), channel_id=1, source_target_pairs={{0,5},{1,4},{2,7},{3,6},{4,1},{5,0},{6,3},{7,2},{8,13},{9,12},{10,... | collective-permute-start | bytes 50696 | tf_op jit(solution)/shard_map/ppermute | solution.py:337
  24.7 1.0 %collective-permute-done.6.refs_0_ = f32[1,4224]{1,0:T(1,128)S(1)} collective-permute-done((f32[1,4224]{1,0:T(1,128)S(1)}, f32[1,4224]{1,0:T(1,128)S(1)}, u32[]{:S(2)}, u32[]{:S(2)}) %collective-permute-start.6) | collective-permute-done | bytes 16928 | tf_op jit(solution)/shard_map/ppermute | solution.py:337
  25.7 2.4 %collective-permute-done.7.refs_1_ = f32[1,4224]{1,0:T(1,128)S(1)} collective-permute-done((f32[1,4224]{1,0:T(1,128)S(1)}, f32[1,4224]{1,0:T(1,128)S(1)}, u32[]{:S(2)}, u32[]{:S(2)}) %collective-permute-start.7) | collective-permute-done | bytes 16928 | tf_op jit(solution)/shard_map/ppermute | solution.py:337
  28.2 0.0 collective-permute-done.8.refs_2_
  28.2 1.2 %shard_map.73 = (f32[1,4224]{1,0:T(1,128)S(1)}, f32[8,128]{1,0:T(8,128)S(1)}, f32[8,640]{1,0:T(8,128)S(1)}) custom-call(f32[1,4224]{1,0:T(1,128)S(1)} %collective-permute-done.6.refs_0_, f32[1,4224]{1,0:T(1,128)S(1)} %collective-permute-done.7.refs_1_, f32[1,4224]{1,0:T(1,128)S(1)} %collective-permute-done.8.refs_2_, f32[1,4224]{1,0:T(1,128)S(1)} %add_add_fusion.1.refs_3_, ...), custom_call_target="tpu_custom_call" | custom-call | tf_op jit(solution)/shard_map/pallas_call | solution.py:312
  29.4 1.7 %collective-permute-start.9 = (f32[8,640]{1,0:T(8,128)S(1)}, f32[8,640]{1,0:T(8,128)S(1)}, u32[]{:S(2)}, u32[]{:S(2)}) collective-permute-start(f32[8,640]{1,0:T(8,128)S(1)} %get-tuple-element.37.refs_1_), channel_id=1, source_target_pairs={{0,17},{1,16},{2,19},{3,18},{4,21},{5,20},{6,23},{7,22},{8,25},{9,... | collective-permute-start | bytes 61448 | tf_op jit(solution)/shard_map/ppermute | solution.py:353
  31.1 1.5 %collective-permute-done.9.refs_0_ = f32[8,640]{1,0:T(8,128)S(1)} collective-permute-done((f32[8,640]{1,0:T(8,128)S(1)}, f32[8,640]{1,0:T(8,128)S(1)}, u32[]{:S(2)}, u32[]{:S(2)}) %collective-permute-start.9) | collective-permute-done | bytes 20512 | tf_op jit(solution)/shard_map/ppermute | solution.py:353
  32.6 1.2 %shard_map.74 = (f32[16,512]{1,0:T(8,128)S(1)}, f32[8,128]{1,0:T(8,128)S(1)}, f32[1,4224]{1,0:T(1,128)S(1)}) custom-call(f32[8,640]{1,0:T(8,128)S(1)} %collective-permute-done.9.refs_0_, f32[8,640]{1,0:T(8,128)S(1)} %get-tuple-element.37.refs_1_, f32[1,512]{1,0:T(1,128)S(1)} %get-tuple-element.32.refs_2_, ...), custom_call_target="tpu_custom_call" | custom-call | tf_op jit(solution)/shard_map/pallas_call | solution.py:312
  33.8 0.7 %collective-permute-start.10 = (f32[1,4224]{1,0:T(1,128)S(1)}, f32[1,4224]{1,0:T(1,128)S(1)}, u32[]{:S(2)}, u32[]{:S(2)}) collective-permute-start(f32[1,4224]{1,0:T(1,128)S(1)} %get-tuple-element.40), channel_id=1, source_target_pairs={{0,2},{1,3},{2,0},{3,1},{4,6},{5,7},{6,4},{7,5},{8,10},{9,11},{10,... | collective-permute-start | bytes 50696 | tf_op jit(solution)/shard_map/ppermute | solution.py:337
  34.5 1.1 %collective-permute-start.11 = (f32[1,4224]{1,0:T(1,128)S(1)}, f32[1,4224]{1,0:T(1,128)S(1)}, u32[]{:S(2)}, u32[]{:S(2)}) collective-permute-start(f32[1,4224]{1,0:T(1,128)S(1)} %get-tuple-element.40), channel_id=1, source_target_pairs={{0,3},{1,2},{2,1},{3,0},{4,7},{5,6},{6,5},{7,4},{8,11},{9,10},{10,... | collective-permute-start | bytes 50696 | tf_op jit(solution)/shard_map/ppermute | solution.py:337
  35.7 0.3 collective-permute-start.12
  36.0 1.7 %collective-permute-done.10 = f32[1,4224]{1,0:T(1,128)S(1)} collective-permute-done((f32[1,4224]{1,0:T(1,128)S(1)}, f32[1,4224]{1,0:T(1,128)S(1)}, u32[]{:S(2)}, u32[]{:S(2)}) %collective-permute-start.10) | collective-permute-done | bytes 16928 | tf_op jit(solution)/shard_map/ppermute | solution.py:337
  37.7 0.1 collective-permute-done.11
  37.8 0.0 collective-permute-done.12
  37.8 1.4 %collective-permute-start.13 = (f32[1,4224]{1,0:T(1,128)S(1)}, f32[1,4224]{1,0:T(1,128)S(1)}, u32[]{:S(2)}, u32[]{:S(2)}) collective-permute-start(f32[1,4224]{1,0:T(1,128)S(1)} %add_add_fusion.refs_3_), channel_id=1, source_target_pairs={{0,13},{1,12},{2,15},{3,14},{4,9},{5,8},{6,11},{7,10},{8,5},{9,4},... | collective-permute-start | bytes 50696 | tf_op jit(solution)/shard_map/ppermute | solution.py:337
  39.3 0.6 %collective-permute-start.14 = (f32[1,4224]{1,0:T(1,128)S(1)}, f32[1,4224]{1,0:T(1,128)S(1)}, u32[]{:S(2)}, u32[]{:S(2)}) collective-permute-start(f32[1,4224]{1,0:T(1,128)S(1)} %add_add_fusion.refs_3_), channel_id=1, source_target_pairs={{0,9},{1,8},{2,11},{3,10},{4,13},{5,12},{6,15},{7,14},{8,1},{9,0},... | collective-permute-start | bytes 50696 | tf_op jit(solution)/shard_map/ppermute | solution.py:337
  39.9 1.9 %collective-permute-start.15 = (f32[1,4224]{1,0:T(1,128)S(1)}, f32[1,4224]{1,0:T(1,128)S(1)}, u32[]{:S(2)}, u32[]{:S(2)}) collective-permute-start(f32[1,4224]{1,0:T(1,128)S(1)} %add_add_fusion.refs_3_), channel_id=1, source_target_pairs={{0,5},{1,4},{2,7},{3,6},{4,1},{5,0},{6,3},{7,2},{8,13},{9,12},{10,... | collective-permute-start | bytes 50696 | tf_op jit(solution)/shard_map/ppermute | solution.py:337
  41.7 1.1 %collective-permute-done.13.refs_0_ = f32[1,4224]{1,0:T(1,128)S(1)} collective-permute-done((f32[1,4224]{1,0:T(1,128)S(1)}, f32[1,4224]{1,0:T(1,128)S(1)}, u32[]{:S(2)}, u32[]{:S(2)}) %collective-permute-start.13) | collective-permute-done | bytes 16928 | tf_op jit(solution)/shard_map/ppermute | solution.py:337
  42.9 0.6 %collective-permute-done.14.refs_1_ = f32[1,4224]{1,0:T(1,128)S(1)} collective-permute-done((f32[1,4224]{1,0:T(1,128)S(1)}, f32[1,4224]{1,0:T(1,128)S(1)}, u32[]{:S(2)}, u32[]{:S(2)}) %collective-permute-start.14) | collective-permute-done | bytes 16928 | tf_op jit(solution)/shard_map/ppermute | solution.py:337
  43.4 0.1 collective-permute-done.15.refs_2_
  43.5 1.3 %shard_map.75 = (f32[8,256]{1,0:T(8,128)S(1)}, f32[8,640]{1,0:T(8,128)S(1)}, f32[24,640]{1,0:T(8,128)S(1)}) custom-call(f32[1,4224]{1,0:T(1,128)S(1)} %collective-permute-done.13.refs_0_, f32[1,4224]{1,0:T(1,128)S(1)} %collective-permute-done.14.refs_1_, f32[1,4224]{1,0:T(1,128)S(1)} %collective-permute-done.15.refs_2_, f32[1,4224]{1,0:T(1,128)S(1)} %add_add_fusion.refs_3_, ...), custom_call_target="tpu_custom_call" | custom-call | tf_op jit(solution)/shard_map/pallas_call | solution.py:312
  44.8 0.3 collective-permute-start.17
  45.1 1.5 %collective-permute-start.16 = (f32[8,640]{1,0:T(8,128)S(1)}, f32[8,640]{1,0:T(8,128)S(1)}, u32[]{:S(2)}, u32[]{:S(2)}) collective-permute-start(f32[8,640]{1,0:T(8,128)S(1)} %get-tuple-element.43), channel_id=1, source_target_pairs={{0,16},{1,17},{2,18},{3,19},{4,20},{5,21},{6,22},{7,23},{8,24},{9,... | collective-permute-start | bytes 61448 | tf_op jit(solution)/shard_map/ppermute | solution.py:353
  46.6 1.7 %collective-permute-done.16.refs_0_ = f32[8,640]{1,0:T(8,128)S(1)} collective-permute-done((f32[8,640]{1,0:T(8,128)S(1)}, f32[8,640]{1,0:T(8,128)S(1)}, u32[]{:S(2)}, u32[]{:S(2)}) %collective-permute-start.16) | collective-permute-done | bytes 20512 | tf_op jit(solution)/shard_map/ppermute | solution.py:353
  48.3 0.0 collective-permute-done.17.refs_1_
  48.3 0.6 %shard_map.76 = (f32[8,512]{1,0:T(8,128)}, f32[8,512]{1,0:T(8,128)}) custom-call(f32[8,640]{1,0:T(8,128)S(1)} %collective-permute-done.16.refs_0_, f32[24,640]{1,0:T(8,128)S(1)} %collective-permute-done.17.refs_1_, f32[24,640]{1,0:T(8,128)S(1)} %get-tuple-element.44.refs_2_, f32[1,512]{1,0:T(1,128)S(1)} %get-tuple-element.45.refs_3_, ...), custom_call_target="tpu_custom_call" | custom-call | tf_op jit(solution)/shard_map/pallas_call | solution.py:312
  (2 shorter events, 0.1 us)
Async XLA Ops:
  2.6 5.4 %collective-permute-start = (bf16[80,512]{1,0:T(8,128)(2,1)S(1)}, bf16[80,512]{1,0:T(8,128)(2,1)S(1)}, u32[]{:S(2)}, u32[]{:S(2)}) collective-permute-start(bf16[80,512]{1,0:T(8,128)(2,1)S(1)} %get-tuple-element.30.refs_2_), channel_id=1, source_target_pairs={{0,17},{1,16},{2,19},{3,18},{4,21},{5,20},{6,23},{7,22},{8,25},{9,... | collective-permute-start | bytes 245768 | tf_op jit(solution)/shard_map/ppermute | solution.py:353
  5.0 3.0 %collective-permute-start.1 = (bf16[80,512]{1,0:T(8,128)(2,1)S(1)}, bf16[80,512]{1,0:T(8,128)(2,1)S(1)}, u32[]{:S(2)}, u32[]{:S(2)}) collective-permute-start(bf16[80,512]{1,0:T(8,128)(2,1)S(1)} %get-tuple-element.30.refs_2_), channel_id=1, source_target_pairs={{0,1},{1,0},{2,3},{3,2},{4,5},{5,4},{6,7},{7,6},{8,9},{9,8},{10,11... | collective-permute-start | bytes 245768 | tf_op jit(solution)/shard_map/ppermute | solution.py:353
  10.7 4.0 %collective-permute-start.2 = (f32[8,512]{1,0:T(8,128)S(1)}, f32[8,512]{1,0:T(8,128)S(1)}, u32[]{:S(2)}, u32[]{:S(2)}) collective-permute-start(f32[8,512]{1,0:T(8,128)S(1)} %get-tuple-element.31.refs_1_), channel_id=1, source_target_pairs={{0,17},{1,16},{2,19},{3,18},{4,21},{5,20},{6,23},{7,22},{8,25},{9,... | collective-permute-start | bytes 49160 | tf_op jit(solution)/shard_map/ppermute | solution.py:353
  15.9 3.8 %collective-permute-start.3 = (f32[1,4224]{1,0:T(1,128)S(1)}, f32[1,4224]{1,0:T(1,128)S(1)}, u32[]{:S(2)}, u32[]{:S(2)}) collective-permute-start(f32[1,4224]{1,0:T(1,128)S(1)} %get-tuple-element.35), channel_id=1, source_target_pairs={{0,2},{1,3},{2,0},{3,1},{4,6},{5,7},{6,4},{7,5},{8,10},{9,11},{10,... | collective-permute-start | bytes 50696 | tf_op jit(solution)/shard_map/ppermute | solution.py:337
  17.5 3.2 %collective-permute-start.4 = (f32[1,4224]{1,0:T(1,128)S(1)}, f32[1,4224]{1,0:T(1,128)S(1)}, u32[]{:S(2)}, u32[]{:S(2)}) collective-permute-start(f32[1,4224]{1,0:T(1,128)S(1)} %get-tuple-element.35), channel_id=1, source_target_pairs={{0,3},{1,2},{2,1},{3,0},{4,7},{5,6},{6,5},{7,4},{8,11},{9,10},{10,... | collective-permute-start | bytes 50696 | tf_op jit(solution)/shard_map/ppermute | solution.py:337
  17.7 3.0 %collective-permute-start.5 = (f32[1,4224]{1,0:T(1,128)S(1)}, f32[1,4224]{1,0:T(1,128)S(1)}, u32[]{:S(2)}, u32[]{:S(2)}) collective-permute-start(f32[1,4224]{1,0:T(1,128)S(1)} %get-tuple-element.35), channel_id=1, source_target_pairs={{0,1},{1,0},{2,3},{3,2},{4,5},{5,4},{6,7},{7,6},{8,9},{9,8},{10,11... | collective-permute-start | bytes 50696 | tf_op jit(solution)/shard_map/ppermute | solution.py:337
  20.7 5.0 %collective-permute-start.6 = (f32[1,4224]{1,0:T(1,128)S(1)}, f32[1,4224]{1,0:T(1,128)S(1)}, u32[]{:S(2)}, u32[]{:S(2)}) collective-permute-start(f32[1,4224]{1,0:T(1,128)S(1)} %add_add_fusion.1.refs_3_), channel_id=1, source_target_pairs={{0,13},{1,12},{2,15},{3,14},{4,9},{5,8},{6,11},{7,10},{8,5},{9,4},... | collective-permute-start | bytes 50696 | tf_op jit(solution)/shard_map/ppermute | solution.py:337
  24.1 4.1 %collective-permute-start.7 = (f32[1,4224]{1,0:T(1,128)S(1)}, f32[1,4224]{1,0:T(1,128)S(1)}, u32[]{:S(2)}, u32[]{:S(2)}) collective-permute-start(f32[1,4224]{1,0:T(1,128)S(1)} %add_add_fusion.1.refs_3_), channel_id=1, source_target_pairs={{0,9},{1,8},{2,11},{3,10},{4,13},{5,12},{6,15},{7,14},{8,1},{9,0},... | collective-permute-start | bytes 50696 | tf_op jit(solution)/shard_map/ppermute | solution.py:337
  24.1 4.1 %collective-permute-start.8 = (f32[1,4224]{1,0:T(1,128)S(1)}, f32[1,4224]{1,0:T(1,128)S(1)}, u32[]{:S(2)}, u32[]{:S(2)}) collective-permute-start(f32[1,4224]{1,0:T(1,128)S(1)} %add_add_fusion.1.refs_3_), channel_id=1, source_target_pairs={{0,5},{1,4},{2,7},{3,6},{4,1},{5,0},{6,3},{7,2},{8,13},{9,12},{10,... | collective-permute-start | bytes 50696 | tf_op jit(solution)/shard_map/ppermute | solution.py:337
  29.4 3.2 %collective-permute-start.9 = (f32[8,640]{1,0:T(8,128)S(1)}, f32[8,640]{1,0:T(8,128)S(1)}, u32[]{:S(2)}, u32[]{:S(2)}) collective-permute-start(f32[8,640]{1,0:T(8,128)S(1)} %get-tuple-element.37.refs_1_), channel_id=1, source_target_pairs={{0,17},{1,16},{2,19},{3,18},{4,21},{5,20},{6,23},{7,22},{8,25},{9,... | collective-permute-start | bytes 61448 | tf_op jit(solution)/shard_map/ppermute | solution.py:353
  33.8 3.9 %collective-permute-start.10 = (f32[1,4224]{1,0:T(1,128)S(1)}, f32[1,4224]{1,0:T(1,128)S(1)}, u32[]{:S(2)}, u32[]{:S(2)}) collective-permute-start(f32[1,4224]{1,0:T(1,128)S(1)} %get-tuple-element.40), channel_id=1, source_target_pairs={{0,2},{1,3},{2,0},{3,1},{4,6},{5,7},{6,4},{7,5},{8,10},{9,11},{10,... | collective-permute-start | bytes 50696 | tf_op jit(solution)/shard_map/ppermute | solution.py:337
  34.5 3.2 %collective-permute-start.11 = (f32[1,4224]{1,0:T(1,128)S(1)}, f32[1,4224]{1,0:T(1,128)S(1)}, u32[]{:S(2)}, u32[]{:S(2)}) collective-permute-start(f32[1,4224]{1,0:T(1,128)S(1)} %get-tuple-element.40), channel_id=1, source_target_pairs={{0,3},{1,2},{2,1},{3,0},{4,7},{5,6},{6,5},{7,4},{8,11},{9,10},{10,... | collective-permute-start | bytes 50696 | tf_op jit(solution)/shard_map/ppermute | solution.py:337
  35.7 2.1 %collective-permute-start.12 = (f32[1,4224]{1,0:T(1,128)S(1)}, f32[1,4224]{1,0:T(1,128)S(1)}, u32[]{:S(2)}, u32[]{:S(2)}) collective-permute-start(f32[1,4224]{1,0:T(1,128)S(1)} %get-tuple-element.40), channel_id=1, source_target_pairs={{0,1},{1,0},{2,3},{3,2},{4,5},{5,4},{6,7},{7,6},{8,9},{9,8},{10,11... | collective-permute-start | bytes 50696 | tf_op jit(solution)/shard_map/ppermute | solution.py:337
  37.8 5.0 %collective-permute-start.13 = (f32[1,4224]{1,0:T(1,128)S(1)}, f32[1,4224]{1,0:T(1,128)S(1)}, u32[]{:S(2)}, u32[]{:S(2)}) collective-permute-start(f32[1,4224]{1,0:T(1,128)S(1)} %add_add_fusion.refs_3_), channel_id=1, source_target_pairs={{0,13},{1,12},{2,15},{3,14},{4,9},{5,8},{6,11},{7,10},{8,5},{9,4},... | collective-permute-start | bytes 50696 | tf_op jit(solution)/shard_map/ppermute | solution.py:337
  39.3 4.2 %collective-permute-start.14 = (f32[1,4224]{1,0:T(1,128)S(1)}, f32[1,4224]{1,0:T(1,128)S(1)}, u32[]{:S(2)}, u32[]{:S(2)}) collective-permute-start(f32[1,4224]{1,0:T(1,128)S(1)} %add_add_fusion.refs_3_), channel_id=1, source_target_pairs={{0,9},{1,8},{2,11},{3,10},{4,13},{5,12},{6,15},{7,14},{8,1},{9,0},... | collective-permute-start | bytes 50696 | tf_op jit(solution)/shard_map/ppermute | solution.py:337
  39.9 3.7 %collective-permute-start.15 = (f32[1,4224]{1,0:T(1,128)S(1)}, f32[1,4224]{1,0:T(1,128)S(1)}, u32[]{:S(2)}, u32[]{:S(2)}) collective-permute-start(f32[1,4224]{1,0:T(1,128)S(1)} %add_add_fusion.refs_3_), channel_id=1, source_target_pairs={{0,5},{1,4},{2,7},{3,6},{4,1},{5,0},{6,3},{7,2},{8,13},{9,12},{10,... | collective-permute-start | bytes 50696 | tf_op jit(solution)/shard_map/ppermute | solution.py:337
  44.8 3.6 %collective-permute-start.17 = (f32[24,640]{1,0:T(8,128)S(1)}, f32[24,640]{1,0:T(8,128)S(1)}, u32[]{:S(2)}, u32[]{:S(2)}) collective-permute-start(f32[24,640]{1,0:T(8,128)S(1)} %get-tuple-element.44.refs_2_), channel_id=1, source_target_pairs={{0,1},{1,0},{2,3},{3,2},{4,5},{5,4},{6,7},{7,6},{8,9},{9,8},{10,11... | collective-permute-start | bytes 184328 | tf_op jit(solution)/shard_map/ppermute | solution.py:353
  45.1 3.2 %collective-permute-start.16 = (f32[8,640]{1,0:T(8,128)S(1)}, f32[8,640]{1,0:T(8,128)S(1)}, u32[]{:S(2)}, u32[]{:S(2)}) collective-permute-start(f32[8,640]{1,0:T(8,128)S(1)} %get-tuple-element.43), channel_id=1, source_target_pairs={{0,16},{1,17},{2,18},{3,19},{4,20},{5,21},{6,22},{7,23},{8,24},{9,... | collective-permute-start | bytes 61448 | tf_op jit(solution)/shard_map/ppermute | solution.py:353

commit v18 on v13

--- a/solution.py
+++ b/solution.py
@@ -34,9 +34,9 @@
 
 
 def product(stacked, high_block, low_block):
-    main = jnp.dot(stacked, high_block, preferred_element_type=f32)
-    rest = jnp.dot(stacked[0:SLOTS], low_block, preferred_element_type=f32)
-    return main[0:SLOTS] + (main[SLOTS:] + rest)
+    total = jnp.dot(stacked, high_block, preferred_element_type=f32)
+    total += jnp.dot(stacked, low_block, preferred_element_type=f32)
+    return total[0:SLOTS] + total[SLOTS:]
 
 
 def slot_lanes(first):

time: 49.1 us -> 49.1 us (level)
  no operation moved by 1% of the time
where the time goes in v18:
time: 49.1 us; the launch traced here: 49 us
  starting transfers between devices  19.6 us (40%)
  waiting for transfers between devices  16 us (33%)
  Pallas kernels  12.6 us (26%)
  between operations  0.71 us (1%)
    ppermute x16, starting transfers between devices, exchange(): parts.insert(0, lax.ppermute(value, axis, pairs))  19.6 us
    ppermute x16, waiting for transfers between devices, exchange(): parts.insert(0, lax.ppermute(value, axis, pairs))  16 us
    pallas_call x9, Pallas kernels, call(): pl.pallas_call(body, out_shape=out_shape, in_specs=[source] * len(args),...  12.6 us
  transfers between devices with their start and end apart: 16, of which 11 were waited for; matrix products, arithmetic and copies ran while one was open for 0% of the time, Pallas kernels for 5%

profile of v18, /device:TPU:0, one launch (start us, length us, event | category | flops | bytes accessed | tf_op | source)
XLA Modules:
  0.0 49.0 jit_solution(10196624693955244671)
XLA Ops:
  0.6 1.9 %shard_map.68 = (bf16[64,4096]{1,0:T(8,128)(2,1)S(1)}, s32[1,4096]{1,0:T(1,128)S(1)}, f32[1,4096]{1,0:T(1,128)S(1)}, f32[1,512]{1,0:T(1,128)S(1)}, bf16[64,512]{1,0:T(8,128)(2,1)S(1)}) custom-call(bf16[64,4096]{1,0:T(8,128)(2,1)} %feat_hbm.1, s32[1,512]{1,0:T(1,128)} %bitcast.6, s32[1,4096]{1,0:T(1,128)} %bitcast.4, f32[1,4096]{1,0:T(1,128)} %bitcast.5, ...), custom_call_target="tpu_custom_call" | custom-call | tf_op jit(solution)/shard_map/pallas_call | solution.py:288
  2.6 3.0 %collective-permute-start = (bf16[64,512]{1,0:T(8,128)(2,1)S(1)}, bf16[64,512]{1,0:T(8,128)(2,1)S(1)}, u32[]{:S(2)}, u32[]{:S(2)}) collective-permute-start(bf16[64,512]{1,0:T(8,128)(2,1)S(1)} %get-tuple-element.28.refs_1_), channel_id=1, source_target_pairs={{0,16},{16,0},{1,17},{17,1},{2,18},{18,2},{3,19},{19,3},{4,20},{20... | collective-permute-start | bytes 196616 | tf_op jit(solution)/shard_map/ppermute | solution.py:312
  5.6 0.7 %shard_map.69 = (bf16[256,4096]{1,0:T(8,128)(2,1)S(1)}, bf16[4096,256]{1,0:T(8,128)(2,1)S(1)}, bf16[16,4096]{1,0:T(8,128)(2,1)S(1)}) custom-call(bf16[64,4096]{1,0:T(8,128)(2,1)S(1)} %get-tuple-element.23.feat_ref, s32[1,4096]{1,0:T(1,128)S(1)} %get-tuple-element.24.slots_ref.refs_3_.refs_4_, f32[1,4096]{1,0:T(1,128)S(1)} %get-tuple-element.25.prices_ref), custom_call_target="tpu_custom_call" | custom-call | flops 4096000 | bytes 4194304 | tf_op jit(solution)/shard_map/pallas_call | solution.py:288
  6.3 1.6 %collective-permute-done.refs_0_ = bf16[64,512]{1,0:T(8,128)(2,1)S(1)} collective-permute-done((bf16[64,512]{1,0:T(8,128)(2,1)S(1)}, bf16[64,512]{1,0:T(8,128)(2,1)S(1)}, u32[]{:S(2)}, u32[]{:S(2)}) %collective-permute-start) | collective-permute-done | bytes 65568 | tf_op jit(solution)/shard_map/ppermute | solution.py:312
  7.8 2.6 %shard_map.70 = (bf16[8192,512]{1,0:T(8,128)(2,1)S(1)}, bf16[256,512]{1,0:T(8,128)(2,1)S(1)}, f32[8,512]{1,0:T(8,128)S(1)}) custom-call(bf16[4096,256]{1,0:T(8,128)(2,1)S(1)} %get-tuple-element.26.turned_ref, bf16[16,4096]{1,0:T(8,128)(2,1)S(1)} %get-tuple-element.27.weight_ref, bf16[64,512]{1,0:T(8,128)(2,1)S(1)} %collective-permute-done.refs_0_, ...), custom_call_target="tpu_custom_call" | custom-call | flops 134217728 | bytes 8388608 | tf_op jit(solution)/shard_map/pallas_call | solution.py:288
  10.4 2.0 %collective-permute-start.1 = (f32[8,512]{1,0:T(8,128)S(1)}, f32[8,512]{1,0:T(8,128)S(1)}, u32[]{:S(2)}, u32[]{:S(2)}) collective-permute-start(f32[8,512]{1,0:T(8,128)S(1)} %get-tuple-element.29.refs_1_), channel_id=1, source_target_pairs={{0,16},{16,0},{1,17},{17,1},{2,18},{18,2},{3,19},{19,3},{4,20},{20... | collective-permute-start | bytes 49160 | tf_op jit(solution)/shard_map/ppermute | solution.py:312
  12.5 1.9 %shard_map.71.refs_4_ = bf16[1024,4096]{1,0:T(8,128)(2,1)S(1)} custom-call(bf16[256,4096]{1,0:T(8,128)(2,1)S(1)} %get-tuple-element.31.columns_ref, bf16[256,512]{1,0:T(8,128)(2,1)S(1)} %get-tuple-element.32.center_ref), custom_call_target="tpu_custom_call" | custom-call | flops 134217728 | bytes 8388608 | tf_op jit(solution)/shard_map/pallas_call | solution.py:288
  14.4 0.0 collective-permute-done.1.refs_0_
  14.4 1.2 %shard_map.72 = (f32[8,512]{1,0:T(8,128)S(1)}, f32[1,4224]{1,0:T(1,128)S(1)}) custom-call(f32[8,512]{1,0:T(8,128)S(1)} %collective-permute-done.1.refs_0_, f32[8,512]{1,0:T(8,128)S(1)} %get-tuple-element.29.refs_1_, f32[1,512]{1,0:T(1,128)S(1)} %get-tuple-element.30.refs_2_, s32[1,4096]{1,0:T(1,128)S(1)} %get-tuple-element.24.slots_ref.refs_3_.refs_4_, ...), custom_call_target="tpu_custom_call" | custom-call | tf_op jit(solution)/shard_map/pallas_call | solution.py:288
  15.6 0.1 collective-permute-start.2
  15.7 1.9 %collective-permute-start.3 = (f32[1,4224]{1,0:T(1,128)S(1)}, f32[1,4224]{1,0:T(1,128)S(1)}, u32[]{:S(2)}, u32[]{:S(2)}) collective-permute-start(f32[1,4224]{1,0:T(1,128)S(1)} %get-tuple-element.33), channel_id=1, source_target_pairs={{0,2},{1,3},{2,0},{3,1},{4,6},{5,7},{6,4},{7,5},{8,10},{9,11},{10,... | collective-permute-start | bytes 50696 | tf_op jit(solution)/shard_map/ppermute | solution.py:312
  17.6 0.0 collective-permute-start.4
  17.6 1.2 %collective-permute-done.2 = f32[1,4224]{1,0:T(1,128)S(1)} collective-permute-done((f32[1,4224]{1,0:T(1,128)S(1)}, f32[1,4224]{1,0:T(1,128)S(1)}, u32[]{:S(2)}, u32[]{:S(2)}) %collective-permute-start.2) | collective-permute-done | bytes 16928 | tf_op jit(solution)/shard_map/ppermute | solution.py:312
  18.8 0.7 %collective-permute-done.3 = f32[1,4224]{1,0:T(1,128)S(1)} collective-permute-done((f32[1,4224]{1,0:T(1,128)S(1)}, f32[1,4224]{1,0:T(1,128)S(1)}, u32[]{:S(2)}, u32[]{:S(2)}) %collective-permute-start.3) | collective-permute-done | bytes 16928 | tf_op jit(solution)/shard_map/ppermute | solution.py:312
  19.5 0.0 collective-permute-done.4
  19.5 4.0 %collective-permute-start.5 = (f32[1,4224]{1,0:T(1,128)S(1)}, f32[1,4224]{1,0:T(1,128)S(1)}, u32[]{:S(2)}, u32[]{:S(2)}) collective-permute-start(f32[1,4224]{1,0:T(1,128)S(1)} %add_add_fusion.1.refs_3_), channel_id=1, source_target_pairs={{0,13},{1,12},{2,15},{3,14},{4,9},{5,8},{6,11},{7,10},{8,5},{9,4},... | collective-permute-start | bytes 50696 | tf_op jit(solution)/shard_map/ppermute | solution.py:312
  23.5 0.0 collective-permute-start.6
  23.6 0.5 collective-permute-start.7
  24.0 1.0 %collective-permute-done.5.refs_0_ = f32[1,4224]{1,0:T(1,128)S(1)} collective-permute-done((f32[1,4224]{1,0:T(1,128)S(1)}, f32[1,4224]{1,0:T(1,128)S(1)}, u32[]{:S(2)}, u32[]{:S(2)}) %collective-permute-start.5) | collective-permute-done | bytes 16928 | tf_op jit(solution)/shard_map/ppermute | solution.py:312
  25.0 2.6 %collective-permute-done.6.refs_1_ = f32[1,4224]{1,0:T(1,128)S(1)} collective-permute-done((f32[1,4224]{1,0:T(1,128)S(1)}, f32[1,4224]{1,0:T(1,128)S(1)}, u32[]{:S(2)}, u32[]{:S(2)}) %collective-permute-start.6) | collective-permute-done | bytes 16928 | tf_op jit(solution)/shard_map/ppermute | solution.py:312
  27.6 0.0 collective-permute-done.7.refs_2_
  27.6 1.2 %shard_map.73 = (f32[1,4224]{1,0:T(1,128)S(1)}, f32[8,128]{1,0:T(8,128)S(1)}, f32[8,640]{1,0:T(8,128)S(1)}) custom-call(f32[1,4224]{1,0:T(1,128)S(1)} %collective-permute-done.5.refs_0_, f32[1,4224]{1,0:T(1,128)S(1)} %collective-permute-done.6.refs_1_, f32[1,4224]{1,0:T(1,128)S(1)} %collective-permute-done.7.refs_2_, f32[1,4224]{1,0:T(1,128)S(1)} %add_add_fusion.1.refs_3_, ...), custom_call_target="tpu_custom_call" | custom-call | tf_op jit(solution)/shard_map/pallas_call | solution.py:288
  28.8 1.5 %collective-permute-start.8 = (f32[8,640]{1,0:T(8,128)S(1)}, f32[8,640]{1,0:T(8,128)S(1)}, u32[]{:S(2)}, u32[]{:S(2)}) collective-permute-start(f32[8,640]{1,0:T(8,128)S(1)} %get-tuple-element.35.refs_1_), channel_id=1, source_target_pairs={{0,16},{16,0},{1,17},{17,1},{2,18},{18,2},{3,19},{19,3},{4,20},{20... | collective-permute-start | bytes 61448 | tf_op jit(solution)/shard_map/ppermute | solution.py:312
  30.3 2.3 %collective-permute-done.8.refs_0_ = f32[8,640]{1,0:T(8,128)S(1)} collective-permute-done((f32[8,640]{1,0:T(8,128)S(1)}, f32[8,640]{1,0:T(8,128)S(1)}, u32[]{:S(2)}, u32[]{:S(2)}) %collective-permute-start.8) | collective-permute-done | bytes 20512 | tf_op jit(solution)/shard_map/ppermute | solution.py:312
  32.6 1.2 %shard_map.74 = (f32[8,512]{1,0:T(8,128)S(1)}, f32[8,128]{1,0:T(8,128)S(1)}, f32[1,4224]{1,0:T(1,128)S(1)}) custom-call(f32[8,640]{1,0:T(8,128)S(1)} %collective-permute-done.8.refs_0_, f32[8,640]{1,0:T(8,128)S(1)} %get-tuple-element.35.refs_1_, f32[1,512]{1,0:T(1,128)S(1)} %get-tuple-element.30.refs_2_, ...), custom_call_target="tpu_custom_call" | custom-call | tf_op jit(solution)/shard_map/pallas_call | solution.py:288
  33.8 0.5 collective-permute-start.10
  34.3 0.4 collective-permute-start.11
  34.7 1.1 %collective-permute-start.9 = (f32[1,4224]{1,0:T(1,128)S(1)}, f32[1,4224]{1,0:T(1,128)S(1)}, u32[]{:S(2)}, u32[]{:S(2)}) collective-permute-start(f32[1,4224]{1,0:T(1,128)S(1)} %get-tuple-element.38), channel_id=1, source_target_pairs={{0,1},{1,0},{2,3},{3,2},{4,5},{5,4},{6,7},{7,6},{8,9},{9,8},{10,11... | collective-permute-start | bytes 50696 | tf_op jit(solution)/shard_map/ppermute | solution.py:312
  35.7 1.3 %collective-permute-done.10 = f32[1,4224]{1,0:T(1,128)S(1)} collective-permute-done((f32[1,4224]{1,0:T(1,128)S(1)}, f32[1,4224]{1,0:T(1,128)S(1)}, u32[]{:S(2)}, u32[]{:S(2)}) %collective-permute-start.10) | collective-permute-done | bytes 16928 | tf_op jit(solution)/shard_map/ppermute | solution.py:312
  37.1 1.0 %collective-permute-done.11 = f32[1,4224]{1,0:T(1,128)S(1)} collective-permute-done((f32[1,4224]{1,0:T(1,128)S(1)}, f32[1,4224]{1,0:T(1,128)S(1)}, u32[]{:S(2)}, u32[]{:S(2)}) %collective-permute-start.11) | collective-permute-done | bytes 16928 | tf_op jit(solution)/shard_map/ppermute | solution.py:312
  38.0 0.0 collective-permute-done.9
  38.1 1.0 %collective-permute-start.12 = (f32[1,4224]{1,0:T(1,128)S(1)}, f32[1,4224]{1,0:T(1,128)S(1)}, u32[]{:S(2)}, u32[]{:S(2)}) collective-permute-start(f32[1,4224]{1,0:T(1,128)S(1)} %add_add_fusion.refs_3_), channel_id=1, source_target_pairs={{0,13},{1,12},{2,15},{3,14},{4,9},{5,8},{6,11},{7,10},{8,5},{9,4},... | collective-permute-start | bytes 50696 | tf_op jit(solution)/shard_map/ppermute | solution.py:312
  39.1 0.5 %collective-permute-start.13 = (f32[1,4224]{1,0:T(1,128)S(1)}, f32[1,4224]{1,0:T(1,128)S(1)}, u32[]{:S(2)}, u32[]{:S(2)}) collective-permute-start(f32[1,4224]{1,0:T(1,128)S(1)} %add_add_fusion.refs_3_), channel_id=1, source_target_pairs={{0,9},{1,8},{2,11},{3,10},{4,13},{5,12},{6,15},{7,14},{8,1},{9,0},... | collective-permute-start | bytes 50696 | tf_op jit(solution)/shard_map/ppermute | solution.py:312
  39.6 1.5 %collective-permute-start.14 = (f32[1,4224]{1,0:T(1,128)S(1)}, f32[1,4224]{1,0:T(1,128)S(1)}, u32[]{:S(2)}, u32[]{:S(2)}) collective-permute-start(f32[1,4224]{1,0:T(1,128)S(1)} %add_add_fusion.refs_3_), channel_id=1, source_target_pairs={{0,5},{1,4},{2,7},{3,6},{4,1},{5,0},{6,3},{7,2},{8,13},{9,12},{10,... | collective-permute-start | bytes 50696 | tf_op jit(solution)/shard_map/ppermute | solution.py:312
  41.1 2.0 %collective-permute-done.12.refs_0_ = f32[1,4224]{1,0:T(1,128)S(1)} collective-permute-done((f32[1,4224]{1,0:T(1,128)S(1)}, f32[1,4224]{1,0:T(1,128)S(1)}, u32[]{:S(2)}, u32[]{:S(2)}) %collective-permute-start.12) | collective-permute-done | bytes 16928 | tf_op jit(solution)/shard_map/ppermute | solution.py:312
  43.1 0.2 collective-permute-done.13.refs_1_
  43.3 0.0 collective-permute-done.14.refs_2_
  43.3 1.3 %shard_map.75 = (f32[8,256]{1,0:T(8,128)S(1)}, f32[8,640]{1,0:T(8,128)S(1)}) custom-call(f32[1,4224]{1,0:T(1,128)S(1)} %collective-permute-done.12.refs_0_, f32[1,4224]{1,0:T(1,128)S(1)} %collective-permute-done.13.refs_1_, f32[1,4224]{1,0:T(1,128)S(1)} %collective-permute-done.14.refs_2_, f32[1,4224]{1,0:T(1,128)S(1)} %add_add_fusion.refs_3_, ...), custom_call_target="tpu_custom_call" | custom-call | tf_op jit(solution)/shard_map/pallas_call | solution.py:288
  44.5 1.5 %collective-permute-start.15 = (f32[8,640]{1,0:T(8,128)S(1)}, f32[8,640]{1,0:T(8,128)S(1)}, u32[]{:S(2)}, u32[]{:S(2)}) collective-permute-start(f32[8,640]{1,0:T(8,128)S(1)} %get-tuple-element.40.refs_1_), channel_id=1, source_target_pairs={{0,16},{16,0},{1,17},{17,1},{2,18},{18,2},{3,19},{19,3},{4,20},{20... | collective-permute-start | bytes 61448 | tf_op jit(solution)/shard_map/ppermute | solution.py:312
  46.1 2.3 %collective-permute-done.15.refs_0_ = f32[8,640]{1,0:T(8,128)S(1)} collective-permute-done((f32[8,640]{1,0:T(8,128)S(1)}, f32[8,640]{1,0:T(8,128)S(1)}, u32[]{:S(2)}, u32[]{:S(2)}) %collective-permute-start.15) | collective-permute-done | bytes 20512 | tf_op jit(solution)/shard_map/ppermute | solution.py:312
  48.3 0.6 %shard_map.76 = (f32[8,512]{1,0:T(8,128)}, f32[8,512]{1,0:T(8,128)}) custom-call(f32[8,640]{1,0:T(8,128)S(1)} %collective-permute-done.15.refs_0_, f32[8,640]{1,0:T(8,128)S(1)} %get-tuple-element.40.refs_1_, f32[1,512]{1,0:T(1,128)S(1)} %get-tuple-element.30.refs_2_, f32[8,512]{1,0:T(8,128)S(1)} %get-tuple-element.36.refs_5_.refs_3_, ...), custom_call_target="tpu_custom_call" | custom-call | tf_op jit(solution)/shard_map/pallas_call | solution.py:288
  (2 shorter events, 0.1 us)
Async XLA Ops:
  2.6 5.2 %collective-permute-start = (bf16[64,512]{1,0:T(8,128)(2,1)S(1)}, bf16[64,512]{1,0:T(8,128)(2,1)S(1)}, u32[]{:S(2)}, u32[]{:S(2)}) collective-permute-start(bf16[64,512]{1,0:T(8,128)(2,1)S(1)} %get-tuple-element.28.refs_1_), channel_id=1, source_target_pairs={{0,16},{16,0},{1,17},{17,1},{2,18},{18,2},{3,19},{19,3},{4,20},{20... | collective-permute-start | bytes 196616 | tf_op jit(solution)/shard_map/ppermute | solution.py:312
  10.4 3.9 %collective-permute-start.1 = (f32[8,512]{1,0:T(8,128)S(1)}, f32[8,512]{1,0:T(8,128)S(1)}, u32[]{:S(2)}, u32[]{:S(2)}) collective-permute-start(f32[8,512]{1,0:T(8,128)S(1)} %get-tuple-element.29.refs_1_), channel_id=1, source_target_pairs={{0,16},{16,0},{1,17},{17,1},{2,18},{18,2},{3,19},{19,3},{4,20},{20... | collective-permute-start | bytes 49160 | tf_op jit(solution)/shard_map/ppermute | solution.py:312
  15.6 3.2 %collective-permute-start.2 = (f32[1,4224]{1,0:T(1,128)S(1)}, f32[1,4224]{1,0:T(1,128)S(1)}, u32[]{:S(2)}, u32[]{:S(2)}) collective-permute-start(f32[1,4224]{1,0:T(1,128)S(1)} %get-tuple-element.33), channel_id=1, source_target_pairs={{0,3},{1,2},{2,1},{3,0},{4,7},{5,6},{6,5},{7,4},{8,11},{9,10},{10,... | collective-permute-start | bytes 50696 | tf_op jit(solution)/shard_map/ppermute | solution.py:312
  15.7 3.8 %collective-permute-start.3 = (f32[1,4224]{1,0:T(1,128)S(1)}, f32[1,4224]{1,0:T(1,128)S(1)}, u32[]{:S(2)}, u32[]{:S(2)}) collective-permute-start(f32[1,4224]{1,0:T(1,128)S(1)} %get-tuple-element.33), channel_id=1, source_target_pairs={{0,2},{1,3},{2,0},{3,1},{4,6},{5,7},{6,4},{7,5},{8,10},{9,11},{10,... | collective-permute-start | bytes 50696 | tf_op jit(solution)/shard_map/ppermute | solution.py:312
  17.6 1.9 %collective-permute-start.4 = (f32[1,4224]{1,0:T(1,128)S(1)}, f32[1,4224]{1,0:T(1,128)S(1)}, u32[]{:S(2)}, u32[]{:S(2)}) collective-permute-start(f32[1,4224]{1,0:T(1,128)S(1)} %get-tuple-element.33), channel_id=1, source_target_pairs={{0,1},{1,0},{2,3},{3,2},{4,5},{5,4},{6,7},{7,6},{8,9},{9,8},{10,11... | collective-permute-start | bytes 50696 | tf_op jit(solution)/shard_map/ppermute | solution.py:312
  19.5 5.5 %collective-permute-start.5 = (f32[1,4224]{1,0:T(1,128)S(1)}, f32[1,4224]{1,0:T(1,128)S(1)}, u32[]{:S(2)}, u32[]{:S(2)}) collective-permute-start(f32[1,4224]{1,0:T(1,128)S(1)} %add_add_fusion.1.refs_3_), channel_id=1, source_target_pairs={{0,13},{1,12},{2,15},{3,14},{4,9},{5,8},{6,11},{7,10},{8,5},{9,4},... | collective-permute-start | bytes 50696 | tf_op jit(solution)/shard_map/ppermute | solution.py:312
  23.5 4.1 %collective-permute-start.6 = (f32[1,4224]{1,0:T(1,128)S(1)}, f32[1,4224]{1,0:T(1,128)S(1)}, u32[]{:S(2)}, u32[]{:S(2)}) collective-permute-start(f32[1,4224]{1,0:T(1,128)S(1)} %add_add_fusion.1.refs_3_), channel_id=1, source_target_pairs={{0,9},{1,8},{2,11},{3,10},{4,13},{5,12},{6,15},{7,14},{8,1},{9,0},... | collective-permute-start | bytes 50696 | tf_op jit(solution)/shard_map/ppermute | solution.py:312
  23.6 4.1 %collective-permute-start.7 = (f32[1,4224]{1,0:T(1,128)S(1)}, f32[1,4224]{1,0:T(1,128)S(1)}, u32[]{:S(2)}, u32[]{:S(2)}) collective-permute-start(f32[1,4224]{1,0:T(1,128)S(1)} %add_add_fusion.1.refs_3_), channel_id=1, source_target_pairs={{0,5},{1,4},{2,7},{3,6},{4,1},{5,0},{6,3},{7,2},{8,13},{9,12},{10,... | collective-permute-start | bytes 50696 | tf_op jit(solution)/shard_map/ppermute | solution.py:312
  28.8 3.8 %collective-permute-start.8 = (f32[8,640]{1,0:T(8,128)S(1)}, f32[8,640]{1,0:T(8,128)S(1)}, u32[]{:S(2)}, u32[]{:S(2)}) collective-permute-start(f32[8,640]{1,0:T(8,128)S(1)} %get-tuple-element.35.refs_1_), channel_id=1, source_target_pairs={{0,16},{16,0},{1,17},{17,1},{2,18},{18,2},{3,19},{19,3},{4,20},{20... | collective-permute-start | bytes 61448 | tf_op jit(solution)/shard_map/ppermute | solution.py:312
  33.8 3.2 %collective-permute-start.10 = (f32[1,4224]{1,0:T(1,128)S(1)}, f32[1,4224]{1,0:T(1,128)S(1)}, u32[]{:S(2)}, u32[]{:S(2)}) collective-permute-start(f32[1,4224]{1,0:T(1,128)S(1)} %get-tuple-element.38), channel_id=1, source_target_pairs={{0,3},{1,2},{2,1},{3,0},{4,7},{5,6},{6,5},{7,4},{8,11},{9,10},{10,... | collective-permute-start | bytes 50696 | tf_op jit(solution)/shard_map/ppermute | solution.py:312
  34.3 3.7 %collective-permute-start.11 = (f32[1,4224]{1,0:T(1,128)S(1)}, f32[1,4224]{1,0:T(1,128)S(1)}, u32[]{:S(2)}, u32[]{:S(2)}) collective-permute-start(f32[1,4224]{1,0:T(1,128)S(1)} %get-tuple-element.38), channel_id=1, source_target_pairs={{0,2},{1,3},{2,0},{3,1},{4,6},{5,7},{6,4},{7,5},{8,10},{9,11},{10,... | collective-permute-start | bytes 50696 | tf_op jit(solution)/shard_map/ppermute | solution.py:312
  34.7 3.4 %collective-permute-start.9 = (f32[1,4224]{1,0:T(1,128)S(1)}, f32[1,4224]{1,0:T(1,128)S(1)}, u32[]{:S(2)}, u32[]{:S(2)}) collective-permute-start(f32[1,4224]{1,0:T(1,128)S(1)} %get-tuple-element.38), channel_id=1, source_target_pairs={{0,1},{1,0},{2,3},{3,2},{4,5},{5,4},{6,7},{7,6},{8,9},{9,8},{10,11... | collective-permute-start | bytes 50696 | tf_op jit(solution)/shard_map/ppermute | solution.py:312
  38.1 5.0 %collective-permute-start.12 = (f32[1,4224]{1,0:T(1,128)S(1)}, f32[1,4224]{1,0:T(1,128)S(1)}, u32[]{:S(2)}, u32[]{:S(2)}) collective-permute-start(f32[1,4224]{1,0:T(1,128)S(1)} %add_add_fusion.refs_3_), channel_id=1, source_target_pairs={{0,13},{1,12},{2,15},{3,14},{4,9},{5,8},{6,11},{7,10},{8,5},{9,4},... | collective-permute-start | bytes 50696 | tf_op jit(solution)/shard_map/ppermute | solution.py:312
  39.1 4.2 %collective-permute-start.13 = (f32[1,4224]{1,0:T(1,128)S(1)}, f32[1,4224]{1,0:T(1,128)S(1)}, u32[]{:S(2)}, u32[]{:S(2)}) collective-permute-start(f32[1,4224]{1,0:T(1,128)S(1)} %add_add_fusion.refs_3_), channel_id=1, source_target_pairs={{0,9},{1,8},{2,11},{3,10},{4,13},{5,12},{6,15},{7,14},{8,1},{9,0},... | collective-permute-start | bytes 50696 | tf_op jit(solution)/shard_map/ppermute | solution.py:312
  39.6 3.7 %collective-permute-start.14 = (f32[1,4224]{1,0:T(1,128)S(1)}, f32[1,4224]{1,0:T(1,128)S(1)}, u32[]{:S(2)}, u32[]{:S(2)}) collective-permute-start(f32[1,4224]{1,0:T(1,128)S(1)} %add_add_fusion.refs_3_), channel_id=1, source_target_pairs={{0,5},{1,4},{2,7},{3,6},{4,1},{5,0},{6,3},{7,2},{8,13},{9,12},{10,... | collective-permute-start | bytes 50696 | tf_op jit(solution)/shard_map/ppermute | solution.py:312
  44.5 3.8 %collective-permute-start.15 = (f32[8,640]{1,0:T(8,128)S(1)}, f32[8,640]{1,0:T(8,128)S(1)}, u32[]{:S(2)}, u32[]{:S(2)}) collective-permute-start(f32[8,640]{1,0:T(8,128)S(1)} %get-tuple-element.40.refs_1_), channel_id=1, source_target_pairs={{0,16},{16,0},{1,17},{17,1},{2,18},{18,2},{3,19},{19,3},{4,20},{20... | collective-permute-start | bytes 61448 | tf_op jit(solution)/shard_map/ppermute | solution.py:312

commit v19 on v13

--- a/solution.py
+++ b/solution.py
@@ -268,7 +268,7 @@
 def finish_body(parts, inv_rows, *refs):
     fold_refs = refs[:parts]
     (scale_ref, target_ref, residual_ref, step_ref, norm_ref, sums_ref,
-     coefficients_ref, out_ref) = refs[parts:]
+     first_hbm, second_hbm, first_ref, second_ref, sems) = refs[parts:]
     count = scale_ref.shape[1]
     folded = total_of(fold_refs)
     target = target_ref[...]
@@ -280,16 +280,22 @@
     square = norm + 2.0 * ratio * cross + ratio * ratio * first_norm
     applied = scale_ref[...] * folded[:, 0:count] * inv_rows + RIDGE * direction
     step = wide(norm / (folded[:, count:] * inv_rows + RIDGE * square), count)
-    coefficients_ref[...] = wide(step_ref[...], count) * target + step * direction
-    out_ref[...] = residual - step * applied
-
-
-def call(body, out_shape, *args, source=VMEM, flops=0, bytes_accessed=0, **more):
+    first_ref[...] = wide(step_ref[...], count) * target + step * direction
+    first_copy = pltpu.make_async_copy(first_ref, first_hbm, sems.at[0])
+    first_copy.start()
+    second_ref[...] = residual - step * applied
+    second_copy = pltpu.make_async_copy(second_ref, second_hbm, sems.at[1])
+    second_copy.start()
+    first_copy.wait()
+    second_copy.wait()
+
+
+def call(body, out_shape, *args, source=VMEM, target=VMEM, flops=0, bytes_accessed=0, **more):
     return pl.pallas_call(
         body,
         out_shape=out_shape,
         in_specs=[source] * len(args),
-        out_specs=jax.tree.map(lambda _: VMEM, out_shape),
+        out_specs=jax.tree.map(lambda _: target, out_shape),
         compiler_params=pltpu.CompilerParams(vmem_limit_bytes=36 * 1024 * 1024),
         cost_estimate=pl.CostEstimate(
             flops=flops, bytes_accessed=bytes_accessed, transcendentals=0
@@ -405,6 +411,12 @@
         partial(finish_body, len(folds), 1.0 / all_rows),
         (vector, vector),
         *folds, scale, target, residual, step, norm, sums,
+        target=HBM,
+        scratch_shapes=[
+            pltpu.VMEM((SLOTS, count), f32),
+            pltpu.VMEM((SLOTS, count), f32),
+            pltpu.SemaphoreType.DMA((2,)),
+        ],
     )
 
 

time: 49.1 us -> 49.2 us (level)
  no operation moved by 1% of the time
where the time goes in v19:
time: 49.2 us; the launch traced here: 49 us
  starting transfers between devices  19.6 us (40%)
  waiting for transfers between devices  16.1 us (33%)
  Pallas kernels  12.6 us (26%)
  between operations  0.71 us (1%)
    ppermute x16, starting transfers between devices, exchange(): parts.insert(0, lax.ppermute(value, axis, pairs))  19.6 us
    ppermute x16, waiting for transfers between devices, exchange(): parts.insert(0, lax.ppermute(value, axis, pairs))  16.1 us
    pallas_call x9, Pallas kernels, call(): pl.pallas_call(body, out_shape=out_shape, in_specs=[source] * len(args),...  12.6 us
  transfers between devices with their start and end apart: 16, of which 11 were waited for; matrix products, arithmetic and copies ran while one was open for 0% of the time, Pallas kernels for 5%

profile of v19, /device:TPU:0, one launch (start us, length us, event | category | flops | bytes accessed | tf_op | source)
XLA Modules:
  0.0 49.0 jit_solution(12181574723050111383)
XLA Ops:
  0.6 1.9 %shard_map.68 = (bf16[64,4096]{1,0:T(8,128)(2,1)S(1)}, s32[1,4096]{1,0:T(1,128)S(1)}, f32[1,4096]{1,0:T(1,128)S(1)}, f32[1,512]{1,0:T(1,128)S(1)}, bf16[64,512]{1,0:T(8,128)(2,1)S(1)}) custom-call(bf16[64,4096]{1,0:T(8,128)(2,1)} %feat_hbm.1, s32[1,512]{1,0:T(1,128)} %bitcast.6, s32[1,4096]{1,0:T(1,128)} %bitcast.4, f32[1,4096]{1,0:T(1,128)} %bitcast.5, ...), custom_call_target="tpu_custom_call" | custom-call | tf_op jit(solution)/shard_map/pallas_call | solution.py:294
  2.6 3.0 %collective-permute-start = (bf16[64,512]{1,0:T(8,128)(2,1)S(1)}, bf16[64,512]{1,0:T(8,128)(2,1)S(1)}, u32[]{:S(2)}, u32[]{:S(2)}) collective-permute-start(bf16[64,512]{1,0:T(8,128)(2,1)S(1)} %get-tuple-element.28.refs_1_), channel_id=1, source_target_pairs={{0,16},{16,0},{1,17},{17,1},{2,18},{18,2},{3,19},{19,3},{4,20},{20... | collective-permute-start | bytes 196616 | tf_op jit(solution)/shard_map/ppermute | solution.py:318
  5.6 0.7 %shard_map.69 = (bf16[256,4096]{1,0:T(8,128)(2,1)S(1)}, bf16[4096,256]{1,0:T(8,128)(2,1)S(1)}, bf16[16,4096]{1,0:T(8,128)(2,1)S(1)}) custom-call(bf16[64,4096]{1,0:T(8,128)(2,1)S(1)} %get-tuple-element.23.feat_ref, s32[1,4096]{1,0:T(1,128)S(1)} %get-tuple-element.24.slots_ref.refs_3_.refs_4_, f32[1,4096]{1,0:T(1,128)S(1)} %get-tuple-element.25.prices_ref), custom_call_target="tpu_custom_call" | custom-call | flops 4096000 | bytes 4194304 | tf_op jit(solution)/shard_map/pallas_call | solution.py:294
  6.3 1.6 %collective-permute-done.refs_0_ = bf16[64,512]{1,0:T(8,128)(2,1)S(1)} collective-permute-done((bf16[64,512]{1,0:T(8,128)(2,1)S(1)}, bf16[64,512]{1,0:T(8,128)(2,1)S(1)}, u32[]{:S(2)}, u32[]{:S(2)}) %collective-permute-start) | collective-permute-done | bytes 65568 | tf_op jit(solution)/shard_map/ppermute | solution.py:318
  7.8 2.5 %shard_map.70 = (bf16[8192,512]{1,0:T(8,128)(2,1)S(1)}, bf16[256,512]{1,0:T(8,128)(2,1)S(1)}, f32[8,512]{1,0:T(8,128)S(1)}) custom-call(bf16[4096,256]{1,0:T(8,128)(2,1)S(1)} %get-tuple-element.26.turned_ref, bf16[16,4096]{1,0:T(8,128)(2,1)S(1)} %get-tuple-element.27.weight_ref, bf16[64,512]{1,0:T(8,128)(2,1)S(1)} %collective-permute-done.refs_0_, ...), custom_call_target="tpu_custom_call" | custom-call | flops 134217728 | bytes 8388608 | tf_op jit(solution)/shard_map/pallas_call | solution.py:294
  10.4 2.1 %collective-permute-start.1 = (f32[8,512]{1,0:T(8,128)S(1)}, f32[8,512]{1,0:T(8,128)S(1)}, u32[]{:S(2)}, u32[]{:S(2)}) collective-permute-start(f32[8,512]{1,0:T(8,128)S(1)} %get-tuple-element.29.refs_1_), channel_id=1, source_target_pairs={{0,16},{16,0},{1,17},{17,1},{2,18},{18,2},{3,19},{19,3},{4,20},{20... | collective-permute-start | bytes 49160 | tf_op jit(solution)/shard_map/ppermute | solution.py:318
  12.4 1.9 %shard_map.71.refs_4_ = bf16[1024,4096]{1,0:T(8,128)(2,1)S(1)} custom-call(bf16[256,4096]{1,0:T(8,128)(2,1)S(1)} %get-tuple-element.31.columns_ref, bf16[256,512]{1,0:T(8,128)(2,1)S(1)} %get-tuple-element.32.center_ref), custom_call_target="tpu_custom_call" | custom-call | flops 134217728 | bytes 8388608 | tf_op jit(solution)/shard_map/pallas_call | solution.py:294
  14.4 0.0 collective-permute-done.1.refs_0_
  14.4 1.2 %shard_map.72 = (f32[8,512]{1,0:T(8,128)S(1)}, f32[1,4224]{1,0:T(1,128)S(1)}) custom-call(f32[8,512]{1,0:T(8,128)S(1)} %collective-permute-done.1.refs_0_, f32[8,512]{1,0:T(8,128)S(1)} %get-tuple-element.29.refs_1_, f32[1,512]{1,0:T(1,128)S(1)} %get-tuple-element.30.refs_2_, s32[1,4096]{1,0:T(1,128)S(1)} %get-tuple-element.24.slots_ref.refs_3_.refs_4_, ...), custom_call_target="tpu_custom_call" | custom-call | tf_op jit(solution)/shard_map/pallas_call | solution.py:294
  15.6 0.1 collective-permute-start.2
  15.7 1.9 %collective-permute-start.3 = (f32[1,4224]{1,0:T(1,128)S(1)}, f32[1,4224]{1,0:T(1,128)S(1)}, u32[]{:S(2)}, u32[]{:S(2)}) collective-permute-start(f32[1,4224]{1,0:T(1,128)S(1)} %get-tuple-element.33), channel_id=1, source_target_pairs={{0,2},{1,3},{2,0},{3,1},{4,6},{5,7},{6,4},{7,5},{8,10},{9,11},{10,... | collective-permute-start | bytes 50696 | tf_op jit(solution)/shard_map/ppermute | solution.py:318
  17.6 0.0 collective-permute-start.4
  17.6 1.2 %collective-permute-done.2 = f32[1,4224]{1,0:T(1,128)S(1)} collective-permute-done((f32[1,4224]{1,0:T(1,128)S(1)}, f32[1,4224]{1,0:T(1,128)S(1)}, u32[]{:S(2)}, u32[]{:S(2)}) %collective-permute-start.2) | collective-permute-done | bytes 16928 | tf_op jit(solution)/shard_map/ppermute | solution.py:318
  18.8 0.7 %collective-permute-done.3 = f32[1,4224]{1,0:T(1,128)S(1)} collective-permute-done((f32[1,4224]{1,0:T(1,128)S(1)}, f32[1,4224]{1,0:T(1,128)S(1)}, u32[]{:S(2)}, u32[]{:S(2)}) %collective-permute-start.3) | collective-permute-done | bytes 16928 | tf_op jit(solution)/shard_map/ppermute | solution.py:318
  19.5 0.0 collective-permute-done.4
  19.5 4.0 %collective-permute-start.5 = (f32[1,4224]{1,0:T(1,128)S(1)}, f32[1,4224]{1,0:T(1,128)S(1)}, u32[]{:S(2)}, u32[]{:S(2)}) collective-permute-start(f32[1,4224]{1,0:T(1,128)S(1)} %add_add_fusion.1.refs_3_), channel_id=1, source_target_pairs={{0,13},{1,12},{2,15},{3,14},{4,9},{5,8},{6,11},{7,10},{8,5},{9,4},... | collective-permute-start | bytes 50696 | tf_op jit(solution)/shard_map/ppermute | solution.py:318
  23.5 0.0 collective-permute-start.6
  23.5 0.5 %collective-permute-start.7 = (f32[1,4224]{1,0:T(1,128)S(1)}, f32[1,4224]{1,0:T(1,128)S(1)}, u32[]{:S(2)}, u32[]{:S(2)}) collective-permute-start(f32[1,4224]{1,0:T(1,128)S(1)} %add_add_fusion.1.refs_3_), channel_id=1, source_target_pairs={{0,5},{1,4},{2,7},{3,6},{4,1},{5,0},{6,3},{7,2},{8,13},{9,12},{10,... | collective-permute-start | bytes 50696 | tf_op jit(solution)/shard_map/ppermute | solution.py:318
  24.0 1.0 %collective-permute-done.5.refs_0_ = f32[1,4224]{1,0:T(1,128)S(1)} collective-permute-done((f32[1,4224]{1,0:T(1,128)S(1)}, f32[1,4224]{1,0:T(1,128)S(1)}, u32[]{:S(2)}, u32[]{:S(2)}) %collective-permute-start.5) | collective-permute-done | bytes 16928 | tf_op jit(solution)/shard_map/ppermute | solution.py:318
  25.0 2.6 %collective-permute-done.6.refs_1_ = f32[1,4224]{1,0:T(1,128)S(1)} collective-permute-done((f32[1,4224]{1,0:T(1,128)S(1)}, f32[1,4224]{1,0:T(1,128)S(1)}, u32[]{:S(2)}, u32[]{:S(2)}) %collective-permute-start.6) | collective-permute-done | bytes 16928 | tf_op jit(solution)/shard_map/ppermute | solution.py:318
  27.6 0.0 collective-permute-done.7.refs_2_
  27.6 1.2 %shard_map.73 = (f32[1,4224]{1,0:T(1,128)S(1)}, f32[8,128]{1,0:T(8,128)S(1)}, f32[8,640]{1,0:T(8,128)S(1)}) custom-call(f32[1,4224]{1,0:T(1,128)S(1)} %collective-permute-done.5.refs_0_, f32[1,4224]{1,0:T(1,128)S(1)} %collective-permute-done.6.refs_1_, f32[1,4224]{1,0:T(1,128)S(1)} %collective-permute-done.7.refs_2_, f32[1,4224]{1,0:T(1,128)S(1)} %add_add_fusion.1.refs_3_, ...), custom_call_target="tpu_custom_call" | custom-call | tf_op jit(solution)/shard_map/pallas_call | solution.py:294
  28.8 1.5 %collective-permute-start.8 = (f32[8,640]{1,0:T(8,128)S(1)}, f32[8,640]{1,0:T(8,128)S(1)}, u32[]{:S(2)}, u32[]{:S(2)}) collective-permute-start(f32[8,640]{1,0:T(8,128)S(1)} %get-tuple-element.35.refs_1_), channel_id=1, source_target_pairs={{0,16},{16,0},{1,17},{17,1},{2,18},{18,2},{3,19},{19,3},{4,20},{20... | collective-permute-start | bytes 61448 | tf_op jit(solution)/shard_map/ppermute | solution.py:318
  30.3 2.3 %collective-permute-done.8.refs_0_ = f32[8,640]{1,0:T(8,128)S(1)} collective-permute-done((f32[8,640]{1,0:T(8,128)S(1)}, f32[8,640]{1,0:T(8,128)S(1)}, u32[]{:S(2)}, u32[]{:S(2)}) %collective-permute-start.8) | collective-permute-done | bytes 20512 | tf_op jit(solution)/shard_map/ppermute | solution.py:318
  32.6 1.2 %shard_map.74 = (f32[8,512]{1,0:T(8,128)S(1)}, f32[8,128]{1,0:T(8,128)S(1)}, f32[1,4224]{1,0:T(1,128)S(1)}) custom-call(f32[8,640]{1,0:T(8,128)S(1)} %collective-permute-done.8.refs_0_, f32[8,640]{1,0:T(8,128)S(1)} %get-tuple-element.35.refs_1_, f32[1,512]{1,0:T(1,128)S(1)} %get-tuple-element.30.refs_2_, ...), custom_call_target="tpu_custom_call" | custom-call | tf_op jit(solution)/shard_map/pallas_call | solution.py:294
  33.8 0.5 collective-permute-start.10
  34.3 0.4 collective-permute-start.11
  34.6 1.1 %collective-permute-start.9 = (f32[1,4224]{1,0:T(1,128)S(1)}, f32[1,4224]{1,0:T(1,128)S(1)}, u32[]{:S(2)}, u32[]{:S(2)}) collective-permute-start(f32[1,4224]{1,0:T(1,128)S(1)} %get-tuple-element.38), channel_id=1, source_target_pairs={{0,1},{1,0},{2,3},{3,2},{4,5},{5,4},{6,7},{7,6},{8,9},{9,8},{10,11... | collective-permute-start | bytes 50696 | tf_op jit(solution)/shard_map/ppermute | solution.py:318
  35.7 1.3 %collective-permute-done.10 = f32[1,4224]{1,0:T(1,128)S(1)} collective-permute-done((f32[1,4224]{1,0:T(1,128)S(1)}, f32[1,4224]{1,0:T(1,128)S(1)}, u32[]{:S(2)}, u32[]{:S(2)}) %collective-permute-start.10) | collective-permute-done | bytes 16928 | tf_op jit(solution)/shard_map/ppermute | solution.py:318
  37.0 1.0 %collective-permute-done.11 = f32[1,4224]{1,0:T(1,128)S(1)} collective-permute-done((f32[1,4224]{1,0:T(1,128)S(1)}, f32[1,4224]{1,0:T(1,128)S(1)}, u32[]{:S(2)}, u32[]{:S(2)}) %collective-permute-start.11) | collective-permute-done | bytes 16928 | tf_op jit(solution)/shard_map/ppermute | solution.py:318
  38.0 0.0 collective-permute-done.9
  38.1 1.1 %collective-permute-start.12 = (f32[1,4224]{1,0:T(1,128)S(1)}, f32[1,4224]{1,0:T(1,128)S(1)}, u32[]{:S(2)}, u32[]{:S(2)}) collective-permute-start(f32[1,4224]{1,0:T(1,128)S(1)} %add_add_fusion.refs_3_), channel_id=1, source_target_pairs={{0,13},{1,12},{2,15},{3,14},{4,9},{5,8},{6,11},{7,10},{8,5},{9,4},... | collective-permute-start | bytes 50696 | tf_op jit(solution)/shard_map/ppermute | solution.py:318
  39.1 0.5 %collective-permute-start.13 = (f32[1,4224]{1,0:T(1,128)S(1)}, f32[1,4224]{1,0:T(1,128)S(1)}, u32[]{:S(2)}, u32[]{:S(2)}) collective-permute-start(f32[1,4224]{1,0:T(1,128)S(1)} %add_add_fusion.refs_3_), channel_id=1, source_target_pairs={{0,9},{1,8},{2,11},{3,10},{4,13},{5,12},{6,15},{7,14},{8,1},{9,0},... | collective-permute-start | bytes 50696 | tf_op jit(solution)/shard_map/ppermute | solution.py:318
  39.6 1.5 %collective-permute-start.14 = (f32[1,4224]{1,0:T(1,128)S(1)}, f32[1,4224]{1,0:T(1,128)S(1)}, u32[]{:S(2)}, u32[]{:S(2)}) collective-permute-start(f32[1,4224]{1,0:T(1,128)S(1)} %add_add_fusion.refs_3_), channel_id=1, source_target_pairs={{0,5},{1,4},{2,7},{3,6},{4,1},{5,0},{6,3},{7,2},{8,13},{9,12},{10,... | collective-permute-start | bytes 50696 | tf_op jit(solution)/shard_map/ppermute | solution.py:318
  41.1 2.0 %collective-permute-done.12.refs_0_ = f32[1,4224]{1,0:T(1,128)S(1)} collective-permute-done((f32[1,4224]{1,0:T(1,128)S(1)}, f32[1,4224]{1,0:T(1,128)S(1)}, u32[]{:S(2)}, u32[]{:S(2)}) %collective-permute-start.12) | collective-permute-done | bytes 16928 | tf_op jit(solution)/shard_map/ppermute | solution.py:318
  43.1 0.2 collective-permute-done.13.refs_1_
  43.3 0.0 collective-permute-done.14.refs_2_
  43.3 1.3 %shard_map.75 = (f32[8,256]{1,0:T(8,128)S(1)}, f32[8,640]{1,0:T(8,128)S(1)}) custom-call(f32[1,4224]{1,0:T(1,128)S(1)} %collective-permute-done.12.refs_0_, f32[1,4224]{1,0:T(1,128)S(1)} %collective-permute-done.13.refs_1_, f32[1,4224]{1,0:T(1,128)S(1)} %collective-permute-done.14.refs_2_, f32[1,4224]{1,0:T(1,128)S(1)} %add_add_fusion.refs_3_, ...), custom_call_target="tpu_custom_call" | custom-call | tf_op jit(solution)/shard_map/pallas_call | solution.py:294
  44.5 1.5 %collective-permute-start.15 = (f32[8,640]{1,0:T(8,128)S(1)}, f32[8,640]{1,0:T(8,128)S(1)}, u32[]{:S(2)}, u32[]{:S(2)}) collective-permute-start(f32[8,640]{1,0:T(8,128)S(1)} %get-tuple-element.40.refs_1_), channel_id=1, source_target_pairs={{0,16},{16,0},{1,17},{17,1},{2,18},{18,2},{3,19},{19,3},{4,20},{20... | collective-permute-start | bytes 61448 | tf_op jit(solution)/shard_map/ppermute | solution.py:318
  46.1 2.3 %collective-permute-done.15.refs_0_ = f32[8,640]{1,0:T(8,128)S(1)} collective-permute-done((f32[8,640]{1,0:T(8,128)S(1)}, f32[8,640]{1,0:T(8,128)S(1)}, u32[]{:S(2)}, u32[]{:S(2)}) %collective-permute-start.15) | collective-permute-done | bytes 20512 | tf_op jit(solution)/shard_map/ppermute | solution.py:318
  48.3 0.7 %shard_map.76 = (f32[8,512]{1,0:T(8,128)}, f32[8,512]{1,0:T(8,128)}) custom-call(f32[8,640]{1,0:T(8,128)S(1)} %collective-permute-done.15.refs_0_, f32[8,640]{1,0:T(8,128)S(1)} %get-tuple-element.40.refs_1_, f32[1,512]{1,0:T(1,128)S(1)} %get-tuple-element.30.refs_2_, f32[8,512]{1,0:T(8,128)S(1)} %get-tuple-element.36.refs_5_.refs_3_, ...), custom_call_target="tpu_custom_call" | custom-call | tf_op jit(solution)/shard_map/pallas_call | solution.py:294
  (2 shorter events, 0.1 us)
Async XLA Ops:
  2.6 5.2 %collective-permute-start = (bf16[64,512]{1,0:T(8,128)(2,1)S(1)}, bf16[64,512]{1,0:T(8,128)(2,1)S(1)}, u32[]{:S(2)}, u32[]{:S(2)}) collective-permute-start(bf16[64,512]{1,0:T(8,128)(2,1)S(1)} %get-tuple-element.28.refs_1_), channel_id=1, source_target_pairs={{0,16},{16,0},{1,17},{17,1},{2,18},{18,2},{3,19},{19,3},{4,20},{20... | collective-permute-start | bytes 196616 | tf_op jit(solution)/shard_map/ppermute | solution.py:318
  10.4 4.0 %collective-permute-start.1 = (f32[8,512]{1,0:T(8,128)S(1)}, f32[8,512]{1,0:T(8,128)S(1)}, u32[]{:S(2)}, u32[]{:S(2)}) collective-permute-start(f32[8,512]{1,0:T(8,128)S(1)} %get-tuple-element.29.refs_1_), channel_id=1, source_target_pairs={{0,16},{16,0},{1,17},{17,1},{2,18},{18,2},{3,19},{19,3},{4,20},{20... | collective-permute-start | bytes 49160 | tf_op jit(solution)/shard_map/ppermute | solution.py:318
  15.6 3.2 %collective-permute-start.2 = (f32[1,4224]{1,0:T(1,128)S(1)}, f32[1,4224]{1,0:T(1,128)S(1)}, u32[]{:S(2)}, u32[]{:S(2)}) collective-permute-start(f32[1,4224]{1,0:T(1,128)S(1)} %get-tuple-element.33), channel_id=1, source_target_pairs={{0,3},{1,2},{2,1},{3,0},{4,7},{5,6},{6,5},{7,4},{8,11},{9,10},{10,... | collective-permute-start | bytes 50696 | tf_op jit(solution)/shard_map/ppermute | solution.py:318
  15.7 3.8 %collective-permute-start.3 = (f32[1,4224]{1,0:T(1,128)S(1)}, f32[1,4224]{1,0:T(1,128)S(1)}, u32[]{:S(2)}, u32[]{:S(2)}) collective-permute-start(f32[1,4224]{1,0:T(1,128)S(1)} %get-tuple-element.33), channel_id=1, source_target_pairs={{0,2},{1,3},{2,0},{3,1},{4,6},{5,7},{6,4},{7,5},{8,10},{9,11},{10,... | collective-permute-start | bytes 50696 | tf_op jit(solution)/shard_map/ppermute | solution.py:318
  17.6 1.9 %collective-permute-start.4 = (f32[1,4224]{1,0:T(1,128)S(1)}, f32[1,4224]{1,0:T(1,128)S(1)}, u32[]{:S(2)}, u32[]{:S(2)}) collective-permute-start(f32[1,4224]{1,0:T(1,128)S(1)} %get-tuple-element.33), channel_id=1, source_target_pairs={{0,1},{1,0},{2,3},{3,2},{4,5},{5,4},{6,7},{7,6},{8,9},{9,8},{10,11... | collective-permute-start | bytes 50696 | tf_op jit(solution)/shard_map/ppermute | solution.py:318
  19.5 5.5 %collective-permute-start.5 = (f32[1,4224]{1,0:T(1,128)S(1)}, f32[1,4224]{1,0:T(1,128)S(1)}, u32[]{:S(2)}, u32[]{:S(2)}) collective-permute-start(f32[1,4224]{1,0:T(1,128)S(1)} %add_add_fusion.1.refs_3_), channel_id=1, source_target_pairs={{0,13},{1,12},{2,15},{3,14},{4,9},{5,8},{6,11},{7,10},{8,5},{9,4},... | collective-permute-start | bytes 50696 | tf_op jit(solution)/shard_map/ppermute | solution.py:318
  23.5 4.1 %collective-permute-start.6 = (f32[1,4224]{1,0:T(1,128)S(1)}, f32[1,4224]{1,0:T(1,128)S(1)}, u32[]{:S(2)}, u32[]{:S(2)}) collective-permute-start(f32[1,4224]{1,0:T(1,128)S(1)} %add_add_fusion.1.refs_3_), channel_id=1, source_target_pairs={{0,9},{1,8},{2,11},{3,10},{4,13},{5,12},{6,15},{7,14},{8,1},{9,0},... | collective-permute-start | bytes 50696 | tf_op jit(solution)/shard_map/ppermute | solution.py:318
  23.5 4.1 %collective-permute-start.7 = (f32[1,4224]{1,0:T(1,128)S(1)}, f32[1,4224]{1,0:T(1,128)S(1)}, u32[]{:S(2)}, u32[]{:S(2)}) collective-permute-start(f32[1,4224]{1,0:T(1,128)S(1)} %add_add_fusion.1.refs_3_), channel_id=1, source_target_pairs={{0,5},{1,4},{2,7},{3,6},{4,1},{5,0},{6,3},{7,2},{8,13},{9,12},{10,... | collective-permute-start | bytes 50696 | tf_op jit(solution)/shard_map/ppermute | solution.py:318
  28.8 3.8 %collective-permute-start.8 = (f32[8,640]{1,0:T(8,128)S(1)}, f32[8,640]{1,0:T(8,128)S(1)}, u32[]{:S(2)}, u32[]{:S(2)}) collective-permute-start(f32[8,640]{1,0:T(8,128)S(1)} %get-tuple-element.35.refs_1_), channel_id=1, source_target_pairs={{0,16},{16,0},{1,17},{17,1},{2,18},{18,2},{3,19},{19,3},{4,20},{20... | collective-permute-start | bytes 61448 | tf_op jit(solution)/shard_map/ppermute | solution.py:318
  33.8 3.2 %collective-permute-start.10 = (f32[1,4224]{1,0:T(1,128)S(1)}, f32[1,4224]{1,0:T(1,128)S(1)}, u32[]{:S(2)}, u32[]{:S(2)}) collective-permute-start(f32[1,4224]{1,0:T(1,128)S(1)} %get-tuple-element.38), channel_id=1, source_target_pairs={{0,3},{1,2},{2,1},{3,0},{4,7},{5,6},{6,5},{7,4},{8,11},{9,10},{10,... | collective-permute-start | bytes 50696 | tf_op jit(solution)/shard_map/ppermute | solution.py:318
  34.3 3.7 %collective-permute-start.11 = (f32[1,4224]{1,0:T(1,128)S(1)}, f32[1,4224]{1,0:T(1,128)S(1)}, u32[]{:S(2)}, u32[]{:S(2)}) collective-permute-start(f32[1,4224]{1,0:T(1,128)S(1)} %get-tuple-element.38), channel_id=1, source_target_pairs={{0,2},{1,3},{2,0},{3,1},{4,6},{5,7},{6,4},{7,5},{8,10},{9,11},{10,... | collective-permute-start | bytes 50696 | tf_op jit(solution)/shard_map/ppermute | solution.py:318
  34.6 3.4 %collective-permute-start.9 = (f32[1,4224]{1,0:T(1,128)S(1)}, f32[1,4224]{1,0:T(1,128)S(1)}, u32[]{:S(2)}, u32[]{:S(2)}) collective-permute-start(f32[1,4224]{1,0:T(1,128)S(1)} %get-tuple-element.38), channel_id=1, source_target_pairs={{0,1},{1,0},{2,3},{3,2},{4,5},{5,4},{6,7},{7,6},{8,9},{9,8},{10,11... | collective-permute-start | bytes 50696 | tf_op jit(solution)/shard_map/ppermute | solution.py:318
  38.1 5.0 %collective-permute-start.12 = (f32[1,4224]{1,0:T(1,128)S(1)}, f32[1,4224]{1,0:T(1,128)S(1)}, u32[]{:S(2)}, u32[]{:S(2)}) collective-permute-start(f32[1,4224]{1,0:T(1,128)S(1)} %add_add_fusion.refs_3_), channel_id=1, source_target_pairs={{0,13},{1,12},{2,15},{3,14},{4,9},{5,8},{6,11},{7,10},{8,5},{9,4},... | collective-permute-start | bytes 50696 | tf_op jit(solution)/shard_map/ppermute | solution.py:318
  39.1 4.2 %collective-permute-start.13 = (f32[1,4224]{1,0:T(1,128)S(1)}, f32[1,4224]{1,0:T(1,128)S(1)}, u32[]{:S(2)}, u32[]{:S(2)}) collective-permute-start(f32[1,4224]{1,0:T(1,128)S(1)} %add_add_fusion.refs_3_), channel_id=1, source_target_pairs={{0,9},{1,8},{2,11},{3,10},{4,13},{5,12},{6,15},{7,14},{8,1},{9,0},... | collective-permute-start | bytes 50696 | tf_op jit(solution)/shard_map/ppermute | solution.py:318
  39.6 3.7 %collective-permute-start.14 = (f32[1,4224]{1,0:T(1,128)S(1)}, f32[1,4224]{1,0:T(1,128)S(1)}, u32[]{:S(2)}, u32[]{:S(2)}) collective-permute-start(f32[1,4224]{1,0:T(1,128)S(1)} %add_add_fusion.refs_3_), channel_id=1, source_target_pairs={{0,5},{1,4},{2,7},{3,6},{4,1},{5,0},{6,3},{7,2},{8,13},{9,12},{10,... | collective-permute-start | bytes 50696 | tf_op jit(solution)/shard_map/ppermute | solution.py:318
  44.5 3.8 %collective-permute-start.15 = (f32[8,640]{1,0:T(8,128)S(1)}, f32[8,640]{1,0:T(8,128)S(1)}, u32[]{:S(2)}, u32[]{:S(2)}) collective-permute-start(f32[8,640]{1,0:T(8,128)S(1)} %get-tuple-element.40.refs_1_), channel_id=1, source_target_pairs={{0,16},{16,0},{1,17},{17,1},{2,18},{18,2},{3,19},{19,3},{4,20},{20... | collective-permute-start | bytes 61448 | tf_op jit(solution)/shard_map/ppermute | solution.py:318

commit v20 on v13

--- a/solution.py
+++ b/solution.py
@@ -11,6 +11,7 @@
 SLOTS = 8
 RIDGE = 0.5
 CHUNK = 512
+BUILD = 1024
 EXTRA = 128
 DEPTH = 256
 STEP = 256
@@ -151,7 +152,7 @@
     total = jnp.zeros(out_ref.shape, f32)
 
     def fold(begin):
-        end = begin + CHUNK
+        end = begin + BUILD
         return product(
             weight_ref[:, begin:end],
             block_ref[begin:end, :],
@@ -160,20 +161,20 @@
 
     def inner(begin):
         return jnp.dot(
-            turned_ref[begin : begin + CHUNK, :], center, preferred_element_type=f32
+            turned_ref[begin : begin + BUILD, :], center, preferred_element_type=f32
         )
 
     ahead = inner(0)
-    for begin in range(0, row_count, CHUNK):
+    for begin in range(0, row_count, BUILD):
         exponent = ahead
-        if begin + CHUNK < row_count:
-            ahead = inner(begin + CHUNK)
+        if begin + BUILD < row_count:
+            ahead = inner(begin + BUILD)
         high, low = kernel_parts(exponent)
-        block_ref[begin : begin + CHUNK, :] = high
-        block_ref[row_count + begin : row_count + begin + CHUNK, :] = low
+        block_ref[begin : begin + BUILD, :] = high
+        block_ref[row_count + begin : row_count + begin + BUILD, :] = low
         if begin > 0:
-            total += fold(begin - CHUNK)
-    out_ref[...] = total + fold(row_count - CHUNK)
+            total += fold(begin - BUILD)
+    out_ref[...] = total + fold(row_count - BUILD)
 
 
 def turned_body(columns_ref, center_ref, block_ref):
@@ -182,17 +183,17 @@
 
     def inner(begin):
         return jnp.dot(
-            center, columns_ref[:, begin : begin + CHUNK], preferred_element_type=f32
+            center, columns_ref[:, begin : begin + BUILD], preferred_element_type=f32
         )
 
     ahead = inner(0)
-    for begin in range(0, row_count, CHUNK):
+    for begin in range(0, row_count, BUILD):
         exponent = ahead
-        if begin + CHUNK < row_count:
-            ahead = inner(begin + CHUNK)
+        if begin + BUILD < row_count:
+            ahead = inner(begin + BUILD)
         high, low = kernel_parts(exponent)
-        block_ref[0:count, begin : begin + CHUNK] = high
-        block_ref[count:, begin : begin + CHUNK] = low
+        block_ref[0:count, begin : begin + BUILD] = high
+        block_ref[count:, begin : begin + BUILD] = low
 
 
 def apply_rows(scaled, turned_ref, slots_ref, out_ref):

time: 49.1 us -> 49.3 us (level)
  no operation moved by 1% of the time
where the time goes in v20:
time: 49.3 us; the launch traced here: 49.2 us
  starting transfers between devices  19.5 us (40%)
  waiting for transfers between devices  16.1 us (33%)
  Pallas kernels  12.8 us (26%)
  between operations  0.71 us (1%)
    ppermute x16, starting transfers between devices, exchange(): parts.insert(0, lax.ppermute(value, axis, pairs))  19.5 us
    ppermute x16, waiting for transfers between devices, exchange(): parts.insert(0, lax.ppermute(value, axis, pairs))  16.1 us
    pallas_call x9, Pallas kernels, call(): pl.pallas_call(body, out_shape=out_shape, in_specs=[source] * len(args),...  12.8 us
  transfers between devices with their start and end apart: 16, of which 11 were waited for; matrix products, arithmetic and copies ran while one was open for 0% of the time, Pallas kernels for 5%

profile of v20, /device:TPU:0, one launch (start us, length us, event | category | flops | bytes accessed | tf_op | source)
XLA Modules:
  0.0 49.2 jit_solution(7580894394791971265)
XLA Ops:
  0.6 1.9 %shard_map.68 = (bf16[64,4096]{1,0:T(8,128)(2,1)S(1)}, s32[1,4096]{1,0:T(1,128)S(1)}, f32[1,4096]{1,0:T(1,128)S(1)}, f32[1,512]{1,0:T(1,128)S(1)}, bf16[64,512]{1,0:T(8,128)(2,1)S(1)}) custom-call(bf16[64,4096]{1,0:T(8,128)(2,1)} %feat_hbm.1, s32[1,512]{1,0:T(1,128)} %bitcast.6, s32[1,4096]{1,0:T(1,128)} %bitcast.4, f32[1,4096]{1,0:T(1,128)} %bitcast.5, ...), custom_call_target="tpu_custom_call" | custom-call | tf_op jit(solution)/shard_map/pallas_call | solution.py:289
  2.6 3.0 %collective-permute-start = (bf16[64,512]{1,0:T(8,128)(2,1)S(1)}, bf16[64,512]{1,0:T(8,128)(2,1)S(1)}, u32[]{:S(2)}, u32[]{:S(2)}) collective-permute-start(bf16[64,512]{1,0:T(8,128)(2,1)S(1)} %get-tuple-element.28.refs_1_), channel_id=1, source_target_pairs={{0,16},{16,0},{1,17},{17,1},{2,18},{18,2},{3,19},{19,3},{4,20},{20... | collective-permute-start | bytes 196616 | tf_op jit(solution)/shard_map/ppermute | solution.py:313
  5.6 0.7 %shard_map.69 = (bf16[256,4096]{1,0:T(8,128)(2,1)S(1)}, bf16[4096,256]{1,0:T(8,128)(2,1)S(1)}, bf16[16,4096]{1,0:T(8,128)(2,1)S(1)}) custom-call(bf16[64,4096]{1,0:T(8,128)(2,1)S(1)} %get-tuple-element.23.feat_ref, s32[1,4096]{1,0:T(1,128)S(1)} %get-tuple-element.24.slots_ref.refs_3_.refs_4_, f32[1,4096]{1,0:T(1,128)S(1)} %get-tuple-element.25.prices_ref), custom_call_target="tpu_custom_call" | custom-call | flops 4096000 | bytes 4194304 | tf_op jit(solution)/shard_map/pallas_call | solution.py:289
  6.3 1.6 %collective-permute-done.refs_0_ = bf16[64,512]{1,0:T(8,128)(2,1)S(1)} collective-permute-done((bf16[64,512]{1,0:T(8,128)(2,1)S(1)}, bf16[64,512]{1,0:T(8,128)(2,1)S(1)}, u32[]{:S(2)}, u32[]{:S(2)}) %collective-permute-start) | collective-permute-done | bytes 65568 | tf_op jit(solution)/shard_map/ppermute | solution.py:313
  7.8 2.8 %shard_map.70 = (bf16[8192,512]{1,0:T(8,128)(2,1)S(1)}, bf16[256,512]{1,0:T(8,128)(2,1)S(1)}, f32[8,512]{1,0:T(8,128)S(1)}) custom-call(bf16[4096,256]{1,0:T(8,128)(2,1)S(1)} %get-tuple-element.26.turned_ref, bf16[16,4096]{1,0:T(8,128)(2,1)S(1)} %get-tuple-element.27.weight_ref, bf16[64,512]{1,0:T(8,128)(2,1)S(1)} %collective-permute-done.refs_0_, ...), custom_call_target="tpu_custom_call" | custom-call | flops 134217728 | bytes 8388608 | tf_op jit(solution)/shard_map/pallas_call | solution.py:289
  10.6 2.0 %collective-permute-start.1 = (f32[8,512]{1,0:T(8,128)S(1)}, f32[8,512]{1,0:T(8,128)S(1)}, u32[]{:S(2)}, u32[]{:S(2)}) collective-permute-start(f32[8,512]{1,0:T(8,128)S(1)} %get-tuple-element.29.refs_1_), channel_id=1, source_target_pairs={{0,16},{16,0},{1,17},{17,1},{2,18},{18,2},{3,19},{19,3},{4,20},{20... | collective-permute-start | bytes 49160 | tf_op jit(solution)/shard_map/ppermute | solution.py:313
  12.6 1.9 %shard_map.71.refs_4_ = bf16[1024,4096]{1,0:T(8,128)(2,1)S(1)} custom-call(bf16[256,4096]{1,0:T(8,128)(2,1)S(1)} %get-tuple-element.31.columns_ref, bf16[256,512]{1,0:T(8,128)(2,1)S(1)} %get-tuple-element.32.center_ref), custom_call_target="tpu_custom_call" | custom-call | flops 134217728 | bytes 8388608 | tf_op jit(solution)/shard_map/pallas_call | solution.py:289
  14.6 0.0 collective-permute-done.1.refs_0_
  14.6 1.2 %shard_map.72 = (f32[8,512]{1,0:T(8,128)S(1)}, f32[1,4224]{1,0:T(1,128)S(1)}) custom-call(f32[8,512]{1,0:T(8,128)S(1)} %collective-permute-done.1.refs_0_, f32[8,512]{1,0:T(8,128)S(1)} %get-tuple-element.29.refs_1_, f32[1,512]{1,0:T(1,128)S(1)} %get-tuple-element.30.refs_2_, s32[1,4096]{1,0:T(1,128)S(1)} %get-tuple-element.24.slots_ref.refs_3_.refs_4_, ...), custom_call_target="tpu_custom_call" | custom-call | tf_op jit(solution)/shard_map/pallas_call | solution.py:289
  15.8 0.1 collective-permute-start.2
  15.9 1.9 %collective-permute-start.3 = (f32[1,4224]{1,0:T(1,128)S(1)}, f32[1,4224]{1,0:T(1,128)S(1)}, u32[]{:S(2)}, u32[]{:S(2)}) collective-permute-start(f32[1,4224]{1,0:T(1,128)S(1)} %get-tuple-element.33), channel_id=1, source_target_pairs={{0,2},{1,3},{2,0},{3,1},{4,6},{5,7},{6,4},{7,5},{8,10},{9,11},{10,... | collective-permute-start | bytes 50696 | tf_op jit(solution)/shard_map/ppermute | solution.py:313
  17.8 0.0 collective-permute-start.4
  17.8 1.2 %collective-permute-done.2 = f32[1,4224]{1,0:T(1,128)S(1)} collective-permute-done((f32[1,4224]{1,0:T(1,128)S(1)}, f32[1,4224]{1,0:T(1,128)S(1)}, u32[]{:S(2)}, u32[]{:S(2)}) %collective-permute-start.2) | collective-permute-done | bytes 16928 | tf_op jit(solution)/shard_map/ppermute | solution.py:313
  19.0 0.7 %collective-permute-done.3 = f32[1,4224]{1,0:T(1,128)S(1)} collective-permute-done((f32[1,4224]{1,0:T(1,128)S(1)}, f32[1,4224]{1,0:T(1,128)S(1)}, u32[]{:S(2)}, u32[]{:S(2)}) %collective-permute-start.3) | collective-permute-done | bytes 16928 | tf_op jit(solution)/shard_map/ppermute | solution.py:313
  19.7 0.0 collective-permute-done.4
  19.7 4.0 %collective-permute-start.5 = (f32[1,4224]{1,0:T(1,128)S(1)}, f32[1,4224]{1,0:T(1,128)S(1)}, u32[]{:S(2)}, u32[]{:S(2)}) collective-permute-start(f32[1,4224]{1,0:T(1,128)S(1)} %add_add_fusion.1.refs_3_), channel_id=1, source_target_pairs={{0,13},{1,12},{2,15},{3,14},{4,9},{5,8},{6,11},{7,10},{8,5},{9,4},... | collective-permute-start | bytes 50696 | tf_op jit(solution)/shard_map/ppermute | solution.py:313
  23.7 0.0 collective-permute-start.6
  23.7 0.5 collective-permute-start.7
  24.2 1.0 %collective-permute-done.5.refs_0_ = f32[1,4224]{1,0:T(1,128)S(1)} collective-permute-done((f32[1,4224]{1,0:T(1,128)S(1)}, f32[1,4224]{1,0:T(1,128)S(1)}, u32[]{:S(2)}, u32[]{:S(2)}) %collective-permute-start.5) | collective-permute-done | bytes 16928 | tf_op jit(solution)/shard_map/ppermute | solution.py:313
  25.2 2.6 %collective-permute-done.6.refs_1_ = f32[1,4224]{1,0:T(1,128)S(1)} collective-permute-done((f32[1,4224]{1,0:T(1,128)S(1)}, f32[1,4224]{1,0:T(1,128)S(1)}, u32[]{:S(2)}, u32[]{:S(2)}) %collective-permute-start.6) | collective-permute-done | bytes 16928 | tf_op jit(solution)/shard_map/ppermute | solution.py:313
  27.8 0.0 collective-permute-done.7.refs_2_
  27.8 1.2 %shard_map.73 = (f32[1,4224]{1,0:T(1,128)S(1)}, f32[8,128]{1,0:T(8,128)S(1)}, f32[8,640]{1,0:T(8,128)S(1)}) custom-call(f32[1,4224]{1,0:T(1,128)S(1)} %collective-permute-done.5.refs_0_, f32[1,4224]{1,0:T(1,128)S(1)} %collective-permute-done.6.refs_1_, f32[1,4224]{1,0:T(1,128)S(1)} %collective-permute-done.7.refs_2_, f32[1,4224]{1,0:T(1,128)S(1)} %add_add_fusion.1.refs_3_, ...), custom_call_target="tpu_custom_call" | custom-call | tf_op jit(solution)/shard_map/pallas_call | solution.py:289
  29.0 1.5 %collective-permute-start.8 = (f32[8,640]{1,0:T(8,128)S(1)}, f32[8,640]{1,0:T(8,128)S(1)}, u32[]{:S(2)}, u32[]{:S(2)}) collective-permute-start(f32[8,640]{1,0:T(8,128)S(1)} %get-tuple-element.35.refs_1_), channel_id=1, source_target_pairs={{0,16},{16,0},{1,17},{17,1},{2,18},{18,2},{3,19},{19,3},{4,20},{20... | collective-permute-start | bytes 61448 | tf_op jit(solution)/shard_map/ppermute | solution.py:313
  30.5 2.3 %collective-permute-done.8.refs_0_ = f32[8,640]{1,0:T(8,128)S(1)} collective-permute-done((f32[8,640]{1,0:T(8,128)S(1)}, f32[8,640]{1,0:T(8,128)S(1)}, u32[]{:S(2)}, u32[]{:S(2)}) %collective-permute-start.8) | collective-permute-done | bytes 20512 | tf_op jit(solution)/shard_map/ppermute | solution.py:313
  32.8 1.2 %shard_map.74 = (f32[8,512]{1,0:T(8,128)S(1)}, f32[8,128]{1,0:T(8,128)S(1)}, f32[1,4224]{1,0:T(1,128)S(1)}) custom-call(f32[8,640]{1,0:T(8,128)S(1)} %collective-permute-done.8.refs_0_, f32[8,640]{1,0:T(8,128)S(1)} %get-tuple-element.35.refs_1_, f32[1,512]{1,0:T(1,128)S(1)} %get-tuple-element.30.refs_2_, ...), custom_call_target="tpu_custom_call" | custom-call | tf_op jit(solution)/shard_map/pallas_call | solution.py:289
  34.0 0.5 collective-permute-start.10
  34.5 0.4 collective-permute-start.11
  34.9 1.1 %collective-permute-start.9 = (f32[1,4224]{1,0:T(1,128)S(1)}, f32[1,4224]{1,0:T(1,128)S(1)}, u32[]{:S(2)}, u32[]{:S(2)}) collective-permute-start(f32[1,4224]{1,0:T(1,128)S(1)} %get-tuple-element.38), channel_id=1, source_target_pairs={{0,1},{1,0},{2,3},{3,2},{4,5},{5,4},{6,7},{7,6},{8,9},{9,8},{10,11... | collective-permute-start | bytes 50696 | tf_op jit(solution)/shard_map/ppermute | solution.py:313
  35.9 1.3 %collective-permute-done.10 = f32[1,4224]{1,0:T(1,128)S(1)} collective-permute-done((f32[1,4224]{1,0:T(1,128)S(1)}, f32[1,4224]{1,0:T(1,128)S(1)}, u32[]{:S(2)}, u32[]{:S(2)}) %collective-permute-start.10) | collective-permute-done | bytes 16928 | tf_op jit(solution)/shard_map/ppermute | solution.py:313
  37.3 1.0 %collective-permute-done.11 = f32[1,4224]{1,0:T(1,128)S(1)} collective-permute-done((f32[1,4224]{1,0:T(1,128)S(1)}, f32[1,4224]{1,0:T(1,128)S(1)}, u32[]{:S(2)}, u32[]{:S(2)}) %collective-permute-start.11) | collective-permute-done | bytes 16928 | tf_op jit(solution)/shard_map/ppermute | solution.py:313
  38.2 0.0 collective-permute-done.9
  38.3 1.0 %collective-permute-start.12 = (f32[1,4224]{1,0:T(1,128)S(1)}, f32[1,4224]{1,0:T(1,128)S(1)}, u32[]{:S(2)}, u32[]{:S(2)}) collective-permute-start(f32[1,4224]{1,0:T(1,128)S(1)} %add_add_fusion.refs_3_), channel_id=1, source_target_pairs={{0,13},{1,12},{2,15},{3,14},{4,9},{5,8},{6,11},{7,10},{8,5},{9,4},... | collective-permute-start | bytes 50696 | tf_op jit(solution)/shard_map/ppermute | solution.py:313
  39.3 0.5 %collective-permute-start.13 = (f32[1,4224]{1,0:T(1,128)S(1)}, f32[1,4224]{1,0:T(1,128)S(1)}, u32[]{:S(2)}, u32[]{:S(2)}) collective-permute-start(f32[1,4224]{1,0:T(1,128)S(1)} %add_add_fusion.refs_3_), channel_id=1, source_target_pairs={{0,9},{1,8},{2,11},{3,10},{4,13},{5,12},{6,15},{7,14},{8,1},{9,0},... | collective-permute-start | bytes 50696 | tf_op jit(solution)/shard_map/ppermute | solution.py:313
  39.8 1.5 %collective-permute-start.14 = (f32[1,4224]{1,0:T(1,128)S(1)}, f32[1,4224]{1,0:T(1,128)S(1)}, u32[]{:S(2)}, u32[]{:S(2)}) collective-permute-start(f32[1,4224]{1,0:T(1,128)S(1)} %add_add_fusion.refs_3_), channel_id=1, source_target_pairs={{0,5},{1,4},{2,7},{3,6},{4,1},{5,0},{6,3},{7,2},{8,13},{9,12},{10,... | collective-permute-start | bytes 50696 | tf_op jit(solution)/shard_map/ppermute | solution.py:313
  41.3 2.0 %collective-permute-done.12.refs_0_ = f32[1,4224]{1,0:T(1,128)S(1)} collective-permute-done((f32[1,4224]{1,0:T(1,128)S(1)}, f32[1,4224]{1,0:T(1,128)S(1)}, u32[]{:S(2)}, u32[]{:S(2)}) %collective-permute-start.12) | collective-permute-done | bytes 16928 | tf_op jit(solution)/shard_map/ppermute | solution.py:313
  43.3 0.2 collective-permute-done.13.refs_1_
  43.5 0.0 collective-permute-done.14.refs_2_
  43.5 1.3 %shard_map.75 = (f32[8,256]{1,0:T(8,128)S(1)}, f32[8,640]{1,0:T(8,128)S(1)}) custom-call(f32[1,4224]{1,0:T(1,128)S(1)} %collective-permute-done.12.refs_0_, f32[1,4224]{1,0:T(1,128)S(1)} %collective-permute-done.13.refs_1_, f32[1,4224]{1,0:T(1,128)S(1)} %collective-permute-done.14.refs_2_, f32[1,4224]{1,0:T(1,128)S(1)} %add_add_fusion.refs_3_, ...), custom_call_target="tpu_custom_call" | custom-call | tf_op jit(solution)/shard_map/pallas_call | solution.py:289
  44.8 1.5 %collective-permute-start.15 = (f32[8,640]{1,0:T(8,128)S(1)}, f32[8,640]{1,0:T(8,128)S(1)}, u32[]{:S(2)}, u32[]{:S(2)}) collective-permute-start(f32[8,640]{1,0:T(8,128)S(1)} %get-tuple-element.40.refs_1_), channel_id=1, source_target_pairs={{0,16},{16,0},{1,17},{17,1},{2,18},{18,2},{3,19},{19,3},{4,20},{20... | collective-permute-start | bytes 61448 | tf_op jit(solution)/shard_map/ppermute | solution.py:313
  46.2 2.3 %collective-permute-done.15.refs_0_ = f32[8,640]{1,0:T(8,128)S(1)} collective-permute-done((f32[8,640]{1,0:T(8,128)S(1)}, f32[8,640]{1,0:T(8,128)S(1)}, u32[]{:S(2)}, u32[]{:S(2)}) %collective-permute-start.15) | collective-permute-done | bytes 20512 | tf_op jit(solution)/shard_map/ppermute | solution.py:313
  48.5 0.6 %shard_map.76 = (f32[8,512]{1,0:T(8,128)}, f32[8,512]{1,0:T(8,128)}) custom-call(f32[8,640]{1,0:T(8,128)S(1)} %collective-permute-done.15.refs_0_, f32[8,640]{1,0:T(8,128)S(1)} %get-tuple-element.40.refs_1_, f32[1,512]{1,0:T(1,128)S(1)} %get-tuple-element.30.refs_2_, f32[8,512]{1,0:T(8,128)S(1)} %get-tuple-element.36.refs_5_.refs_3_, ...), custom_call_target="tpu_custom_call" | custom-call | tf_op jit(solution)/shard_map/pallas_call | solution.py:289
  (2 shorter events, 0.1 us)
Async XLA Ops:
  2.6 5.2 %collective-permute-start = (bf16[64,512]{1,0:T(8,128)(2,1)S(1)}, bf16[64,512]{1,0:T(8,128)(2,1)S(1)}, u32[]{:S(2)}, u32[]{:S(2)}) collective-permute-start(bf16[64,512]{1,0:T(8,128)(2,1)S(1)} %get-tuple-element.28.refs_1_), channel_id=1, source_target_pairs={{0,16},{16,0},{1,17},{17,1},{2,18},{18,2},{3,19},{19,3},{4,20},{20... | collective-permute-start | bytes 196616 | tf_op jit(solution)/shard_map/ppermute | solution.py:313
  10.6 4.0 %collective-permute-start.1 = (f32[8,512]{1,0:T(8,128)S(1)}, f32[8,512]{1,0:T(8,128)S(1)}, u32[]{:S(2)}, u32[]{:S(2)}) collective-permute-start(f32[8,512]{1,0:T(8,128)S(1)} %get-tuple-element.29.refs_1_), channel_id=1, source_target_pairs={{0,16},{16,0},{1,17},{17,1},{2,18},{18,2},{3,19},{19,3},{4,20},{20... | collective-permute-start | bytes 49160 | tf_op jit(solution)/shard_map/ppermute | solution.py:313
  15.8 3.2 %collective-permute-start.2 = (f32[1,4224]{1,0:T(1,128)S(1)}, f32[1,4224]{1,0:T(1,128)S(1)}, u32[]{:S(2)}, u32[]{:S(2)}) collective-permute-start(f32[1,4224]{1,0:T(1,128)S(1)} %get-tuple-element.33), channel_id=1, source_target_pairs={{0,3},{1,2},{2,1},{3,0},{4,7},{5,6},{6,5},{7,4},{8,11},{9,10},{10,... | collective-permute-start | bytes 50696 | tf_op jit(solution)/shard_map/ppermute | solution.py:313
  15.9 3.8 %collective-permute-start.3 = (f32[1,4224]{1,0:T(1,128)S(1)}, f32[1,4224]{1,0:T(1,128)S(1)}, u32[]{:S(2)}, u32[]{:S(2)}) collective-permute-start(f32[1,4224]{1,0:T(1,128)S(1)} %get-tuple-element.33), channel_id=1, source_target_pairs={{0,2},{1,3},{2,0},{3,1},{4,6},{5,7},{6,4},{7,5},{8,10},{9,11},{10,... | collective-permute-start | bytes 50696 | tf_op jit(solution)/shard_map/ppermute | solution.py:313
  17.8 1.9 %collective-permute-start.4 = (f32[1,4224]{1,0:T(1,128)S(1)}, f32[1,4224]{1,0:T(1,128)S(1)}, u32[]{:S(2)}, u32[]{:S(2)}) collective-permute-start(f32[1,4224]{1,0:T(1,128)S(1)} %get-tuple-element.33), channel_id=1, source_target_pairs={{0,1},{1,0},{2,3},{3,2},{4,5},{5,4},{6,7},{7,6},{8,9},{9,8},{10,11... | collective-permute-start | bytes 50696 | tf_op jit(solution)/shard_map/ppermute | solution.py:313
  19.7 5.5 %collective-permute-start.5 = (f32[1,4224]{1,0:T(1,128)S(1)}, f32[1,4224]{1,0:T(1,128)S(1)}, u32[]{:S(2)}, u32[]{:S(2)}) collective-permute-start(f32[1,4224]{1,0:T(1,128)S(1)} %add_add_fusion.1.refs_3_), channel_id=1, source_target_pairs={{0,13},{1,12},{2,15},{3,14},{4,9},{5,8},{6,11},{7,10},{8,5},{9,4},... | collective-permute-start | bytes 50696 | tf_op jit(solution)/shard_map/ppermute | solution.py:313
  23.7 4.1 %collective-permute-start.6 = (f32[1,4224]{1,0:T(1,128)S(1)}, f32[1,4224]{1,0:T(1,128)S(1)}, u32[]{:S(2)}, u32[]{:S(2)}) collective-permute-start(f32[1,4224]{1,0:T(1,128)S(1)} %add_add_fusion.1.refs_3_), channel_id=1, source_target_pairs={{0,9},{1,8},{2,11},{3,10},{4,13},{5,12},{6,15},{7,14},{8,1},{9,0},... | collective-permute-start | bytes 50696 | tf_op jit(solution)/shard_map/ppermute | solution.py:313
  23.7 4.1 %collective-permute-start.7 = (f32[1,4224]{1,0:T(1,128)S(1)}, f32[1,4224]{1,0:T(1,128)S(1)}, u32[]{:S(2)}, u32[]{:S(2)}) collective-permute-start(f32[1,4224]{1,0:T(1,128)S(1)} %add_add_fusion.1.refs_3_), channel_id=1, source_target_pairs={{0,5},{1,4},{2,7},{3,6},{4,1},{5,0},{6,3},{7,2},{8,13},{9,12},{10,... | collective-permute-start | bytes 50696 | tf_op jit(solution)/shard_map/ppermute | solution.py:313
  29.0 3.8 %collective-permute-start.8 = (f32[8,640]{1,0:T(8,128)S(1)}, f32[8,640]{1,0:T(8,128)S(1)}, u32[]{:S(2)}, u32[]{:S(2)}) collective-permute-start(f32[8,640]{1,0:T(8,128)S(1)} %get-tuple-element.35.refs_1_), channel_id=1, source_target_pairs={{0,16},{16,0},{1,17},{17,1},{2,18},{18,2},{3,19},{19,3},{4,20},{20... | collective-permute-start | bytes 61448 | tf_op jit(solution)/shard_map/ppermute | solution.py:313
  34.0 3.2 %collective-permute-start.10 = (f32[1,4224]{1,0:T(1,128)S(1)}, f32[1,4224]{1,0:T(1,128)S(1)}, u32[]{:S(2)}, u32[]{:S(2)}) collective-permute-start(f32[1,4224]{1,0:T(1,128)S(1)} %get-tuple-element.38), channel_id=1, source_target_pairs={{0,3},{1,2},{2,1},{3,0},{4,7},{5,6},{6,5},{7,4},{8,11},{9,10},{10,... | collective-permute-start | bytes 50696 | tf_op jit(solution)/shard_map/ppermute | solution.py:313
  34.5 3.7 %collective-permute-start.11 = (f32[1,4224]{1,0:T(1,128)S(1)}, f32[1,4224]{1,0:T(1,128)S(1)}, u32[]{:S(2)}, u32[]{:S(2)}) collective-permute-start(f32[1,4224]{1,0:T(1,128)S(1)} %get-tuple-element.38), channel_id=1, source_target_pairs={{0,2},{1,3},{2,0},{3,1},{4,6},{5,7},{6,4},{7,5},{8,10},{9,11},{10,... | collective-permute-start | bytes 50696 | tf_op jit(solution)/shard_map/ppermute | solution.py:313
  34.9 3.4 %collective-permute-start.9 = (f32[1,4224]{1,0:T(1,128)S(1)}, f32[1,4224]{1,0:T(1,128)S(1)}, u32[]{:S(2)}, u32[]{:S(2)}) collective-permute-start(f32[1,4224]{1,0:T(1,128)S(1)} %get-tuple-element.38), channel_id=1, source_target_pairs={{0,1},{1,0},{2,3},{3,2},{4,5},{5,4},{6,7},{7,6},{8,9},{9,8},{10,11... | collective-permute-start | bytes 50696 | tf_op jit(solution)/shard_map/ppermute | solution.py:313
  38.3 5.0 %collective-permute-start.12 = (f32[1,4224]{1,0:T(1,128)S(1)}, f32[1,4224]{1,0:T(1,128)S(1)}, u32[]{:S(2)}, u32[]{:S(2)}) collective-permute-start(f32[1,4224]{1,0:T(1,128)S(1)} %add_add_fusion.refs_3_), channel_id=1, source_target_pairs={{0,13},{1,12},{2,15},{3,14},{4,9},{5,8},{6,11},{7,10},{8,5},{9,4},... | collective-permute-start | bytes 50696 | tf_op jit(solution)/shard_map/ppermute | solution.py:313
  39.3 4.2 %collective-permute-start.13 = (f32[1,4224]{1,0:T(1,128)S(1)}, f32[1,4224]{1,0:T(1,128)S(1)}, u32[]{:S(2)}, u32[]{:S(2)}) collective-permute-start(f32[1,4224]{1,0:T(1,128)S(1)} %add_add_fusion.refs_3_), channel_id=1, source_target_pairs={{0,9},{1,8},{2,11},{3,10},{4,13},{5,12},{6,15},{7,14},{8,1},{9,0},... | collective-permute-start | bytes 50696 | tf_op jit(solution)/shard_map/ppermute | solution.py:313
  39.8 3.7 %collective-permute-start.14 = (f32[1,4224]{1,0:T(1,128)S(1)}, f32[1,4224]{1,0:T(1,128)S(1)}, u32[]{:S(2)}, u32[]{:S(2)}) collective-permute-start(f32[1,4224]{1,0:T(1,128)S(1)} %add_add_fusion.refs_3_), channel_id=1, source_target_pairs={{0,5},{1,4},{2,7},{3,6},{4,1},{5,0},{6,3},{7,2},{8,13},{9,12},{10,... | collective-permute-start | bytes 50696 | tf_op jit(solution)/shard_map/ppermute | solution.py:313
  44.8 3.8 %collective-permute-start.15 = (f32[8,640]{1,0:T(8,128)S(1)}, f32[8,640]{1,0:T(8,128)S(1)}, u32[]{:S(2)}, u32[]{:S(2)}) collective-permute-start(f32[8,640]{1,0:T(8,128)S(1)} %get-tuple-element.40.refs_1_), channel_id=1, source_target_pairs={{0,16},{16,0},{1,17},{17,1},{2,18},{18,2},{3,19},{19,3},{4,20},{20... | collective-permute-start | bytes 61448 | tf_op jit(solution)/shard_map/ppermute | solution.py:313

commit v21 on v13

--- a/solution.py
+++ b/solution.py
@@ -98,8 +98,11 @@
     feat_ref, slots_ref, prices_ref, scale_ref, out_ref, idx_ref, hit_ref, sems = refs
     row_count = feat_ref.shape[1]
     count = out_ref.shape[1]
-    sources = (idx_hbm, feat_hbm, slots_hbm, prices_hbm, scale_hbm)
-    targets = (idx_ref, feat_ref, slots_ref, prices_ref, scale_ref)
+    bands = [pl.ds(first, 16) for first in range(0, feat_ref.shape[0], 16)]
+    sources = [idx_hbm, *(feat_hbm.at[band, :] for band in bands)]
+    targets = [idx_ref, *(feat_ref.at[band, :] for band in bands)]
+    sources += [slots_hbm, prices_hbm, scale_hbm]
+    targets += [slots_ref, prices_ref, scale_ref]
     copies = [
         pltpu.make_async_copy(source, target, sems.at[place])
         for place, (source, target) in enumerate(zip(sources, targets))
@@ -118,11 +121,12 @@
 
     for begin in range(0, row_count, STEP):
         hit_ref[begin : begin + STEP, :] = hits(begin)
-    copies[1].wait()
+    for copy in copies[1 : 1 + len(bands)]:
+        copy.wait()
     out_ref[...] = jnp.dot(
         feat_ref[...], hit_ref[...], preferred_element_type=f32
     ).astype(bf16)
-    for copy in copies[2:]:
+    for copy in copies[1 + len(bands) :]:
         copy.wait()
 
 
@@ -354,7 +358,7 @@
         scratch_shapes=[
             pltpu.VMEM((1, count), jnp.int32),
             pltpu.VMEM((row_count, count), bf16),
-            pltpu.SemaphoreType.DMA((5,)),
+            pltpu.SemaphoreType.DMA((4 + depth // 16,)),
         ],
     )
     centers = exchange(picked, "dp")

time: 49.1 us -> 49.2 us (level)
  no operation moved by 1% of the time
where the time goes in v21:
time: 49.2 us; the launch traced here: 49.1 us
  starting transfers between devices  19.6 us (40%)
  waiting for transfers between devices  16 us (33%)
  Pallas kernels  12.6 us (26%)
  between operations  0.71 us (1%)
    ppermute x16, starting transfers between devices, exchange(): parts.insert(0, lax.ppermute(value, axis, pairs))  19.6 us
    ppermute x16, waiting for transfers between devices, exchange(): parts.insert(0, lax.ppermute(value, axis, pairs))  16 us
    pallas_call x9, Pallas kernels, call(): pl.pallas_call(body, out_shape=out_shape, in_specs=[source] * len(args),...  12.6 us
  transfers between devices with their start and end apart: 16, of which 11 were waited for; matrix products, arithmetic and copies ran while one was open for 0% of the time, Pallas kernels for 5%

profile of v21, /device:TPU:0, one launch (start us, length us, event | category | flops | bytes accessed | tf_op | source)
XLA Modules:
  0.0 49.1 jit_solution(18167151213245262533)
XLA Ops:
  0.6 2.0 %shard_map.68 = (bf16[64,4096]{1,0:T(8,128)(2,1)S(1)}, s32[1,4096]{1,0:T(1,128)S(1)}, f32[1,4096]{1,0:T(1,128)S(1)}, f32[1,512]{1,0:T(1,128)S(1)}, bf16[64,512]{1,0:T(8,128)(2,1)S(1)}) custom-call(bf16[64,4096]{1,0:T(8,128)(2,1)} %feat_hbm.1, s32[1,512]{1,0:T(1,128)} %bitcast.6, s32[1,4096]{1,0:T(1,128)} %bitcast.4, f32[1,4096]{1,0:T(1,128)} %bitcast.5, ...), custom_call_target="tpu_custom_call" | custom-call | tf_op jit(solution)/shard_map/pallas_call | solution.py:292
  2.7 3.0 %collective-permute-start = (bf16[64,512]{1,0:T(8,128)(2,1)S(1)}, bf16[64,512]{1,0:T(8,128)(2,1)S(1)}, u32[]{:S(2)}, u32[]{:S(2)}) collective-permute-start(bf16[64,512]{1,0:T(8,128)(2,1)S(1)} %get-tuple-element.28.refs_1_), channel_id=1, source_target_pairs={{0,16},{16,0},{1,17},{17,1},{2,18},{18,2},{3,19},{19,3},{4,20},{20... | collective-permute-start | bytes 196616 | tf_op jit(solution)/shard_map/ppermute | solution.py:316
  5.7 0.7 %shard_map.69 = (bf16[256,4096]{1,0:T(8,128)(2,1)S(1)}, bf16[4096,256]{1,0:T(8,128)(2,1)S(1)}, bf16[16,4096]{1,0:T(8,128)(2,1)S(1)}) custom-call(bf16[64,4096]{1,0:T(8,128)(2,1)S(1)} %get-tuple-element.23.feat_ref, s32[1,4096]{1,0:T(1,128)S(1)} %get-tuple-element.24.slots_ref.refs_3_.refs_4_, f32[1,4096]{1,0:T(1,128)S(1)} %get-tuple-element.25.prices_ref), custom_call_target="tpu_custom_call" | custom-call | flops 4096000 | bytes 4194304 | tf_op jit(solution)/shard_map/pallas_call | solution.py:292
  6.3 1.6 %collective-permute-done.refs_0_ = bf16[64,512]{1,0:T(8,128)(2,1)S(1)} collective-permute-done((bf16[64,512]{1,0:T(8,128)(2,1)S(1)}, bf16[64,512]{1,0:T(8,128)(2,1)S(1)}, u32[]{:S(2)}, u32[]{:S(2)}) %collective-permute-start) | collective-permute-done | bytes 65568 | tf_op jit(solution)/shard_map/ppermute | solution.py:316
  7.9 2.5 %shard_map.70 = (bf16[8192,512]{1,0:T(8,128)(2,1)S(1)}, bf16[256,512]{1,0:T(8,128)(2,1)S(1)}, f32[8,512]{1,0:T(8,128)S(1)}) custom-call(bf16[4096,256]{1,0:T(8,128)(2,1)S(1)} %get-tuple-element.26.turned_ref, bf16[16,4096]{1,0:T(8,128)(2,1)S(1)} %get-tuple-element.27.weight_ref, bf16[64,512]{1,0:T(8,128)(2,1)S(1)} %collective-permute-done.refs_0_, ...), custom_call_target="tpu_custom_call" | custom-call | flops 134217728 | bytes 8388608 | tf_op jit(solution)/shard_map/pallas_call | solution.py:292
  10.4 2.1 %collective-permute-start.1 = (f32[8,512]{1,0:T(8,128)S(1)}, f32[8,512]{1,0:T(8,128)S(1)}, u32[]{:S(2)}, u32[]{:S(2)}) collective-permute-start(f32[8,512]{1,0:T(8,128)S(1)} %get-tuple-element.29.refs_1_), channel_id=1, source_target_pairs={{0,16},{16,0},{1,17},{17,1},{2,18},{18,2},{3,19},{19,3},{4,20},{20... | collective-permute-start | bytes 49160 | tf_op jit(solution)/shard_map/ppermute | solution.py:316
  12.5 1.9 %shard_map.71.refs_4_ = bf16[1024,4096]{1,0:T(8,128)(2,1)S(1)} custom-call(bf16[256,4096]{1,0:T(8,128)(2,1)S(1)} %get-tuple-element.31.columns_ref, bf16[256,512]{1,0:T(8,128)(2,1)S(1)} %get-tuple-element.32.center_ref), custom_call_target="tpu_custom_call" | custom-call | flops 134217728 | bytes 8388608 | tf_op jit(solution)/shard_map/pallas_call | solution.py:292
  14.4 0.0 collective-permute-done.1.refs_0_
  14.4 1.2 %shard_map.72 = (f32[8,512]{1,0:T(8,128)S(1)}, f32[1,4224]{1,0:T(1,128)S(1)}) custom-call(f32[8,512]{1,0:T(8,128)S(1)} %collective-permute-done.1.refs_0_, f32[8,512]{1,0:T(8,128)S(1)} %get-tuple-element.29.refs_1_, f32[1,512]{1,0:T(1,128)S(1)} %get-tuple-element.30.refs_2_, s32[1,4096]{1,0:T(1,128)S(1)} %get-tuple-element.24.slots_ref.refs_3_.refs_4_, ...), custom_call_target="tpu_custom_call" | custom-call | tf_op jit(solution)/shard_map/pallas_call | solution.py:292
  15.7 0.1 collective-permute-start.2
  15.7 1.9 %collective-permute-start.3 = (f32[1,4224]{1,0:T(1,128)S(1)}, f32[1,4224]{1,0:T(1,128)S(1)}, u32[]{:S(2)}, u32[]{:S(2)}) collective-permute-start(f32[1,4224]{1,0:T(1,128)S(1)} %get-tuple-element.33), channel_id=1, source_target_pairs={{0,2},{1,3},{2,0},{3,1},{4,6},{5,7},{6,4},{7,5},{8,10},{9,11},{10,... | collective-permute-start | bytes 50696 | tf_op jit(solution)/shard_map/ppermute | solution.py:316
  17.7 0.0 collective-permute-start.4
  17.7 1.2 %collective-permute-done.2 = f32[1,4224]{1,0:T(1,128)S(1)} collective-permute-done((f32[1,4224]{1,0:T(1,128)S(1)}, f32[1,4224]{1,0:T(1,128)S(1)}, u32[]{:S(2)}, u32[]{:S(2)}) %collective-permute-start.2) | collective-permute-done | bytes 16928 | tf_op jit(solution)/shard_map/ppermute | solution.py:316
  18.9 0.7 %collective-permute-done.3 = f32[1,4224]{1,0:T(1,128)S(1)} collective-permute-done((f32[1,4224]{1,0:T(1,128)S(1)}, f32[1,4224]{1,0:T(1,128)S(1)}, u32[]{:S(2)}, u32[]{:S(2)}) %collective-permute-start.3) | collective-permute-done | bytes 16928 | tf_op jit(solution)/shard_map/ppermute | solution.py:316
  19.5 0.0 collective-permute-done.4
  19.6 4.0 %collective-permute-start.5 = (f32[1,4224]{1,0:T(1,128)S(1)}, f32[1,4224]{1,0:T(1,128)S(1)}, u32[]{:S(2)}, u32[]{:S(2)}) collective-permute-start(f32[1,4224]{1,0:T(1,128)S(1)} %add_add_fusion.1.refs_3_), channel_id=1, source_target_pairs={{0,13},{1,12},{2,15},{3,14},{4,9},{5,8},{6,11},{7,10},{8,5},{9,4},... | collective-permute-start | bytes 50696 | tf_op jit(solution)/shard_map/ppermute | solution.py:316
  23.6 0.0 collective-permute-start.6
  23.6 0.5 collective-permute-start.7
  24.1 1.0 %collective-permute-done.5.refs_0_ = f32[1,4224]{1,0:T(1,128)S(1)} collective-permute-done((f32[1,4224]{1,0:T(1,128)S(1)}, f32[1,4224]{1,0:T(1,128)S(1)}, u32[]{:S(2)}, u32[]{:S(2)}) %collective-permute-start.5) | collective-permute-done | bytes 16928 | tf_op jit(solution)/shard_map/ppermute | solution.py:316
  25.1 2.6 %collective-permute-done.6.refs_1_ = f32[1,4224]{1,0:T(1,128)S(1)} collective-permute-done((f32[1,4224]{1,0:T(1,128)S(1)}, f32[1,4224]{1,0:T(1,128)S(1)}, u32[]{:S(2)}, u32[]{:S(2)}) %collective-permute-start.6) | collective-permute-done | bytes 16928 | tf_op jit(solution)/shard_map/ppermute | solution.py:316
  27.7 0.0 collective-permute-done.7.refs_2_
  27.7 1.2 %shard_map.73 = (f32[1,4224]{1,0:T(1,128)S(1)}, f32[8,128]{1,0:T(8,128)S(1)}, f32[8,640]{1,0:T(8,128)S(1)}) custom-call(f32[1,4224]{1,0:T(1,128)S(1)} %collective-permute-done.5.refs_0_, f32[1,4224]{1,0:T(1,128)S(1)} %collective-permute-done.6.refs_1_, f32[1,4224]{1,0:T(1,128)S(1)} %collective-permute-done.7.refs_2_, f32[1,4224]{1,0:T(1,128)S(1)} %add_add_fusion.1.refs_3_, ...), custom_call_target="tpu_custom_call" | custom-call | tf_op jit(solution)/shard_map/pallas_call | solution.py:292
  28.9 1.5 %collective-permute-start.8 = (f32[8,640]{1,0:T(8,128)S(1)}, f32[8,640]{1,0:T(8,128)S(1)}, u32[]{:S(2)}, u32[]{:S(2)}) collective-permute-start(f32[8,640]{1,0:T(8,128)S(1)} %get-tuple-element.35.refs_1_), channel_id=1, source_target_pairs={{0,16},{16,0},{1,17},{17,1},{2,18},{18,2},{3,19},{19,3},{4,20},{20... | collective-permute-start | bytes 61448 | tf_op jit(solution)/shard_map/ppermute | solution.py:316
  30.4 2.3 %collective-permute-done.8.refs_0_ = f32[8,640]{1,0:T(8,128)S(1)} collective-permute-done((f32[8,640]{1,0:T(8,128)S(1)}, f32[8,640]{1,0:T(8,128)S(1)}, u32[]{:S(2)}, u32[]{:S(2)}) %collective-permute-start.8) | collective-permute-done | bytes 20512 | tf_op jit(solution)/shard_map/ppermute | solution.py:316
  32.7 1.2 %shard_map.74 = (f32[8,512]{1,0:T(8,128)S(1)}, f32[8,128]{1,0:T(8,128)S(1)}, f32[1,4224]{1,0:T(1,128)S(1)}) custom-call(f32[8,640]{1,0:T(8,128)S(1)} %collective-permute-done.8.refs_0_, f32[8,640]{1,0:T(8,128)S(1)} %get-tuple-element.35.refs_1_, f32[1,512]{1,0:T(1,128)S(1)} %get-tuple-element.30.refs_2_, ...), custom_call_target="tpu_custom_call" | custom-call | tf_op jit(solution)/shard_map/pallas_call | solution.py:292
  33.9 0.5 collective-permute-start.10
  34.4 0.4 collective-permute-start.11
  34.7 1.1 %collective-permute-start.9 = (f32[1,4224]{1,0:T(1,128)S(1)}, f32[1,4224]{1,0:T(1,128)S(1)}, u32[]{:S(2)}, u32[]{:S(2)}) collective-permute-start(f32[1,4224]{1,0:T(1,128)S(1)} %get-tuple-element.38), channel_id=1, source_target_pairs={{0,1},{1,0},{2,3},{3,2},{4,5},{5,4},{6,7},{7,6},{8,9},{9,8},{10,11... | collective-permute-start | bytes 50696 | tf_op jit(solution)/shard_map/ppermute | solution.py:316
  35.8 1.3 %collective-permute-done.10 = f32[1,4224]{1,0:T(1,128)S(1)} collective-permute-done((f32[1,4224]{1,0:T(1,128)S(1)}, f32[1,4224]{1,0:T(1,128)S(1)}, u32[]{:S(2)}, u32[]{:S(2)}) %collective-permute-start.10) | collective-permute-done | bytes 16928 | tf_op jit(solution)/shard_map/ppermute | solution.py:316
  37.1 1.0 %collective-permute-done.11 = f32[1,4224]{1,0:T(1,128)S(1)} collective-permute-done((f32[1,4224]{1,0:T(1,128)S(1)}, f32[1,4224]{1,0:T(1,128)S(1)}, u32[]{:S(2)}, u32[]{:S(2)}) %collective-permute-start.11) | collective-permute-done | bytes 16928 | tf_op jit(solution)/shard_map/ppermute | solution.py:316
  38.1 0.0 collective-permute-done.9
  38.2 1.0 %collective-permute-start.12 = (f32[1,4224]{1,0:T(1,128)S(1)}, f32[1,4224]{1,0:T(1,128)S(1)}, u32[]{:S(2)}, u32[]{:S(2)}) collective-permute-start(f32[1,4224]{1,0:T(1,128)S(1)} %add_add_fusion.refs_3_), channel_id=1, source_target_pairs={{0,13},{1,12},{2,15},{3,14},{4,9},{5,8},{6,11},{7,10},{8,5},{9,4},... | collective-permute-start | bytes 50696 | tf_op jit(solution)/shard_map/ppermute | solution.py:316
  39.2 0.5 %collective-permute-start.13 = (f32[1,4224]{1,0:T(1,128)S(1)}, f32[1,4224]{1,0:T(1,128)S(1)}, u32[]{:S(2)}, u32[]{:S(2)}) collective-permute-start(f32[1,4224]{1,0:T(1,128)S(1)} %add_add_fusion.refs_3_), channel_id=1, source_target_pairs={{0,9},{1,8},{2,11},{3,10},{4,13},{5,12},{6,15},{7,14},{8,1},{9,0},... | collective-permute-start | bytes 50696 | tf_op jit(solution)/shard_map/ppermute | solution.py:316
  39.7 1.5 %collective-permute-start.14 = (f32[1,4224]{1,0:T(1,128)S(1)}, f32[1,4224]{1,0:T(1,128)S(1)}, u32[]{:S(2)}, u32[]{:S(2)}) collective-permute-start(f32[1,4224]{1,0:T(1,128)S(1)} %add_add_fusion.refs_3_), channel_id=1, source_target_pairs={{0,5},{1,4},{2,7},{3,6},{4,1},{5,0},{6,3},{7,2},{8,13},{9,12},{10,... | collective-permute-start | bytes 50696 | tf_op jit(solution)/shard_map/ppermute | solution.py:316
  41.2 2.0 %collective-permute-done.12.refs_0_ = f32[1,4224]{1,0:T(1,128)S(1)} collective-permute-done((f32[1,4224]{1,0:T(1,128)S(1)}, f32[1,4224]{1,0:T(1,128)S(1)}, u32[]{:S(2)}, u32[]{:S(2)}) %collective-permute-start.12) | collective-permute-done | bytes 16928 | tf_op jit(solution)/shard_map/ppermute | solution.py:316
  43.2 0.2 collective-permute-done.13.refs_1_
  43.4 0.0 collective-permute-done.14.refs_2_
  43.4 1.3 %shard_map.75 = (f32[8,256]{1,0:T(8,128)S(1)}, f32[8,640]{1,0:T(8,128)S(1)}) custom-call(f32[1,4224]{1,0:T(1,128)S(1)} %collective-permute-done.12.refs_0_, f32[1,4224]{1,0:T(1,128)S(1)} %collective-permute-done.13.refs_1_, f32[1,4224]{1,0:T(1,128)S(1)} %collective-permute-done.14.refs_2_, f32[1,4224]{1,0:T(1,128)S(1)} %add_add_fusion.refs_3_, ...), custom_call_target="tpu_custom_call" | custom-call | tf_op jit(solution)/shard_map/pallas_call | solution.py:292
  44.6 1.5 %collective-permute-start.15 = (f32[8,640]{1,0:T(8,128)S(1)}, f32[8,640]{1,0:T(8,128)S(1)}, u32[]{:S(2)}, u32[]{:S(2)}) collective-permute-start(f32[8,640]{1,0:T(8,128)S(1)} %get-tuple-element.40.refs_1_), channel_id=1, source_target_pairs={{0,16},{16,0},{1,17},{17,1},{2,18},{18,2},{3,19},{19,3},{4,20},{20... | collective-permute-start | bytes 61448 | tf_op jit(solution)/shard_map/ppermute | solution.py:316
  46.1 2.3 %collective-permute-done.15.refs_0_ = f32[8,640]{1,0:T(8,128)S(1)} collective-permute-done((f32[8,640]{1,0:T(8,128)S(1)}, f32[8,640]{1,0:T(8,128)S(1)}, u32[]{:S(2)}, u32[]{:S(2)}) %collective-permute-start.15) | collective-permute-done | bytes 20512 | tf_op jit(solution)/shard_map/ppermute | solution.py:316
  48.4 0.6 %shard_map.76 = (f32[8,512]{1,0:T(8,128)}, f32[8,512]{1,0:T(8,128)}) custom-call(f32[8,640]{1,0:T(8,128)S(1)} %collective-permute-done.15.refs_0_, f32[8,640]{1,0:T(8,128)S(1)} %get-tuple-element.40.refs_1_, f32[1,512]{1,0:T(1,128)S(1)} %get-tuple-element.30.refs_2_, f32[8,512]{1,0:T(8,128)S(1)} %get-tuple-element.36.refs_5_.refs_3_, ...), custom_call_target="tpu_custom_call" | custom-call | tf_op jit(solution)/shard_map/pallas_call | solution.py:292
  (2 shorter events, 0.1 us)
Async XLA Ops:
  2.7 5.2 %collective-permute-start = (bf16[64,512]{1,0:T(8,128)(2,1)S(1)}, bf16[64,512]{1,0:T(8,128)(2,1)S(1)}, u32[]{:S(2)}, u32[]{:S(2)}) collective-permute-start(bf16[64,512]{1,0:T(8,128)(2,1)S(1)} %get-tuple-element.28.refs_1_), channel_id=1, source_target_pairs={{0,16},{16,0},{1,17},{17,1},{2,18},{18,2},{3,19},{19,3},{4,20},{20... | collective-permute-start | bytes 196616 | tf_op jit(solution)/shard_map/ppermute | solution.py:316
  10.4 4.0 %collective-permute-start.1 = (f32[8,512]{1,0:T(8,128)S(1)}, f32[8,512]{1,0:T(8,128)S(1)}, u32[]{:S(2)}, u32[]{:S(2)}) collective-permute-start(f32[8,512]{1,0:T(8,128)S(1)} %get-tuple-element.29.refs_1_), channel_id=1, source_target_pairs={{0,16},{16,0},{1,17},{17,1},{2,18},{18,2},{3,19},{19,3},{4,20},{20... | collective-permute-start | bytes 49160 | tf_op jit(solution)/shard_map/ppermute | solution.py:316
  15.7 3.2 %collective-permute-start.2 = (f32[1,4224]{1,0:T(1,128)S(1)}, f32[1,4224]{1,0:T(1,128)S(1)}, u32[]{:S(2)}, u32[]{:S(2)}) collective-permute-start(f32[1,4224]{1,0:T(1,128)S(1)} %get-tuple-element.33), channel_id=1, source_target_pairs={{0,3},{1,2},{2,1},{3,0},{4,7},{5,6},{6,5},{7,4},{8,11},{9,10},{10,... | collective-permute-start | bytes 50696 | tf_op jit(solution)/shard_map/ppermute | solution.py:316
  15.7 3.8 %collective-permute-start.3 = (f32[1,4224]{1,0:T(1,128)S(1)}, f32[1,4224]{1,0:T(1,128)S(1)}, u32[]{:S(2)}, u32[]{:S(2)}) collective-permute-start(f32[1,4224]{1,0:T(1,128)S(1)} %get-tuple-element.33), channel_id=1, source_target_pairs={{0,2},{1,3},{2,0},{3,1},{4,6},{5,7},{6,4},{7,5},{8,10},{9,11},{10,... | collective-permute-start | bytes 50696 | tf_op jit(solution)/shard_map/ppermute | solution.py:316
  17.7 1.9 %collective-permute-start.4 = (f32[1,4224]{1,0:T(1,128)S(1)}, f32[1,4224]{1,0:T(1,128)S(1)}, u32[]{:S(2)}, u32[]{:S(2)}) collective-permute-start(f32[1,4224]{1,0:T(1,128)S(1)} %get-tuple-element.33), channel_id=1, source_target_pairs={{0,1},{1,0},{2,3},{3,2},{4,5},{5,4},{6,7},{7,6},{8,9},{9,8},{10,11... | collective-permute-start | bytes 50696 | tf_op jit(solution)/shard_map/ppermute | solution.py:316
  19.6 5.5 %collective-permute-start.5 = (f32[1,4224]{1,0:T(1,128)S(1)}, f32[1,4224]{1,0:T(1,128)S(1)}, u32[]{:S(2)}, u32[]{:S(2)}) collective-permute-start(f32[1,4224]{1,0:T(1,128)S(1)} %add_add_fusion.1.refs_3_), channel_id=1, source_target_pairs={{0,13},{1,12},{2,15},{3,14},{4,9},{5,8},{6,11},{7,10},{8,5},{9,4},... | collective-permute-start | bytes 50696 | tf_op jit(solution)/shard_map/ppermute | solution.py:316
  23.6 4.1 %collective-permute-start.6 = (f32[1,4224]{1,0:T(1,128)S(1)}, f32[1,4224]{1,0:T(1,128)S(1)}, u32[]{:S(2)}, u32[]{:S(2)}) collective-permute-start(f32[1,4224]{1,0:T(1,128)S(1)} %add_add_fusion.1.refs_3_), channel_id=1, source_target_pairs={{0,9},{1,8},{2,11},{3,10},{4,13},{5,12},{6,15},{7,14},{8,1},{9,0},... | collective-permute-start | bytes 50696 | tf_op jit(solution)/shard_map/ppermute | solution.py:316
  23.6 4.1 %collective-permute-start.7 = (f32[1,4224]{1,0:T(1,128)S(1)}, f32[1,4224]{1,0:T(1,128)S(1)}, u32[]{:S(2)}, u32[]{:S(2)}) collective-permute-start(f32[1,4224]{1,0:T(1,128)S(1)} %add_add_fusion.1.refs_3_), channel_id=1, source_target_pairs={{0,5},{1,4},{2,7},{3,6},{4,1},{5,0},{6,3},{7,2},{8,13},{9,12},{10,... | collective-permute-start | bytes 50696 | tf_op jit(solution)/shard_map/ppermute | solution.py:316
  28.9 3.8 %collective-permute-start.8 = (f32[8,640]{1,0:T(8,128)S(1)}, f32[8,640]{1,0:T(8,128)S(1)}, u32[]{:S(2)}, u32[]{:S(2)}) collective-permute-start(f32[8,640]{1,0:T(8,128)S(1)} %get-tuple-element.35.refs_1_), channel_id=1, source_target_pairs={{0,16},{16,0},{1,17},{17,1},{2,18},{18,2},{3,19},{19,3},{4,20},{20... | collective-permute-start | bytes 61448 | tf_op jit(solution)/shard_map/ppermute | solution.py:316
  33.9 3.2 %collective-permute-start.10 = (f32[1,4224]{1,0:T(1,128)S(1)}, f32[1,4224]{1,0:T(1,128)S(1)}, u32[]{:S(2)}, u32[]{:S(2)}) collective-permute-start(f32[1,4224]{1,0:T(1,128)S(1)} %get-tuple-element.38), channel_id=1, source_target_pairs={{0,3},{1,2},{2,1},{3,0},{4,7},{5,6},{6,5},{7,4},{8,11},{9,10},{10,... | collective-permute-start | bytes 50696 | tf_op jit(solution)/shard_map/ppermute | solution.py:316
  34.4 3.7 %collective-permute-start.11 = (f32[1,4224]{1,0:T(1,128)S(1)}, f32[1,4224]{1,0:T(1,128)S(1)}, u32[]{:S(2)}, u32[]{:S(2)}) collective-permute-start(f32[1,4224]{1,0:T(1,128)S(1)} %get-tuple-element.38), channel_id=1, source_target_pairs={{0,2},{1,3},{2,0},{3,1},{4,6},{5,7},{6,4},{7,5},{8,10},{9,11},{10,... | collective-permute-start | bytes 50696 | tf_op jit(solution)/shard_map/ppermute | solution.py:316
  34.7 3.4 %collective-permute-start.9 = (f32[1,4224]{1,0:T(1,128)S(1)}, f32[1,4224]{1,0:T(1,128)S(1)}, u32[]{:S(2)}, u32[]{:S(2)}) collective-permute-start(f32[1,4224]{1,0:T(1,128)S(1)} %get-tuple-element.38), channel_id=1, source_target_pairs={{0,1},{1,0},{2,3},{3,2},{4,5},{5,4},{6,7},{7,6},{8,9},{9,8},{10,11... | collective-permute-start | bytes 50696 | tf_op jit(solution)/shard_map/ppermute | solution.py:316
  38.2 5.0 %collective-permute-start.12 = (f32[1,4224]{1,0:T(1,128)S(1)}, f32[1,4224]{1,0:T(1,128)S(1)}, u32[]{:S(2)}, u32[]{:S(2)}) collective-permute-start(f32[1,4224]{1,0:T(1,128)S(1)} %add_add_fusion.refs_3_), channel_id=1, source_target_pairs={{0,13},{1,12},{2,15},{3,14},{4,9},{5,8},{6,11},{7,10},{8,5},{9,4},... | collective-permute-start | bytes 50696 | tf_op jit(solution)/shard_map/ppermute | solution.py:316
  39.2 4.2 %collective-permute-start.13 = (f32[1,4224]{1,0:T(1,128)S(1)}, f32[1,4224]{1,0:T(1,128)S(1)}, u32[]{:S(2)}, u32[]{:S(2)}) collective-permute-start(f32[1,4224]{1,0:T(1,128)S(1)} %add_add_fusion.refs_3_), channel_id=1, source_target_pairs={{0,9},{1,8},{2,11},{3,10},{4,13},{5,12},{6,15},{7,14},{8,1},{9,0},... | collective-permute-start | bytes 50696 | tf_op jit(solution)/shard_map/ppermute | solution.py:316
  39.7 3.7 %collective-permute-start.14 = (f32[1,4224]{1,0:T(1,128)S(1)}, f32[1,4224]{1,0:T(1,128)S(1)}, u32[]{:S(2)}, u32[]{:S(2)}) collective-permute-start(f32[1,4224]{1,0:T(1,128)S(1)} %add_add_fusion.refs_3_), channel_id=1, source_target_pairs={{0,5},{1,4},{2,7},{3,6},{4,1},{5,0},{6,3},{7,2},{8,13},{9,12},{10,... | collective-permute-start | bytes 50696 | tf_op jit(solution)/shard_map/ppermute | solution.py:316
  44.6 3.8 %collective-permute-start.15 = (f32[8,640]{1,0:T(8,128)S(1)}, f32[8,640]{1,0:T(8,128)S(1)}, u32[]{:S(2)}, u32[]{:S(2)}) collective-permute-start(f32[8,640]{1,0:T(8,128)S(1)} %get-tuple-element.40.refs_1_), channel_id=1, source_target_pairs={{0,16},{16,0},{1,17},{17,1},{2,18},{18,2},{3,19},{19,3},{4,20},{20... | collective-permute-start | bytes 61448 | tf_op jit(solution)/shard_map/ppermute | solution.py:316

commit v22 on v17

--- a/solution.py
+++ b/solution.py
@@ -74,11 +74,6 @@
     return jnp.where(lax.axis_index("dp") == 0, own, moved)
 
 
-def home_total(refs):
-    far, moved, own = (ref[...].astype(f32) for ref in refs)
-    return far + resident(moved, own)
-
-
 def row_sum(value):
     return jnp.sum(value, axis=1, keepdims=True)
 
@@ -103,10 +98,20 @@
     return high, (value - high.astype(f32)).astype(bf16)
 
 
+def pick(feat_ref, idx, hit_ref):
+    row_count, count = hit_ref.shape
+    local_idx = idx - lax.axis_index("dp") * row_count
+    row = lax.broadcasted_iota(jnp.int32, (STEP, count), 0).astype(f32).astype(bf16)
+    block = lax.div(local_idx, STEP)
+    place = (local_idx - block * STEP).astype(f32)
+    for begin in range(0, row_count, STEP):
+        own = jnp.where(block == begin // STEP, place, -1.0).astype(bf16)
+        hit = jnp.where(row == own, jnp.ones_like(row), jnp.zeros_like(row))
+        hit_ref[begin : begin + STEP, :] = hit
+
+
 def pick_body(feat_hbm, idx_hbm, slots_hbm, prices_hbm, scale_hbm, *refs):
-    feat_ref, slots_ref, prices_ref, scale_ref, out_ref, idx_ref, hit_ref, sems = refs
-    row_count = feat_ref.shape[1]
-    count = out_ref.shape[1]
+    feat_ref, idx_ref, slots_ref, prices_ref, scale_ref, out_ref, hit_ref, sems = refs
     sources = (idx_hbm, feat_hbm, slots_hbm, prices_hbm, scale_hbm)
     targets = (idx_ref, feat_ref, slots_ref, prices_ref, scale_ref)
     copies = [
@@ -116,26 +121,26 @@
     for copy in copies:
         copy.start()
     copies[0].wait()
-    local_idx = idx_ref[...] - lax.axis_index("dp") * row_count
-    row = lax.broadcasted_iota(jnp.int32, (STEP, count), 0).astype(f32).astype(bf16)
-    block = lax.div(local_idx, STEP)
-    place = (local_idx - block * STEP).astype(f32)
-
-    def hits(begin):
-        own = jnp.where(block == begin // STEP, place, -1.0).astype(bf16)
-        return jnp.where(row == own, jnp.ones_like(row), jnp.zeros_like(row))
-
-    for begin in range(0, row_count, STEP):
-        hit_ref[begin : begin + STEP, :] = hits(begin)
+    pick(feat_ref, idx_ref[...], hit_ref)
     copies[1].wait()
     picked = jnp.dot(feat_ref[...], hit_ref[...], preferred_element_type=f32)
     for copy in copies[2:]:
         copy.wait()
-    row = lax.broadcasted_iota(jnp.int32, (16, count), 0)
-    extra = jnp.zeros((16, count), f32)
+    row = lax.broadcasted_iota(jnp.int32, (16, picked.shape[1]), 0)
+    extra = jnp.zeros(row.shape, f32)
     for place, part in enumerate(split3(scale_ref[...])):
         extra = jnp.where(row == place, part, extra)
     out_ref[...] = jnp.concatenate([picked, extra], axis=0).astype(bf16)
+
+
+def pick_beside_body(feat_ref, moved_idx_ref, idx_ref, picked_ref, out_ref, hit_ref):
+    first = lax.axis_index("dp") == 0
+    pick(feat_ref, jnp.where(first, idx_ref[...], moved_idx_ref[...]), hit_ref)
+    out_ref[0:-16, :] = jnp.dot(
+        feat_ref[...], hit_ref[...], preferred_element_type=f32
+    ).astype(bf16)
+    own = picked_ref[-16:, :].astype(f32)
+    out_ref[-16:, :] = jnp.where(first, own, 0.0).astype(bf16)
 
 
 def columns_body(feat_ref, slots_ref, prices_ref, columns_ref, turned_ref, weight_ref):
@@ -154,8 +159,10 @@
 
 def rows_body(crossed, parts, turned_ref, weight_ref, *refs):
     center_refs, (block_ref, center_ref, scale_ref, out_ref) = refs[:parts], refs[parts:]
-    arrived = home_total(center_refs) if crossed else total_of(center_refs).astype(f32)
+    arrived = total_of(center_refs).astype(f32)
     rows = arrived[-16:] * (1.0 / lax.axis_size("dp"))
+    if crossed:
+        rows = jnp.where(lax.axis_index("dp") == 0, rows, arrived[-16:])
     scale_ref[...] = rows[0:1] + (rows[1:2] + rows[2:3])
     center = arrived[:-16]
     center = jnp.concatenate(
@@ -388,6 +395,7 @@
     def share(value):
         return [moved(value, across), value] if crossed else exchange(value, "dp")
 
+    moved_idx = moved(center_idx, beside) if crossed else center_idx
     inputs = [
         pltpu.with_memory_space_constraint(array, pltpu.HBM)
         for array in (
@@ -398,10 +406,11 @@
             center_scale.reshape(1, count),
         )
     ]
-    features, slots, prices, own_scale, picked = call(
+    features, idx, slots, prices, own_scale, picked = call(
         pick_body,
         (
             shaped(features.shape, bf16),
+            shaped((1, count), jnp.int32),
             shaped((1, row_count), jnp.int32),
             shaped((1, row_count)),
             shaped((1, count)),
@@ -410,13 +419,20 @@
         *inputs,
         sources=[HBM] * 5,
         scratch_shapes=[
-            pltpu.VMEM((1, count), jnp.int32),
             pltpu.VMEM((row_count, count), bf16),
             pltpu.SemaphoreType.DMA((5,)),
         ],
     )
     if crossed:
-        centers = [moved(picked, outward), moved(picked, beside), picked]
+        resident_picks = call(
+            pick_beside_body,
+            shaped((depth + 16, count), bf16),
+            features, moved_idx.reshape(1, count), idx, picked,
+            flops=128 * row_count * count,
+            bytes_accessed=128 * row_count,
+            scratch_shapes=[pltpu.VMEM((row_count, count), bf16)],
+        )
+        centers = [moved(picked, outward), resident_picks]
     else:
         centers = exchange(picked, "dp")
     columns, turned_columns, weight = call(

time: 49.1 us -> 49 us (level)
  waiting for transfers between devices: 14.4 us -> 13.5 us
  Pallas kernels: 12.7 us -> 13.5 us
    ppermute x6, waiting for transfers between devices: 4.9 us -> 3.98 us  [moved(): return lax.ppermute(value, ('dp', 'centers'), pairs_over(target_of))]
    pallas_call x9 -> x10, Pallas kernels: 12.7 us -> 13.5 us  [call(): pl.pallas_call(body, out_shape=out_shape, in_specs=sources or [VMEM] * le...]
  transfers between devices with their start and end apart: 18 -> 18, of which waited for: 12 -> 13; matrix products, arithmetic and copies ran while one was open for 0% -> 0% of each run, Pallas kernels for 5% -> 7%
where the time goes in v22:
time: 49 us; the launch traced here: 48.9 us
  starting transfers between devices  21.1 us (43%)
  Pallas kernels  13.5 us (28%)
  waiting for transfers between devices  13.5 us (28%)
  between operations  0.71 us (1%)
    pallas_call x10, Pallas kernels, call(): pl.pallas_call(body, out_shape=out_shape, in_specs=sources or [VMEM] * le...  13.5 us
    ppermute x12, starting transfers between devices, exchange(): parts.insert(0, lax.ppermute(value, axis, pairs))  12.4 us
    ppermute x12, waiting for transfers between devices, exchange(): parts.insert(0, lax.ppermute(value, axis, pairs))  9.53 us
    ppermute x6, starting transfers between devices, moved(): return lax.ppermute(value, ('dp', 'centers'), pairs_over(target_of))  8.73 us
    ppermute x6, waiting for transfers between devices, moved(): return lax.ppermute(value, ('dp', 'centers'), pairs_over(target_of))  3.98 us
  transfers between devices with their start and end apart: 18, of which 13 were waited for; matrix products, arithmetic and copies ran while one was open for 0% of the time, Pallas kernels for 7%

profile of v22, /device:TPU:0, one launch (start us, length us, event | category | flops | bytes accessed | tf_op | source)
XLA Modules:
  0.0 48.9 jit_solution(16151510310183269291)
XLA Ops:
  0.6 2.0 %shard_map.68 = (bf16[64,4096]{1,0:T(8,128)(2,1)S(1)}, s32[1,512]{1,0:T(1,128)S(1)}, s32[1,4096]{1,0:T(1,128)S(1)}, f32[1,4096]{1,0:T(1,128)S(1)}, f32[1,512]{1,0:T(1,128)S(1)}, /*index=5*/bf16[80,512]{1,0:T(8,128)(2,1)S(1)}) custom-call(bf16[64,4096]{1,0:T(8,128)(2,1)} %feat_hbm.1, s32[1,512]{1,0:T(1,128)} %bitcast.9, s32[1,4096]{1,0:T(1,128)} %bitcast.6, ...), custom_call_target="tpu_custom_call" | custom-call | tf_op jit(solution)/shard_map/pallas_call | solution.py:319
  2.6 2.4 %collective-permute-start = (bf16[80,512]{1,0:T(8,128)(2,1)S(1)}, bf16[80,512]{1,0:T(8,128)(2,1)S(1)}, u32[]{:S(2)}, u32[]{:S(2)}) collective-permute-start(bf16[80,512]{1,0:T(8,128)(2,1)S(1)} %get-tuple-element.31.picked_ref), channel_id=1, source_target_pairs={{0,17},{1,16},{2,19},{3,18},{4,21},{5,20},{6,23},{7,22},{8,25},{9,... | collective-permute-start | bytes 245768 | tf_op jit(solution)/shard_map/ppermute | solution.py:360
  5.0 0.7 %collective-permute-start.1 = (s32[512]{0:T(512)}, s32[512]{0:T(512)S(1)}, u32[]{:S(2)}, u32[]{:S(2)}) collective-permute-start(s32[512]{0:T(512)} %param.8), channel_id=1, source_target_pairs={{0,1},{1,0},{2,3},{3,2},{4,5},{5,4},{6,7},{7,6},{8,9},{9,8},{10,11... | collective-permute-start | bytes 6152 | tf_op jit(solution)/shard_map/ppermute | solution.py:360
  5.7 0.7 %shard_map.69 = (bf16[256,4096]{1,0:T(8,128)(2,1)S(1)}, bf16[4096,256]{1,0:T(8,128)(2,1)S(1)}, bf16[16,4096]{1,0:T(8,128)(2,1)S(1)}) custom-call(bf16[64,4096]{1,0:T(8,128)(2,1)S(1)} %get-tuple-element.26.feat_ref, s32[1,4096]{1,0:T(1,128)S(1)} %get-tuple-element.27.slots_ref.refs_3_.refs_4_, f32[1,4096]{1,0:T(1,128)S(1)} %get-tuple-element.28.prices_ref), custom_call_target="tpu_custom_call" | custom-call | flops 4096000 | bytes 4194304 | tf_op jit(solution)/shard_map/pallas_call | solution.py:319
  6.4 0.4 collective-permute-done.1
  6.7 0.9 %shard_map.70.refs_1_ = bf16[80,512]{1,0:T(8,128)(2,1)S(1)} custom-call(bf16[64,4096]{1,0:T(8,128)(2,1)S(1)} %get-tuple-element.26.feat_ref, s32[1,512]{1,0:T(1,128)S(1)} %bitcast.5, s32[1,512]{1,0:T(1,128)S(1)} %get-tuple-element.32.idx_ref, bf16[80,512]{1,0:T(8,128)(2,1)S(1)} %get-tuple-element.31.picked_ref), custom_call_target="tpu_custom_call" | custom-call | flops 268435456 | bytes 524288 | tf_op jit(solution)/shard_map/pallas_call | solution.py:319
  7.6 0.4 collective-permute-done.refs_0_
  8.0 2.5 %shard_map.71 = (bf16[8192,512]{1,0:T(8,128)(2,1)S(1)}, bf16[256,512]{1,0:T(8,128)(2,1)S(1)}, f32[1,512]{1,0:T(1,128)S(1)}, f32[8,512]{1,0:T(8,128)S(1)}) custom-call(bf16[4096,256]{1,0:T(8,128)(2,1)S(1)} %get-tuple-element.29.turned_ref, bf16[16,4096]{1,0:T(8,128)(2,1)S(1)} %get-tuple-element.30.weight_ref, ...), custom_call_target="tpu_custom_call" | custom-call | flops 134217728 | bytes 8388608 | tf_op jit(solution)/shard_map/pallas_call | solution.py:319
  10.6 2.1 %collective-permute-start.2 = (f32[8,512]{1,0:T(8,128)S(1)}, f32[8,512]{1,0:T(8,128)S(1)}, u32[]{:S(2)}, u32[]{:S(2)}) collective-permute-start(f32[8,512]{1,0:T(8,128)S(1)} %get-tuple-element.33.refs_1_), channel_id=1, source_target_pairs={{0,17},{1,16},{2,19},{3,18},{4,21},{5,20},{6,23},{7,22},{8,25},{9,... | collective-permute-start | bytes 49160 | tf_op jit(solution)/shard_map/ppermute | solution.py:360
  12.6 1.9 %shard_map.72.refs_4_ = bf16[1024,4096]{1,0:T(8,128)(2,1)S(1)} custom-call(bf16[256,4096]{1,0:T(8,128)(2,1)S(1)} %get-tuple-element.35.columns_ref, bf16[256,512]{1,0:T(8,128)(2,1)S(1)} %get-tuple-element.36.center_ref), custom_call_target="tpu_custom_call" | custom-call | flops 134217728 | bytes 8388608 | tf_op jit(solution)/shard_map/pallas_call | solution.py:319
  14.6 0.0 collective-permute-done.2.refs_0_
  14.6 1.2 %shard_map.73 = (f32[8,512]{1,0:T(8,128)S(1)}, f32[1,4224]{1,0:T(1,128)S(1)}) custom-call(f32[8,512]{1,0:T(8,128)S(1)} %collective-permute-done.2.refs_0_, f32[8,512]{1,0:T(8,128)S(1)} %get-tuple-element.33.refs_1_, f32[1,512]{1,0:T(1,128)S(1)} %get-tuple-element.34.refs_2_, s32[1,4096]{1,0:T(1,128)S(1)} %get-tuple-element.27.slots_ref.refs_3_.refs_4_, ...), custom_call_target="tpu_custom_call" | custom-call | tf_op jit(solution)/shard_map/pallas_call | solution.py:319
  15.8 1.6 %collective-permute-start.3 = (f32[1,4224]{1,0:T(1,128)S(1)}, f32[1,4224]{1,0:T(1,128)S(1)}, u32[]{:S(2)}, u32[]{:S(2)}) collective-permute-start(f32[1,4224]{1,0:T(1,128)S(1)} %get-tuple-element.37), channel_id=1, source_target_pairs={{0,2},{1,3},{2,0},{3,1},{4,6},{5,7},{6,4},{7,5},{8,10},{9,11},{10,... | collective-permute-start | bytes 50696 | tf_op jit(solution)/shard_map/ppermute | solution.py:344
  17.4 0.2 collective-permute-start.4
  17.6 0.4 collective-permute-start.5
  18.0 1.6 %collective-permute-done.3 = f32[1,4224]{1,0:T(1,128)S(1)} collective-permute-done((f32[1,4224]{1,0:T(1,128)S(1)}, f32[1,4224]{1,0:T(1,128)S(1)}, u32[]{:S(2)}, u32[]{:S(2)}) %collective-permute-start.3) | collective-permute-done | bytes 16928 | tf_op jit(solution)/shard_map/ppermute | solution.py:344
  19.6 0.9 %collective-permute-done.4 = f32[1,4224]{1,0:T(1,128)S(1)} collective-permute-done((f32[1,4224]{1,0:T(1,128)S(1)}, f32[1,4224]{1,0:T(1,128)S(1)}, u32[]{:S(2)}, u32[]{:S(2)}) %collective-permute-start.4) | collective-permute-done | bytes 16928 | tf_op jit(solution)/shard_map/ppermute | solution.py:344
  20.6 0.0 collective-permute-done.5
  20.6 3.4 %collective-permute-start.6 = (f32[1,4224]{1,0:T(1,128)S(1)}, f32[1,4224]{1,0:T(1,128)S(1)}, u32[]{:S(2)}, u32[]{:S(2)}) collective-permute-start(f32[1,4224]{1,0:T(1,128)S(1)} %add_add_fusion.1.refs_3_), channel_id=1, source_target_pairs={{0,13},{1,12},{2,15},{3,14},{4,9},{5,8},{6,11},{7,10},{8,5},{9,4},... | collective-permute-start | bytes 50696 | tf_op jit(solution)/shard_map/ppermute | solution.py:344
  24.0 0.0 collective-permute-start.7
  24.0 0.6 %collective-permute-start.8 = (f32[1,4224]{1,0:T(1,128)S(1)}, f32[1,4224]{1,0:T(1,128)S(1)}, u32[]{:S(2)}, u32[]{:S(2)}) collective-permute-start(f32[1,4224]{1,0:T(1,128)S(1)} %add_add_fusion.1.refs_3_), channel_id=1, source_target_pairs={{0,5},{1,4},{2,7},{3,6},{4,1},{5,0},{6,3},{7,2},{8,13},{9,12},{10,... | collective-permute-start | bytes 50696 | tf_op jit(solution)/shard_map/ppermute | solution.py:344
  24.7 1.0 %collective-permute-done.6.refs_0_ = f32[1,4224]{1,0:T(1,128)S(1)} collective-permute-done((f32[1,4224]{1,0:T(1,128)S(1)}, f32[1,4224]{1,0:T(1,128)S(1)}, u32[]{:S(2)}, u32[]{:S(2)}) %collective-permute-start.6) | collective-permute-done | bytes 16928 | tf_op jit(solution)/shard_map/ppermute | solution.py:344
  25.6 2.4 %collective-permute-done.7.refs_1_ = f32[1,4224]{1,0:T(1,128)S(1)} collective-permute-done((f32[1,4224]{1,0:T(1,128)S(1)}, f32[1,4224]{1,0:T(1,128)S(1)}, u32[]{:S(2)}, u32[]{:S(2)}) %collective-permute-start.7) | collective-permute-done | bytes 16928 | tf_op jit(solution)/shard_map/ppermute | solution.py:344
  28.1 0.0 collective-permute-done.8.refs_2_
  28.1 1.2 %shard_map.74 = (f32[1,4224]{1,0:T(1,128)S(1)}, f32[8,128]{1,0:T(8,128)S(1)}, f32[8,640]{1,0:T(8,128)S(1)}) custom-call(f32[1,4224]{1,0:T(1,128)S(1)} %collective-permute-done.6.refs_0_, f32[1,4224]{1,0:T(1,128)S(1)} %collective-permute-done.7.refs_1_, f32[1,4224]{1,0:T(1,128)S(1)} %collective-permute-done.8.refs_2_, f32[1,4224]{1,0:T(1,128)S(1)} %add_add_fusion.1.refs_3_, ...), custom_call_target="tpu_custom_call" | custom-call | tf_op jit(solution)/shard_map/pallas_call | solution.py:319
  29.3 1.7 %collective-permute-start.9 = (f32[8,640]{1,0:T(8,128)S(1)}, f32[8,640]{1,0:T(8,128)S(1)}, u32[]{:S(2)}, u32[]{:S(2)}) collective-permute-start(f32[8,640]{1,0:T(8,128)S(1)} %get-tuple-element.39.refs_1_), channel_id=1, source_target_pairs={{0,17},{1,16},{2,19},{3,18},{4,21},{5,20},{6,23},{7,22},{8,25},{9,... | collective-permute-start | bytes 61448 | tf_op jit(solution)/shard_map/ppermute | solution.py:360
  31.0 1.5 %collective-permute-done.9.refs_0_ = f32[8,640]{1,0:T(8,128)S(1)} collective-permute-done((f32[8,640]{1,0:T(8,128)S(1)}, f32[8,640]{1,0:T(8,128)S(1)}, u32[]{:S(2)}, u32[]{:S(2)}) %collective-permute-start.9) | collective-permute-done | bytes 20512 | tf_op jit(solution)/shard_map/ppermute | solution.py:360
  32.5 1.2 %shard_map.75 = (f32[16,512]{1,0:T(8,128)S(1)}, f32[8,128]{1,0:T(8,128)S(1)}, f32[1,4224]{1,0:T(1,128)S(1)}) custom-call(f32[8,640]{1,0:T(8,128)S(1)} %collective-permute-done.9.refs_0_, f32[8,640]{1,0:T(8,128)S(1)} %get-tuple-element.39.refs_1_, f32[1,512]{1,0:T(1,128)S(1)} %get-tuple-element.34.refs_2_, ...), custom_call_target="tpu_custom_call" | custom-call | tf_op jit(solution)/shard_map/pallas_call | solution.py:319
  33.7 0.7 %collective-permute-start.10 = (f32[1,4224]{1,0:T(1,128)S(1)}, f32[1,4224]{1,0:T(1,128)S(1)}, u32[]{:S(2)}, u32[]{:S(2)}) collective-permute-start(f32[1,4224]{1,0:T(1,128)S(1)} %get-tuple-element.42), channel_id=1, source_target_pairs={{0,2},{1,3},{2,0},{3,1},{4,6},{5,7},{6,4},{7,5},{8,10},{9,11},{10,... | collective-permute-start | bytes 50696 | tf_op jit(solution)/shard_map/ppermute | solution.py:344
  34.4 1.1 %collective-permute-start.11 = (f32[1,4224]{1,0:T(1,128)S(1)}, f32[1,4224]{1,0:T(1,128)S(1)}, u32[]{:S(2)}, u32[]{:S(2)}) collective-permute-start(f32[1,4224]{1,0:T(1,128)S(1)} %get-tuple-element.42), channel_id=1, source_target_pairs={{0,3},{1,2},{2,1},{3,0},{4,7},{5,6},{6,5},{7,4},{8,11},{9,10},{10,... | collective-permute-start | bytes 50696 | tf_op jit(solution)/shard_map/ppermute | solution.py:344
  35.6 0.3 collective-permute-start.12
  35.9 1.7 %collective-permute-done.10 = f32[1,4224]{1,0:T(1,128)S(1)} collective-permute-done((f32[1,4224]{1,0:T(1,128)S(1)}, f32[1,4224]{1,0:T(1,128)S(1)}, u32[]{:S(2)}, u32[]{:S(2)}) %collective-permute-start.10) | collective-permute-done | bytes 16928 | tf_op jit(solution)/shard_map/ppermute | solution.py:344
  37.6 0.1 collective-permute-done.11
  37.7 0.0 collective-permute-done.12
  37.7 1.4 %collective-permute-start.13 = (f32[1,4224]{1,0:T(1,128)S(1)}, f32[1,4224]{1,0:T(1,128)S(1)}, u32[]{:S(2)}, u32[]{:S(2)}) collective-permute-start(f32[1,4224]{1,0:T(1,128)S(1)} %add_add_fusion.refs_3_), channel_id=1, source_target_pairs={{0,13},{1,12},{2,15},{3,14},{4,9},{5,8},{6,11},{7,10},{8,5},{9,4},... | collective-permute-start | bytes 50696 | tf_op jit(solution)/shard_map/ppermute | solution.py:344
  39.2 0.6 %collective-permute-start.14 = (f32[1,4224]{1,0:T(1,128)S(1)}, f32[1,4224]{1,0:T(1,128)S(1)}, u32[]{:S(2)}, u32[]{:S(2)}) collective-permute-start(f32[1,4224]{1,0:T(1,128)S(1)} %add_add_fusion.refs_3_), channel_id=1, source_target_pairs={{0,9},{1,8},{2,11},{3,10},{4,13},{5,12},{6,15},{7,14},{8,1},{9,0},... | collective-permute-start | bytes 50696 | tf_op jit(solution)/shard_map/ppermute | solution.py:344
  39.8 1.9 %collective-permute-start.15 = (f32[1,4224]{1,0:T(1,128)S(1)}, f32[1,4224]{1,0:T(1,128)S(1)}, u32[]{:S(2)}, u32[]{:S(2)}) collective-permute-start(f32[1,4224]{1,0:T(1,128)S(1)} %add_add_fusion.refs_3_), channel_id=1, source_target_pairs={{0,5},{1,4},{2,7},{3,6},{4,1},{5,0},{6,3},{7,2},{8,13},{9,12},{10,... | collective-permute-start | bytes 50696 | tf_op jit(solution)/shard_map/ppermute | solution.py:344
  41.6 1.1 %collective-permute-done.13.refs_0_ = f32[1,4224]{1,0:T(1,128)S(1)} collective-permute-done((f32[1,4224]{1,0:T(1,128)S(1)}, f32[1,4224]{1,0:T(1,128)S(1)}, u32[]{:S(2)}, u32[]{:S(2)}) %collective-permute-start.13) | collective-permute-done | bytes 16928 | tf_op jit(solution)/shard_map/ppermute | solution.py:344
  42.8 0.6 %collective-permute-done.14.refs_1_ = f32[1,4224]{1,0:T(1,128)S(1)} collective-permute-done((f32[1,4224]{1,0:T(1,128)S(1)}, f32[1,4224]{1,0:T(1,128)S(1)}, u32[]{:S(2)}, u32[]{:S(2)}) %collective-permute-start.14) | collective-permute-done | bytes 16928 | tf_op jit(solution)/shard_map/ppermute | solution.py:344
  43.4 0.1 collective-permute-done.15.refs_2_
  43.4 1.3 %shard_map.76 = (f32[8,256]{1,0:T(8,128)S(1)}, f32[8,640]{1,0:T(8,128)S(1)}, f32[24,640]{1,0:T(8,128)S(1)}) custom-call(f32[1,4224]{1,0:T(1,128)S(1)} %collective-permute-done.13.refs_0_, f32[1,4224]{1,0:T(1,128)S(1)} %collective-permute-done.14.refs_1_, f32[1,4224]{1,0:T(1,128)S(1)} %collective-permute-done.15.refs_2_, f32[1,4224]{1,0:T(1,128)S(1)} %add_add_fusion.refs_3_, ...), custom_call_target="tpu_custom_call" | custom-call | tf_op jit(solution)/shard_map/pallas_call | solution.py:319
  44.7 0.3 collective-permute-start.17
  45.0 1.5 %collective-permute-start.16 = (f32[8,640]{1,0:T(8,128)S(1)}, f32[8,640]{1,0:T(8,128)S(1)}, u32[]{:S(2)}, u32[]{:S(2)}) collective-permute-start(f32[8,640]{1,0:T(8,128)S(1)} %get-tuple-element.45), channel_id=1, source_target_pairs={{0,16},{1,17},{2,18},{3,19},{4,20},{5,21},{6,22},{7,23},{8,24},{9,... | collective-permute-start | bytes 61448 | tf_op jit(solution)/shard_map/ppermute | solution.py:360
  46.5 1.7 %collective-permute-done.16.refs_0_ = f32[8,640]{1,0:T(8,128)S(1)} collective-permute-done((f32[8,640]{1,0:T(8,128)S(1)}, f32[8,640]{1,0:T(8,128)S(1)}, u32[]{:S(2)}, u32[]{:S(2)}) %collective-permute-start.16) | collective-permute-done | bytes 20512 | tf_op jit(solution)/shard_map/ppermute | solution.py:360
  48.2 0.0 collective-permute-done.17.refs_1_
  48.2 0.6 %shard_map.77 = (f32[8,512]{1,0:T(8,128)}, f32[8,512]{1,0:T(8,128)}) custom-call(f32[8,640]{1,0:T(8,128)S(1)} %collective-permute-done.16.refs_0_, f32[24,640]{1,0:T(8,128)S(1)} %collective-permute-done.17.refs_1_, f32[24,640]{1,0:T(8,128)S(1)} %get-tuple-element.46.refs_2_, f32[1,512]{1,0:T(1,128)S(1)} %get-tuple-element.47.refs_3_, ...), custom_call_target="tpu_custom_call" | custom-call | tf_op jit(solution)/shard_map/pallas_call | solution.py:319
  (2 shorter events, 0.1 us)
Async XLA Ops:
  2.6 5.4 %collective-permute-start = (bf16[80,512]{1,0:T(8,128)(2,1)S(1)}, bf16[80,512]{1,0:T(8,128)(2,1)S(1)}, u32[]{:S(2)}, u32[]{:S(2)}) collective-permute-start(bf16[80,512]{1,0:T(8,128)(2,1)S(1)} %get-tuple-element.31.picked_ref), channel_id=1, source_target_pairs={{0,17},{1,16},{2,19},{3,18},{4,21},{5,20},{6,23},{7,22},{8,25},{9,... | collective-permute-start | bytes 245768 | tf_op jit(solution)/shard_map/ppermute | solution.py:360
  5.0 1.7 %collective-permute-start.1 = (s32[512]{0:T(512)}, s32[512]{0:T(512)S(1)}, u32[]{:S(2)}, u32[]{:S(2)}) collective-permute-start(s32[512]{0:T(512)} %param.8), channel_id=1, source_target_pairs={{0,1},{1,0},{2,3},{3,2},{4,5},{5,4},{6,7},{7,6},{8,9},{9,8},{10,11... | collective-permute-start | bytes 6152 | tf_op jit(solution)/shard_map/ppermute | solution.py:360
  10.6 4.0 %collective-permute-start.2 = (f32[8,512]{1,0:T(8,128)S(1)}, f32[8,512]{1,0:T(8,128)S(1)}, u32[]{:S(2)}, u32[]{:S(2)}) collective-permute-start(f32[8,512]{1,0:T(8,128)S(1)} %get-tuple-element.33.refs_1_), channel_id=1, source_target_pairs={{0,17},{1,16},{2,19},{3,18},{4,21},{5,20},{6,23},{7,22},{8,25},{9,... | collective-permute-start | bytes 49160 | tf_op jit(solution)/shard_map/ppermute | solution.py:360
  15.8 3.8 %collective-permute-start.3 = (f32[1,4224]{1,0:T(1,128)S(1)}, f32[1,4224]{1,0:T(1,128)S(1)}, u32[]{:S(2)}, u32[]{:S(2)}) collective-permute-start(f32[1,4224]{1,0:T(1,128)S(1)} %get-tuple-element.37), channel_id=1, source_target_pairs={{0,2},{1,3},{2,0},{3,1},{4,6},{5,7},{6,4},{7,5},{8,10},{9,11},{10,... | collective-permute-start | bytes 50696 | tf_op jit(solution)/shard_map/ppermute | solution.py:344
  17.4 3.2 %collective-permute-start.4 = (f32[1,4224]{1,0:T(1,128)S(1)}, f32[1,4224]{1,0:T(1,128)S(1)}, u32[]{:S(2)}, u32[]{:S(2)}) collective-permute-start(f32[1,4224]{1,0:T(1,128)S(1)} %get-tuple-element.37), channel_id=1, source_target_pairs={{0,3},{1,2},{2,1},{3,0},{4,7},{5,6},{6,5},{7,4},{8,11},{9,10},{10,... | collective-permute-start | bytes 50696 | tf_op jit(solution)/shard_map/ppermute | solution.py:344
  17.6 3.0 %collective-permute-start.5 = (f32[1,4224]{1,0:T(1,128)S(1)}, f32[1,4224]{1,0:T(1,128)S(1)}, u32[]{:S(2)}, u32[]{:S(2)}) collective-permute-start(f32[1,4224]{1,0:T(1,128)S(1)} %get-tuple-element.37), channel_id=1, source_target_pairs={{0,1},{1,0},{2,3},{3,2},{4,5},{5,4},{6,7},{7,6},{8,9},{9,8},{10,11... | collective-permute-start | bytes 50696 | tf_op jit(solution)/shard_map/ppermute | solution.py:344
  20.6 5.0 %collective-permute-start.6 = (f32[1,4224]{1,0:T(1,128)S(1)}, f32[1,4224]{1,0:T(1,128)S(1)}, u32[]{:S(2)}, u32[]{:S(2)}) collective-permute-start(f32[1,4224]{1,0:T(1,128)S(1)} %add_add_fusion.1.refs_3_), channel_id=1, source_target_pairs={{0,13},{1,12},{2,15},{3,14},{4,9},{5,8},{6,11},{7,10},{8,5},{9,4},... | collective-permute-start | bytes 50696 | tf_op jit(solution)/shard_map/ppermute | solution.py:344
  24.0 4.1 %collective-permute-start.7 = (f32[1,4224]{1,0:T(1,128)S(1)}, f32[1,4224]{1,0:T(1,128)S(1)}, u32[]{:S(2)}, u32[]{:S(2)}) collective-permute-start(f32[1,4224]{1,0:T(1,128)S(1)} %add_add_fusion.1.refs_3_), channel_id=1, source_target_pairs={{0,9},{1,8},{2,11},{3,10},{4,13},{5,12},{6,15},{7,14},{8,1},{9,0},... | collective-permute-start | bytes 50696 | tf_op jit(solution)/shard_map/ppermute | solution.py:344
  24.0 4.1 %collective-permute-start.8 = (f32[1,4224]{1,0:T(1,128)S(1)}, f32[1,4224]{1,0:T(1,128)S(1)}, u32[]{:S(2)}, u32[]{:S(2)}) collective-permute-start(f32[1,4224]{1,0:T(1,128)S(1)} %add_add_fusion.1.refs_3_), channel_id=1, source_target_pairs={{0,5},{1,4},{2,7},{3,6},{4,1},{5,0},{6,3},{7,2},{8,13},{9,12},{10,... | collective-permute-start | bytes 50696 | tf_op jit(solution)/shard_map/ppermute | solution.py:344
  29.3 3.2 %collective-permute-start.9 = (f32[8,640]{1,0:T(8,128)S(1)}, f32[8,640]{1,0:T(8,128)S(1)}, u32[]{:S(2)}, u32[]{:S(2)}) collective-permute-start(f32[8,640]{1,0:T(8,128)S(1)} %get-tuple-element.39.refs_1_), channel_id=1, source_target_pairs={{0,17},{1,16},{2,19},{3,18},{4,21},{5,20},{6,23},{7,22},{8,25},{9,... | collective-permute-start | bytes 61448 | tf_op jit(solution)/shard_map/ppermute | solution.py:360
  33.7 3.9 %collective-permute-start.10 = (f32[1,4224]{1,0:T(1,128)S(1)}, f32[1,4224]{1,0:T(1,128)S(1)}, u32[]{:S(2)}, u32[]{:S(2)}) collective-permute-start(f32[1,4224]{1,0:T(1,128)S(1)} %get-tuple-element.42), channel_id=1, source_target_pairs={{0,2},{1,3},{2,0},{3,1},{4,6},{5,7},{6,4},{7,5},{8,10},{9,11},{10,... | collective-permute-start | bytes 50696 | tf_op jit(solution)/shard_map/ppermute | solution.py:344
  34.4 3.3 %collective-permute-start.11 = (f32[1,4224]{1,0:T(1,128)S(1)}, f32[1,4224]{1,0:T(1,128)S(1)}, u32[]{:S(2)}, u32[]{:S(2)}) collective-permute-start(f32[1,4224]{1,0:T(1,128)S(1)} %get-tuple-element.42), channel_id=1, source_target_pairs={{0,3},{1,2},{2,1},{3,0},{4,7},{5,6},{6,5},{7,4},{8,11},{9,10},{10,... | collective-permute-start | bytes 50696 | tf_op jit(solution)/shard_map/ppermute | solution.py:344
  35.6 2.1 %collective-permute-start.12 = (f32[1,4224]{1,0:T(1,128)S(1)}, f32[1,4224]{1,0:T(1,128)S(1)}, u32[]{:S(2)}, u32[]{:S(2)}) collective-permute-start(f32[1,4224]{1,0:T(1,128)S(1)} %get-tuple-element.42), channel_id=1, source_target_pairs={{0,1},{1,0},{2,3},{3,2},{4,5},{5,4},{6,7},{7,6},{8,9},{9,8},{10,11... | collective-permute-start | bytes 50696 | tf_op jit(solution)/shard_map/ppermute | solution.py:344
  37.7 5.0 %collective-permute-start.13 = (f32[1,4224]{1,0:T(1,128)S(1)}, f32[1,4224]{1,0:T(1,128)S(1)}, u32[]{:S(2)}, u32[]{:S(2)}) collective-permute-start(f32[1,4224]{1,0:T(1,128)S(1)} %add_add_fusion.refs_3_), channel_id=1, source_target_pairs={{0,13},{1,12},{2,15},{3,14},{4,9},{5,8},{6,11},{7,10},{8,5},{9,4},... | collective-permute-start | bytes 50696 | tf_op jit(solution)/shard_map/ppermute | solution.py:344
  39.2 4.2 %collective-permute-start.14 = (f32[1,4224]{1,0:T(1,128)S(1)}, f32[1,4224]{1,0:T(1,128)S(1)}, u32[]{:S(2)}, u32[]{:S(2)}) collective-permute-start(f32[1,4224]{1,0:T(1,128)S(1)} %add_add_fusion.refs_3_), channel_id=1, source_target_pairs={{0,9},{1,8},{2,11},{3,10},{4,13},{5,12},{6,15},{7,14},{8,1},{9,0},... | collective-permute-start | bytes 50696 | tf_op jit(solution)/shard_map/ppermute | solution.py:344
  39.8 3.7 %collective-permute-start.15 = (f32[1,4224]{1,0:T(1,128)S(1)}, f32[1,4224]{1,0:T(1,128)S(1)}, u32[]{:S(2)}, u32[]{:S(2)}) collective-permute-start(f32[1,4224]{1,0:T(1,128)S(1)} %add_add_fusion.refs_3_), channel_id=1, source_target_pairs={{0,5},{1,4},{2,7},{3,6},{4,1},{5,0},{6,3},{7,2},{8,13},{9,12},{10,... | collective-permute-start | bytes 50696 | tf_op jit(solution)/shard_map/ppermute | solution.py:344
  44.7 3.5 %collective-permute-start.17 = (f32[24,640]{1,0:T(8,128)S(1)}, f32[24,640]{1,0:T(8,128)S(1)}, u32[]{:S(2)}, u32[]{:S(2)}) collective-permute-start(f32[24,640]{1,0:T(8,128)S(1)} %get-tuple-element.46.refs_2_), channel_id=1, source_target_pairs={{0,1},{1,0},{2,3},{3,2},{4,5},{5,4},{6,7},{7,6},{8,9},{9,8},{10,11... | collective-permute-start | bytes 184328 | tf_op jit(solution)/shard_map/ppermute | solution.py:360
  45.0 3.2 %collective-permute-start.16 = (f32[8,640]{1,0:T(8,128)S(1)}, f32[8,640]{1,0:T(8,128)S(1)}, u32[]{:S(2)}, u32[]{:S(2)}) collective-permute-start(f32[8,640]{1,0:T(8,128)S(1)} %get-tuple-element.45), channel_id=1, source_target_pairs={{0,16},{1,17},{2,18},{3,19},{4,20},{5,21},{6,22},{7,23},{8,24},{9,... | collective-permute-start | bytes 61448 | tf_op jit(solution)/shard_map/ppermute | solution.py:360

commit v23 on v22

--- a/solution.py
+++ b/solution.py
@@ -126,21 +126,15 @@
     picked = jnp.dot(feat_ref[...], hit_ref[...], preferred_element_type=f32)
     for copy in copies[2:]:
         copy.wait()
-    row = lax.broadcasted_iota(jnp.int32, (16, picked.shape[1]), 0)
-    extra = jnp.zeros(row.shape, f32)
-    for place, part in enumerate(split3(scale_ref[...])):
-        extra = jnp.where(row == place, part, extra)
-    out_ref[...] = jnp.concatenate([picked, extra], axis=0).astype(bf16)
-
-
-def pick_beside_body(feat_ref, moved_idx_ref, idx_ref, picked_ref, out_ref, hit_ref):
+    out_ref[...] = picked.astype(bf16)
+
+
+def pick_beside_body(feat_ref, moved_idx_ref, idx_ref, out_ref, hit_ref):
     first = lax.axis_index("dp") == 0
     pick(feat_ref, jnp.where(first, idx_ref[...], moved_idx_ref[...]), hit_ref)
-    out_ref[0:-16, :] = jnp.dot(
+    out_ref[...] = jnp.dot(
         feat_ref[...], hit_ref[...], preferred_element_type=f32
     ).astype(bf16)
-    own = picked_ref[-16:, :].astype(f32)
-    out_ref[-16:, :] = jnp.where(first, own, 0.0).astype(bf16)
 
 
 def columns_body(feat_ref, slots_ref, prices_ref, columns_ref, turned_ref, weight_ref):
@@ -157,14 +151,10 @@
         weight_ref[:, here] = stack2(weight)
 
 
-def rows_body(crossed, parts, turned_ref, weight_ref, *refs):
+def rows_body(parts, turned_ref, weight_ref, moved_scale_ref, own_scale_ref, *refs):
     center_refs, (block_ref, center_ref, scale_ref, out_ref) = refs[:parts], refs[parts:]
-    arrived = total_of(center_refs).astype(f32)
-    rows = arrived[-16:] * (1.0 / lax.axis_size("dp"))
-    if crossed:
-        rows = jnp.where(lax.axis_index("dp") == 0, rows, arrived[-16:])
-    scale_ref[...] = rows[0:1] + (rows[1:2] + rows[2:3])
-    center = arrived[:-16]
+    scale_ref[...] = resident(moved_scale_ref[...], own_scale_ref[...])
+    center = total_of(center_refs).astype(f32)
     center = jnp.concatenate(
         [*split3(center * FACTOR), norm_rows(center, 0)], axis=0
     ).astype(bf16)
@@ -277,10 +267,8 @@
 
 def second_fold_body(parts, *refs):
     row_refs = refs[:parts]
-    slots_ref, block_ref, rows_ref, norm_ref, state_ref, sums_ref, out_ref, bundle_ref = refs[parts:]
+    slots_ref, block_ref, rows_ref, norm_ref, sums_ref, out_ref = refs[parts:]
     row_count = slots_ref.shape[1]
-    bundle_ref[SLOTS:, 0 : state_ref.shape[1]] = state_ref[...]
-    bundle_ref[SLOTS:, state_ref.shape[1] :] = jnp.zeros((2 * SLOTS, EXTRA), f32)
     latest = total_of(row_refs)
     norm = spread(from_lanes(latest[:, row_count:], 0))
     ratio = norm / norm_ref[...]
@@ -288,22 +276,21 @@
     sums_ref[:, EXTRA:] = spread(from_lanes(latest[:, row_count:], SLOTS))
     rows = latest[:, 0:row_count] + wide(ratio, row_count) * rows_ref[:, 0:row_count]
     fold_rows(rows, block_ref, slots_ref, out_ref)
-    bundle_ref[0:SLOTS, :] = out_ref[...]
 
 
 def finish_body(crossed, parts, inv_rows, *refs):
     fold_refs = refs[:parts]
-    (scale_ref, step_ref, norm_ref, sums_ref,
+    (moved_ref, state_ref, scale_ref, step_ref, norm_ref, sums_ref,
      coefficients_ref, out_ref) = refs[parts:]
     count = scale_ref.shape[1]
-    bundle = fold_refs[-1][...]
     if crossed:
-        far_ref, moved_ref = fold_refs[:-1]
-        bundle = resident(moved_ref[...], bundle)
-        folded = far_ref[...] + bundle[0:SLOTS]
+        far, moved, own = (ref[...] for ref in fold_refs)
+        folded = far + resident(moved, own)
+        state = resident(moved_ref[...], state_ref[...])
     else:
-        folded = total_of(fold_refs[:-1])
-    target, residual = bundle[SLOTS : 2 * SLOTS, 0:count], bundle[2 * SLOTS :, 0:count]
+        folded = total_of(fold_refs)
+        state = state_ref[...]
+    target, residual = state[0:SLOTS], state[SLOTS:]
     first_norm = norm_ref[...]
     norm, cross = sums_ref[:, 0:EXTRA], sums_ref[:, EXTRA:]
     ratio = norm / first_norm
@@ -395,7 +382,6 @@
     def share(value):
         return [moved(value, across), value] if crossed else exchange(value, "dp")
 
-    moved_idx = moved(center_idx, beside) if crossed else center_idx
     inputs = [
         pltpu.with_memory_space_constraint(array, pltpu.HBM)
         for array in (
@@ -414,7 +400,7 @@
             shaped((1, row_count), jnp.int32),
             shaped((1, row_count)),
             shaped((1, count)),
-            shaped((depth + 16, count), bf16),
+            shaped((depth, count), bf16),
         ),
         *inputs,
         sources=[HBM] * 5,
@@ -424,17 +410,20 @@
         ],
     )
     if crossed:
+        moved_idx = moved(center_idx, beside)
         resident_picks = call(
             pick_beside_body,
-            shaped((depth + 16, count), bf16),
-            features, moved_idx.reshape(1, count), idx, picked,
+            shaped((depth, count), bf16),
+            features, moved_idx.reshape(1, count), idx,
             flops=128 * row_count * count,
             bytes_accessed=128 * row_count,
             scratch_shapes=[pltpu.VMEM((row_count, count), bf16)],
         )
         centers = [moved(picked, outward), resident_picks]
+        moved_scale = moved(center_scale, beside).reshape(1, count)
     else:
         centers = exchange(picked, "dp")
+        moved_scale = own_scale
     columns, turned_columns, weight = call(
         columns_body,
         (
@@ -447,14 +436,14 @@
         bytes_accessed=1024 * row_count,
     )
     block, center, scale, first = call(
-        partial(rows_body, crossed, len(centers)),
+        partial(rows_body, len(centers)),
         (
             shaped((2 * row_count, count), bf16),
             shaped((DEPTH, count), bf16),
             shaped((1, count)),
             vector,
         ),
-        turned_columns, weight, *centers,
+        turned_columns, weight, moved_scale, own_scale, *centers,
         **pass_cost,
     )
     firsts = share(first)
@@ -477,23 +466,21 @@
         *folds, scale, slots, turned, target, norm,
     )
     latest = exchange(latest, "centers")
-    sums, folded, bundle = call(
+    sums, folded = call(
         partial(second_fold_body, len(latest)),
-        (
-            shaped((SLOTS, 2 * EXTRA)),
-            fold_shape,
-            shaped((3 * SLOTS, count + EXTRA)),
-        ),
-        *latest, slots, block, rows, norm, state,
+        (shaped((SLOTS, 2 * EXTRA)), fold_shape),
+        *latest, slots, block, rows, norm,
     )
     if crossed:
-        folds = [moved(folded, homeward), moved(bundle, beside), bundle]
+        folds = [moved(folded, homeward), moved(folded, beside), folded]
+        moved_state = moved(state, beside)
     else:
-        folds = exchange(folded, "dp") + [bundle]
+        folds = exchange(folded, "dp")
+        moved_state = state
     return call(
         partial(finish_body, crossed, len(folds), 1.0 / all_rows),
         (vector, vector),
-        *folds, own_scale, step, norm, sums,
+        *folds, moved_state, state, own_scale, step, norm, sums,
     )
 
 

time: 49 us -> 48.4 us (0.988)
  waiting for transfers between devices: 13.5 us -> 12.9 us
    ppermute x6 -> x8, waiting for transfers between devices: 3.98 us -> 3.73 us  [moved(): return lax.ppermute(value, ('dp', 'centers'), pairs_over(target_of))]
    ppermute x6 -> x8, starting transfers between devices: 8.73 us -> 8.73 us  [moved(): return lax.ppermute(value, ('dp', 'centers'), pairs_over(target_of))]
  transfers between devices with their start and end apart: 18 -> 20, of which waited for: 13 -> 13; matrix products, arithmetic and copies ran while one was open for 0% -> 0% of each run, Pallas kernels for 7% -> 10%
where the time goes in v23:
time: 48.4 us; the launch traced here: 48.2 us
  starting transfers between devices  21.1 us (44%)
  Pallas kernels  13.5 us (28%)
  waiting for transfers between devices  12.9 us (27%)
  between operations  0.72 us (1%)
    pallas_call x10, Pallas kernels, call(): pl.pallas_call(body, out_shape=out_shape, in_specs=sources or [VMEM] * le...  13.5 us
    ppermute x12, starting transfers between devices, exchange(): parts.insert(0, lax.ppermute(value, axis, pairs))  12.3 us
    ppermute x12, waiting for transfers between devices, exchange(): parts.insert(0, lax.ppermute(value, axis, pairs))  9.17 us
    ppermute x8, starting transfers between devices, moved(): return lax.ppermute(value, ('dp', 'centers'), pairs_over(target_of))  8.73 us
    ppermute x8, waiting for transfers between devices, moved(): return lax.ppermute(value, ('dp', 'centers'), pairs_over(target_of))  3.73 us
  transfers between devices with their start and end apart: 20, of which 13 were waited for; matrix products, arithmetic and copies ran while one was open for 0% of the time, Pallas kernels for 10%

profile of v23, /device:TPU:0, one launch (start us, length us, event | category | flops | bytes accessed | tf_op | source)
XLA Modules:
  0.0 48.2 jit_solution(14543858500997218202)
XLA Ops:
  0.6 2.0 %shard_map.68 = (bf16[64,4096]{1,0:T(8,128)(2,1)S(1)}, s32[1,512]{1,0:T(1,128)S(1)}, s32[1,4096]{1,0:T(1,128)S(1)}, f32[1,4096]{1,0:T(1,128)S(1)}, f32[1,512]{1,0:T(1,128)S(1)}, /*index=5*/bf16[64,512]{1,0:T(8,128)(2,1)S(1)}) custom-call(bf16[64,4096]{1,0:T(8,128)(2,1)} %feat_hbm.1, s32[1,512]{1,0:T(1,128)} %bitcast.10, s32[1,4096]{1,0:T(1,128)} %bitcast.8, ...), custom_call_target="tpu_custom_call" | custom-call | tf_op jit(solution)/shard_map/pallas_call | solution.py:306
  2.6 2.4 %collective-permute-start.1 = (bf16[64,512]{1,0:T(8,128)(2,1)S(1)}, bf16[64,512]{1,0:T(8,128)(2,1)S(1)}, u32[]{:S(2)}, u32[]{:S(2)}) collective-permute-start(bf16[64,512]{1,0:T(8,128)(2,1)S(1)} %get-tuple-element.31), channel_id=1, source_target_pairs={{0,17},{1,16},{2,19},{3,18},{4,21},{5,20},{6,23},{7,22},{8,25},{9,... | collective-permute-start | bytes 196616 | tf_op jit(solution)/shard_map/ppermute | solution.py:347
  5.0 0.7 %collective-permute-start.2 = (s32[512]{0:T(512)}, s32[512]{0:T(512)S(1)}, u32[]{:S(2)}, u32[]{:S(2)}) collective-permute-start(s32[512]{0:T(512)} %param.8), channel_id=1, source_target_pairs={{0,1},{1,0},{2,3},{3,2},{4,5},{5,4},{6,7},{7,6},{8,9},{9,8},{10,11... | collective-permute-start | bytes 6152 | tf_op jit(solution)/shard_map/ppermute | solution.py:347
  5.7 0.0 collective-permute-start
  5.7 0.7 %shard_map.69 = (bf16[256,4096]{1,0:T(8,128)(2,1)S(1)}, bf16[4096,256]{1,0:T(8,128)(2,1)S(1)}, bf16[16,4096]{1,0:T(8,128)(2,1)S(1)}) custom-call(bf16[64,4096]{1,0:T(8,128)(2,1)S(1)} %get-tuple-element.25.feat_ref, s32[1,4096]{1,0:T(1,128)S(1)} %get-tuple-element.26.slots_ref.refs_3_.refs_4_, f32[1,4096]{1,0:T(1,128)S(1)} %get-tuple-element.27.prices_ref), custom_call_target="tpu_custom_call" | custom-call | flops 4096000 | bytes 4194304 | tf_op jit(solution)/shard_map/pallas_call | solution.py:306
  6.4 0.4 collective-permute-done.2
  6.7 0.9 %shard_map.70.refs_1_ = bf16[64,512]{1,0:T(8,128)(2,1)S(1)} custom-call(bf16[64,4096]{1,0:T(8,128)(2,1)S(1)} %get-tuple-element.25.feat_ref, s32[1,512]{1,0:T(1,128)S(1)} %bitcast.7, s32[1,512]{1,0:T(1,128)S(1)} %get-tuple-element.32.idx_ref), custom_call_target="tpu_custom_call" | custom-call | flops 268435456 | bytes 524288 | tf_op jit(solution)/shard_map/pallas_call | solution.py:306
  7.6 0.0 collective-permute-done
  7.6 0.2 collective-permute-done.1.refs_0_
  7.8 2.5 %shard_map.71 = (bf16[8192,512]{1,0:T(8,128)(2,1)S(1)}, bf16[256,512]{1,0:T(8,128)(2,1)S(1)}, f32[1,512]{1,0:T(1,128)S(1)}, f32[8,512]{1,0:T(8,128)S(1)}) custom-call(bf16[4096,256]{1,0:T(8,128)(2,1)S(1)} %get-tuple-element.28.turned_ref, bf16[16,4096]{1,0:T(8,128)(2,1)S(1)} %get-tuple-element.29.weight_ref, f32[1,512]{1,0:T(1,128)S(1)} %bitcast.6, ...), custom_call_target="tpu_custom_call" | custom-call | flops 134217728 | bytes 8388608 | tf_op jit(solution)/shard_map/pallas_call | solution.py:306
  10.4 1.9 %collective-permute-start.3 = (f32[8,512]{1,0:T(8,128)S(1)}, f32[8,512]{1,0:T(8,128)S(1)}, u32[]{:S(2)}, u32[]{:S(2)}) collective-permute-start(f32[8,512]{1,0:T(8,128)S(1)} %get-tuple-element.33.refs_1_), channel_id=1, source_target_pairs={{0,17},{1,16},{2,19},{3,18},{4,21},{5,20},{6,23},{7,22},{8,25},{9,... | collective-permute-start | bytes 49160 | tf_op jit(solution)/shard_map/ppermute | solution.py:347
  12.3 1.9 %shard_map.72.refs_4_ = bf16[1024,4096]{1,0:T(8,128)(2,1)S(1)} custom-call(bf16[256,4096]{1,0:T(8,128)(2,1)S(1)} %get-tuple-element.35.columns_ref, bf16[256,512]{1,0:T(8,128)(2,1)S(1)} %get-tuple-element.36.center_ref), custom_call_target="tpu_custom_call" | custom-call | flops 134217728 | bytes 8388608 | tf_op jit(solution)/shard_map/pallas_call | solution.py:306
  14.2 0.0 collective-permute-done.3.refs_0_
  14.2 1.2 %shard_map.73 = (f32[8,512]{1,0:T(8,128)S(1)}, f32[1,4224]{1,0:T(1,128)S(1)}) custom-call(f32[8,512]{1,0:T(8,128)S(1)} %collective-permute-done.3.refs_0_, f32[8,512]{1,0:T(8,128)S(1)} %get-tuple-element.33.refs_1_, f32[1,512]{1,0:T(1,128)S(1)} %get-tuple-element.34.refs_2_, s32[1,4096]{1,0:T(1,128)S(1)} %get-tuple-element.26.slots_ref.refs_3_.refs_4_, ...), custom_call_target="tpu_custom_call" | custom-call | tf_op jit(solution)/shard_map/pallas_call | solution.py:306
  15.4 1.6 %collective-permute-start.4 = (f32[1,4224]{1,0:T(1,128)S(1)}, f32[1,4224]{1,0:T(1,128)S(1)}, u32[]{:S(2)}, u32[]{:S(2)}) collective-permute-start(f32[1,4224]{1,0:T(1,128)S(1)} %get-tuple-element.37), channel_id=1, source_target_pairs={{0,2},{1,3},{2,0},{3,1},{4,6},{5,7},{6,4},{7,5},{8,10},{9,11},{10,... | collective-permute-start | bytes 50696 | tf_op jit(solution)/shard_map/ppermute | solution.py:331
  17.0 0.3 collective-permute-start.5
  17.3 0.4 collective-permute-start.6
  17.6 1.6 %collective-permute-done.4 = f32[1,4224]{1,0:T(1,128)S(1)} collective-permute-done((f32[1,4224]{1,0:T(1,128)S(1)}, f32[1,4224]{1,0:T(1,128)S(1)}, u32[]{:S(2)}, u32[]{:S(2)}) %collective-permute-start.4) | collective-permute-done | bytes 16928 | tf_op jit(solution)/shard_map/ppermute | solution.py:331
  19.2 0.9 %collective-permute-done.5 = f32[1,4224]{1,0:T(1,128)S(1)} collective-permute-done((f32[1,4224]{1,0:T(1,128)S(1)}, f32[1,4224]{1,0:T(1,128)S(1)}, u32[]{:S(2)}, u32[]{:S(2)}) %collective-permute-start.5) | collective-permute-done | bytes 16928 | tf_op jit(solution)/shard_map/ppermute | solution.py:331
  20.2 0.0 collective-permute-done.6
  20.2 3.4 %collective-permute-start.7 = (f32[1,4224]{1,0:T(1,128)S(1)}, f32[1,4224]{1,0:T(1,128)S(1)}, u32[]{:S(2)}, u32[]{:S(2)}) collective-permute-start(f32[1,4224]{1,0:T(1,128)S(1)} %add_add_fusion.1.refs_3_), channel_id=1, source_target_pairs={{0,13},{1,12},{2,15},{3,14},{4,9},{5,8},{6,11},{7,10},{8,5},{9,4},... | collective-permute-start | bytes 50696 | tf_op jit(solution)/shard_map/ppermute | solution.py:331
  23.7 0.0 collective-permute-start.8
  23.7 0.6 %collective-permute-start.9 = (f32[1,4224]{1,0:T(1,128)S(1)}, f32[1,4224]{1,0:T(1,128)S(1)}, u32[]{:S(2)}, u32[]{:S(2)}) collective-permute-start(f32[1,4224]{1,0:T(1,128)S(1)} %add_add_fusion.1.refs_3_), channel_id=1, source_target_pairs={{0,5},{1,4},{2,7},{3,6},{4,1},{5,0},{6,3},{7,2},{8,13},{9,12},{10,... | collective-permute-start | bytes 50696 | tf_op jit(solution)/shard_map/ppermute | solution.py:331
  24.3 1.0 %collective-permute-done.7.refs_0_ = f32[1,4224]{1,0:T(1,128)S(1)} collective-permute-done((f32[1,4224]{1,0:T(1,128)S(1)}, f32[1,4224]{1,0:T(1,128)S(1)}, u32[]{:S(2)}, u32[]{:S(2)}) %collective-permute-start.7) | collective-permute-done | bytes 16928 | tf_op jit(solution)/shard_map/ppermute | solution.py:331
  25.3 2.5 %collective-permute-done.8.refs_1_ = f32[1,4224]{1,0:T(1,128)S(1)} collective-permute-done((f32[1,4224]{1,0:T(1,128)S(1)}, f32[1,4224]{1,0:T(1,128)S(1)}, u32[]{:S(2)}, u32[]{:S(2)}) %collective-permute-start.8) | collective-permute-done | bytes 16928 | tf_op jit(solution)/shard_map/ppermute | solution.py:331
  27.7 0.0 collective-permute-done.9.refs_2_
  27.7 1.2 %shard_map.74 = (f32[1,4224]{1,0:T(1,128)S(1)}, f32[8,128]{1,0:T(8,128)S(1)}, f32[8,640]{1,0:T(8,128)S(1)}) custom-call(f32[1,4224]{1,0:T(1,128)S(1)} %collective-permute-done.7.refs_0_, f32[1,4224]{1,0:T(1,128)S(1)} %collective-permute-done.8.refs_1_, f32[1,4224]{1,0:T(1,128)S(1)} %collective-permute-done.9.refs_2_, f32[1,4224]{1,0:T(1,128)S(1)} %add_add_fusion.1.refs_3_, ...), custom_call_target="tpu_custom_call" | custom-call | tf_op jit(solution)/shard_map/pallas_call | solution.py:306
  28.9 1.7 %collective-permute-start.10 = (f32[8,640]{1,0:T(8,128)S(1)}, f32[8,640]{1,0:T(8,128)S(1)}, u32[]{:S(2)}, u32[]{:S(2)}) collective-permute-start(f32[8,640]{1,0:T(8,128)S(1)} %get-tuple-element.39.refs_1_), channel_id=1, source_target_pairs={{0,17},{1,16},{2,19},{3,18},{4,21},{5,20},{6,23},{7,22},{8,25},{9,... | collective-permute-start | bytes 61448 | tf_op jit(solution)/shard_map/ppermute | solution.py:347
  30.6 1.5 %collective-permute-done.10.refs_0_ = f32[8,640]{1,0:T(8,128)S(1)} collective-permute-done((f32[8,640]{1,0:T(8,128)S(1)}, f32[8,640]{1,0:T(8,128)S(1)}, u32[]{:S(2)}, u32[]{:S(2)}) %collective-permute-start.10) | collective-permute-done | bytes 20512 | tf_op jit(solution)/shard_map/ppermute | solution.py:347
  32.1 1.2 %shard_map.75 = (f32[16,512]{1,0:T(8,128)S(1)}, f32[8,128]{1,0:T(8,128)S(1)}, f32[1,4224]{1,0:T(1,128)S(1)}) custom-call(f32[8,640]{1,0:T(8,128)S(1)} %collective-permute-done.10.refs_0_, f32[8,640]{1,0:T(8,128)S(1)} %get-tuple-element.39.refs_1_, f32[1,512]{1,0:T(1,128)S(1)} %get-tuple-element.34.refs_2_, ...), custom_call_target="tpu_custom_call" | custom-call | tf_op jit(solution)/shard_map/pallas_call | solution.py:306
  33.4 0.7 %collective-permute-start.11 = (f32[1,4224]{1,0:T(1,128)S(1)}, f32[1,4224]{1,0:T(1,128)S(1)}, u32[]{:S(2)}, u32[]{:S(2)}) collective-permute-start(f32[1,4224]{1,0:T(1,128)S(1)} %get-tuple-element.42), channel_id=1, source_target_pairs={{0,2},{1,3},{2,0},{3,1},{4,6},{5,7},{6,4},{7,5},{8,10},{9,11},{10,... | collective-permute-start | bytes 50696 | tf_op jit(solution)/shard_map/ppermute | solution.py:331
  34.1 1.0 %collective-permute-start.12 = (f32[1,4224]{1,0:T(1,128)S(1)}, f32[1,4224]{1,0:T(1,128)S(1)}, u32[]{:S(2)}, u32[]{:S(2)}) collective-permute-start(f32[1,4224]{1,0:T(1,128)S(1)} %get-tuple-element.42), channel_id=1, source_target_pairs={{0,3},{1,2},{2,1},{3,0},{4,7},{5,6},{6,5},{7,4},{8,11},{9,10},{10,... | collective-permute-start | bytes 50696 | tf_op jit(solution)/shard_map/ppermute | solution.py:331
  35.1 0.4 collective-permute-start.13
  35.6 1.7 %collective-permute-done.11 = f32[1,4224]{1,0:T(1,128)S(1)} collective-permute-done((f32[1,4224]{1,0:T(1,128)S(1)}, f32[1,4224]{1,0:T(1,128)S(1)}, u32[]{:S(2)}, u32[]{:S(2)}) %collective-permute-start.11) | collective-permute-done | bytes 16928 | tf_op jit(solution)/shard_map/ppermute | solution.py:331
  37.3 0.1 collective-permute-done.12
  37.4 0.0 collective-permute-done.13
  37.4 1.4 %collective-permute-start.14 = (f32[1,4224]{1,0:T(1,128)S(1)}, f32[1,4224]{1,0:T(1,128)S(1)}, u32[]{:S(2)}, u32[]{:S(2)}) collective-permute-start(f32[1,4224]{1,0:T(1,128)S(1)} %add_add_fusion.refs_3_), channel_id=1, source_target_pairs={{0,13},{1,12},{2,15},{3,14},{4,9},{5,8},{6,11},{7,10},{8,5},{9,4},... | collective-permute-start | bytes 50696 | tf_op jit(solution)/shard_map/ppermute | solution.py:331
  38.8 0.6 %collective-permute-start.15 = (f32[1,4224]{1,0:T(1,128)S(1)}, f32[1,4224]{1,0:T(1,128)S(1)}, u32[]{:S(2)}, u32[]{:S(2)}) collective-permute-start(f32[1,4224]{1,0:T(1,128)S(1)} %add_add_fusion.refs_3_), channel_id=1, source_target_pairs={{0,9},{1,8},{2,11},{3,10},{4,13},{5,12},{6,15},{7,14},{8,1},{9,0},... | collective-permute-start | bytes 50696 | tf_op jit(solution)/shard_map/ppermute | solution.py:331
  39.4 1.9 %collective-permute-start.16 = (f32[1,4224]{1,0:T(1,128)S(1)}, f32[1,4224]{1,0:T(1,128)S(1)}, u32[]{:S(2)}, u32[]{:S(2)}) collective-permute-start(f32[1,4224]{1,0:T(1,128)S(1)} %add_add_fusion.refs_3_), channel_id=1, source_target_pairs={{0,5},{1,4},{2,7},{3,6},{4,1},{5,0},{6,3},{7,2},{8,13},{9,12},{10,... | collective-permute-start | bytes 50696 | tf_op jit(solution)/shard_map/ppermute | solution.py:331
  41.3 0.4 collective-permute-start.19
  41.7 0.7 %collective-permute-done.14.refs_0_ = f32[1,4224]{1,0:T(1,128)S(1)} collective-permute-done((f32[1,4224]{1,0:T(1,128)S(1)}, f32[1,4224]{1,0:T(1,128)S(1)}, u32[]{:S(2)}, u32[]{:S(2)}) %collective-permute-start.14) | collective-permute-done | bytes 16928 | tf_op jit(solution)/shard_map/ppermute | solution.py:331
  42.4 0.6 %collective-permute-done.15.refs_1_ = f32[1,4224]{1,0:T(1,128)S(1)} collective-permute-done((f32[1,4224]{1,0:T(1,128)S(1)}, f32[1,4224]{1,0:T(1,128)S(1)}, u32[]{:S(2)}, u32[]{:S(2)}) %collective-permute-start.15) | collective-permute-done | bytes 16928 | tf_op jit(solution)/shard_map/ppermute | solution.py:331
  43.0 0.1 collective-permute-done.16.refs_2_
  43.1 1.3 %shard_map.76 = (f32[8,256]{1,0:T(8,128)S(1)}, f32[8,640]{1,0:T(8,128)S(1)}) custom-call(f32[1,4224]{1,0:T(1,128)S(1)} %collective-permute-done.14.refs_0_, f32[1,4224]{1,0:T(1,128)S(1)} %collective-permute-done.15.refs_1_, f32[1,4224]{1,0:T(1,128)S(1)} %collective-permute-done.16.refs_2_, f32[1,4224]{1,0:T(1,128)S(1)} %add_add_fusion.refs_3_, ...), custom_call_target="tpu_custom_call" | custom-call | tf_op jit(solution)/shard_map/pallas_call | solution.py:306
  44.3 1.6 %collective-permute-start.17 = (f32[8,640]{1,0:T(8,128)S(1)}, f32[8,640]{1,0:T(8,128)S(1)}, u32[]{:S(2)}, u32[]{:S(2)}) collective-permute-start(f32[8,640]{1,0:T(8,128)S(1)} %get-tuple-element.44.refs_2_), channel_id=1, source_target_pairs={{0,16},{1,17},{2,18},{3,19},{4,20},{5,21},{6,22},{7,23},{8,24},{9,... | collective-permute-start | bytes 61448 | tf_op jit(solution)/shard_map/ppermute | solution.py:347
  45.9 0.0 collective-permute-start.18
  45.9 0.0 collective-permute-done.19.refs_3_
  45.9 1.6 %collective-permute-done.17.refs_0_ = f32[8,640]{1,0:T(8,128)S(1)} collective-permute-done((f32[8,640]{1,0:T(8,128)S(1)}, f32[8,640]{1,0:T(8,128)S(1)}, u32[]{:S(2)}, u32[]{:S(2)}) %collective-permute-start.17) | collective-permute-done | bytes 20512 | tf_op jit(solution)/shard_map/ppermute | solution.py:347
  47.6 0.0 collective-permute-done.18.refs_1_
  47.6 0.6 %shard_map.77 = (f32[8,512]{1,0:T(8,128)}, f32[8,512]{1,0:T(8,128)}) custom-call(f32[8,640]{1,0:T(8,128)S(1)} %collective-permute-done.17.refs_0_, f32[8,640]{1,0:T(8,128)S(1)} %collective-permute-done.18.refs_1_, f32[8,640]{1,0:T(8,128)S(1)} %get-tuple-element.44.refs_2_, f32[16,512]{1,0:T(8,128)S(1)} %collective-permute-done.19.refs_3_, ...), custom_call_target="tpu_custom_call" | custom-call | tf_op jit(solution)/shard_map/pallas_call | solution.py:306
  (2 shorter events, 0.1 us)
Async XLA Ops:
  2.6 5.2 %collective-permute-start.1 = (bf16[64,512]{1,0:T(8,128)(2,1)S(1)}, bf16[64,512]{1,0:T(8,128)(2,1)S(1)}, u32[]{:S(2)}, u32[]{:S(2)}) collective-permute-start(bf16[64,512]{1,0:T(8,128)(2,1)S(1)} %get-tuple-element.31), channel_id=1, source_target_pairs={{0,17},{1,16},{2,19},{3,18},{4,21},{5,20},{6,23},{7,22},{8,25},{9,... | collective-permute-start | bytes 196616 | tf_op jit(solution)/shard_map/ppermute | solution.py:347
  5.0 1.7 %collective-permute-start.2 = (s32[512]{0:T(512)}, s32[512]{0:T(512)S(1)}, u32[]{:S(2)}, u32[]{:S(2)}) collective-permute-start(s32[512]{0:T(512)} %param.8), channel_id=1, source_target_pairs={{0,1},{1,0},{2,3},{3,2},{4,5},{5,4},{6,7},{7,6},{8,9},{9,8},{10,11... | collective-permute-start | bytes 6152 | tf_op jit(solution)/shard_map/ppermute | solution.py:347
  5.7 1.9 %collective-permute-start = (f32[512]{0:T(512)}, f32[512]{0:T(512)S(1)}, u32[]{:S(2)}, u32[]{:S(2)}) collective-permute-start(f32[512]{0:T(512)} %param.9), channel_id=1, source_target_pairs={{0,1},{1,0},{2,3},{3,2},{4,5},{5,4},{6,7},{7,6},{8,9},{9,8},{10,11... | collective-permute-start | bytes 6152 | tf_op jit(solution)/shard_map/ppermute | solution.py:347
  10.4 3.8 %collective-permute-start.3 = (f32[8,512]{1,0:T(8,128)S(1)}, f32[8,512]{1,0:T(8,128)S(1)}, u32[]{:S(2)}, u32[]{:S(2)}) collective-permute-start(f32[8,512]{1,0:T(8,128)S(1)} %get-tuple-element.33.refs_1_), channel_id=1, source_target_pairs={{0,17},{1,16},{2,19},{3,18},{4,21},{5,20},{6,23},{7,22},{8,25},{9,... | collective-permute-start | bytes 49160 | tf_op jit(solution)/shard_map/ppermute | solution.py:347
  15.4 3.8 %collective-permute-start.4 = (f32[1,4224]{1,0:T(1,128)S(1)}, f32[1,4224]{1,0:T(1,128)S(1)}, u32[]{:S(2)}, u32[]{:S(2)}) collective-permute-start(f32[1,4224]{1,0:T(1,128)S(1)} %get-tuple-element.37), channel_id=1, source_target_pairs={{0,2},{1,3},{2,0},{3,1},{4,6},{5,7},{6,4},{7,5},{8,10},{9,11},{10,... | collective-permute-start | bytes 50696 | tf_op jit(solution)/shard_map/ppermute | solution.py:331
  17.0 3.2 %collective-permute-start.5 = (f32[1,4224]{1,0:T(1,128)S(1)}, f32[1,4224]{1,0:T(1,128)S(1)}, u32[]{:S(2)}, u32[]{:S(2)}) collective-permute-start(f32[1,4224]{1,0:T(1,128)S(1)} %get-tuple-element.37), channel_id=1, source_target_pairs={{0,3},{1,2},{2,1},{3,0},{4,7},{5,6},{6,5},{7,4},{8,11},{9,10},{10,... | collective-permute-start | bytes 50696 | tf_op jit(solution)/shard_map/ppermute | solution.py:331
  17.3 2.9 %collective-permute-start.6 = (f32[1,4224]{1,0:T(1,128)S(1)}, f32[1,4224]{1,0:T(1,128)S(1)}, u32[]{:S(2)}, u32[]{:S(2)}) collective-permute-start(f32[1,4224]{1,0:T(1,128)S(1)} %get-tuple-element.37), channel_id=1, source_target_pairs={{0,1},{1,0},{2,3},{3,2},{4,5},{5,4},{6,7},{7,6},{8,9},{9,8},{10,11... | collective-permute-start | bytes 50696 | tf_op jit(solution)/shard_map/ppermute | solution.py:331
  20.2 5.0 %collective-permute-start.7 = (f32[1,4224]{1,0:T(1,128)S(1)}, f32[1,4224]{1,0:T(1,128)S(1)}, u32[]{:S(2)}, u32[]{:S(2)}) collective-permute-start(f32[1,4224]{1,0:T(1,128)S(1)} %add_add_fusion.1.refs_3_), channel_id=1, source_target_pairs={{0,13},{1,12},{2,15},{3,14},{4,9},{5,8},{6,11},{7,10},{8,5},{9,4},... | collective-permute-start | bytes 50696 | tf_op jit(solution)/shard_map/ppermute | solution.py:331
  23.7 4.1 %collective-permute-start.8 = (f32[1,4224]{1,0:T(1,128)S(1)}, f32[1,4224]{1,0:T(1,128)S(1)}, u32[]{:S(2)}, u32[]{:S(2)}) collective-permute-start(f32[1,4224]{1,0:T(1,128)S(1)} %add_add_fusion.1.refs_3_), channel_id=1, source_target_pairs={{0,9},{1,8},{2,11},{3,10},{4,13},{5,12},{6,15},{7,14},{8,1},{9,0},... | collective-permute-start | bytes 50696 | tf_op jit(solution)/shard_map/ppermute | solution.py:331
  23.7 4.1 %collective-permute-start.9 = (f32[1,4224]{1,0:T(1,128)S(1)}, f32[1,4224]{1,0:T(1,128)S(1)}, u32[]{:S(2)}, u32[]{:S(2)}) collective-permute-start(f32[1,4224]{1,0:T(1,128)S(1)} %add_add_fusion.1.refs_3_), channel_id=1, source_target_pairs={{0,5},{1,4},{2,7},{3,6},{4,1},{5,0},{6,3},{7,2},{8,13},{9,12},{10,... | collective-permute-start | bytes 50696 | tf_op jit(solution)/shard_map/ppermute | solution.py:331
  28.9 3.2 %collective-permute-start.10 = (f32[8,640]{1,0:T(8,128)S(1)}, f32[8,640]{1,0:T(8,128)S(1)}, u32[]{:S(2)}, u32[]{:S(2)}) collective-permute-start(f32[8,640]{1,0:T(8,128)S(1)} %get-tuple-element.39.refs_1_), channel_id=1, source_target_pairs={{0,17},{1,16},{2,19},{3,18},{4,21},{5,20},{6,23},{7,22},{8,25},{9,... | collective-permute-start | bytes 61448 | tf_op jit(solution)/shard_map/ppermute | solution.py:347
  33.4 3.9 %collective-permute-start.11 = (f32[1,4224]{1,0:T(1,128)S(1)}, f32[1,4224]{1,0:T(1,128)S(1)}, u32[]{:S(2)}, u32[]{:S(2)}) collective-permute-start(f32[1,4224]{1,0:T(1,128)S(1)} %get-tuple-element.42), channel_id=1, source_target_pairs={{0,2},{1,3},{2,0},{3,1},{4,6},{5,7},{6,4},{7,5},{8,10},{9,11},{10,... | collective-permute-start | bytes 50696 | tf_op jit(solution)/shard_map/ppermute | solution.py:331
  34.1 3.3 %collective-permute-start.12 = (f32[1,4224]{1,0:T(1,128)S(1)}, f32[1,4224]{1,0:T(1,128)S(1)}, u32[]{:S(2)}, u32[]{:S(2)}) collective-permute-start(f32[1,4224]{1,0:T(1,128)S(1)} %get-tuple-element.42), channel_id=1, source_target_pairs={{0,3},{1,2},{2,1},{3,0},{4,7},{5,6},{6,5},{7,4},{8,11},{9,10},{10,... | collective-permute-start | bytes 50696 | tf_op jit(solution)/shard_map/ppermute | solution.py:331
  35.1 2.2 %collective-permute-start.13 = (f32[1,4224]{1,0:T(1,128)S(1)}, f32[1,4224]{1,0:T(1,128)S(1)}, u32[]{:S(2)}, u32[]{:S(2)}) collective-permute-start(f32[1,4224]{1,0:T(1,128)S(1)} %get-tuple-element.42), channel_id=1, source_target_pairs={{0,1},{1,0},{2,3},{3,2},{4,5},{5,4},{6,7},{7,6},{8,9},{9,8},{10,11... | collective-permute-start | bytes 50696 | tf_op jit(solution)/shard_map/ppermute | solution.py:331
  37.4 5.0 %collective-permute-start.14 = (f32[1,4224]{1,0:T(1,128)S(1)}, f32[1,4224]{1,0:T(1,128)S(1)}, u32[]{:S(2)}, u32[]{:S(2)}) collective-permute-start(f32[1,4224]{1,0:T(1,128)S(1)} %add_add_fusion.refs_3_), channel_id=1, source_target_pairs={{0,13},{1,12},{2,15},{3,14},{4,9},{5,8},{6,11},{7,10},{8,5},{9,4},... | collective-permute-start | bytes 50696 | tf_op jit(solution)/shard_map/ppermute | solution.py:331
  38.8 4.2 %collective-permute-start.15 = (f32[1,4224]{1,0:T(1,128)S(1)}, f32[1,4224]{1,0:T(1,128)S(1)}, u32[]{:S(2)}, u32[]{:S(2)}) collective-permute-start(f32[1,4224]{1,0:T(1,128)S(1)} %add_add_fusion.refs_3_), channel_id=1, source_target_pairs={{0,9},{1,8},{2,11},{3,10},{4,13},{5,12},{6,15},{7,14},{8,1},{9,0},... | collective-permute-start | bytes 50696 | tf_op jit(solution)/shard_map/ppermute | solution.py:331
  39.4 3.7 %collective-permute-start.16 = (f32[1,4224]{1,0:T(1,128)S(1)}, f32[1,4224]{1,0:T(1,128)S(1)}, u32[]{:S(2)}, u32[]{:S(2)}) collective-permute-start(f32[1,4224]{1,0:T(1,128)S(1)} %add_add_fusion.refs_3_), channel_id=1, source_target_pairs={{0,5},{1,4},{2,7},{3,6},{4,1},{5,0},{6,3},{7,2},{8,13},{9,12},{10,... | collective-permute-start | bytes 50696 | tf_op jit(solution)/shard_map/ppermute | solution.py:331
  41.3 4.6 %collective-permute-start.19 = (f32[16,512]{1,0:T(8,128)S(1)}, f32[16,512]{1,0:T(8,128)S(1)}, u32[]{:S(2)}, u32[]{:S(2)}) collective-permute-start(f32[16,512]{1,0:T(8,128)S(1)} %get-tuple-element.45.refs_4_), channel_id=1, source_target_pairs={{0,1},{1,0},{2,3},{3,2},{4,5},{5,4},{6,7},{7,6},{8,9},{9,8},{10,11... | collective-permute-start | bytes 98312 | tf_op jit(solution)/shard_map/ppermute | solution.py:347
  44.3 3.2 %collective-permute-start.17 = (f32[8,640]{1,0:T(8,128)S(1)}, f32[8,640]{1,0:T(8,128)S(1)}, u32[]{:S(2)}, u32[]{:S(2)}) collective-permute-start(f32[8,640]{1,0:T(8,128)S(1)} %get-tuple-element.44.refs_2_), channel_id=1, source_target_pairs={{0,16},{1,17},{2,18},{3,19},{4,20},{5,21},{6,22},{7,23},{8,24},{9,... | collective-permute-start | bytes 61448 | tf_op jit(solution)/shard_map/ppermute | solution.py:347
  45.9 1.6 %collective-permute-start.18 = (f32[8,640]{1,0:T(8,128)S(1)}, f32[8,640]{1,0:T(8,128)S(1)}, u32[]{:S(2)}, u32[]{:S(2)}) collective-permute-start(f32[8,640]{1,0:T(8,128)S(1)} %get-tuple-element.44.refs_2_), channel_id=1, source_target_pairs={{0,1},{1,0},{2,3},{3,2},{4,5},{5,4},{6,7},{7,6},{8,9},{9,8},{10,11... | collective-permute-start | bytes 61448 | tf_op jit(solution)/shard_map/ppermute | solution.py:347

commit v24 on v23

--- a/solution.py
+++ b/solution.py
@@ -110,8 +110,14 @@
         hit_ref[begin : begin + STEP, :] = hit
 
 
+def store_halves(picked, left_ref, right_ref):
+    half = left_ref.shape[1]
+    left_ref[...] = picked[:, :half].astype(bf16)
+    right_ref[...] = picked[:, half:].astype(bf16)
+
+
 def pick_body(feat_hbm, idx_hbm, slots_hbm, prices_hbm, scale_hbm, *refs):
-    feat_ref, idx_ref, slots_ref, prices_ref, scale_ref, out_ref, hit_ref, sems = refs
+    feat_ref, idx_ref, slots_ref, prices_ref, scale_ref, left_ref, right_ref, hit_ref, sems = refs
     sources = (idx_hbm, feat_hbm, slots_hbm, prices_hbm, scale_hbm)
     targets = (idx_ref, feat_ref, slots_ref, prices_ref, scale_ref)
     copies = [
@@ -126,15 +132,14 @@
     picked = jnp.dot(feat_ref[...], hit_ref[...], preferred_element_type=f32)
     for copy in copies[2:]:
         copy.wait()
-    out_ref[...] = picked.astype(bf16)
-
-
-def pick_beside_body(feat_ref, moved_idx_ref, idx_ref, out_ref, hit_ref):
+    store_halves(picked, left_ref, right_ref)
+
+
+def pick_beside_body(feat_ref, moved_idx_ref, idx_ref, left_ref, right_ref, hit_ref):
     first = lax.axis_index("dp") == 0
     pick(feat_ref, jnp.where(first, idx_ref[...], moved_idx_ref[...]), hit_ref)
-    out_ref[...] = jnp.dot(
-        feat_ref[...], hit_ref[...], preferred_element_type=f32
-    ).astype(bf16)
+    picked = jnp.dot(feat_ref[...], hit_ref[...], preferred_element_type=f32)
+    store_halves(picked, left_ref, right_ref)
 
 
 def columns_body(feat_ref, slots_ref, prices_ref, columns_ref, turned_ref, weight_ref):
@@ -152,9 +157,11 @@
 
 
 def rows_body(parts, turned_ref, weight_ref, moved_scale_ref, own_scale_ref, *refs):
-    center_refs, (block_ref, center_ref, scale_ref, out_ref) = refs[:parts], refs[parts:]
+    left_refs, right_refs = refs[:parts], refs[parts : 2 * parts]
+    block_ref, center_ref, scale_ref, out_ref = refs[2 * parts :]
     scale_ref[...] = resident(moved_scale_ref[...], own_scale_ref[...])
-    center = total_of(center_refs).astype(f32)
+    center = jnp.concatenate([total_of(left_refs), total_of(right_refs)], axis=1)
+    center = center.astype(f32)
     center = jnp.concatenate(
         [*split3(center * FACTOR), norm_rows(center, 0)], axis=0
     ).astype(bf16)
@@ -316,7 +323,7 @@
     )(*args)
 
 
-def exchange(value, axis):
+def exchange(value, axis, later=(1, 2, 3)):
     size = lax.axis_size(axis)
     parts = [value]
     stride = 1
@@ -325,7 +332,7 @@
         span = min(4, size // stride)
         side = 0 if stride == 1 else 1
         parts = [value]
-        offsets = (1, 3, 2) if stride == 1 else (1, 2, 3)
+        offsets = (1, 3, 2) if stride == 1 else later
         for offset in offsets[: span - 1]:
             pairs = [(i, i ^ (offset * stride) ^ side) for i in range(size)]
             parts.insert(0, lax.ppermute(value, axis, pairs))
@@ -392,7 +399,8 @@
             center_scale.reshape(1, count),
         )
     ]
-    features, idx, slots, prices, own_scale, picked = call(
+    picked_half = shaped((depth, count // 2), bf16)
+    features, idx, slots, prices, own_scale, *picked = call(
         pick_body,
         (
             shaped(features.shape, bf16),
@@ -400,7 +408,8 @@
             shaped((1, row_count), jnp.int32),
             shaped((1, row_count)),
             shaped((1, count)),
-            shaped((depth, count), bf16),
+            picked_half,
+            picked_half,
         ),
         *inputs,
         sources=[HBM] * 5,
@@ -413,16 +422,18 @@
         moved_idx = moved(center_idx, beside)
         resident_picks = call(
             pick_beside_body,
-            shaped((depth, count), bf16),
+            (picked_half, picked_half),
             features, moved_idx.reshape(1, count), idx,
             flops=128 * row_count * count,
             bytes_accessed=128 * row_count,
             scratch_shapes=[pltpu.VMEM((row_count, count), bf16)],
         )
-        centers = [moved(picked, outward), resident_picks]
+        centers = [
+            [moved(part, outward), other] for part, other in zip(picked, resident_picks)
+        ]
         moved_scale = moved(center_scale, beside).reshape(1, count)
     else:
-        centers = exchange(picked, "dp")
+        centers = [exchange(part, "dp") for part in picked]
         moved_scale = own_scale
     columns, turned_columns, weight = call(
         columns_body,
@@ -436,14 +447,14 @@
         bytes_accessed=1024 * row_count,
     )
     block, center, scale, first = call(
-        partial(rows_body, len(centers)),
+        partial(rows_body, len(centers[0])),
         (
             shaped((2 * row_count, count), bf16),
             shaped((DEPTH, count), bf16),
             shaped((1, count)),
             vector,
         ),
-        turned_columns, weight, moved_scale, own_scale, *centers,
+        turned_columns, weight, moved_scale, own_scale, *centers[0], *centers[1],
         **pass_cost,
     )
     firsts = share(first)
@@ -455,7 +466,7 @@
         (vector, row_shape),
         *firsts, scale, slots, turned,
     )
-    rows = exchange(rows, "centers")
+    rows = exchange(rows, "centers", (3, 1, 2))
     rows, norm, folded = call(
         partial(first_fold_body, len(rows)), (row_shape, narrow, fold_shape), *rows, slots, block
     )

time: 48.4 us -> 49.2 us (1.017)
  waiting for transfers between devices: 12.9 us -> 16.4 us
  starting transfers between devices: 21.1 us -> 18.3 us
    ppermute x8 -> x9, waiting for transfers between devices: 3.73 us -> 7.17 us  [moved(): return lax.ppermute(value, ('dp', 'centers'), pairs_over(target_of))]
    ppermute x8 -> x9, starting transfers between devices: 8.73 us -> 6.01 us  [moved(): return lax.ppermute(value, ('dp', 'centers'), pairs_over(target_of))]
  transfers between devices with their start and end apart: 20 -> 21, of which waited for: 13 -> 13; matrix products, arithmetic and copies ran while one was open for 0% -> 0% of each run, Pallas kernels for 10% -> 10%
where the time goes in v24:
time: 49.2 us; the launch traced here: 49 us
  starting transfers between devices  18.3 us (37%)
  waiting for transfers between devices  16.4 us (33%)
  Pallas kernels  13.5 us (27%)
  between operations  0.72 us (1%)
    pallas_call x10, Pallas kernels, call(): pl.pallas_call(body, out_shape=out_shape, in_specs=sources or [VMEM] * le...  13.5 us
    ppermute x12, starting transfers between devices, exchange(): parts.insert(0, lax.ppermute(value, axis, pairs))  12.3 us
    ppermute x12, waiting for transfers between devices, exchange(): parts.insert(0, lax.ppermute(value, axis, pairs))  9.23 us
    ppermute x9, waiting for transfers between devices, moved(): return lax.ppermute(value, ('dp', 'centers'), pairs_over(target_of))  7.17 us
    ppermute x9, starting transfers between devices, moved(): return lax.ppermute(value, ('dp', 'centers'), pairs_over(target_of))  6.01 us
  transfers between devices with their start and end apart: 21, of which 13 were waited for; matrix products, arithmetic and copies ran while one was open for 0% of the time, Pallas kernels for 10%

profile of v24, /device:TPU:0, one launch (start us, length us, event | category | flops | bytes accessed | tf_op | source)
XLA Modules:
  0.0 49.0 jit_solution(14797409043974668969)
XLA Ops:
  0.6 2.0 %shard_map.68 = (bf16[64,4096]{1,0:T(8,128)(2,1)S(1)}, s32[1,512]{1,0:T(1,128)S(1)}, s32[1,4096]{1,0:T(1,128)S(1)}, f32[1,4096]{1,0:T(1,128)S(1)}, f32[1,512]{1,...) custom-call(bf16[64,4096]{1,0:T(8,128)(2,1)} %feat_hbm.1, s32[1,512]{1,0:T(1,128)} %bitcast.10, ...), custom_call_target="tpu_custom_call" | custom-call | tf_op jit(solution)/shard_map/pallas_call | solution.py:313
  2.6 2.4 %collective-permute-start.1 = (bf16[64,256]{1,0:T(8,128)(2,1)S(1)}, bf16[64,256]{1,0:T(8,128)(2,1)S(1)}, u32[]{:S(2)}, u32[]{:S(2)}) collective-permute-start(bf16[64,256]{1,0:T(8,128)(2,1)S(1)} %get-tuple-element.34), channel_id=1, source_target_pairs={{0,17},{1,16},{2,19},{3,18},{4,21},{5,20},{6,23},{7,22},{8,25},{9,... | collective-permute-start | bytes 98312 | tf_op jit(solution)/shard_map/ppermute | solution.py:354
  5.0 0.1 collective-permute-start.3
  5.1 0.7 %collective-permute-start.2 = (s32[512]{0:T(512)}, s32[512]{0:T(512)S(1)}, u32[]{:S(2)}, u32[]{:S(2)}) collective-permute-start(s32[512]{0:T(512)} %param.8), channel_id=1, source_target_pairs={{0,1},{1,0},{2,3},{3,2},{4,5},{5,4},{6,7},{7,6},{8,9},{9,8},{10,11... | collective-permute-start | bytes 6152 | tf_op jit(solution)/shard_map/ppermute | solution.py:354
  5.8 0.0 collective-permute-start
  5.8 0.7 %shard_map.69 = (bf16[256,4096]{1,0:T(8,128)(2,1)S(1)}, bf16[4096,256]{1,0:T(8,128)(2,1)S(1)}, bf16[16,4096]{1,0:T(8,128)(2,1)S(1)}) custom-call(bf16[64,4096]{1,0:T(8,128)(2,1)S(1)} %get-tuple-element.28.feat_ref, s32[1,4096]{1,0:T(1,128)S(1)} %get-tuple-element.29.slots_ref.refs_3_.refs_4_, f32[1,4096]{1,0:T(1,128)S(1)} %get-tuple-element.30.prices_ref), custom_call_target="tpu_custom_call" | custom-call | flops 4096000 | bytes 4194304 | tf_op jit(solution)/shard_map/pallas_call | solution.py:313
  6.4 0.4 collective-permute-done.2
  6.8 0.9 %shard_map.70 = (bf16[64,256]{1,0:T(8,128)(2,1)S(1)}, bf16[64,256]{1,0:T(8,128)(2,1)S(1)}) custom-call(bf16[64,4096]{1,0:T(8,128)(2,1)S(1)} %get-tuple-element.28.feat_ref, s32[1,512]{1,0:T(1,128)S(1)} %bitcast.7, s32[1,512]{1,0:T(1,128)S(1)} %get-tuple-element.35.idx_ref), custom_call_target="tpu_custom_call" | custom-call | flops 268435456 | bytes 524288 | tf_op jit(solution)/shard_map/pallas_call | solution.py:313
  7.7 0.0 collective-permute-done
  7.7 0.0 collective-permute-done.1.refs_0_
  7.7 1.3 %collective-permute-done.3.refs_2_ = bf16[64,256]{1,0:T(8,128)(2,1)S(1)} collective-permute-done((bf16[64,256]{1,0:T(8,128)(2,1)S(1)}, bf16[64,256]{1,0:T(8,128)(2,1)S(1)}, u32[]{:S(2)}, u32[]{:S(2)}) %collective-permute-start.3) | collective-permute-done | bytes 32800 | tf_op jit(solution)/shard_map/ppermute | solution.py:354
  9.0 2.6 %shard_map.71 = (bf16[8192,512]{1,0:T(8,128)(2,1)S(1)}, bf16[256,512]{1,0:T(8,128)(2,1)S(1)}, f32[1,512]{1,0:T(1,128)S(1)}, f32[8,512]{1,0:T(8,128)S(1)}) custom-call(bf16[4096,256]{1,0:T(8,128)(2,1)S(1)} %get-tuple-element.31.turned_ref, bf16[16,4096]{1,0:T(8,128)(2,1)S(1)} %get-tuple-element.32.weight_ref, f32[1,512]{1,0:T(1,128)S(1)} %bitcast.6, ...), custom_call_target="tpu_custom_call" | custom-call | flops 134217728 | bytes 8388608 | tf_op jit(solution)/shard_map/pallas_call | solution.py:313
  11.6 0.7 %collective-permute-start.4 = (f32[8,512]{1,0:T(8,128)S(1)}, f32[8,512]{1,0:T(8,128)S(1)}, u32[]{:S(2)}, u32[]{:S(2)}) collective-permute-start(f32[8,512]{1,0:T(8,128)S(1)} %get-tuple-element.39.refs_1_), channel_id=1, source_target_pairs={{0,17},{1,16},{2,19},{3,18},{4,21},{5,20},{6,23},{7,22},{8,25},{9,... | collective-permute-start | bytes 49160 | tf_op jit(solution)/shard_map/ppermute | solution.py:354
  12.3 1.9 %shard_map.72.refs_4_ = bf16[1024,4096]{1,0:T(8,128)(2,1)S(1)} custom-call(bf16[256,4096]{1,0:T(8,128)(2,1)S(1)} %get-tuple-element.41.columns_ref, bf16[256,512]{1,0:T(8,128)(2,1)S(1)} %get-tuple-element.42.center_ref), custom_call_target="tpu_custom_call" | custom-call | flops 134217728 | bytes 8388608 | tf_op jit(solution)/shard_map/pallas_call | solution.py:313
  14.2 0.7 %collective-permute-done.4.refs_0_ = f32[8,512]{1,0:T(8,128)S(1)} collective-permute-done((f32[8,512]{1,0:T(8,128)S(1)}, f32[8,512]{1,0:T(8,128)S(1)}, u32[]{:S(2)}, u32[]{:S(2)}) %collective-permute-start.4) | collective-permute-done | bytes 16416 | tf_op jit(solution)/shard_map/ppermute | solution.py:354
  15.0 1.2 %shard_map.73 = (f32[8,512]{1,0:T(8,128)S(1)}, f32[1,4224]{1,0:T(1,128)S(1)}) custom-call(f32[8,512]{1,0:T(8,128)S(1)} %collective-permute-done.4.refs_0_, f32[8,512]{1,0:T(8,128)S(1)} %get-tuple-element.39.refs_1_, f32[1,512]{1,0:T(1,128)S(1)} %get-tuple-element.40.refs_2_, s32[1,4096]{1,0:T(1,128)S(1)} %get-tuple-element.29.slots_ref.refs_3_.refs_4_, ...), custom_call_target="tpu_custom_call" | custom-call | tf_op jit(solution)/shard_map/pallas_call | solution.py:313
  16.2 1.6 %collective-permute-start.5 = (f32[1,4224]{1,0:T(1,128)S(1)}, f32[1,4224]{1,0:T(1,128)S(1)}, u32[]{:S(2)}, u32[]{:S(2)}) collective-permute-start(f32[1,4224]{1,0:T(1,128)S(1)} %get-tuple-element.43), channel_id=1, source_target_pairs={{0,2},{1,3},{2,0},{3,1},{4,6},{5,7},{6,4},{7,5},{8,10},{9,11},{10,... | collective-permute-start | bytes 50696 | tf_op jit(solution)/shard_map/ppermute | solution.py:338
  17.8 0.0 collective-permute-start.6
  17.8 0.6 %collective-permute-start.7 = (f32[1,4224]{1,0:T(1,128)S(1)}, f32[1,4224]{1,0:T(1,128)S(1)}, u32[]{:S(2)}, u32[]{:S(2)}) collective-permute-start(f32[1,4224]{1,0:T(1,128)S(1)} %get-tuple-element.43), channel_id=1, source_target_pairs={{0,1},{1,0},{2,3},{3,2},{4,5},{5,4},{6,7},{7,6},{8,9},{9,8},{10,11... | collective-permute-start | bytes 50696 | tf_op jit(solution)/shard_map/ppermute | solution.py:338
  18.4 1.6 %collective-permute-done.5 = f32[1,4224]{1,0:T(1,128)S(1)} collective-permute-done((f32[1,4224]{1,0:T(1,128)S(1)}, f32[1,4224]{1,0:T(1,128)S(1)}, u32[]{:S(2)}, u32[]{:S(2)}) %collective-permute-start.5) | collective-permute-done | bytes 16928 | tf_op jit(solution)/shard_map/ppermute | solution.py:338
  20.0 1.1 %collective-permute-done.6 = f32[1,4224]{1,0:T(1,128)S(1)} collective-permute-done((f32[1,4224]{1,0:T(1,128)S(1)}, f32[1,4224]{1,0:T(1,128)S(1)}, u32[]{:S(2)}, u32[]{:S(2)}) %collective-permute-start.6) | collective-permute-done | bytes 16928 | tf_op jit(solution)/shard_map/ppermute | solution.py:338
  21.1 0.0 collective-permute-done.7
  21.1 3.4 %collective-permute-start.10 = (f32[1,4224]{1,0:T(1,128)S(1)}, f32[1,4224]{1,0:T(1,128)S(1)}, u32[]{:S(2)}, u32[]{:S(2)}) collective-permute-start(f32[1,4224]{1,0:T(1,128)S(1)} %add_add_fusion.1.refs_3_), channel_id=1, source_target_pairs={{0,13},{1,12},{2,15},{3,14},{4,9},{5,8},{6,11},{7,10},{8,5},{9,4},... | collective-permute-start | bytes 50696 | tf_op jit(solution)/shard_map/ppermute | solution.py:338
  24.5 0.0 collective-permute-start.8
  24.5 0.6 %collective-permute-start.9 = (f32[1,4224]{1,0:T(1,128)S(1)}, f32[1,4224]{1,0:T(1,128)S(1)}, u32[]{:S(2)}, u32[]{:S(2)}) collective-permute-start(f32[1,4224]{1,0:T(1,128)S(1)} %add_add_fusion.1.refs_3_), channel_id=1, source_target_pairs={{0,5},{1,4},{2,7},{3,6},{4,1},{5,0},{6,3},{7,2},{8,13},{9,12},{10,... | collective-permute-start | bytes 50696 | tf_op jit(solution)/shard_map/ppermute | solution.py:338
  25.2 1.0 %collective-permute-done.10.refs_2_ = f32[1,4224]{1,0:T(1,128)S(1)} collective-permute-done((f32[1,4224]{1,0:T(1,128)S(1)}, f32[1,4224]{1,0:T(1,128)S(1)}, u32[]{:S(2)}, u32[]{:S(2)}) %collective-permute-start.10) | collective-permute-done | bytes 16928 | tf_op jit(solution)/shard_map/ppermute | solution.py:338
  26.2 2.4 %collective-permute-done.8.refs_0_ = f32[1,4224]{1,0:T(1,128)S(1)} collective-permute-done((f32[1,4224]{1,0:T(1,128)S(1)}, f32[1,4224]{1,0:T(1,128)S(1)}, u32[]{:S(2)}, u32[]{:S(2)}) %collective-permute-start.8) | collective-permute-done | bytes 16928 | tf_op jit(solution)/shard_map/ppermute | solution.py:338
  28.6 0.0 collective-permute-done.9.refs_1_
  28.6 1.2 %shard_map.74 = (f32[1,4224]{1,0:T(1,128)S(1)}, f32[8,128]{1,0:T(8,128)S(1)}, f32[8,640]{1,0:T(8,128)S(1)}) custom-call(f32[1,4224]{1,0:T(1,128)S(1)} %collective-permute-done.8.refs_0_, f32[1,4224]{1,0:T(1,128)S(1)} %collective-permute-done.9.refs_1_, f32[1,4224]{1,0:T(1,128)S(1)} %collective-permute-done.10.refs_2_, f32[1,4224]{1,0:T(1,128)S(1)} %add_add_fusion.1.refs_3_, ...), custom_call_target="tpu_custom_call" | custom-call | tf_op jit(solution)/shard_map/pallas_call | solution.py:313
  29.8 0.9 %collective-permute-start.11 = (f32[8,640]{1,0:T(8,128)S(1)}, f32[8,640]{1,0:T(8,128)S(1)}, u32[]{:S(2)}, u32[]{:S(2)}) collective-permute-start(f32[8,640]{1,0:T(8,128)S(1)} %get-tuple-element.45.refs_1_), channel_id=1, source_target_pairs={{0,17},{1,16},{2,19},{3,18},{4,21},{5,20},{6,23},{7,22},{8,25},{9,... | collective-permute-start | bytes 61448 | tf_op jit(solution)/shard_map/ppermute | solution.py:354
  30.6 2.4 %collective-permute-done.11.refs_0_ = f32[8,640]{1,0:T(8,128)S(1)} collective-permute-done((f32[8,640]{1,0:T(8,128)S(1)}, f32[8,640]{1,0:T(8,128)S(1)}, u32[]{:S(2)}, u32[]{:S(2)}) %collective-permute-start.11) | collective-permute-done | bytes 20512 | tf_op jit(solution)/shard_map/ppermute | solution.py:354
  33.0 1.2 %shard_map.75 = (f32[16,512]{1,0:T(8,128)S(1)}, f32[8,128]{1,0:T(8,128)S(1)}, f32[1,4224]{1,0:T(1,128)S(1)}) custom-call(f32[8,640]{1,0:T(8,128)S(1)} %collective-permute-done.11.refs_0_, f32[8,640]{1,0:T(8,128)S(1)} %get-tuple-element.45.refs_1_, f32[1,512]{1,0:T(1,128)S(1)} %get-tuple-element.40.refs_2_, ...), custom_call_target="tpu_custom_call" | custom-call | tf_op jit(solution)/shard_map/pallas_call | solution.py:313
  34.2 0.6 %collective-permute-start.12 = (f32[1,4224]{1,0:T(1,128)S(1)}, f32[1,4224]{1,0:T(1,128)S(1)}, u32[]{:S(2)}, u32[]{:S(2)}) collective-permute-start(f32[1,4224]{1,0:T(1,128)S(1)} %get-tuple-element.48), channel_id=1, source_target_pairs={{0,2},{1,3},{2,0},{3,1},{4,6},{5,7},{6,4},{7,5},{8,10},{9,11},{10,... | collective-permute-start | bytes 50696 | tf_op jit(solution)/shard_map/ppermute | solution.py:338
  34.8 1.3 %collective-permute-start.13 = (f32[1,4224]{1,0:T(1,128)S(1)}, f32[1,4224]{1,0:T(1,128)S(1)}, u32[]{:S(2)}, u32[]{:S(2)}) collective-permute-start(f32[1,4224]{1,0:T(1,128)S(1)} %get-tuple-element.48), channel_id=1, source_target_pairs={{0,3},{1,2},{2,1},{3,0},{4,7},{5,6},{6,5},{7,4},{8,11},{9,10},{10,... | collective-permute-start | bytes 50696 | tf_op jit(solution)/shard_map/ppermute | solution.py:338
  36.1 0.3 collective-permute-start.14
  36.4 1.7 %collective-permute-done.12 = f32[1,4224]{1,0:T(1,128)S(1)} collective-permute-done((f32[1,4224]{1,0:T(1,128)S(1)}, f32[1,4224]{1,0:T(1,128)S(1)}, u32[]{:S(2)}, u32[]{:S(2)}) %collective-permute-start.12) | collective-permute-done | bytes 16928 | tf_op jit(solution)/shard_map/ppermute | solution.py:338
  38.2 0.0 collective-permute-done.13
  38.2 0.0 collective-permute-done.14
  38.2 1.3 %collective-permute-start.15 = (f32[1,4224]{1,0:T(1,128)S(1)}, f32[1,4224]{1,0:T(1,128)S(1)}, u32[]{:S(2)}, u32[]{:S(2)}) collective-permute-start(f32[1,4224]{1,0:T(1,128)S(1)} %add_add_fusion.refs_3_), channel_id=1, source_target_pairs={{0,13},{1,12},{2,15},{3,14},{4,9},{5,8},{6,11},{7,10},{8,5},{9,4},... | collective-permute-start | bytes 50696 | tf_op jit(solution)/shard_map/ppermute | solution.py:338
  39.5 0.6 %collective-permute-start.16 = (f32[1,4224]{1,0:T(1,128)S(1)}, f32[1,4224]{1,0:T(1,128)S(1)}, u32[]{:S(2)}, u32[]{:S(2)}) collective-permute-start(f32[1,4224]{1,0:T(1,128)S(1)} %add_add_fusion.refs_3_), channel_id=1, source_target_pairs={{0,9},{1,8},{2,11},{3,10},{4,13},{5,12},{6,15},{7,14},{8,1},{9,0},... | collective-permute-start | bytes 50696 | tf_op jit(solution)/shard_map/ppermute | solution.py:338
  40.1 2.0 %collective-permute-start.17 = (f32[1,4224]{1,0:T(1,128)S(1)}, f32[1,4224]{1,0:T(1,128)S(1)}, u32[]{:S(2)}, u32[]{:S(2)}) collective-permute-start(f32[1,4224]{1,0:T(1,128)S(1)} %add_add_fusion.refs_3_), channel_id=1, source_target_pairs={{0,5},{1,4},{2,7},{3,6},{4,1},{5,0},{6,3},{7,2},{8,13},{9,12},{10,... | collective-permute-start | bytes 50696 | tf_op jit(solution)/shard_map/ppermute | solution.py:338
  42.1 0.4 collective-permute-start.20
  42.5 0.7 %collective-permute-done.15.refs_0_ = f32[1,4224]{1,0:T(1,128)S(1)} collective-permute-done((f32[1,4224]{1,0:T(1,128)S(1)}, f32[1,4224]{1,0:T(1,128)S(1)}, u32[]{:S(2)}, u32[]{:S(2)}) %collective-permute-start.15) | collective-permute-done | bytes 16928 | tf_op jit(solution)/shard_map/ppermute | solution.py:338
  43.2 0.6 %collective-permute-done.16.refs_1_ = f32[1,4224]{1,0:T(1,128)S(1)} collective-permute-done((f32[1,4224]{1,0:T(1,128)S(1)}, f32[1,4224]{1,0:T(1,128)S(1)}, u32[]{:S(2)}, u32[]{:S(2)}) %collective-permute-start.16) | collective-permute-done | bytes 16928 | tf_op jit(solution)/shard_map/ppermute | solution.py:338
  43.8 0.1 collective-permute-done.17.refs_2_
  43.9 1.3 %shard_map.76 = (f32[8,256]{1,0:T(8,128)S(1)}, f32[8,640]{1,0:T(8,128)S(1)}) custom-call(f32[1,4224]{1,0:T(1,128)S(1)} %collective-permute-done.15.refs_0_, f32[1,4224]{1,0:T(1,128)S(1)} %collective-permute-done.16.refs_1_, f32[1,4224]{1,0:T(1,128)S(1)} %collective-permute-done.17.refs_2_, f32[1,4224]{1,0:T(1,128)S(1)} %add_add_fusion.refs_3_, ...), custom_call_target="tpu_custom_call" | custom-call | tf_op jit(solution)/shard_map/pallas_call | solution.py:313
  45.1 0.8 %collective-permute-start.18 = (f32[8,640]{1,0:T(8,128)S(1)}, f32[8,640]{1,0:T(8,128)S(1)}, u32[]{:S(2)}, u32[]{:S(2)}) collective-permute-start(f32[8,640]{1,0:T(8,128)S(1)} %get-tuple-element.50.refs_2_), channel_id=1, source_target_pairs={{0,16},{1,17},{2,18},{3,19},{4,20},{5,21},{6,22},{7,23},{8,24},{9,... | collective-permute-start | bytes 61448 | tf_op jit(solution)/shard_map/ppermute | solution.py:354
  46.0 0.0 collective-permute-start.19
  46.0 0.0 collective-permute-done.20.refs_3_
  46.0 2.4 %collective-permute-done.18.refs_0_ = f32[8,640]{1,0:T(8,128)S(1)} collective-permute-done((f32[8,640]{1,0:T(8,128)S(1)}, f32[8,640]{1,0:T(8,128)S(1)}, u32[]{:S(2)}, u32[]{:S(2)}) %collective-permute-start.18) | collective-permute-done | bytes 20512 | tf_op jit(solution)/shard_map/ppermute | solution.py:354
  48.4 0.0 collective-permute-done.19.refs_1_
  48.4 0.6 %shard_map.77 = (f32[8,512]{1,0:T(8,128)}, f32[8,512]{1,0:T(8,128)}) custom-call(f32[8,640]{1,0:T(8,128)S(1)} %collective-permute-done.18.refs_0_, f32[8,640]{1,0:T(8,128)S(1)} %collective-permute-done.19.refs_1_, f32[8,640]{1,0:T(8,128)S(1)} %get-tuple-element.50.refs_2_, f32[16,512]{1,0:T(8,128)S(1)} %collective-permute-done.20.refs_3_, ...), custom_call_target="tpu_custom_call" | custom-call | tf_op jit(solution)/shard_map/pallas_call | solution.py:313
  (2 shorter events, 0.1 us)
Async XLA Ops:
  2.6 5.1 %collective-permute-start.1 = (bf16[64,256]{1,0:T(8,128)(2,1)S(1)}, bf16[64,256]{1,0:T(8,128)(2,1)S(1)}, u32[]{:S(2)}, u32[]{:S(2)}) collective-permute-start(bf16[64,256]{1,0:T(8,128)(2,1)S(1)} %get-tuple-element.34), channel_id=1, source_target_pairs={{0,17},{1,16},{2,19},{3,18},{4,21},{5,20},{6,23},{7,22},{8,25},{9,... | collective-permute-start | bytes 98312 | tf_op jit(solution)/shard_map/ppermute | solution.py:354
  5.0 4.0 %collective-permute-start.3 = (bf16[64,256]{1,0:T(8,128)(2,1)S(1)}, bf16[64,256]{1,0:T(8,128)(2,1)S(1)}, u32[]{:S(2)}, u32[]{:S(2)}) collective-permute-start(bf16[64,256]{1,0:T(8,128)(2,1)S(1)} %get-tuple-element.37), channel_id=1, source_target_pairs={{0,17},{1,16},{2,19},{3,18},{4,21},{5,20},{6,23},{7,22},{8,25},{9,... | collective-permute-start | bytes 98312 | tf_op jit(solution)/shard_map/ppermute | solution.py:354
  5.1 1.7 %collective-permute-start.2 = (s32[512]{0:T(512)}, s32[512]{0:T(512)S(1)}, u32[]{:S(2)}, u32[]{:S(2)}) collective-permute-start(s32[512]{0:T(512)} %param.8), channel_id=1, source_target_pairs={{0,1},{1,0},{2,3},{3,2},{4,5},{5,4},{6,7},{7,6},{8,9},{9,8},{10,11... | collective-permute-start | bytes 6152 | tf_op jit(solution)/shard_map/ppermute | solution.py:354
  5.8 1.9 %collective-permute-start = (f32[512]{0:T(512)}, f32[512]{0:T(512)S(1)}, u32[]{:S(2)}, u32[]{:S(2)}) collective-permute-start(f32[512]{0:T(512)} %param.9), channel_id=1, source_target_pairs={{0,1},{1,0},{2,3},{3,2},{4,5},{5,4},{6,7},{7,6},{8,9},{9,8},{10,11... | collective-permute-start | bytes 6152 | tf_op jit(solution)/shard_map/ppermute | solution.py:354
  11.6 3.4 %collective-permute-start.4 = (f32[8,512]{1,0:T(8,128)S(1)}, f32[8,512]{1,0:T(8,128)S(1)}, u32[]{:S(2)}, u32[]{:S(2)}) collective-permute-start(f32[8,512]{1,0:T(8,128)S(1)} %get-tuple-element.39.refs_1_), channel_id=1, source_target_pairs={{0,17},{1,16},{2,19},{3,18},{4,21},{5,20},{6,23},{7,22},{8,25},{9,... | collective-permute-start | bytes 49160 | tf_op jit(solution)/shard_map/ppermute | solution.py:354
  16.2 3.8 %collective-permute-start.5 = (f32[1,4224]{1,0:T(1,128)S(1)}, f32[1,4224]{1,0:T(1,128)S(1)}, u32[]{:S(2)}, u32[]{:S(2)}) collective-permute-start(f32[1,4224]{1,0:T(1,128)S(1)} %get-tuple-element.43), channel_id=1, source_target_pairs={{0,2},{1,3},{2,0},{3,1},{4,6},{5,7},{6,4},{7,5},{8,10},{9,11},{10,... | collective-permute-start | bytes 50696 | tf_op jit(solution)/shard_map/ppermute | solution.py:338
  17.8 3.3 %collective-permute-start.6 = (f32[1,4224]{1,0:T(1,128)S(1)}, f32[1,4224]{1,0:T(1,128)S(1)}, u32[]{:S(2)}, u32[]{:S(2)}) collective-permute-start(f32[1,4224]{1,0:T(1,128)S(1)} %get-tuple-element.43), channel_id=1, source_target_pairs={{0,3},{1,2},{2,1},{3,0},{4,7},{5,6},{6,5},{7,4},{8,11},{9,10},{10,... | collective-permute-start | bytes 50696 | tf_op jit(solution)/shard_map/ppermute | solution.py:338
  17.8 3.3 %collective-permute-start.7 = (f32[1,4224]{1,0:T(1,128)S(1)}, f32[1,4224]{1,0:T(1,128)S(1)}, u32[]{:S(2)}, u32[]{:S(2)}) collective-permute-start(f32[1,4224]{1,0:T(1,128)S(1)} %get-tuple-element.43), channel_id=1, source_target_pairs={{0,1},{1,0},{2,3},{3,2},{4,5},{5,4},{6,7},{7,6},{8,9},{9,8},{10,11... | collective-permute-start | bytes 50696 | tf_op jit(solution)/shard_map/ppermute | solution.py:338
  21.1 5.0 %collective-permute-start.10 = (f32[1,4224]{1,0:T(1,128)S(1)}, f32[1,4224]{1,0:T(1,128)S(1)}, u32[]{:S(2)}, u32[]{:S(2)}) collective-permute-start(f32[1,4224]{1,0:T(1,128)S(1)} %add_add_fusion.1.refs_3_), channel_id=1, source_target_pairs={{0,13},{1,12},{2,15},{3,14},{4,9},{5,8},{6,11},{7,10},{8,5},{9,4},... | collective-permute-start | bytes 50696 | tf_op jit(solution)/shard_map/ppermute | solution.py:338
  24.5 4.1 %collective-permute-start.8 = (f32[1,4224]{1,0:T(1,128)S(1)}, f32[1,4224]{1,0:T(1,128)S(1)}, u32[]{:S(2)}, u32[]{:S(2)}) collective-permute-start(f32[1,4224]{1,0:T(1,128)S(1)} %add_add_fusion.1.refs_3_), channel_id=1, source_target_pairs={{0,9},{1,8},{2,11},{3,10},{4,13},{5,12},{6,15},{7,14},{8,1},{9,0},... | collective-permute-start | bytes 50696 | tf_op jit(solution)/shard_map/ppermute | solution.py:338
  24.5 4.1 %collective-permute-start.9 = (f32[1,4224]{1,0:T(1,128)S(1)}, f32[1,4224]{1,0:T(1,128)S(1)}, u32[]{:S(2)}, u32[]{:S(2)}) collective-permute-start(f32[1,4224]{1,0:T(1,128)S(1)} %add_add_fusion.1.refs_3_), channel_id=1, source_target_pairs={{0,5},{1,4},{2,7},{3,6},{4,1},{5,0},{6,3},{7,2},{8,13},{9,12},{10,... | collective-permute-start | bytes 50696 | tf_op jit(solution)/shard_map/ppermute | solution.py:338
  29.8 3.2 %collective-permute-start.11 = (f32[8,640]{1,0:T(8,128)S(1)}, f32[8,640]{1,0:T(8,128)S(1)}, u32[]{:S(2)}, u32[]{:S(2)}) collective-permute-start(f32[8,640]{1,0:T(8,128)S(1)} %get-tuple-element.45.refs_1_), channel_id=1, source_target_pairs={{0,17},{1,16},{2,19},{3,18},{4,21},{5,20},{6,23},{7,22},{8,25},{9,... | collective-permute-start | bytes 61448 | tf_op jit(solution)/shard_map/ppermute | solution.py:354
  34.2 3.9 %collective-permute-start.12 = (f32[1,4224]{1,0:T(1,128)S(1)}, f32[1,4224]{1,0:T(1,128)S(1)}, u32[]{:S(2)}, u32[]{:S(2)}) collective-permute-start(f32[1,4224]{1,0:T(1,128)S(1)} %get-tuple-element.48), channel_id=1, source_target_pairs={{0,2},{1,3},{2,0},{3,1},{4,6},{5,7},{6,4},{7,5},{8,10},{9,11},{10,... | collective-permute-start | bytes 50696 | tf_op jit(solution)/shard_map/ppermute | solution.py:338
  34.8 3.4 %collective-permute-start.13 = (f32[1,4224]{1,0:T(1,128)S(1)}, f32[1,4224]{1,0:T(1,128)S(1)}, u32[]{:S(2)}, u32[]{:S(2)}) collective-permute-start(f32[1,4224]{1,0:T(1,128)S(1)} %get-tuple-element.48), channel_id=1, source_target_pairs={{0,3},{1,2},{2,1},{3,0},{4,7},{5,6},{6,5},{7,4},{8,11},{9,10},{10,... | collective-permute-start | bytes 50696 | tf_op jit(solution)/shard_map/ppermute | solution.py:338
  36.1 2.1 %collective-permute-start.14 = (f32[1,4224]{1,0:T(1,128)S(1)}, f32[1,4224]{1,0:T(1,128)S(1)}, u32[]{:S(2)}, u32[]{:S(2)}) collective-permute-start(f32[1,4224]{1,0:T(1,128)S(1)} %get-tuple-element.48), channel_id=1, source_target_pairs={{0,1},{1,0},{2,3},{3,2},{4,5},{5,4},{6,7},{7,6},{8,9},{9,8},{10,11... | collective-permute-start | bytes 50696 | tf_op jit(solution)/shard_map/ppermute | solution.py:338
  38.2 5.0 %collective-permute-start.15 = (f32[1,4224]{1,0:T(1,128)S(1)}, f32[1,4224]{1,0:T(1,128)S(1)}, u32[]{:S(2)}, u32[]{:S(2)}) collective-permute-start(f32[1,4224]{1,0:T(1,128)S(1)} %add_add_fusion.refs_3_), channel_id=1, source_target_pairs={{0,13},{1,12},{2,15},{3,14},{4,9},{5,8},{6,11},{7,10},{8,5},{9,4},... | collective-permute-start | bytes 50696 | tf_op jit(solution)/shard_map/ppermute | solution.py:338
  39.5 4.3 %collective-permute-start.16 = (f32[1,4224]{1,0:T(1,128)S(1)}, f32[1,4224]{1,0:T(1,128)S(1)}, u32[]{:S(2)}, u32[]{:S(2)}) collective-permute-start(f32[1,4224]{1,0:T(1,128)S(1)} %add_add_fusion.refs_3_), channel_id=1, source_target_pairs={{0,9},{1,8},{2,11},{3,10},{4,13},{5,12},{6,15},{7,14},{8,1},{9,0},... | collective-permute-start | bytes 50696 | tf_op jit(solution)/shard_map/ppermute | solution.py:338
  40.1 3.8 %collective-permute-start.17 = (f32[1,4224]{1,0:T(1,128)S(1)}, f32[1,4224]{1,0:T(1,128)S(1)}, u32[]{:S(2)}, u32[]{:S(2)}) collective-permute-start(f32[1,4224]{1,0:T(1,128)S(1)} %add_add_fusion.refs_3_), channel_id=1, source_target_pairs={{0,5},{1,4},{2,7},{3,6},{4,1},{5,0},{6,3},{7,2},{8,13},{9,12},{10,... | collective-permute-start | bytes 50696 | tf_op jit(solution)/shard_map/ppermute | solution.py:338
  42.1 3.9 %collective-permute-start.20 = (f32[16,512]{1,0:T(8,128)S(1)}, f32[16,512]{1,0:T(8,128)S(1)}, u32[]{:S(2)}, u32[]{:S(2)}) collective-permute-start(f32[16,512]{1,0:T(8,128)S(1)} %get-tuple-element.51.refs_4_), channel_id=1, source_target_pairs={{0,1},{1,0},{2,3},{3,2},{4,5},{5,4},{6,7},{7,6},{8,9},{9,8},{10,11... | collective-permute-start | bytes 98312 | tf_op jit(solution)/shard_map/ppermute | solution.py:354
  45.1 3.2 %collective-permute-start.18 = (f32[8,640]{1,0:T(8,128)S(1)}, f32[8,640]{1,0:T(8,128)S(1)}, u32[]{:S(2)}, u32[]{:S(2)}) collective-permute-start(f32[8,640]{1,0:T(8,128)S(1)} %get-tuple-element.50.refs_2_), channel_id=1, source_target_pairs={{0,16},{1,17},{2,18},{3,19},{4,20},{5,21},{6,22},{7,23},{8,24},{9,... | collective-permute-start | bytes 61448 | tf_op jit(solution)/shard_map/ppermute | solution.py:354
  46.0 2.4 %collective-permute-start.19 = (f32[8,640]{1,0:T(8,128)S(1)}, f32[8,640]{1,0:T(8,128)S(1)}, u32[]{:S(2)}, u32[]{:S(2)}) collective-permute-start(f32[8,640]{1,0:T(8,128)S(1)} %get-tuple-element.50.refs_2_), channel_id=1, source_target_pairs={{0,1},{1,0},{2,3},{3,2},{4,5},{5,4},{6,7},{7,6},{8,9},{9,8},{10,11... | collective-permute-start | bytes 61448 | tf_op jit(solution)/shard_map/ppermute | solution.py:354

commit v25 on v23

--- a/solution.py
+++ b/solution.py
@@ -98,20 +98,29 @@
     return high, (value - high.astype(f32)).astype(bf16)
 
 
-def pick(feat_ref, idx, hit_ref):
-    row_count, count = hit_ref.shape
+def place_of(idx, row_count):
     local_idx = idx - lax.axis_index("dp") * row_count
-    row = lax.broadcasted_iota(jnp.int32, (STEP, count), 0).astype(f32).astype(bf16)
     block = lax.div(local_idx, STEP)
-    place = (local_idx - block * STEP).astype(f32)
-    for begin in range(0, row_count, STEP):
-        own = jnp.where(block == begin // STEP, place, -1.0).astype(bf16)
-        hit = jnp.where(row == own, jnp.ones_like(row), jnp.zeros_like(row))
-        hit_ref[begin : begin + STEP, :] = hit
+    place = (local_idx - block * STEP).astype(f32).astype(bf16)
+    row = lax.broadcasted_iota(jnp.int32, (STEP, idx.shape[1]), 0).astype(f32).astype(bf16)
+    return block, jnp.where(row == place, jnp.ones_like(row), jnp.zeros_like(row))
+
+
+def pick(feat_ref, block, hit):
+    depth, row_count = feat_ref.shape
+    blocks = range(row_count // STEP)
+    stacked = jnp.concatenate(
+        [feat_ref[:, turn * STEP : (turn + 1) * STEP] for turn in blocks], axis=0
+    )
+    product = jnp.dot(stacked, hit, preferred_element_type=f32)
+    picked = jnp.zeros((depth, hit.shape[1]), f32)
+    for turn in blocks:
+        picked = jnp.where(block == turn, product[turn * depth : (turn + 1) * depth], picked)
+    return picked
 
 
 def pick_body(feat_hbm, idx_hbm, slots_hbm, prices_hbm, scale_hbm, *refs):
-    feat_ref, idx_ref, slots_ref, prices_ref, scale_ref, out_ref, hit_ref, sems = refs
+    feat_ref, idx_ref, slots_ref, prices_ref, scale_ref, out_ref, sems = refs
     sources = (idx_hbm, feat_hbm, slots_hbm, prices_hbm, scale_hbm)
     targets = (idx_ref, feat_ref, slots_ref, prices_ref, scale_ref)
     copies = [
@@ -121,20 +130,18 @@
     for copy in copies:
         copy.start()
     copies[0].wait()
-    pick(feat_ref, idx_ref[...], hit_ref)
+    block, hit = place_of(idx_ref[...], feat_ref.shape[1])
     copies[1].wait()
-    picked = jnp.dot(feat_ref[...], hit_ref[...], preferred_element_type=f32)
+    picked = pick(feat_ref, block, hit)
     for copy in copies[2:]:
         copy.wait()
     out_ref[...] = picked.astype(bf16)
 
 
-def pick_beside_body(feat_ref, moved_idx_ref, idx_ref, out_ref, hit_ref):
-    first = lax.axis_index("dp") == 0
-    pick(feat_ref, jnp.where(first, idx_ref[...], moved_idx_ref[...]), hit_ref)
-    out_ref[...] = jnp.dot(
-        feat_ref[...], hit_ref[...], preferred_element_type=f32
-    ).astype(bf16)
+def pick_beside_body(feat_ref, moved_idx_ref, idx_ref, out_ref):
+    idx = jnp.where(lax.axis_index("dp") == 0, idx_ref[...], moved_idx_ref[...])
+    block, hit = place_of(idx, feat_ref.shape[1])
+    out_ref[...] = pick(feat_ref, block, hit).astype(bf16)
 
 
 def columns_body(feat_ref, slots_ref, prices_ref, columns_ref, turned_ref, weight_ref):
@@ -404,10 +411,7 @@
         ),
         *inputs,
         sources=[HBM] * 5,
-        scratch_shapes=[
-            pltpu.VMEM((row_count, count), bf16),
-            pltpu.SemaphoreType.DMA((5,)),
-        ],
+        scratch_shapes=[pltpu.SemaphoreType.DMA((5,))],
     )
     if crossed:
         moved_idx = moved(center_idx, beside)
@@ -417,7 +421,6 @@
             features, moved_idx.reshape(1, count), idx,
             flops=128 * row_count * count,
             bytes_accessed=128 * row_count,
-            scratch_shapes=[pltpu.VMEM((row_count, count), bf16)],
         )
         centers = [moved(picked, outward), resident_picks]
         moved_scale = moved(center_scale, beside).reshape(1, count)

time: 48.4 us -> 48 us (level)
  Pallas kernels: 13.5 us -> 12.7 us
    pallas_call x10, Pallas kernels: 13.5 us -> 12.7 us  [call(): pl.pallas_call(body, out_shape=out_shape, in_specs=sources or [VMEM] * le...]
  transfers between devices with their start and end apart: 20 -> 20, of which waited for: 13 -> 13; matrix products, arithmetic and copies ran while one was open for 0% -> 0% of each run, Pallas kernels for 10% -> 9%
where the time goes in v25:
time: 48 us; the launch traced here: 47.8 us
  starting transfers between devices  21.1 us (44%)
  waiting for transfers between devices  13.3 us (28%)
  Pallas kernels  12.7 us (26%)
  between operations  0.72 us (2%)
    pallas_call x10, Pallas kernels, call(): pl.pallas_call(body, out_shape=out_shape, in_specs=sources or [VMEM] * le...  12.7 us
    ppermute x12, starting transfers between devices, exchange(): parts.insert(0, lax.ppermute(value, axis, pairs))  12.3 us
    ppermute x12, waiting for transfers between devices, exchange(): parts.insert(0, lax.ppermute(value, axis, pairs))  9.18 us
    ppermute x8, starting transfers between devices, moved(): return lax.ppermute(value, ('dp', 'centers'), pairs_over(target_of))  8.72 us
    ppermute x8, waiting for transfers between devices, moved(): return lax.ppermute(value, ('dp', 'centers'), pairs_over(target_of))  4.12 us
  transfers between devices with their start and end apart: 20, of which 13 were waited for; matrix products, arithmetic and copies ran while one was open for 0% of the time, Pallas kernels for 9%

profile of v25, /device:TPU:0, one launch (start us, length us, event | category | flops | bytes accessed | tf_op | source)
XLA Modules:
  0.0 47.8 jit_solution(6256151475123504870)
XLA Ops:
  0.6 1.6 %shard_map.68 = (bf16[64,4096]{1,0:T(8,128)(2,1)S(1)}, s32[1,512]{1,0:T(1,128)S(1)}, s32[1,4096]{1,0:T(1,128)S(1)}, f32[1,4096]{1,0:T(1,128)S(1)}, f32[1,512]{1,0:T(1,128)S(1)}, /*index=5*/bf16[64,512]{1,0:T(8,128)(2,1)S(1)}) custom-call(bf16[64,4096]{1,0:T(8,128)(2,1)} %feat_hbm.1, s32[1,512]{1,0:T(1,128)} %bitcast.10, s32[1,4096]{1,0:T(1,128)} %bitcast.8, ...), custom_call_target="tpu_custom_call" | custom-call | tf_op jit(solution)/shard_map/pallas_call | solution.py:313
  2.2 2.4 %collective-permute-start.1 = (bf16[64,512]{1,0:T(8,128)(2,1)S(1)}, bf16[64,512]{1,0:T(8,128)(2,1)S(1)}, u32[]{:S(2)}, u32[]{:S(2)}) collective-permute-start(bf16[64,512]{1,0:T(8,128)(2,1)S(1)} %get-tuple-element.31), channel_id=1, source_target_pairs={{0,17},{1,16},{2,19},{3,18},{4,21},{5,20},{6,23},{7,22},{8,25},{9,... | collective-permute-start | bytes 196616 | tf_op jit(solution)/shard_map/ppermute | solution.py:354
  4.6 0.7 %collective-permute-start.2 = (s32[512]{0:T(512)}, s32[512]{0:T(512)S(1)}, u32[]{:S(2)}, u32[]{:S(2)}) collective-permute-start(s32[512]{0:T(512)} %param.8), channel_id=1, source_target_pairs={{0,1},{1,0},{2,3},{3,2},{4,5},{5,4},{6,7},{7,6},{8,9},{9,8},{10,11... | collective-permute-start | bytes 6152 | tf_op jit(solution)/shard_map/ppermute | solution.py:354
  5.3 0.0 collective-permute-start
  5.3 0.7 %shard_map.69 = (bf16[256,4096]{1,0:T(8,128)(2,1)S(1)}, bf16[4096,256]{1,0:T(8,128)(2,1)S(1)}, bf16[16,4096]{1,0:T(8,128)(2,1)S(1)}) custom-call(bf16[64,4096]{1,0:T(8,128)(2,1)S(1)} %get-tuple-element.25.feat_ref, s32[1,4096]{1,0:T(1,128)S(1)} %get-tuple-element.26.slots_ref.refs_3_.refs_4_, f32[1,4096]{1,0:T(1,128)S(1)} %get-tuple-element.27.prices_ref), custom_call_target="tpu_custom_call" | custom-call | flops 4096000 | bytes 4194304 | tf_op jit(solution)/shard_map/pallas_call | solution.py:313
  6.0 0.4 collective-permute-done.2
  6.3 0.5 shard_map.70.refs_1_
  6.8 0.0 collective-permute-done
  6.8 0.6 %collective-permute-done.1.refs_0_ = bf16[64,512]{1,0:T(8,128)(2,1)S(1)} collective-permute-done((bf16[64,512]{1,0:T(8,128)(2,1)S(1)}, bf16[64,512]{1,0:T(8,128)(2,1)S(1)}, u32[]{:S(2)}, u32[]{:S(2)}) %collective-permute-start.1) | collective-permute-done | bytes 65568 | tf_op jit(solution)/shard_map/ppermute | solution.py:354
  7.4 2.5 %shard_map.71 = (bf16[8192,512]{1,0:T(8,128)(2,1)S(1)}, bf16[256,512]{1,0:T(8,128)(2,1)S(1)}, f32[1,512]{1,0:T(1,128)S(1)}, f32[8,512]{1,0:T(8,128)S(1)}) custom-call(bf16[4096,256]{1,0:T(8,128)(2,1)S(1)} %get-tuple-element.28.turned_ref, bf16[16,4096]{1,0:T(8,128)(2,1)S(1)} %get-tuple-element.29.weight_ref, f32[1,512]{1,0:T(1,128)S(1)} %bitcast.6, ...), custom_call_target="tpu_custom_call" | custom-call | flops 134217728 | bytes 8388608 | tf_op jit(solution)/shard_map/pallas_call | solution.py:313
  10.0 1.9 %collective-permute-start.3 = (f32[8,512]{1,0:T(8,128)S(1)}, f32[8,512]{1,0:T(8,128)S(1)}, u32[]{:S(2)}, u32[]{:S(2)}) collective-permute-start(f32[8,512]{1,0:T(8,128)S(1)} %get-tuple-element.33.refs_1_), channel_id=1, source_target_pairs={{0,17},{1,16},{2,19},{3,18},{4,21},{5,20},{6,23},{7,22},{8,25},{9,... | collective-permute-start | bytes 49160 | tf_op jit(solution)/shard_map/ppermute | solution.py:354
  11.9 1.9 %shard_map.72.refs_4_ = bf16[1024,4096]{1,0:T(8,128)(2,1)S(1)} custom-call(bf16[256,4096]{1,0:T(8,128)(2,1)S(1)} %get-tuple-element.35.columns_ref, bf16[256,512]{1,0:T(8,128)(2,1)S(1)} %get-tuple-element.36.center_ref), custom_call_target="tpu_custom_call" | custom-call | flops 134217728 | bytes 8388608 | tf_op jit(solution)/shard_map/pallas_call | solution.py:313
  13.8 0.0 collective-permute-done.3.refs_0_
  13.8 1.2 %shard_map.73 = (f32[8,512]{1,0:T(8,128)S(1)}, f32[1,4224]{1,0:T(1,128)S(1)}) custom-call(f32[8,512]{1,0:T(8,128)S(1)} %collective-permute-done.3.refs_0_, f32[8,512]{1,0:T(8,128)S(1)} %get-tuple-element.33.refs_1_, f32[1,512]{1,0:T(1,128)S(1)} %get-tuple-element.34.refs_2_, s32[1,4096]{1,0:T(1,128)S(1)} %get-tuple-element.26.slots_ref.refs_3_.refs_4_, ...), custom_call_target="tpu_custom_call" | custom-call | tf_op jit(solution)/shard_map/pallas_call | solution.py:313
  15.0 1.6 %collective-permute-start.4 = (f32[1,4224]{1,0:T(1,128)S(1)}, f32[1,4224]{1,0:T(1,128)S(1)}, u32[]{:S(2)}, u32[]{:S(2)}) collective-permute-start(f32[1,4224]{1,0:T(1,128)S(1)} %get-tuple-element.37), channel_id=1, source_target_pairs={{0,2},{1,3},{2,0},{3,1},{4,6},{5,7},{6,4},{7,5},{8,10},{9,11},{10,... | collective-permute-start | bytes 50696 | tf_op jit(solution)/shard_map/ppermute | solution.py:338
  16.6 0.3 collective-permute-start.5
  16.9 0.4 collective-permute-start.6
  17.2 1.6 %collective-permute-done.4 = f32[1,4224]{1,0:T(1,128)S(1)} collective-permute-done((f32[1,4224]{1,0:T(1,128)S(1)}, f32[1,4224]{1,0:T(1,128)S(1)}, u32[]{:S(2)}, u32[]{:S(2)}) %collective-permute-start.4) | collective-permute-done | bytes 16928 | tf_op jit(solution)/shard_map/ppermute | solution.py:338
  18.8 1.0 %collective-permute-done.5 = f32[1,4224]{1,0:T(1,128)S(1)} collective-permute-done((f32[1,4224]{1,0:T(1,128)S(1)}, f32[1,4224]{1,0:T(1,128)S(1)}, u32[]{:S(2)}, u32[]{:S(2)}) %collective-permute-start.5) | collective-permute-done | bytes 16928 | tf_op jit(solution)/shard_map/ppermute | solution.py:338
  19.8 0.0 collective-permute-done.6
  19.8 3.4 %collective-permute-start.7 = (f32[1,4224]{1,0:T(1,128)S(1)}, f32[1,4224]{1,0:T(1,128)S(1)}, u32[]{:S(2)}, u32[]{:S(2)}) collective-permute-start(f32[1,4224]{1,0:T(1,128)S(1)} %add_add_fusion.1.refs_3_), channel_id=1, source_target_pairs={{0,13},{1,12},{2,15},{3,14},{4,9},{5,8},{6,11},{7,10},{8,5},{9,4},... | collective-permute-start | bytes 50696 | tf_op jit(solution)/shard_map/ppermute | solution.py:338
  23.3 0.0 collective-permute-start.8
  23.3 0.6 %collective-permute-start.9 = (f32[1,4224]{1,0:T(1,128)S(1)}, f32[1,4224]{1,0:T(1,128)S(1)}, u32[]{:S(2)}, u32[]{:S(2)}) collective-permute-start(f32[1,4224]{1,0:T(1,128)S(1)} %add_add_fusion.1.refs_3_), channel_id=1, source_target_pairs={{0,5},{1,4},{2,7},{3,6},{4,1},{5,0},{6,3},{7,2},{8,13},{9,12},{10,... | collective-permute-start | bytes 50696 | tf_op jit(solution)/shard_map/ppermute | solution.py:338
  23.9 1.0 %collective-permute-done.7.refs_0_ = f32[1,4224]{1,0:T(1,128)S(1)} collective-permute-done((f32[1,4224]{1,0:T(1,128)S(1)}, f32[1,4224]{1,0:T(1,128)S(1)}, u32[]{:S(2)}, u32[]{:S(2)}) %collective-permute-start.7) | collective-permute-done | bytes 16928 | tf_op jit(solution)/shard_map/ppermute | solution.py:338
  24.9 2.5 %collective-permute-done.8.refs_1_ = f32[1,4224]{1,0:T(1,128)S(1)} collective-permute-done((f32[1,4224]{1,0:T(1,128)S(1)}, f32[1,4224]{1,0:T(1,128)S(1)}, u32[]{:S(2)}, u32[]{:S(2)}) %collective-permute-start.8) | collective-permute-done | bytes 16928 | tf_op jit(solution)/shard_map/ppermute | solution.py:338
  27.3 0.0 collective-permute-done.9.refs_2_
  27.3 1.2 %shard_map.74 = (f32[1,4224]{1,0:T(1,128)S(1)}, f32[8,128]{1,0:T(8,128)S(1)}, f32[8,640]{1,0:T(8,128)S(1)}) custom-call(f32[1,4224]{1,0:T(1,128)S(1)} %collective-permute-done.7.refs_0_, f32[1,4224]{1,0:T(1,128)S(1)} %collective-permute-done.8.refs_1_, f32[1,4224]{1,0:T(1,128)S(1)} %collective-permute-done.9.refs_2_, f32[1,4224]{1,0:T(1,128)S(1)} %add_add_fusion.1.refs_3_, ...), custom_call_target="tpu_custom_call" | custom-call | tf_op jit(solution)/shard_map/pallas_call | solution.py:313
  28.5 1.7 %collective-permute-start.10 = (f32[8,640]{1,0:T(8,128)S(1)}, f32[8,640]{1,0:T(8,128)S(1)}, u32[]{:S(2)}, u32[]{:S(2)}) collective-permute-start(f32[8,640]{1,0:T(8,128)S(1)} %get-tuple-element.39.refs_1_), channel_id=1, source_target_pairs={{0,17},{1,16},{2,19},{3,18},{4,21},{5,20},{6,23},{7,22},{8,25},{9,... | collective-permute-start | bytes 61448 | tf_op jit(solution)/shard_map/ppermute | solution.py:354
  30.2 1.5 %collective-permute-done.10.refs_0_ = f32[8,640]{1,0:T(8,128)S(1)} collective-permute-done((f32[8,640]{1,0:T(8,128)S(1)}, f32[8,640]{1,0:T(8,128)S(1)}, u32[]{:S(2)}, u32[]{:S(2)}) %collective-permute-start.10) | collective-permute-done | bytes 20512 | tf_op jit(solution)/shard_map/ppermute | solution.py:354
  31.8 1.2 %shard_map.75 = (f32[16,512]{1,0:T(8,128)S(1)}, f32[8,128]{1,0:T(8,128)S(1)}, f32[1,4224]{1,0:T(1,128)S(1)}) custom-call(f32[8,640]{1,0:T(8,128)S(1)} %collective-permute-done.10.refs_0_, f32[8,640]{1,0:T(8,128)S(1)} %get-tuple-element.39.refs_1_, f32[1,512]{1,0:T(1,128)S(1)} %get-tuple-element.34.refs_2_, ...), custom_call_target="tpu_custom_call" | custom-call | tf_op jit(solution)/shard_map/pallas_call | solution.py:313
  33.0 0.7 %collective-permute-start.11 = (f32[1,4224]{1,0:T(1,128)S(1)}, f32[1,4224]{1,0:T(1,128)S(1)}, u32[]{:S(2)}, u32[]{:S(2)}) collective-permute-start(f32[1,4224]{1,0:T(1,128)S(1)} %get-tuple-element.42), channel_id=1, source_target_pairs={{0,2},{1,3},{2,0},{3,1},{4,6},{5,7},{6,4},{7,5},{8,10},{9,11},{10,... | collective-permute-start | bytes 50696 | tf_op jit(solution)/shard_map/ppermute | solution.py:338
  33.7 1.1 %collective-permute-start.12 = (f32[1,4224]{1,0:T(1,128)S(1)}, f32[1,4224]{1,0:T(1,128)S(1)}, u32[]{:S(2)}, u32[]{:S(2)}) collective-permute-start(f32[1,4224]{1,0:T(1,128)S(1)} %get-tuple-element.42), channel_id=1, source_target_pairs={{0,3},{1,2},{2,1},{3,0},{4,7},{5,6},{6,5},{7,4},{8,11},{9,10},{10,... | collective-permute-start | bytes 50696 | tf_op jit(solution)/shard_map/ppermute | solution.py:338
  34.7 0.4 collective-permute-start.13
  35.2 1.7 %collective-permute-done.11 = f32[1,4224]{1,0:T(1,128)S(1)} collective-permute-done((f32[1,4224]{1,0:T(1,128)S(1)}, f32[1,4224]{1,0:T(1,128)S(1)}, u32[]{:S(2)}, u32[]{:S(2)}) %collective-permute-start.11) | collective-permute-done | bytes 16928 | tf_op jit(solution)/shard_map/ppermute | solution.py:338
  36.9 0.1 collective-permute-done.12
  37.0 0.0 collective-permute-done.13
  37.0 1.4 %collective-permute-start.14 = (f32[1,4224]{1,0:T(1,128)S(1)}, f32[1,4224]{1,0:T(1,128)S(1)}, u32[]{:S(2)}, u32[]{:S(2)}) collective-permute-start(f32[1,4224]{1,0:T(1,128)S(1)} %add_add_fusion.refs_3_), channel_id=1, source_target_pairs={{0,13},{1,12},{2,15},{3,14},{4,9},{5,8},{6,11},{7,10},{8,5},{9,4},... | collective-permute-start | bytes 50696 | tf_op jit(solution)/shard_map/ppermute | solution.py:338
  38.4 0.6 %collective-permute-start.15 = (f32[1,4224]{1,0:T(1,128)S(1)}, f32[1,4224]{1,0:T(1,128)S(1)}, u32[]{:S(2)}, u32[]{:S(2)}) collective-permute-start(f32[1,4224]{1,0:T(1,128)S(1)} %add_add_fusion.refs_3_), channel_id=1, source_target_pairs={{0,9},{1,8},{2,11},{3,10},{4,13},{5,12},{6,15},{7,14},{8,1},{9,0},... | collective-permute-start | bytes 50696 | tf_op jit(solution)/shard_map/ppermute | solution.py:338
  39.0 1.9 %collective-permute-start.16 = (f32[1,4224]{1,0:T(1,128)S(1)}, f32[1,4224]{1,0:T(1,128)S(1)}, u32[]{:S(2)}, u32[]{:S(2)}) collective-permute-start(f32[1,4224]{1,0:T(1,128)S(1)} %add_add_fusion.refs_3_), channel_id=1, source_target_pairs={{0,5},{1,4},{2,7},{3,6},{4,1},{5,0},{6,3},{7,2},{8,13},{9,12},{10,... | collective-permute-start | bytes 50696 | tf_op jit(solution)/shard_map/ppermute | solution.py:338
  40.9 0.4 collective-permute-start.19
  41.3 0.7 %collective-permute-done.14.refs_0_ = f32[1,4224]{1,0:T(1,128)S(1)} collective-permute-done((f32[1,4224]{1,0:T(1,128)S(1)}, f32[1,4224]{1,0:T(1,128)S(1)}, u32[]{:S(2)}, u32[]{:S(2)}) %collective-permute-start.14) | collective-permute-done | bytes 16928 | tf_op jit(solution)/shard_map/ppermute | solution.py:338
  42.0 0.6 %collective-permute-done.15.refs_1_ = f32[1,4224]{1,0:T(1,128)S(1)} collective-permute-done((f32[1,4224]{1,0:T(1,128)S(1)}, f32[1,4224]{1,0:T(1,128)S(1)}, u32[]{:S(2)}, u32[]{:S(2)}) %collective-permute-start.15) | collective-permute-done | bytes 16928 | tf_op jit(solution)/shard_map/ppermute | solution.py:338
  42.6 0.1 collective-permute-done.16.refs_2_
  42.7 1.3 %shard_map.76 = (f32[8,256]{1,0:T(8,128)S(1)}, f32[8,640]{1,0:T(8,128)S(1)}) custom-call(f32[1,4224]{1,0:T(1,128)S(1)} %collective-permute-done.14.refs_0_, f32[1,4224]{1,0:T(1,128)S(1)} %collective-permute-done.15.refs_1_, f32[1,4224]{1,0:T(1,128)S(1)} %collective-permute-done.16.refs_2_, f32[1,4224]{1,0:T(1,128)S(1)} %add_add_fusion.refs_3_, ...), custom_call_target="tpu_custom_call" | custom-call | tf_op jit(solution)/shard_map/pallas_call | solution.py:313
  43.9 1.6 %collective-permute-start.17 = (f32[8,640]{1,0:T(8,128)S(1)}, f32[8,640]{1,0:T(8,128)S(1)}, u32[]{:S(2)}, u32[]{:S(2)}) collective-permute-start(f32[8,640]{1,0:T(8,128)S(1)} %get-tuple-element.44.refs_2_), channel_id=1, source_target_pairs={{0,16},{1,17},{2,18},{3,19},{4,20},{5,21},{6,22},{7,23},{8,24},{9,... | collective-permute-start | bytes 61448 | tf_op jit(solution)/shard_map/ppermute | solution.py:354
  45.5 0.0 collective-permute-start.18
  45.5 0.0 collective-permute-done.19.refs_3_
  45.5 1.6 %collective-permute-done.17.refs_0_ = f32[8,640]{1,0:T(8,128)S(1)} collective-permute-done((f32[8,640]{1,0:T(8,128)S(1)}, f32[8,640]{1,0:T(8,128)S(1)}, u32[]{:S(2)}, u32[]{:S(2)}) %collective-permute-start.17) | collective-permute-done | bytes 20512 | tf_op jit(solution)/shard_map/ppermute | solution.py:354
  47.2 0.0 collective-permute-done.18.refs_1_
  47.2 0.6 %shard_map.77 = (f32[8,512]{1,0:T(8,128)}, f32[8,512]{1,0:T(8,128)}) custom-call(f32[8,640]{1,0:T(8,128)S(1)} %collective-permute-done.17.refs_0_, f32[8,640]{1,0:T(8,128)S(1)} %collective-permute-done.18.refs_1_, f32[8,640]{1,0:T(8,128)S(1)} %get-tuple-element.44.refs_2_, f32[16,512]{1,0:T(8,128)S(1)} %collective-permute-done.19.refs_3_, ...), custom_call_target="tpu_custom_call" | custom-call | tf_op jit(solution)/shard_map/pallas_call | solution.py:313
  (2 shorter events, 0.1 us)
Async XLA Ops:
  2.2 5.2 %collective-permute-start.1 = (bf16[64,512]{1,0:T(8,128)(2,1)S(1)}, bf16[64,512]{1,0:T(8,128)(2,1)S(1)}, u32[]{:S(2)}, u32[]{:S(2)}) collective-permute-start(bf16[64,512]{1,0:T(8,128)(2,1)S(1)} %get-tuple-element.31), channel_id=1, source_target_pairs={{0,17},{1,16},{2,19},{3,18},{4,21},{5,20},{6,23},{7,22},{8,25},{9,... | collective-permute-start | bytes 196616 | tf_op jit(solution)/shard_map/ppermute | solution.py:354
  4.6 1.7 %collective-permute-start.2 = (s32[512]{0:T(512)}, s32[512]{0:T(512)S(1)}, u32[]{:S(2)}, u32[]{:S(2)}) collective-permute-start(s32[512]{0:T(512)} %param.8), channel_id=1, source_target_pairs={{0,1},{1,0},{2,3},{3,2},{4,5},{5,4},{6,7},{7,6},{8,9},{9,8},{10,11... | collective-permute-start | bytes 6152 | tf_op jit(solution)/shard_map/ppermute | solution.py:354
  5.3 1.5 %collective-permute-start = (f32[512]{0:T(512)}, f32[512]{0:T(512)S(1)}, u32[]{:S(2)}, u32[]{:S(2)}) collective-permute-start(f32[512]{0:T(512)} %param.9), channel_id=1, source_target_pairs={{0,1},{1,0},{2,3},{3,2},{4,5},{5,4},{6,7},{7,6},{8,9},{9,8},{10,11... | collective-permute-start | bytes 6152 | tf_op jit(solution)/shard_map/ppermute | solution.py:354
  10.0 3.8 %collective-permute-start.3 = (f32[8,512]{1,0:T(8,128)S(1)}, f32[8,512]{1,0:T(8,128)S(1)}, u32[]{:S(2)}, u32[]{:S(2)}) collective-permute-start(f32[8,512]{1,0:T(8,128)S(1)} %get-tuple-element.33.refs_1_), channel_id=1, source_target_pairs={{0,17},{1,16},{2,19},{3,18},{4,21},{5,20},{6,23},{7,22},{8,25},{9,... | collective-permute-start | bytes 49160 | tf_op jit(solution)/shard_map/ppermute | solution.py:354
  15.0 3.8 %collective-permute-start.4 = (f32[1,4224]{1,0:T(1,128)S(1)}, f32[1,4224]{1,0:T(1,128)S(1)}, u32[]{:S(2)}, u32[]{:S(2)}) collective-permute-start(f32[1,4224]{1,0:T(1,128)S(1)} %get-tuple-element.37), channel_id=1, source_target_pairs={{0,2},{1,3},{2,0},{3,1},{4,6},{5,7},{6,4},{7,5},{8,10},{9,11},{10,... | collective-permute-start | bytes 50696 | tf_op jit(solution)/shard_map/ppermute | solution.py:338
  16.6 3.2 %collective-permute-start.5 = (f32[1,4224]{1,0:T(1,128)S(1)}, f32[1,4224]{1,0:T(1,128)S(1)}, u32[]{:S(2)}, u32[]{:S(2)}) collective-permute-start(f32[1,4224]{1,0:T(1,128)S(1)} %get-tuple-element.37), channel_id=1, source_target_pairs={{0,3},{1,2},{2,1},{3,0},{4,7},{5,6},{6,5},{7,4},{8,11},{9,10},{10,... | collective-permute-start | bytes 50696 | tf_op jit(solution)/shard_map/ppermute | solution.py:338
  16.9 2.9 %collective-permute-start.6 = (f32[1,4224]{1,0:T(1,128)S(1)}, f32[1,4224]{1,0:T(1,128)S(1)}, u32[]{:S(2)}, u32[]{:S(2)}) collective-permute-start(f32[1,4224]{1,0:T(1,128)S(1)} %get-tuple-element.37), channel_id=1, source_target_pairs={{0,1},{1,0},{2,3},{3,2},{4,5},{5,4},{6,7},{7,6},{8,9},{9,8},{10,11... | collective-permute-start | bytes 50696 | tf_op jit(solution)/shard_map/ppermute | solution.py:338
  19.8 5.0 %collective-permute-start.7 = (f32[1,4224]{1,0:T(1,128)S(1)}, f32[1,4224]{1,0:T(1,128)S(1)}, u32[]{:S(2)}, u32[]{:S(2)}) collective-permute-start(f32[1,4224]{1,0:T(1,128)S(1)} %add_add_fusion.1.refs_3_), channel_id=1, source_target_pairs={{0,13},{1,12},{2,15},{3,14},{4,9},{5,8},{6,11},{7,10},{8,5},{9,4},... | collective-permute-start | bytes 50696 | tf_op jit(solution)/shard_map/ppermute | solution.py:338
  23.3 4.1 %collective-permute-start.8 = (f32[1,4224]{1,0:T(1,128)S(1)}, f32[1,4224]{1,0:T(1,128)S(1)}, u32[]{:S(2)}, u32[]{:S(2)}) collective-permute-start(f32[1,4224]{1,0:T(1,128)S(1)} %add_add_fusion.1.refs_3_), channel_id=1, source_target_pairs={{0,9},{1,8},{2,11},{3,10},{4,13},{5,12},{6,15},{7,14},{8,1},{9,0},... | collective-permute-start | bytes 50696 | tf_op jit(solution)/shard_map/ppermute | solution.py:338
  23.3 4.1 %collective-permute-start.9 = (f32[1,4224]{1,0:T(1,128)S(1)}, f32[1,4224]{1,0:T(1,128)S(1)}, u32[]{:S(2)}, u32[]{:S(2)}) collective-permute-start(f32[1,4224]{1,0:T(1,128)S(1)} %add_add_fusion.1.refs_3_), channel_id=1, source_target_pairs={{0,5},{1,4},{2,7},{3,6},{4,1},{5,0},{6,3},{7,2},{8,13},{9,12},{10,... | collective-permute-start | bytes 50696 | tf_op jit(solution)/shard_map/ppermute | solution.py:338
  28.5 3.2 %collective-permute-start.10 = (f32[8,640]{1,0:T(8,128)S(1)}, f32[8,640]{1,0:T(8,128)S(1)}, u32[]{:S(2)}, u32[]{:S(2)}) collective-permute-start(f32[8,640]{1,0:T(8,128)S(1)} %get-tuple-element.39.refs_1_), channel_id=1, source_target_pairs={{0,17},{1,16},{2,19},{3,18},{4,21},{5,20},{6,23},{7,22},{8,25},{9,... | collective-permute-start | bytes 61448 | tf_op jit(solution)/shard_map/ppermute | solution.py:354
  33.0 3.9 %collective-permute-start.11 = (f32[1,4224]{1,0:T(1,128)S(1)}, f32[1,4224]{1,0:T(1,128)S(1)}, u32[]{:S(2)}, u32[]{:S(2)}) collective-permute-start(f32[1,4224]{1,0:T(1,128)S(1)} %get-tuple-element.42), channel_id=1, source_target_pairs={{0,2},{1,3},{2,0},{3,1},{4,6},{5,7},{6,4},{7,5},{8,10},{9,11},{10,... | collective-permute-start | bytes 50696 | tf_op jit(solution)/shard_map/ppermute | solution.py:338
  33.7 3.3 %collective-permute-start.12 = (f32[1,4224]{1,0:T(1,128)S(1)}, f32[1,4224]{1,0:T(1,128)S(1)}, u32[]{:S(2)}, u32[]{:S(2)}) collective-permute-start(f32[1,4224]{1,0:T(1,128)S(1)} %get-tuple-element.42), channel_id=1, source_target_pairs={{0,3},{1,2},{2,1},{3,0},{4,7},{5,6},{6,5},{7,4},{8,11},{9,10},{10,... | collective-permute-start | bytes 50696 | tf_op jit(solution)/shard_map/ppermute | solution.py:338
  34.7 2.2 %collective-permute-start.13 = (f32[1,4224]{1,0:T(1,128)S(1)}, f32[1,4224]{1,0:T(1,128)S(1)}, u32[]{:S(2)}, u32[]{:S(2)}) collective-permute-start(f32[1,4224]{1,0:T(1,128)S(1)} %get-tuple-element.42), channel_id=1, source_target_pairs={{0,1},{1,0},{2,3},{3,2},{4,5},{5,4},{6,7},{7,6},{8,9},{9,8},{10,11... | collective-permute-start | bytes 50696 | tf_op jit(solution)/shard_map/ppermute | solution.py:338
  37.0 5.0 %collective-permute-start.14 = (f32[1,4224]{1,0:T(1,128)S(1)}, f32[1,4224]{1,0:T(1,128)S(1)}, u32[]{:S(2)}, u32[]{:S(2)}) collective-permute-start(f32[1,4224]{1,0:T(1,128)S(1)} %add_add_fusion.refs_3_), channel_id=1, source_target_pairs={{0,13},{1,12},{2,15},{3,14},{4,9},{5,8},{6,11},{7,10},{8,5},{9,4},... | collective-permute-start | bytes 50696 | tf_op jit(solution)/shard_map/ppermute | solution.py:338
  38.4 4.2 %collective-permute-start.15 = (f32[1,4224]{1,0:T(1,128)S(1)}, f32[1,4224]{1,0:T(1,128)S(1)}, u32[]{:S(2)}, u32[]{:S(2)}) collective-permute-start(f32[1,4224]{1,0:T(1,128)S(1)} %add_add_fusion.refs_3_), channel_id=1, source_target_pairs={{0,9},{1,8},{2,11},{3,10},{4,13},{5,12},{6,15},{7,14},{8,1},{9,0},... | collective-permute-start | bytes 50696 | tf_op jit(solution)/shard_map/ppermute | solution.py:338
  39.0 3.7 %collective-permute-start.16 = (f32[1,4224]{1,0:T(1,128)S(1)}, f32[1,4224]{1,0:T(1,128)S(1)}, u32[]{:S(2)}, u32[]{:S(2)}) collective-permute-start(f32[1,4224]{1,0:T(1,128)S(1)} %add_add_fusion.refs_3_), channel_id=1, source_target_pairs={{0,5},{1,4},{2,7},{3,6},{4,1},{5,0},{6,3},{7,2},{8,13},{9,12},{10,... | collective-permute-start | bytes 50696 | tf_op jit(solution)/shard_map/ppermute | solution.py:338
  40.9 4.6 %collective-permute-start.19 = (f32[16,512]{1,0:T(8,128)S(1)}, f32[16,512]{1,0:T(8,128)S(1)}, u32[]{:S(2)}, u32[]{:S(2)}) collective-permute-start(f32[16,512]{1,0:T(8,128)S(1)} %get-tuple-element.45.refs_4_), channel_id=1, source_target_pairs={{0,1},{1,0},{2,3},{3,2},{4,5},{5,4},{6,7},{7,6},{8,9},{9,8},{10,11... | collective-permute-start | bytes 98312 | tf_op jit(solution)/shard_map/ppermute | solution.py:354
  43.9 3.2 %collective-permute-start.17 = (f32[8,640]{1,0:T(8,128)S(1)}, f32[8,640]{1,0:T(8,128)S(1)}, u32[]{:S(2)}, u32[]{:S(2)}) collective-permute-start(f32[8,640]{1,0:T(8,128)S(1)} %get-tuple-element.44.refs_2_), channel_id=1, source_target_pairs={{0,16},{1,17},{2,18},{3,19},{4,20},{5,21},{6,22},{7,23},{8,24},{9,... | collective-permute-start | bytes 61448 | tf_op jit(solution)/shard_map/ppermute | solution.py:354
  45.5 1.6 %collective-permute-start.18 = (f32[8,640]{1,0:T(8,128)S(1)}, f32[8,640]{1,0:T(8,128)S(1)}, u32[]{:S(2)}, u32[]{:S(2)}) collective-permute-start(f32[8,640]{1,0:T(8,128)S(1)} %get-tuple-element.44.refs_2_), channel_id=1, source_target_pairs={{0,1},{1,0},{2,3},{3,2},{4,5},{5,4},{6,7},{7,6},{8,9},{9,8},{10,11... | collective-permute-start | bytes 61448 | tf_op jit(solution)/shard_map/ppermute | solution.py:354

commit v26 on v25

--- a/solution.py
+++ b/solution.py
@@ -106,23 +106,28 @@
     return block, jnp.where(row == place, jnp.ones_like(row), jnp.zeros_like(row))
 
 
-def pick(feat_ref, block, hit):
-    depth, row_count = feat_ref.shape
-    blocks = range(row_count // STEP)
+def pick(feat_ref, block, hit, picked, blocks):
+    depth = feat_ref.shape[0]
     stacked = jnp.concatenate(
         [feat_ref[:, turn * STEP : (turn + 1) * STEP] for turn in blocks], axis=0
     )
     product = jnp.dot(stacked, hit, preferred_element_type=f32)
-    picked = jnp.zeros((depth, hit.shape[1]), f32)
-    for turn in blocks:
-        picked = jnp.where(block == turn, product[turn * depth : (turn + 1) * depth], picked)
+    for step, turn in enumerate(blocks):
+        picked = jnp.where(block == turn, product[step * depth : (step + 1) * depth], picked)
     return picked
 
 
 def pick_body(feat_hbm, idx_hbm, slots_hbm, prices_hbm, scale_hbm, *refs):
     feat_ref, idx_ref, slots_ref, prices_ref, scale_ref, out_ref, sems = refs
-    sources = (idx_hbm, feat_hbm, slots_hbm, prices_hbm, scale_hbm)
-    targets = (idx_ref, feat_ref, slots_ref, prices_ref, scale_ref)
+    blocks = feat_ref.shape[1] // STEP
+    left = pl.ds(0, blocks // 2 * STEP)
+    right = pl.ds(blocks // 2 * STEP, (blocks - blocks // 2) * STEP)
+    sources = (
+        idx_hbm, feat_hbm.at[:, left], feat_hbm.at[:, right], slots_hbm, prices_hbm, scale_hbm
+    )
+    targets = (
+        idx_ref, feat_ref.at[:, left], feat_ref.at[:, right], slots_ref, prices_ref, scale_ref
+    )
     copies = [
         pltpu.make_async_copy(source, target, sems.at[place])
         for place, (source, target) in enumerate(zip(sources, targets))
@@ -131,9 +136,12 @@
         copy.start()
     copies[0].wait()
     block, hit = place_of(idx_ref[...], feat_ref.shape[1])
+    picked = jnp.zeros(out_ref.shape, f32)
     copies[1].wait()
-    picked = pick(feat_ref, block, hit)
-    for copy in copies[2:]:
+    picked = pick(feat_ref, block, hit, picked, range(blocks // 2))
+    copies[2].wait()
+    picked = pick(feat_ref, block, hit, picked, range(blocks // 2, blocks))
+    for copy in copies[3:]:
         copy.wait()
     out_ref[...] = picked.astype(bf16)
 
@@ -141,7 +149,9 @@
 def pick_beside_body(feat_ref, moved_idx_ref, idx_ref, out_ref):
     idx = jnp.where(lax.axis_index("dp") == 0, idx_ref[...], moved_idx_ref[...])
     block, hit = place_of(idx, feat_ref.shape[1])
-    out_ref[...] = pick(feat_ref, block, hit).astype(bf16)
+    picked = jnp.zeros(out_ref.shape, f32)
+    blocks = range(feat_ref.shape[1] // STEP)
+    out_ref[...] = pick(feat_ref, block, hit, picked, blocks).astype(bf16)
 
 
 def columns_body(feat_ref, slots_ref, prices_ref, columns_ref, turned_ref, weight_ref):
@@ -411,7 +421,7 @@
         ),
         *inputs,
         sources=[HBM] * 5,
-        scratch_shapes=[pltpu.SemaphoreType.DMA((5,))],
+        scratch_shapes=[pltpu.SemaphoreType.DMA((6,))],
     )
     if crossed:
         moved_idx = moved(center_idx, beside)

time: 48 us -> 48 us (level)
  no operation moved by 1% of the time
where the time goes in v26:
time: 48 us; the launch traced here: 47.9 us
  starting transfers between devices  21.1 us (44%)
  waiting for transfers between devices  13.3 us (28%)
  Pallas kernels  12.7 us (26%)
  between operations  0.72 us (2%)
    pallas_call x10, Pallas kernels, call(): pl.pallas_call(body, out_shape=out_shape, in_specs=sources or [VMEM] * le...  12.7 us
    ppermute x12, starting transfers between devices, exchange(): parts.insert(0, lax.ppermute(value, axis, pairs))  12.4 us
    ppermute x12, waiting for transfers between devices, exchange(): parts.insert(0, lax.ppermute(value, axis, pairs))  9.2 us
    ppermute x8, starting transfers between devices, moved(): return lax.ppermute(value, ('dp', 'centers'), pairs_over(target_of))  8.69 us
    ppermute x8, waiting for transfers between devices, moved(): return lax.ppermute(value, ('dp', 'centers'), pairs_over(target_of))  4.1 us
  transfers between devices with their start and end apart: 20, of which 13 were waited for; matrix products, arithmetic and copies ran while one was open for 0% of the time, Pallas kernels for 9%

profile of v26, /device:TPU:0, one launch (start us, length us, event | category | flops | bytes accessed | tf_op | source)
XLA Modules:
  0.0 47.9 jit_solution(6401757362710958755)
XLA Ops:
  0.6 1.6 %shard_map.68 = (bf16[64,4096]{1,0:T(8,128)(2,1)S(1)}, s32[1,512]{1,0:T(1,128)S(1)}, s32[1,4096]{1,0:T(1,128)S(1)}, f32[1,4096]{1,0:T(1,128)S(1)}, f32[1,512]{1,0:T(1,128)S(1)}, /*index=5*/bf16[64,512]{1,0:T(8,128)(2,1)S(1)}) custom-call(bf16[64,4096]{1,0:T(8,128)(2,1)} %feat_hbm.1, s32[1,512]{1,0:T(1,128)} %bitcast.10, s32[1,4096]{1,0:T(1,128)} %bitcast.8, ...), custom_call_target="tpu_custom_call" | custom-call | tf_op jit(solution)/shard_map/pallas_call | solution.py:323
  2.3 2.4 %collective-permute-start.1 = (bf16[64,512]{1,0:T(8,128)(2,1)S(1)}, bf16[64,512]{1,0:T(8,128)(2,1)S(1)}, u32[]{:S(2)}, u32[]{:S(2)}) collective-permute-start(bf16[64,512]{1,0:T(8,128)(2,1)S(1)} %get-tuple-element.31), channel_id=1, source_target_pairs={{0,17},{1,16},{2,19},{3,18},{4,21},{5,20},{6,23},{7,22},{8,25},{9,... | collective-permute-start | bytes 196616 | tf_op jit(solution)/shard_map/ppermute | solution.py:364
  4.7 0.7 %collective-permute-start.2 = (s32[512]{0:T(512)}, s32[512]{0:T(512)S(1)}, u32[]{:S(2)}, u32[]{:S(2)}) collective-permute-start(s32[512]{0:T(512)} %param.8), channel_id=1, source_target_pairs={{0,1},{1,0},{2,3},{3,2},{4,5},{5,4},{6,7},{7,6},{8,9},{9,8},{10,11... | collective-permute-start | bytes 6152 | tf_op jit(solution)/shard_map/ppermute | solution.py:364
  5.4 0.0 collective-permute-start
  5.4 0.7 %shard_map.69 = (bf16[256,4096]{1,0:T(8,128)(2,1)S(1)}, bf16[4096,256]{1,0:T(8,128)(2,1)S(1)}, bf16[16,4096]{1,0:T(8,128)(2,1)S(1)}) custom-call(bf16[64,4096]{1,0:T(8,128)(2,1)S(1)} %get-tuple-element.25.feat_ref, s32[1,4096]{1,0:T(1,128)S(1)} %get-tuple-element.26.slots_ref.refs_3_.refs_4_, f32[1,4096]{1,0:T(1,128)S(1)} %get-tuple-element.27.prices_ref), custom_call_target="tpu_custom_call" | custom-call | flops 4096000 | bytes 4194304 | tf_op jit(solution)/shard_map/pallas_call | solution.py:323
  6.0 0.4 collective-permute-done.2
  6.4 0.5 shard_map.70.refs_1_
  6.9 0.0 collective-permute-done
  6.9 0.6 %collective-permute-done.1.refs_0_ = bf16[64,512]{1,0:T(8,128)(2,1)S(1)} collective-permute-done((bf16[64,512]{1,0:T(8,128)(2,1)S(1)}, bf16[64,512]{1,0:T(8,128)(2,1)S(1)}, u32[]{:S(2)}, u32[]{:S(2)}) %collective-permute-start.1) | collective-permute-done | bytes 65568 | tf_op jit(solution)/shard_map/ppermute | solution.py:364
  7.5 2.5 %shard_map.71 = (bf16[8192,512]{1,0:T(8,128)(2,1)S(1)}, bf16[256,512]{1,0:T(8,128)(2,1)S(1)}, f32[1,512]{1,0:T(1,128)S(1)}, f32[8,512]{1,0:T(8,128)S(1)}) custom-call(bf16[4096,256]{1,0:T(8,128)(2,1)S(1)} %get-tuple-element.28.turned_ref, bf16[16,4096]{1,0:T(8,128)(2,1)S(1)} %get-tuple-element.29.weight_ref, f32[1,512]{1,0:T(1,128)S(1)} %bitcast.6, ...), custom_call_target="tpu_custom_call" | custom-call | flops 134217728 | bytes 8388608 | tf_op jit(solution)/shard_map/pallas_call | solution.py:323
  10.0 1.9 %collective-permute-start.3 = (f32[8,512]{1,0:T(8,128)S(1)}, f32[8,512]{1,0:T(8,128)S(1)}, u32[]{:S(2)}, u32[]{:S(2)}) collective-permute-start(f32[8,512]{1,0:T(8,128)S(1)} %get-tuple-element.33.refs_1_), channel_id=1, source_target_pairs={{0,17},{1,16},{2,19},{3,18},{4,21},{5,20},{6,23},{7,22},{8,25},{9,... | collective-permute-start | bytes 49160 | tf_op jit(solution)/shard_map/ppermute | solution.py:364
  11.9 1.9 %shard_map.72.refs_4_ = bf16[1024,4096]{1,0:T(8,128)(2,1)S(1)} custom-call(bf16[256,4096]{1,0:T(8,128)(2,1)S(1)} %get-tuple-element.35.columns_ref, bf16[256,512]{1,0:T(8,128)(2,1)S(1)} %get-tuple-element.36.center_ref), custom_call_target="tpu_custom_call" | custom-call | flops 134217728 | bytes 8388608 | tf_op jit(solution)/shard_map/pallas_call | solution.py:323
  13.9 0.0 collective-permute-done.3.refs_0_
  13.9 1.2 %shard_map.73 = (f32[8,512]{1,0:T(8,128)S(1)}, f32[1,4224]{1,0:T(1,128)S(1)}) custom-call(f32[8,512]{1,0:T(8,128)S(1)} %collective-permute-done.3.refs_0_, f32[8,512]{1,0:T(8,128)S(1)} %get-tuple-element.33.refs_1_, f32[1,512]{1,0:T(1,128)S(1)} %get-tuple-element.34.refs_2_, s32[1,4096]{1,0:T(1,128)S(1)} %get-tuple-element.26.slots_ref.refs_3_.refs_4_, ...), custom_call_target="tpu_custom_call" | custom-call | tf_op jit(solution)/shard_map/pallas_call | solution.py:323
  15.1 1.6 %collective-permute-start.4 = (f32[1,4224]{1,0:T(1,128)S(1)}, f32[1,4224]{1,0:T(1,128)S(1)}, u32[]{:S(2)}, u32[]{:S(2)}) collective-permute-start(f32[1,4224]{1,0:T(1,128)S(1)} %get-tuple-element.37), channel_id=1, source_target_pairs={{0,2},{1,3},{2,0},{3,1},{4,6},{5,7},{6,4},{7,5},{8,10},{9,11},{10,... | collective-permute-start | bytes 50696 | tf_op jit(solution)/shard_map/ppermute | solution.py:348
  16.7 0.3 collective-permute-start.5
  16.9 0.4 collective-permute-start.6
  17.3 1.6 %collective-permute-done.4 = f32[1,4224]{1,0:T(1,128)S(1)} collective-permute-done((f32[1,4224]{1,0:T(1,128)S(1)}, f32[1,4224]{1,0:T(1,128)S(1)}, u32[]{:S(2)}, u32[]{:S(2)}) %collective-permute-start.4) | collective-permute-done | bytes 16928 | tf_op jit(solution)/shard_map/ppermute | solution.py:348
  18.9 0.9 %collective-permute-done.5 = f32[1,4224]{1,0:T(1,128)S(1)} collective-permute-done((f32[1,4224]{1,0:T(1,128)S(1)}, f32[1,4224]{1,0:T(1,128)S(1)}, u32[]{:S(2)}, u32[]{:S(2)}) %collective-permute-start.5) | collective-permute-done | bytes 16928 | tf_op jit(solution)/shard_map/ppermute | solution.py:348
  19.9 0.0 collective-permute-done.6
  19.9 3.4 %collective-permute-start.7 = (f32[1,4224]{1,0:T(1,128)S(1)}, f32[1,4224]{1,0:T(1,128)S(1)}, u32[]{:S(2)}, u32[]{:S(2)}) collective-permute-start(f32[1,4224]{1,0:T(1,128)S(1)} %add_add_fusion.1.refs_3_), channel_id=1, source_target_pairs={{0,13},{1,12},{2,15},{3,14},{4,9},{5,8},{6,11},{7,10},{8,5},{9,4},... | collective-permute-start | bytes 50696 | tf_op jit(solution)/shard_map/ppermute | solution.py:348
  23.3 0.0 collective-permute-start.8
  23.3 0.6 %collective-permute-start.9 = (f32[1,4224]{1,0:T(1,128)S(1)}, f32[1,4224]{1,0:T(1,128)S(1)}, u32[]{:S(2)}, u32[]{:S(2)}) collective-permute-start(f32[1,4224]{1,0:T(1,128)S(1)} %add_add_fusion.1.refs_3_), channel_id=1, source_target_pairs={{0,5},{1,4},{2,7},{3,6},{4,1},{5,0},{6,3},{7,2},{8,13},{9,12},{10,... | collective-permute-start | bytes 50696 | tf_op jit(solution)/shard_map/ppermute | solution.py:348
  23.9 1.0 %collective-permute-done.7.refs_0_ = f32[1,4224]{1,0:T(1,128)S(1)} collective-permute-done((f32[1,4224]{1,0:T(1,128)S(1)}, f32[1,4224]{1,0:T(1,128)S(1)}, u32[]{:S(2)}, u32[]{:S(2)}) %collective-permute-start.7) | collective-permute-done | bytes 16928 | tf_op jit(solution)/shard_map/ppermute | solution.py:348
  24.9 2.5 %collective-permute-done.8.refs_1_ = f32[1,4224]{1,0:T(1,128)S(1)} collective-permute-done((f32[1,4224]{1,0:T(1,128)S(1)}, f32[1,4224]{1,0:T(1,128)S(1)}, u32[]{:S(2)}, u32[]{:S(2)}) %collective-permute-start.8) | collective-permute-done | bytes 16928 | tf_op jit(solution)/shard_map/ppermute | solution.py:348
  27.4 0.0 collective-permute-done.9.refs_2_
  27.4 1.2 %shard_map.74 = (f32[1,4224]{1,0:T(1,128)S(1)}, f32[8,128]{1,0:T(8,128)S(1)}, f32[8,640]{1,0:T(8,128)S(1)}) custom-call(f32[1,4224]{1,0:T(1,128)S(1)} %collective-permute-done.7.refs_0_, f32[1,4224]{1,0:T(1,128)S(1)} %collective-permute-done.8.refs_1_, f32[1,4224]{1,0:T(1,128)S(1)} %collective-permute-done.9.refs_2_, f32[1,4224]{1,0:T(1,128)S(1)} %add_add_fusion.1.refs_3_, ...), custom_call_target="tpu_custom_call" | custom-call | tf_op jit(solution)/shard_map/pallas_call | solution.py:323
  28.6 1.7 %collective-permute-start.10 = (f32[8,640]{1,0:T(8,128)S(1)}, f32[8,640]{1,0:T(8,128)S(1)}, u32[]{:S(2)}, u32[]{:S(2)}) collective-permute-start(f32[8,640]{1,0:T(8,128)S(1)} %get-tuple-element.39.refs_1_), channel_id=1, source_target_pairs={{0,17},{1,16},{2,19},{3,18},{4,21},{5,20},{6,23},{7,22},{8,25},{9,... | collective-permute-start | bytes 61448 | tf_op jit(solution)/shard_map/ppermute | solution.py:364
  30.3 1.5 %collective-permute-done.10.refs_0_ = f32[8,640]{1,0:T(8,128)S(1)} collective-permute-done((f32[8,640]{1,0:T(8,128)S(1)}, f32[8,640]{1,0:T(8,128)S(1)}, u32[]{:S(2)}, u32[]{:S(2)}) %collective-permute-start.10) | collective-permute-done | bytes 20512 | tf_op jit(solution)/shard_map/ppermute | solution.py:364
  31.8 1.2 %shard_map.75 = (f32[16,512]{1,0:T(8,128)S(1)}, f32[8,128]{1,0:T(8,128)S(1)}, f32[1,4224]{1,0:T(1,128)S(1)}) custom-call(f32[8,640]{1,0:T(8,128)S(1)} %collective-permute-done.10.refs_0_, f32[8,640]{1,0:T(8,128)S(1)} %get-tuple-element.39.refs_1_, f32[1,512]{1,0:T(1,128)S(1)} %get-tuple-element.34.refs_2_, ...), custom_call_target="tpu_custom_call" | custom-call | tf_op jit(solution)/shard_map/pallas_call | solution.py:323
  33.0 0.8 %collective-permute-start.11 = (f32[1,4224]{1,0:T(1,128)S(1)}, f32[1,4224]{1,0:T(1,128)S(1)}, u32[]{:S(2)}, u32[]{:S(2)}) collective-permute-start(f32[1,4224]{1,0:T(1,128)S(1)} %get-tuple-element.42), channel_id=1, source_target_pairs={{0,2},{1,3},{2,0},{3,1},{4,6},{5,7},{6,4},{7,5},{8,10},{9,11},{10,... | collective-permute-start | bytes 50696 | tf_op jit(solution)/shard_map/ppermute | solution.py:348
  33.8 1.0 %collective-permute-start.12 = (f32[1,4224]{1,0:T(1,128)S(1)}, f32[1,4224]{1,0:T(1,128)S(1)}, u32[]{:S(2)}, u32[]{:S(2)}) collective-permute-start(f32[1,4224]{1,0:T(1,128)S(1)} %get-tuple-element.42), channel_id=1, source_target_pairs={{0,3},{1,2},{2,1},{3,0},{4,7},{5,6},{6,5},{7,4},{8,11},{9,10},{10,... | collective-permute-start | bytes 50696 | tf_op jit(solution)/shard_map/ppermute | solution.py:348
  34.8 0.4 collective-permute-start.13
  35.2 1.6 %collective-permute-done.11 = f32[1,4224]{1,0:T(1,128)S(1)} collective-permute-done((f32[1,4224]{1,0:T(1,128)S(1)}, f32[1,4224]{1,0:T(1,128)S(1)}, u32[]{:S(2)}, u32[]{:S(2)}) %collective-permute-start.11) | collective-permute-done | bytes 16928 | tf_op jit(solution)/shard_map/ppermute | solution.py:348
  36.9 0.1 collective-permute-done.12
  37.0 0.0 collective-permute-done.13
  37.1 1.5 %collective-permute-start.14 = (f32[1,4224]{1,0:T(1,128)S(1)}, f32[1,4224]{1,0:T(1,128)S(1)}, u32[]{:S(2)}, u32[]{:S(2)}) collective-permute-start(f32[1,4224]{1,0:T(1,128)S(1)} %add_add_fusion.refs_3_), channel_id=1, source_target_pairs={{0,13},{1,12},{2,15},{3,14},{4,9},{5,8},{6,11},{7,10},{8,5},{9,4},... | collective-permute-start | bytes 50696 | tf_op jit(solution)/shard_map/ppermute | solution.py:348
  38.6 0.6 %collective-permute-start.15 = (f32[1,4224]{1,0:T(1,128)S(1)}, f32[1,4224]{1,0:T(1,128)S(1)}, u32[]{:S(2)}, u32[]{:S(2)}) collective-permute-start(f32[1,4224]{1,0:T(1,128)S(1)} %add_add_fusion.refs_3_), channel_id=1, source_target_pairs={{0,9},{1,8},{2,11},{3,10},{4,13},{5,12},{6,15},{7,14},{8,1},{9,0},... | collective-permute-start | bytes 50696 | tf_op jit(solution)/shard_map/ppermute | solution.py:348
  39.1 1.9 %collective-permute-start.16 = (f32[1,4224]{1,0:T(1,128)S(1)}, f32[1,4224]{1,0:T(1,128)S(1)}, u32[]{:S(2)}, u32[]{:S(2)}) collective-permute-start(f32[1,4224]{1,0:T(1,128)S(1)} %add_add_fusion.refs_3_), channel_id=1, source_target_pairs={{0,5},{1,4},{2,7},{3,6},{4,1},{5,0},{6,3},{7,2},{8,13},{9,12},{10,... | collective-permute-start | bytes 50696 | tf_op jit(solution)/shard_map/ppermute | solution.py:348
  41.0 0.4 collective-permute-start.19
  41.4 0.7 %collective-permute-done.14.refs_0_ = f32[1,4224]{1,0:T(1,128)S(1)} collective-permute-done((f32[1,4224]{1,0:T(1,128)S(1)}, f32[1,4224]{1,0:T(1,128)S(1)}, u32[]{:S(2)}, u32[]{:S(2)}) %collective-permute-start.14) | collective-permute-done | bytes 16928 | tf_op jit(solution)/shard_map/ppermute | solution.py:348
  42.1 0.5 %collective-permute-done.15.refs_1_ = f32[1,4224]{1,0:T(1,128)S(1)} collective-permute-done((f32[1,4224]{1,0:T(1,128)S(1)}, f32[1,4224]{1,0:T(1,128)S(1)}, u32[]{:S(2)}, u32[]{:S(2)}) %collective-permute-start.15) | collective-permute-done | bytes 16928 | tf_op jit(solution)/shard_map/ppermute | solution.py:348
  42.6 0.1 collective-permute-done.16.refs_2_
  42.8 1.3 %shard_map.76 = (f32[8,256]{1,0:T(8,128)S(1)}, f32[8,640]{1,0:T(8,128)S(1)}) custom-call(f32[1,4224]{1,0:T(1,128)S(1)} %collective-permute-done.14.refs_0_, f32[1,4224]{1,0:T(1,128)S(1)} %collective-permute-done.15.refs_1_, f32[1,4224]{1,0:T(1,128)S(1)} %collective-permute-done.16.refs_2_, f32[1,4224]{1,0:T(1,128)S(1)} %add_add_fusion.refs_3_, ...), custom_call_target="tpu_custom_call" | custom-call | tf_op jit(solution)/shard_map/pallas_call | solution.py:323
  44.0 1.6 %collective-permute-start.17 = (f32[8,640]{1,0:T(8,128)S(1)}, f32[8,640]{1,0:T(8,128)S(1)}, u32[]{:S(2)}, u32[]{:S(2)}) collective-permute-start(f32[8,640]{1,0:T(8,128)S(1)} %get-tuple-element.44.refs_2_), channel_id=1, source_target_pairs={{0,16},{1,17},{2,18},{3,19},{4,20},{5,21},{6,22},{7,23},{8,24},{9,... | collective-permute-start | bytes 61448 | tf_op jit(solution)/shard_map/ppermute | solution.py:364
  45.6 0.0 collective-permute-start.18
  45.6 0.0 collective-permute-done.19.refs_3_
  45.6 1.6 %collective-permute-done.17.refs_0_ = f32[8,640]{1,0:T(8,128)S(1)} collective-permute-done((f32[8,640]{1,0:T(8,128)S(1)}, f32[8,640]{1,0:T(8,128)S(1)}, u32[]{:S(2)}, u32[]{:S(2)}) %collective-permute-start.17) | collective-permute-done | bytes 20512 | tf_op jit(solution)/shard_map/ppermute | solution.py:364
  47.2 0.0 collective-permute-done.18.refs_1_
  47.2 0.6 %shard_map.77 = (f32[8,512]{1,0:T(8,128)}, f32[8,512]{1,0:T(8,128)}) custom-call(f32[8,640]{1,0:T(8,128)S(1)} %collective-permute-done.17.refs_0_, f32[8,640]{1,0:T(8,128)S(1)} %collective-permute-done.18.refs_1_, f32[8,640]{1,0:T(8,128)S(1)} %get-tuple-element.44.refs_2_, f32[16,512]{1,0:T(8,128)S(1)} %collective-permute-done.19.refs_3_, ...), custom_call_target="tpu_custom_call" | custom-call | tf_op jit(solution)/shard_map/pallas_call | solution.py:323
  (2 shorter events, 0.1 us)
Async XLA Ops:
  2.3 5.2 %collective-permute-start.1 = (bf16[64,512]{1,0:T(8,128)(2,1)S(1)}, bf16[64,512]{1,0:T(8,128)(2,1)S(1)}, u32[]{:S(2)}, u32[]{:S(2)}) collective-permute-start(bf16[64,512]{1,0:T(8,128)(2,1)S(1)} %get-tuple-element.31), channel_id=1, source_target_pairs={{0,17},{1,16},{2,19},{3,18},{4,21},{5,20},{6,23},{7,22},{8,25},{9,... | collective-permute-start | bytes 196616 | tf_op jit(solution)/shard_map/ppermute | solution.py:364
  4.7 1.7 %collective-permute-start.2 = (s32[512]{0:T(512)}, s32[512]{0:T(512)S(1)}, u32[]{:S(2)}, u32[]{:S(2)}) collective-permute-start(s32[512]{0:T(512)} %param.8), channel_id=1, source_target_pairs={{0,1},{1,0},{2,3},{3,2},{4,5},{5,4},{6,7},{7,6},{8,9},{9,8},{10,11... | collective-permute-start | bytes 6152 | tf_op jit(solution)/shard_map/ppermute | solution.py:364
  5.4 1.5 %collective-permute-start = (f32[512]{0:T(512)}, f32[512]{0:T(512)S(1)}, u32[]{:S(2)}, u32[]{:S(2)}) collective-permute-start(f32[512]{0:T(512)} %param.9), channel_id=1, source_target_pairs={{0,1},{1,0},{2,3},{3,2},{4,5},{5,4},{6,7},{7,6},{8,9},{9,8},{10,11... | collective-permute-start | bytes 6152 | tf_op jit(solution)/shard_map/ppermute | solution.py:364
  10.0 3.8 %collective-permute-start.3 = (f32[8,512]{1,0:T(8,128)S(1)}, f32[8,512]{1,0:T(8,128)S(1)}, u32[]{:S(2)}, u32[]{:S(2)}) collective-permute-start(f32[8,512]{1,0:T(8,128)S(1)} %get-tuple-element.33.refs_1_), channel_id=1, source_target_pairs={{0,17},{1,16},{2,19},{3,18},{4,21},{5,20},{6,23},{7,22},{8,25},{9,... | collective-permute-start | bytes 49160 | tf_op jit(solution)/shard_map/ppermute | solution.py:364
  15.1 3.8 %collective-permute-start.4 = (f32[1,4224]{1,0:T(1,128)S(1)}, f32[1,4224]{1,0:T(1,128)S(1)}, u32[]{:S(2)}, u32[]{:S(2)}) collective-permute-start(f32[1,4224]{1,0:T(1,128)S(1)} %get-tuple-element.37), channel_id=1, source_target_pairs={{0,2},{1,3},{2,0},{3,1},{4,6},{5,7},{6,4},{7,5},{8,10},{9,11},{10,... | collective-permute-start | bytes 50696 | tf_op jit(solution)/shard_map/ppermute | solution.py:348
  16.7 3.2 %collective-permute-start.5 = (f32[1,4224]{1,0:T(1,128)S(1)}, f32[1,4224]{1,0:T(1,128)S(1)}, u32[]{:S(2)}, u32[]{:S(2)}) collective-permute-start(f32[1,4224]{1,0:T(1,128)S(1)} %get-tuple-element.37), channel_id=1, source_target_pairs={{0,3},{1,2},{2,1},{3,0},{4,7},{5,6},{6,5},{7,4},{8,11},{9,10},{10,... | collective-permute-start | bytes 50696 | tf_op jit(solution)/shard_map/ppermute | solution.py:348
  16.9 2.9 %collective-permute-start.6 = (f32[1,4224]{1,0:T(1,128)S(1)}, f32[1,4224]{1,0:T(1,128)S(1)}, u32[]{:S(2)}, u32[]{:S(2)}) collective-permute-start(f32[1,4224]{1,0:T(1,128)S(1)} %get-tuple-element.37), channel_id=1, source_target_pairs={{0,1},{1,0},{2,3},{3,2},{4,5},{5,4},{6,7},{7,6},{8,9},{9,8},{10,11... | collective-permute-start | bytes 50696 | tf_op jit(solution)/shard_map/ppermute | solution.py:348
  19.9 5.0 %collective-permute-start.7 = (f32[1,4224]{1,0:T(1,128)S(1)}, f32[1,4224]{1,0:T(1,128)S(1)}, u32[]{:S(2)}, u32[]{:S(2)}) collective-permute-start(f32[1,4224]{1,0:T(1,128)S(1)} %add_add_fusion.1.refs_3_), channel_id=1, source_target_pairs={{0,13},{1,12},{2,15},{3,14},{4,9},{5,8},{6,11},{7,10},{8,5},{9,4},... | collective-permute-start | bytes 50696 | tf_op jit(solution)/shard_map/ppermute | solution.py:348
  23.3 4.1 %collective-permute-start.8 = (f32[1,4224]{1,0:T(1,128)S(1)}, f32[1,4224]{1,0:T(1,128)S(1)}, u32[]{:S(2)}, u32[]{:S(2)}) collective-permute-start(f32[1,4224]{1,0:T(1,128)S(1)} %add_add_fusion.1.refs_3_), channel_id=1, source_target_pairs={{0,9},{1,8},{2,11},{3,10},{4,13},{5,12},{6,15},{7,14},{8,1},{9,0},... | collective-permute-start | bytes 50696 | tf_op jit(solution)/shard_map/ppermute | solution.py:348
  23.3 4.1 %collective-permute-start.9 = (f32[1,4224]{1,0:T(1,128)S(1)}, f32[1,4224]{1,0:T(1,128)S(1)}, u32[]{:S(2)}, u32[]{:S(2)}) collective-permute-start(f32[1,4224]{1,0:T(1,128)S(1)} %add_add_fusion.1.refs_3_), channel_id=1, source_target_pairs={{0,5},{1,4},{2,7},{3,6},{4,1},{5,0},{6,3},{7,2},{8,13},{9,12},{10,... | collective-permute-start | bytes 50696 | tf_op jit(solution)/shard_map/ppermute | solution.py:348
  28.6 3.2 %collective-permute-start.10 = (f32[8,640]{1,0:T(8,128)S(1)}, f32[8,640]{1,0:T(8,128)S(1)}, u32[]{:S(2)}, u32[]{:S(2)}) collective-permute-start(f32[8,640]{1,0:T(8,128)S(1)} %get-tuple-element.39.refs_1_), channel_id=1, source_target_pairs={{0,17},{1,16},{2,19},{3,18},{4,21},{5,20},{6,23},{7,22},{8,25},{9,... | collective-permute-start | bytes 61448 | tf_op jit(solution)/shard_map/ppermute | solution.py:364
  33.0 3.8 %collective-permute-start.11 = (f32[1,4224]{1,0:T(1,128)S(1)}, f32[1,4224]{1,0:T(1,128)S(1)}, u32[]{:S(2)}, u32[]{:S(2)}) collective-permute-start(f32[1,4224]{1,0:T(1,128)S(1)} %get-tuple-element.42), channel_id=1, source_target_pairs={{0,2},{1,3},{2,0},{3,1},{4,6},{5,7},{6,4},{7,5},{8,10},{9,11},{10,... | collective-permute-start | bytes 50696 | tf_op jit(solution)/shard_map/ppermute | solution.py:348
  33.8 3.2 %collective-permute-start.12 = (f32[1,4224]{1,0:T(1,128)S(1)}, f32[1,4224]{1,0:T(1,128)S(1)}, u32[]{:S(2)}, u32[]{:S(2)}) collective-permute-start(f32[1,4224]{1,0:T(1,128)S(1)} %get-tuple-element.42), channel_id=1, source_target_pairs={{0,3},{1,2},{2,1},{3,0},{4,7},{5,6},{6,5},{7,4},{8,11},{9,10},{10,... | collective-permute-start | bytes 50696 | tf_op jit(solution)/shard_map/ppermute | solution.py:348
  34.8 2.2 %collective-permute-start.13 = (f32[1,4224]{1,0:T(1,128)S(1)}, f32[1,4224]{1,0:T(1,128)S(1)}, u32[]{:S(2)}, u32[]{:S(2)}) collective-permute-start(f32[1,4224]{1,0:T(1,128)S(1)} %get-tuple-element.42), channel_id=1, source_target_pairs={{0,1},{1,0},{2,3},{3,2},{4,5},{5,4},{6,7},{7,6},{8,9},{9,8},{10,11... | collective-permute-start | bytes 50696 | tf_op jit(solution)/shard_map/ppermute | solution.py:348
  37.1 5.0 %collective-permute-start.14 = (f32[1,4224]{1,0:T(1,128)S(1)}, f32[1,4224]{1,0:T(1,128)S(1)}, u32[]{:S(2)}, u32[]{:S(2)}) collective-permute-start(f32[1,4224]{1,0:T(1,128)S(1)} %add_add_fusion.refs_3_), channel_id=1, source_target_pairs={{0,13},{1,12},{2,15},{3,14},{4,9},{5,8},{6,11},{7,10},{8,5},{9,4},... | collective-permute-start | bytes 50696 | tf_op jit(solution)/shard_map/ppermute | solution.py:348
  38.6 4.1 %collective-permute-start.15 = (f32[1,4224]{1,0:T(1,128)S(1)}, f32[1,4224]{1,0:T(1,128)S(1)}, u32[]{:S(2)}, u32[]{:S(2)}) collective-permute-start(f32[1,4224]{1,0:T(1,128)S(1)} %add_add_fusion.refs_3_), channel_id=1, source_target_pairs={{0,9},{1,8},{2,11},{3,10},{4,13},{5,12},{6,15},{7,14},{8,1},{9,0},... | collective-permute-start | bytes 50696 | tf_op jit(solution)/shard_map/ppermute | solution.py:348
  39.1 3.7 %collective-permute-start.16 = (f32[1,4224]{1,0:T(1,128)S(1)}, f32[1,4224]{1,0:T(1,128)S(1)}, u32[]{:S(2)}, u32[]{:S(2)}) collective-permute-start(f32[1,4224]{1,0:T(1,128)S(1)} %add_add_fusion.refs_3_), channel_id=1, source_target_pairs={{0,5},{1,4},{2,7},{3,6},{4,1},{5,0},{6,3},{7,2},{8,13},{9,12},{10,... | collective-permute-start | bytes 50696 | tf_op jit(solution)/shard_map/ppermute | solution.py:348
  41.0 4.6 %collective-permute-start.19 = (f32[16,512]{1,0:T(8,128)S(1)}, f32[16,512]{1,0:T(8,128)S(1)}, u32[]{:S(2)}, u32[]{:S(2)}) collective-permute-start(f32[16,512]{1,0:T(8,128)S(1)} %get-tuple-element.45.refs_4_), channel_id=1, source_target_pairs={{0,1},{1,0},{2,3},{3,2},{4,5},{5,4},{6,7},{7,6},{8,9},{9,8},{10,11... | collective-permute-start | bytes 98312 | tf_op jit(solution)/shard_map/ppermute | solution.py:364
  44.0 3.2 %collective-permute-start.17 = (f32[8,640]{1,0:T(8,128)S(1)}, f32[8,640]{1,0:T(8,128)S(1)}, u32[]{:S(2)}, u32[]{:S(2)}) collective-permute-start(f32[8,640]{1,0:T(8,128)S(1)} %get-tuple-element.44.refs_2_), channel_id=1, source_target_pairs={{0,16},{1,17},{2,18},{3,19},{4,20},{5,21},{6,22},{7,23},{8,24},{9,... | collective-permute-start | bytes 61448 | tf_op jit(solution)/shard_map/ppermute | solution.py:364
  45.6 1.6 %collective-permute-start.18 = (f32[8,640]{1,0:T(8,128)S(1)}, f32[8,640]{1,0:T(8,128)S(1)}, u32[]{:S(2)}, u32[]{:S(2)}) collective-permute-start(f32[8,640]{1,0:T(8,128)S(1)} %get-tuple-element.44.refs_2_), channel_id=1, source_target_pairs={{0,1},{1,0},{2,3},{3,2},{4,5},{5,4},{6,7},{7,6},{8,9},{9,8},{10,11... | collective-permute-start | bytes 61448 | tf_op jit(solution)/shard_map/ppermute | solution.py:364

commit v27 on v25

--- a/solution.py
+++ b/solution.py
@@ -224,11 +224,18 @@
 def fold_rows(rows, block_ref, slots_ref, out_ref):
     row_count, count = slots_ref.shape[1], block_ref.shape[1]
     weight = jnp.where(slot_mask(slots_ref[...]), rows, 0.0)
-    out_ref[:, 0:count] = product(
+    folded = product(
         stack2(weight), block_ref[0:row_count, :], block_ref[row_count:, :]
     )
-    square = row_sum(weight * weight)
-    out_ref[:, count : count + EXTRA] = spread(square)
+    for slot in range(SLOTS):
+        out_ref[:, slot * count : (slot + 1) * count] = folded[slot : slot + 1]
+    out_ref[:, SLOTS * count :] = to_lanes(row_sum(weight * weight), 0)
+
+
+def unfold(row, count):
+    folded = [row[:, slot * count : (slot + 1) * count] for slot in range(SLOTS)]
+    square = spread(from_lanes(row[:, SLOTS * count :], 0))
+    return jnp.concatenate([*folded], axis=0), square
 
 
 def first_apply_body(parts, scale_over_root, *refs):
@@ -256,12 +263,12 @@
     (scale_ref, slots_ref, turned_ref, target_ref, norm_ref,
      state_ref, step_ref, out_ref) = refs[parts:]
     row_count, count = turned_ref.shape[1], scale_ref.shape[1]
-    folded = total_of(fold_refs)
+    folded, square = unfold(total_of(fold_refs), count)
     scale = scale_ref[...]
     target = target_ref[...]
     norm = norm_ref[...]
-    applied = scale * folded[:, 0:count] * inv_rows + RIDGE * target
-    step = norm / (folded[:, count:] * inv_rows + RIDGE * norm)
+    applied = scale * folded * inv_rows + RIDGE * target
+    step = norm / (square * inv_rows + RIDGE * norm)
     residual = target - wide(step, count) * applied
     state_ref[0:SLOTS, :] = target
     state_ref[SLOTS:, :] = residual
@@ -297,14 +304,15 @@
     else:
         folded = total_of(fold_refs)
         state = state_ref[...]
+    folded, rows_square = unfold(folded, count)
     target, residual = state[0:SLOTS], state[SLOTS:]
     first_norm = norm_ref[...]
     norm, cross = sums_ref[:, 0:EXTRA], sums_ref[:, EXTRA:]
     ratio = norm / first_norm
     direction = residual + wide(ratio, count) * target
     square = norm + 2.0 * ratio * cross + ratio * ratio * first_norm
-    applied = scale_ref[...] * folded[:, 0:count] * inv_rows + RIDGE * direction
-    step = wide(norm / (folded[:, count:] * inv_rows + RIDGE * square), count)
+    applied = scale_ref[...] * folded * inv_rows + RIDGE * direction
+    step = wide(norm / (rows_square * inv_rows + RIDGE * square), count)
     coefficients_ref[...] = wide(step_ref[...], count) * target + step * direction
     out_ref[...] = residual - step * applied
 
@@ -379,7 +387,7 @@
     count = center_idx.shape[0]
     all_rows = row_count * lax.axis_size("dp")
     row_shape = shaped((1, row_count + EXTRA))
-    fold_shape = shaped((SLOTS, count + EXTRA))
+    fold_shape = shaped((1, SLOTS * count + EXTRA))
     vector = shaped((SLOTS, count))
     narrow = shaped((SLOTS, EXTRA))
     pass_cost = dict(flops=64 * row_count * count, bytes_accessed=4 * row_count * count)

time: 48 us -> 48 us (level)
  no operation moved by 1% of the time
where the time goes in v27:
time: 48 us; the launch traced here: 47.9 us
  starting transfers between devices  21.1 us (44%)
  waiting for transfers between devices  13.2 us (28%)
  Pallas kernels  12.8 us (27%)
  between operations  0.72 us (2%)
    pallas_call x10, Pallas kernels, call(): pl.pallas_call(body, out_shape=out_shape, in_specs=sources or [VMEM] * le...  12.8 us
    ppermute x12, starting transfers between devices, exchange(): parts.insert(0, lax.ppermute(value, axis, pairs))  12.3 us
    ppermute x12, waiting for transfers between devices, exchange(): parts.insert(0, lax.ppermute(value, axis, pairs))  9.18 us
    ppermute x8, starting transfers between devices, moved(): return lax.ppermute(value, ('dp', 'centers'), pairs_over(target_of))  8.72 us
    ppermute x8, waiting for transfers between devices, moved(): return lax.ppermute(value, ('dp', 'centers'), pairs_over(target_of))  4.05 us
  transfers between devices with their start and end apart: 20, of which 13 were waited for; matrix products, arithmetic and copies ran while one was open for 0% of the time, Pallas kernels for 9%

profile of v27, /device:TPU:0, one launch (start us, length us, event | category | flops | bytes accessed | tf_op | source)
XLA Modules:
  0.0 47.9 jit_solution(13000664757935231977)
XLA Ops:
  0.6 1.6 %shard_map.68 = (bf16[64,4096]{1,0:T(8,128)(2,1)S(1)}, s32[1,512]{1,0:T(1,128)S(1)}, s32[1,4096]{1,0:T(1,128)S(1)}, f32[1,4096]{1,0:T(1,128)S(1)}, f32[1,512]{1,0:T(1,128)S(1)}, /*index=5*/bf16[64,512]{1,0:T(8,128)(2,1)S(1)}) custom-call(bf16[64,4096]{1,0:T(8,128)(2,1)} %feat_hbm.1, s32[1,512]{1,0:T(1,128)} %bitcast.10, s32[1,4096]{1,0:T(1,128)} %bitcast.8, ...), custom_call_target="tpu_custom_call" | custom-call | tf_op jit(solution)/shard_map/pallas_call | solution.py:321
  2.2 2.4 %collective-permute-start.1 = (bf16[64,512]{1,0:T(8,128)(2,1)S(1)}, bf16[64,512]{1,0:T(8,128)(2,1)S(1)}, u32[]{:S(2)}, u32[]{:S(2)}) collective-permute-start(bf16[64,512]{1,0:T(8,128)(2,1)S(1)} %get-tuple-element.31), channel_id=1, source_target_pairs={{0,17},{1,16},{2,19},{3,18},{4,21},{5,20},{6,23},{7,22},{8,25},{9,... | collective-permute-start | bytes 196616 | tf_op jit(solution)/shard_map/ppermute | solution.py:362
  4.6 0.7 %collective-permute-start.2 = (s32[512]{0:T(512)}, s32[512]{0:T(512)S(1)}, u32[]{:S(2)}, u32[]{:S(2)}) collective-permute-start(s32[512]{0:T(512)} %param.8), channel_id=1, source_target_pairs={{0,1},{1,0},{2,3},{3,2},{4,5},{5,4},{6,7},{7,6},{8,9},{9,8},{10,11... | collective-permute-start | bytes 6152 | tf_op jit(solution)/shard_map/ppermute | solution.py:362
  5.3 0.0 collective-permute-start
  5.3 0.7 %shard_map.69 = (bf16[256,4096]{1,0:T(8,128)(2,1)S(1)}, bf16[4096,256]{1,0:T(8,128)(2,1)S(1)}, bf16[16,4096]{1,0:T(8,128)(2,1)S(1)}) custom-call(bf16[64,4096]{1,0:T(8,128)(2,1)S(1)} %get-tuple-element.25.feat_ref, s32[1,4096]{1,0:T(1,128)S(1)} %get-tuple-element.26.slots_ref.refs_3_.refs_4_, f32[1,4096]{1,0:T(1,128)S(1)} %get-tuple-element.27.prices_ref), custom_call_target="tpu_custom_call" | custom-call | flops 4096000 | bytes 4194304 | tf_op jit(solution)/shard_map/pallas_call | solution.py:321
  6.0 0.4 collective-permute-done.2
  6.3 0.5 shard_map.70.refs_1_
  6.8 0.0 collective-permute-done
  6.8 0.6 %collective-permute-done.1.refs_0_ = bf16[64,512]{1,0:T(8,128)(2,1)S(1)} collective-permute-done((bf16[64,512]{1,0:T(8,128)(2,1)S(1)}, bf16[64,512]{1,0:T(8,128)(2,1)S(1)}, u32[]{:S(2)}, u32[]{:S(2)}) %collective-permute-start.1) | collective-permute-done | bytes 65568 | tf_op jit(solution)/shard_map/ppermute | solution.py:362
  7.4 2.5 %shard_map.71 = (bf16[8192,512]{1,0:T(8,128)(2,1)S(1)}, bf16[256,512]{1,0:T(8,128)(2,1)S(1)}, f32[1,512]{1,0:T(1,128)S(1)}, f32[8,512]{1,0:T(8,128)S(1)}) custom-call(bf16[4096,256]{1,0:T(8,128)(2,1)S(1)} %get-tuple-element.28.turned_ref, bf16[16,4096]{1,0:T(8,128)(2,1)S(1)} %get-tuple-element.29.weight_ref, f32[1,512]{1,0:T(1,128)S(1)} %bitcast.6, ...), custom_call_target="tpu_custom_call" | custom-call | flops 134217728 | bytes 8388608 | tf_op jit(solution)/shard_map/pallas_call | solution.py:321
  10.0 1.9 %collective-permute-start.3 = (f32[8,512]{1,0:T(8,128)S(1)}, f32[8,512]{1,0:T(8,128)S(1)}, u32[]{:S(2)}, u32[]{:S(2)}) collective-permute-start(f32[8,512]{1,0:T(8,128)S(1)} %get-tuple-element.33.refs_1_), channel_id=1, source_target_pairs={{0,17},{1,16},{2,19},{3,18},{4,21},{5,20},{6,23},{7,22},{8,25},{9,... | collective-permute-start | bytes 49160 | tf_op jit(solution)/shard_map/ppermute | solution.py:362
  11.9 1.9 %shard_map.72.refs_4_ = bf16[1024,4096]{1,0:T(8,128)(2,1)S(1)} custom-call(bf16[256,4096]{1,0:T(8,128)(2,1)S(1)} %get-tuple-element.35.columns_ref, bf16[256,512]{1,0:T(8,128)(2,1)S(1)} %get-tuple-element.36.center_ref), custom_call_target="tpu_custom_call" | custom-call | flops 134217728 | bytes 8388608 | tf_op jit(solution)/shard_map/pallas_call | solution.py:321
  13.8 0.0 collective-permute-done.3.refs_0_
  13.8 1.2 %shard_map.73 = (f32[8,512]{1,0:T(8,128)S(1)}, f32[1,4224]{1,0:T(1,128)S(1)}) custom-call(f32[8,512]{1,0:T(8,128)S(1)} %collective-permute-done.3.refs_0_, f32[8,512]{1,0:T(8,128)S(1)} %get-tuple-element.33.refs_1_, f32[1,512]{1,0:T(1,128)S(1)} %get-tuple-element.34.refs_2_, s32[1,4096]{1,0:T(1,128)S(1)} %get-tuple-element.26.slots_ref.refs_3_.refs_4_, ...), custom_call_target="tpu_custom_call" | custom-call | tf_op jit(solution)/shard_map/pallas_call | solution.py:321
  15.0 1.6 %collective-permute-start.4 = (f32[1,4224]{1,0:T(1,128)S(1)}, f32[1,4224]{1,0:T(1,128)S(1)}, u32[]{:S(2)}, u32[]{:S(2)}) collective-permute-start(f32[1,4224]{1,0:T(1,128)S(1)} %get-tuple-element.37), channel_id=1, source_target_pairs={{0,2},{1,3},{2,0},{3,1},{4,6},{5,7},{6,4},{7,5},{8,10},{9,11},{10,... | collective-permute-start | bytes 50696 | tf_op jit(solution)/shard_map/ppermute | solution.py:346
  16.6 0.3 collective-permute-start.5
  16.9 0.4 collective-permute-start.6
  17.2 1.6 %collective-permute-done.4 = f32[1,4224]{1,0:T(1,128)S(1)} collective-permute-done((f32[1,4224]{1,0:T(1,128)S(1)}, f32[1,4224]{1,0:T(1,128)S(1)}, u32[]{:S(2)}, u32[]{:S(2)}) %collective-permute-start.4) | collective-permute-done | bytes 16928 | tf_op jit(solution)/shard_map/ppermute | solution.py:346
  18.8 1.0 %collective-permute-done.5 = f32[1,4224]{1,0:T(1,128)S(1)} collective-permute-done((f32[1,4224]{1,0:T(1,128)S(1)}, f32[1,4224]{1,0:T(1,128)S(1)}, u32[]{:S(2)}, u32[]{:S(2)}) %collective-permute-start.5) | collective-permute-done | bytes 16928 | tf_op jit(solution)/shard_map/ppermute | solution.py:346
  19.8 0.0 collective-permute-done.6
  19.8 3.4 %collective-permute-start.7 = (f32[1,4224]{1,0:T(1,128)S(1)}, f32[1,4224]{1,0:T(1,128)S(1)}, u32[]{:S(2)}, u32[]{:S(2)}) collective-permute-start(f32[1,4224]{1,0:T(1,128)S(1)} %add_add_fusion.1.refs_3_), channel_id=1, source_target_pairs={{0,13},{1,12},{2,15},{3,14},{4,9},{5,8},{6,11},{7,10},{8,5},{9,4},... | collective-permute-start | bytes 50696 | tf_op jit(solution)/shard_map/ppermute | solution.py:346
  23.3 0.0 collective-permute-start.8
  23.3 0.6 %collective-permute-start.9 = (f32[1,4224]{1,0:T(1,128)S(1)}, f32[1,4224]{1,0:T(1,128)S(1)}, u32[]{:S(2)}, u32[]{:S(2)}) collective-permute-start(f32[1,4224]{1,0:T(1,128)S(1)} %add_add_fusion.1.refs_3_), channel_id=1, source_target_pairs={{0,5},{1,4},{2,7},{3,6},{4,1},{5,0},{6,3},{7,2},{8,13},{9,12},{10,... | collective-permute-start | bytes 50696 | tf_op jit(solution)/shard_map/ppermute | solution.py:346
  23.9 1.0 %collective-permute-done.7.refs_0_ = f32[1,4224]{1,0:T(1,128)S(1)} collective-permute-done((f32[1,4224]{1,0:T(1,128)S(1)}, f32[1,4224]{1,0:T(1,128)S(1)}, u32[]{:S(2)}, u32[]{:S(2)}) %collective-permute-start.7) | collective-permute-done | bytes 16928 | tf_op jit(solution)/shard_map/ppermute | solution.py:346
  24.9 2.5 %collective-permute-done.8.refs_1_ = f32[1,4224]{1,0:T(1,128)S(1)} collective-permute-done((f32[1,4224]{1,0:T(1,128)S(1)}, f32[1,4224]{1,0:T(1,128)S(1)}, u32[]{:S(2)}, u32[]{:S(2)}) %collective-permute-start.8) | collective-permute-done | bytes 16928 | tf_op jit(solution)/shard_map/ppermute | solution.py:346
  27.3 0.0 collective-permute-done.9.refs_2_
  27.3 1.2 %shard_map.74 = (f32[1,4224]{1,0:T(1,128)S(1)}, f32[8,128]{1,0:T(8,128)S(1)}, f32[1,4224]{1,0:T(1,128)S(1)}) custom-call(f32[1,4224]{1,0:T(1,128)S(1)} %collective-permute-done.7.refs_0_, f32[1,4224]{1,0:T(1,128)S(1)} %collective-permute-done.8.refs_1_, f32[1,4224]{1,0:T(1,128)S(1)} %collective-permute-done.9.refs_2_, f32[1,4224]{1,0:T(1,128)S(1)} %add_add_fusion.1.refs_3_, ...), custom_call_target="tpu_custom_call" | custom-call | tf_op jit(solution)/shard_map/pallas_call | solution.py:321
  28.5 1.7 %collective-permute-start.10 = (f32[1,4224]{1,0:T(1,128)S(1)}, f32[1,4224]{1,0:T(1,128)S(1)}, u32[]{:S(2)}, u32[]{:S(2)}) collective-permute-start(f32[1,4224]{1,0:T(1,128)S(1)} %get-tuple-element.39.refs_1_), channel_id=1, source_target_pairs={{0,17},{1,16},{2,19},{3,18},{4,21},{5,20},{6,23},{7,22},{8,25},{9,... | collective-permute-start | bytes 50696 | tf_op jit(solution)/shard_map/ppermute | solution.py:362
  30.2 1.5 %collective-permute-done.10.refs_0_ = f32[1,4224]{1,0:T(1,128)S(1)} collective-permute-done((f32[1,4224]{1,0:T(1,128)S(1)}, f32[1,4224]{1,0:T(1,128)S(1)}, u32[]{:S(2)}, u32[]{:S(2)}) %collective-permute-start.10) | collective-permute-done | bytes 16928 | tf_op jit(solution)/shard_map/ppermute | solution.py:362
  31.7 1.3 %shard_map.75 = (f32[16,512]{1,0:T(8,128)S(1)}, f32[8,128]{1,0:T(8,128)S(1)}, f32[1,4224]{1,0:T(1,128)S(1)}) custom-call(f32[1,4224]{1,0:T(1,128)S(1)} %collective-permute-done.10.refs_0_, f32[1,4224]{1,0:T(1,128)S(1)} %get-tuple-element.39.refs_1_, f32[1,512]{1,0:T(1,128)S(1)} %get-tuple-element.34.refs_2_, ...), custom_call_target="tpu_custom_call" | custom-call | tf_op jit(solution)/shard_map/pallas_call | solution.py:321
  33.0 0.7 %collective-permute-start.11 = (f32[1,4224]{1,0:T(1,128)S(1)}, f32[1,4224]{1,0:T(1,128)S(1)}, u32[]{:S(2)}, u32[]{:S(2)}) collective-permute-start(f32[1,4224]{1,0:T(1,128)S(1)} %get-tuple-element.42), channel_id=1, source_target_pairs={{0,2},{1,3},{2,0},{3,1},{4,6},{5,7},{6,4},{7,5},{8,10},{9,11},{10,... | collective-permute-start | bytes 50696 | tf_op jit(solution)/shard_map/ppermute | solution.py:346
  33.7 1.1 %collective-permute-start.12 = (f32[1,4224]{1,0:T(1,128)S(1)}, f32[1,4224]{1,0:T(1,128)S(1)}, u32[]{:S(2)}, u32[]{:S(2)}) collective-permute-start(f32[1,4224]{1,0:T(1,128)S(1)} %get-tuple-element.42), channel_id=1, source_target_pairs={{0,3},{1,2},{2,1},{3,0},{4,7},{5,6},{6,5},{7,4},{8,11},{9,10},{10,... | collective-permute-start | bytes 50696 | tf_op jit(solution)/shard_map/ppermute | solution.py:346
  34.8 0.4 collective-permute-start.13
  35.2 1.7 %collective-permute-done.11 = f32[1,4224]{1,0:T(1,128)S(1)} collective-permute-done((f32[1,4224]{1,0:T(1,128)S(1)}, f32[1,4224]{1,0:T(1,128)S(1)}, u32[]{:S(2)}, u32[]{:S(2)}) %collective-permute-start.11) | collective-permute-done | bytes 16928 | tf_op jit(solution)/shard_map/ppermute | solution.py:346
  36.9 0.1 collective-permute-done.12
  37.0 0.0 collective-permute-done.13
  37.0 1.4 %collective-permute-start.14 = (f32[1,4224]{1,0:T(1,128)S(1)}, f32[1,4224]{1,0:T(1,128)S(1)}, u32[]{:S(2)}, u32[]{:S(2)}) collective-permute-start(f32[1,4224]{1,0:T(1,128)S(1)} %add_add_fusion.refs_3_), channel_id=1, source_target_pairs={{0,13},{1,12},{2,15},{3,14},{4,9},{5,8},{6,11},{7,10},{8,5},{9,4},... | collective-permute-start | bytes 50696 | tf_op jit(solution)/shard_map/ppermute | solution.py:346
  38.4 0.6 %collective-permute-start.15 = (f32[1,4224]{1,0:T(1,128)S(1)}, f32[1,4224]{1,0:T(1,128)S(1)}, u32[]{:S(2)}, u32[]{:S(2)}) collective-permute-start(f32[1,4224]{1,0:T(1,128)S(1)} %add_add_fusion.refs_3_), channel_id=1, source_target_pairs={{0,9},{1,8},{2,11},{3,10},{4,13},{5,12},{6,15},{7,14},{8,1},{9,0},... | collective-permute-start | bytes 50696 | tf_op jit(solution)/shard_map/ppermute | solution.py:346
  39.0 1.9 %collective-permute-start.16 = (f32[1,4224]{1,0:T(1,128)S(1)}, f32[1,4224]{1,0:T(1,128)S(1)}, u32[]{:S(2)}, u32[]{:S(2)}) collective-permute-start(f32[1,4224]{1,0:T(1,128)S(1)} %add_add_fusion.refs_3_), channel_id=1, source_target_pairs={{0,5},{1,4},{2,7},{3,6},{4,1},{5,0},{6,3},{7,2},{8,13},{9,12},{10,... | collective-permute-start | bytes 50696 | tf_op jit(solution)/shard_map/ppermute | solution.py:346
  40.9 0.4 collective-permute-start.19
  41.4 0.7 %collective-permute-done.14.refs_0_ = f32[1,4224]{1,0:T(1,128)S(1)} collective-permute-done((f32[1,4224]{1,0:T(1,128)S(1)}, f32[1,4224]{1,0:T(1,128)S(1)}, u32[]{:S(2)}, u32[]{:S(2)}) %collective-permute-start.14) | collective-permute-done | bytes 16928 | tf_op jit(solution)/shard_map/ppermute | solution.py:346
  42.1 0.6 %collective-permute-done.15.refs_1_ = f32[1,4224]{1,0:T(1,128)S(1)} collective-permute-done((f32[1,4224]{1,0:T(1,128)S(1)}, f32[1,4224]{1,0:T(1,128)S(1)}, u32[]{:S(2)}, u32[]{:S(2)}) %collective-permute-start.15) | collective-permute-done | bytes 16928 | tf_op jit(solution)/shard_map/ppermute | solution.py:346
  42.7 0.1 collective-permute-done.16.refs_2_
  42.7 1.3 %shard_map.76 = (f32[8,256]{1,0:T(8,128)S(1)}, f32[1,4224]{1,0:T(1,128)S(1)}) custom-call(f32[1,4224]{1,0:T(1,128)S(1)} %collective-permute-done.14.refs_0_, f32[1,4224]{1,0:T(1,128)S(1)} %collective-permute-done.15.refs_1_, f32[1,4224]{1,0:T(1,128)S(1)} %collective-permute-done.16.refs_2_, f32[1,4224]{1,0:T(1,128)S(1)} %add_add_fusion.refs_3_, ...), custom_call_target="tpu_custom_call" | custom-call | tf_op jit(solution)/shard_map/pallas_call | solution.py:321
  44.0 1.6 %collective-permute-start.17 = (f32[1,4224]{1,0:T(1,128)S(1)}, f32[1,4224]{1,0:T(1,128)S(1)}, u32[]{:S(2)}, u32[]{:S(2)}) collective-permute-start(f32[1,4224]{1,0:T(1,128)S(1)} %get-tuple-element.44.refs_2_), channel_id=1, source_target_pairs={{0,16},{1,17},{2,18},{3,19},{4,20},{5,21},{6,22},{7,23},{8,24},{9,... | collective-permute-start | bytes 50696 | tf_op jit(solution)/shard_map/ppermute | solution.py:362
  45.6 0.0 collective-permute-start.18
  45.6 0.0 collective-permute-done.19.refs_3_
  45.6 1.6 %collective-permute-done.17.refs_0_ = f32[1,4224]{1,0:T(1,128)S(1)} collective-permute-done((f32[1,4224]{1,0:T(1,128)S(1)}, f32[1,4224]{1,0:T(1,128)S(1)}, u32[]{:S(2)}, u32[]{:S(2)}) %collective-permute-start.17) | collective-permute-done | bytes 16928 | tf_op jit(solution)/shard_map/ppermute | solution.py:362
  47.2 0.0 collective-permute-done.18.refs_1_
  47.2 0.7 %shard_map.77 = (f32[8,512]{1,0:T(8,128)}, f32[8,512]{1,0:T(8,128)}) custom-call(f32[1,4224]{1,0:T(1,128)S(1)} %collective-permute-done.17.refs_0_, f32[1,4224]{1,0:T(1,128)S(1)} %collective-permute-done.18.refs_1_, f32[1,4224]{1,0:T(1,128)S(1)} %get-tuple-element.44.refs_2_, f32[16,512]{1,0:T(8,128)S(1)} %collective-permute-done.19.refs_3_, ...), custom_call_target="tpu_custom_call" | custom-call | tf_op jit(solution)/shard_map/pallas_call | solution.py:321
  (2 shorter events, 0.1 us)
Async XLA Ops:
  2.2 5.2 %collective-permute-start.1 = (bf16[64,512]{1,0:T(8,128)(2,1)S(1)}, bf16[64,512]{1,0:T(8,128)(2,1)S(1)}, u32[]{:S(2)}, u32[]{:S(2)}) collective-permute-start(bf16[64,512]{1,0:T(8,128)(2,1)S(1)} %get-tuple-element.31), channel_id=1, source_target_pairs={{0,17},{1,16},{2,19},{3,18},{4,21},{5,20},{6,23},{7,22},{8,25},{9,... | collective-permute-start | bytes 196616 | tf_op jit(solution)/shard_map/ppermute | solution.py:362
  4.6 1.7 %collective-permute-start.2 = (s32[512]{0:T(512)}, s32[512]{0:T(512)S(1)}, u32[]{:S(2)}, u32[]{:S(2)}) collective-permute-start(s32[512]{0:T(512)} %param.8), channel_id=1, source_target_pairs={{0,1},{1,0},{2,3},{3,2},{4,5},{5,4},{6,7},{7,6},{8,9},{9,8},{10,11... | collective-permute-start | bytes 6152 | tf_op jit(solution)/shard_map/ppermute | solution.py:362
  5.3 1.5 %collective-permute-start = (f32[512]{0:T(512)}, f32[512]{0:T(512)S(1)}, u32[]{:S(2)}, u32[]{:S(2)}) collective-permute-start(f32[512]{0:T(512)} %param.9), channel_id=1, source_target_pairs={{0,1},{1,0},{2,3},{3,2},{4,5},{5,4},{6,7},{7,6},{8,9},{9,8},{10,11... | collective-permute-start | bytes 6152 | tf_op jit(solution)/shard_map/ppermute | solution.py:362
  10.0 3.8 %collective-permute-start.3 = (f32[8,512]{1,0:T(8,128)S(1)}, f32[8,512]{1,0:T(8,128)S(1)}, u32[]{:S(2)}, u32[]{:S(2)}) collective-permute-start(f32[8,512]{1,0:T(8,128)S(1)} %get-tuple-element.33.refs_1_), channel_id=1, source_target_pairs={{0,17},{1,16},{2,19},{3,18},{4,21},{5,20},{6,23},{7,22},{8,25},{9,... | collective-permute-start | bytes 49160 | tf_op jit(solution)/shard_map/ppermute | solution.py:362
  15.0 3.8 %collective-permute-start.4 = (f32[1,4224]{1,0:T(1,128)S(1)}, f32[1,4224]{1,0:T(1,128)S(1)}, u32[]{:S(2)}, u32[]{:S(2)}) collective-permute-start(f32[1,4224]{1,0:T(1,128)S(1)} %get-tuple-element.37), channel_id=1, source_target_pairs={{0,2},{1,3},{2,0},{3,1},{4,6},{5,7},{6,4},{7,5},{8,10},{9,11},{10,... | collective-permute-start | bytes 50696 | tf_op jit(solution)/shard_map/ppermute | solution.py:346
  16.6 3.2 %collective-permute-start.5 = (f32[1,4224]{1,0:T(1,128)S(1)}, f32[1,4224]{1,0:T(1,128)S(1)}, u32[]{:S(2)}, u32[]{:S(2)}) collective-permute-start(f32[1,4224]{1,0:T(1,128)S(1)} %get-tuple-element.37), channel_id=1, source_target_pairs={{0,3},{1,2},{2,1},{3,0},{4,7},{5,6},{6,5},{7,4},{8,11},{9,10},{10,... | collective-permute-start | bytes 50696 | tf_op jit(solution)/shard_map/ppermute | solution.py:346
  16.9 2.9 %collective-permute-start.6 = (f32[1,4224]{1,0:T(1,128)S(1)}, f32[1,4224]{1,0:T(1,128)S(1)}, u32[]{:S(2)}, u32[]{:S(2)}) collective-permute-start(f32[1,4224]{1,0:T(1,128)S(1)} %get-tuple-element.37), channel_id=1, source_target_pairs={{0,1},{1,0},{2,3},{3,2},{4,5},{5,4},{6,7},{7,6},{8,9},{9,8},{10,11... | collective-permute-start | bytes 50696 | tf_op jit(solution)/shard_map/ppermute | solution.py:346
  19.8 5.0 %collective-permute-start.7 = (f32[1,4224]{1,0:T(1,128)S(1)}, f32[1,4224]{1,0:T(1,128)S(1)}, u32[]{:S(2)}, u32[]{:S(2)}) collective-permute-start(f32[1,4224]{1,0:T(1,128)S(1)} %add_add_fusion.1.refs_3_), channel_id=1, source_target_pairs={{0,13},{1,12},{2,15},{3,14},{4,9},{5,8},{6,11},{7,10},{8,5},{9,4},... | collective-permute-start | bytes 50696 | tf_op jit(solution)/shard_map/ppermute | solution.py:346
  23.3 4.1 %collective-permute-start.8 = (f32[1,4224]{1,0:T(1,128)S(1)}, f32[1,4224]{1,0:T(1,128)S(1)}, u32[]{:S(2)}, u32[]{:S(2)}) collective-permute-start(f32[1,4224]{1,0:T(1,128)S(1)} %add_add_fusion.1.refs_3_), channel_id=1, source_target_pairs={{0,9},{1,8},{2,11},{3,10},{4,13},{5,12},{6,15},{7,14},{8,1},{9,0},... | collective-permute-start | bytes 50696 | tf_op jit(solution)/shard_map/ppermute | solution.py:346
  23.3 4.1 %collective-permute-start.9 = (f32[1,4224]{1,0:T(1,128)S(1)}, f32[1,4224]{1,0:T(1,128)S(1)}, u32[]{:S(2)}, u32[]{:S(2)}) collective-permute-start(f32[1,4224]{1,0:T(1,128)S(1)} %add_add_fusion.1.refs_3_), channel_id=1, source_target_pairs={{0,5},{1,4},{2,7},{3,6},{4,1},{5,0},{6,3},{7,2},{8,13},{9,12},{10,... | collective-permute-start | bytes 50696 | tf_op jit(solution)/shard_map/ppermute | solution.py:346
  28.5 3.2 %collective-permute-start.10 = (f32[1,4224]{1,0:T(1,128)S(1)}, f32[1,4224]{1,0:T(1,128)S(1)}, u32[]{:S(2)}, u32[]{:S(2)}) collective-permute-start(f32[1,4224]{1,0:T(1,128)S(1)} %get-tuple-element.39.refs_1_), channel_id=1, source_target_pairs={{0,17},{1,16},{2,19},{3,18},{4,21},{5,20},{6,23},{7,22},{8,25},{9,... | collective-permute-start | bytes 50696 | tf_op jit(solution)/shard_map/ppermute | solution.py:362
  33.0 3.9 %collective-permute-start.11 = (f32[1,4224]{1,0:T(1,128)S(1)}, f32[1,4224]{1,0:T(1,128)S(1)}, u32[]{:S(2)}, u32[]{:S(2)}) collective-permute-start(f32[1,4224]{1,0:T(1,128)S(1)} %get-tuple-element.42), channel_id=1, source_target_pairs={{0,2},{1,3},{2,0},{3,1},{4,6},{5,7},{6,4},{7,5},{8,10},{9,11},{10,... | collective-permute-start | bytes 50696 | tf_op jit(solution)/shard_map/ppermute | solution.py:346
  33.7 3.3 %collective-permute-start.12 = (f32[1,4224]{1,0:T(1,128)S(1)}, f32[1,4224]{1,0:T(1,128)S(1)}, u32[]{:S(2)}, u32[]{:S(2)}) collective-permute-start(f32[1,4224]{1,0:T(1,128)S(1)} %get-tuple-element.42), channel_id=1, source_target_pairs={{0,3},{1,2},{2,1},{3,0},{4,7},{5,6},{6,5},{7,4},{8,11},{9,10},{10,... | collective-permute-start | bytes 50696 | tf_op jit(solution)/shard_map/ppermute | solution.py:346
  34.8 2.2 %collective-permute-start.13 = (f32[1,4224]{1,0:T(1,128)S(1)}, f32[1,4224]{1,0:T(1,128)S(1)}, u32[]{:S(2)}, u32[]{:S(2)}) collective-permute-start(f32[1,4224]{1,0:T(1,128)S(1)} %get-tuple-element.42), channel_id=1, source_target_pairs={{0,1},{1,0},{2,3},{3,2},{4,5},{5,4},{6,7},{7,6},{8,9},{9,8},{10,11... | collective-permute-start | bytes 50696 | tf_op jit(solution)/shard_map/ppermute | solution.py:346
  37.0 5.0 %collective-permute-start.14 = (f32[1,4224]{1,0:T(1,128)S(1)}, f32[1,4224]{1,0:T(1,128)S(1)}, u32[]{:S(2)}, u32[]{:S(2)}) collective-permute-start(f32[1,4224]{1,0:T(1,128)S(1)} %add_add_fusion.refs_3_), channel_id=1, source_target_pairs={{0,13},{1,12},{2,15},{3,14},{4,9},{5,8},{6,11},{7,10},{8,5},{9,4},... | collective-permute-start | bytes 50696 | tf_op jit(solution)/shard_map/ppermute | solution.py:346
  38.4 4.2 %collective-permute-start.15 = (f32[1,4224]{1,0:T(1,128)S(1)}, f32[1,4224]{1,0:T(1,128)S(1)}, u32[]{:S(2)}, u32[]{:S(2)}) collective-permute-start(f32[1,4224]{1,0:T(1,128)S(1)} %add_add_fusion.refs_3_), channel_id=1, source_target_pairs={{0,9},{1,8},{2,11},{3,10},{4,13},{5,12},{6,15},{7,14},{8,1},{9,0},... | collective-permute-start | bytes 50696 | tf_op jit(solution)/shard_map/ppermute | solution.py:346
  39.0 3.7 %collective-permute-start.16 = (f32[1,4224]{1,0:T(1,128)S(1)}, f32[1,4224]{1,0:T(1,128)S(1)}, u32[]{:S(2)}, u32[]{:S(2)}) collective-permute-start(f32[1,4224]{1,0:T(1,128)S(1)} %add_add_fusion.refs_3_), channel_id=1, source_target_pairs={{0,5},{1,4},{2,7},{3,6},{4,1},{5,0},{6,3},{7,2},{8,13},{9,12},{10,... | collective-permute-start | bytes 50696 | tf_op jit(solution)/shard_map/ppermute | solution.py:346
  40.9 4.6 %collective-permute-start.19 = (f32[16,512]{1,0:T(8,128)S(1)}, f32[16,512]{1,0:T(8,128)S(1)}, u32[]{:S(2)}, u32[]{:S(2)}) collective-permute-start(f32[16,512]{1,0:T(8,128)S(1)} %get-tuple-element.45.refs_4_), channel_id=1, source_target_pairs={{0,1},{1,0},{2,3},{3,2},{4,5},{5,4},{6,7},{7,6},{8,9},{9,8},{10,11... | collective-permute-start | bytes 98312 | tf_op jit(solution)/shard_map/ppermute | solution.py:362
  44.0 3.2 %collective-permute-start.17 = (f32[1,4224]{1,0:T(1,128)S(1)}, f32[1,4224]{1,0:T(1,128)S(1)}, u32[]{:S(2)}, u32[]{:S(2)}) collective-permute-start(f32[1,4224]{1,0:T(1,128)S(1)} %get-tuple-element.44.refs_2_), channel_id=1, source_target_pairs={{0,16},{1,17},{2,18},{3,19},{4,20},{5,21},{6,22},{7,23},{8,24},{9,... | collective-permute-start | bytes 50696 | tf_op jit(solution)/shard_map/ppermute | solution.py:362
  45.6 1.6 %collective-permute-start.18 = (f32[1,4224]{1,0:T(1,128)S(1)}, f32[1,4224]{1,0:T(1,128)S(1)}, u32[]{:S(2)}, u32[]{:S(2)}) collective-permute-start(f32[1,4224]{1,0:T(1,128)S(1)} %get-tuple-element.44.refs_2_), channel_id=1, source_target_pairs={{0,1},{1,0},{2,3},{3,2},{4,5},{5,4},{6,7},{7,6},{8,9},{9,8},{10,11... | collective-permute-start | bytes 50696 | tf_op jit(solution)/shard_map/ppermute | solution.py:362

commit v28 on v25

--- a/solution.py
+++ b/solution.py
@@ -332,7 +332,7 @@
         span = min(4, size // stride)
         side = 0 if stride == 1 else 1
         parts = [value]
-        offsets = (1, 3, 2) if stride == 1 else (1, 2, 3)
+        offsets = (3, 1, 2) if stride == 1 else (1, 2, 3)
         for offset in offsets[: span - 1]:
             pairs = [(i, i ^ (offset * stride) ^ side) for i in range(size)]
             parts.insert(0, lax.ppermute(value, axis, pairs))

time: 48 us -> 48.7 us (1.015)
  waiting for transfers between devices: 13.3 us -> 14.6 us
  starting transfers between devices: 21.1 us -> 20.5 us
    ppermute x8, starting transfers between devices: 8.72 us -> 7.86 us  [moved(): return lax.ppermute(value, ('dp', 'centers'), pairs_over(target_of))]
    ppermute x12, waiting for transfers between devices: 9.18 us -> 9.85 us  [exchange(): parts.insert(0, lax.ppermute(value, axis, pairs))]
    ppermute x8, waiting for transfers between devices: 4.12 us -> 4.75 us  [moved(): return lax.ppermute(value, ('dp', 'centers'), pairs_over(target_of))]
  transfers between devices with their start and end apart: 20 -> 20, of which waited for: 13 -> 12; matrix products, arithmetic and copies ran while one was open for 0% -> 0% of each run, Pallas kernels for 9% -> 9%
where the time goes in v28:
time: 48.7 us; the launch traced here: 48.5 us
  starting transfers between devices  20.5 us (42%)
  waiting for transfers between devices  14.6 us (30%)
  Pallas kernels  12.7 us (26%)
  between operations  0.72 us (1%)
    pallas_call x10, Pallas kernels, call(): pl.pallas_call(body, out_shape=out_shape, in_specs=sources or [VMEM] * le...  12.7 us
    ppermute x12, starting transfers between devices, exchange(): parts.insert(0, lax.ppermute(value, axis, pairs))  12.6 us
    ppermute x12, waiting for transfers between devices, exchange(): parts.insert(0, lax.ppermute(value, axis, pairs))  9.85 us
    ppermute x8, starting transfers between devices, moved(): return lax.ppermute(value, ('dp', 'centers'), pairs_over(target_of))  7.86 us
    ppermute x8, waiting for transfers between devices, moved(): return lax.ppermute(value, ('dp', 'centers'), pairs_over(target_of))  4.75 us
  transfers between devices with their start and end apart: 20, of which 12 were waited for; matrix products, arithmetic and copies ran while one was open for 0% of the time, Pallas kernels for 9%

profile of v28, /device:TPU:0, one launch (start us, length us, event | category | flops | bytes accessed | tf_op | source)
XLA Modules:
  0.0 48.5 jit_solution(14859212172406684326)
XLA Ops:
  0.6 1.6 %shard_map.68 = (bf16[64,4096]{1,0:T(8,128)(2,1)S(1)}, s32[1,512]{1,0:T(1,128)S(1)}, s32[1,4096]{1,0:T(1,128)S(1)}, f32[1,4096]{1,0:T(1,128)S(1)}, f32[1,512]{1,0:T(1,128)S(1)}, /*index=5*/bf16[64,512]{1,0:T(8,128)(2,1)S(1)}) custom-call(bf16[64,4096]{1,0:T(8,128)(2,1)} %feat_hbm.1, s32[1,512]{1,0:T(1,128)} %bitcast.10, s32[1,4096]{1,0:T(1,128)} %bitcast.8, ...), custom_call_target="tpu_custom_call" | custom-call | tf_op jit(solution)/shard_map/pallas_call | solution.py:313
  2.2 2.4 %collective-permute-start.1 = (bf16[64,512]{1,0:T(8,128)(2,1)S(1)}, bf16[64,512]{1,0:T(8,128)(2,1)S(1)}, u32[]{:S(2)}, u32[]{:S(2)}) collective-permute-start(bf16[64,512]{1,0:T(8,128)(2,1)S(1)} %get-tuple-element.31), channel_id=1, source_target_pairs={{0,17},{1,16},{2,19},{3,18},{4,21},{5,20},{6,23},{7,22},{8,25},{9,... | collective-permute-start | bytes 196616 | tf_op jit(solution)/shard_map/ppermute | solution.py:354
  4.6 0.7 %collective-permute-start.2 = (s32[512]{0:T(512)}, s32[512]{0:T(512)S(1)}, u32[]{:S(2)}, u32[]{:S(2)}) collective-permute-start(s32[512]{0:T(512)} %param.8), channel_id=1, source_target_pairs={{0,1},{1,0},{2,3},{3,2},{4,5},{5,4},{6,7},{7,6},{8,9},{9,8},{10,11... | collective-permute-start | bytes 6152 | tf_op jit(solution)/shard_map/ppermute | solution.py:354
  5.3 0.0 collective-permute-start
  5.3 0.7 %shard_map.69 = (bf16[256,4096]{1,0:T(8,128)(2,1)S(1)}, bf16[4096,256]{1,0:T(8,128)(2,1)S(1)}, bf16[16,4096]{1,0:T(8,128)(2,1)S(1)}) custom-call(bf16[64,4096]{1,0:T(8,128)(2,1)S(1)} %get-tuple-element.25.feat_ref, s32[1,4096]{1,0:T(1,128)S(1)} %get-tuple-element.26.slots_ref.refs_3_.refs_4_, f32[1,4096]{1,0:T(1,128)S(1)} %get-tuple-element.27.prices_ref), custom_call_target="tpu_custom_call" | custom-call | flops 4096000 | bytes 4194304 | tf_op jit(solution)/shard_map/pallas_call | solution.py:313
  6.0 0.4 collective-permute-done.2
  6.3 0.5 shard_map.70.refs_1_
  6.8 0.0 collective-permute-done
  6.8 0.6 %collective-permute-done.1.refs_0_ = bf16[64,512]{1,0:T(8,128)(2,1)S(1)} collective-permute-done((bf16[64,512]{1,0:T(8,128)(2,1)S(1)}, bf16[64,512]{1,0:T(8,128)(2,1)S(1)}, u32[]{:S(2)}, u32[]{:S(2)}) %collective-permute-start.1) | collective-permute-done | bytes 65568 | tf_op jit(solution)/shard_map/ppermute | solution.py:354
  7.4 2.5 %shard_map.71 = (bf16[8192,512]{1,0:T(8,128)(2,1)S(1)}, bf16[256,512]{1,0:T(8,128)(2,1)S(1)}, f32[1,512]{1,0:T(1,128)S(1)}, f32[8,512]{1,0:T(8,128)S(1)}) custom-call(bf16[4096,256]{1,0:T(8,128)(2,1)S(1)} %get-tuple-element.28.turned_ref, bf16[16,4096]{1,0:T(8,128)(2,1)S(1)} %get-tuple-element.29.weight_ref, f32[1,512]{1,0:T(1,128)S(1)} %bitcast.6, ...), custom_call_target="tpu_custom_call" | custom-call | flops 134217728 | bytes 8388608 | tf_op jit(solution)/shard_map/pallas_call | solution.py:313
  10.0 1.9 %collective-permute-start.3 = (f32[8,512]{1,0:T(8,128)S(1)}, f32[8,512]{1,0:T(8,128)S(1)}, u32[]{:S(2)}, u32[]{:S(2)}) collective-permute-start(f32[8,512]{1,0:T(8,128)S(1)} %get-tuple-element.33.refs_1_), channel_id=1, source_target_pairs={{0,17},{1,16},{2,19},{3,18},{4,21},{5,20},{6,23},{7,22},{8,25},{9,... | collective-permute-start | bytes 49160 | tf_op jit(solution)/shard_map/ppermute | solution.py:354
  11.9 1.9 %shard_map.72.refs_4_ = bf16[1024,4096]{1,0:T(8,128)(2,1)S(1)} custom-call(bf16[256,4096]{1,0:T(8,128)(2,1)S(1)} %get-tuple-element.35.columns_ref, bf16[256,512]{1,0:T(8,128)(2,1)S(1)} %get-tuple-element.36.center_ref), custom_call_target="tpu_custom_call" | custom-call | flops 134217728 | bytes 8388608 | tf_op jit(solution)/shard_map/pallas_call | solution.py:313
  13.8 0.0 collective-permute-done.3.refs_0_
  13.8 1.2 %shard_map.73 = (f32[8,512]{1,0:T(8,128)S(1)}, f32[1,4224]{1,0:T(1,128)S(1)}) custom-call(f32[8,512]{1,0:T(8,128)S(1)} %collective-permute-done.3.refs_0_, f32[8,512]{1,0:T(8,128)S(1)} %get-tuple-element.33.refs_1_, f32[1,512]{1,0:T(1,128)S(1)} %get-tuple-element.34.refs_2_, s32[1,4096]{1,0:T(1,128)S(1)} %get-tuple-element.26.slots_ref.refs_3_.refs_4_, ...), custom_call_target="tpu_custom_call" | custom-call | tf_op jit(solution)/shard_map/pallas_call | solution.py:313
  15.0 1.6 %collective-permute-start.4 = (f32[1,4224]{1,0:T(1,128)S(1)}, f32[1,4224]{1,0:T(1,128)S(1)}, u32[]{:S(2)}, u32[]{:S(2)}) collective-permute-start(f32[1,4224]{1,0:T(1,128)S(1)} %get-tuple-element.37), channel_id=1, source_target_pairs={{0,2},{1,3},{2,0},{3,1},{4,6},{5,7},{6,4},{7,5},{8,10},{9,11},{10,... | collective-permute-start | bytes 50696 | tf_op jit(solution)/shard_map/ppermute | solution.py:338
  16.6 0.1 collective-permute-start.5
  16.8 0.5 collective-permute-start.6
  17.2 1.6 %collective-permute-done.4 = f32[1,4224]{1,0:T(1,128)S(1)} collective-permute-done((f32[1,4224]{1,0:T(1,128)S(1)}, f32[1,4224]{1,0:T(1,128)S(1)}, u32[]{:S(2)}, u32[]{:S(2)}) %collective-permute-start.4) | collective-permute-done | bytes 16928 | tf_op jit(solution)/shard_map/ppermute | solution.py:338
  18.8 0.0 collective-permute-done.5
  18.8 1.1 %collective-permute-done.6 = f32[1,4224]{1,0:T(1,128)S(1)} collective-permute-done((f32[1,4224]{1,0:T(1,128)S(1)}, f32[1,4224]{1,0:T(1,128)S(1)}, u32[]{:S(2)}, u32[]{:S(2)}) %collective-permute-start.6) | collective-permute-done | bytes 16928 | tf_op jit(solution)/shard_map/ppermute | solution.py:338
  20.0 3.6 %collective-permute-start.7 = (f32[1,4224]{1,0:T(1,128)S(1)}, f32[1,4224]{1,0:T(1,128)S(1)}, u32[]{:S(2)}, u32[]{:S(2)}) collective-permute-start(f32[1,4224]{1,0:T(1,128)S(1)} %add_add_fusion.1.refs_3_), channel_id=1, source_target_pairs={{0,13},{1,12},{2,15},{3,14},{4,9},{5,8},{6,11},{7,10},{8,5},{9,4},... | collective-permute-start | bytes 50696 | tf_op jit(solution)/shard_map/ppermute | solution.py:338
  23.6 0.0 collective-permute-start.8
  23.6 0.5 %collective-permute-start.9 = (f32[1,4224]{1,0:T(1,128)S(1)}, f32[1,4224]{1,0:T(1,128)S(1)}, u32[]{:S(2)}, u32[]{:S(2)}) collective-permute-start(f32[1,4224]{1,0:T(1,128)S(1)} %add_add_fusion.1.refs_3_), channel_id=1, source_target_pairs={{0,5},{1,4},{2,7},{3,6},{4,1},{5,0},{6,3},{7,2},{8,13},{9,12},{10,... | collective-permute-start | bytes 50696 | tf_op jit(solution)/shard_map/ppermute | solution.py:338
  24.1 1.0 %collective-permute-done.7.refs_0_ = f32[1,4224]{1,0:T(1,128)S(1)} collective-permute-done((f32[1,4224]{1,0:T(1,128)S(1)}, f32[1,4224]{1,0:T(1,128)S(1)}, u32[]{:S(2)}, u32[]{:S(2)}) %collective-permute-start.7) | collective-permute-done | bytes 16928 | tf_op jit(solution)/shard_map/ppermute | solution.py:338
  25.1 2.6 %collective-permute-done.8.refs_1_ = f32[1,4224]{1,0:T(1,128)S(1)} collective-permute-done((f32[1,4224]{1,0:T(1,128)S(1)}, f32[1,4224]{1,0:T(1,128)S(1)}, u32[]{:S(2)}, u32[]{:S(2)}) %collective-permute-start.8) | collective-permute-done | bytes 16928 | tf_op jit(solution)/shard_map/ppermute | solution.py:338
  27.7 0.0 collective-permute-done.9.refs_2_
  27.7 1.2 %shard_map.74 = (f32[1,4224]{1,0:T(1,128)S(1)}, f32[8,128]{1,0:T(8,128)S(1)}, f32[8,640]{1,0:T(8,128)S(1)}) custom-call(f32[1,4224]{1,0:T(1,128)S(1)} %collective-permute-done.7.refs_0_, f32[1,4224]{1,0:T(1,128)S(1)} %collective-permute-done.8.refs_1_, f32[1,4224]{1,0:T(1,128)S(1)} %collective-permute-done.9.refs_2_, f32[1,4224]{1,0:T(1,128)S(1)} %add_add_fusion.1.refs_3_, ...), custom_call_target="tpu_custom_call" | custom-call | tf_op jit(solution)/shard_map/pallas_call | solution.py:313
  28.9 1.3 %collective-permute-start.10 = (f32[8,640]{1,0:T(8,128)S(1)}, f32[8,640]{1,0:T(8,128)S(1)}, u32[]{:S(2)}, u32[]{:S(2)}) collective-permute-start(f32[8,640]{1,0:T(8,128)S(1)} %get-tuple-element.39.refs_1_), channel_id=1, source_target_pairs={{0,17},{1,16},{2,19},{3,18},{4,21},{5,20},{6,23},{7,22},{8,25},{9,... | collective-permute-start | bytes 61448 | tf_op jit(solution)/shard_map/ppermute | solution.py:354
  30.1 2.0 %collective-permute-done.10.refs_0_ = f32[8,640]{1,0:T(8,128)S(1)} collective-permute-done((f32[8,640]{1,0:T(8,128)S(1)}, f32[8,640]{1,0:T(8,128)S(1)}, u32[]{:S(2)}, u32[]{:S(2)}) %collective-permute-start.10) | collective-permute-done | bytes 20512 | tf_op jit(solution)/shard_map/ppermute | solution.py:354
  32.1 1.2 %shard_map.75 = (f32[16,512]{1,0:T(8,128)S(1)}, f32[8,128]{1,0:T(8,128)S(1)}, f32[1,4224]{1,0:T(1,128)S(1)}) custom-call(f32[8,640]{1,0:T(8,128)S(1)} %collective-permute-done.10.refs_0_, f32[8,640]{1,0:T(8,128)S(1)} %get-tuple-element.39.refs_1_, f32[1,512]{1,0:T(1,128)S(1)} %get-tuple-element.34.refs_2_, ...), custom_call_target="tpu_custom_call" | custom-call | tf_op jit(solution)/shard_map/pallas_call | solution.py:313
  33.3 0.6 %collective-permute-start.11 = (f32[1,4224]{1,0:T(1,128)S(1)}, f32[1,4224]{1,0:T(1,128)S(1)}, u32[]{:S(2)}, u32[]{:S(2)}) collective-permute-start(f32[1,4224]{1,0:T(1,128)S(1)} %get-tuple-element.42), channel_id=1, source_target_pairs={{0,2},{1,3},{2,0},{3,1},{4,6},{5,7},{6,4},{7,5},{8,10},{9,11},{10,... | collective-permute-start | bytes 50696 | tf_op jit(solution)/shard_map/ppermute | solution.py:338
  33.9 0.0 collective-permute-start.12
  33.9 1.6 %collective-permute-start.13 = (f32[1,4224]{1,0:T(1,128)S(1)}, f32[1,4224]{1,0:T(1,128)S(1)}, u32[]{:S(2)}, u32[]{:S(2)}) collective-permute-start(f32[1,4224]{1,0:T(1,128)S(1)} %get-tuple-element.42), channel_id=1, source_target_pairs={{0,3},{1,2},{2,1},{3,0},{4,7},{5,6},{6,5},{7,4},{8,11},{9,10},{10,... | collective-permute-start | bytes 50696 | tf_op jit(solution)/shard_map/ppermute | solution.py:338
  35.5 1.7 %collective-permute-done.11 = f32[1,4224]{1,0:T(1,128)S(1)} collective-permute-done((f32[1,4224]{1,0:T(1,128)S(1)}, f32[1,4224]{1,0:T(1,128)S(1)}, u32[]{:S(2)}, u32[]{:S(2)}) %collective-permute-start.11) | collective-permute-done | bytes 16928 | tf_op jit(solution)/shard_map/ppermute | solution.py:338
  37.2 0.0 collective-permute-done.12
  37.2 0.0 collective-permute-done.13
  37.3 1.6 %collective-permute-start.14 = (f32[1,4224]{1,0:T(1,128)S(1)}, f32[1,4224]{1,0:T(1,128)S(1)}, u32[]{:S(2)}, u32[]{:S(2)}) collective-permute-start(f32[1,4224]{1,0:T(1,128)S(1)} %add_add_fusion.refs_3_), channel_id=1, source_target_pairs={{0,13},{1,12},{2,15},{3,14},{4,9},{5,8},{6,11},{7,10},{8,5},{9,4},... | collective-permute-start | bytes 50696 | tf_op jit(solution)/shard_map/ppermute | solution.py:338
  38.9 0.3 collective-permute-start.15
  39.2 2.2 %collective-permute-start.16 = (f32[1,4224]{1,0:T(1,128)S(1)}, f32[1,4224]{1,0:T(1,128)S(1)}, u32[]{:S(2)}, u32[]{:S(2)}) collective-permute-start(f32[1,4224]{1,0:T(1,128)S(1)} %add_add_fusion.refs_3_), channel_id=1, source_target_pairs={{0,5},{1,4},{2,7},{3,6},{4,1},{5,0},{6,3},{7,2},{8,13},{9,12},{10,... | collective-permute-start | bytes 50696 | tf_op jit(solution)/shard_map/ppermute | solution.py:338
  41.4 0.2 collective-permute-start.19
  41.6 0.7 %collective-permute-done.14.refs_0_ = f32[1,4224]{1,0:T(1,128)S(1)} collective-permute-done((f32[1,4224]{1,0:T(1,128)S(1)}, f32[1,4224]{1,0:T(1,128)S(1)}, u32[]{:S(2)}, u32[]{:S(2)}) %collective-permute-start.14) | collective-permute-done | bytes 16928 | tf_op jit(solution)/shard_map/ppermute | solution.py:338
  42.3 0.8 %collective-permute-done.15.refs_1_ = f32[1,4224]{1,0:T(1,128)S(1)} collective-permute-done((f32[1,4224]{1,0:T(1,128)S(1)}, f32[1,4224]{1,0:T(1,128)S(1)}, u32[]{:S(2)}, u32[]{:S(2)}) %collective-permute-start.15) | collective-permute-done | bytes 16928 | tf_op jit(solution)/shard_map/ppermute | solution.py:338
  43.1 0.3 collective-permute-done.16.refs_2_
  43.4 1.3 %shard_map.76 = (f32[8,256]{1,0:T(8,128)S(1)}, f32[8,640]{1,0:T(8,128)S(1)}) custom-call(f32[1,4224]{1,0:T(1,128)S(1)} %collective-permute-done.14.refs_0_, f32[1,4224]{1,0:T(1,128)S(1)} %collective-permute-done.15.refs_1_, f32[1,4224]{1,0:T(1,128)S(1)} %collective-permute-done.16.refs_2_, f32[1,4224]{1,0:T(1,128)S(1)} %add_add_fusion.refs_3_, ...), custom_call_target="tpu_custom_call" | custom-call | tf_op jit(solution)/shard_map/pallas_call | solution.py:313
  44.7 1.4 %collective-permute-start.17 = (f32[8,640]{1,0:T(8,128)S(1)}, f32[8,640]{1,0:T(8,128)S(1)}, u32[]{:S(2)}, u32[]{:S(2)}) collective-permute-start(f32[8,640]{1,0:T(8,128)S(1)} %get-tuple-element.44.refs_2_), channel_id=1, source_target_pairs={{0,16},{1,17},{2,18},{3,19},{4,20},{5,21},{6,22},{7,23},{8,24},{9,... | collective-permute-start | bytes 61448 | tf_op jit(solution)/shard_map/ppermute | solution.py:354
  46.1 0.0 collective-permute-start.18
  46.1 0.0 collective-permute-done.19.refs_3_
  46.1 1.8 %collective-permute-done.17.refs_0_ = f32[8,640]{1,0:T(8,128)S(1)} collective-permute-done((f32[8,640]{1,0:T(8,128)S(1)}, f32[8,640]{1,0:T(8,128)S(1)}, u32[]{:S(2)}, u32[]{:S(2)}) %collective-permute-start.17) | collective-permute-done | bytes 20512 | tf_op jit(solution)/shard_map/ppermute | solution.py:354
  47.9 0.0 collective-permute-done.18.refs_1_
  47.9 0.6 %shard_map.77 = (f32[8,512]{1,0:T(8,128)}, f32[8,512]{1,0:T(8,128)}) custom-call(f32[8,640]{1,0:T(8,128)S(1)} %collective-permute-done.17.refs_0_, f32[8,640]{1,0:T(8,128)S(1)} %collective-permute-done.18.refs_1_, f32[8,640]{1,0:T(8,128)S(1)} %get-tuple-element.44.refs_2_, f32[16,512]{1,0:T(8,128)S(1)} %collective-permute-done.19.refs_3_, ...), custom_call_target="tpu_custom_call" | custom-call | tf_op jit(solution)/shard_map/pallas_call | solution.py:313
  (2 shorter events, 0.1 us)
Async XLA Ops:
  2.2 5.2 %collective-permute-start.1 = (bf16[64,512]{1,0:T(8,128)(2,1)S(1)}, bf16[64,512]{1,0:T(8,128)(2,1)S(1)}, u32[]{:S(2)}, u32[]{:S(2)}) collective-permute-start(bf16[64,512]{1,0:T(8,128)(2,1)S(1)} %get-tuple-element.31), channel_id=1, source_target_pairs={{0,17},{1,16},{2,19},{3,18},{4,21},{5,20},{6,23},{7,22},{8,25},{9,... | collective-permute-start | bytes 196616 | tf_op jit(solution)/shard_map/ppermute | solution.py:354
  4.6 1.7 %collective-permute-start.2 = (s32[512]{0:T(512)}, s32[512]{0:T(512)S(1)}, u32[]{:S(2)}, u32[]{:S(2)}) collective-permute-start(s32[512]{0:T(512)} %param.8), channel_id=1, source_target_pairs={{0,1},{1,0},{2,3},{3,2},{4,5},{5,4},{6,7},{7,6},{8,9},{9,8},{10,11... | collective-permute-start | bytes 6152 | tf_op jit(solution)/shard_map/ppermute | solution.py:354
  5.3 1.5 %collective-permute-start = (f32[512]{0:T(512)}, f32[512]{0:T(512)S(1)}, u32[]{:S(2)}, u32[]{:S(2)}) collective-permute-start(f32[512]{0:T(512)} %param.9), channel_id=1, source_target_pairs={{0,1},{1,0},{2,3},{3,2},{4,5},{5,4},{6,7},{7,6},{8,9},{9,8},{10,11... | collective-permute-start | bytes 6152 | tf_op jit(solution)/shard_map/ppermute | solution.py:354
  10.0 3.8 %collective-permute-start.3 = (f32[8,512]{1,0:T(8,128)S(1)}, f32[8,512]{1,0:T(8,128)S(1)}, u32[]{:S(2)}, u32[]{:S(2)}) collective-permute-start(f32[8,512]{1,0:T(8,128)S(1)} %get-tuple-element.33.refs_1_), channel_id=1, source_target_pairs={{0,17},{1,16},{2,19},{3,18},{4,21},{5,20},{6,23},{7,22},{8,25},{9,... | collective-permute-start | bytes 49160 | tf_op jit(solution)/shard_map/ppermute | solution.py:354
  15.0 3.8 %collective-permute-start.4 = (f32[1,4224]{1,0:T(1,128)S(1)}, f32[1,4224]{1,0:T(1,128)S(1)}, u32[]{:S(2)}, u32[]{:S(2)}) collective-permute-start(f32[1,4224]{1,0:T(1,128)S(1)} %get-tuple-element.37), channel_id=1, source_target_pairs={{0,2},{1,3},{2,0},{3,1},{4,6},{5,7},{6,4},{7,5},{8,10},{9,11},{10,... | collective-permute-start | bytes 50696 | tf_op jit(solution)/shard_map/ppermute | solution.py:338
  16.6 2.2 %collective-permute-start.5 = (f32[1,4224]{1,0:T(1,128)S(1)}, f32[1,4224]{1,0:T(1,128)S(1)}, u32[]{:S(2)}, u32[]{:S(2)}) collective-permute-start(f32[1,4224]{1,0:T(1,128)S(1)} %get-tuple-element.37), channel_id=1, source_target_pairs={{0,1},{1,0},{2,3},{3,2},{4,5},{5,4},{6,7},{7,6},{8,9},{9,8},{10,11... | collective-permute-start | bytes 50696 | tf_op jit(solution)/shard_map/ppermute | solution.py:338
  16.8 3.2 %collective-permute-start.6 = (f32[1,4224]{1,0:T(1,128)S(1)}, f32[1,4224]{1,0:T(1,128)S(1)}, u32[]{:S(2)}, u32[]{:S(2)}) collective-permute-start(f32[1,4224]{1,0:T(1,128)S(1)} %get-tuple-element.37), channel_id=1, source_target_pairs={{0,3},{1,2},{2,1},{3,0},{4,7},{5,6},{6,5},{7,4},{8,11},{9,10},{10,... | collective-permute-start | bytes 50696 | tf_op jit(solution)/shard_map/ppermute | solution.py:338
  20.0 5.1 %collective-permute-start.7 = (f32[1,4224]{1,0:T(1,128)S(1)}, f32[1,4224]{1,0:T(1,128)S(1)}, u32[]{:S(2)}, u32[]{:S(2)}) collective-permute-start(f32[1,4224]{1,0:T(1,128)S(1)} %add_add_fusion.1.refs_3_), channel_id=1, source_target_pairs={{0,13},{1,12},{2,15},{3,14},{4,9},{5,8},{6,11},{7,10},{8,5},{9,4},... | collective-permute-start | bytes 50696 | tf_op jit(solution)/shard_map/ppermute | solution.py:338
  23.6 4.1 %collective-permute-start.8 = (f32[1,4224]{1,0:T(1,128)S(1)}, f32[1,4224]{1,0:T(1,128)S(1)}, u32[]{:S(2)}, u32[]{:S(2)}) collective-permute-start(f32[1,4224]{1,0:T(1,128)S(1)} %add_add_fusion.1.refs_3_), channel_id=1, source_target_pairs={{0,9},{1,8},{2,11},{3,10},{4,13},{5,12},{6,15},{7,14},{8,1},{9,0},... | collective-permute-start | bytes 50696 | tf_op jit(solution)/shard_map/ppermute | solution.py:338
  23.6 4.1 %collective-permute-start.9 = (f32[1,4224]{1,0:T(1,128)S(1)}, f32[1,4224]{1,0:T(1,128)S(1)}, u32[]{:S(2)}, u32[]{:S(2)}) collective-permute-start(f32[1,4224]{1,0:T(1,128)S(1)} %add_add_fusion.1.refs_3_), channel_id=1, source_target_pairs={{0,5},{1,4},{2,7},{3,6},{4,1},{5,0},{6,3},{7,2},{8,13},{9,12},{10,... | collective-permute-start | bytes 50696 | tf_op jit(solution)/shard_map/ppermute | solution.py:338
  28.9 3.2 %collective-permute-start.10 = (f32[8,640]{1,0:T(8,128)S(1)}, f32[8,640]{1,0:T(8,128)S(1)}, u32[]{:S(2)}, u32[]{:S(2)}) collective-permute-start(f32[8,640]{1,0:T(8,128)S(1)} %get-tuple-element.39.refs_1_), channel_id=1, source_target_pairs={{0,17},{1,16},{2,19},{3,18},{4,21},{5,20},{6,23},{7,22},{8,25},{9,... | collective-permute-start | bytes 61448 | tf_op jit(solution)/shard_map/ppermute | solution.py:354
  33.3 3.9 %collective-permute-start.11 = (f32[1,4224]{1,0:T(1,128)S(1)}, f32[1,4224]{1,0:T(1,128)S(1)}, u32[]{:S(2)}, u32[]{:S(2)}) collective-permute-start(f32[1,4224]{1,0:T(1,128)S(1)} %get-tuple-element.42), channel_id=1, source_target_pairs={{0,2},{1,3},{2,0},{3,1},{4,6},{5,7},{6,4},{7,5},{8,10},{9,11},{10,... | collective-permute-start | bytes 50696 | tf_op jit(solution)/shard_map/ppermute | solution.py:338
  33.9 3.4 %collective-permute-start.12 = (f32[1,4224]{1,0:T(1,128)S(1)}, f32[1,4224]{1,0:T(1,128)S(1)}, u32[]{:S(2)}, u32[]{:S(2)}) collective-permute-start(f32[1,4224]{1,0:T(1,128)S(1)} %get-tuple-element.42), channel_id=1, source_target_pairs={{0,1},{1,0},{2,3},{3,2},{4,5},{5,4},{6,7},{7,6},{8,9},{9,8},{10,11... | collective-permute-start | bytes 50696 | tf_op jit(solution)/shard_map/ppermute | solution.py:338
  33.9 3.4 %collective-permute-start.13 = (f32[1,4224]{1,0:T(1,128)S(1)}, f32[1,4224]{1,0:T(1,128)S(1)}, u32[]{:S(2)}, u32[]{:S(2)}) collective-permute-start(f32[1,4224]{1,0:T(1,128)S(1)} %get-tuple-element.42), channel_id=1, source_target_pairs={{0,3},{1,2},{2,1},{3,0},{4,7},{5,6},{6,5},{7,4},{8,11},{9,10},{10,... | collective-permute-start | bytes 50696 | tf_op jit(solution)/shard_map/ppermute | solution.py:338
  37.3 5.0 %collective-permute-start.14 = (f32[1,4224]{1,0:T(1,128)S(1)}, f32[1,4224]{1,0:T(1,128)S(1)}, u32[]{:S(2)}, u32[]{:S(2)}) collective-permute-start(f32[1,4224]{1,0:T(1,128)S(1)} %add_add_fusion.refs_3_), channel_id=1, source_target_pairs={{0,13},{1,12},{2,15},{3,14},{4,9},{5,8},{6,11},{7,10},{8,5},{9,4},... | collective-permute-start | bytes 50696 | tf_op jit(solution)/shard_map/ppermute | solution.py:338
  38.9 4.2 %collective-permute-start.15 = (f32[1,4224]{1,0:T(1,128)S(1)}, f32[1,4224]{1,0:T(1,128)S(1)}, u32[]{:S(2)}, u32[]{:S(2)}) collective-permute-start(f32[1,4224]{1,0:T(1,128)S(1)} %add_add_fusion.refs_3_), channel_id=1, source_target_pairs={{0,9},{1,8},{2,11},{3,10},{4,13},{5,12},{6,15},{7,14},{8,1},{9,0},... | collective-permute-start | bytes 50696 | tf_op jit(solution)/shard_map/ppermute | solution.py:338
  39.2 4.2 %collective-permute-start.16 = (f32[1,4224]{1,0:T(1,128)S(1)}, f32[1,4224]{1,0:T(1,128)S(1)}, u32[]{:S(2)}, u32[]{:S(2)}) collective-permute-start(f32[1,4224]{1,0:T(1,128)S(1)} %add_add_fusion.refs_3_), channel_id=1, source_target_pairs={{0,5},{1,4},{2,7},{3,6},{4,1},{5,0},{6,3},{7,2},{8,13},{9,12},{10,... | collective-permute-start | bytes 50696 | tf_op jit(solution)/shard_map/ppermute | solution.py:338
  41.4 4.7 %collective-permute-start.19 = (f32[16,512]{1,0:T(8,128)S(1)}, f32[16,512]{1,0:T(8,128)S(1)}, u32[]{:S(2)}, u32[]{:S(2)}) collective-permute-start(f32[16,512]{1,0:T(8,128)S(1)} %get-tuple-element.45.refs_4_), channel_id=1, source_target_pairs={{0,1},{1,0},{2,3},{3,2},{4,5},{5,4},{6,7},{7,6},{8,9},{9,8},{10,11... | collective-permute-start | bytes 98312 | tf_op jit(solution)/shard_map/ppermute | solution.py:354
  44.7 3.2 %collective-permute-start.17 = (f32[8,640]{1,0:T(8,128)S(1)}, f32[8,640]{1,0:T(8,128)S(1)}, u32[]{:S(2)}, u32[]{:S(2)}) collective-permute-start(f32[8,640]{1,0:T(8,128)S(1)} %get-tuple-element.44.refs_2_), channel_id=1, source_target_pairs={{0,16},{1,17},{2,18},{3,19},{4,20},{5,21},{6,22},{7,23},{8,24},{9,... | collective-permute-start | bytes 61448 | tf_op jit(solution)/shard_map/ppermute | solution.py:354
  46.1 1.8 %collective-permute-start.18 = (f32[8,640]{1,0:T(8,128)S(1)}, f32[8,640]{1,0:T(8,128)S(1)}, u32[]{:S(2)}, u32[]{:S(2)}) collective-permute-start(f32[8,640]{1,0:T(8,128)S(1)} %get-tuple-element.44.refs_2_), channel_id=1, source_target_pairs={{0,1},{1,0},{2,3},{3,2},{4,5},{5,4},{6,7},{7,6},{8,9},{9,8},{10,11... | collective-permute-start | bytes 61448 | tf_op jit(solution)/shard_map/ppermute | solution.py:354
